TPU v7x, 32 devices: a whole 2x2x4 slice. The times are simulated.
32 devices in a mesh: tile: 16 (over z, x, core), pos: 2 (over y).
Axes of the slice: x: 2, y: 2, z: 4, core: 2. Of those that a mesh axis runs over, the one named last changes fastest.
Arguments:
- tile_object: bfloat16 [16, 2, 2, 256, 256], P('tile'), may hold values from -5 to 5
- probe_modes: float32 [2, 256, 2, 256], replicated, may hold values from -6 to 6
- patterns: bfloat16 [16, 2, 2, 256, 256], P('tile', 'pos'), may hold values from 0 to 8
- offsets: int32 [16, 2, 2, 2], P('tile', 'pos'), may hold values from 0 to 255, as said below
- counts: int32 [16, 2], P('tile', 'pos'), may hold values from 0 to 2, as said below
Outputs:
- new_object: bfloat16 [16, 2, 2, 256, 256], P('tile')
- new_probe: float32 [2, 256, 2, 256], replicated
Inputs may be any that keep to these rules, and one draw needn't show every extreme that they name: In each tile the 2 counts add up to exactly 2, and one device of every tile holds 2. Tiles in the last tile row have row offsets of at most 0, tiles in the last tile column column offsets of at most 0, so every patch lies inside the object. Slots past a device's count hold offsets too and are not used.
All inputs are finite; a program needn't handle non-finite values.
Results may differ from a plain program's by a relative error of at most 0.011.
Values may be sent and summed in bfloat16 or wider, within the bound.
No kernel may reach another device: no remote copies, remote signals or barrier semaphores. Data moves between devices by JAX's collectives and lax.ppermute only.
A program may use at most 64 MiB of HBM per device.

v0:
```python
import math

import jax
import jax.numpy as jnp
import numpy as np
from jax import lax
from jax.sharding import PartitionSpec as P

GRID_ROWS = 4


fresnel_coeff = 0.25
object_rate = 0.05
probe_rate = 0.15


def from_behind(block, axis, distance):
    devices = range(lax.axis_size(axis))
    route = [(i - distance, i) for i in devices if i - distance in devices]
    return lax.ppermute(block, axis, route)


def real_embed(part_re, part_im):
    upper_half = np.concatenate([part_re, -part_im], axis=1)
    lower_half = np.concatenate([part_im, part_re], axis=1)
    stacked = np.concatenate([upper_half, lower_half], axis=0)
    return jnp.asarray(stacked, dtype=jnp.float32).astype(jnp.bfloat16)


def build_tables(pixels):
    indices = np.arange(pixels)
    angles = indices[:, None] * indices[None, :] % pixels * (2.0 * math.pi / pixels)
    norm_scale = 1.0 / math.sqrt(pixels)
    dft_re = np.cos(angles) * norm_scale
    dft_im = -np.sin(angles) * norm_scale
    frequency = np.where(indices < pixels // 2, indices, indices - pixels)
    phases = -2.0 * math.pi * fresnel_coeff / pixels * (frequency * frequency)
    phase_sum = phases[:, None] + angles
    kern_re = np.sum(np.cos(phase_sum), axis=0) / pixels
    kern_im = np.sum(np.sin(phase_sum), axis=0) / pixels
    lag_index = (indices[:, None] - indices[None, :]) % pixels
    prop_re = kern_re[lag_index]
    prop_im = kern_im[lag_index]
    return (
        real_embed(prop_re, prop_im),
        real_embed(prop_re, -prop_im),
        real_embed(dft_re, dft_im),
        real_embed(dft_re, -dft_im),
    )


def transform(matrix, wave_now):
    pixels = wave_now.shape[1]
    mode_count = wave_now.shape[2]
    flat_wave = wave_now.astype(jnp.bfloat16).reshape(2 * pixels, mode_count * pixels)
    first_pass = jnp.dot(matrix, flat_wave, preferred_element_type=jnp.float32)
    first_pass = first_pass.astype(jnp.bfloat16).reshape(2, pixels, mode_count, pixels)
    table_re = matrix[:pixels, :pixels]
    table_im = matrix[pixels:, :pixels]
    out_re = jnp.einsum(
        "rmc,dc->rmd", first_pass[0], table_re, preferred_element_type=jnp.float32
    ) - jnp.einsum("rmc,dc->rmd", first_pass[1], table_im, preferred_element_type=jnp.float32)
    out_im = jnp.einsum(
        "rmc,dc->rmd", first_pass[0], table_im, preferred_element_type=jnp.float32
    ) + jnp.einsum("rmc,dc->rmd", first_pass[1], table_re, preferred_element_type=jnp.float32)
    return jnp.stack([out_re, out_im])


def complex_mul(first, second):
    return jnp.stack(
        [first[0] * second[0] - first[1] * second[1], first[0] * second[1] + first[1] * second[0]]
    )


def conjugate(complex_value):
    return jnp.stack([complex_value[0], -complex_value[1]])


def position_terms(patch, probe_modes, pattern, matrices):
    depth = patch.shape[0]
    layers = [patch[layer_index][:, :, None, :] for layer_index in range(depth)]
    wave_now = complex_mul(probe_modes, layers[0])
    layer_index = 1
    moved = transform(matrices[0], wave_now)
    arrives = [moved]
    wave_now = complex_mul(layers[layer_index], moved)
    far_field = transform(matrices[2], wave_now)
    intensity = jnp.sum(far_field[0] * far_field[0] + far_field[1] * far_field[1], axis=1)
    residual = intensity - pattern
    backward = transform(matrices[3], far_field * residual[None, :, None, :])
    slice_grads = [None] * depth
    layer_index = 1
    slice_grads[layer_index] = jnp.sum(
        complex_mul(conjugate(arrives[layer_index - 1]), backward), axis=2
    )
    backward = transform(matrices[1], complex_mul(conjugate(layers[layer_index]), backward))
    slice_grads[0] = jnp.sum(complex_mul(conjugate(probe_modes), backward), axis=2)
    probe_term = complex_mul(conjugate(layers[0]), backward)
    return (jnp.stack(slice_grads), probe_term)


def shards(tile_object, probe_modes, patterns, offsets, counts):
    pixels = probe_modes.shape[1]
    matrices = build_tables(pixels)
    own_tile = tile_object[0]
    depth = own_tile.shape[0]
    tile_side = own_tile.shape[2]
    grid_cols = lax.axis_size("tile") // GRID_ROWS
    received = []
    for reach_tiles, edge_strip in (
        (1, own_tile),
        (grid_cols, own_tile),
        (grid_cols + 1, own_tile),
    ):
        received.append(from_behind(edge_strip, "tile", -reach_tiles))
    upper_rows = jnp.concatenate([own_tile, received[0]], axis=3)
    lower_rows = jnp.concatenate([received[1], received[2]], axis=3)
    extended = jnp.concatenate([upper_rows, lower_rows], axis=2)
    per_slot = patterns.shape[2]
    slot_patterns = patterns[0, 0]
    slot_offsets = offsets[0, 0]
    weights = (jnp.arange(per_slot, dtype=jnp.int32) < counts[0, 0]).astype(jnp.float32)
    zero_index = jnp.zeros((), jnp.int32)

    def accumulate(totals, position):
        grad_extended, grad_probe = totals
        pattern, placement, weight = position
        start = (zero_index, zero_index, placement[0], placement[1])
        patch = lax.dynamic_slice(extended, start, (depth, 2, pixels, pixels)).astype(jnp.float32)
        object_term, probe_term = position_terms(
            patch, probe_modes, pattern.astype(jnp.float32), matrices
        )
        current = lax.dynamic_slice(grad_extended, start, (depth, 2, pixels, pixels))
        grad_extended = lax.dynamic_update_slice(
            grad_extended, current + weight * object_term, start
        )
        return ((grad_extended, grad_probe + weight * probe_term), None)

    initial = (jnp.zeros(extended.shape, jnp.float32), jnp.zeros(probe_modes.shape, jnp.float32))
    (grad_extended, grad_probe), _ = lax.scan(
        accumulate, initial, (slot_patterns, slot_offsets, weights)
    )
    core_grad = grad_extended[:, :, :tile_side, :tile_side]
    for reach_tiles, edge_strip in (
        (1, grad_extended[:, :, :tile_side, tile_side:]),
        (grid_cols, grad_extended[:, :, tile_side:, :tile_side]),
        (grid_cols + 1, grad_extended[:, :, tile_side:, tile_side:]),
    ):
        arrived = from_behind(edge_strip, "tile", reach_tiles)
        core_grad = core_grad.at[:, :, : edge_strip.shape[2], : edge_strip.shape[3]].add(arrived)
    tile_grad = lax.psum(core_grad, "pos")
    probe_total = lax.psum(grad_probe, ("tile", "pos"))
    positions_all = lax.axis_size("tile") * lax.axis_size("pos") * (per_slot // 2)
    new_object = (own_tile.astype(jnp.float32) - object_rate * tile_grad).astype(jnp.bfloat16)[None]
    new_probe = probe_modes - probe_rate / math.sqrt(positions_all) * probe_total
    return (new_object, new_probe)


def solution(mesh):
    placed = (
        P("tile", None, None, None, None),
        P(),
        P("tile", "pos", None, None, None),
        P("tile", "pos", None, None),
        P("tile", "pos"),
    )
    return jax.shard_map(
        shards,
        mesh=mesh,
        in_specs=placed,
        out_specs=(P("tile", None, None, None, None), P()),
        check_vma=False,
    )
```

profile of v0, /device:TPU:0, one launch (start us, length us, event | category | flops | bytes accessed | tf_op | source)
XLA Modules:
  0.0 334.8 jit_solution(16754975067838032719)
XLA Ops:
  7.2 1.3 collective-permute-start.1
  8.5 1.3 collective-permute-start
  9.8 1.3 collective-permute-start.2
  11.8 1.3 copy.51
  13.9 11.2 %collective-permute-done.1 = bf16[2,2,256,256]{3,2,1,0:T(8,128)(2,1)S(1)} collective-permute-done((bf16[2,2,256,256]{3,2,1,0:T(8,128)(2,1)}, bf16[2,2,256,256]{3,2,1,0:T(8,128)(2,1)S(1)}, u32[]{:S(2)}, u32[]{:S(2)}) %collective-permute-start.1) | collective-permute-done | bytes 524320 | tf_op jit(solution)/shard_map/ppermute | solution.py:20
  25.1 9.7 %collective-permute-done.2 = bf16[2,2,256,256]{3,2,1,0:T(8,128)(2,1)} collective-permute-done((bf16[2,2,256,256]{3,2,1,0:T(8,128)(2,1)}, bf16[2,2,256,256]{3,2,1,0:T(8,128)(2,1)}, u32[]{:S(2)}, u32[]{:S(2)}) %collective-permute-start.2) | collective-permute-done | bytes 524320 | tf_op jit(solution)/shard_map/ppermute | solution.py:20
  34.8 2.7 maximum_maximum_fusion
  37.5 2.5 broadcast_in_dim.10
  40.0 86.8 %while.20 = (s32[]{:T(128)}, f32[2,2,512,512]{3,2,1,0:T(8,128)}, f32[2,256,2,256]{3,1,2,0:T(8,128)}, s32[2,2]{1,0:T(2,128)S(1)}, f32[2]{0:T(128)S(1)}, /*index=5...) while((s32[]{:T(128)}, f32[2,2,512,512]{3,2,1,0:T(8,128)}, ...), condition=%wide.region_4.5_spmd.clone, body=%wide.region_0.4_spmd.clone.sunk | while | flops 2160394240 | bytes 71434552 | solution.py:140
  44.8 1.5 dynamic-slice_convert_fusion.2
  47.3 1.5 fusion.194
  48.9 1.2 fusion.197
  50.0 1.2 convolution_subtract_fusion.6
  52.4 1.2 convolution_add_fusion.7
  54.5 1.5 fusion.199
  56.0 1.2 fusion.202
  57.2 1.2 fusion.201
  58.4 1.2 convolution_subtract_fusion.7
  59.6 1.2 add_reduce_fusion.2
  65.6 1.5 subtract_bitcast_fusion.3
  67.1 1.9 maximum_reduce_fusion.5
  69.0 2.4 fusion.214
  71.4 11.1 %dynamic_update_slice.6 = f32[2,2,512,512]{3,2,1,0:T(8,128)} dynamic-update-slice(f32[2,2,512,512]{3,2,1,0:T(8,128)} %get-tuple-element.473, f32[2,2,256,256]{3,2,1,0:T(8,128)S(1)} %fusion.214, s32[]{:T(128)} %constant.130.clone.1..sunk, s32[]{:T(128)} %constant.130.clone.1..sunk, s32[]{:T(128)S(6)} %select_n.16, s32[]{:T(128)S(6)} %select_n.17) | dynamic-update-slice | bytes 2097156 | tf_op jit(solution)/shard_map/while/body/eval_jaxpr/dynamic_update_slice | solution.py:134
  87.4 1.5 dynamic-slice_convert_fusion.2
  89.8 1.5 fusion.194
  92.6 1.2 convolution_subtract_fusion.6
  95.0 1.2 convolution_add_fusion.7
  97.0 1.5 fusion.199
  98.6 1.2 fusion.202
  99.8 1.2 fusion.201
  101.0 1.2 convolution_subtract_fusion.7
  102.2 1.2 add_reduce_fusion.2
  108.2 1.5 subtract_bitcast_fusion.3
  109.7 3.1 maximum_reduce_fusion.5
  112.8 2.4 fusion.214
  115.2 11.6 %dynamic_update_slice.6 = f32[2,2,512,512]{3,2,1,0:T(8,128)} dynamic-update-slice(f32[2,2,512,512]{3,2,1,0:T(8,128)} %get-tuple-element.473, f32[2,2,256,256]{3,2,1,0:T(8,128)S(1)} %fusion.214, s32[]{:T(128)} %constant.130.clone.1..sunk, s32[]{:T(128)} %constant.130.clone.1..sunk, s32[]{:T(128)S(6)} %select_n.16, s32[]{:T(128)S(6)} %select_n.17) | dynamic-update-slice | bytes 2097156 | tf_op jit(solution)/shard_map/while/body/eval_jaxpr/dynamic_update_slice | solution.py:134
  126.8 3.7 %fusion.64 = (f32[2,2,256,256]{3,2,1,0:T(8,128)}, f32[2,2,256,256]{3,2,1,0:T(8,128)}, f32[2,2,256,256]{3,2,1,0:T(8,128)}) fusion(f32[2,2,512,512]{3,2,1,0:T(8,128)} %get-tuple-element.178), kind=kLoop, calls=%fused_computation.110 | loop fusion | bytes 6291456 | tf_op jit(solution)/shard_map/slice | solution.py:145
  130.5 4.5 %collective-permute-start.3 = (f32[2,2,256,256]{3,2,1,0:T(8,128)}, f32[2,2,256,256]{3,2,1,0:T(8,128)S(1)}, u32[]{:S(2)}, u32[]{:S(2)}) collective-permute-start(f32[2,2,256,256]{3,2,1,0:T(8,128)} %get-tuple-element.310), channel_id=1, source_target_pairs={{0,2},{2,4},{4,6},{6,8},{8,10},{10,12},{12,14},{14,16},{16,18},{18... | collective-permute-start | bytes 3145736 | tf_op jit(solution)/shard_map/ppermute | solution.py:20
  135.0 4.8 %collective-permute-start.5 = (f32[2,2,256,256]{3,2,1,0:T(8,128)}, f32[2,2,256,256]{3,2,1,0:T(8,128)}, u32[]{:S(2)}, u32[]{:S(2)}) collective-permute-start(f32[2,2,256,256]{3,2,1,0:T(8,128)} %get-tuple-element.311), channel_id=1, source_target_pairs={{0,10},{2,12},{4,14},{6,16},{8,18},{10,20},{12,22},{14,24},{16,26}... | collective-permute-start | bytes 3145736 | tf_op jit(solution)/shard_map/ppermute | solution.py:20
  139.8 3.4 %collective-permute-start.4 = (f32[2,2,256,256]{3,2,1,0:T(8,128)}, f32[2,2,256,256]{3,2,1,0:T(8,128)}, u32[]{:S(2)}, u32[]{:S(2)}) collective-permute-start(f32[2,2,256,256]{3,2,1,0:T(8,128)} %get-tuple-element.312), channel_id=1, source_target_pairs={{0,8},{2,10},{4,12},{6,14},{8,16},{10,18},{12,20},{14,22},{16,24},... | collective-permute-start | bytes 3145736 | tf_op jit(solution)/shard_map/ppermute | solution.py:20
  143.2 3.0 copy.52
  146.3 13.4 %collective-permute-done.5 = f32[2,2,256,256]{3,2,1,0:T(8,128)} collective-permute-done((f32[2,2,256,256]{3,2,1,0:T(8,128)}, f32[2,2,256,256]{3,2,1,0:T(8,128)}, u32[]{:S(2)}, u32[]{:S(2)}) %collective-permute-start.5) | collective-permute-done | bytes 1048608 | tf_op jit(solution)/shard_map/ppermute | solution.py:20
  159.8 26.7 %collective-permute-done.4 = f32[2,2,256,256]{3,2,1,0:T(8,128)} collective-permute-done((f32[2,2,256,256]{3,2,1,0:T(8,128)}, f32[2,2,256,256]{3,2,1,0:T(8,128)}, u32[]{:S(2)}, u32[]{:S(2)}) %collective-permute-start.4) | collective-permute-done | bytes 1048608 | tf_op jit(solution)/shard_map/ppermute | solution.py:20
  186.4 3.2 add_add_fusion
  189.7 94.7 %all-reduce.5.cloned.1.call-done = f32[2,256,2,256]{3,2,1,0:T(2,128)} async-done(((f32[2,256,2,256]{3,2,1,0:T(2,128)}), f32[2,256,2,256]{3,2,1,0:T(2,128)}) %all-reduce.5.cloned.1.call-update) | async-done | bytes 1048592 | tf_op jit(solution)/shard_map/psum | solution.py:152
  284.4 2.9 multiply_subtract_fusion
  287.3 38.5 %all-reduce.3.cloned.1.call-done = f32[2,2,256,256]{3,2,1,0:T(8,128)} async-done(((f32[2,2,256,256]{3,2,1,0:T(8,128)}), f32[2,2,256,256]{3,2,1,0:T(8,128)}) %all-reduce.3.cloned.1.call-update) | async-done | bytes 1048592 | tf_op jit(solution)/shard_map/psum | solution.py:151
  325.8 2.1 fusion.57
  (92 shorter events, 19.9 us)
Async XLA Ops:
  7.2 277.2 %all-reduce.5.cloned.1.call-start = ((), (), s32[]{:S(2)}) async-start(), calls=%async_computation.1 | async-start | bytes 2097152 | tf_op jit(solution)/shard_map/psum | solution.py:152
  7.2 17.9 %collective-permute-start.1 = (bf16[2,2,256,256]{3,2,1,0:T(8,128)(2,1)}, bf16[2,2,256,256]{3,2,1,0:T(8,128)(2,1)S(1)}, u32[]{:S(2)}, u32[]{:S(2)}) collective-permute-start(bf16[2,2,256,256]{3,2,1,0:T(8,128)(2,1)} %bitcast.335), channel_id=1, source_target_pairs={{8,0},{10,2},{12,4},{14,6},{16,8},{18,10},{20,12},{22,14},{24,16},... | collective-permute-start | bytes 1572872 | tf_op jit(solution)/shard_map/ppermute | solution.py:20
  8.5 16.6 %collective-permute-start = (bf16[2,2,256,256]{3,2,1,0:T(8,128)(2,1)}, bf16[2,2,256,256]{3,2,1,0:T(8,128)(2,1)S(1)}, u32[]{:S(2)}, u32[]{:S(2)}) collective-permute-start(bf16[2,2,256,256]{3,2,1,0:T(8,128)(2,1)} %bitcast.336), channel_id=1, source_target_pairs={{2,0},{4,2},{6,4},{8,6},{10,8},{12,10},{14,12},{16,14},{18,16},{20... | collective-permute-start | bytes 1572872 | tf_op jit(solution)/shard_map/ppermute | solution.py:20
  9.8 25.0 %collective-permute-start.2 = (bf16[2,2,256,256]{3,2,1,0:T(8,128)(2,1)}, bf16[2,2,256,256]{3,2,1,0:T(8,128)(2,1)}, u32[]{:S(2)}, u32[]{:S(2)}) collective-permute-start(bf16[2,2,256,256]{3,2,1,0:T(8,128)(2,1)} %bitcast.337), channel_id=1, source_target_pairs={{10,0},{12,2},{14,4},{16,6},{18,8},{20,10},{22,12},{24,14},{26,16}... | collective-permute-start | bytes 1572872 | tf_op jit(solution)/shard_map/ppermute | solution.py:20
  13.9 26.1 %copy-start = (bf16[512,512]{1,0:T(8,128)(2,1)S(1)}, bf16[512,512]{1,0:T(8,128)(2,1)}, u32[]{:S(2)}) copy-start(bf16[512,512]{1,0:T(8,128)(2,1)} %constant.145) | copy-start | bytes 1572868
  13.9 26.1 %copy-start.1 = (bf16[512,512]{1,0:T(8,128)(2,1)S(1)}, bf16[512,512]{1,0:T(8,128)(2,1)}, u32[]{:S(2)}) copy-start(bf16[512,512]{1,0:T(8,128)(2,1)} %constant.144) | copy-start | bytes 1572868
  13.9 26.1 %copy-start.4 = (bf16[1,1,2,256,256]{4,3,2,1,0:T(8,128)(2,1)S(1)}, bf16[1,1,2,256,256]{4,3,2,1,0:T(8,128)(2,1)}, u32[]{:S(2)}) copy-start(bf16[1,1,2,256,256]{4,3,2,1,0:T(8,128)(2,1)} %param.25) | copy-start | bytes 786436
  13.9 26.1 %copy-start.5 = (s32[1,1,2,2]{3,2,1,0:T(2,128)S(1)}, s32[1,1,2,2]{3,2,1,0:T(2,128)}, u32[]{:S(2)}) copy-start(s32[1,1,2,2]{3,2,1,0:T(2,128)} %param.26) | copy-start | bytes 52
  130.5 15.9 %collective-permute-start.3 = (f32[2,2,256,256]{3,2,1,0:T(8,128)}, f32[2,2,256,256]{3,2,1,0:T(8,128)S(1)}, u32[]{:S(2)}, u32[]{:S(2)}) collective-permute-start(f32[2,2,256,256]{3,2,1,0:T(8,128)} %get-tuple-element.310), channel_id=1, source_target_pairs={{0,2},{2,4},{4,6},{6,8},{8,10},{10,12},{12,14},{14,16},{16,18},{18... | collective-permute-start | bytes 3145736 | tf_op jit(solution)/shard_map/ppermute | solution.py:20
  135.0 24.8 %collective-permute-start.5 = (f32[2,2,256,256]{3,2,1,0:T(8,128)}, f32[2,2,256,256]{3,2,1,0:T(8,128)}, u32[]{:S(2)}, u32[]{:S(2)}) collective-permute-start(f32[2,2,256,256]{3,2,1,0:T(8,128)} %get-tuple-element.311), channel_id=1, source_target_pairs={{0,10},{2,12},{4,14},{6,16},{8,18},{10,20},{12,22},{14,24},{16,26}... | collective-permute-start | bytes 3145736 | tf_op jit(solution)/shard_map/ppermute | solution.py:20
  139.8 46.6 %collective-permute-start.4 = (f32[2,2,256,256]{3,2,1,0:T(8,128)}, f32[2,2,256,256]{3,2,1,0:T(8,128)}, u32[]{:S(2)}, u32[]{:S(2)}) collective-permute-start(f32[2,2,256,256]{3,2,1,0:T(8,128)} %get-tuple-element.312), channel_id=1, source_target_pairs={{0,8},{2,10},{4,12},{6,14},{8,16},{10,18},{12,20},{14,22},{16,24},... | collective-permute-start | bytes 3145736 | tf_op jit(solution)/shard_map/ppermute | solution.py:20
  146.3 138.1 %copy-start.2 = (f32[2,256,2,256]{3,2,1,0:T(2,128)S(1)}, f32[2,256,2,256]{3,2,1,0:T(2,128)}, u32[]{:S(2)}) copy-start(f32[2,256,2,256]{3,2,1,0:T(2,128)} %param.24) | copy-start | bytes 3145732
  146.3 179.5 %copy-start.3 = (bf16[1,2,2,256,256]{4,3,2,1,0:T(8,128)(2,1)S(1)}, bf16[1,2,2,256,256]{4,3,2,1,0:T(8,128)(2,1)}, u32[]{:S(2)}) copy-start(bf16[1,2,2,256,256]{4,3,2,1,0:T(8,128)(2,1)} %param.23) | copy-start | bytes 1572868
  146.3 179.5 %all-reduce.3.cloned.1.call-start = ((), (), s32[]{:S(2)}) async-start(), calls=%async_computation | async-start | bytes 2097152 | tf_op jit(solution)/shard_map/psum | solution.py:151
Sparse Core Ops, SparseCore 0:
  146.4 137.9 all-reduce.4
  286.8 39.0 all-reduce.2
where the time goes:
time: 337 us; the launch traced here: 335 us
  waiting for transfers between devices  194 us (58%)
  local copies, waits for them, and re-layouts  41.2 us (12%)
  matrix products  34.1 us (10%)
  other arithmetic  26.1 us (8%)
  starting transfers between devices  16.7 us (5%)
  between operations  14.8 us (4%)
  loops' own time  7.82 us (2%)
    psum x1, waiting for transfers between devices, shards(): probe_total = lax.psum(grad_probe, ('tile', 'pos'))  94.7 us
    ppermute x6, waiting for transfers between devices, from_behind(): return lax.ppermute(block, axis, route)  60.9 us
    psum x1, waiting for transfers between devices, shards(): tile_grad = lax.psum(core_grad, 'pos')  38.5 us
    dynamic_update_slice x2, local copies, waits for them, and re-layouts, accumulate(): lax.dynamic_update_slice(grad_extended, current + weight * object_term, s...  22.7 us
    ppermute x6, starting transfers between devices, from_behind(): return lax.ppermute(block, axis, route)  16.6 us
    dot_general x8, matrix products, transform(): jnp.einsum('rmc,dc->rmd', first_pass[1], table_im, preferred_element_type...  8.64 us
    dot_general x8, matrix products, transform(): first_pass = jnp.dot(matrix, flat_wave, preferred_element_type=jnp.float32)  8.07 us
    another operation x1, loops' own time, shards(): lax.scan(accumulate, initial, (slot_patterns, slot_offsets, weights))  7.82 us
  transfers between devices with their start and end apart: 8, of which 6 were waited for; matrix products, arithmetic and copies ran while one was open for 3% of the time, Pallas kernels for 0%

commit v1 on v0

v1 whole, which is shorter than its diff:
```python
import functools
import math

import jax
import jax.numpy as jnp
import numpy as np
from jax import lax
from jax.experimental import pallas as pl
from jax.experimental.pallas import tpu as pltpu
from jax.sharding import PartitionSpec as P

GRID_ROWS = 4


fresnel_coeff = 0.25
object_rate = 0.05
probe_rate = 0.15

f32 = jnp.float32
bf16 = jnp.bfloat16


def from_behind(block, axis, distance):
    devices = range(lax.axis_size(axis))
    route = [(i - distance, i) for i in devices if i - distance in devices]
    return lax.ppermute(block, axis, route)


def real_embed(part_re, part_im):
    upper_half = np.concatenate([part_re, -part_im], axis=1)
    lower_half = np.concatenate([part_im, part_re], axis=1)
    stacked = np.concatenate([upper_half, lower_half], axis=0)
    return jnp.asarray(stacked, dtype=f32).astype(bf16)


def build_tables(pixels):
    indices = np.arange(pixels)
    angles = indices[:, None] * indices[None, :] % pixels * (2.0 * math.pi / pixels)
    norm_scale = 1.0 / math.sqrt(pixels)
    dft_re = np.cos(angles) * norm_scale
    dft_im = -np.sin(angles) * norm_scale
    frequency = np.where(indices < pixels // 2, indices, indices - pixels)
    phases = -2.0 * math.pi * fresnel_coeff / pixels * (frequency * frequency)
    phase_sum = phases[:, None] + angles
    kern_re = np.sum(np.cos(phase_sum), axis=0) / pixels
    kern_im = np.sum(np.sin(phase_sum), axis=0) / pixels
    lag_index = (indices[:, None] - indices[None, :]) % pixels
    prop_re = kern_re[lag_index]
    prop_im = kern_im[lag_index]
    return (
        real_embed(prop_re, prop_im),
        real_embed(prop_re, -prop_im),
        real_embed(dft_re, dft_im),
        real_embed(dft_re, -dft_im),
    )


def dot(a, b):
    return jnp.dot(a, b, preferred_element_type=f32)


def position_kernel(
    spot_ref, own_ref, right_ref, below_ref, diag_ref, probe_ref, pattern_ref, prop_ref,
    prop_c_ref, dft_ref, dft_c_ref, home_ref, next_ref, down_ref, term_ref,
):
    depth, _, n, _ = own_ref.shape
    modes = probe_ref.shape[2] // n
    row, col = spot_ref[0], spot_ref[1]
    i_out = lax.broadcasted_iota(jnp.int32, (n, 2 * n), 0)
    i_in = lax.broadcasted_iota(jnp.int32, (n, 2 * n), 1)
    take_rows = (i_in == i_out + row).astype(f32).astype(bf16)
    take_cols_t = (i_in == i_out + col).astype(f32).astype(bf16)
    j_in = lax.broadcasted_iota(jnp.int32, (2 * n, n), 0)
    j_out = lax.broadcasted_iota(jnp.int32, (2 * n, n), 1)
    take_cols = (j_in == j_out + col).astype(f32).astype(bf16)
    take_rows_t = (j_in == j_out + row).astype(f32).astype(bf16)
    wrap_cols = take_cols_t[:, :n] + take_cols_t[:, n:]

    def patch(layer, part):
        window = (layer, part)
        upper = jnp.concatenate([own_ref[window], right_ref[window]], axis=1)
        lower = jnp.concatenate([below_ref[window], diag_ref[window]], axis=1)
        rows = dot(take_rows, jnp.concatenate([upper, lower], axis=0)).astype(bf16)
        return dot(rows, take_cols)

    def spread(layer, part, grad):
        grad = grad.astype(bf16)
        rows = dot(take_rows_t, grad).astype(bf16)
        wide = dot(rows[:n], take_cols_t).astype(bf16)
        home_ref[layer, part] = wide[:, :n]
        next_ref[layer, part] = wide[:, n:]
        down_ref[layer, part] = dot(rows[n:], wrap_cols).astype(bf16)

    def transform(left_ref, right_ref, wave_re, wave_im):
        wave = jnp.concatenate([wave_re.astype(bf16), wave_im.astype(bf16)], axis=0)
        first = dot(left_ref[...], wave).astype(bf16)
        first = jnp.concatenate([first[:n], first[n:]], axis=1)
        out = dot(first, right_ref[...])
        return out[:, :n], out[:, n:]

    layers = [(patch(layer, 0), patch(layer, 1)) for layer in range(depth)]
    near = layers[0]
    far = layers[1]
    arrives = []
    fields = []
    for mode in range(modes):
        lanes = pl.ds(mode * n, n)
        p_re, p_im = probe_ref[0, :, lanes], probe_ref[1, :, lanes]
        a_re, a_im = transform(
            prop_ref, prop_c_ref, p_re * near[0] - p_im * near[1], p_re * near[1] + p_im * near[0]
        )
        arrives.append((a_re, a_im))
        fields.append(
            transform(
                dft_ref, dft_c_ref, far[0] * a_re - far[1] * a_im, far[0] * a_im + far[1] * a_re
            )
        )
    intensity = sum(f_re * f_re + f_im * f_im for f_re, f_im in fields)
    residual = intensity - pattern_ref[...].astype(f32)
    grad_far = [0.0, 0.0]
    grad_near = [0.0, 0.0]
    for mode in range(modes):
        lanes = pl.ds(mode * n, n)
        f_re, f_im = fields[mode]
        a_re, a_im = arrives[mode]
        b_re, b_im = transform(dft_c_ref, dft_ref, f_re * residual, f_im * residual)
        grad_far[0] += a_re * b_re + a_im * b_im
        grad_far[1] += a_re * b_im - a_im * b_re
        b_re, b_im = transform(
            prop_c_ref, prop_ref, far[0] * b_re + far[1] * b_im, far[0] * b_im - far[1] * b_re
        )
        p_re, p_im = probe_ref[0, :, lanes], probe_ref[1, :, lanes]
        grad_near[0] += p_re * b_re + p_im * b_im
        grad_near[1] += p_re * b_im - p_im * b_re
        term_ref[0, :, lanes] = (near[0] * b_re + near[1] * b_im).astype(bf16)
        term_ref[1, :, lanes] = (near[0] * b_im - near[1] * b_re).astype(bf16)
    for layer, grad in enumerate((grad_near, grad_far)):
        for part in range(2):
            spread(layer, part, grad[part])


def position_terms(spot, own, right, below, diag, probe, pattern, tables):
    tile = jax.ShapeDtypeStruct(own.shape, bf16)
    vmem = pl.BlockSpec(memory_space=pltpu.VMEM)
    return pl.pallas_call(
        position_kernel,
        out_shape=(tile, tile, tile, jax.ShapeDtypeStruct(probe.shape, bf16)),
        in_specs=[pl.BlockSpec(memory_space=pltpu.SMEM)] + [vmem] * 10,
        out_specs=(vmem,) * 4,
        compiler_params=pltpu.CompilerParams(vmem_limit_bytes=40 * 2**20),
        cost_estimate=pl.CostEstimate(
            flops=5_000_000_000, bytes_accessed=10_000_000, transcendentals=0
        ),
        name="position",
    )(spot, own, right, below, diag, probe, pattern, *tables)


def pick_position(patterns, offsets, counts):
    owners = lax.axis_size("pos")
    if owners == 2:
        swap = [(0, 1), (1, 0)]
        other_spot = lax.ppermute(offsets[1], "pos", swap)
        other_pattern = lax.ppermute(patterns[1], "pos", swap)
        busy = counts == 2
        return jnp.where(busy, offsets[0], other_spot), jnp.where(busy, patterns[0], other_pattern)
    all_counts = lax.all_gather(counts, "pos")
    ends = jnp.cumsum(all_counts)
    rank = lax.axis_index("pos")
    source = jnp.sum((ends <= rank).astype(jnp.int32))
    slot = rank - (ends[source] - all_counts[source])
    all_offsets = lax.all_gather(offsets, "pos")
    all_patterns = lax.all_gather(patterns, "pos")
    return all_offsets[source, slot], all_patterns[source, slot]


def probe_sum(term):
    devices = lax.axis_size("tile") * lax.axis_size("pos")
    rows = term.shape[0] * term.shape[1] // devices
    blocks = term.reshape(devices, rows, term.shape[2])
    mine = lax.all_to_all(blocks, ("tile", "pos"), 0, 0, tiled=True)
    total = jnp.sum(mine.astype(f32), axis=0).astype(bf16)
    return lax.all_gather(total, ("tile", "pos"), tiled=True).reshape(term.shape)


def shards(tile_object, probe_modes, patterns, offsets, counts):
    pixels = probe_modes.shape[1]
    tables = build_tables(pixels)
    own = tile_object[0]
    grid_cols = lax.axis_size("tile") // GRID_ROWS
    below = from_behind(own, "tile", -grid_cols)
    right = from_behind(own, "tile", -1)
    spot, pattern = pick_position(patterns[0, 0], offsets[0, 0], counts[0, 0])
    spot_above = from_behind(spot, "tile", grid_cols)
    diag = from_behind(below, "tile", -1)
    probe = probe_modes.reshape(2, pixels, -1)
    home, beside, down, term = position_terms(
        spot, own, right, below, diag, probe, pattern, tables
    )
    from_above = from_behind(down, "tile", grid_cols)
    total = probe_sum(term)
    split = jnp.arange(pixels, dtype=jnp.int32) < spot_above[1]
    zero = jnp.zeros((), bf16)
    beside = beside + jnp.where(split, from_above, zero)
    from_left = from_behind(beside, "tile", 1)
    part = (
        home.astype(f32) + jnp.where(split, zero, from_above).astype(f32) + from_left.astype(f32)
    ).astype(bf16)
    part = lax.optimization_barrier(part)
    if lax.axis_size("pos") == 2:
        tile_grad = part.astype(f32) + lax.ppermute(part, "pos", [(0, 1), (1, 0)]).astype(f32)
    else:
        tile_grad = lax.psum(part.astype(f32), "pos")
    new_object = (own.astype(f32) - object_rate * tile_grad).astype(bf16)[None]
    positions_all = lax.axis_size("tile") * lax.axis_size("pos") * (patterns.shape[2] // 2)
    step = probe_rate / math.sqrt(positions_all)
    new_probe = probe_modes - step * total.astype(f32).reshape(probe_modes.shape)
    return (new_object, new_probe)


def solution(mesh):
    placed = (
        P("tile", None, None, None, None),
        P(),
        P("tile", "pos", None, None, None),
        P("tile", "pos", None, None),
        P("tile", "pos"),
    )
    return jax.shard_map(
        shards,
        mesh=mesh,
        in_specs=placed,
        out_specs=(P("tile", None, None, None, None), P()),
        check_vma=False,
    )
```

time: 337 us -> 158 us (0.47)
  waiting for transfers between devices: 194 us -> 32.2 us
  blocking collectives: 0 us -> 69.3 us
  matrix products: 34.1 us -> 0 us
  local copies, waits for them, and re-layouts: 41.2 us -> 14.1 us
  other arithmetic: 26.1 us -> 5.7 us
  between operations: 14.8 us -> 1.47 us
  starting transfers between devices: 16.7 us -> 26.3 us
  Pallas kernels: 0 us -> 8.3 us
  loops' own time: 7.82 us -> 0 us
    psum x2 -> x0, waiting for transfers between devices: 133 us -> none  [the longest x1 94.7 us: shards(): probe_total = lax.psum(grad_probe, ('tile', 'pos'))]
    all_gather x0 -> x1, blocking collectives: none -> 69.3 us  [probe_sum(): lax.all_gather(total, ('tile', 'pos'), tiled=True).reshape(term.shape)]
    ppermute x6, waiting for transfers between devices: 60.9 us -> 21 us  [from_behind(): return lax.ppermute(block, axis, route)]
    dot_general x40 -> x0, matrix products: 34.1 us -> none  [the longest x8 8.64 us: transform(): jnp.einsum('rmc,dc->rmd', first_pass[1], table_im, preferred_element_type...]
    dynamic_update_slice x2 -> x0, local copies, waits for them, and re-layouts: 22.7 us -> none  [accumulate(): lax.dynamic_update_slice(grad_extended, current + weight * object_term, s...]
    all_to_all x0 -> x1, waiting for transfers between devices: none -> 9.28 us  [probe_sum(): mine = lax.all_to_all(blocks, ('tile', 'pos'), 0, 0, tiled=True)]
    pallas_call x0 -> x1, Pallas kernels: none -> 8.3 us  [position_terms(): pl.pallas_call(position_kernel, out_shape=(tile, tile, tile, jax.ShapeDty...]
    add x3 -> x1, other arithmetic: 8.12 us -> 0.06 us  [shards(): beside = beside + jnp.where(split, from_above, zero)]
  transfers between devices with their start and end apart: 8 -> 10, of which waited for: 6 -> 5; matrix products, arithmetic and copies ran while one was open for 3% -> 6% of each run, Pallas kernels for 0% -> 0%
where the time goes in v1:
time: 158 us; the launch traced here: 157 us
  blocking collectives  69.3 us (44%)
  waiting for transfers between devices  32.2 us (20%)
  starting transfers between devices  26.3 us (17%)
  local copies, waits for them, and re-layouts  14.1 us (9%)
  Pallas kernels  8.3 us (5%)
  other arithmetic  5.7 us (4%)
    all_gather x1, blocking collectives, probe_sum(): lax.all_gather(total, ('tile', 'pos'), tiled=True).reshape(term.shape)  69.3 us
    ppermute x6, waiting for transfers between devices, from_behind(): return lax.ppermute(block, axis, route)  21 us
    ppermute x6, starting transfers between devices, from_behind(): return lax.ppermute(block, axis, route)  13.5 us
    all_to_all x1, waiting for transfers between devices, probe_sum(): mine = lax.all_to_all(blocks, ('tile', 'pos'), 0, 0, tiled=True)  9.28 us
    pallas_call x1, Pallas kernels, position_terms(): pl.pallas_call(position_kernel, out_shape=(tile, tile, tile, jax.ShapeDty...  8.3 us
    unnamed x24, local copies, waits for them, and re-layouts  7.85 us
    all_to_all x1, starting transfers between devices, probe_sum(): mine = lax.all_to_all(blocks, ('tile', 'pos'), 0, 0, tiled=True)  6.37 us
  transfers between devices with their start and end apart: 10, of which 5 were waited for; matrix products, arithmetic and copies ran while one was open for 6% of the time, Pallas kernels for 0%

profile of v1, /device:TPU:0, one launch (start us, length us, event | category | flops | bytes accessed | tf_op | source)
XLA Modules:
  0.0 157.4 jit_solution(1816086116117389005)
XLA Ops:
  0.6 0.0 copy-start.11
  0.6 1.3 collective-permute-start.2
  1.9 1.3 collective-permute-start.1
  3.2 0.0 copy-done.11
  3.3 3.0 %collective-permute-start = (s32[2]{0:T(128)S(1)}, s32[2]{0:T(128)S(1)}, u32[]{:S(2)}, u32[]{:S(2)}) collective-permute-start(s32[2]{0:T(128)S(1)} %slice_bitcast_fusion.1), channel_id=1, source_target_pairs={{0,1},{1,0},{2,3},{3,2},{4,5},{5,4},{6,7},{7,6},{8,9},{9,8},{10,11... | collective-permute-start | bytes 32 | tf_op jit(solution)/shard_map/ppermute | solution.py:162
  6.3 11.4 %collective-permute-done.2.below_ref = bf16[2,2,256,256]{3,2,1,0:T(8,128)(2,1)S(1)} collective-permute-done((bf16[2,2,256,256]{3,2,1,0:T(8,128)(2,1)}, bf16[2,2,256,256]{3,2,1,0:T(8,128)(2,1)S(1)}, u32[]{:S(2)}, u32[]{:S(2)}) %collective-permute-start.2) | collective-permute-done | bytes 524320 | tf_op jit(solution)/shard_map/ppermute | solution.py:26
  17.7 1.3 collective-permute-start.3
  19.0 1.6 slice_bitcast_fusion
  20.6 1.7 %collective-permute-start.4 = (bf16[256,256]{1,0:T(8,128)(2,1)}, bf16[256,256]{1,0:T(8,128)(2,1)S(1)}, u32[]{:S(2)}, u32[]{:S(2)}) collective-permute-start(bf16[256,256]{1,0:T(8,128)(2,1)} %slice_bitcast_fusion), channel_id=1, source_target_pairs={{0,1},{1,0},{2,3},{3,2},{4,5},{5,4},{6,7},{7,6},{8,9},{9,8},{10,11... | collective-permute-start | bytes 393224 | tf_op jit(solution)/shard_map/ppermute | solution.py:163
  22.9 0.0 copy-start.10
  22.9 0.0 copy-start
  22.9 2.1 %reshape.26.probe_ref = f32[2,256,512]{2,1,0:T(8,128)S(1)} reshape(f32[2,256,2,256]{3,2,1,0:T(2,128)} %param.10) | data formatting | bytes 2097152 | tf_op jit(solution)/shard_map/reshape | solution.py:195
  25.1 0.0 collective-permute-done
  25.1 1.9 %collective-permute-done.4 = bf16[256,256]{1,0:T(8,128)(2,1)S(1)} collective-permute-done((bf16[256,256]{1,0:T(8,128)(2,1)}, bf16[256,256]{1,0:T(8,128)(2,1)S(1)}, u32[]{:S(2)}, u32[]{:S(2)}) %collective-permute-start.4) | collective-permute-done | bytes 131104 | tf_op jit(solution)/shard_map/ppermute | solution.py:163
  27.0 0.0 copy-done.10
  27.0 0.0 collective-permute-done.1.right_ref
  27.0 0.0 copy-start.1
  27.0 0.8 copy-done.1
  27.8 0.0 collective-permute-done.3.diag_ref
  27.8 0.8 copy-done.3
  28.6 0.0 copy-done
  28.6 1.0 copy-done.2
  29.7 1.0 copy-done.4
  30.7 1.0 copy-done.5
  31.7 1.0 copy-done.6
  32.8 1.0 copy-done.7
  33.8 1.0 copy-done.8
  34.9 8.3 %position.1 = (bf16[2,2,256,256]{3,2,1,0:T(8,128)(2,1)S(1)}, bf16[2,2,256,256]{3,2,1,0:T(8,128)(2,1)S(1)}, bf16[2,2,256,256]{3,2,1,0:T(8,128)(2,1)}, bf16[2,256,512]{2,1,0:T(8,128)(2,1)}) custom-call(s32[2]{0:T(128)S(1)} %broadcast_select_fusion.spot_ref, bf16[2,2,256,256]{3,2,1,0:T(8,128)(2,1)S(1)} %bitcast.17, bf16[2,2,256,256]{3,2,1,0:T(8,128)(2,1)S(1)} %copy-done.2, ...), custom_call_target="tpu_custom_call" | custom-call | flops 5000000000 | bytes 10000000 | tf_op jit(solution)/shard_map/position/pallas_call | solution.py:145
  43.2 4.0 %collective-permute-start.6 = (bf16[2,2,256,256]{3,2,1,0:T(8,128)(2,1)}, bf16[2,2,256,256]{3,2,1,0:T(8,128)(2,1)S(1)}, u32[]{:S(2)}, u32[]{:S(2)}) collective-permute-start(bf16[2,2,256,256]{3,2,1,0:T(8,128)(2,1)} %get-tuple-element.7), channel_id=1, source_target_pairs={{0,8},{2,10},{4,12},{6,14},{8,16},{10,18},{12,20},{14,22},{16,24},... | collective-permute-start | bytes 1572872 | tf_op jit(solution)/shard_map/ppermute | solution.py:26
  47.2 3.5 %collective-permute-start.5 = (s32[2]{0:T(128)S(1)}, s32[2]{0:T(128)S(1)}, u32[]{:S(2)}, u32[]{:S(2)}) collective-permute-start(s32[2]{0:T(128)S(1)} %broadcast_select_fusion.spot_ref), channel_id=1, source_target_pairs={{0,8},{2,10},{4,12},{6,14},{8,16},{10,18},{12,20},{14,22},{16,24},... | collective-permute-start | bytes 32 | tf_op jit(solution)/shard_map/ppermute | solution.py:26
  50.6 8.1 %collective-permute-done.5 = s32[2]{0:T(128)S(1)} collective-permute-done((s32[2]{0:T(128)S(1)}, s32[2]{0:T(128)S(1)}, u32[]{:S(2)}, u32[]{:S(2)}) %collective-permute-start.5) | collective-permute-done | bytes 40 | tf_op jit(solution)/shard_map/ppermute | solution.py:26
  58.7 0.6 slice.23
  59.3 0.6 iota_compare_fusion
  59.9 6.4 %all-to-all-start = ((bf16[32,16,512]{2,1,0:T(8,128)(2,1)}), bf16[32,16,512]{2,1,0:T(8,128)(2,1)S(1)}, u32[]{:S(2)}, u32[]{:S(2)}) async-start(bf16[32,16,512]{2,1,0:T(8,128)(2,1)} %bitcast.8), calls=%async_computation | async-start | bytes 1048576 | tf_op jit(solution)/shard_map/all_to_all | solution.py:180
  66.3 0.0 collective-permute-done.6
  66.3 0.1 select_add_fusion
  66.4 2.2 %collective-permute-start.7 = (bf16[2,2,256,256]{3,2,1,0:T(8,128)(2,1)S(1)}, bf16[2,2,256,256]{3,2,1,0:T(8,128)(2,1)S(1)}, u32[]{:S(2)}, u32[]{:S(2)}) collective-permute-start(bf16[2,2,256,256]{3,2,1,0:T(8,128)(2,1)S(1)} %select_add_fusion), channel_id=1, source_target_pairs={{0,2},{2,4},{4,6},{6,8},{8,10},{10,12},{12,14},{14,16},{16,18},{18... | collective-permute-start | bytes 1572872 | tf_op jit(solution)/shard_map/ppermute | solution.py:26
  68.6 1.5 collective-permute-done.7
  70.1 0.2 add_convert_fusion
  70.3 1.7 %collective-permute-start.8 = (bf16[2,2,256,256]{3,2,1,0:T(8,128)(2,1)S(1)}, bf16[2,2,256,256]{3,2,1,0:T(8,128)(2,1)}, u32[]{:S(2)}, u32[]{:S(2)}) collective-permute-start(bf16[2,2,256,256]{3,2,1,0:T(8,128)(2,1)S(1)} %add_convert_fusion), channel_id=1, source_target_pairs={{0,1},{1,0},{2,3},{3,2},{4,5},{5,4},{6,7},{7,6},{8,9},{9,8},{10,11... | collective-permute-start | bytes 1572872 | tf_op jit(solution)/shard_map/ppermute | solution.py:210
  72.0 9.3 %all-to-all-done = bf16[32,16,512]{2,1,0:T(8,128)(2,1)S(1)} async-done(((bf16[32,16,512]{2,1,0:T(8,128)(2,1)}), bf16[32,16,512]{2,1,0:T(8,128)(2,1)S(1)}, u32[]{:S(2)}, u32[]{:S(2)}) %all-to-all-start) | async-done | bytes 524320 | tf_op jit(solution)/shard_map/all_to_all | solution.py:180
  81.3 0.1 reduce_sum.12
  81.4 69.3 %all_gather.3 = bf16[512,512]{1,0:T(8,128)(2,1)S(1)} all-gather(bf16[16,512]{1,0:T(8,128)(2,1)S(1)} %reduce_sum.12), channel_id=1, replica_groups=mesh['tile'=16,'pos'=2] {'tile','pos'}, dimensions={0}, use_global_device_ids=true | all-gather | bytes 540672 | tf_op jit(solution)/shard_map/all_gather | solution.py:182
  150.7 1.1 convert_multiply_fusion
  151.8 2.0 %mul.19 = f32[2,256,2,256]{3,2,1,0:T(2,128)S(1)} reshape(f32[512,512]{1,0:T(8,128)} %convert_multiply_fusion) | data formatting | bytes 2097152 | tf_op jit(solution)/shard_map/mul | solution.py:216
  153.8 1.5 sub.7
  155.3 0.0 collective-permute-done.8
  155.3 2.1 %fusion = bf16[1,2,2,256,256]{4,3,2,1,0:T(8,128)(2,1)} fusion(bf16[2,2,256,256]{3,2,1,0:T(8,128)(2,1)} %collective-permute-done.8, bf16[2,2,256,256]{3,2,1,0:T(8,128)(2,1)S(1)} %add_convert_fusion, bf16[1,2,2,256,256]{4,3,2,1,0:T(8,128)(2,1)S(1)} %copy-done), kind=kLoop, calls=%fused_computation.3 | loop fusion | flops 1835008 | bytes 2097152 | tf_op jit(solution)/shard_map/broadcast_in_dim | solution.py:213
  (12 shorter events, 0.0 us)
Async XLA Ops:
  0.6 2.6 %copy-start.11 = (s32[1,1,2,2]{3,2,1,0:T(2,128)S(1)}, s32[1,1,2,2]{3,2,1,0:T(2,128)}, u32[]{:S(2)}) copy-start(s32[1,1,2,2]{3,2,1,0:T(2,128)} %param.12) | copy-start | bytes 52
  0.6 17.1 %collective-permute-start.2 = (bf16[2,2,256,256]{3,2,1,0:T(8,128)(2,1)}, bf16[2,2,256,256]{3,2,1,0:T(8,128)(2,1)S(1)}, u32[]{:S(2)}, u32[]{:S(2)}) collective-permute-start(bf16[2,2,256,256]{3,2,1,0:T(8,128)(2,1)} %bitcast.15), channel_id=1, source_target_pairs={{8,0},{10,2},{12,4},{14,6},{16,8},{18,10},{20,12},{22,14},{24,16},... | collective-permute-start | bytes 1572872 | tf_op jit(solution)/shard_map/ppermute | solution.py:26
  1.9 25.1 %collective-permute-start.1 = (bf16[2,2,256,256]{3,2,1,0:T(8,128)(2,1)}, bf16[2,2,256,256]{3,2,1,0:T(8,128)(2,1)S(1)}, u32[]{:S(2)}, u32[]{:S(2)}) collective-permute-start(bf16[2,2,256,256]{3,2,1,0:T(8,128)(2,1)} %bitcast.16), channel_id=1, source_target_pairs={{2,0},{4,2},{6,4},{8,6},{10,8},{12,10},{14,12},{16,14},{18,16},{20... | collective-permute-start | bytes 1572872 | tf_op jit(solution)/shard_map/ppermute | solution.py:26
  3.3 21.8 %collective-permute-start = (s32[2]{0:T(128)S(1)}, s32[2]{0:T(128)S(1)}, u32[]{:S(2)}, u32[]{:S(2)}) collective-permute-start(s32[2]{0:T(128)S(1)} %slice_bitcast_fusion.1), channel_id=1, source_target_pairs={{0,1},{1,0},{2,3},{3,2},{4,5},{5,4},{6,7},{7,6},{8,9},{9,8},{10,11... | collective-permute-start | bytes 32 | tf_op jit(solution)/shard_map/ppermute | solution.py:162
  17.7 10.1 %collective-permute-start.3 = (bf16[2,2,256,256]{3,2,1,0:T(8,128)(2,1)S(1)}, bf16[2,2,256,256]{3,2,1,0:T(8,128)(2,1)S(1)}, u32[]{:S(2)}, u32[]{:S(2)}) collective-permute-start(bf16[2,2,256,256]{3,2,1,0:T(8,128)(2,1)S(1)} %collective-permute-done.2.below_ref), channel_id=1, source_target_pairs={{2,0},{4,2},{6,4},{8,6},{10,8},{12,10},{14,12},{16,14},{18,16},{20... | collective-permute-start | bytes 1572872 | tf_op jit(solution)/shard_map/ppermute | solution.py:26
  20.6 6.4 %collective-permute-start.4 = (bf16[256,256]{1,0:T(8,128)(2,1)}, bf16[256,256]{1,0:T(8,128)(2,1)S(1)}, u32[]{:S(2)}, u32[]{:S(2)}) collective-permute-start(bf16[256,256]{1,0:T(8,128)(2,1)} %slice_bitcast_fusion), channel_id=1, source_target_pairs={{0,1},{1,0},{2,3},{3,2},{4,5},{5,4},{6,7},{7,6},{8,9},{9,8},{10,11... | collective-permute-start | bytes 393224 | tf_op jit(solution)/shard_map/ppermute | solution.py:163
  22.9 4.1 %copy-start.10 = (bf16[1,1,2,256,256]{4,3,2,1,0:T(8,128)(2,1)S(1)}, bf16[1,1,2,256,256]{4,3,2,1,0:T(8,128)(2,1)}, u32[]{:S(2)}) copy-start(bf16[1,1,2,256,256]{4,3,2,1,0:T(8,128)(2,1)} %param.11) | copy-start | bytes 786436
  22.9 5.7 %copy-start = (bf16[1,2,2,256,256]{4,3,2,1,0:T(8,128)(2,1)S(1)}, bf16[1,2,2,256,256]{4,3,2,1,0:T(8,128)(2,1)}, u32[]{:S(2)}) copy-start(bf16[1,2,2,256,256]{4,3,2,1,0:T(8,128)(2,1)} %param.9) | copy-start | bytes 1572868
  27.0 0.8 copy-start.1
  27.8 0.8 copy-start.3
  28.6 1.0 copy-start.2
  29.7 1.0 copy-start.4
  30.7 1.0 copy-start.5
  31.7 1.0 copy-start.6
  32.8 1.0 copy-start.7
  33.8 1.0 copy-start.8
  43.2 23.1 %collective-permute-start.6 = (bf16[2,2,256,256]{3,2,1,0:T(8,128)(2,1)}, bf16[2,2,256,256]{3,2,1,0:T(8,128)(2,1)S(1)}, u32[]{:S(2)}, u32[]{:S(2)}) collective-permute-start(bf16[2,2,256,256]{3,2,1,0:T(8,128)(2,1)} %get-tuple-element.7), channel_id=1, source_target_pairs={{0,8},{2,10},{4,12},{6,14},{8,16},{10,18},{12,20},{14,22},{16,24},... | collective-permute-start | bytes 1572872 | tf_op jit(solution)/shard_map/ppermute | solution.py:26
  47.2 11.5 %collective-permute-start.5 = (s32[2]{0:T(128)S(1)}, s32[2]{0:T(128)S(1)}, u32[]{:S(2)}, u32[]{:S(2)}) collective-permute-start(s32[2]{0:T(128)S(1)} %broadcast_select_fusion.spot_ref), channel_id=1, source_target_pairs={{0,8},{2,10},{4,12},{6,14},{8,16},{10,18},{12,20},{14,22},{16,24},... | collective-permute-start | bytes 32 | tf_op jit(solution)/shard_map/ppermute | solution.py:26
  59.9 21.4 %all-to-all-start = ((bf16[32,16,512]{2,1,0:T(8,128)(2,1)}), bf16[32,16,512]{2,1,0:T(8,128)(2,1)S(1)}, u32[]{:S(2)}, u32[]{:S(2)}) async-start(bf16[32,16,512]{2,1,0:T(8,128)(2,1)} %bitcast.8), calls=%async_computation | async-start | bytes 1048576 | tf_op jit(solution)/shard_map/all_to_all | solution.py:180
  66.4 3.7 %collective-permute-start.7 = (bf16[2,2,256,256]{3,2,1,0:T(8,128)(2,1)S(1)}, bf16[2,2,256,256]{3,2,1,0:T(8,128)(2,1)S(1)}, u32[]{:S(2)}, u32[]{:S(2)}) collective-permute-start(bf16[2,2,256,256]{3,2,1,0:T(8,128)(2,1)S(1)} %select_add_fusion), channel_id=1, source_target_pairs={{0,2},{2,4},{4,6},{6,8},{8,10},{10,12},{12,14},{14,16},{16,18},{18... | collective-permute-start | bytes 1572872 | tf_op jit(solution)/shard_map/ppermute | solution.py:26
  70.3 85.0 %collective-permute-start.8 = (bf16[2,2,256,256]{3,2,1,0:T(8,128)(2,1)S(1)}, bf16[2,2,256,256]{3,2,1,0:T(8,128)(2,1)}, u32[]{:S(2)}, u32[]{:S(2)}) collective-permute-start(bf16[2,2,256,256]{3,2,1,0:T(8,128)(2,1)S(1)} %add_convert_fusion), channel_id=1, source_target_pairs={{0,1},{1,0},{2,3},{3,2},{4,5},{5,4},{6,7},{7,6},{8,9},{9,8},{10,11... | collective-permute-start | bytes 1572872 | tf_op jit(solution)/shard_map/ppermute | solution.py:210
  151.8 2.0 %copy-start.9 = (f32[2,256,2,256]{3,2,1,0:T(2,128)S(1)}, f32[2,256,2,256]{3,2,1,0:T(2,128)}, u32[]{:S(2)}) copy-start(f32[2,256,2,256]{3,2,1,0:T(2,128)} %param.10) | copy-start | bytes 3145732

commit v2 on v1

v2 whole, which is shorter than its diff:
```python
import math

import jax
import jax.numpy as jnp
import numpy as np
from jax import lax
from jax.experimental import pallas as pl
from jax.experimental.pallas import tpu as pltpu
from jax.sharding import PartitionSpec as P

GRID_ROWS = 4


fresnel_coeff = 0.25
object_rate = 0.05
probe_rate = 0.15

f32 = jnp.float32
bf16 = jnp.bfloat16


def from_behind(block, axis, distance):
    size = lax.axis_size(axis)
    return lax.ppermute(block, axis, [((i - distance) % size, i) for i in range(size)])


def real_embed(part_re, part_im):
    upper_half = np.concatenate([part_re, -part_im], axis=1)
    lower_half = np.concatenate([part_im, part_re], axis=1)
    stacked = np.concatenate([upper_half, lower_half], axis=0)
    return jnp.asarray(stacked, dtype=f32).astype(bf16)


def build_tables(pixels):
    indices = np.arange(pixels)
    angles = indices[:, None] * indices[None, :] % pixels * (2.0 * math.pi / pixels)
    norm_scale = 1.0 / math.sqrt(pixels)
    dft_re = np.cos(angles) * norm_scale
    dft_im = -np.sin(angles) * norm_scale
    frequency = np.where(indices < pixels // 2, indices, indices - pixels)
    phases = -2.0 * math.pi * fresnel_coeff / pixels * (frequency * frequency)
    phase_sum = phases[:, None] + angles
    kern_re = np.sum(np.cos(phase_sum), axis=0) / pixels
    kern_im = np.sum(np.sin(phase_sum), axis=0) / pixels
    lag_index = (indices[:, None] - indices[None, :]) % pixels
    prop_re = kern_re[lag_index]
    prop_im = kern_im[lag_index]
    return (
        real_embed(prop_re, prop_im),
        real_embed(prop_re, -prop_im),
        real_embed(dft_re, dft_im),
        real_embed(dft_re, -dft_im),
    )


def dot(a, b):
    return jnp.dot(a, b, preferred_element_type=f32)


def shift_tables(row, col, n):
    i_out = lax.broadcasted_iota(jnp.int32, (n, 2 * n), 0)
    i_in = lax.broadcasted_iota(jnp.int32, (n, 2 * n), 1)
    j_in = lax.broadcasted_iota(jnp.int32, (2 * n, n), 0)
    j_out = lax.broadcasted_iota(jnp.int32, (2 * n, n), 1)
    rows = (i_in == i_out + row).astype(f32).astype(bf16)
    cols = (j_in == j_out + col).astype(f32).astype(bf16)
    rows_t = (j_in == j_out + row).astype(f32).astype(bf16)
    cols_t = (i_in == i_out + col).astype(f32).astype(bf16)
    return rows, cols, rows_t, cols_t


def patch(shifts, own_ref, right_ref, below_ref, diag_ref, part):
    upper = jnp.concatenate([own_ref[part], right_ref[part]], axis=1)
    lower = jnp.concatenate([below_ref[part], diag_ref[part]], axis=1)
    rows = dot(shifts[0], jnp.concatenate([upper, lower], axis=0)).astype(bf16)
    return dot(rows, shifts[1])


def transform(left_ref, right_ref, wave_re, wave_im):
    n = wave_re.shape[0]
    wave = jnp.concatenate([wave_re.astype(bf16), wave_im.astype(bf16)], axis=0)
    first = dot(left_ref[...], wave).astype(bf16)
    first = jnp.concatenate([first[:n], first[n:]], axis=1)
    out = dot(first, right_ref[...])
    return out[:, :n], out[:, n:]


def arrive_kernel(
    spot_ref, spot_above_ref, own_ref, right_ref, below_ref, diag_ref, probe_ref, prop_ref,
    prop_c_ref, near_ref, arrive_ref, split_ref,
):
    n = own_ref.shape[1]
    lanes = lax.broadcasted_iota(jnp.int32, split_ref.shape, 1)
    split_ref[...] = (lanes < spot_above_ref[1]).astype(f32)
    shifts = shift_tables(spot_ref[0], spot_ref[1], n)
    tiles = (own_ref, right_ref, below_ref, diag_ref)
    near = [patch(shifts, *tiles, part) for part in range(2)]
    for part in range(2):
        near_ref[part] = near[part].astype(bf16)
    for mode in range(probe_ref.shape[2] // n):
        lanes = pl.ds(mode * n, n)
        p_re, p_im = probe_ref[0, :, lanes], probe_ref[1, :, lanes]
        a_re, a_im = transform(
            prop_ref, prop_c_ref, p_re * near[0] - p_im * near[1], p_re * near[1] + p_im * near[0]
        )
        arrive_ref[0, :, lanes] = a_re
        arrive_ref[1, :, lanes] = a_im


def gradient_kernel(
    spot_ref, own_ref, right_ref, below_ref, diag_ref, near_ref, arrive_ref, probe_ref,
    pattern_ref, prop_ref, prop_c_ref, dft_ref, dft_c_ref,
    home0_ref, next0_ref, down0_ref, home1_ref, next1_ref, down1_ref, term_ref,
):
    n = own_ref.shape[1]
    modes = probe_ref.shape[2] // n
    shifts = shift_tables(spot_ref[0], spot_ref[1], n)
    wrap_cols = shifts[3][:, :n] + shifts[3][:, n:]

    def spread(home_ref, next_ref, down_ref, part, grad):
        rows = dot(shifts[2], grad.astype(bf16)).astype(bf16)
        wide = dot(rows[:n], shifts[3]).astype(bf16)
        home_ref[part] = wide[:, :n]
        next_ref[part] = wide[:, n:]
        down_ref[part] = dot(rows[n:], wrap_cols).astype(bf16)

    tiles = (own_ref, right_ref, below_ref, diag_ref)
    far = [patch(shifts, *tiles, part) for part in range(2)]
    fields = []
    for mode in range(modes):
        lanes = pl.ds(mode * n, n)
        a_re, a_im = arrive_ref[0, :, lanes], arrive_ref[1, :, lanes]
        fields.append(
            transform(
                dft_ref, dft_c_ref, far[0] * a_re - far[1] * a_im, far[0] * a_im + far[1] * a_re
            )
        )
    intensity = sum(f_re * f_re + f_im * f_im for f_re, f_im in fields)
    residual = intensity - pattern_ref[...].astype(f32)
    grad_far = [0.0, 0.0]
    waves = []
    for mode in range(modes):
        lanes = pl.ds(mode * n, n)
        f_re, f_im = fields[mode]
        a_re, a_im = arrive_ref[0, :, lanes], arrive_ref[1, :, lanes]
        b_re, b_im = transform(dft_c_ref, dft_ref, f_re * residual, f_im * residual)
        grad_far[0] += a_re * b_re + a_im * b_im
        grad_far[1] += a_re * b_im - a_im * b_re
        waves.append((far[0] * b_re + far[1] * b_im, far[0] * b_im - far[1] * b_re))
    grad_near = [0.0, 0.0]
    near = [near_ref[part].astype(f32) for part in range(2)]
    for mode in range(modes):
        lanes = pl.ds(mode * n, n)
        b_re, b_im = transform(prop_c_ref, prop_ref, *waves[mode])
        p_re, p_im = probe_ref[0, :, lanes], probe_ref[1, :, lanes]
        grad_near[0] += p_re * b_re + p_im * b_im
        grad_near[1] += p_re * b_im - p_im * b_re
        term_ref[0, :, lanes] = (near[0] * b_re + near[1] * b_im).astype(bf16)
        term_ref[1, :, lanes] = (near[0] * b_im - near[1] * b_re).astype(bf16)
    for part in range(2):
        spread(home1_ref, next1_ref, down1_ref, part, grad_far[part])
        spread(home0_ref, next0_ref, down0_ref, part, grad_near[part])


def call_kernel(kernel, outs, flops, spots, *arrays):
    vmem = pl.BlockSpec(memory_space=pltpu.VMEM)
    smem = pl.BlockSpec(memory_space=pltpu.SMEM)
    return pl.pallas_call(
        kernel,
        out_shape=outs,
        in_specs=[smem] * len(spots) + [vmem] * len(arrays),
        out_specs=(vmem,) * len(outs),
        compiler_params=pltpu.CompilerParams(vmem_limit_bytes=16 * 2**20),
        cost_estimate=pl.CostEstimate(flops=flops, bytes_accessed=6_000_000, transcendentals=0),
    )(*spots, *arrays)


def pick_position(patterns, offsets, counts):
    owners = lax.axis_size("pos")
    if owners == 2:
        swap = [(0, 1), (1, 0)]
        other_spot = lax.ppermute(offsets[1], "pos", swap)
        other_pattern = lax.ppermute(patterns[1], "pos", swap)
        busy = counts == 2
        return jnp.where(busy, offsets[0], other_spot), jnp.where(busy, patterns[0], other_pattern)
    all_counts = lax.all_gather(counts, "pos")
    ends = jnp.cumsum(all_counts)
    rank = lax.axis_index("pos")
    source = jnp.sum((ends <= rank).astype(jnp.int32))
    slot = rank - (ends[source] - all_counts[source])
    all_offsets = lax.all_gather(offsets, "pos")
    all_patterns = lax.all_gather(patterns, "pos")
    return all_offsets[source, slot], all_patterns[source, slot]


def block_sum_kernel(blocks_ref, out_ref):
    total = blocks_ref[0].astype(f32)
    for block in range(1, blocks_ref.shape[0]):
        total += blocks_ref[block].astype(f32)
    total = total.astype(bf16)
    for copy in range(out_ref.shape[0]):
        out_ref[copy] = total


def block_sum(blocks, copies):
    vmem = pl.BlockSpec(memory_space=pltpu.VMEM)
    return pl.pallas_call(
        block_sum_kernel,
        out_shape=jax.ShapeDtypeStruct((copies,) + blocks.shape[1:], bf16),
        in_specs=[vmem],
        out_specs=vmem,
        compiler_params=pltpu.CompilerParams(vmem_limit_bytes=4 * 2**20),
        cost_estimate=pl.CostEstimate(
            flops=blocks.size, bytes_accessed=4 * blocks.size, transcendentals=0
        ),
    )(blocks)


def probe_sum(term):
    tiles, owners = lax.axis_size("tile"), lax.axis_size("pos")
    members = tiles // GRID_ROWS * owners
    same_row = [[row * members + i for i in range(members)] for row in range(GRID_ROWS)]
    same_place = [[row * members + i for row in range(GRID_ROWS)] for i in range(members)]
    blocks = term.reshape(members, term.size // term.shape[-1] // members, term.shape[-1])

    def exchange(x, groups):
        return lax.all_to_all(
            x, ("tile", "pos"), 0, 0, axis_index_groups=groups, tiled=True
        )

    blocks = block_sum(exchange(blocks, same_row), GRID_ROWS)
    blocks = block_sum(exchange(blocks, same_place), members)
    return exchange(blocks, same_row).reshape(term.shape)


def shards(tile_object, probe_modes, patterns, offsets, counts):
    pixels = probe_modes.shape[1]
    prop, prop_c, dft, dft_c = build_tables(pixels)
    own = [tile_object[0, 0], tile_object[0, 1]]
    grid_cols = lax.axis_size("tile") // GRID_ROWS
    below = [from_behind(own[s], "tile", -grid_cols) for s in range(2)]
    right = [from_behind(own[s], "tile", -1) for s in range(2)]
    spot, pattern = pick_position(patterns[0, 0], offsets[0, 0], counts[0, 0])
    spot_above = from_behind(spot, "tile", grid_cols)
    diag = [from_behind(below[s], "tile", -1) for s in range(2)]
    probe = probe_modes.reshape(2, pixels, -1)
    tile = jax.ShapeDtypeStruct(own[0].shape, bf16)
    near, arrive, split = call_kernel(
        arrive_kernel,
        (tile, jax.ShapeDtypeStruct(probe.shape, f32), jax.ShapeDtypeStruct((1, pixels), f32)),
        1_500_000_000,
        (spot, spot_above), own[0], right[0], below[0], diag[0], probe, prop, prop_c,
    )
    home0, next0, down0, home1, next1, down1, term = call_kernel(
        gradient_kernel,
        (tile,) * 6 + (jax.ShapeDtypeStruct(probe.shape, bf16),),
        4_000_000_000,
        (spot,), own[1], right[1], below[1], diag[1], near, arrive, probe, pattern,
        prop, prop_c, dft, dft_c,
    )
    total = probe_sum(term)
    split = split[0] > 0
    zero = jnp.zeros((), bf16)
    new_slices = []
    for s, (home, beside, down) in enumerate(((home0, next0, down0), (home1, next1, down1))):
        from_above = from_behind(down, "tile", grid_cols)
        beside = beside + jnp.where(split, from_above, zero)
        from_left = from_behind(beside, "tile", 1)
        kept = home.astype(f32) + jnp.where(split, zero, from_above).astype(f32)
        part = lax.optimization_barrier((kept + from_left.astype(f32)).astype(bf16))
        if lax.axis_size("pos") == 2:
            other = lax.ppermute(part, "pos", [(0, 1), (1, 0)])
            tile_grad = part.astype(f32) + other.astype(f32)
        else:
            tile_grad = lax.psum(part.astype(f32), "pos")
        new_slices.append((own[s].astype(f32) - object_rate * tile_grad).astype(bf16))
    new_object = jnp.stack(new_slices)[None]
    positions_all = lax.axis_size("tile") * lax.axis_size("pos") * (patterns.shape[2] // 2)
    step = probe_rate / math.sqrt(positions_all)
    new_probe = probe_modes - step * total.astype(f32).reshape(probe_modes.shape)
    return (new_object, new_probe)


def solution(mesh):
    placed = (
        P("tile", None, None, None, None),
        P(),
        P("tile", "pos", None, None, None),
        P("tile", "pos", None, None),
        P("tile", "pos"),
    )
    return jax.shard_map(
        shards,
        mesh=mesh,
        in_specs=placed,
        out_specs=(P("tile", None, None, None, None), P()),
        check_vma=False,
    )
```

time: 158 us -> 86.9 us (0.55)
  blocking collectives: 69.3 us -> 0 us
  starting transfers between devices: 26.3 us -> 35.8 us
  local copies, waits for them, and re-layouts: 14.1 us -> 5.53 us
  other arithmetic: 5.7 us -> 3.05 us
    all_gather x1 -> x0, blocking collectives: 69.3 us -> none  [probe_sum(): lax.all_gather(total, ('tile', 'pos'), tiled=True).reshape(term.shape)]
    all_to_all x1 -> x3, starting transfers between devices: 6.37 us -> 17.8 us  [exchange(): lax.all_to_all(x, ('tile', 'pos'), 0, 0, axis_index_groups=groups, tiled=...]
    ppermute x7 -> x13, waiting for transfers between devices: 21 us -> 13 us  [the longest x11 12.7 us: from_behind(): lax.ppermute(block, axis, [((i - distance) % size, i) for i in range(size)])]
    all_to_all x1 -> x3, waiting for transfers between devices: 9.28 us -> 16.7 us  [exchange(): lax.all_to_all(x, ('tile', 'pos'), 0, 0, axis_index_groups=groups, tiled=...]
    unnamed x24 -> x20, local copies, waits for them, and re-layouts: 7.85 us -> 1.61 us
    pallas_call x1 -> x4, Pallas kernels: 8.3 us -> 9.15 us  [the longest x2 7.54 us: call_kernel(): pl.pallas_call(kernel, out_shape=outs, in_specs=[smem] * len(spots) + [vm...]
    ppermute x7 -> x13, starting transfers between devices: 15.2 us -> 15.8 us  [the longest x11 13.7 us: from_behind(): lax.ppermute(block, axis, [((i - distance) % size, i) for i in range(size)])]
  transfers between devices with their start and end apart: 10 -> 18, of which waited for: 5 -> 9; matrix products, arithmetic and copies ran while one was open for 6% -> 4% of each run, Pallas kernels for 0% -> 4%
where the time goes in v2:
time: 86.9 us; the launch traced here: 86.4 us
  starting transfers between devices  35.8 us (41%)
  waiting for transfers between devices  31.4 us (36%)
  Pallas kernels  9.15 us (11%)
  local copies, waits for them, and re-layouts  5.53 us (6%)
  other arithmetic  3.05 us (4%)
  between operations  1.51 us (2%)
    all_to_all x3, starting transfers between devices, exchange(): lax.all_to_all(x, ('tile', 'pos'), 0, 0, axis_index_groups=groups, tiled=...  17.8 us
    all_to_all x3, waiting for transfers between devices, exchange(): lax.all_to_all(x, ('tile', 'pos'), 0, 0, axis_index_groups=groups, tiled=...  16.7 us
    ppermute x11, starting transfers between devices, from_behind(): lax.ppermute(block, axis, [((i - distance) % size, i) for i in range(size)])  13.7 us
    ppermute x11, waiting for transfers between devices, from_behind(): lax.ppermute(block, axis, [((i - distance) % size, i) for i in range(size)])  12.7 us
    pallas_call x2, Pallas kernels, call_kernel(): pl.pallas_call(kernel, out_shape=outs, in_specs=[smem] * len(spots) + [vm...  7.54 us
    reshape x1, local copies, waits for them, and re-layouts, shards(): probe = probe_modes.reshape(2, pixels, -1)  2.12 us
    ppermute x2, starting transfers between devices, shards(): other = lax.ppermute(part, 'pos', [(0, 1), (1, 0)])  2.09 us
  transfers between devices with their start and end apart: 18, of which 9 were waited for; matrix products, arithmetic and copies ran while one was open for 4% of the time, Pallas kernels for 4%

profile of v2, /device:TPU:0, one launch (start us, length us, event | category | flops | bytes accessed | tf_op | source)
XLA Modules:
  0.0 86.4 jit_solution(5348198719910503364)
XLA Ops:
  0.6 1.1 %slice_bitcast_fusion.1 = (bf16[2,256,256]{2,1,0:T(8,128)(2,1)S(1)}, bf16[2,256,256]{2,1,0:T(8,128)(2,1)S(1)}) fusion(bf16[1,2,2,256,256]{4,3,2,1,0:T(8,128)(2,1)} %param.9), kind=kLoop, calls=%fused_computation.11 | loop fusion | bytes 1048576 | tf_op jit(solution)/shard_map/squeeze | solution.py:239
  1.8 0.0 copy-start.9
  1.8 5.1 %collective-permute-start.6 = (bf16[2,256,256]{2,1,0:T(8,128)(2,1)S(1)}, bf16[2,256,256]{2,1,0:T(8,128)(2,1)S(1)}, u32[]{:S(2)}, u32[]{:S(2)}) collective-permute-start(bf16[2,256,256]{2,1,0:T(8,128)(2,1)S(1)} %get-tuple-element.24.own_ref), channel_id=1, source_target_pairs={{8,0},{10,2},{12,4},{14,6},{16,8},{18,10},{20,12},{22,14},{24,16},... | collective-permute-start | bytes 786440 | tf_op jit(solution)/shard_map/ppermute | solution.py:24
  6.9 0.5 collective-permute-start.5
  7.4 0.4 collective-permute-start.2
  7.9 0.7 collective-permute-start.1
  8.5 1.5 %collective-permute-start = (s32[2]{0:T(128)S(1)}, s32[2]{0:T(128)S(1)}, u32[]{:S(2)}, u32[]{:S(2)}) collective-permute-start(s32[2]{0:T(128)S(1)} %slice_bitcast_fusion.3), channel_id=1, source_target_pairs={{0,1},{1,0},{2,3},{3,2},{4,5},{5,4},{6,7},{7,6},{8,9},{9,8},{10,11... | collective-permute-start | bytes 32 | tf_op jit(solution)/shard_map/ppermute | solution.py:182
  10.7 0.0 copy-start
  10.7 2.1 %reshape.28.probe_ref = f32[2,256,512]{2,1,0:T(8,128)S(1)} reshape(f32[2,256,2,256]{3,2,1,0:T(2,128)} %param.10) | data formatting | bytes 2097152 | tf_op jit(solution)/shard_map/reshape | solution.py:246
  12.9 0.0 collective-permute-done
  12.9 0.7 collective-permute-start.8
  13.6 0.0 collective-permute-done.6.below_ref
  13.6 2.6 %collective-permute-start.7 = (bf16[2,256,256]{2,1,0:T(8,128)(2,1)S(1)}, bf16[2,256,256]{2,1,0:T(8,128)(2,1)S(1)}, u32[]{:S(2)}, u32[]{:S(2)}) collective-permute-start(bf16[2,256,256]{2,1,0:T(8,128)(2,1)S(1)} %collective-permute-done.6.below_ref), channel_id=1, source_target_pairs={{2,0},{4,2},{6,4},{8,6},{10,8},{12,10},{14,12},{16,14},{18,16},{20... | collective-permute-start | bytes 786440 | tf_op jit(solution)/shard_map/ppermute | solution.py:24
  16.2 1.7 %collective-permute-done.8 = bf16[256,256]{1,0:T(8,128)(2,1)S(1)} collective-permute-done((bf16[256,256]{1,0:T(8,128)(2,1)S(1)}, bf16[256,256]{1,0:T(8,128)(2,1)S(1)}, u32[]{:S(2)}, u32[]{:S(2)}) %collective-permute-start.8) | collective-permute-done | bytes 131104 | tf_op jit(solution)/shard_map/ppermute | solution.py:183
  17.9 1.6 %collective-permute-start.4 = (s32[2]{0:T(128)S(1)}, s32[2]{0:T(128)S(1)}, u32[]{:S(2)}, u32[]{:S(2)}) collective-permute-start(s32[2]{0:T(128)S(1)} %broadcast_select_fusion.spot_ref), channel_id=1, source_target_pairs={{24,0},{26,2},{28,4},{30,6},{0,8},{2,10},{4,12},{6,14},{8,16},{10,... | collective-permute-start | bytes 32 | tf_op jit(solution)/shard_map/ppermute | solution.py:24
  19.5 1.4 %collective-permute-done.2.below_ref = bf16[2,256,256]{2,1,0:T(8,128)(2,1)S(1)} collective-permute-done((bf16[2,256,256]{2,1,0:T(8,128)(2,1)S(1)}, bf16[2,256,256]{2,1,0:T(8,128)(2,1)S(1)}, u32[]{:S(2)}, u32[]{:S(2)}) %collective-permute-start.2) | collective-permute-done | bytes 262176 | tf_op jit(solution)/shard_map/ppermute | solution.py:24
  20.9 1.0 %collective-permute-start.3 = (bf16[2,256,256]{2,1,0:T(8,128)(2,1)S(1)}, bf16[2,256,256]{2,1,0:T(8,128)(2,1)S(1)}, u32[]{:S(2)}, u32[]{:S(2)}) collective-permute-start(bf16[2,256,256]{2,1,0:T(8,128)(2,1)S(1)} %collective-permute-done.2.below_ref), channel_id=1, source_target_pairs={{2,0},{4,2},{6,4},{8,6},{10,8},{12,10},{14,12},{16,14},{18,16},{20... | collective-permute-start | bytes 786440 | tf_op jit(solution)/shard_map/ppermute | solution.py:24
  21.9 5.5 %collective-permute-done.4.spot_above_ref = s32[2]{0:T(128)S(1)} collective-permute-done((s32[2]{0:T(128)S(1)}, s32[2]{0:T(128)S(1)}, u32[]{:S(2)}, u32[]{:S(2)}) %collective-permute-start.4) | collective-permute-done | bytes 40 | tf_op jit(solution)/shard_map/ppermute | solution.py:24
  27.4 0.0 copy-start.2
  27.4 1.0 %copy-done.2 = bf16[512,512]{1,0:T(8,128)(2,1)S(1)} copy-done((bf16[512,512]{1,0:T(8,128)(2,1)S(1)}, bf16[512,512]{1,0:T(8,128)(2,1)}, u32[]{:S(2)}) %copy-start.2) | copy-done | bytes 524312
  28.4 2.2 %shard_map.104 = (bf16[2,256,256]{2,1,0:T(8,128)(2,1)S(1)}, f32[2,256,512]{2,1,0:T(8,128)S(1)}, f32[1,256]{1,0:T(1,128)S(1)}) custom-call(s32[2]{0:T(128)S(1)} %broadcast_select_fusion.spot_ref, s32[2]{0:T(128)S(1)} %collective-permute-done.4.spot_above_ref, bf16[2,256,256]{2,1,0:T(8,128)(2,1)S(1)} %get-tuple-element.24.own_ref, ...), custom_call_target="tpu_custom_call" | custom-call | flops 1500000000 | bytes 6000000 | tf_op jit(solution)/shard_map/pallas_call | solution.py:168
  30.7 5.3 %shard_map.105 = (bf16[2,256,256]{2,1,0:T(8,128)(2,1)S(1)}, bf16[2,256,256]{2,1,0:T(8,128)(2,1)S(1)}, bf16[2,256,256]{2,1,0:T(8,128)(2,1)S(1)}, bf16[2,256,256]{...) custom-call(s32[2]{0:T(128)S(1)} %broadcast_select_fusion.spot_ref, ...), custom_call_target="tpu_custom_call" | custom-call | flops 4000000000 | bytes 6000000 | tf_op jit(solution)/shard_map/pallas_call | solution.py:168
  36.0 1.6 %collective-permute-start.9 = (bf16[2,256,256]{2,1,0:T(8,128)(2,1)S(1)}, bf16[2,256,256]{2,1,0:T(8,128)(2,1)S(1)}, u32[]{:S(2)}, u32[]{:S(2)}) collective-permute-start(bf16[2,256,256]{2,1,0:T(8,128)(2,1)S(1)} %get-tuple-element.16), channel_id=1, source_target_pairs={{24,0},{26,2},{28,4},{30,6},{0,8},{2,10},{4,12},{6,14},{8,16},{10,... | collective-permute-start | bytes 786440 | tf_op jit(solution)/shard_map/ppermute | solution.py:24
  37.7 0.1 collective-permute-start.12
  37.7 3.5 %all-to-all-start = ((bf16[8,64,512]{2,1,0:T(8,128)(2,1)}), bf16[8,64,512]{2,1,0:T(8,128)(2,1)S(1)}, u32[]{:S(2)}, u32[]{:S(2)}) async-start(bf16[8,64,512]{2,1,0:T(8,128)(2,1)} %bitcast.10), calls=%async_computation | async-start | bytes 1048576 | tf_op jit(solution)/shard_map/all_to_all | solution.py:227
  41.3 3.0 %collective-permute-done.9 = bf16[2,256,256]{2,1,0:T(8,128)(2,1)S(1)} collective-permute-done((bf16[2,256,256]{2,1,0:T(8,128)(2,1)S(1)}, bf16[2,256,256]{2,1,0:T(8,128)(2,1)S(1)}, u32[]{:S(2)}, u32[]{:S(2)}) %collective-permute-start.9) | collective-permute-done | bytes 262176 | tf_op jit(solution)/shard_map/ppermute | solution.py:24
  44.3 2.8 %collective-permute-done.12 = bf16[2,256,256]{2,1,0:T(8,128)(2,1)S(1)} collective-permute-done((bf16[2,256,256]{2,1,0:T(8,128)(2,1)S(1)}, bf16[2,256,256]{2,1,0:T(8,128)(2,1)S(1)}, u32[]{:S(2)}, u32[]{:S(2)}) %collective-permute-start.12) | collective-permute-done | bytes 262176 | tf_op jit(solution)/shard_map/ppermute | solution.py:24
  47.1 0.1 select_add_fusion.1
  47.1 0.1 collective-permute-start.10
  47.2 0.1 collective-permute-start.13
  47.3 2.7 %all-to-all-done.blocks_ref = bf16[8,64,512]{2,1,0:T(8,128)(2,1)S(1)} async-done(((bf16[8,64,512]{2,1,0:T(8,128)(2,1)}), bf16[8,64,512]{2,1,0:T(8,128)(2,1)S(1)}, u32[]{:S(2)}, u32[]{:S(2)}) %all-to-all-start) | async-done | bytes 524320 | tf_op jit(solution)/shard_map/all_to_all | solution.py:227
  50.0 0.8 shard_map.106
  50.8 10.6 %all-to-all-start.1 = ((bf16[4,64,512]{2,1,0:T(8,128)(2,1)}), bf16[4,64,512]{2,1,0:T(8,128)(2,1)S(1)}, u32[]{:S(2)}, u32[]{:S(2)}) async-start(bf16[4,64,512]{2,1,0:T(8,128)(2,1)} %shard_map.106), calls=%async_computation.1 | async-start | bytes 524288 | tf_op jit(solution)/shard_map/all_to_all | solution.py:227
  61.4 0.2 add_convert_fusion.1
  61.7 1.5 %collective-permute-start.14 = (bf16[2,256,256]{2,1,0:T(8,128)(2,1)S(1)}, bf16[2,256,256]{2,1,0:T(8,128)(2,1)S(1)}, u32[]{:S(2)}, u32[]{:S(2)}) collective-permute-start(bf16[2,256,256]{2,1,0:T(8,128)(2,1)S(1)} %get-tuple-element.27), channel_id=1, source_target_pairs={{0,1},{1,0},{2,3},{3,2},{4,5},{5,4},{6,7},{7,6},{8,9},{9,8},{10,11... | collective-permute-start | bytes 786440 | tf_op jit(solution)/shard_map/ppermute | solution.py:272
  63.2 0.6 collective-permute-start.11
  63.8 6.5 %all-to-all-done.1.blocks_ref = bf16[4,64,512]{2,1,0:T(8,128)(2,1)S(1)} async-done(((bf16[4,64,512]{2,1,0:T(8,128)(2,1)}), bf16[4,64,512]{2,1,0:T(8,128)(2,1)S(1)}, u32[]{:S(2)}, u32[]{:S(2)}) %all-to-all-start.1) | async-done | bytes 262176 | tf_op jit(solution)/shard_map/all_to_all | solution.py:227
  70.3 0.8 shard_map.107
  71.1 3.6 %all-to-all-start.2 = ((bf16[8,64,512]{2,1,0:T(8,128)(2,1)}), bf16[8,64,512]{2,1,0:T(8,128)(2,1)S(1)}, u32[]{:S(2)}, u32[]{:S(2)}) async-start(bf16[8,64,512]{2,1,0:T(8,128)(2,1)} %shard_map.107), calls=%async_computation.2 | async-start | bytes 1048576 | tf_op jit(solution)/shard_map/all_to_all | solution.py:227
  74.8 0.3 collective-permute-done.11
  75.1 0.2 fusion
  75.3 0.8 maximum_bitcast_fusion
  76.2 7.4 %all-to-all-done.2 = bf16[8,64,512]{2,1,0:T(8,128)(2,1)S(1)} async-done(((bf16[8,64,512]{2,1,0:T(8,128)(2,1)}), bf16[8,64,512]{2,1,0:T(8,128)(2,1)S(1)}, u32[]{:S(2)}, u32[]{:S(2)}) %all-to-all-start.2) | async-done | bytes 524320 | tf_op jit(solution)/shard_map/all_to_all | solution.py:227
  83.5 0.1 convert_multiply_fusion
  83.7 0.0 copy-start.6
  83.7 0.7 mul.19
  84.4 0.5 copy-done.6
  84.9 1.5 %sub.11 = f32[2,256,2,256]{3,2,1,0:T(2,128)} subtract(f32[2,256,2,256]{3,2,1,0:T(2,128)S(1)} %copy-done.6, f32[2,256,2,256]{3,2,1,0:T(2,128)S(1)} %mul.19) | non-fusion elementwise | flops 262144 | bytes 3145728 | tf_op jit(solution)/shard_map/sub | solution.py:280
  (26 shorter events, 0.1 us)
Async XLA Ops:
  0.6 9.4 %copy-start.8 = (bf16[1,1,2,256,256]{4,3,2,1,0:T(8,128)(2,1)S(1)}, bf16[1,1,2,256,256]{4,3,2,1,0:T(8,128)(2,1)}, u32[]{:S(2)}) copy-start(bf16[1,1,2,256,256]{4,3,2,1,0:T(8,128)(2,1)} %param.11) | copy-start | bytes 786436
  1.8 6.8 %copy-start.9 = (s32[1,1,2,2]{3,2,1,0:T(2,128)S(1)}, s32[1,1,2,2]{3,2,1,0:T(2,128)}, u32[]{:S(2)}) copy-start(s32[1,1,2,2]{3,2,1,0:T(2,128)} %param.12) | copy-start | bytes 52
  1.8 11.8 %collective-permute-start.6 = (bf16[2,256,256]{2,1,0:T(8,128)(2,1)S(1)}, bf16[2,256,256]{2,1,0:T(8,128)(2,1)S(1)}, u32[]{:S(2)}, u32[]{:S(2)}) collective-permute-start(bf16[2,256,256]{2,1,0:T(8,128)(2,1)S(1)} %get-tuple-element.24.own_ref), channel_id=1, source_target_pairs={{8,0},{10,2},{12,4},{14,6},{16,8},{18,10},{20,12},{22,14},{24,16},... | collective-permute-start | bytes 786440 | tf_op jit(solution)/shard_map/ppermute | solution.py:24
  6.9 20.5 %collective-permute-start.5 = (bf16[2,256,256]{2,1,0:T(8,128)(2,1)S(1)}, bf16[2,256,256]{2,1,0:T(8,128)(2,1)S(1)}, u32[]{:S(2)}, u32[]{:S(2)}) collective-permute-start(bf16[2,256,256]{2,1,0:T(8,128)(2,1)S(1)} %get-tuple-element.24.own_ref), channel_id=1, source_target_pairs={{2,0},{4,2},{6,4},{8,6},{10,8},{12,10},{14,12},{16,14},{18,16},{20... | collective-permute-start | bytes 786440 | tf_op jit(solution)/shard_map/ppermute | solution.py:24
  7.4 13.5 %collective-permute-start.2 = (bf16[2,256,256]{2,1,0:T(8,128)(2,1)S(1)}, bf16[2,256,256]{2,1,0:T(8,128)(2,1)S(1)}, u32[]{:S(2)}, u32[]{:S(2)}) collective-permute-start(bf16[2,256,256]{2,1,0:T(8,128)(2,1)S(1)} %get-tuple-element.25.own_ref), channel_id=1, source_target_pairs={{8,0},{10,2},{12,4},{14,6},{16,8},{18,10},{20,12},{22,14},{24,16},... | collective-permute-start | bytes 786440 | tf_op jit(solution)/shard_map/ppermute | solution.py:24
  7.9 22.8 %collective-permute-start.1 = (bf16[2,256,256]{2,1,0:T(8,128)(2,1)S(1)}, bf16[2,256,256]{2,1,0:T(8,128)(2,1)S(1)}, u32[]{:S(2)}, u32[]{:S(2)}) collective-permute-start(bf16[2,256,256]{2,1,0:T(8,128)(2,1)S(1)} %get-tuple-element.25.own_ref), channel_id=1, source_target_pairs={{2,0},{4,2},{6,4},{8,6},{10,8},{12,10},{14,12},{16,14},{18,16},{20... | collective-permute-start | bytes 786440 | tf_op jit(solution)/shard_map/ppermute | solution.py:24
  8.5 4.3 %collective-permute-start = (s32[2]{0:T(128)S(1)}, s32[2]{0:T(128)S(1)}, u32[]{:S(2)}, u32[]{:S(2)}) collective-permute-start(s32[2]{0:T(128)S(1)} %slice_bitcast_fusion.3), channel_id=1, source_target_pairs={{0,1},{1,0},{2,3},{3,2},{4,5},{5,4},{6,7},{7,6},{8,9},{9,8},{10,11... | collective-permute-start | bytes 32 | tf_op jit(solution)/shard_map/ppermute | solution.py:182
  10.7 16.7 %copy-start = (bf16[512,512]{1,0:T(8,128)(2,1)S(1)}, bf16[512,512]{1,0:T(8,128)(2,1)}, u32[]{:S(2)}) copy-start(bf16[512,512]{1,0:T(8,128)(2,1)} %constant.28.prop_c_ref) | copy-start | bytes 1572868
  12.9 5.0 %collective-permute-start.8 = (bf16[256,256]{1,0:T(8,128)(2,1)S(1)}, bf16[256,256]{1,0:T(8,128)(2,1)S(1)}, u32[]{:S(2)}, u32[]{:S(2)}) collective-permute-start(bf16[256,256]{1,0:T(8,128)(2,1)S(1)} %slice_bitcast_fusion.2), channel_id=1, source_target_pairs={{0,1},{1,0},{2,3},{3,2},{4,5},{5,4},{6,7},{7,6},{8,9},{9,8},{10,11... | collective-permute-start | bytes 393224 | tf_op jit(solution)/shard_map/ppermute | solution.py:183
  13.6 13.8 %collective-permute-start.7 = (bf16[2,256,256]{2,1,0:T(8,128)(2,1)S(1)}, bf16[2,256,256]{2,1,0:T(8,128)(2,1)S(1)}, u32[]{:S(2)}, u32[]{:S(2)}) collective-permute-start(bf16[2,256,256]{2,1,0:T(8,128)(2,1)S(1)} %collective-permute-done.6.below_ref), channel_id=1, source_target_pairs={{2,0},{4,2},{6,4},{8,6},{10,8},{12,10},{14,12},{16,14},{18,16},{20... | collective-permute-start | bytes 786440 | tf_op jit(solution)/shard_map/ppermute | solution.py:24
  17.9 9.5 %collective-permute-start.4 = (s32[2]{0:T(128)S(1)}, s32[2]{0:T(128)S(1)}, u32[]{:S(2)}, u32[]{:S(2)}) collective-permute-start(s32[2]{0:T(128)S(1)} %broadcast_select_fusion.spot_ref), channel_id=1, source_target_pairs={{24,0},{26,2},{28,4},{30,6},{0,8},{2,10},{4,12},{6,14},{8,16},{10,... | collective-permute-start | bytes 32 | tf_op jit(solution)/shard_map/ppermute | solution.py:24
  20.9 9.8 %collective-permute-start.3 = (bf16[2,256,256]{2,1,0:T(8,128)(2,1)S(1)}, bf16[2,256,256]{2,1,0:T(8,128)(2,1)S(1)}, u32[]{:S(2)}, u32[]{:S(2)}) collective-permute-start(bf16[2,256,256]{2,1,0:T(8,128)(2,1)S(1)} %collective-permute-done.2.below_ref), channel_id=1, source_target_pairs={{2,0},{4,2},{6,4},{8,6},{10,8},{12,10},{14,12},{16,14},{18,16},{20... | collective-permute-start | bytes 786440 | tf_op jit(solution)/shard_map/ppermute | solution.py:24
  21.8 8.9 %copy-start.1 = (bf16[512,512]{1,0:T(8,128)(2,1)S(1)}, bf16[512,512]{1,0:T(8,128)(2,1)}, u32[]{:S(2)}) copy-start(bf16[512,512]{1,0:T(8,128)(2,1)} %constant.28.prop_c_ref) | copy-start | bytes 1572868
  27.4 1.0 %copy-start.2 = (bf16[512,512]{1,0:T(8,128)(2,1)S(1)}, bf16[512,512]{1,0:T(8,128)(2,1)}, u32[]{:S(2)}) copy-start(bf16[512,512]{1,0:T(8,128)(2,1)} %constant.27.prop_ref) | copy-start | bytes 1572868
  28.4 2.3 %copy-start.3 = (bf16[512,512]{1,0:T(8,128)(2,1)S(1)}, bf16[512,512]{1,0:T(8,128)(2,1)}, u32[]{:S(2)}) copy-start(bf16[512,512]{1,0:T(8,128)(2,1)} %constant.27.prop_ref) | copy-start | bytes 1572868
  28.4 2.3 %copy-start.4 = (bf16[512,512]{1,0:T(8,128)(2,1)S(1)}, bf16[512,512]{1,0:T(8,128)(2,1)}, u32[]{:S(2)}) copy-start(bf16[512,512]{1,0:T(8,128)(2,1)} %constant.30.dft_c_ref) | copy-start | bytes 1572868
  28.4 2.3 %copy-start.5 = (bf16[512,512]{1,0:T(8,128)(2,1)S(1)}, bf16[512,512]{1,0:T(8,128)(2,1)}, u32[]{:S(2)}) copy-start(bf16[512,512]{1,0:T(8,128)(2,1)} %constant.29.dft_ref) | copy-start | bytes 1572868
  36.0 8.2 %collective-permute-start.9 = (bf16[2,256,256]{2,1,0:T(8,128)(2,1)S(1)}, bf16[2,256,256]{2,1,0:T(8,128)(2,1)S(1)}, u32[]{:S(2)}, u32[]{:S(2)}) collective-permute-start(bf16[2,256,256]{2,1,0:T(8,128)(2,1)S(1)} %get-tuple-element.16), channel_id=1, source_target_pairs={{24,0},{26,2},{28,4},{30,6},{0,8},{2,10},{4,12},{6,14},{8,16},{10,... | collective-permute-start | bytes 786440 | tf_op jit(solution)/shard_map/ppermute | solution.py:24
  37.7 9.4 %collective-permute-start.12 = (bf16[2,256,256]{2,1,0:T(8,128)(2,1)S(1)}, bf16[2,256,256]{2,1,0:T(8,128)(2,1)S(1)}, u32[]{:S(2)}, u32[]{:S(2)}) collective-permute-start(bf16[2,256,256]{2,1,0:T(8,128)(2,1)S(1)} %get-tuple-element.19), channel_id=1, source_target_pairs={{24,0},{26,2},{28,4},{30,6},{0,8},{2,10},{4,12},{6,14},{8,16},{10,... | collective-permute-start | bytes 786440 | tf_op jit(solution)/shard_map/ppermute | solution.py:24
  37.7 12.3 %all-to-all-start = ((bf16[8,64,512]{2,1,0:T(8,128)(2,1)}), bf16[8,64,512]{2,1,0:T(8,128)(2,1)S(1)}, u32[]{:S(2)}, u32[]{:S(2)}) async-start(bf16[8,64,512]{2,1,0:T(8,128)(2,1)} %bitcast.10), calls=%async_computation | async-start | bytes 1048576 | tf_op jit(solution)/shard_map/all_to_all | solution.py:227
  47.1 14.3 %collective-permute-start.10 = (bf16[2,256,256]{2,1,0:T(8,128)(2,1)S(1)}, bf16[2,256,256]{2,1,0:T(8,128)(2,1)S(1)}, u32[]{:S(2)}, u32[]{:S(2)}) collective-permute-start(bf16[2,256,256]{2,1,0:T(8,128)(2,1)S(1)} %get-tuple-element.28), channel_id=1, source_target_pairs={{30,0},{0,2},{2,4},{4,6},{6,8},{8,10},{10,12},{12,14},{14,16},{16,... | collective-permute-start | bytes 786440 | tf_op jit(solution)/shard_map/ppermute | solution.py:24
  47.2 14.2 %collective-permute-start.13 = (bf16[2,256,256]{2,1,0:T(8,128)(2,1)S(1)}, bf16[2,256,256]{2,1,0:T(8,128)(2,1)S(1)}, u32[]{:S(2)}, u32[]{:S(2)}) collective-permute-start(bf16[2,256,256]{2,1,0:T(8,128)(2,1)S(1)} %get-tuple-element.29), channel_id=1, source_target_pairs={{30,0},{0,2},{2,4},{4,6},{6,8},{8,10},{10,12},{12,14},{14,16},{16,... | collective-permute-start | bytes 786440 | tf_op jit(solution)/shard_map/ppermute | solution.py:24
  50.8 19.5 %all-to-all-start.1 = ((bf16[4,64,512]{2,1,0:T(8,128)(2,1)}), bf16[4,64,512]{2,1,0:T(8,128)(2,1)S(1)}, u32[]{:S(2)}, u32[]{:S(2)}) async-start(bf16[4,64,512]{2,1,0:T(8,128)(2,1)} %shard_map.106), calls=%async_computation.1 | async-start | bytes 524288 | tf_op jit(solution)/shard_map/all_to_all | solution.py:227
  61.7 13.1 %collective-permute-start.14 = (bf16[2,256,256]{2,1,0:T(8,128)(2,1)S(1)}, bf16[2,256,256]{2,1,0:T(8,128)(2,1)S(1)}, u32[]{:S(2)}, u32[]{:S(2)}) collective-permute-start(bf16[2,256,256]{2,1,0:T(8,128)(2,1)S(1)} %get-tuple-element.27), channel_id=1, source_target_pairs={{0,1},{1,0},{2,3},{3,2},{4,5},{5,4},{6,7},{7,6},{8,9},{9,8},{10,11... | collective-permute-start | bytes 786440 | tf_op jit(solution)/shard_map/ppermute | solution.py:272
  63.2 11.9 %collective-permute-start.11 = (bf16[2,256,256]{2,1,0:T(8,128)(2,1)S(1)}, bf16[2,256,256]{2,1,0:T(8,128)(2,1)S(1)}, u32[]{:S(2)}, u32[]{:S(2)}) collective-permute-start(bf16[2,256,256]{2,1,0:T(8,128)(2,1)S(1)} %get-tuple-element.26), channel_id=1, source_target_pairs={{0,1},{1,0},{2,3},{3,2},{4,5},{5,4},{6,7},{7,6},{8,9},{9,8},{10,11... | collective-permute-start | bytes 786440 | tf_op jit(solution)/shard_map/ppermute | solution.py:272
  71.1 3.9 %copy-start.7 = (bf16[1,2,2,256,256]{4,3,2,1,0:T(8,128)(2,1)S(1)}, bf16[1,2,2,256,256]{4,3,2,1,0:T(8,128)(2,1)}, u32[]{:S(2)}) copy-start(bf16[1,2,2,256,256]{4,3,2,1,0:T(8,128)(2,1)} %param.9) | copy-start | bytes 1572868
  71.1 12.4 %all-to-all-start.2 = ((bf16[8,64,512]{2,1,0:T(8,128)(2,1)}), bf16[8,64,512]{2,1,0:T(8,128)(2,1)S(1)}, u32[]{:S(2)}, u32[]{:S(2)}) async-start(bf16[8,64,512]{2,1,0:T(8,128)(2,1)} %shard_map.107), calls=%async_computation.2 | async-start | bytes 1048576 | tf_op jit(solution)/shard_map/all_to_all | solution.py:227
  83.7 1.2 %copy-start.6 = (f32[2,256,2,256]{3,2,1,0:T(2,128)S(1)}, f32[2,256,2,256]{3,2,1,0:T(2,128)}, u32[]{:S(2)}) copy-start(f32[2,256,2,256]{3,2,1,0:T(2,128)} %param.10) | copy-start | bytes 3145732

commit v3 on v2

v3 whole, which is shorter than its diff:
```python
import math

import jax
import jax.numpy as jnp
import numpy as np
from jax import lax
from jax.experimental import pallas as pl
from jax.experimental.pallas import tpu as pltpu
from jax.sharding import PartitionSpec as P

GRID_ROWS = 4


fresnel_coeff = 0.25
object_rate = 0.05
probe_rate = 0.15

f32 = jnp.float32
bf16 = jnp.bfloat16


def from_behind(block, rows, cols):
    tiles = lax.axis_size("tile")
    across = tiles // GRID_ROWS

    def source(i):
        return (i // across - rows) % GRID_ROWS * across + (i % across - cols) % across

    return lax.ppermute(block, "tile", [(source(i), i) for i in range(tiles)])


def real_embed(part_re, part_im):
    upper_half = np.concatenate([part_re, -part_im], axis=1)
    lower_half = np.concatenate([part_im, part_re], axis=1)
    stacked = np.concatenate([upper_half, lower_half], axis=0)
    return jnp.asarray(stacked, dtype=f32).astype(bf16)


def build_tables(pixels):
    indices = np.arange(pixels)
    angles = indices[:, None] * indices[None, :] % pixels * (2.0 * math.pi / pixels)
    norm_scale = 1.0 / math.sqrt(pixels)
    dft_re = np.cos(angles) * norm_scale
    dft_im = -np.sin(angles) * norm_scale
    frequency = np.where(indices < pixels // 2, indices, indices - pixels)
    phases = -2.0 * math.pi * fresnel_coeff / pixels * (frequency * frequency)
    phase_sum = phases[:, None] + angles
    kern_re = np.sum(np.cos(phase_sum), axis=0) / pixels
    kern_im = np.sum(np.sin(phase_sum), axis=0) / pixels
    lag_index = (indices[:, None] - indices[None, :]) % pixels
    prop_re = kern_re[lag_index]
    prop_im = kern_im[lag_index]
    return real_embed(prop_re, prop_im), real_embed(dft_re, dft_im)


def dot(a, b):
    return jnp.dot(a, b, preferred_element_type=f32)


def shift_tables(offsets_ref, counts_ref, message_ref):
    n = message_ref.shape[1]
    sent = message_ref[n:, :].astype(f32)
    busy = counts_ref[0, 0] == offsets_ref.shape[2]
    row = jnp.where(busy, offsets_ref[0, 0, 0, 0], sent[0:1].astype(jnp.int32))
    col = jnp.where(busy, offsets_ref[0, 0, 0, 1], sent[1:2].astype(jnp.int32))
    i_out = lax.broadcasted_iota(jnp.int32, (n, 2 * n), 0)
    i_in = lax.broadcasted_iota(jnp.int32, (n, 2 * n), 1)
    j_in = lax.broadcasted_iota(jnp.int32, (2 * n, n), 0)
    j_out = lax.broadcasted_iota(jnp.int32, (2 * n, n), 1)
    row2 = jnp.concatenate([row, row], axis=1)
    col2 = jnp.concatenate([col, col], axis=1)
    rows = (i_in == i_out + row2).astype(f32).astype(bf16)
    cols = (j_in == j_out + col).astype(f32).astype(bf16)
    rows_t = (j_in == j_out + row).astype(f32).astype(bf16)
    cols_t = (i_in == i_out + col2).astype(f32).astype(bf16)
    return rows, cols, rows_t, cols_t, col, busy


def patch(shifts, own_ref, right_ref, below_ref, diag_ref, part):
    upper = jnp.concatenate([own_ref[part], right_ref[part]], axis=1)
    lower = jnp.concatenate([below_ref[part], diag_ref[part]], axis=1)
    rows = dot(shifts[0], jnp.concatenate([upper, lower], axis=0)).astype(bf16)
    return dot(rows, shifts[1])


def transform(table_ref, wave_re, wave_im):
    n = wave_re.shape[0]
    table = table_ref[...]
    wave = jnp.concatenate([wave_re.astype(bf16), wave_im.astype(bf16)], axis=0)
    first = dot(table, wave)
    first = jnp.concatenate([first[:n].astype(bf16), (-first[n:]).astype(bf16)], axis=1)
    out = dot(first, table)
    return out[:, :n], out[:, n:]


def probe_plane(probe_ref, part, mode, modes):
    lane_tiles = 2
    n = probe_ref.shape[0] // (2 * lane_tiles * modes)
    step = lane_tiles * modes
    halves = [
        probe_ref[pl.ds(part * n * step + tile * modes + mode, n, stride=step), :]
        for tile in range(lane_tiles)
    ]
    return jnp.concatenate(halves, axis=1)


def cut_kernel(offsets_ref, tile_ref, patterns_ref, *refs):
    slices, message_ref, sems = refs[:-2], refs[-2], refs[-1]
    n = message_ref.shape[1]
    copies = [
        pltpu.make_async_copy(tile_ref.at[0, s], ref, sems.at[s]) for s, ref in enumerate(slices)
    ]
    to_pattern = message_ref.at[pl.ds(0, n), :]
    copies.append(pltpu.make_async_copy(patterns_ref.at[0, 0, 1], to_pattern, sems.at[len(slices)]))
    for copy in copies:
        copy.start()
    at = lax.broadcasted_iota(jnp.int32, (16, n), 0)
    row, col = offsets_ref[0, 0, 1, 0], offsets_ref[0, 0, 1, 1]
    rows = jnp.where(at == 0, row, jnp.where(at == 1, col, 0))
    message_ref[pl.ds(n, 16), :] = rows.astype(f32).astype(bf16)
    for copy in copies:
        copy.wait()


def arrive_kernel(
    offsets_ref, counts_ref, message_ref, own_ref, right_ref, below_ref, diag_ref, probe_ref,
    prop_hbm, near_ref, arrive_ref, prop_ref, sems,
):
    n = own_ref.shape[1]
    modes = arrive_ref.shape[2] // n
    parts = sems.shape[0]
    size = prop_ref.shape[0] // parts
    fetches = []
    for at in range(parts):
        rows = pl.ds(at * size, size)
        copy = pltpu.make_async_copy(prop_hbm.at[rows, :], prop_ref.at[rows, :], sems.at[at])
        copy.start()
        fetches.append(copy)
    shifts = shift_tables(offsets_ref, counts_ref, message_ref)
    tiles = (own_ref, right_ref.at[0], below_ref, diag_ref)
    near = [patch(shifts, *tiles, part) for part in range(2)]
    for part in range(2):
        near_ref[part] = near[part].astype(bf16)
    for copy in fetches:
        copy.wait()
    for mode in range(modes):
        lanes = pl.ds(mode * n, n)
        p_re = probe_plane(probe_ref, 0, mode, modes)
        p_im = probe_plane(probe_ref, 1, mode, modes)
        a_re, a_neg = transform(
            prop_ref, p_re * near[0] - p_im * near[1], p_re * near[1] + p_im * near[0]
        )
        arrive_ref[0, :, lanes] = a_re
        arrive_ref[1, :, lanes] = -a_neg


def gradient_kernel(
    offsets_ref, counts_ref, message_ref, own_ref, right_ref, below_ref, diag_ref,
    near_ref, arrive_ref, probe_ref, patterns_ref, prop_ref, dft_ref,
    home0_ref, next0_ref, down0_ref, home1_ref, next1_ref, down1_ref, keep_ref, give_ref,
    term_ref,
):
    n = own_ref.shape[1]
    modes = arrive_ref.shape[2] // n
    shifts = shift_tables(offsets_ref, counts_ref, message_ref)
    rows_t, cols_t, col, busy = shifts[2:]
    wrap_cols = cols_t[:, :n] + cols_t[:, n:]
    edge = lax.broadcasted_iota(jnp.int32, (16, n), 1) < col
    edge = edge.astype(f32).astype(bf16)

    def spread(home_ref, next_ref, down_ref, grad):
        for part in range(2):
            rows = dot(rows_t, grad[part].astype(bf16)).astype(bf16)
            wide = dot(rows[:n], cols_t).astype(bf16)
            home_ref[part] = wide[:, :n]
            next_ref[part] = wide[:, n:]
            down_ref[pl.ds(part * n, n), :] = dot(rows[n:], wrap_cols).astype(bf16)
        down_ref[pl.ds(2 * n, 16), :] = edge

    tiles = (own_ref, right_ref.at[1], below_ref, diag_ref)
    far = [patch(shifts, *tiles, part) for part in range(2)]
    fields = []
    for mode in range(modes):
        lanes = pl.ds(mode * n, n)
        a_re, a_im = arrive_ref[0, :, lanes], arrive_ref[1, :, lanes]
        fields.append(
            transform(dft_ref, far[0] * a_re - far[1] * a_im, far[0] * a_im + far[1] * a_re)
        )
    intensity = sum(f_re * f_re + f_neg * f_neg for f_re, f_neg in fields)
    pattern = jnp.where(busy, patterns_ref[0, 0, 0].astype(f32), message_ref[:n, :].astype(f32))
    residual = intensity - pattern
    grad_far = [0.0, 0.0]
    waves = []
    for mode in range(modes):
        lanes = pl.ds(mode * n, n)
        f_re, f_neg = fields[mode]
        a_re, a_im = arrive_ref[0, :, lanes], arrive_ref[1, :, lanes]
        b_re, b_im = transform(dft_ref, f_re * residual, f_neg * residual)
        grad_far[0] += a_re * b_re + a_im * b_im
        grad_far[1] += a_re * b_im - a_im * b_re
        waves.append((far[0] * b_re + far[1] * b_im, far[1] * b_re - far[0] * b_im))
    grad_near = [0.0, 0.0]
    near = [near_ref[part].astype(f32) for part in range(2)]
    for mode in range(modes):
        lanes = pl.ds(mode * n, n)
        b_re, b_im = transform(prop_ref, *waves[mode])
        p_re = probe_plane(probe_ref, 0, mode, modes)
        p_im = probe_plane(probe_ref, 1, mode, modes)
        grad_near[0] += p_re * b_re + p_im * b_im
        grad_near[1] += p_re * b_im - p_im * b_re
        term_ref[0, :, lanes] = (near[0] * b_re + near[1] * b_im).astype(bf16)
        term_ref[1, :, lanes] = (near[0] * b_im - near[1] * b_re).astype(bf16)
    core = place_of(core_group())
    keep_ref[...] = term_ref[core]
    give_ref[...] = term_ref[1 - core]
    spread(home1_ref, next1_ref, down1_ref, grad_far)
    spread(home0_ref, next0_ref, down0_ref, grad_near)


def core_group():
    return [lax.axis_size("pos")]


def place_of(group):
    flat = lax.axis_index("tile") * lax.axis_size("pos") + lax.axis_index("pos")
    return sum(flat // mask % 2 * (1 << at) for at, mask in enumerate(group))


def call_kernel(
    kernel, outs, scalars, arrays, flops=1_000_000, scratch=(), limit=16, apart=(), after=()
):
    vmem = pl.BlockSpec(memory_space=pltpu.VMEM)
    smem = pl.BlockSpec(memory_space=pltpu.SMEM)
    hbm = pl.BlockSpec(memory_space=pltpu.HBM)
    anywhere = pl.BlockSpec(memory_space=pl.ANY)
    moved = sum(x.size * x.dtype.itemsize for x in list(arrays) + list(outs))
    used = len(scalars) + len(arrays) + len(apart)

    def body(*refs):
        kernel(*refs[:used], *refs[used + len(after) :])

    return pl.pallas_call(
        body,
        out_shape=outs,
        in_specs=[smem] * len(scalars) + [vmem] * len(arrays) + [hbm] * len(apart)
        + [anywhere] * len(after),
        out_specs=[vmem] * len(outs),
        scratch_shapes=scratch,
        compiler_params=pltpu.CompilerParams(vmem_limit_bytes=limit * 2**20),
        cost_estimate=pl.CostEstimate(flops=flops, bytes_accessed=moved, transcendentals=0),
    )(*scalars, *arrays, *apart, *after)


def shape_of(kind, *dims):
    return jax.ShapeDtypeStruct(dims, kind)


def handed_over(message, patterns, offsets, counts):
    owners = lax.axis_size("pos")
    slots, pixels = patterns.shape[2], patterns.shape[4]
    if owners == slots:
        return lax.ppermute(message, "pos", [(i, 1 - i) for i in range(2)]), counts
    all_counts = lax.all_gather(counts[0, 0], "pos")
    ends = jnp.cumsum(all_counts)
    rank = lax.axis_index("pos")
    source = jnp.sum((ends <= rank).astype(jnp.int32))
    slot = rank - (ends[source] - all_counts[source])
    spot = lax.all_gather(offsets[0, 0], "pos")[source, slot]
    pattern = lax.all_gather(patterns[0, 0], "pos")[source, slot]
    rows = jnp.broadcast_to(spot.astype(bf16)[:, None], (2, pixels))
    blank = jnp.zeros((14, pixels), bf16)
    return jnp.concatenate([pattern, rows, blank], axis=0), jnp.zeros_like(counts)


def fold_kernel(group, keep_ref, *refs):
    blocks = refs[-1]
    got = len(refs) - 1 - blocks.shape[0]
    arrived, keep_out, give_outs = refs[:got], refs[got], refs[got + 1 : -1]
    total = keep_ref[...].astype(f32)
    for ref in arrived:
        total += ref[...].astype(f32)
    size = blocks.shape[1]
    for block in range(blocks.shape[0]):
        blocks[block] = total[block * size : (block + 1) * size]
    here = place_of(group)
    keep_out[...] = blocks[here]
    for distance, ref in enumerate(give_outs, 1):
        ref[...] = blocks[here ^ distance].astype(bf16)


def add_kernel(keep_ref, *refs):
    total = keep_ref[...].astype(f32)
    for ref in refs[:-1]:
        total += ref[...].astype(f32)
    refs[-1][...] = total.astype(bf16)


def place_kernel(group, add, *refs):
    arrived, out_ref, blocks = refs[:-2], refs[-2], refs[-1]
    here = place_of(group)
    for distance, ref in enumerate(arrived):
        blocks[here ^ distance] = ref[...]
    size = blocks.shape[1]
    if add:
        total = blocks[0].astype(f32)
        for block in range(1, blocks.shape[0]):
            total += blocks[block].astype(f32)
        out_ref[...] = total.astype(bf16)
    else:
        for block in range(blocks.shape[0]):
            out_ref[pl.ds(block * size, size), :] = blocks[block]


def probe_kernel(step, modes, mine_ref, other_ref, probe_ref, out_ref):
    core = place_of(core_group())
    lane_tiles = 2
    n = mine_ref.shape[0]
    stride = lane_tiles * modes
    for part in range(2):
        total = jnp.where(core == part, mine_ref[...].astype(f32), other_ref[...].astype(f32))
        for mode in range(modes):
            for tile in range(lane_tiles):
                lane = (mode * lane_tiles + tile) * 128
                where = pl.ds(part * n * stride + tile * modes + mode, n, stride=stride)
                out_ref[where, :] = probe_ref[where, :] - step * total[:, lane : lane + 128]


def exchange_groups():
    tiles, owners = lax.axis_size("tile"), lax.axis_size("pos")
    bits = [1 << bit for bit in range(owners.bit_length() - 1)]
    bits += [owners << bit for bit in range(1, tiles.bit_length() - 1)]
    return [bits[at : at + 2] for at in range(0, len(bits), 2)]


def swap_with(x, group, distance):
    mask = sum(bit for at, bit in enumerate(group) if distance >> at & 1)
    devices = lax.axis_size("tile") * lax.axis_size("pos")
    return lax.ppermute(x, ("tile", "pos"), [(i, i ^ mask) for i in range(devices)])


def joined(group, x, add, after=()):
    blocks = 1 << len(group)
    arrived = [x] + [swap_with(x, group, at) for at in range(1, blocks)]
    rows = x.shape[0] * (1 if add else blocks)
    (out,) = call_kernel(
        lambda *refs: place_kernel(group, add, *refs),
        [shape_of(bf16, rows, x.shape[1])],
        [],
        arrived,
        scratch=[pltpu.VMEM((blocks,) + x.shape, bf16)],
        limit=4,
        after=after,
    )
    return out


def shards(tile_object, probe_modes, patterns, offsets, counts):
    _, pixels, modes, _ = probe_modes.shape
    prop, dft = build_tables(pixels)
    tile = shape_of(bf16, 2, pixels, pixels)
    message = shape_of(bf16, pixels + 16, pixels)
    *own, message = call_kernel(
        cut_kernel,
        [tile, tile, message],
        [offsets],
        [],
        apart=[tile_object, patterns],
        scratch=[pltpu.SemaphoreType.DMA((3,))],
        limit=4,
    )
    below = [from_behind(own[s], -1, 0) for s in range(2)]
    right = from_behind(tile_object[0], 0, -1)
    message, counts = handed_over(message, patterns, offsets, counts)
    diag = [from_behind(below[s], 0, -1) for s in range(2)]
    lane_tiles = pixels // 128
    probe = probe_modes.reshape(2, pixels, modes, lane_tiles, 128)
    probe = probe.transpose(0, 1, 3, 2, 4).reshape(-1, 128)
    width = modes * pixels
    near, arrive = call_kernel(
        arrive_kernel,
        [tile, shape_of(f32, 2, pixels, width)],
        [offsets, counts],
        [message, own[0], right, below[0], diag[0], probe],
        flops=1_500_000_000,
        apart=[prop],
        scratch=[pltpu.VMEM(prop.shape, bf16), pltpu.SemaphoreType.DMA((4,))],
    )
    half = shape_of(bf16, pixels, width)
    down = shape_of(bf16, 2 * pixels + 16, pixels)
    home0, next0, down0, home1, next1, down1, keep, give = call_kernel(
        gradient_kernel,
        [tile, tile, down, tile, tile, down, half, half],
        [offsets, counts],
        [message, own[1], right, below[1], diag[1], near, arrive, probe, patterns, prop, dft],
        flops=4_000_000_000,
        scratch=[pltpu.VMEM((2, pixels, width), bf16)],
    )
    zero = jnp.zeros((), bf16)

    def from_above(down):
        arrived = from_behind(down, 1, 0)
        return arrived[: 2 * pixels].reshape(2, pixels, pixels), arrived[2 * pixels] > 0

    def beside(next_tile, above, split):
        return next_tile + jnp.where(split, above, zero)

    def part(home, above, split, from_left):
        kept = home.astype(f32) + jnp.where(split, zero, above).astype(f32)
        return lax.optimization_barrier((kept + from_left.astype(f32)).astype(bf16))

    def over_owners(part):
        if lax.axis_size("pos") == 2:
            other = lax.ppermute(part, "pos", [(0, 1), (1, 0)])
            return part.astype(f32) + other.astype(f32)
        return lax.psum(part.astype(f32), "pos")

    core, groups = core_group(), exchange_groups()
    arrived = [swap_with(give, core, 1)]
    above1, split1 = from_above(down1)
    above0, split0 = from_above(down0)
    scattered = []
    while len(groups) > 1 and keep.shape[0] >> len(groups[0]) >= 16:
        group, groups = groups[0], groups[1:]
        blocks = 1 << len(group)
        size = keep.shape[0] // blocks
        keep, *gives = call_kernel(
            lambda *refs, group=group: fold_kernel(group, *refs),
            [shape_of(f32, size, width)] + [shape_of(bf16, size, width)] * (blocks - 1),
            [],
            [keep] + arrived,
            scratch=[pltpu.VMEM((blocks, size, width), f32)],
            limit=4,
        )
        arrived = [swap_with(x, group, at) for at, x in enumerate(gives, 1)]
        scattered.append(group)
    beside1 = beside(next1, above1, split1)
    from_left1 = from_behind(beside1, 0, 1)
    (total,) = call_kernel(
        add_kernel,
        [shape_of(bf16, *keep.shape)],
        [],
        [keep] + arrived,
        limit=4,
        after=[beside1],
    )
    beside0 = beside(next0, above0, split0)
    from_left0 = from_behind(beside0, 0, 1)
    part1 = part(home1, above1, split1, from_left1)
    for group in groups:
        total = joined(group, total, True, after=[beside0, part1])
    part0 = part(home0, above0, split0, from_left0)
    for group in reversed(scattered):
        total = joined(group, total, False, after=[part0])
    tile_grads = [over_owners(part0), over_owners(part1)]
    other = swap_with(total, core, 1)
    new_slices = [
        (own[s].astype(f32) - object_rate * tile_grads[s]).astype(bf16) for s in range(2)
    ]
    new_object = jnp.stack(new_slices)[None]
    positions_all = lax.axis_size("tile") * lax.axis_size("pos") * (patterns.shape[2] // 2)
    step = probe_rate / math.sqrt(positions_all)
    (new_probe,) = call_kernel(
        lambda *refs: probe_kernel(step, modes, *refs),
        [shape_of(f32, *probe.shape)],
        [],
        [total, other, probe],
        limit=8,
    )
    new_probe = new_probe.reshape(2, pixels, lane_tiles, modes, 128).transpose(0, 1, 3, 2, 4)
    return (new_object, new_probe.reshape(probe_modes.shape))


def solution(mesh):
    placed = (
        P("tile", None, None, None, None),
        P(),
        P("tile", "pos", None, None, None),
        P("tile", "pos", None, None),
        P("tile", "pos"),
    )
    return jax.shard_map(
        shards,
        mesh=mesh,
        in_specs=placed,
        out_specs=(P("tile", None, None, None, None), P()),
        check_vma=False,
    )
```

time: 86.9 us -> 73.7 us (0.85)
  starting transfers between devices: 35.8 us -> 25.1 us
  local copies, waits for them, and re-layouts: 5.53 us -> 3.3 us
  Pallas kernels: 9.15 us -> 10.8 us
  other arithmetic: 3.05 us -> 1.45 us
    all_to_all x3 -> x0, starting transfers between devices: 17.8 us -> none  [exchange(): lax.all_to_all(x, ('tile', 'pos'), 0, 0, axis_index_groups=groups, tiled=...]
    all_to_all x3 -> x0, waiting for transfers between devices: 16.7 us -> none  [exchange(): lax.all_to_all(x, ('tile', 'pos'), 0, 0, axis_index_groups=groups, tiled=...]
    ppermute x15 -> x23, waiting for transfers between devices: 14.7 us -> 31.3 us  [the longest x9 19.5 us: from_behind(): return lax.ppermute(block, 'tile', [(source(i), i) for i in range(tiles)])]
    ppermute x15 -> x23, starting transfers between devices: 18 us -> 25.1 us  [the longest x11 11.6 us: swap_with(): lax.ppermute(x, ('tile', 'pos'), [(i, i ^ mask) for i in range(devices)])]
    reshape x1 -> x0, local copies, waits for them, and re-layouts: 2.12 us -> none  [shards(): probe = probe_modes.reshape(2, pixels, -1)]
    pallas_call x4 -> x8, Pallas kernels: 9.15 us -> 10.8 us  [call_kernel(): pl.pallas_call(body, out_shape=outs, in_specs=[smem] * len(scalars) + [vm...]
    unnamed x20 -> x16, local copies, waits for them, and re-layouts: 1.61 us -> 3.26 us
    sub x1 -> x0, other arithmetic: 1.51 us -> none  [shards(): probe_modes - step * total.astype(f32).reshape(probe_modes.shape)]
  transfers between devices with their start and end apart: 18 -> 23, of which waited for: 9 -> 11; matrix products, arithmetic and copies ran while one was open for 4% -> 2% of each run, Pallas kernels for 4% -> 6%
where the time goes in v3:
time: 73.7 us; the launch traced here: 73.5 us
  waiting for transfers between devices  31.3 us (42%)
  starting transfers between devices  25.1 us (34%)
  Pallas kernels  10.8 us (15%)
  local copies, waits for them, and re-layouts  3.3 us (4%)
  between operations  1.49 us (2%)
  other arithmetic  1.45 us (2%)
    ppermute x9, waiting for transfers between devices, from_behind(): return lax.ppermute(block, 'tile', [(source(i), i) for i in range(tiles)])  19.5 us
    ppermute x11, starting transfers between devices, swap_with(): lax.ppermute(x, ('tile', 'pos'), [(i, i ^ mask) for i in range(devices)])  11.6 us
    pallas_call x8, Pallas kernels, call_kernel(): pl.pallas_call(body, out_shape=outs, in_specs=[smem] * len(scalars) + [vm...  10.8 us
    ppermute x9, starting transfers between devices, from_behind(): return lax.ppermute(block, 'tile', [(source(i), i) for i in range(tiles)])  8.86 us
    ppermute x11, waiting for transfers between devices, swap_with(): lax.ppermute(x, ('tile', 'pos'), [(i, i ^ mask) for i in range(devices)])  6.34 us
    ppermute x2, waiting for transfers between devices, over_owners(): other = lax.ppermute(part, 'pos', [(0, 1), (1, 0)])  4.25 us
    unnamed x16, local copies, waits for them, and re-layouts  3.26 us
    ppermute x2, starting transfers between devices, over_owners(): other = lax.ppermute(part, 'pos', [(0, 1), (1, 0)])  3.1 us
  transfers between devices with their start and end apart: 23, of which 11 were waited for; matrix products, arithmetic and copies ran while one was open for 2% of the time, Pallas kernels for 6%

profile of v3, /device:TPU:0, one launch (start us, length us, event | category | flops | bytes accessed | tf_op | source)
XLA Modules:
  0.0 73.5 jit_solution(2427733538038421373)
XLA Ops:
  0.6 2.4 %collective-permute-start.1 = (bf16[2,2,256,256]{3,2,1,0:T(8,128)(2,1)}, bf16[2,2,256,256]{3,2,1,0:T(8,128)(2,1)S(1)}, u32[]{:S(2)}, u32[]{:S(2)}) collective-permute-start(bf16[2,2,256,256]{3,2,1,0:T(8,128)(2,1)} %bitcast.22), channel_id=1, source_target_pairs={{2,0},{4,2},{6,4},{0,6},{10,8},{12,10},{14,12},{8,14},{18,16},{20,... | collective-permute-start | bytes 1572872 | tf_op jit(solution)/shard_map/ppermute | solution.py:29
  3.1 1.1 %copy-done.2 = bf16[1,2,2,256,256]{4,3,2,1,0:T(8,128)(2,1)S(1)} copy-done((bf16[1,2,2,256,256]{4,3,2,1,0:T(8,128)(2,1)S(1)}, bf16[1,2,2,256,256]{4,3,2,1,0:T(8,128)(2,1)}, u32[]{:S(2)}) %copy-start.2) | copy-done | bytes 524312
  4.1 0.9 %copy-done.3 = bf16[1,1,2,256,256]{4,3,2,1,0:T(8,128)(2,1)S(1)} copy-done((bf16[1,1,2,256,256]{4,3,2,1,0:T(8,128)(2,1)S(1)}, bf16[1,1,2,256,256]{4,3,2,1,0:T(8,128)(2,1)}, u32[]{:S(2)}) %copy-start.3) | copy-done | bytes 262168
  5.1 0.8 %shard_map.86 = (bf16[2,256,256]{2,1,0:T(8,128)(2,1)S(1)}, bf16[2,256,256]{2,1,0:T(8,128)(2,1)S(1)}, bf16[272,256]{1,0:T(8,128)(2,1)S(1)}) custom-call(s32[1,1,2,2]{3,2,1,0:T(2,128)S(1)} %copy-done.5, bf16[1,2,2,256,256]{4,3,2,1,0:T(8,128)(2,1)S(1)} %copy-done.2, bf16[1,1,2,256,256]{4,3,2,1,0:T(8,128)(2,1)S(1)} %copy-done.3), custom_call_target="tpu_custom_call" | custom-call | flops 1000000 | bytes 663552 | tf_op jit(solution)/shard_map/pallas_call | solution.py:242
  5.9 3.7 %collective-permute-start.4 = (bf16[2,256,256]{2,1,0:T(8,128)(2,1)S(1)}, bf16[2,256,256]{2,1,0:T(8,128)(2,1)S(1)}, u32[]{:S(2)}, u32[]{:S(2)}) collective-permute-start(bf16[2,256,256]{2,1,0:T(8,128)(2,1)S(1)} %get-tuple-element.19.refs_3_), channel_id=1, source_target_pairs={{8,0},{10,2},{12,4},{14,6},{16,8},{18,10},{20,12},{22,14},{24,16},... | collective-permute-start | bytes 786440 | tf_op jit(solution)/shard_map/ppermute | solution.py:29
  9.6 0.4 collective-permute-start.2
  10.0 6.3 %collective-permute-done.4.refs_5_ = bf16[2,256,256]{2,1,0:T(8,128)(2,1)S(1)} collective-permute-done((bf16[2,256,256]{2,1,0:T(8,128)(2,1)S(1)}, bf16[2,256,256]{2,1,0:T(8,128)(2,1)S(1)}, u32[]{:S(2)}, u32[]{:S(2)}) %collective-permute-start.4) | collective-permute-done | bytes 262176 | tf_op jit(solution)/shard_map/ppermute | solution.py:29
  16.3 0.0 collective-permute-start.5
  16.3 1.5 %collective-permute-start = (bf16[272,256]{1,0:T(8,128)(2,1)S(1)}, bf16[272,256]{1,0:T(8,128)(2,1)S(1)}, u32[]{:S(2)}, u32[]{:S(2)}) collective-permute-start(bf16[272,256]{1,0:T(8,128)(2,1)S(1)} %get-tuple-element.20), channel_id=1, source_target_pairs={{0,1},{1,0},{2,3},{3,2},{4,5},{5,4},{6,7},{7,6},{8,9},{9,8},{10,11... | collective-permute-start | bytes 417800 | tf_op jit(solution)/shard_map/ppermute | solution.py:262
  17.8 2.6 %collective-permute-done.2.refs_5_ = bf16[2,256,256]{2,1,0:T(8,128)(2,1)S(1)} collective-permute-done((bf16[2,256,256]{2,1,0:T(8,128)(2,1)S(1)}, bf16[2,256,256]{2,1,0:T(8,128)(2,1)S(1)}, u32[]{:S(2)}, u32[]{:S(2)}) %collective-permute-start.2) | collective-permute-done | bytes 262176 | tf_op jit(solution)/shard_map/ppermute | solution.py:29
  20.5 0.1 collective-permute-start.3
  21.2 1.2 %collective-permute-done.refs_2_ = bf16[272,256]{1,0:T(8,128)(2,1)S(1)} collective-permute-done((bf16[272,256]{1,0:T(8,128)(2,1)S(1)}, bf16[272,256]{1,0:T(8,128)(2,1)S(1)}, u32[]{:S(2)}, u32[]{:S(2)}) %collective-permute-start) | collective-permute-done | bytes 139296 | tf_op jit(solution)/shard_map/ppermute | solution.py:262
  22.4 0.0 copy-start
  22.4 1.2 %copy-done = f32[2,256,2,256]{3,2,1,0:T(2,128)S(1)} copy-done((f32[2,256,2,256]{3,2,1,0:T(2,128)S(1)}, f32[2,256,2,256]{3,2,1,0:T(2,128)}, u32[]{:S(2)}) %copy-start) | copy-done | bytes 1048600
  23.6 3.0 %shard_map.87 = (bf16[2,256,256]{2,1,0:T(8,128)(2,1)S(1)}, f32[2,256,512]{2,1,0:T(8,128)S(1)}) custom-call(s32[1,1,2,2]{3,2,1,0:T(2,128)S(1)} %copy-done.5, s32[1,1]{1,0:T(1,128)S(6)} %copy.11.refs_1_, bf16[272,256]{1,0:T(8,128)(2,1)S(1)} %collective-permute-done.refs_2_, bf16[2,256,256]{2,1,0:T(8,128)(2,1)S(1)} %get-tuple-element.19.refs_3_, ...), custom_call_target="tpu_custom_call" | custom-call | flops 1500000000 | bytes 3809280 | tf_op jit(solution)/shard_map/pallas_call | solution.py:242
  26.7 5.5 %shard_map.88 = (bf16[2,256,256]{2,1,0:T(8,128)(2,1)S(1)}, bf16[2,256,256]{2,1,0:T(8,128)(2,1)S(1)}, bf16[528,256]{1,0:T(8,128)(2,1)S(1)}, bf16[2,256,256]{2,1,0...) custom-call(s32[1,1,2,2]{3,2,1,0:T(2,128)S(1)} %copy-done.5, ...), custom_call_target="tpu_custom_call" | custom-call | flops 4000000000 | bytes 7233536 | tf_op jit(solution)/shard_map/pallas_call | solution.py:242
  32.3 0.5 collective-permute-start.6
  32.8 1.6 %collective-permute-start.9 = (bf16[528,256]{1,0:T(8,128)(2,1)S(1)}, bf16[528,256]{1,0:T(8,128)(2,1)S(1)}, u32[]{:S(2)}, u32[]{:S(2)}) collective-permute-start(bf16[528,256]{1,0:T(8,128)(2,1)S(1)} %get-tuple-element.28), channel_id=1, source_target_pairs={{24,0},{26,2},{28,4},{30,6},{0,8},{2,10},{4,12},{6,14},{8,16},{10,... | collective-permute-start | bytes 811016 | tf_op jit(solution)/shard_map/ppermute | solution.py:29
  34.4 0.1 shard_map.89
  34.5 1.6 %collective-permute-start.13 = (bf16[64,512]{1,0:T(8,128)(2,1)S(1)}, bf16[64,512]{1,0:T(8,128)(2,1)S(1)}, u32[]{:S(2)}, u32[]{:S(2)}) collective-permute-start(bf16[64,512]{1,0:T(8,128)(2,1)S(1)} %get-tuple-element.33), channel_id=1, source_target_pairs={{0,1},{1,0},{2,3},{3,2},{4,5},{5,4},{6,7},{7,6},{8,9},{9,8},{10,11... | collective-permute-start | bytes 196616 | tf_op jit(solution)/shard_map/ppermute | solution.py:338
  36.0 1.1 %collective-permute-start.14 = (bf16[64,512]{1,0:T(8,128)(2,1)S(1)}, bf16[64,512]{1,0:T(8,128)(2,1)S(1)}, u32[]{:S(2)}, u32[]{:S(2)}) collective-permute-start(bf16[64,512]{1,0:T(8,128)(2,1)S(1)} %get-tuple-element.34), channel_id=1, source_target_pairs={{0,4},{1,5},{2,6},{3,7},{4,0},{5,1},{6,2},{7,3},{8,12},{9,13},{10,... | collective-permute-start | bytes 196616 | tf_op jit(solution)/shard_map/ppermute | solution.py:338
  37.1 0.9 %collective-permute-start.15 = (bf16[64,512]{1,0:T(8,128)(2,1)S(1)}, bf16[64,512]{1,0:T(8,128)(2,1)S(1)}, u32[]{:S(2)}, u32[]{:S(2)}) collective-permute-start(bf16[64,512]{1,0:T(8,128)(2,1)S(1)} %get-tuple-element.35), channel_id=1, source_target_pairs={{0,5},{1,4},{2,7},{3,6},{4,1},{5,0},{6,3},{7,2},{8,13},{9,12},{10,... | collective-permute-start | bytes 196616 | tf_op jit(solution)/shard_map/ppermute | solution.py:338
  38.0 5.9 %collective-permute-done.6 = bf16[528,256]{1,0:T(8,128)(2,1)S(1)} collective-permute-done((bf16[528,256]{1,0:T(8,128)(2,1)S(1)}, bf16[528,256]{1,0:T(8,128)(2,1)S(1)}, u32[]{:S(2)}, u32[]{:S(2)}) %collective-permute-start.6) | collective-permute-done | bytes 270368 | tf_op jit(solution)/shard_map/ppermute | solution.py:29
  44.0 0.1 collective-permute-start.7
  44.1 4.7 %collective-permute-done.9 = bf16[528,256]{1,0:T(8,128)(2,1)S(1)} collective-permute-done((bf16[528,256]{1,0:T(8,128)(2,1)S(1)}, bf16[528,256]{1,0:T(8,128)(2,1)S(1)}, u32[]{:S(2)}, u32[]{:S(2)}) %collective-permute-start.9) | collective-permute-done | bytes 270368 | tf_op jit(solution)/shard_map/ppermute | solution.py:29
  48.8 0.1 collective-permute-start.10
  49.0 1.8 %collective-permute-start.18 = (bf16[64,512]{1,0:T(8,128)(2,1)S(1)}, bf16[64,512]{1,0:T(8,128)(2,1)S(1)}, u32[]{:S(2)}, u32[]{:S(2)}) collective-permute-start(bf16[64,512]{1,0:T(8,128)(2,1)S(1)} %shard_map.90.refs_0_), channel_id=1, source_target_pairs={{0,24},{1,25},{2,26},{3,27},{4,28},{5,29},{6,30},{7,31},{8,16},{9,... | collective-permute-start | bytes 196616 | tf_op jit(solution)/shard_map/ppermute | solution.py:338
  50.8 2.6 %collective-permute-start.16 = (bf16[64,512]{1,0:T(8,128)(2,1)S(1)}, bf16[64,512]{1,0:T(8,128)(2,1)S(1)}, u32[]{:S(2)}, u32[]{:S(2)}) collective-permute-start(bf16[64,512]{1,0:T(8,128)(2,1)S(1)} %shard_map.90.refs_0_), channel_id=1, source_target_pairs={{0,8},{1,9},{2,10},{3,11},{4,12},{5,13},{6,14},{7,15},{8,0},{9,1},... | collective-permute-start | bytes 196616 | tf_op jit(solution)/shard_map/ppermute | solution.py:338
  53.4 0.1 add_convert_fusion.1.refs_4_
  53.6 1.6 %collective-permute-start.8 = (bf16[2,256,256]{2,1,0:T(8,128)(2,1)S(1)}, bf16[2,256,256]{2,1,0:T(8,128)(2,1)S(1)}, u32[]{:S(2)}, u32[]{:S(2)}) collective-permute-start(bf16[2,256,256]{2,1,0:T(8,128)(2,1)S(1)} %add_convert_fusion.1.refs_4_), channel_id=1, source_target_pairs={{0,1},{1,0},{2,3},{3,2},{4,5},{5,4},{6,7},{7,6},{8,9},{9,8},{10,11... | collective-permute-start | bytes 786440 | tf_op jit(solution)/shard_map/ppermute | solution.py:413
  55.2 0.1 add_convert_fusion.refs_5_
  55.3 0.5 collective-permute-done.18.refs_3_
  55.7 2.9 %collective-permute-done.17.refs_2_ = bf16[64,512]{1,0:T(8,128)(2,1)S(1)} collective-permute-done((bf16[64,512]{1,0:T(8,128)(2,1)S(1)}, bf16[64,512]{1,0:T(8,128)(2,1)S(1)}, u32[]{:S(2)}, u32[]{:S(2)}) %collective-permute-start.17) | collective-permute-done | bytes 65568 | tf_op jit(solution)/shard_map/ppermute | solution.py:338
  58.6 0.1 shard_map.91.refs_0_
  58.7 2.1 %collective-permute-start.21 = (bf16[64,512]{1,0:T(8,128)(2,1)S(1)}, bf16[64,512]{1,0:T(8,128)(2,1)S(1)}, u32[]{:S(2)}, u32[]{:S(2)}) collective-permute-start(bf16[64,512]{1,0:T(8,128)(2,1)S(1)} %shard_map.91.refs_0_), channel_id=1, source_target_pairs={{0,5},{1,4},{2,7},{3,6},{4,1},{5,0},{6,3},{7,2},{8,13},{9,12},{10,... | collective-permute-start | bytes 196616 | tf_op jit(solution)/shard_map/ppermute | solution.py:338
  60.8 0.9 %collective-permute-start.20 = (bf16[64,512]{1,0:T(8,128)(2,1)S(1)}, bf16[64,512]{1,0:T(8,128)(2,1)S(1)}, u32[]{:S(2)}, u32[]{:S(2)}) collective-permute-start(bf16[64,512]{1,0:T(8,128)(2,1)S(1)} %shard_map.91.refs_0_), channel_id=1, source_target_pairs={{0,4},{1,5},{2,6},{3,7},{4,0},{5,1},{6,2},{7,3},{8,12},{9,13},{10,... | collective-permute-start | bytes 196616 | tf_op jit(solution)/shard_map/ppermute | solution.py:338
  61.8 0.5 collective-permute-start.19
  62.3 1.5 %collective-permute-start.11 = (bf16[2,256,256]{2,1,0:T(8,128)(2,1)S(1)}, bf16[2,256,256]{2,1,0:T(8,128)(2,1)S(1)}, u32[]{:S(2)}, u32[]{:S(2)}) collective-permute-start(bf16[2,256,256]{2,1,0:T(8,128)(2,1)S(1)} %add_convert_fusion.refs_5_), channel_id=1, source_target_pairs={{0,1},{1,0},{2,3},{3,2},{4,5},{5,4},{6,7},{7,6},{8,9},{9,8},{10,11... | collective-permute-start | bytes 786440 | tf_op jit(solution)/shard_map/ppermute | solution.py:413
  63.8 0.9 %collective-permute-done.21.refs_3_ = bf16[64,512]{1,0:T(8,128)(2,1)S(1)} collective-permute-done((bf16[64,512]{1,0:T(8,128)(2,1)S(1)}, bf16[64,512]{1,0:T(8,128)(2,1)S(1)}, u32[]{:S(2)}, u32[]{:S(2)}) %collective-permute-start.21) | collective-permute-done | bytes 65568 | tf_op jit(solution)/shard_map/ppermute | solution.py:338
  64.7 0.6 collective-permute-done.20.refs_2_
  65.3 1.4 %collective-permute-done.19.refs_1_ = bf16[64,512]{1,0:T(8,128)(2,1)S(1)} collective-permute-done((bf16[64,512]{1,0:T(8,128)(2,1)S(1)}, bf16[64,512]{1,0:T(8,128)(2,1)S(1)}, u32[]{:S(2)}, u32[]{:S(2)}) %collective-permute-start.19) | collective-permute-done | bytes 65568 | tf_op jit(solution)/shard_map/ppermute | solution.py:338
  66.8 0.1 shard_map.92.refs_0_
  66.8 0.1 collective-permute-start.22
  66.9 0.1 fusion
  67.1 4.2 %collective-permute-done.11 = bf16[2,256,256]{2,1,0:T(8,128)(2,1)S(1)} collective-permute-done((bf16[2,256,256]{2,1,0:T(8,128)(2,1)S(1)}, bf16[2,256,256]{2,1,0:T(8,128)(2,1)S(1)}, u32[]{:S(2)}, u32[]{:S(2)}) %collective-permute-start.11) | collective-permute-done | bytes 262176 | tf_op jit(solution)/shard_map/ppermute | solution.py:413
  71.3 0.1 fusion.1
  71.4 0.8 %maximum_bitcast_fusion = bf16[1,2,2,256,256]{4,3,2,1,0:T(8,128)(2,1)} fusion(bf16[1,2,256,256]{3,2,1,0:T(8,128)(2,1)S(1)} %fusion.1, bf16[1,2,256,256]{3,2,1,0:T(8,128)(2,1)S(1)} %fusion), kind=kLoop, calls=%fused_computation | loop fusion | flops 262144 | bytes 1048576 | tf_op jit(solution)/shard_map/broadcast_in_dim | solution.py:459
  72.3 1.2 %shard_map.93 = f32[2048,128]{1,0:T(8,128)} custom-call(bf16[256,512]{1,0:T(8,128)(2,1)S(1)} %shard_map.92.refs_0_, bf16[256,512]{1,0:T(8,128)(2,1)S(1)} %collective-permute-done.22.refs_1_, f32[2048,128]{1,0:T(8,128)S(1)} %bitcast.21), custom_call_target="tpu_custom_call" | custom-call | flops 1000000 | bytes 2621440 | tf_op jit(solution)/shard_map/pallas_call | solution.py:242
  (33 shorter events, 0.2 us)
Async XLA Ops:
  0.6 2.4 %copy-start.5 = (s32[1,1,2,2]{3,2,1,0:T(2,128)S(1)}, s32[1,1,2,2]{3,2,1,0:T(2,128)}, u32[]{:S(2)}) copy-start(s32[1,1,2,2]{3,2,1,0:T(2,128)} %refs_0_.5) | copy-start | bytes 52
  0.6 21.8 %collective-permute-start.1 = (bf16[2,2,256,256]{3,2,1,0:T(8,128)(2,1)}, bf16[2,2,256,256]{3,2,1,0:T(8,128)(2,1)S(1)}, u32[]{:S(2)}, u32[]{:S(2)}) collective-permute-start(bf16[2,2,256,256]{3,2,1,0:T(8,128)(2,1)} %bitcast.22), channel_id=1, source_target_pairs={{2,0},{4,2},{6,4},{0,6},{10,8},{12,10},{14,12},{8,14},{18,16},{20,... | collective-permute-start | bytes 1572872 | tf_op jit(solution)/shard_map/ppermute | solution.py:29
  3.1 1.1 %copy-start.2 = (bf16[1,2,2,256,256]{4,3,2,1,0:T(8,128)(2,1)S(1)}, bf16[1,2,2,256,256]{4,3,2,1,0:T(8,128)(2,1)}, u32[]{:S(2)}) copy-start(bf16[1,2,2,256,256]{4,3,2,1,0:T(8,128)(2,1)} %refs_1_.3) | copy-start | bytes 1572868
  4.1 0.9 %copy-start.3 = (bf16[1,1,2,256,256]{4,3,2,1,0:T(8,128)(2,1)S(1)}, bf16[1,1,2,256,256]{4,3,2,1,0:T(8,128)(2,1)}, u32[]{:S(2)}) copy-start(bf16[1,1,2,256,256]{4,3,2,1,0:T(8,128)(2,1)} %refs_10_.1) | copy-start | bytes 786436
  5.1 17.3 %copy-start.6 = (bf16[512,512]{1,0:T(8,128)(2,1)S(1)}, bf16[512,512]{1,0:T(8,128)(2,1)}, u32[]{:S(2)}) copy-start(bf16[512,512]{1,0:T(8,128)(2,1)} %constant.15.refs_8_.refs_11_) | copy-start | bytes 1572868
  5.9 10.4 %collective-permute-start.4 = (bf16[2,256,256]{2,1,0:T(8,128)(2,1)S(1)}, bf16[2,256,256]{2,1,0:T(8,128)(2,1)S(1)}, u32[]{:S(2)}, u32[]{:S(2)}) collective-permute-start(bf16[2,256,256]{2,1,0:T(8,128)(2,1)S(1)} %get-tuple-element.19.refs_3_), channel_id=1, source_target_pairs={{8,0},{10,2},{12,4},{14,6},{16,8},{18,10},{20,12},{22,14},{24,16},... | collective-permute-start | bytes 786440 | tf_op jit(solution)/shard_map/ppermute | solution.py:29
  9.6 10.9 %collective-permute-start.2 = (bf16[2,256,256]{2,1,0:T(8,128)(2,1)S(1)}, bf16[2,256,256]{2,1,0:T(8,128)(2,1)S(1)}, u32[]{:S(2)}, u32[]{:S(2)}) collective-permute-start(bf16[2,256,256]{2,1,0:T(8,128)(2,1)S(1)} %get-tuple-element.21.refs_3_), channel_id=1, source_target_pairs={{8,0},{10,2},{12,4},{14,6},{16,8},{18,10},{20,12},{22,14},{24,16},... | collective-permute-start | bytes 786440 | tf_op jit(solution)/shard_map/ppermute | solution.py:29
  16.3 6.1 %collective-permute-start.5 = (bf16[2,256,256]{2,1,0:T(8,128)(2,1)S(1)}, bf16[2,256,256]{2,1,0:T(8,128)(2,1)S(1)}, u32[]{:S(2)}, u32[]{:S(2)}) collective-permute-start(bf16[2,256,256]{2,1,0:T(8,128)(2,1)S(1)} %collective-permute-done.4.refs_5_), channel_id=1, source_target_pairs={{2,0},{4,2},{6,4},{0,6},{10,8},{12,10},{14,12},{8,14},{18,16},{20,... | collective-permute-start | bytes 786440 | tf_op jit(solution)/shard_map/ppermute | solution.py:29
  16.3 6.1 %collective-permute-start = (bf16[272,256]{1,0:T(8,128)(2,1)S(1)}, bf16[272,256]{1,0:T(8,128)(2,1)S(1)}, u32[]{:S(2)}, u32[]{:S(2)}) collective-permute-start(bf16[272,256]{1,0:T(8,128)(2,1)S(1)} %get-tuple-element.20), channel_id=1, source_target_pairs={{0,1},{1,0},{2,3},{3,2},{4,5},{5,4},{6,7},{7,6},{8,9},{9,8},{10,11... | collective-permute-start | bytes 417800 | tf_op jit(solution)/shard_map/ppermute | solution.py:262
  20.5 6.2 %collective-permute-start.3 = (bf16[2,256,256]{2,1,0:T(8,128)(2,1)S(1)}, bf16[2,256,256]{2,1,0:T(8,128)(2,1)S(1)}, u32[]{:S(2)}, u32[]{:S(2)}) collective-permute-start(bf16[2,256,256]{2,1,0:T(8,128)(2,1)S(1)} %collective-permute-done.2.refs_5_), channel_id=1, source_target_pairs={{2,0},{4,2},{6,4},{0,6},{10,8},{12,10},{14,12},{8,14},{18,16},{20,... | collective-permute-start | bytes 786440 | tf_op jit(solution)/shard_map/ppermute | solution.py:29
  22.4 1.2 %copy-start = (f32[2,256,2,256]{3,2,1,0:T(2,128)S(1)}, f32[2,256,2,256]{3,2,1,0:T(2,128)}, u32[]{:S(2)}) copy-start(f32[2,256,2,256]{3,2,1,0:T(2,128)} %param.8) | copy-start | bytes 3145732
  23.6 3.0 %copy-start.1 = (f32[2,256,2,256]{3,2,1,0:T(2,128)S(1)}, f32[2,256,2,256]{3,2,1,0:T(2,128)}, u32[]{:S(2)}) copy-start(f32[2,256,2,256]{3,2,1,0:T(2,128)} %param.8) | copy-start | bytes 3145732
  23.6 3.1 %copy-start.4 = (bf16[1,1,2,256,256]{4,3,2,1,0:T(8,128)(2,1)S(1)}, bf16[1,1,2,256,256]{4,3,2,1,0:T(8,128)(2,1)}, u32[]{:S(2)}) copy-start(bf16[1,1,2,256,256]{4,3,2,1,0:T(8,128)(2,1)} %refs_10_.1) | copy-start | bytes 786436
  23.6 3.1 %copy-start.7 = (bf16[512,512]{1,0:T(8,128)(2,1)S(1)}, bf16[512,512]{1,0:T(8,128)(2,1)}, u32[]{:S(2)}) copy-start(bf16[512,512]{1,0:T(8,128)(2,1)} %constant.16.refs_12_) | copy-start | bytes 1572868
  32.3 11.7 %collective-permute-start.6 = (bf16[528,256]{1,0:T(8,128)(2,1)S(1)}, bf16[528,256]{1,0:T(8,128)(2,1)S(1)}, u32[]{:S(2)}, u32[]{:S(2)}) collective-permute-start(bf16[528,256]{1,0:T(8,128)(2,1)S(1)} %get-tuple-element.25), channel_id=1, source_target_pairs={{24,0},{26,2},{28,4},{30,6},{0,8},{2,10},{4,12},{6,14},{8,16},{10,... | collective-permute-start | bytes 811016 | tf_op jit(solution)/shard_map/ppermute | solution.py:29
  32.8 1.6 %collective-permute-start.12 = (bf16[256,512]{1,0:T(8,128)(2,1)S(1)}, bf16[256,512]{1,0:T(8,128)(2,1)S(1)}, u32[]{:S(2)}, u32[]{:S(2)}) collective-permute-start(bf16[256,512]{1,0:T(8,128)(2,1)S(1)} %get-tuple-element.31), channel_id=1, source_target_pairs={{0,2},{1,3},{2,0},{3,1},{4,6},{5,7},{6,4},{7,5},{8,10},{9,11},{10,... | collective-permute-start | bytes 786440 | tf_op jit(solution)/shard_map/ppermute | solution.py:338
  32.8 16.0 %collective-permute-start.9 = (bf16[528,256]{1,0:T(8,128)(2,1)S(1)}, bf16[528,256]{1,0:T(8,128)(2,1)S(1)}, u32[]{:S(2)}, u32[]{:S(2)}) collective-permute-start(bf16[528,256]{1,0:T(8,128)(2,1)S(1)} %get-tuple-element.28), channel_id=1, source_target_pairs={{24,0},{26,2},{28,4},{30,6},{0,8},{2,10},{4,12},{6,14},{8,16},{10,... | collective-permute-start | bytes 811016 | tf_op jit(solution)/shard_map/ppermute | solution.py:29
  34.5 14.5 %collective-permute-start.13 = (bf16[64,512]{1,0:T(8,128)(2,1)S(1)}, bf16[64,512]{1,0:T(8,128)(2,1)S(1)}, u32[]{:S(2)}, u32[]{:S(2)}) collective-permute-start(bf16[64,512]{1,0:T(8,128)(2,1)S(1)} %get-tuple-element.33), channel_id=1, source_target_pairs={{0,1},{1,0},{2,3},{3,2},{4,5},{5,4},{6,7},{7,6},{8,9},{9,8},{10,11... | collective-permute-start | bytes 196616 | tf_op jit(solution)/shard_map/ppermute | solution.py:338
  36.0 12.9 %collective-permute-start.14 = (bf16[64,512]{1,0:T(8,128)(2,1)S(1)}, bf16[64,512]{1,0:T(8,128)(2,1)S(1)}, u32[]{:S(2)}, u32[]{:S(2)}) collective-permute-start(bf16[64,512]{1,0:T(8,128)(2,1)S(1)} %get-tuple-element.34), channel_id=1, source_target_pairs={{0,4},{1,5},{2,6},{3,7},{4,0},{5,1},{6,2},{7,3},{8,12},{9,13},{10,... | collective-permute-start | bytes 196616 | tf_op jit(solution)/shard_map/ppermute | solution.py:338
  37.1 11.8 %collective-permute-start.15 = (bf16[64,512]{1,0:T(8,128)(2,1)S(1)}, bf16[64,512]{1,0:T(8,128)(2,1)S(1)}, u32[]{:S(2)}, u32[]{:S(2)}) collective-permute-start(bf16[64,512]{1,0:T(8,128)(2,1)S(1)} %get-tuple-element.35), channel_id=1, source_target_pairs={{0,5},{1,4},{2,7},{3,6},{4,1},{5,0},{6,3},{7,2},{8,13},{9,12},{10,... | collective-permute-start | bytes 196616 | tf_op jit(solution)/shard_map/ppermute | solution.py:338
  44.0 9.4 %collective-permute-start.7 = (bf16[2,256,256]{2,1,0:T(8,128)(2,1)S(1)}, bf16[2,256,256]{2,1,0:T(8,128)(2,1)S(1)}, u32[]{:S(2)}, u32[]{:S(2)}) collective-permute-start(bf16[2,256,256]{2,1,0:T(8,128)(2,1)S(1)} %select_add_fusion.1.refs_4_), channel_id=1, source_target_pairs={{6,0},{0,2},{2,4},{4,6},{14,8},{8,10},{10,12},{12,14},{22,16},{16,... | collective-permute-start | bytes 786440 | tf_op jit(solution)/shard_map/ppermute | solution.py:29
  48.8 6.3 %collective-permute-start.10 = (bf16[2,256,256]{2,1,0:T(8,128)(2,1)S(1)}, bf16[2,256,256]{2,1,0:T(8,128)(2,1)S(1)}, u32[]{:S(2)}, u32[]{:S(2)}) collective-permute-start(bf16[2,256,256]{2,1,0:T(8,128)(2,1)S(1)} %select_add_fusion.refs_4_), channel_id=1, source_target_pairs={{6,0},{0,2},{2,4},{4,6},{14,8},{8,10},{10,12},{12,14},{22,16},{16,... | collective-permute-start | bytes 786440 | tf_op jit(solution)/shard_map/ppermute | solution.py:29
  49.0 6.8 %collective-permute-start.18 = (bf16[64,512]{1,0:T(8,128)(2,1)S(1)}, bf16[64,512]{1,0:T(8,128)(2,1)S(1)}, u32[]{:S(2)}, u32[]{:S(2)}) collective-permute-start(bf16[64,512]{1,0:T(8,128)(2,1)S(1)} %shard_map.90.refs_0_), channel_id=1, source_target_pairs={{0,24},{1,25},{2,26},{3,27},{4,28},{5,29},{6,30},{7,31},{8,16},{9,... | collective-permute-start | bytes 196616 | tf_op jit(solution)/shard_map/ppermute | solution.py:338
  50.8 7.8 %collective-permute-start.17 = (bf16[64,512]{1,0:T(8,128)(2,1)S(1)}, bf16[64,512]{1,0:T(8,128)(2,1)S(1)}, u32[]{:S(2)}, u32[]{:S(2)}) collective-permute-start(bf16[64,512]{1,0:T(8,128)(2,1)S(1)} %shard_map.90.refs_0_), channel_id=1, source_target_pairs={{0,16},{1,17},{2,18},{3,19},{4,20},{5,21},{6,22},{7,23},{8,24},{9,... | collective-permute-start | bytes 196616 | tf_op jit(solution)/shard_map/ppermute | solution.py:338
  50.8 7.8 %collective-permute-start.16 = (bf16[64,512]{1,0:T(8,128)(2,1)S(1)}, bf16[64,512]{1,0:T(8,128)(2,1)S(1)}, u32[]{:S(2)}, u32[]{:S(2)}) collective-permute-start(bf16[64,512]{1,0:T(8,128)(2,1)S(1)} %shard_map.90.refs_0_), channel_id=1, source_target_pairs={{0,8},{1,9},{2,10},{3,11},{4,12},{5,13},{6,14},{7,15},{8,0},{9,1},... | collective-permute-start | bytes 196616 | tf_op jit(solution)/shard_map/ppermute | solution.py:338
  53.6 13.3 %collective-permute-start.8 = (bf16[2,256,256]{2,1,0:T(8,128)(2,1)S(1)}, bf16[2,256,256]{2,1,0:T(8,128)(2,1)S(1)}, u32[]{:S(2)}, u32[]{:S(2)}) collective-permute-start(bf16[2,256,256]{2,1,0:T(8,128)(2,1)S(1)} %add_convert_fusion.1.refs_4_), channel_id=1, source_target_pairs={{0,1},{1,0},{2,3},{3,2},{4,5},{5,4},{6,7},{7,6},{8,9},{9,8},{10,11... | collective-permute-start | bytes 786440 | tf_op jit(solution)/shard_map/ppermute | solution.py:413
  58.7 6.0 %collective-permute-start.21 = (bf16[64,512]{1,0:T(8,128)(2,1)S(1)}, bf16[64,512]{1,0:T(8,128)(2,1)S(1)}, u32[]{:S(2)}, u32[]{:S(2)}) collective-permute-start(bf16[64,512]{1,0:T(8,128)(2,1)S(1)} %shard_map.91.refs_0_), channel_id=1, source_target_pairs={{0,5},{1,4},{2,7},{3,6},{4,1},{5,0},{6,3},{7,2},{8,13},{9,12},{10,... | collective-permute-start | bytes 196616 | tf_op jit(solution)/shard_map/ppermute | solution.py:338
  60.8 4.5 %collective-permute-start.20 = (bf16[64,512]{1,0:T(8,128)(2,1)S(1)}, bf16[64,512]{1,0:T(8,128)(2,1)S(1)}, u32[]{:S(2)}, u32[]{:S(2)}) collective-permute-start(bf16[64,512]{1,0:T(8,128)(2,1)S(1)} %shard_map.91.refs_0_), channel_id=1, source_target_pairs={{0,4},{1,5},{2,6},{3,7},{4,0},{5,1},{6,2},{7,3},{8,12},{9,13},{10,... | collective-permute-start | bytes 196616 | tf_op jit(solution)/shard_map/ppermute | solution.py:338
  61.8 5.0 %collective-permute-start.19 = (bf16[64,512]{1,0:T(8,128)(2,1)S(1)}, bf16[64,512]{1,0:T(8,128)(2,1)S(1)}, u32[]{:S(2)}, u32[]{:S(2)}) collective-permute-start(bf16[64,512]{1,0:T(8,128)(2,1)S(1)} %shard_map.91.refs_0_), channel_id=1, source_target_pairs={{0,1},{1,0},{2,3},{3,2},{4,5},{5,4},{6,7},{7,6},{8,9},{9,8},{10,11... | collective-permute-start | bytes 196616 | tf_op jit(solution)/shard_map/ppermute | solution.py:338
  62.3 9.0 %collective-permute-start.11 = (bf16[2,256,256]{2,1,0:T(8,128)(2,1)S(1)}, bf16[2,256,256]{2,1,0:T(8,128)(2,1)S(1)}, u32[]{:S(2)}, u32[]{:S(2)}) collective-permute-start(bf16[2,256,256]{2,1,0:T(8,128)(2,1)S(1)} %add_convert_fusion.refs_5_), channel_id=1, source_target_pairs={{0,1},{1,0},{2,3},{3,2},{4,5},{5,4},{6,7},{7,6},{8,9},{9,8},{10,11... | collective-permute-start | bytes 786440 | tf_op jit(solution)/shard_map/ppermute | solution.py:413
  66.8 5.4 %collective-permute-start.22 = (bf16[256,512]{1,0:T(8,128)(2,1)S(1)}, bf16[256,512]{1,0:T(8,128)(2,1)S(1)}, u32[]{:S(2)}, u32[]{:S(2)}) collective-permute-start(bf16[256,512]{1,0:T(8,128)(2,1)S(1)} %shard_map.92.refs_0_), channel_id=1, source_target_pairs={{0,2},{1,3},{2,0},{3,1},{4,6},{5,7},{6,4},{7,5},{8,10},{9,11},{10,... | collective-permute-start | bytes 786440 | tf_op jit(solution)/shard_map/ppermute | solution.py:338

commit v4 on v3

v4 whole, which is shorter than its diff:
```python
import math

import jax
import jax.numpy as jnp
import numpy as np
from jax import lax
from jax.experimental import pallas as pl
from jax.experimental.pallas import tpu as pltpu
from jax.sharding import PartitionSpec as P

GRID_ROWS = 4


fresnel_coeff = 0.25
object_rate = 0.05
probe_rate = 0.15

f32 = jnp.float32
bf16 = jnp.bfloat16


def from_behind(block, rows, cols):
    tiles = lax.axis_size("tile")
    across = tiles // GRID_ROWS

    def source(i):
        return (i // across - rows) % GRID_ROWS * across + (i % across - cols) % across

    return lax.ppermute(block, "tile", [(source(i), i) for i in range(tiles)])


def real_embed(part_re, part_im):
    upper_half = np.concatenate([part_re, -part_im], axis=1)
    lower_half = np.concatenate([part_im, part_re], axis=1)
    stacked = np.concatenate([upper_half, lower_half], axis=0)
    return jnp.asarray(stacked, dtype=f32).astype(bf16)


def build_tables(pixels):
    indices = np.arange(pixels)
    angles = indices[:, None] * indices[None, :] % pixels * (2.0 * math.pi / pixels)
    norm_scale = 1.0 / math.sqrt(pixels)
    dft_re = np.cos(angles) * norm_scale
    dft_im = -np.sin(angles) * norm_scale
    frequency = np.where(indices < pixels // 2, indices, indices - pixels)
    phases = -2.0 * math.pi * fresnel_coeff / pixels * (frequency * frequency)
    phase_sum = phases[:, None] + angles
    kern_re = np.sum(np.cos(phase_sum), axis=0) / pixels
    kern_im = np.sum(np.sin(phase_sum), axis=0) / pixels
    lag_index = (indices[:, None] - indices[None, :]) % pixels
    prop_re = kern_re[lag_index]
    prop_im = kern_im[lag_index]
    return real_embed(prop_re, prop_im), real_embed(dft_re, dft_im)


def dot(a, b):
    return jnp.dot(a, b, preferred_element_type=f32)


def shift_tables(offsets_ref, counts_ref, message_ref):
    n = message_ref.shape[1]
    sent = message_ref[n:, :].astype(f32)
    busy = counts_ref[0, 0] == offsets_ref.shape[2]
    row = jnp.where(busy, offsets_ref[0, 0, 0, 0], sent[0:1].astype(jnp.int32))
    col = jnp.where(busy, offsets_ref[0, 0, 0, 1], sent[1:2].astype(jnp.int32))
    i_out = lax.broadcasted_iota(jnp.int32, (n, 2 * n), 0)
    i_in = lax.broadcasted_iota(jnp.int32, (n, 2 * n), 1)
    j_in = lax.broadcasted_iota(jnp.int32, (2 * n, n), 0)
    j_out = lax.broadcasted_iota(jnp.int32, (2 * n, n), 1)
    row2 = jnp.concatenate([row, row], axis=1)
    col2 = jnp.concatenate([col, col], axis=1)
    rows = (i_in == i_out + row2).astype(f32).astype(bf16)
    cols = (j_in == j_out + col).astype(f32).astype(bf16)
    rows_t = (j_in == j_out + row).astype(f32).astype(bf16)
    cols_t = (i_in == i_out + col2).astype(f32).astype(bf16)
    return rows, cols, rows_t, cols_t, col, busy


def patch(shifts, own_ref, right_ref, below_ref, diag_ref, part):
    upper = jnp.concatenate([own_ref[part], right_ref[part]], axis=1)
    lower = jnp.concatenate([below_ref[part], diag_ref[part]], axis=1)
    rows = dot(shifts[0], jnp.concatenate([upper, lower], axis=0)).astype(bf16)
    return dot(rows, shifts[1])


def transform(table_ref, wave_re, wave_im):
    n = wave_re.shape[0]
    table = table_ref[...]
    wave = jnp.concatenate([wave_re.astype(bf16), wave_im.astype(bf16)], axis=0)
    first = dot(table, wave)
    first = jnp.concatenate([first[:n].astype(bf16), (-first[n:]).astype(bf16)], axis=1)
    out = dot(first, table)
    return out[:, :n], out[:, n:]


def probe_plane(probe_ref, part, mode, modes):
    lane_tiles = 2
    n = probe_ref.shape[0] // (2 * lane_tiles * modes)
    step = lane_tiles * modes
    halves = [
        probe_ref[pl.ds(part * n * step + tile * modes + mode, n, stride=step), :]
        for tile in range(lane_tiles)
    ]
    return jnp.concatenate(halves, axis=1)


def ready_kernel(tile_ref, probe_ref, prop_ref, own_ref, planes_ref, table_ref):
    own_ref[...] = tile_ref[0, 1]
    table_ref[...] = prop_ref[...]
    n = planes_ref.shape[1]
    modes = planes_ref.shape[2] // n
    for part in range(2):
        for mode in range(modes):
            planes_ref[part, :, pl.ds(mode * n, n)] = probe_plane(probe_ref, part, mode, modes)


def arrive_kernel(
    offsets_ref, counts_ref, message_ref, own_ref, right_ref, below_ref, diag_ref, planes_ref,
    prop_ref, near_ref, arrive_ref,
):
    n = own_ref.shape[1]
    shifts = shift_tables(offsets_ref, counts_ref, message_ref)
    tiles = (own_ref, right_ref.at[0], below_ref, diag_ref)
    near = [patch(shifts, *tiles, part) for part in range(2)]
    for part in range(2):
        near_ref[part] = near[part].astype(bf16)
    for mode in range(planes_ref.shape[2] // n):
        lanes = pl.ds(mode * n, n)
        p_re, p_im = planes_ref[0, :, lanes], planes_ref[1, :, lanes]
        a_re, a_neg = transform(
            prop_ref, p_re * near[0] - p_im * near[1], p_re * near[1] + p_im * near[0]
        )
        arrive_ref[0, :, lanes] = a_re
        arrive_ref[1, :, lanes] = -a_neg


def spread(shifts, grad, home_ref, next_ref, down_ref):
    rows_t, cols_t, col = shifts[2:5]
    n = rows_t.shape[1]
    wrap_cols = cols_t[:, :n] + cols_t[:, n:]
    for part in range(2):
        rows = dot(rows_t, grad[part].astype(bf16)).astype(bf16)
        wide = dot(rows[:n], cols_t).astype(bf16)
        home_ref[part] = wide[:, :n]
        next_ref[part] = wide[:, n:]
        down_ref[pl.ds(part * n, n), :] = dot(rows[n:], wrap_cols).astype(bf16)
    edge = lax.broadcasted_iota(jnp.int32, (16, n), 1) < col
    down_ref[pl.ds(2 * n, 16), :] = edge.astype(f32).astype(bf16)


def gradient_kernel(
    offsets_ref, counts_ref, message_ref, own_ref, right_ref, below_ref, diag_ref, near_ref,
    arrive_ref, planes_ref, patterns_ref, prop_ref, dft_ref,
    home_ref, next_ref, down_ref, grad_ref, keep_ref, give_ref, term_ref,
):
    n = own_ref.shape[1]
    modes = planes_ref.shape[2] // n
    shifts = shift_tables(offsets_ref, counts_ref, message_ref)
    busy = shifts[5]
    tiles = (own_ref, right_ref.at[1], below_ref, diag_ref)
    far = [patch(shifts, *tiles, part) for part in range(2)]
    fields = []
    for mode in range(modes):
        lanes = pl.ds(mode * n, n)
        a_re, a_im = arrive_ref[0, :, lanes], arrive_ref[1, :, lanes]
        fields.append(
            transform(dft_ref, far[0] * a_re - far[1] * a_im, far[0] * a_im + far[1] * a_re)
        )
    intensity = sum(f_re * f_re + f_neg * f_neg for f_re, f_neg in fields)
    pattern = jnp.where(busy, patterns_ref[0, 0, 0].astype(f32), message_ref[:n, :].astype(f32))
    residual = intensity - pattern
    grad_far = [0.0, 0.0]
    waves = []
    for mode in range(modes):
        lanes = pl.ds(mode * n, n)
        f_re, f_neg = fields[mode]
        a_re, a_im = arrive_ref[0, :, lanes], arrive_ref[1, :, lanes]
        b_re, b_im = transform(dft_ref, f_re * residual, f_neg * residual)
        grad_far[0] += a_re * b_re + a_im * b_im
        grad_far[1] += a_re * b_im - a_im * b_re
        waves.append((far[0] * b_re + far[1] * b_im, far[1] * b_re - far[0] * b_im))
    grad_near = [0.0, 0.0]
    near = [near_ref[part].astype(f32) for part in range(2)]
    for mode in range(modes):
        lanes = pl.ds(mode * n, n)
        b_re, b_im = transform(prop_ref, *waves[mode])
        p_re, p_im = planes_ref[0, :, lanes], planes_ref[1, :, lanes]
        grad_near[0] += p_re * b_re + p_im * b_im
        grad_near[1] += p_re * b_im - p_im * b_re
        term_ref[0, :, lanes] = (near[0] * b_re + near[1] * b_im).astype(bf16)
        term_ref[1, :, lanes] = (near[0] * b_im - near[1] * b_re).astype(bf16)
    core = place_of(core_group())
    keep_ref[...] = term_ref[core]
    give_ref[...] = term_ref[1 - core]
    for part in range(2):
        grad_ref[part] = grad_near[part].astype(bf16)
    spread(shifts, grad_far, home_ref, next_ref, down_ref)


def spread_kernel(offsets_ref, counts_ref, message_ref, grad_ref, home_ref, next_ref, down_ref):
    shifts = shift_tables(offsets_ref, counts_ref, message_ref)
    spread(shifts, [grad_ref[part] for part in range(2)], home_ref, next_ref, down_ref)


def beside_kernel(next_ref, above_ref, out_ref):
    n = out_ref.shape[1]
    split = above_ref[pl.ds(2 * n, 16), :].astype(f32)[0:1] > 0
    for part in range(2):
        above = above_ref[pl.ds(part * n, n), :].astype(f32)
        total = next_ref[part].astype(f32) + jnp.where(split, above, 0.0)
        out_ref[part] = total.astype(bf16)


def part_kernel(home_ref, above_ref, left_ref, out_ref):
    n = out_ref.shape[1]
    split = above_ref[pl.ds(2 * n, 16), :].astype(f32)[0:1] > 0
    for part in range(2):
        above = above_ref[pl.ds(part * n, n), :].astype(f32)
        total = home_ref[part].astype(f32) + jnp.where(split, 0.0, above)
        out_ref[part] = (total + left_ref[part].astype(f32)).astype(bf16)


def update_kernel(layer, own_ref, part_ref, other_ref, *refs):
    out_hbm, new_ref, sem = refs[-3:]
    grad = part_ref[...].astype(f32) + other_ref[...].astype(f32)
    new_ref[...] = (own_ref[...].astype(f32) - object_rate * grad).astype(bf16)
    copy = pltpu.make_async_copy(new_ref, out_hbm.at[0, layer], sem.at[0])
    copy.start()
    copy.wait()


def core_group():
    return [lax.axis_size("pos")]


def place_of(group):
    flat = lax.axis_index("tile") * lax.axis_size("pos") + lax.axis_index("pos")
    return sum(flat // mask % 2 * (1 << at) for at, mask in enumerate(group))


def job(kernel, outs, arrays, scalars=(), scratch=()):
    return kernel, list(outs), list(scalars), list(arrays), list(scratch)


def run(*jobs, flops=1_000_000, limit=4, after=()):
    vmem = pl.BlockSpec(memory_space=pltpu.VMEM)
    smem = pl.BlockSpec(memory_space=pltpu.SMEM)
    anywhere = pl.BlockSpec(memory_space=pl.ANY)
    kernels, outs, scalars, arrays, scratch = zip(*jobs)
    ins = [x + y for x, y in zip(scalars, arrays)]
    specs = [[smem] * len(x) + [vmem] * len(y) for x, y in zip(scalars, arrays)]

    def taken(refs, lists):
        parts = []
        for items in lists:
            parts.append(refs[: len(items)])
            refs = refs[len(items) :]
        return parts, refs

    def body(*refs):
        in_refs, refs = taken(refs, ins)
        out_refs, refs = taken(refs[len(after) :], outs)
        scratch_refs, _ = taken(refs, scratch)
        for kernel, *parts in zip(kernels, in_refs, out_refs, scratch_refs):
            kernel(*parts[0], *parts[1], *parts[2])

    moved = sum(x.size * x.dtype.itemsize for x in sum(ins, []) + sum(outs, []))
    results = pl.pallas_call(
        body,
        out_shape=sum(outs, []),
        in_specs=sum(specs, []) + [anywhere] * len(after),
        out_specs=[vmem] * len(sum(outs, [])),
        scratch_shapes=sum(scratch, []),
        compiler_params=pltpu.CompilerParams(vmem_limit_bytes=limit * 2**20),
        cost_estimate=pl.CostEstimate(flops=flops, bytes_accessed=moved, transcendentals=0),
    )(*sum(ins, []), *after)
    results, _ = taken(results, outs)
    return results[0] if len(jobs) == 1 else results


def updated(layer, own, part, other, like, so_far, after):
    vmem = pl.BlockSpec(memory_space=pltpu.VMEM)
    anywhere = pl.BlockSpec(memory_space=pl.ANY)
    extra = [x for x in (so_far,) if x is not None] + list(after)
    return pl.pallas_call(
        lambda *refs: update_kernel(layer, *refs),
        out_shape=like,
        in_specs=[vmem] * 3 + [anywhere] * len(extra),
        out_specs=pl.BlockSpec(memory_space=pl.ANY),
        scratch_shapes=[pltpu.VMEM(own.shape, bf16), pltpu.SemaphoreType.DMA((1,))],
        input_output_aliases={} if so_far is None else {3: 0},
        compiler_params=pltpu.CompilerParams(vmem_limit_bytes=4 * 2**20),
        cost_estimate=pl.CostEstimate(
            flops=own.size, bytes_accessed=8 * own.size, transcendentals=0
        ),
    )(own, part, other, *extra)


def shape_of(kind, *dims):
    return jax.ShapeDtypeStruct(dims, kind)


def handed_over(patterns, offsets, counts):
    owners = lax.axis_size("pos")
    slots, pixels = patterns.shape[2], patterns.shape[4]

    def message(pattern, spot):
        at = lax.broadcasted_iota(jnp.int32, (16, pixels), 0)
        rows = jnp.where(at == 0, spot[0], jnp.where(at == 1, spot[1], 0))
        return jnp.concatenate([pattern, rows.astype(bf16)], axis=0)

    if owners == slots:
        sent = message(patterns[0, 0, 1], offsets[0, 0, 1])
        return sent, lax.ppermute(sent, "pos", [(i, 1 - i) for i in range(2)]), counts
    all_counts = lax.all_gather(counts[0, 0], "pos")
    ends = jnp.cumsum(all_counts)
    rank = lax.axis_index("pos")
    source = jnp.sum((ends <= rank).astype(jnp.int32))
    slot = rank - (ends[source] - all_counts[source])
    spot = lax.all_gather(offsets[0, 0], "pos")[source, slot]
    pattern = lax.all_gather(patterns[0, 0], "pos")[source, slot]
    sent = message(pattern, spot)
    return sent, sent, jnp.zeros_like(counts)


def fold_kernel(group, keep_ref, *refs):
    blocks = refs[-1]
    got = len(refs) - 1 - blocks.shape[0]
    arrived, keep_out, give_outs = refs[:got], refs[got], refs[got + 1 : -1]
    total = keep_ref[...].astype(f32)
    for ref in arrived:
        total += ref[...].astype(f32)
    size = blocks.shape[1]
    for block in range(blocks.shape[0]):
        blocks[block] = total[block * size : (block + 1) * size]
    here = place_of(group)
    keep_out[...] = blocks[here]
    for distance, ref in enumerate(give_outs, 1):
        ref[...] = blocks[here ^ distance].astype(bf16)


def add_kernel(keep_ref, *refs):
    total = keep_ref[...].astype(f32)
    for ref in refs[:-1]:
        total += ref[...].astype(f32)
    refs[-1][...] = total.astype(bf16)


def place_kernel(group, add, *refs):
    arrived, out_ref, blocks = refs[:-2], refs[-2], refs[-1]
    here = place_of(group)
    for distance, ref in enumerate(arrived):
        blocks[here ^ distance] = ref[...]
    size = blocks.shape[1]
    if add:
        total = blocks[0].astype(f32)
        for block in range(1, blocks.shape[0]):
            total += blocks[block].astype(f32)
        out_ref[...] = total.astype(bf16)
    else:
        for block in range(blocks.shape[0]):
            out_ref[pl.ds(block * size, size), :] = blocks[block]


def probe_kernel(step, modes, mine_ref, other_ref, probe_ref, out_ref):
    core = place_of(core_group())
    lane_tiles = 2
    n = mine_ref.shape[0]
    stride = lane_tiles * modes
    for part in range(2):
        total = jnp.where(core == part, mine_ref[...].astype(f32), other_ref[...].astype(f32))
        for mode in range(modes):
            for tile in range(lane_tiles):
                lane = (mode * lane_tiles + tile) * 128
                where = pl.ds(part * n * stride + tile * modes + mode, n, stride=stride)
                out_ref[where, :] = probe_ref[where, :] - step * total[:, lane : lane + 128]


def exchange_groups():
    tiles, owners = lax.axis_size("tile"), lax.axis_size("pos")
    bits = [1 << bit for bit in range(owners.bit_length() - 1)]
    bits += [owners << bit for bit in range(1, tiles.bit_length() - 1)]
    return [bits[at : at + 2] for at in range(0, len(bits), 2)]


def swap_with(x, group, distance):
    mask = sum(bit for at, bit in enumerate(group) if distance >> at & 1)
    devices = lax.axis_size("tile") * lax.axis_size("pos")
    return lax.ppermute(x, ("tile", "pos"), [(i, i ^ mask) for i in range(devices)])


def joined(group, x, add):
    blocks = 1 << len(group)
    arrived = [x] + [swap_with(x, group, at) for at in range(1, blocks)]
    return job(
        lambda *refs: place_kernel(group, add, *refs),
        [shape_of(bf16, x.shape[0] * (1 if add else blocks), x.shape[1])],
        arrived,
        scratch=[pltpu.VMEM((blocks,) + x.shape, bf16)],
    )


def folded(group, keep, arrived):
    blocks = 1 << len(group)
    size, width = keep.shape[0] // blocks, keep.shape[1]
    return job(
        lambda *refs: fold_kernel(group, *refs),
        [shape_of(f32, size, width)] + [shape_of(bf16, size, width)] * (blocks - 1),
        [keep] + arrived,
        scratch=[pltpu.VMEM((blocks, size, width), f32)],
    )


def shards(tile_object, probe_modes, patterns, offsets, counts):
    _, pixels, modes, _ = probe_modes.shape
    width = modes * pixels
    lane_tiles = pixels // 128
    prop, dft = build_tables(pixels)
    tile = shape_of(bf16, 2, pixels, pixels)
    planes = shape_of(f32, 2, pixels, width)
    probe = probe_modes.reshape(2, pixels, modes, lane_tiles, 128)
    probe = probe.transpose(0, 1, 3, 2, 4).reshape(-1, 128)

    own0 = tile_object[0, 0]
    below0 = from_behind(own0, -1, 0)
    right = from_behind(tile_object[0], 0, -1)
    sent, message, counts = handed_over(patterns, offsets, counts)
    own1, probe_planes, table = run(
        job(ready_kernel, [tile, planes, shape_of(bf16, *prop.shape)], [tile_object, probe, prop]),
        limit=16,
        after=[own0, sent],
    )
    below1 = from_behind(own1, -1, 0)
    diag0 = from_behind(below0, 0, -1)
    diag1 = from_behind(below1, 0, -1)
    near, arrive = run(
        job(
            arrive_kernel,
            [tile, planes],
            [message, own0, right, below0, diag0, probe_planes, table],
            scalars=[offsets, counts],
        ),
        flops=1_500_000_000,
        limit=16,
    )
    half = shape_of(bf16, pixels, width)
    down = shape_of(bf16, 2 * pixels + 16, pixels)
    home1, next1, down1, grad0, keep, give = run(
        job(
            gradient_kernel,
            [tile, tile, down, tile, half, half],
            [message, own1, right, below1, diag1, near, arrive, probe_planes, patterns, table, dft],
            scalars=[offsets, counts],
            scratch=[pltpu.VMEM((2, pixels, width), bf16)],
        ),
        flops=4_000_000_000,
        limit=16,
    )

    core, groups = core_group(), exchange_groups()
    above1 = from_behind(down1, 1, 0)
    arrived = [swap_with(give, core, 1)]
    side = [
        job(
            spread_kernel,
            [tile, tile, down],
            [message, grad0],
            scalars=[offsets, counts],
        )
    ]
    scattered = []
    while len(groups) > 1 and keep.shape[0] >> len(groups[0]) >= 16:
        group, groups = groups[0], groups[1:]
        done = run(folded(group, keep, arrived), *side, limit=8)
        if side:
            done, (home0, next0, down0) = done
            above0 = from_behind(down0, 1, 0)
            side = []
        keep, *gives = done
        arrived = [swap_with(x, group, at) for at, x in enumerate(gives, 1)]
        scattered.append(group)
    (beside1,), (total,) = run(
        job(beside_kernel, [tile], [next1, above1]),
        job(add_kernel, [shape_of(bf16, *keep.shape)], [keep] + arrived),
    )
    from_left1 = from_behind(beside1, 0, 1)
    (beside0,) = run(job(beside_kernel, [tile], [next0, above0]), after=[total])
    from_left0 = from_behind(beside0, 0, 1)
    (total,), (part1,) = run(
        joined(groups[0], total, True),
        job(part_kernel, [tile], [home1, above1, from_left1]),
        after=[beside0],
    )
    for group in groups[1:]:
        (total,) = run(joined(group, total, True))

    def from_owners(part):
        if lax.axis_size("pos") == 2:
            return lax.ppermute(part, "pos", [(0, 1), (1, 0)])
        return lax.psum(part.astype(f32), "pos") - part.astype(f32)

    other1 = from_owners(part1)
    (total,), (part0,) = run(
        joined(scattered[-1], total, False),
        job(part_kernel, [tile], [home0, above0, from_left0]),
    )
    other0 = from_owners(part0)
    for group in reversed(scattered[:-1]):
        (total,) = run(joined(group, total, False))
    other_half = swap_with(total, core, 1)
    positions_all = lax.axis_size("tile") * lax.axis_size("pos") * (patterns.shape[2] // 2)
    step = probe_rate / math.sqrt(positions_all)
    like = shape_of(bf16, *tile_object.shape)
    new_object = updated(1, own1, part1, other1, like, None, [])
    (new_probe,) = run(
        job(
            lambda *refs: probe_kernel(step, modes, *refs),
            [shape_of(f32, *probe.shape)],
            [total, other_half, probe],
        ),
        limit=8,
    )
    new_object = updated(0, own0, part0, other0, like, new_object, [new_probe])
    new_probe = new_probe.reshape(2, pixels, lane_tiles, modes, 128).transpose(0, 1, 3, 2, 4)
    return (new_object, new_probe.reshape(probe_modes.shape))


def solution(mesh):
    placed = (
        P("tile", None, None, None, None),
        P(),
        P("tile", "pos", None, None, None),
        P("tile", "pos", None, None),
        P("tile", "pos"),
    )
    return jax.shard_map(
        shards,
        mesh=mesh,
        in_specs=placed,
        out_specs=(P("tile", None, None, None, None), P()),
        check_vma=False,
    )
```

time: 73.7 us -> 78.3 us (1.062)
  local copies, waits for them, and re-layouts: 3.3 us -> 7.3 us
  Pallas kernels: 10.8 us -> 12.2 us
    ppermute x9, waiting for transfers between devices: 19.5 us -> 15.4 us  [from_behind(): return lax.ppermute(block, 'tile', [(source(i), i) for i in range(tiles)])]
    ppermute x11, waiting for transfers between devices: 6.34 us -> 8.76 us  [swap_with(): lax.ppermute(x, ('tile', 'pos'), [(i, i ^ mask) for i in range(devices)])]
    squeeze x0 -> x2, local copies, waits for them, and re-layouts: none -> 1.97 us  [the longest x1 1.06 us: shards(): own0 = tile_object[0, 0]]
    ppermute x3, waiting for transfers between devices: 5.41 us -> 7.06 us  [the longest x2 7.06 us: from_owners(): return lax.ppermute(part, 'pos', [(0, 1), (1, 0)])]
    pallas_call x8 -> x11, Pallas kernels: 10.8 us -> 12.2 us  [the longest x9 10.6 us: run(): pl.pallas_call(body, out_shape=sum(outs, []), in_specs=sum(specs, []) + [...]
    slice x2 -> x1, local copies, waits for them, and re-layouts: 0.04 us -> 1.34 us  [message(): rows = jnp.where(at == 0, spot[0], jnp.where(at == 1, spot[1], 0))]
    ppermute x11, starting transfers between devices: 11.6 us -> 12.7 us  [swap_with(): lax.ppermute(x, ('tile', 'pos'), [(i, i ^ mask) for i in range(devices)])]
    ppermute x9, starting transfers between devices: 8.86 us -> 7.93 us  [from_behind(): return lax.ppermute(block, 'tile', [(source(i), i) for i in range(tiles)])]
  transfers between devices with their start and end apart: 23 -> 23, of which waited for: 11 -> 12; matrix products, arithmetic and copies ran while one was open for 2% -> 5% of each run, Pallas kernels for 6% -> 8%
where the time goes in v4:
time: 78.3 us; the launch traced here: 77.9 us
  waiting for transfers between devices  31.2 us (40%)
  starting transfers between devices  24.4 us (31%)
  Pallas kernels  12.2 us (16%)
  local copies, waits for them, and re-layouts  7.3 us (9%)
  between operations  1.47 us (2%)
  other arithmetic  1.38 us (2%)
    ppermute x9, waiting for transfers between devices, from_behind(): return lax.ppermute(block, 'tile', [(source(i), i) for i in range(tiles)])  15.4 us
    ppermute x11, starting transfers between devices, swap_with(): lax.ppermute(x, ('tile', 'pos'), [(i, i ^ mask) for i in range(devices)])  12.7 us
    pallas_call x9, Pallas kernels, run(): pl.pallas_call(body, out_shape=sum(outs, []), in_specs=sum(specs, []) + [...  10.6 us
    ppermute x11, waiting for transfers between devices, swap_with(): lax.ppermute(x, ('tile', 'pos'), [(i, i ^ mask) for i in range(devices)])  8.76 us
    ppermute x9, starting transfers between devices, from_behind(): return lax.ppermute(block, 'tile', [(source(i), i) for i in range(tiles)])  7.93 us
    ppermute x2, waiting for transfers between devices, from_owners(): return lax.ppermute(part, 'pos', [(0, 1), (1, 0)])  7.06 us
    unnamed x14, local copies, waits for them, and re-layouts  3.99 us
    ppermute x2, starting transfers between devices, from_owners(): return lax.ppermute(part, 'pos', [(0, 1), (1, 0)])  2.25 us
  transfers between devices with their start and end apart: 23, of which 12 were waited for; matrix products, arithmetic and copies ran while one was open for 5% of the time, Pallas kernels for 8%

profile of v4, /device:TPU:0, one launch (start us, length us, event | category | flops | bytes accessed | tf_op | source)
XLA Modules:
  0.0 77.9 jit_solution(11364396467009901418)
XLA Ops:
  0.6 1.1 %slice_bitcast_fusion.refs_3_.refs_0_ = bf16[2,256,256]{2,1,0:T(8,128)(2,1)S(1)} fusion(bf16[1,2,2,256,256]{4,3,2,1,0:T(8,128)(2,1)} %refs_0_.3), kind=kLoop, calls=%fused_computation | loop fusion | bytes 524288 | tf_op jit(solution)/shard_map/squeeze | solution.py:424
  1.7 5.1 %collective-permute-start.4 = (bf16[2,256,256]{2,1,0:T(8,128)(2,1)S(1)}, bf16[2,256,256]{2,1,0:T(8,128)(2,1)S(1)}, u32[]{:S(2)}, u32[]{:S(2)}) collective-permute-start(bf16[2,256,256]{2,1,0:T(8,128)(2,1)S(1)} %slice_bitcast_fusion.refs_3_.refs_0_), channel_id=1, source_target_pairs={{8,0},{10,2},{12,4},{14,6},{16,8},{18,10},{20,12},{22,14},{24,16},... | collective-permute-start | bytes 786440 | tf_op jit(solution)/shard_map/ppermute | solution.py:29
  6.8 0.7 collective-permute-start.1
  7.5 1.3 %fusion = (s32[1,1,1,1]{3,2,1,0:T(1,128)}, s32[1,1,1,1]{3,2,1,0:T(1,128)}) fusion(s32[1,1,2,2]{3,2,1,0:T(2,128)} %refs_2_.1), kind=kLoop, calls=%fused_computation.6 | loop fusion | bytes 16 | tf_op jit(solution)/shard_map/slice | solution.py:309
  8.8 0.6 compare_select_fusion
  9.4 0.9 %slice_bitcast_fusion.1 = bf16[256,256]{1,0:T(8,128)(2,1)S(1)} fusion(bf16[1,1,2,256,256]{4,3,2,1,0:T(8,128)(2,1)} %refs_10_.1), kind=kLoop, calls=%fused_computation.2 | loop fusion | bytes 262144 | tf_op jit(solution)/shard_map/squeeze | solution.py:313
  10.4 0.7 select_convert_fusion
  11.1 1.0 %copy-done.2 = bf16[1,2,2,256,256]{4,3,2,1,0:T(8,128)(2,1)S(1)} copy-done((bf16[1,2,2,256,256]{4,3,2,1,0:T(8,128)(2,1)S(1)}, bf16[1,2,2,256,256]{4,3,2,1,0:T(8,128)(2,1)}, u32[]{:S(2)}) %copy-start.2) | copy-done | bytes 524312
  12.2 1.0 %copy-done.3 = bf16[512,512]{1,0:T(8,128)(2,1)S(1)} copy-done((bf16[512,512]{1,0:T(8,128)(2,1)S(1)}, bf16[512,512]{1,0:T(8,128)(2,1)}, u32[]{:S(2)}) %copy-start.3) | copy-done | bytes 524312
  13.2 0.1 shard_map.86
  13.3 0.5 collective-permute-start.2
  13.8 0.7 collective-permute-start.5
  14.5 1.5 %collective-permute-start = (bf16[272,256]{1,0:T(8,128)(2,1)S(1)}, bf16[272,256]{1,0:T(8,128)(2,1)S(1)}, u32[]{:S(2)}, u32[]{:S(2)}) collective-permute-start(bf16[272,256]{1,0:T(8,128)(2,1)S(1)} %pad_maximum_fusion.refs_4_), channel_id=1, source_target_pairs={{0,1},{1,0},{2,3},{3,2},{4,5},{5,4},{6,7},{7,6},{8,9},{9,8},{10,11... | collective-permute-start | bytes 417800 | tf_op jit(solution)/shard_map/ppermute | solution.py:314
  16.0 5.4 %collective-permute-done.2.refs_5_ = bf16[2,256,256]{2,1,0:T(8,128)(2,1)S(1)} collective-permute-done((bf16[2,256,256]{2,1,0:T(8,128)(2,1)S(1)}, bf16[2,256,256]{2,1,0:T(8,128)(2,1)S(1)}, u32[]{:S(2)}, u32[]{:S(2)}) %collective-permute-start.2) | collective-permute-done | bytes 262176 | tf_op jit(solution)/shard_map/ppermute | solution.py:29
  21.4 0.8 %collective-permute-start.3 = (bf16[2,256,256]{2,1,0:T(8,128)(2,1)S(1)}, bf16[2,256,256]{2,1,0:T(8,128)(2,1)S(1)}, u32[]{:S(2)}, u32[]{:S(2)}) collective-permute-start(bf16[2,256,256]{2,1,0:T(8,128)(2,1)S(1)} %collective-permute-done.2.refs_5_), channel_id=1, source_target_pairs={{2,0},{4,2},{6,4},{0,6},{10,8},{12,10},{14,12},{8,14},{18,16},{20,... | collective-permute-start | bytes 786440 | tf_op jit(solution)/shard_map/ppermute | solution.py:29
  23.0 0.7 copy-done.5
  23.6 2.3 %shard_map.87 = (bf16[2,256,256]{2,1,0:T(8,128)(2,1)S(1)}, f32[2,256,512]{2,1,0:T(8,128)S(1)}) custom-call(s32[1,1,2,2]{3,2,1,0:T(2,128)S(1)} %copy-done.5, s32[1,1]{1,0:T(1,128)S(6)} %copy.13.refs_1_.refs_3_, bf16[272,256]{1,0:T(8,128)(2,1)S(1)} %collective-permute-done.refs_2_.refs_4_, bf16[2,256,256]{2,1,0:T(8,128)(2,1)S(1)} %slice_bitcast_fusion.refs_3_.refs_0_, ...), custom_call_target="tpu_custom_call" | custom-call | flops 1500000000 | bytes 4333588 | tf_op jit(solution)/shard_map/pallas_call | solution.py:268
  26.0 0.2 collective-permute-done.3.refs_6_
  26.2 5.0 %shard_map.88 = (bf16[2,256,256]{2,1,0:T(8,128)(2,1)S(1)}, bf16[2,256,256]{2,1,0:T(8,128)(2,1)S(1)}, bf16[528,256]{1,0:T(8,128)(2,1)S(1)}, bf16[2,256,256]{2,1,0...) custom-call(s32[1,1,2,2]{3,2,1,0:T(2,128)S(1)} %copy-done.5, ...), custom_call_target="tpu_custom_call" | custom-call | flops 4000000000 | bytes 6701076 | tf_op jit(solution)/shard_map/pallas_call | solution.py:268
  31.2 1.0 %collective-permute-start.7 = (bf16[256,512]{1,0:T(8,128)(2,1)S(1)}, bf16[256,512]{1,0:T(8,128)(2,1)S(1)}, u32[]{:S(2)}, u32[]{:S(2)}) collective-permute-start(bf16[256,512]{1,0:T(8,128)(2,1)S(1)} %get-tuple-element.34), channel_id=1, source_target_pairs={{0,2},{1,3},{2,0},{3,1},{4,6},{5,7},{6,4},{7,5},{8,10},{9,11},{10,... | collective-permute-start | bytes 786440 | tf_op jit(solution)/shard_map/ppermute | solution.py:389
  32.2 1.2 %collective-permute-done.7.refs_1_ = bf16[256,512]{1,0:T(8,128)(2,1)S(1)} collective-permute-done((bf16[256,512]{1,0:T(8,128)(2,1)S(1)}, bf16[256,512]{1,0:T(8,128)(2,1)S(1)}, u32[]{:S(2)}, u32[]{:S(2)}) %collective-permute-start.7) | collective-permute-done | bytes 262176 | tf_op jit(solution)/shard_map/ppermute | solution.py:389
  33.4 1.3 %shard_map.89 = (f32[64,512]{1,0:T(8,128)S(1)}, bf16[64,512]{1,0:T(8,128)(2,1)S(1)}, bf16[64,512]{1,0:T(8,128)(2,1)S(1)}, bf16[64,512]{1,0:T(8,128)(2,1)S(1)}, b...) custom-call(bf16[256,512]{1,0:T(8,128)(2,1)S(1)} %get-tuple-element.33.refs_0_, ...), custom_call_target="tpu_custom_call" | custom-call | flops 1000000 | bytes 2048020 | tf_op jit(solution)/shard_map/pallas_call | solution.py:268
  34.7 1.6 %collective-permute-start.8 = (bf16[64,512]{1,0:T(8,128)(2,1)S(1)}, bf16[64,512]{1,0:T(8,128)(2,1)S(1)}, u32[]{:S(2)}, u32[]{:S(2)}) collective-permute-start(bf16[64,512]{1,0:T(8,128)(2,1)S(1)} %get-tuple-element.37), channel_id=1, source_target_pairs={{0,1},{1,0},{2,3},{3,2},{4,5},{5,4},{6,7},{7,6},{8,9},{9,8},{10,11... | collective-permute-start | bytes 196616 | tf_op jit(solution)/shard_map/ppermute | solution.py:389
  36.3 1.4 %collective-permute-start.9 = (bf16[64,512]{1,0:T(8,128)(2,1)S(1)}, bf16[64,512]{1,0:T(8,128)(2,1)S(1)}, u32[]{:S(2)}, u32[]{:S(2)}) collective-permute-start(bf16[64,512]{1,0:T(8,128)(2,1)S(1)} %get-tuple-element.38), channel_id=1, source_target_pairs={{0,4},{1,5},{2,6},{3,7},{4,0},{5,1},{6,2},{7,3},{8,12},{9,13},{10,... | collective-permute-start | bytes 196616 | tf_op jit(solution)/shard_map/ppermute | solution.py:389
  37.7 0.6 collective-permute-start.10
  38.3 5.0 %collective-permute-done.6.refs_1_.refs_5_ = bf16[528,256]{1,0:T(8,128)(2,1)S(1)} collective-permute-done((bf16[528,256]{1,0:T(8,128)(2,1)S(1)}, bf16[528,256]{1,0:T(8,128)(2,1)S(1)}, u32[]{:S(2)}, u32[]{:S(2)}) %collective-permute-start.6) | collective-permute-done | bytes 270368 | tf_op jit(solution)/shard_map/ppermute | solution.py:29
  43.3 0.1 shard_map.90
  43.5 4.7 %collective-permute-done.15.refs_1_.refs_5_ = bf16[528,256]{1,0:T(8,128)(2,1)S(1)} collective-permute-done((bf16[528,256]{1,0:T(8,128)(2,1)S(1)}, bf16[528,256]{1,0:T(8,128)(2,1)S(1)}, u32[]{:S(2)}, u32[]{:S(2)}) %collective-permute-start.15) | collective-permute-done | bytes 270368 | tf_op jit(solution)/shard_map/ppermute | solution.py:29
  48.4 0.5 collective-permute-start.13
  48.9 3.9 %collective-permute-start.11 = (bf16[64,512]{1,0:T(8,128)(2,1)S(1)}, bf16[64,512]{1,0:T(8,128)(2,1)S(1)}, u32[]{:S(2)}, u32[]{:S(2)}) collective-permute-start(bf16[64,512]{1,0:T(8,128)(2,1)S(1)} %get-tuple-element.40.refs_2_.refs_0_), channel_id=1, source_target_pairs={{0,8},{1,9},{2,10},{3,11},{4,12},{5,13},{6,14},{7,15},{8,0},{9,1},... | collective-permute-start | bytes 196616 | tf_op jit(solution)/shard_map/ppermute | solution.py:389
  52.8 2.2 %collective-permute-done.13.refs_3_ = bf16[64,512]{1,0:T(8,128)(2,1)S(1)} collective-permute-done((bf16[64,512]{1,0:T(8,128)(2,1)S(1)}, bf16[64,512]{1,0:T(8,128)(2,1)S(1)}, u32[]{:S(2)}, u32[]{:S(2)}) %collective-permute-start.13) | collective-permute-done | bytes 65568 | tf_op jit(solution)/shard_map/ppermute | solution.py:389
  55.0 2.4 %collective-permute-done.12.refs_2_ = bf16[64,512]{1,0:T(8,128)(2,1)S(1)} collective-permute-done((bf16[64,512]{1,0:T(8,128)(2,1)S(1)}, bf16[64,512]{1,0:T(8,128)(2,1)S(1)}, u32[]{:S(2)}, u32[]{:S(2)}) %collective-permute-start.12) | collective-permute-done | bytes 65568 | tf_op jit(solution)/shard_map/ppermute | solution.py:389
  57.5 0.2 shard_map.92
  57.7 2.0 %collective-permute-start.18 = (bf16[64,512]{1,0:T(8,128)(2,1)S(1)}, bf16[64,512]{1,0:T(8,128)(2,1)S(1)}, u32[]{:S(2)}, u32[]{:S(2)}) collective-permute-start(bf16[64,512]{1,0:T(8,128)(2,1)S(1)} %get-tuple-element.45.refs_0_), channel_id=1, source_target_pairs={{0,5},{1,4},{2,7},{3,6},{4,1},{5,0},{6,3},{7,2},{8,13},{9,12},{10,... | collective-permute-start | bytes 196616 | tf_op jit(solution)/shard_map/ppermute | solution.py:389
  59.7 1.1 %collective-permute-start.17 = (bf16[64,512]{1,0:T(8,128)(2,1)S(1)}, bf16[64,512]{1,0:T(8,128)(2,1)S(1)}, u32[]{:S(2)}, u32[]{:S(2)}) collective-permute-start(bf16[64,512]{1,0:T(8,128)(2,1)S(1)} %get-tuple-element.45.refs_0_), channel_id=1, source_target_pairs={{0,4},{1,5},{2,6},{3,7},{4,0},{5,1},{6,2},{7,3},{8,12},{9,13},{10,... | collective-permute-start | bytes 196616 | tf_op jit(solution)/shard_map/ppermute | solution.py:389
  60.7 0.5 collective-permute-start.16
  61.2 1.5 %collective-permute-start.21 = (bf16[2,256,256]{2,1,0:T(8,128)(2,1)S(1)}, bf16[2,256,256]{2,1,0:T(8,128)(2,1)S(1)}, u32[]{:S(2)}, u32[]{:S(2)}) collective-permute-start(bf16[2,256,256]{2,1,0:T(8,128)(2,1)S(1)} %get-tuple-element.48.refs_1_), channel_id=1, source_target_pairs={{0,1},{1,0},{2,3},{3,2},{4,5},{5,4},{6,7},{7,6},{8,9},{9,8},{10,11... | collective-permute-start | bytes 786440 | tf_op jit(solution)/shard_map/ppermute | solution.py:499
  62.8 0.8 %collective-permute-done.18.refs_3_ = bf16[64,512]{1,0:T(8,128)(2,1)S(1)} collective-permute-done((bf16[64,512]{1,0:T(8,128)(2,1)S(1)}, bf16[64,512]{1,0:T(8,128)(2,1)S(1)}, u32[]{:S(2)}, u32[]{:S(2)}) %collective-permute-start.18) | collective-permute-done | bytes 65568 | tf_op jit(solution)/shard_map/ppermute | solution.py:389
  63.6 0.7 collective-permute-done.17.refs_2_
  64.2 1.5 %collective-permute-done.16.refs_1_ = bf16[64,512]{1,0:T(8,128)(2,1)S(1)} collective-permute-done((bf16[64,512]{1,0:T(8,128)(2,1)S(1)}, bf16[64,512]{1,0:T(8,128)(2,1)S(1)}, u32[]{:S(2)}, u32[]{:S(2)}) %collective-permute-start.16) | collective-permute-done | bytes 65568 | tf_op jit(solution)/shard_map/ppermute | solution.py:389
  65.8 0.2 shard_map.93
  66.0 0.7 collective-permute-start.20
  66.8 4.6 %collective-permute-done.21.refs_2_ = bf16[2,256,256]{2,1,0:T(8,128)(2,1)S(1)} collective-permute-done((bf16[2,256,256]{2,1,0:T(8,128)(2,1)S(1)}, bf16[2,256,256]{2,1,0:T(8,128)(2,1)S(1)}, u32[]{:S(2)}, u32[]{:S(2)}) %collective-permute-start.21) | collective-permute-done | bytes 262176 | tf_op jit(solution)/shard_map/ppermute | solution.py:499
  71.4 0.8 %shard_map.94.refs_3_ = bf16[1,2,2,256,256]{4,3,2,1,0:T(8,128)(2,1)} custom-call(bf16[2,256,256]{2,1,0:T(8,128)(2,1)S(1)} %get-tuple-element.26.refs_3_.refs_0_, bf16[2,256,256]{2,1,0:T(8,128)(2,1)S(1)} %get-tuple-element.48.refs_1_, bf16[2,256,256]{2,1,0:T(8,128)(2,1)S(1)} %collective-permute-done.21.refs_2_), custom_call_target="tpu_custom_call" | custom-call | flops 131072 | bytes 1048576 | tf_op jit(solution)/shard_map/pallas_call | solution.py:285
  72.2 1.2 %shard_map.95.refs_4_ = f32[2048,128]{1,0:T(8,128)} custom-call(bf16[256,512]{1,0:T(8,128)(2,1)S(1)} %get-tuple-element.49.refs_0_, bf16[256,512]{1,0:T(8,128)(2,1)S(1)} %collective-permute-done.22.refs_1_, f32[2048,128]{1,0:T(8,128)S(1)} %bitcast.18), custom_call_target="tpu_custom_call" | custom-call | flops 1000000 | bytes 2621440 | tf_op jit(solution)/shard_map/pallas_call | solution.py:268
  73.4 2.5 %collective-permute-done.20.refs_2_ = bf16[2,256,256]{2,1,0:T(8,128)(2,1)S(1)} collective-permute-done((bf16[2,256,256]{2,1,0:T(8,128)(2,1)S(1)}, bf16[2,256,256]{2,1,0:T(8,128)(2,1)S(1)}, u32[]{:S(2)}, u32[]{:S(2)}) %collective-permute-start.20) | collective-permute-done | bytes 262176 | tf_op jit(solution)/shard_map/ppermute | solution.py:499
  75.9 1.2 %copy-done.1 = f32[2048,128]{1,0:T(8,128)S(1)} copy-done((f32[2048,128]{1,0:T(8,128)S(1)}, f32[2048,128]{1,0:T(8,128)}, u32[]{:S(2)}) %copy-start.1) | copy-done | bytes 1048600
  77.1 0.8 %shard_map.96 = bf16[1,2,2,256,256]{4,3,2,1,0:T(8,128)(2,1)} custom-call(bf16[2,256,256]{2,1,0:T(8,128)(2,1)S(1)} %slice_bitcast_fusion.refs_3_.refs_0_, bf16[2,256,256]{2,1,0:T(8,128)(2,1)S(1)} %get-tuple-element.47.refs_1_, bf16[2,256,256]{2,1,0:T(8,128)(2,1)S(1)} %collective-permute-done.20.refs_2_, ...), custom_call_target="tpu_custom_call", output_to_operand_aliasing={{}: (3, {})} | custom-call | flops 131072 | bytes 1048576 | tf_op jit(solution)/shard_map/pallas_call | solution.py:285
  (30 shorter events, 0.4 us)
Async XLA Ops:
  0.6 10.5 %copy-start = (f32[2,256,2,256]{3,2,1,0:T(2,128)S(1)}, f32[2,256,2,256]{3,2,1,0:T(2,128)}, u32[]{:S(2)}) copy-start(f32[2,256,2,256]{3,2,1,0:T(2,128)} %param.8) | copy-start | bytes 3145732
  1.7 12.1 %collective-permute-start.4 = (bf16[2,256,256]{2,1,0:T(8,128)(2,1)S(1)}, bf16[2,256,256]{2,1,0:T(8,128)(2,1)S(1)}, u32[]{:S(2)}, u32[]{:S(2)}) collective-permute-start(bf16[2,256,256]{2,1,0:T(8,128)(2,1)S(1)} %slice_bitcast_fusion.refs_3_.refs_0_), channel_id=1, source_target_pairs={{8,0},{10,2},{12,4},{14,6},{16,8},{18,10},{20,12},{22,14},{24,16},... | collective-permute-start | bytes 786440 | tf_op jit(solution)/shard_map/ppermute | solution.py:29
  6.8 16.1 %collective-permute-start.1 = (bf16[2,2,256,256]{3,2,1,0:T(8,128)(2,1)}, bf16[2,2,256,256]{3,2,1,0:T(8,128)(2,1)S(1)}, u32[]{:S(2)}, u32[]{:S(2)}) collective-permute-start(bf16[2,2,256,256]{3,2,1,0:T(8,128)(2,1)} %bitcast.20), channel_id=1, source_target_pairs={{2,0},{4,2},{6,4},{0,6},{10,8},{12,10},{14,12},{8,14},{18,16},{20,... | collective-permute-start | bytes 1572872 | tf_op jit(solution)/shard_map/ppermute | solution.py:29
  11.1 1.0 %copy-start.2 = (bf16[1,2,2,256,256]{4,3,2,1,0:T(8,128)(2,1)S(1)}, bf16[1,2,2,256,256]{4,3,2,1,0:T(8,128)(2,1)}, u32[]{:S(2)}) copy-start(bf16[1,2,2,256,256]{4,3,2,1,0:T(8,128)(2,1)} %refs_0_.3) | copy-start | bytes 1572868
  12.2 1.0 %copy-start.3 = (bf16[512,512]{1,0:T(8,128)(2,1)S(1)}, bf16[512,512]{1,0:T(8,128)(2,1)}, u32[]{:S(2)}) copy-start(bf16[512,512]{1,0:T(8,128)(2,1)} %constant.15.refs_2_) | copy-start | bytes 1572868
  13.3 8.1 %collective-permute-start.2 = (bf16[2,256,256]{2,1,0:T(8,128)(2,1)S(1)}, bf16[2,256,256]{2,1,0:T(8,128)(2,1)S(1)}, u32[]{:S(2)}, u32[]{:S(2)}) collective-permute-start(bf16[2,256,256]{2,1,0:T(8,128)(2,1)S(1)} %get-tuple-element.26.refs_3_.refs_0_), channel_id=1, source_target_pairs={{8,0},{10,2},{12,4},{14,6},{16,8},{18,10},{20,12},{22,14},{24,16},... | collective-permute-start | bytes 786440 | tf_op jit(solution)/shard_map/ppermute | solution.py:29
  13.8 9.1 %collective-permute-start.5 = (bf16[2,256,256]{2,1,0:T(8,128)(2,1)S(1)}, bf16[2,256,256]{2,1,0:T(8,128)(2,1)S(1)}, u32[]{:S(2)}, u32[]{:S(2)}) collective-permute-start(bf16[2,256,256]{2,1,0:T(8,128)(2,1)S(1)} %collective-permute-done.4.refs_5_), channel_id=1, source_target_pairs={{2,0},{4,2},{6,4},{0,6},{10,8},{12,10},{14,12},{8,14},{18,16},{20,... | collective-permute-start | bytes 786440 | tf_op jit(solution)/shard_map/ppermute | solution.py:29
  14.5 8.4 %collective-permute-start = (bf16[272,256]{1,0:T(8,128)(2,1)S(1)}, bf16[272,256]{1,0:T(8,128)(2,1)S(1)}, u32[]{:S(2)}, u32[]{:S(2)}) collective-permute-start(bf16[272,256]{1,0:T(8,128)(2,1)S(1)} %pad_maximum_fusion.refs_4_), channel_id=1, source_target_pairs={{0,1},{1,0},{2,3},{3,2},{4,5},{5,4},{6,7},{7,6},{8,9},{9,8},{10,11... | collective-permute-start | bytes 417800 | tf_op jit(solution)/shard_map/ppermute | solution.py:314
  21.4 4.7 %collective-permute-start.3 = (bf16[2,256,256]{2,1,0:T(8,128)(2,1)S(1)}, bf16[2,256,256]{2,1,0:T(8,128)(2,1)S(1)}, u32[]{:S(2)}, u32[]{:S(2)}) collective-permute-start(bf16[2,256,256]{2,1,0:T(8,128)(2,1)S(1)} %collective-permute-done.2.refs_5_), channel_id=1, source_target_pairs={{2,0},{4,2},{6,4},{0,6},{10,8},{12,10},{14,12},{8,14},{18,16},{20,... | collective-permute-start | bytes 786440 | tf_op jit(solution)/shard_map/ppermute | solution.py:29
  23.0 0.7 copy-start.5
  23.6 2.5 %copy-start.4 = (bf16[1,1,2,256,256]{4,3,2,1,0:T(8,128)(2,1)S(1)}, bf16[1,1,2,256,256]{4,3,2,1,0:T(8,128)(2,1)}, u32[]{:S(2)}) copy-start(bf16[1,1,2,256,256]{4,3,2,1,0:T(8,128)(2,1)} %refs_10_.1) | copy-start | bytes 786436
  23.6 2.5 %copy-start.6 = (bf16[512,512]{1,0:T(8,128)(2,1)S(1)}, bf16[512,512]{1,0:T(8,128)(2,1)}, u32[]{:S(2)}) copy-start(bf16[512,512]{1,0:T(8,128)(2,1)} %constant.16.refs_12_) | copy-start | bytes 1572868
  31.2 2.2 %collective-permute-start.7 = (bf16[256,512]{1,0:T(8,128)(2,1)S(1)}, bf16[256,512]{1,0:T(8,128)(2,1)S(1)}, u32[]{:S(2)}, u32[]{:S(2)}) collective-permute-start(bf16[256,512]{1,0:T(8,128)(2,1)S(1)} %get-tuple-element.34), channel_id=1, source_target_pairs={{0,2},{1,3},{2,0},{3,1},{4,6},{5,7},{6,4},{7,5},{8,10},{9,11},{10,... | collective-permute-start | bytes 786440 | tf_op jit(solution)/shard_map/ppermute | solution.py:389
  32.2 11.1 %collective-permute-start.6 = (bf16[528,256]{1,0:T(8,128)(2,1)S(1)}, bf16[528,256]{1,0:T(8,128)(2,1)S(1)}, u32[]{:S(2)}, u32[]{:S(2)}) collective-permute-start(bf16[528,256]{1,0:T(8,128)(2,1)S(1)} %get-tuple-element.32), channel_id=1, source_target_pairs={{24,0},{26,2},{28,4},{30,6},{0,8},{2,10},{4,12},{6,14},{8,16},{10,... | collective-permute-start | bytes 811016 | tf_op jit(solution)/shard_map/ppermute | solution.py:29
  34.7 13.6 %collective-permute-start.15 = (bf16[528,256]{1,0:T(8,128)(2,1)S(1)}, bf16[528,256]{1,0:T(8,128)(2,1)S(1)}, u32[]{:S(2)}, u32[]{:S(2)}) collective-permute-start(bf16[528,256]{1,0:T(8,128)(2,1)S(1)} %get-tuple-element.44), channel_id=1, source_target_pairs={{24,0},{26,2},{28,4},{30,6},{0,8},{2,10},{4,12},{6,14},{8,16},{10,... | collective-permute-start | bytes 811016 | tf_op jit(solution)/shard_map/ppermute | solution.py:29
  34.7 8.6 %collective-permute-start.8 = (bf16[64,512]{1,0:T(8,128)(2,1)S(1)}, bf16[64,512]{1,0:T(8,128)(2,1)S(1)}, u32[]{:S(2)}, u32[]{:S(2)}) collective-permute-start(bf16[64,512]{1,0:T(8,128)(2,1)S(1)} %get-tuple-element.37), channel_id=1, source_target_pairs={{0,1},{1,0},{2,3},{3,2},{4,5},{5,4},{6,7},{7,6},{8,9},{9,8},{10,11... | collective-permute-start | bytes 196616 | tf_op jit(solution)/shard_map/ppermute | solution.py:389
  36.3 7.0 %collective-permute-start.9 = (bf16[64,512]{1,0:T(8,128)(2,1)S(1)}, bf16[64,512]{1,0:T(8,128)(2,1)S(1)}, u32[]{:S(2)}, u32[]{:S(2)}) collective-permute-start(bf16[64,512]{1,0:T(8,128)(2,1)S(1)} %get-tuple-element.38), channel_id=1, source_target_pairs={{0,4},{1,5},{2,6},{3,7},{4,0},{5,1},{6,2},{7,3},{8,12},{9,13},{10,... | collective-permute-start | bytes 196616 | tf_op jit(solution)/shard_map/ppermute | solution.py:389
  37.7 5.6 %collective-permute-start.10 = (bf16[64,512]{1,0:T(8,128)(2,1)S(1)}, bf16[64,512]{1,0:T(8,128)(2,1)S(1)}, u32[]{:S(2)}, u32[]{:S(2)}) collective-permute-start(bf16[64,512]{1,0:T(8,128)(2,1)S(1)} %get-tuple-element.39), channel_id=1, source_target_pairs={{0,5},{1,4},{2,7},{3,6},{4,1},{5,0},{6,3},{7,2},{8,13},{9,12},{10,... | collective-permute-start | bytes 196616 | tf_op jit(solution)/shard_map/ppermute | solution.py:389
  43.5 14.0 %collective-permute-start.14 = (bf16[2,256,256]{2,1,0:T(8,128)(2,1)S(1)}, bf16[2,256,256]{2,1,0:T(8,128)(2,1)S(1)}, u32[]{:S(2)}, u32[]{:S(2)}) collective-permute-start(bf16[2,256,256]{2,1,0:T(8,128)(2,1)S(1)} %get-tuple-element.42), channel_id=1, source_target_pairs={{6,0},{0,2},{2,4},{4,6},{14,8},{8,10},{10,12},{12,14},{22,16},{16,... | collective-permute-start | bytes 786440 | tf_op jit(solution)/shard_map/ppermute | solution.py:29
  48.3 17.4 %collective-permute-start.19 = (bf16[2,256,256]{2,1,0:T(8,128)(2,1)S(1)}, bf16[2,256,256]{2,1,0:T(8,128)(2,1)S(1)}, u32[]{:S(2)}, u32[]{:S(2)}) collective-permute-start(bf16[2,256,256]{2,1,0:T(8,128)(2,1)S(1)} %shard_map.91.refs_7_), channel_id=1, source_target_pairs={{6,0},{0,2},{2,4},{4,6},{14,8},{8,10},{10,12},{12,14},{22,16},{16,... | collective-permute-start | bytes 786440 | tf_op jit(solution)/shard_map/ppermute | solution.py:29
  48.4 6.7 %collective-permute-start.13 = (bf16[64,512]{1,0:T(8,128)(2,1)S(1)}, bf16[64,512]{1,0:T(8,128)(2,1)S(1)}, u32[]{:S(2)}, u32[]{:S(2)}) collective-permute-start(bf16[64,512]{1,0:T(8,128)(2,1)S(1)} %get-tuple-element.40.refs_2_.refs_0_), channel_id=1, source_target_pairs={{0,24},{1,25},{2,26},{3,27},{4,28},{5,29},{6,30},{7,31},{8,16},{9,... | collective-permute-start | bytes 196616 | tf_op jit(solution)/shard_map/ppermute | solution.py:389
  48.9 8.5 %collective-permute-start.12 = (bf16[64,512]{1,0:T(8,128)(2,1)S(1)}, bf16[64,512]{1,0:T(8,128)(2,1)S(1)}, u32[]{:S(2)}, u32[]{:S(2)}) collective-permute-start(bf16[64,512]{1,0:T(8,128)(2,1)S(1)} %get-tuple-element.40.refs_2_.refs_0_), channel_id=1, source_target_pairs={{0,16},{1,17},{2,18},{3,19},{4,20},{5,21},{6,22},{7,23},{8,24},{9,... | collective-permute-start | bytes 196616 | tf_op jit(solution)/shard_map/ppermute | solution.py:389
  48.9 8.5 %collective-permute-start.11 = (bf16[64,512]{1,0:T(8,128)(2,1)S(1)}, bf16[64,512]{1,0:T(8,128)(2,1)S(1)}, u32[]{:S(2)}, u32[]{:S(2)}) collective-permute-start(bf16[64,512]{1,0:T(8,128)(2,1)S(1)} %get-tuple-element.40.refs_2_.refs_0_), channel_id=1, source_target_pairs={{0,8},{1,9},{2,10},{3,11},{4,12},{5,13},{6,14},{7,15},{8,0},{9,1},... | collective-permute-start | bytes 196616 | tf_op jit(solution)/shard_map/ppermute | solution.py:389
  57.7 5.9 %collective-permute-start.18 = (bf16[64,512]{1,0:T(8,128)(2,1)S(1)}, bf16[64,512]{1,0:T(8,128)(2,1)S(1)}, u32[]{:S(2)}, u32[]{:S(2)}) collective-permute-start(bf16[64,512]{1,0:T(8,128)(2,1)S(1)} %get-tuple-element.45.refs_0_), channel_id=1, source_target_pairs={{0,5},{1,4},{2,7},{3,6},{4,1},{5,0},{6,3},{7,2},{8,13},{9,12},{10,... | collective-permute-start | bytes 196616 | tf_op jit(solution)/shard_map/ppermute | solution.py:389
  59.7 4.5 %collective-permute-start.17 = (bf16[64,512]{1,0:T(8,128)(2,1)S(1)}, bf16[64,512]{1,0:T(8,128)(2,1)S(1)}, u32[]{:S(2)}, u32[]{:S(2)}) collective-permute-start(bf16[64,512]{1,0:T(8,128)(2,1)S(1)} %get-tuple-element.45.refs_0_), channel_id=1, source_target_pairs={{0,4},{1,5},{2,6},{3,7},{4,0},{5,1},{6,2},{7,3},{8,12},{9,13},{10,... | collective-permute-start | bytes 196616 | tf_op jit(solution)/shard_map/ppermute | solution.py:389
  60.7 5.0 %collective-permute-start.16 = (bf16[64,512]{1,0:T(8,128)(2,1)S(1)}, bf16[64,512]{1,0:T(8,128)(2,1)S(1)}, u32[]{:S(2)}, u32[]{:S(2)}) collective-permute-start(bf16[64,512]{1,0:T(8,128)(2,1)S(1)} %get-tuple-element.45.refs_0_), channel_id=1, source_target_pairs={{0,1},{1,0},{2,3},{3,2},{4,5},{5,4},{6,7},{7,6},{8,9},{9,8},{10,11... | collective-permute-start | bytes 196616 | tf_op jit(solution)/shard_map/ppermute | solution.py:389
  61.2 10.1 %collective-permute-start.21 = (bf16[2,256,256]{2,1,0:T(8,128)(2,1)S(1)}, bf16[2,256,256]{2,1,0:T(8,128)(2,1)S(1)}, u32[]{:S(2)}, u32[]{:S(2)}) collective-permute-start(bf16[2,256,256]{2,1,0:T(8,128)(2,1)S(1)} %get-tuple-element.48.refs_1_), channel_id=1, source_target_pairs={{0,1},{1,0},{2,3},{3,2},{4,5},{5,4},{6,7},{7,6},{8,9},{9,8},{10,11... | collective-permute-start | bytes 786440 | tf_op jit(solution)/shard_map/ppermute | solution.py:499
  66.0 6.2 %collective-permute-start.22 = (bf16[256,512]{1,0:T(8,128)(2,1)S(1)}, bf16[256,512]{1,0:T(8,128)(2,1)S(1)}, u32[]{:S(2)}, u32[]{:S(2)}) collective-permute-start(bf16[256,512]{1,0:T(8,128)(2,1)S(1)} %get-tuple-element.49.refs_0_), channel_id=1, source_target_pairs={{0,2},{1,3},{2,0},{3,1},{4,6},{5,7},{6,4},{7,5},{8,10},{9,11},{10,... | collective-permute-start | bytes 786440 | tf_op jit(solution)/shard_map/ppermute | solution.py:389
  66.0 9.8 %collective-permute-start.20 = (bf16[2,256,256]{2,1,0:T(8,128)(2,1)S(1)}, bf16[2,256,256]{2,1,0:T(8,128)(2,1)S(1)}, u32[]{:S(2)}, u32[]{:S(2)}) collective-permute-start(bf16[2,256,256]{2,1,0:T(8,128)(2,1)S(1)} %get-tuple-element.47.refs_1_), channel_id=1, source_target_pairs={{0,1},{1,0},{2,3},{3,2},{4,5},{5,4},{6,7},{7,6},{8,9},{9,8},{10,11... | collective-permute-start | bytes 786440 | tf_op jit(solution)/shard_map/ppermute | solution.py:499
  75.9 1.2 %copy-start.1 = (f32[2048,128]{1,0:T(8,128)S(1)}, f32[2048,128]{1,0:T(8,128)}, u32[]{:S(2)}) copy-start(f32[2048,128]{1,0:T(8,128)} %shard_map.95.refs_4_) | copy-start | bytes 3145732

commit v5 on v4

--- a/solution.py
+++ b/solution.py
@@ -57,12 +57,13 @@
     return jnp.dot(a, b, preferred_element_type=f32)
 
 
-def shift_tables(offsets_ref, counts_ref, message_ref):
-    n = message_ref.shape[1]
-    sent = message_ref[n:, :].astype(f32)
-    busy = counts_ref[0, 0] == offsets_ref.shape[2]
-    row = jnp.where(busy, offsets_ref[0, 0, 0, 0], sent[0:1].astype(jnp.int32))
-    col = jnp.where(busy, offsets_ref[0, 0, 0, 1], sent[1:2].astype(jnp.int32))
+def shift_tables(mine_ref, sent_ref):
+    n = mine_ref.shape[1]
+    mine = mine_ref[n:, :].astype(f32)
+    sent = sent_ref[n:, :].astype(f32)
+    busy = mine[2:3] > 0
+    row = jnp.where(busy, mine[0:1], sent[0:1]).astype(jnp.int32)
+    col = jnp.where(busy, mine[1:2], sent[1:2]).astype(jnp.int32)
     i_out = lax.broadcasted_iota(jnp.int32, (n, 2 * n), 0)
     i_in = lax.broadcasted_iota(jnp.int32, (n, 2 * n), 1)
     j_in = lax.broadcasted_iota(jnp.int32, (2 * n, n), 0)
@@ -104,10 +105,20 @@
     return jnp.concatenate(halves, axis=1)
 
 
-def ready_kernel(tile_ref, probe_ref, prop_ref, own_ref, planes_ref, table_ref):
-    own_ref[...] = tile_ref[0, 1]
+def ready_kernel(
+    offsets_ref, counts_ref, own_ref, patterns_ref, probe_ref, prop_ref,
+    own_out, mine_ref, sent_ref, planes_ref, table_ref,
+):
+    own_out[...] = own_ref[...]
     table_ref[...] = prop_ref[...]
     n = planes_ref.shape[1]
+    at = lax.broadcasted_iota(jnp.int32, (16, n), 0)
+    busy = (counts_ref[0, 0] == patterns_ref.shape[2]).astype(jnp.int32)
+    for slot, ref in enumerate((mine_ref, sent_ref)):
+        row, col = offsets_ref[0, 0, slot, 0], offsets_ref[0, 0, slot, 1]
+        rows = jnp.where(at == 0, row, jnp.where(at == 1, col, busy))
+        ref[pl.ds(0, n), :] = patterns_ref[0, 0, slot]
+        ref[pl.ds(n, 16), :] = rows.astype(f32).astype(bf16)
     modes = planes_ref.shape[2] // n
     for part in range(2):
         for mode in range(modes):
@@ -115,11 +126,11 @@
 
 
 def arrive_kernel(
-    offsets_ref, counts_ref, message_ref, own_ref, right_ref, below_ref, diag_ref, planes_ref,
-    prop_ref, near_ref, arrive_ref,
+    mine_ref, sent_ref, own_ref, right_ref, below_ref, diag_ref, planes_ref, prop_ref,
+    near_ref, arrive_ref,
 ):
     n = own_ref.shape[1]
-    shifts = shift_tables(offsets_ref, counts_ref, message_ref)
+    shifts = shift_tables(mine_ref, sent_ref)
     tiles = (own_ref, right_ref.at[0], below_ref, diag_ref)
     near = [patch(shifts, *tiles, part) for part in range(2)]
     for part in range(2):
@@ -149,13 +160,13 @@
 
 
 def gradient_kernel(
-    offsets_ref, counts_ref, message_ref, own_ref, right_ref, below_ref, diag_ref, near_ref,
-    arrive_ref, planes_ref, patterns_ref, prop_ref, dft_ref,
+    mine_ref, sent_ref, own_ref, right_ref, below_ref, diag_ref, near_ref, arrive_ref,
+    planes_ref, prop_ref, dft_ref,
     home_ref, next_ref, down_ref, grad_ref, keep_ref, give_ref, term_ref,
 ):
     n = own_ref.shape[1]
     modes = planes_ref.shape[2] // n
-    shifts = shift_tables(offsets_ref, counts_ref, message_ref)
+    shifts = shift_tables(mine_ref, sent_ref)
     busy = shifts[5]
     tiles = (own_ref, right_ref.at[1], below_ref, diag_ref)
     far = [patch(shifts, *tiles, part) for part in range(2)]
@@ -167,7 +178,7 @@
             transform(dft_ref, far[0] * a_re - far[1] * a_im, far[0] * a_im + far[1] * a_re)
         )
     intensity = sum(f_re * f_re + f_neg * f_neg for f_re, f_neg in fields)
-    pattern = jnp.where(busy, patterns_ref[0, 0, 0].astype(f32), message_ref[:n, :].astype(f32))
+    pattern = jnp.where(busy, mine_ref[:n, :].astype(f32), sent_ref[:n, :].astype(f32))
     residual = intensity - pattern
     grad_far = [0.0, 0.0]
     waves = []
@@ -197,8 +208,8 @@
     spread(shifts, grad_far, home_ref, next_ref, down_ref)
 
 
-def spread_kernel(offsets_ref, counts_ref, message_ref, grad_ref, home_ref, next_ref, down_ref):
-    shifts = shift_tables(offsets_ref, counts_ref, message_ref)
+def spread_kernel(mine_ref, sent_ref, grad_ref, home_ref, next_ref, down_ref):
+    shifts = shift_tables(mine_ref, sent_ref)
     spread(shifts, [grad_ref[part] for part in range(2)], home_ref, next_ref, down_ref)
 
 
@@ -300,18 +311,8 @@
     return jax.ShapeDtypeStruct(dims, kind)
 
 
-def handed_over(patterns, offsets, counts):
-    owners = lax.axis_size("pos")
-    slots, pixels = patterns.shape[2], patterns.shape[4]
-
-    def message(pattern, spot):
-        at = lax.broadcasted_iota(jnp.int32, (16, pixels), 0)
-        rows = jnp.where(at == 0, spot[0], jnp.where(at == 1, spot[1], 0))
-        return jnp.concatenate([pattern, rows.astype(bf16)], axis=0)
-
-    if owners == slots:
-        sent = message(patterns[0, 0, 1], offsets[0, 0, 1])
-        return sent, lax.ppermute(sent, "pos", [(i, 1 - i) for i in range(2)]), counts
+def gathered_message(patterns, offsets, counts):
+    pixels = patterns.shape[4]
     all_counts = lax.all_gather(counts[0, 0], "pos")
     ends = jnp.cumsum(all_counts)
     rank = lax.axis_index("pos")
@@ -319,8 +320,9 @@
     slot = rank - (ends[source] - all_counts[source])
     spot = lax.all_gather(offsets[0, 0], "pos")[source, slot]
     pattern = lax.all_gather(patterns[0, 0], "pos")[source, slot]
-    sent = message(pattern, spot)
-    return sent, sent, jnp.zeros_like(counts)
+    at = lax.broadcasted_iota(jnp.int32, (16, pixels), 0)
+    rows = jnp.where(at == 0, spot[0], jnp.where(at == 1, spot[1], 0))
+    return jnp.concatenate([pattern, rows.astype(bf16)], axis=0)
 
 
 def fold_kernel(group, keep_ref, *refs):
@@ -362,8 +364,9 @@
             out_ref[pl.ds(block * size, size), :] = blocks[block]
 
 
-def probe_kernel(step, modes, mine_ref, other_ref, probe_ref, out_ref):
+def probe_kernel(step, modes, mine_ref, other_ref, probe_ref, out_ref, token_ref):
     core = place_of(core_group())
+    token_ref[...] = jnp.zeros_like(token_ref)
     lane_tiles = 2
     n = mine_ref.shape[0]
     stride = lane_tiles * modes
@@ -389,15 +392,18 @@
     return lax.ppermute(x, ("tile", "pos"), [(i, i ^ mask) for i in range(devices)])
 
 
-def joined(group, x, add):
+def joined(group, x, arrived, add):
     blocks = 1 << len(group)
-    arrived = [x] + [swap_with(x, group, at) for at in range(1, blocks)]
     return job(
         lambda *refs: place_kernel(group, add, *refs),
         [shape_of(bf16, x.shape[0] * (1 if add else blocks), x.shape[1])],
-        arrived,
+        [x] + arrived,
         scratch=[pltpu.VMEM((blocks,) + x.shape, bf16)],
     )
+
+
+def swapped(x, group):
+    return [swap_with(x, group, at) for at in range(1, 1 << len(group))]
 
 
 def folded(group, keep, arrived):
@@ -421,24 +427,33 @@
     probe = probe_modes.reshape(2, pixels, modes, lane_tiles, 128)
     probe = probe.transpose(0, 1, 3, 2, 4).reshape(-1, 128)
 
-    own0 = tile_object[0, 0]
-    below0 = from_behind(own0, -1, 0)
+    own = [tile_object[0, 0], tile_object[0, 1]]
+    below0 = from_behind(own[0], -1, 0)
     right = from_behind(tile_object[0], 0, -1)
-    sent, message, counts = handed_over(patterns, offsets, counts)
-    own1, probe_planes, table = run(
-        job(ready_kernel, [tile, planes, shape_of(bf16, *prop.shape)], [tile_object, probe, prop]),
+    exchanged = lax.axis_size("pos") == patterns.shape[2]
+    message = shape_of(bf16, pixels + 16, pixels)
+    own1, mine, sent, probe_planes, table = run(
+        job(
+            ready_kernel,
+            [tile, message, message, planes, shape_of(bf16, *prop.shape)],
+            [own[1], patterns, probe, prop],
+            scalars=[offsets, counts if exchanged else jnp.zeros_like(counts)],
+        ),
         limit=16,
-        after=[own0, sent],
+        after=[own[0]],
     )
     below1 = from_behind(own1, -1, 0)
+    if exchanged:
+        sent = lax.ppermute(sent, "pos", [(i, 1 - i) for i in range(2)])
+    else:
+        sent = gathered_message(patterns, offsets, counts)
     diag0 = from_behind(below0, 0, -1)
     diag1 = from_behind(below1, 0, -1)
     near, arrive = run(
         job(
             arrive_kernel,
             [tile, planes],
-            [message, own0, right, below0, diag0, probe_planes, table],
-            scalars=[offsets, counts],
+            [mine, sent, own[0], right, below0, diag0, probe_planes, table],
         ),
         flops=1_500_000_000,
         limit=16,
@@ -449,25 +464,22 @@
         job(
             gradient_kernel,
             [tile, tile, down, tile, half, half],
-            [message, own1, right, below1, diag1, near, arrive, probe_planes, patterns, table, dft],
-            scalars=[offsets, counts],
+            [mine, sent, own1, right, below1, diag1, near, arrive, probe_planes, table, dft],
             scratch=[pltpu.VMEM((2, pixels, width), bf16)],
         ),
         flops=4_000_000_000,
         limit=16,
     )
 
+    def over_owners(part):
+        if lax.axis_size("pos") == 2:
+            return lax.ppermute(part, "pos", [(0, 1), (1, 0)])
+        return lax.psum(part.astype(f32), "pos") - part.astype(f32)
+
     core, groups = core_group(), exchange_groups()
     above1 = from_behind(down1, 1, 0)
     arrived = [swap_with(give, core, 1)]
-    side = [
-        job(
-            spread_kernel,
-            [tile, tile, down],
-            [message, grad0],
-            scalars=[offsets, counts],
-        )
-    ]
+    side = [job(spread_kernel, [tile, tile, down], [mine, sent, grad0])]
     scattered = []
     while len(groups) > 1 and keep.shape[0] >> len(groups[0]) >= 16:
         group, groups = groups[0], groups[1:]
@@ -484,43 +496,34 @@
         job(add_kernel, [shape_of(bf16, *keep.shape)], [keep] + arrived),
     )
     from_left1 = from_behind(beside1, 0, 1)
-    (beside0,) = run(job(beside_kernel, [tile], [next0, above0]), after=[total])
+    arrived = swapped(total, groups[0])
+    (beside0,) = run(job(beside_kernel, [tile], [next0, above0]), after=arrived[:1])
     from_left0 = from_behind(beside0, 0, 1)
-    (total,), (part1,) = run(
-        joined(groups[0], total, True),
-        job(part_kernel, [tile], [home1, above1, from_left1]),
-        after=[beside0],
-    )
+    (part1,) = run(job(part_kernel, [tile], [home1, above1, from_left1]), after=[beside0])
+    other1 = over_owners(part1)
+    (total,) = run(joined(groups[0], total, arrived, True), after=[part1])
     for group in groups[1:]:
-        (total,) = run(joined(group, total, True))
-
-    def from_owners(part):
-        if lax.axis_size("pos") == 2:
-            return lax.ppermute(part, "pos", [(0, 1), (1, 0)])
-        return lax.psum(part.astype(f32), "pos") - part.astype(f32)
-
-    other1 = from_owners(part1)
-    (total,), (part0,) = run(
-        joined(scattered[-1], total, False),
-        job(part_kernel, [tile], [home0, above0, from_left0]),
-    )
-    other0 = from_owners(part0)
+        (total,) = run(joined(group, total, swapped(total, group), True))
+    arrived = swapped(total, scattered[-1])
+    (part0,) = run(job(part_kernel, [tile], [home0, above0, from_left0]), after=arrived[1:2])
+    other0 = over_owners(part0)
+    (total,) = run(joined(scattered[-1], total, arrived, False), after=[part0])
     for group in reversed(scattered[:-1]):
-        (total,) = run(joined(group, total, False))
+        (total,) = run(joined(group, total, swapped(total, group), False))
     other_half = swap_with(total, core, 1)
     positions_all = lax.axis_size("tile") * lax.axis_size("pos") * (patterns.shape[2] // 2)
     step = probe_rate / math.sqrt(positions_all)
-    like = shape_of(bf16, *tile_object.shape)
-    new_object = updated(1, own1, part1, other1, like, None, [])
-    (new_probe,) = run(
+    new_probe, token = run(
         job(
             lambda *refs: probe_kernel(step, modes, *refs),
-            [shape_of(f32, *probe.shape)],
+            [shape_of(f32, *probe.shape), shape_of(f32, 8, 128)],
             [total, other_half, probe],
         ),
         limit=8,
     )
-    new_object = updated(0, own0, part0, other0, like, new_object, [new_probe])
+    like = shape_of(bf16, *tile_object.shape)
+    new_object = updated(1, own1, part1, other1, like, None, [])
+    new_object = updated(0, own[0], part0, other0, like, new_object, [token])
     new_probe = new_probe.reshape(2, pixels, lane_tiles, modes, 128).transpose(0, 1, 3, 2, 4)
     return (new_object, new_probe.reshape(probe_modes.shape))
 

time: 78.3 us -> 76.8 us (0.981)
  waiting for transfers between devices: 31.2 us -> 37.6 us
  local copies, waits for them, and re-layouts: 7.3 us -> 3.82 us
  starting transfers between devices: 24.4 us -> 22.9 us
  Pallas kernels: 12.2 us -> 10.8 us
  other arithmetic: 1.38 us -> 0 us
    ppermute x11, waiting for transfers between devices: 8.76 us -> 16.3 us  [swap_with(): lax.ppermute(x, ('tile', 'pos'), [(i, i ^ mask) for i in range(devices)])]
    ppermute x9, waiting for transfers between devices: 15.4 us -> 13.8 us  [from_behind(): return lax.ppermute(block, 'tile', [(source(i), i) for i in range(tiles)])]
    pallas_call x9 -> x11, Pallas kernels: 10.6 us -> 9.16 us  [run(): pl.pallas_call(body, out_shape=sum(outs, []), in_specs=sum(specs, []) + [...]
    slice x1 -> x0, local copies, waits for them, and re-layouts: 1.34 us -> none  [message(): rows = jnp.where(at == 0, spot[0], jnp.where(at == 1, spot[1], 0))]
    unnamed x14 -> x10, local copies, waits for them, and re-layouts: 3.99 us -> 2.67 us
    ppermute x11, starting transfers between devices: 12.7 us -> 11.5 us  [swap_with(): lax.ppermute(x, ('tile', 'pos'), [(i, i ^ mask) for i in range(devices)])]
    squeeze x2 -> x1, local copies, waits for them, and re-layouts: 1.97 us -> 1.15 us  [shards(): own = [tile_object[0, 0], tile_object[0, 1]]]
  transfers between devices with their start and end apart: 23 -> 23, of which waited for: 12 -> 12; matrix products, arithmetic and copies ran while one was open for 5% -> 0% of each run, Pallas kernels for 8% -> 8%
where the time goes in v5:
time: 76.8 us; the launch traced here: 76.6 us
  waiting for transfers between devices  37.6 us (49%)
  starting transfers between devices  22.9 us (30%)
  Pallas kernels  10.8 us (14%)
  local copies, waits for them, and re-layouts  3.82 us (5%)
  between operations  1.44 us (2%)
    ppermute x11, waiting for transfers between devices, swap_with(): lax.ppermute(x, ('tile', 'pos'), [(i, i ^ mask) for i in range(devices)])  16.3 us
    ppermute x9, waiting for transfers between devices, from_behind(): return lax.ppermute(block, 'tile', [(source(i), i) for i in range(tiles)])  13.8 us
    ppermute x11, starting transfers between devices, swap_with(): lax.ppermute(x, ('tile', 'pos'), [(i, i ^ mask) for i in range(devices)])  11.5 us
    pallas_call x11, Pallas kernels, run(): pl.pallas_call(body, out_shape=sum(outs, []), in_specs=sum(specs, []) + [...  9.16 us
    ppermute x2, waiting for transfers between devices, over_owners(): return lax.ppermute(part, 'pos', [(0, 1), (1, 0)])  7.46 us
    ppermute x9, starting transfers between devices, from_behind(): return lax.ppermute(block, 'tile', [(source(i), i) for i in range(tiles)])  7.36 us
    unnamed x10, local copies, waits for them, and re-layouts  2.67 us
    ppermute x2, starting transfers between devices, over_owners(): return lax.ppermute(part, 'pos', [(0, 1), (1, 0)])  2.55 us
  transfers between devices with their start and end apart: 23, of which 12 were waited for; matrix products, arithmetic and copies ran while one was open for 0% of the time, Pallas kernels for 8%

profile of v5, /device:TPU:0, one launch (start us, length us, event | category | flops | bytes accessed | tf_op | source)
XLA Modules:
  0.0 76.6 jit_solution(11006256156077740145)
XLA Ops:
  0.6 1.2 %slice_bitcast_fusion = (bf16[2,256,256]{2,1,0:T(8,128)(2,1)S(1)}, bf16[2,256,256]{2,1,0:T(8,128)(2,1)S(1)}) fusion(bf16[1,2,2,256,256]{4,3,2,1,0:T(8,128)(2,1)} %param.7), kind=kLoop, calls=%fused_computation | loop fusion | bytes 1048576 | tf_op jit(solution)/shard_map/squeeze | solution.py:430
  1.8 5.1 %collective-permute-start.4 = (bf16[2,256,256]{2,1,0:T(8,128)(2,1)S(1)}, bf16[2,256,256]{2,1,0:T(8,128)(2,1)S(1)}, u32[]{:S(2)}, u32[]{:S(2)}) collective-permute-start(bf16[2,256,256]{2,1,0:T(8,128)(2,1)S(1)} %get-tuple-element.51.refs_6_.refs_2_.refs_0_), channel_id=1, source_target_pairs={{8,0},{10,2},{12,4},{14,6},{16,8},{18,10},{20,12},{22,14},{24,16},... | collective-permute-start | bytes 786440 | tf_op jit(solution)/shard_map/ppermute | solution.py:29
  6.9 0.7 collective-permute-start.1
  8.2 0.7 copy-done.3
  8.9 1.0 %copy-done.1 = bf16[512,512]{1,0:T(8,128)(2,1)S(1)} copy-done((bf16[512,512]{1,0:T(8,128)(2,1)S(1)}, bf16[512,512]{1,0:T(8,128)(2,1)}, u32[]{:S(2)}) %copy-start.1) | copy-done | bytes 524312
  9.9 0.9 %copy-done.2 = bf16[1,1,2,256,256]{4,3,2,1,0:T(8,128)(2,1)S(1)} copy-done((bf16[1,1,2,256,256]{4,3,2,1,0:T(8,128)(2,1)S(1)}, bf16[1,1,2,256,256]{4,3,2,1,0:T(8,128)(2,1)}, u32[]{:S(2)}) %copy-start.2) | copy-done | bytes 262168
  10.9 0.7 shard_map.86
  11.6 0.5 collective-permute-start.2
  12.1 0.7 collective-permute-done.4.refs_4_
  12.8 1.5 %collective-permute-start = (bf16[272,256]{1,0:T(8,128)(2,1)S(1)}, bf16[272,256]{1,0:T(8,128)(2,1)S(1)}, u32[]{:S(2)}, u32[]{:S(2)}) collective-permute-start(bf16[272,256]{1,0:T(8,128)(2,1)S(1)} %get-tuple-element.27), channel_id=1, source_target_pairs={{0,1},{1,0},{2,3},{3,2},{4,5},{5,4},{6,7},{7,6},{8,9},{9,8},{10,11... | collective-permute-start | bytes 417800 | tf_op jit(solution)/shard_map/ppermute | solution.py:447
  14.3 5.4 %collective-permute-done.2.refs_4_ = bf16[2,256,256]{2,1,0:T(8,128)(2,1)S(1)} collective-permute-done((bf16[2,256,256]{2,1,0:T(8,128)(2,1)S(1)}, bf16[2,256,256]{2,1,0:T(8,128)(2,1)S(1)}, u32[]{:S(2)}, u32[]{:S(2)}) %collective-permute-start.2) | collective-permute-done | bytes 262176 | tf_op jit(solution)/shard_map/ppermute | solution.py:29
  19.7 0.8 %collective-permute-start.3 = (bf16[2,256,256]{2,1,0:T(8,128)(2,1)S(1)}, bf16[2,256,256]{2,1,0:T(8,128)(2,1)S(1)}, u32[]{:S(2)}, u32[]{:S(2)}) collective-permute-start(bf16[2,256,256]{2,1,0:T(8,128)(2,1)S(1)} %collective-permute-done.2.refs_4_), channel_id=1, source_target_pairs={{2,0},{4,2},{6,4},{0,6},{10,8},{12,10},{14,12},{8,14},{18,16},{20,... | collective-permute-start | bytes 786440 | tf_op jit(solution)/shard_map/ppermute | solution.py:29
  20.5 1.7 %shard_map.87 = (bf16[2,256,256]{2,1,0:T(8,128)(2,1)S(1)}, f32[2,256,512]{2,1,0:T(8,128)S(1)}) custom-call(bf16[272,256]{1,0:T(8,128)(2,1)S(1)} %get-tuple-element.26.refs_0_.refs_2_, bf16[272,256]{1,0:T(8,128)(2,1)S(1)} %collective-permute-done.refs_1_.refs_3_, bf16[2,256,256]{2,1,0:T(8,128)(2,1)S(1)} %get-tuple-element.51.refs_6_.refs_2_.refs_0_, ...), custom_call_target="tpu_custom_call" | custom-call | flops 1500000000 | bytes 4472832 | tf_op jit(solution)/shard_map/pallas_call | solution.py:279
  22.3 2.1 %collective-permute-done.3.refs_5_ = bf16[2,256,256]{2,1,0:T(8,128)(2,1)S(1)} collective-permute-done((bf16[2,256,256]{2,1,0:T(8,128)(2,1)S(1)}, bf16[2,256,256]{2,1,0:T(8,128)(2,1)S(1)}, u32[]{:S(2)}, u32[]{:S(2)}) %collective-permute-start.3) | collective-permute-done | bytes 262176 | tf_op jit(solution)/shard_map/ppermute | solution.py:29
  24.4 4.2 %shard_map.88 = (bf16[2,256,256]{2,1,0:T(8,128)(2,1)S(1)}, bf16[2,256,256]{2,1,0:T(8,128)(2,1)S(1)}, bf16[528,256]{1,0:T(8,128)(2,1)S(1)}, bf16[2,256,256]{2,1,0...) custom-call(bf16[272,256]{1,0:T(8,128)(2,1)S(1)} %get-tuple-element.26.refs_0_.refs_2_, ...), custom_call_target="tpu_custom_call" | custom-call | flops 4000000000 | bytes 6578176 | tf_op jit(solution)/shard_map/pallas_call | solution.py:279
  28.6 1.0 %collective-permute-start.6 = (bf16[256,512]{1,0:T(8,128)(2,1)S(1)}, bf16[256,512]{1,0:T(8,128)(2,1)S(1)}, u32[]{:S(2)}, u32[]{:S(2)}) collective-permute-start(bf16[256,512]{1,0:T(8,128)(2,1)S(1)} %get-tuple-element.34), channel_id=1, source_target_pairs={{0,2},{1,3},{2,0},{3,1},{4,6},{5,7},{6,4},{7,5},{8,10},{9,11},{10,... | collective-permute-start | bytes 786440 | tf_op jit(solution)/shard_map/ppermute | solution.py:392
  29.6 1.2 %collective-permute-done.6.refs_1_ = bf16[256,512]{1,0:T(8,128)(2,1)S(1)} collective-permute-done((bf16[256,512]{1,0:T(8,128)(2,1)S(1)}, bf16[256,512]{1,0:T(8,128)(2,1)S(1)}, u32[]{:S(2)}, u32[]{:S(2)}) %collective-permute-start.6) | collective-permute-done | bytes 262176 | tf_op jit(solution)/shard_map/ppermute | solution.py:392
  30.8 0.8 %shard_map.89 = (f32[64,512]{1,0:T(8,128)S(1)}, bf16[64,512]{1,0:T(8,128)(2,1)S(1)}, bf16[64,512]{1,0:T(8,128)(2,1)S(1)}, bf16[64,512]{1,0:T(8,128)(2,1)S(1)}, b...) custom-call(bf16[256,512]{1,0:T(8,128)(2,1)S(1)} %get-tuple-element.33.refs_0_, ...), custom_call_target="tpu_custom_call" | custom-call | flops 1000000 | bytes 2187264 | tf_op jit(solution)/shard_map/pallas_call | solution.py:279
  31.6 0.1 collective-permute-start.7
  31.6 1.6 %collective-permute-start.9 = (bf16[64,512]{1,0:T(8,128)(2,1)S(1)}, bf16[64,512]{1,0:T(8,128)(2,1)S(1)}, u32[]{:S(2)}, u32[]{:S(2)}) collective-permute-start(bf16[64,512]{1,0:T(8,128)(2,1)S(1)} %get-tuple-element.42), channel_id=1, source_target_pairs={{0,1},{1,0},{2,3},{3,2},{4,5},{5,4},{6,7},{7,6},{8,9},{9,8},{10,11... | collective-permute-start | bytes 196616 | tf_op jit(solution)/shard_map/ppermute | solution.py:392
  33.2 1.4 %collective-permute-start.10 = (bf16[64,512]{1,0:T(8,128)(2,1)S(1)}, bf16[64,512]{1,0:T(8,128)(2,1)S(1)}, u32[]{:S(2)}, u32[]{:S(2)}) collective-permute-start(bf16[64,512]{1,0:T(8,128)(2,1)S(1)} %get-tuple-element.43), channel_id=1, source_target_pairs={{0,4},{1,5},{2,6},{3,7},{4,0},{5,1},{6,2},{7,3},{8,12},{9,13},{10,... | collective-permute-start | bytes 196616 | tf_op jit(solution)/shard_map/ppermute | solution.py:392
  34.6 0.6 collective-permute-start.11
  35.2 5.6 %collective-permute-done.8.refs_1_ = bf16[528,256]{1,0:T(8,128)(2,1)S(1)} collective-permute-done((bf16[528,256]{1,0:T(8,128)(2,1)S(1)}, bf16[528,256]{1,0:T(8,128)(2,1)S(1)}, u32[]{:S(2)}, u32[]{:S(2)}) %collective-permute-start.8) | collective-permute-done | bytes 270368 | tf_op jit(solution)/shard_map/ppermute | solution.py:29
  40.8 0.1 shard_map.90
  41.0 1.6 %collective-permute-start.12 = (bf16[64,512]{1,0:T(8,128)(2,1)S(1)}, bf16[64,512]{1,0:T(8,128)(2,1)S(1)}, u32[]{:S(2)}, u32[]{:S(2)}) collective-permute-start(bf16[64,512]{1,0:T(8,128)(2,1)S(1)} %get-tuple-element.45.refs_0_), channel_id=1, source_target_pairs={{0,8},{1,9},{2,10},{3,11},{4,12},{5,13},{6,14},{7,15},{8,0},{9,1},... | collective-permute-start | bytes 196616 | tf_op jit(solution)/shard_map/ppermute | solution.py:392
  42.6 4.5 %collective-permute-done.12.refs_2_.refs_1_ = bf16[64,512]{1,0:T(8,128)(2,1)S(1)} collective-permute-done((bf16[64,512]{1,0:T(8,128)(2,1)S(1)}, bf16[64,512]{1,0:T(8,128)(2,1)S(1)}, u32[]{:S(2)}, u32[]{:S(2)}) %collective-permute-start.12) | collective-permute-done | bytes 65568 | tf_op jit(solution)/shard_map/ppermute | solution.py:392
  47.0 0.1 shard_map.91.refs_3_
  47.1 0.2 collective-permute-start.13
  47.3 1.4 %collective-permute-start.15 = (bf16[64,512]{1,0:T(8,128)(2,1)S(1)}, bf16[64,512]{1,0:T(8,128)(2,1)S(1)}, u32[]{:S(2)}, u32[]{:S(2)}) collective-permute-start(bf16[64,512]{1,0:T(8,128)(2,1)S(1)} %get-tuple-element.45.refs_0_), channel_id=1, source_target_pairs={{0,24},{1,25},{2,26},{3,27},{4,28},{5,29},{6,30},{7,31},{8,16},{9,... | collective-permute-start | bytes 196616 | tf_op jit(solution)/shard_map/ppermute | solution.py:392
  48.7 0.3 collective-permute-start.14
  48.9 0.1 shard_map.92.refs_4_.refs_1_
  49.1 4.7 %collective-permute-done.15.refs_3_ = bf16[64,512]{1,0:T(8,128)(2,1)S(1)} collective-permute-done((bf16[64,512]{1,0:T(8,128)(2,1)S(1)}, bf16[64,512]{1,0:T(8,128)(2,1)S(1)}, u32[]{:S(2)}, u32[]{:S(2)}) %collective-permute-start.15) | collective-permute-done | bytes 65568 | tf_op jit(solution)/shard_map/ppermute | solution.py:392
  53.8 2.9 %collective-permute-done.14.refs_2_ = bf16[64,512]{1,0:T(8,128)(2,1)S(1)} collective-permute-done((bf16[64,512]{1,0:T(8,128)(2,1)S(1)}, bf16[64,512]{1,0:T(8,128)(2,1)S(1)}, u32[]{:S(2)}, u32[]{:S(2)}) %collective-permute-start.14) | collective-permute-done | bytes 65568 | tf_op jit(solution)/shard_map/ppermute | solution.py:392
  56.7 0.1 shard_map.93.refs_0_
  56.8 1.3 %collective-permute-start.17 = (bf16[64,512]{1,0:T(8,128)(2,1)S(1)}, bf16[64,512]{1,0:T(8,128)(2,1)S(1)}, u32[]{:S(2)}, u32[]{:S(2)}) collective-permute-start(bf16[64,512]{1,0:T(8,128)(2,1)S(1)} %shard_map.93.refs_0_), channel_id=1, source_target_pairs={{0,4},{1,5},{2,6},{3,7},{4,0},{5,1},{6,2},{7,3},{8,12},{9,13},{10,... | collective-permute-start | bytes 196616 | tf_op jit(solution)/shard_map/ppermute | solution.py:392
  58.1 1.8 %collective-permute-start.21 = (bf16[64,512]{1,0:T(8,128)(2,1)S(1)}, bf16[64,512]{1,0:T(8,128)(2,1)S(1)}, u32[]{:S(2)}, u32[]{:S(2)}) collective-permute-start(bf16[64,512]{1,0:T(8,128)(2,1)S(1)} %shard_map.93.refs_0_), channel_id=1, source_target_pairs={{0,5},{1,4},{2,7},{3,6},{4,1},{5,0},{6,3},{7,2},{8,13},{9,12},{10,... | collective-permute-start | bytes 196616 | tf_op jit(solution)/shard_map/ppermute | solution.py:392
  59.9 0.5 collective-permute-start.20
  60.4 1.5 %collective-permute-start.19 = (bf16[2,256,256]{2,1,0:T(8,128)(2,1)S(1)}, bf16[2,256,256]{2,1,0:T(8,128)(2,1)S(1)}, u32[]{:S(2)}, u32[]{:S(2)}) collective-permute-start(bf16[2,256,256]{2,1,0:T(8,128)(2,1)S(1)} %shard_map.92.refs_4_.refs_1_), channel_id=1, source_target_pairs={{0,1},{1,0},{2,3},{3,2},{4,5},{5,4},{6,7},{7,6},{8,9},{9,8},{10,11... | collective-permute-start | bytes 786440 | tf_op jit(solution)/shard_map/ppermute | solution.py:476
  61.9 0.1 shard_map.94.refs_4_.refs_1_
  62.0 1.6 %collective-permute-done.21.refs_3_ = bf16[64,512]{1,0:T(8,128)(2,1)S(1)} collective-permute-done((bf16[64,512]{1,0:T(8,128)(2,1)S(1)}, bf16[64,512]{1,0:T(8,128)(2,1)S(1)}, u32[]{:S(2)}, u32[]{:S(2)}) %collective-permute-start.21) | collective-permute-done | bytes 65568 | tf_op jit(solution)/shard_map/ppermute | solution.py:392
  63.6 1.4 %collective-permute-done.20.refs_1_ = bf16[64,512]{1,0:T(8,128)(2,1)S(1)} collective-permute-done((bf16[64,512]{1,0:T(8,128)(2,1)S(1)}, bf16[64,512]{1,0:T(8,128)(2,1)S(1)}, u32[]{:S(2)}, u32[]{:S(2)}) %collective-permute-start.20) | collective-permute-done | bytes 65568 | tf_op jit(solution)/shard_map/ppermute | solution.py:392
  65.1 0.1 collective-permute-start.22
  65.2 1.0 %collective-permute-start.18 = (bf16[2,256,256]{2,1,0:T(8,128)(2,1)S(1)}, bf16[2,256,256]{2,1,0:T(8,128)(2,1)S(1)}, u32[]{:S(2)}, u32[]{:S(2)}) collective-permute-start(bf16[2,256,256]{2,1,0:T(8,128)(2,1)S(1)} %shard_map.94.refs_4_.refs_1_), channel_id=1, source_target_pairs={{0,1},{1,0},{2,3},{3,2},{4,5},{5,4},{6,7},{7,6},{8,9},{9,8},{10,11... | collective-permute-start | bytes 786440 | tf_op jit(solution)/shard_map/ppermute | solution.py:476
  66.2 4.4 %collective-permute-done.19.refs_2_ = bf16[2,256,256]{2,1,0:T(8,128)(2,1)S(1)} collective-permute-done((bf16[2,256,256]{2,1,0:T(8,128)(2,1)S(1)}, bf16[2,256,256]{2,1,0:T(8,128)(2,1)S(1)}, u32[]{:S(2)}, u32[]{:S(2)}) %collective-permute-start.19) | collective-permute-done | bytes 262176 | tf_op jit(solution)/shard_map/ppermute | solution.py:476
  70.7 0.8 %shard_map.95.refs_3_ = bf16[1,2,2,256,256]{4,3,2,1,0:T(8,128)(2,1)} custom-call(bf16[2,256,256]{2,1,0:T(8,128)(2,1)S(1)} %get-tuple-element.28.refs_2_.refs_0_, bf16[2,256,256]{2,1,0:T(8,128)(2,1)S(1)} %shard_map.92.refs_4_.refs_1_, bf16[2,256,256]{2,1,0:T(8,128)(2,1)S(1)} %collective-permute-done.19.refs_2_), custom_call_target="tpu_custom_call" | custom-call | flops 131072 | bytes 1048576 | tf_op jit(solution)/shard_map/pallas_call | solution.py:296
  71.5 1.2 %shard_map.97 = (f32[2048,128]{1,0:T(8,128)}, f32[8,128]{1,0:T(8,128)S(1)}) custom-call(bf16[256,512]{1,0:T(8,128)(2,1)S(1)} %shard_map.96.refs_0_, bf16[256,512]{1,0:T(8,128)(2,1)S(1)} %collective-permute-done.22.refs_1_, f32[2048,128]{1,0:T(8,128)S(1)} %bitcast.16), custom_call_target="tpu_custom_call" | custom-call | flops 1000000 | bytes 2625536 | tf_op jit(solution)/shard_map/pallas_call | solution.py:279
  72.7 3.0 %collective-permute-done.18.refs_2_ = bf16[2,256,256]{2,1,0:T(8,128)(2,1)S(1)} collective-permute-done((bf16[2,256,256]{2,1,0:T(8,128)(2,1)S(1)}, bf16[2,256,256]{2,1,0:T(8,128)(2,1)S(1)}, u32[]{:S(2)}, u32[]{:S(2)}) %collective-permute-start.18) | collective-permute-done | bytes 262176 | tf_op jit(solution)/shard_map/ppermute | solution.py:476
  75.7 0.8 %shard_map.98 = bf16[1,2,2,256,256]{4,3,2,1,0:T(8,128)(2,1)} custom-call(bf16[2,256,256]{2,1,0:T(8,128)(2,1)S(1)} %get-tuple-element.51.refs_6_.refs_2_.refs_0_, bf16[2,256,256]{2,1,0:T(8,128)(2,1)S(1)} %shard_map.94.refs_4_.refs_1_, bf16[2,256,256]{2,1,0:T(8,128)(2,1)S(1)} %collective-permute-done.18.refs_2_, ...), custom_call_target="tpu_custom_call", output_to_operand_aliasing={{}: (3, {})} | custom-call | flops 131072 | bytes 1048576 | tf_op jit(solution)/shard_map/pallas_call | solution.py:296
  (22 shorter events, 0.2 us)
Async XLA Ops:
  0.6 7.6 %copy-start = (f32[2,256,2,256]{3,2,1,0:T(2,128)S(1)}, f32[2,256,2,256]{3,2,1,0:T(2,128)}, u32[]{:S(2)}) copy-start(f32[2,256,2,256]{3,2,1,0:T(2,128)} %param.8) | copy-start | bytes 3145732
  1.8 11.0 %collective-permute-start.4 = (bf16[2,256,256]{2,1,0:T(8,128)(2,1)S(1)}, bf16[2,256,256]{2,1,0:T(8,128)(2,1)S(1)}, u32[]{:S(2)}, u32[]{:S(2)}) collective-permute-start(bf16[2,256,256]{2,1,0:T(8,128)(2,1)S(1)} %get-tuple-element.51.refs_6_.refs_2_.refs_0_), channel_id=1, source_target_pairs={{8,0},{10,2},{12,4},{14,6},{16,8},{18,10},{20,12},{22,14},{24,16},... | collective-permute-start | bytes 786440 | tf_op jit(solution)/shard_map/ppermute | solution.py:29
  6.9 13.6 %collective-permute-start.1 = (bf16[2,2,256,256]{3,2,1,0:T(8,128)(2,1)}, bf16[2,2,256,256]{3,2,1,0:T(8,128)(2,1)S(1)}, u32[]{:S(2)}, u32[]{:S(2)}) collective-permute-start(bf16[2,2,256,256]{3,2,1,0:T(8,128)(2,1)} %bitcast.17), channel_id=1, source_target_pairs={{2,0},{4,2},{6,4},{0,6},{10,8},{12,10},{14,12},{8,14},{18,16},{20,... | collective-permute-start | bytes 1572872 | tf_op jit(solution)/shard_map/ppermute | solution.py:29
  8.2 0.7 copy-start.3
  8.9 1.0 %copy-start.1 = (bf16[512,512]{1,0:T(8,128)(2,1)S(1)}, bf16[512,512]{1,0:T(8,128)(2,1)}, u32[]{:S(2)}) copy-start(bf16[512,512]{1,0:T(8,128)(2,1)} %constant.10.refs_5_) | copy-start | bytes 1572868
  9.9 0.9 %copy-start.2 = (bf16[1,1,2,256,256]{4,3,2,1,0:T(8,128)(2,1)S(1)}, bf16[1,1,2,256,256]{4,3,2,1,0:T(8,128)(2,1)}, u32[]{:S(2)}) copy-start(bf16[1,1,2,256,256]{4,3,2,1,0:T(8,128)(2,1)} %refs_3_.1) | copy-start | bytes 786436
  11.6 8.1 %collective-permute-start.2 = (bf16[2,256,256]{2,1,0:T(8,128)(2,1)S(1)}, bf16[2,256,256]{2,1,0:T(8,128)(2,1)S(1)}, u32[]{:S(2)}, u32[]{:S(2)}) collective-permute-start(bf16[2,256,256]{2,1,0:T(8,128)(2,1)S(1)} %get-tuple-element.28.refs_2_.refs_0_), channel_id=1, source_target_pairs={{8,0},{10,2},{12,4},{14,6},{16,8},{18,10},{20,12},{22,14},{24,16},... | collective-permute-start | bytes 786440 | tf_op jit(solution)/shard_map/ppermute | solution.py:29
  12.8 7.7 %collective-permute-start.5 = (bf16[2,256,256]{2,1,0:T(8,128)(2,1)S(1)}, bf16[2,256,256]{2,1,0:T(8,128)(2,1)S(1)}, u32[]{:S(2)}, u32[]{:S(2)}) collective-permute-start(bf16[2,256,256]{2,1,0:T(8,128)(2,1)S(1)} %collective-permute-done.4.refs_4_), channel_id=1, source_target_pairs={{2,0},{4,2},{6,4},{0,6},{10,8},{12,10},{14,12},{8,14},{18,16},{20,... | collective-permute-start | bytes 786440 | tf_op jit(solution)/shard_map/ppermute | solution.py:29
  12.8 7.7 %collective-permute-start = (bf16[272,256]{1,0:T(8,128)(2,1)S(1)}, bf16[272,256]{1,0:T(8,128)(2,1)S(1)}, u32[]{:S(2)}, u32[]{:S(2)}) collective-permute-start(bf16[272,256]{1,0:T(8,128)(2,1)S(1)} %get-tuple-element.27), channel_id=1, source_target_pairs={{0,1},{1,0},{2,3},{3,2},{4,5},{5,4},{6,7},{7,6},{8,9},{9,8},{10,11... | collective-permute-start | bytes 417800 | tf_op jit(solution)/shard_map/ppermute | solution.py:447
  19.7 4.7 %collective-permute-start.3 = (bf16[2,256,256]{2,1,0:T(8,128)(2,1)S(1)}, bf16[2,256,256]{2,1,0:T(8,128)(2,1)S(1)}, u32[]{:S(2)}, u32[]{:S(2)}) collective-permute-start(bf16[2,256,256]{2,1,0:T(8,128)(2,1)S(1)} %collective-permute-done.2.refs_4_), channel_id=1, source_target_pairs={{2,0},{4,2},{6,4},{0,6},{10,8},{12,10},{14,12},{8,14},{18,16},{20,... | collective-permute-start | bytes 786440 | tf_op jit(solution)/shard_map/ppermute | solution.py:29
  20.5 3.9 %copy-start.4 = (bf16[512,512]{1,0:T(8,128)(2,1)S(1)}, bf16[512,512]{1,0:T(8,128)(2,1)}, u32[]{:S(2)}) copy-start(bf16[512,512]{1,0:T(8,128)(2,1)} %constant.11.refs_10_) | copy-start | bytes 1572868
  28.6 2.2 %collective-permute-start.6 = (bf16[256,512]{1,0:T(8,128)(2,1)S(1)}, bf16[256,512]{1,0:T(8,128)(2,1)S(1)}, u32[]{:S(2)}, u32[]{:S(2)}) collective-permute-start(bf16[256,512]{1,0:T(8,128)(2,1)S(1)} %get-tuple-element.34), channel_id=1, source_target_pairs={{0,2},{1,3},{2,0},{3,1},{4,6},{5,7},{6,4},{7,5},{8,10},{9,11},{10,... | collective-permute-start | bytes 786440 | tf_op jit(solution)/shard_map/ppermute | solution.py:392
  29.6 11.1 %collective-permute-start.8 = (bf16[528,256]{1,0:T(8,128)(2,1)S(1)}, bf16[528,256]{1,0:T(8,128)(2,1)S(1)}, u32[]{:S(2)}, u32[]{:S(2)}) collective-permute-start(bf16[528,256]{1,0:T(8,128)(2,1)S(1)} %get-tuple-element.40), channel_id=1, source_target_pairs={{24,0},{26,2},{28,4},{30,6},{0,8},{2,10},{4,12},{6,14},{8,16},{10,... | collective-permute-start | bytes 811016 | tf_op jit(solution)/shard_map/ppermute | solution.py:29
  31.6 15.5 %collective-permute-start.7 = (bf16[528,256]{1,0:T(8,128)(2,1)S(1)}, bf16[528,256]{1,0:T(8,128)(2,1)S(1)}, u32[]{:S(2)}, u32[]{:S(2)}) collective-permute-start(bf16[528,256]{1,0:T(8,128)(2,1)S(1)} %get-tuple-element.37), channel_id=1, source_target_pairs={{24,0},{26,2},{28,4},{30,6},{0,8},{2,10},{4,12},{6,14},{8,16},{10,... | collective-permute-start | bytes 811016 | tf_op jit(solution)/shard_map/ppermute | solution.py:29
  31.6 9.1 %collective-permute-start.9 = (bf16[64,512]{1,0:T(8,128)(2,1)S(1)}, bf16[64,512]{1,0:T(8,128)(2,1)S(1)}, u32[]{:S(2)}, u32[]{:S(2)}) collective-permute-start(bf16[64,512]{1,0:T(8,128)(2,1)S(1)} %get-tuple-element.42), channel_id=1, source_target_pairs={{0,1},{1,0},{2,3},{3,2},{4,5},{5,4},{6,7},{7,6},{8,9},{9,8},{10,11... | collective-permute-start | bytes 196616 | tf_op jit(solution)/shard_map/ppermute | solution.py:392
  33.2 7.5 %collective-permute-start.10 = (bf16[64,512]{1,0:T(8,128)(2,1)S(1)}, bf16[64,512]{1,0:T(8,128)(2,1)S(1)}, u32[]{:S(2)}, u32[]{:S(2)}) collective-permute-start(bf16[64,512]{1,0:T(8,128)(2,1)S(1)} %get-tuple-element.43), channel_id=1, source_target_pairs={{0,4},{1,5},{2,6},{3,7},{4,0},{5,1},{6,2},{7,3},{8,12},{9,13},{10,... | collective-permute-start | bytes 196616 | tf_op jit(solution)/shard_map/ppermute | solution.py:392
  34.6 6.2 %collective-permute-start.11 = (bf16[64,512]{1,0:T(8,128)(2,1)S(1)}, bf16[64,512]{1,0:T(8,128)(2,1)S(1)}, u32[]{:S(2)}, u32[]{:S(2)}) collective-permute-start(bf16[64,512]{1,0:T(8,128)(2,1)S(1)} %get-tuple-element.44), channel_id=1, source_target_pairs={{0,5},{1,4},{2,7},{3,6},{4,1},{5,0},{6,3},{7,2},{8,13},{9,12},{10,... | collective-permute-start | bytes 196616 | tf_op jit(solution)/shard_map/ppermute | solution.py:392
  40.9 8.1 %collective-permute-start.16 = (bf16[2,256,256]{2,1,0:T(8,128)(2,1)S(1)}, bf16[2,256,256]{2,1,0:T(8,128)(2,1)S(1)}, u32[]{:S(2)}, u32[]{:S(2)}) collective-permute-start(bf16[2,256,256]{2,1,0:T(8,128)(2,1)S(1)} %get-tuple-element.47), channel_id=1, source_target_pairs={{6,0},{0,2},{2,4},{4,6},{14,8},{8,10},{10,12},{12,14},{22,16},{16,... | collective-permute-start | bytes 786440 | tf_op jit(solution)/shard_map/ppermute | solution.py:29
  41.0 6.1 %collective-permute-start.12 = (bf16[64,512]{1,0:T(8,128)(2,1)S(1)}, bf16[64,512]{1,0:T(8,128)(2,1)S(1)}, u32[]{:S(2)}, u32[]{:S(2)}) collective-permute-start(bf16[64,512]{1,0:T(8,128)(2,1)S(1)} %get-tuple-element.45.refs_0_), channel_id=1, source_target_pairs={{0,8},{1,9},{2,10},{3,11},{4,12},{5,13},{6,14},{7,15},{8,0},{9,1},... | collective-permute-start | bytes 196616 | tf_op jit(solution)/shard_map/ppermute | solution.py:392
  47.1 14.8 %collective-permute-start.13 = (bf16[2,256,256]{2,1,0:T(8,128)(2,1)S(1)}, bf16[2,256,256]{2,1,0:T(8,128)(2,1)S(1)}, u32[]{:S(2)}, u32[]{:S(2)}) collective-permute-start(bf16[2,256,256]{2,1,0:T(8,128)(2,1)S(1)} %shard_map.91.refs_3_), channel_id=1, source_target_pairs={{6,0},{0,2},{2,4},{4,6},{14,8},{8,10},{10,12},{12,14},{22,16},{16,... | collective-permute-start | bytes 786440 | tf_op jit(solution)/shard_map/ppermute | solution.py:29
  47.3 6.5 %collective-permute-start.15 = (bf16[64,512]{1,0:T(8,128)(2,1)S(1)}, bf16[64,512]{1,0:T(8,128)(2,1)S(1)}, u32[]{:S(2)}, u32[]{:S(2)}) collective-permute-start(bf16[64,512]{1,0:T(8,128)(2,1)S(1)} %get-tuple-element.45.refs_0_), channel_id=1, source_target_pairs={{0,24},{1,25},{2,26},{3,27},{4,28},{5,29},{6,30},{7,31},{8,16},{9,... | collective-permute-start | bytes 196616 | tf_op jit(solution)/shard_map/ppermute | solution.py:392
  48.7 8.1 %collective-permute-start.14 = (bf16[64,512]{1,0:T(8,128)(2,1)S(1)}, bf16[64,512]{1,0:T(8,128)(2,1)S(1)}, u32[]{:S(2)}, u32[]{:S(2)}) collective-permute-start(bf16[64,512]{1,0:T(8,128)(2,1)S(1)} %get-tuple-element.45.refs_0_), channel_id=1, source_target_pairs={{0,16},{1,17},{2,18},{3,19},{4,20},{5,21},{6,22},{7,23},{8,24},{9,... | collective-permute-start | bytes 196616 | tf_op jit(solution)/shard_map/ppermute | solution.py:392
  56.8 5.1 %collective-permute-start.17 = (bf16[64,512]{1,0:T(8,128)(2,1)S(1)}, bf16[64,512]{1,0:T(8,128)(2,1)S(1)}, u32[]{:S(2)}, u32[]{:S(2)}) collective-permute-start(bf16[64,512]{1,0:T(8,128)(2,1)S(1)} %shard_map.93.refs_0_), channel_id=1, source_target_pairs={{0,4},{1,5},{2,6},{3,7},{4,0},{5,1},{6,2},{7,3},{8,12},{9,13},{10,... | collective-permute-start | bytes 196616 | tf_op jit(solution)/shard_map/ppermute | solution.py:392
  58.1 5.5 %collective-permute-start.21 = (bf16[64,512]{1,0:T(8,128)(2,1)S(1)}, bf16[64,512]{1,0:T(8,128)(2,1)S(1)}, u32[]{:S(2)}, u32[]{:S(2)}) collective-permute-start(bf16[64,512]{1,0:T(8,128)(2,1)S(1)} %shard_map.93.refs_0_), channel_id=1, source_target_pairs={{0,5},{1,4},{2,7},{3,6},{4,1},{5,0},{6,3},{7,2},{8,13},{9,12},{10,... | collective-permute-start | bytes 196616 | tf_op jit(solution)/shard_map/ppermute | solution.py:392
  59.9 5.2 %collective-permute-start.20 = (bf16[64,512]{1,0:T(8,128)(2,1)S(1)}, bf16[64,512]{1,0:T(8,128)(2,1)S(1)}, u32[]{:S(2)}, u32[]{:S(2)}) collective-permute-start(bf16[64,512]{1,0:T(8,128)(2,1)S(1)} %shard_map.93.refs_0_), channel_id=1, source_target_pairs={{0,1},{1,0},{2,3},{3,2},{4,5},{5,4},{6,7},{7,6},{8,9},{9,8},{10,11... | collective-permute-start | bytes 196616 | tf_op jit(solution)/shard_map/ppermute | solution.py:392
  60.4 10.3 %collective-permute-start.19 = (bf16[2,256,256]{2,1,0:T(8,128)(2,1)S(1)}, bf16[2,256,256]{2,1,0:T(8,128)(2,1)S(1)}, u32[]{:S(2)}, u32[]{:S(2)}) collective-permute-start(bf16[2,256,256]{2,1,0:T(8,128)(2,1)S(1)} %shard_map.92.refs_4_.refs_1_), channel_id=1, source_target_pairs={{0,1},{1,0},{2,3},{3,2},{4,5},{5,4},{6,7},{7,6},{8,9},{9,8},{10,11... | collective-permute-start | bytes 786440 | tf_op jit(solution)/shard_map/ppermute | solution.py:476
  65.1 6.4 %collective-permute-start.22 = (bf16[256,512]{1,0:T(8,128)(2,1)S(1)}, bf16[256,512]{1,0:T(8,128)(2,1)S(1)}, u32[]{:S(2)}, u32[]{:S(2)}) collective-permute-start(bf16[256,512]{1,0:T(8,128)(2,1)S(1)} %shard_map.96.refs_0_), channel_id=1, source_target_pairs={{0,2},{1,3},{2,0},{3,1},{4,6},{5,7},{6,4},{7,5},{8,10},{9,11},{10,... | collective-permute-start | bytes 786440 | tf_op jit(solution)/shard_map/ppermute | solution.py:392
  65.2 10.6 %collective-permute-start.18 = (bf16[2,256,256]{2,1,0:T(8,128)(2,1)S(1)}, bf16[2,256,256]{2,1,0:T(8,128)(2,1)S(1)}, u32[]{:S(2)}, u32[]{:S(2)}) collective-permute-start(bf16[2,256,256]{2,1,0:T(8,128)(2,1)S(1)} %shard_map.94.refs_4_.refs_1_), channel_id=1, source_target_pairs={{0,1},{1,0},{2,3},{3,2},{4,5},{5,4},{6,7},{7,6},{8,9},{9,8},{10,11... | collective-permute-start | bytes 786440 | tf_op jit(solution)/shard_map/ppermute | solution.py:476

commit v6 on v5

--- a/solution.py
+++ b/solution.py
@@ -19,14 +19,28 @@
 bf16 = jnp.bfloat16
 
 
-def from_behind(block, rows, cols):
+def from_left(block, cols):
     tiles = lax.axis_size("tile")
     across = tiles // GRID_ROWS
-
-    def source(i):
-        return (i // across - rows) % GRID_ROWS * across + (i % across - cols) % across
-
-    return lax.ppermute(block, "tile", [(source(i), i) for i in range(tiles)])
+    route = [(i // across * across + (i % across - cols) % across, i) for i in range(tiles)]
+    return lax.ppermute(block, "tile", route)
+
+
+def from_rows(block):
+    tiles = lax.axis_size("tile")
+    across = tiles // GRID_ROWS
+    blocks = []
+    for odd in range(2):
+        route = []
+        for i in range(tiles):
+            other = ((i // across + odd) ^ 1) - odd
+            route.append((i, i if other in (-1, GRID_ROWS) else other * across + i % across))
+        blocks.append(lax.ppermute(block, "tile", route))
+    return blocks
+
+
+def tile_row():
+    return lax.axis_index("tile") // (lax.axis_size("tile") // GRID_ROWS)
 
 
 def real_embed(part_re, part_im):
@@ -213,21 +227,36 @@
     spread(shifts, [grad_ref[part] for part in range(2)], home_ref, next_ref, down_ref)
 
 
-def beside_kernel(next_ref, above_ref, out_ref):
-    n = out_ref.shape[1]
-    split = above_ref[pl.ds(2 * n, 16), :].astype(f32)[0:1] > 0
-    for part in range(2):
-        above = above_ref[pl.ds(part * n, n), :].astype(f32)
-        total = next_ref[part].astype(f32) + jnp.where(split, above, 0.0)
+def below_kernel(even_ref, odd_ref, out_ref):
+    up = lax.rem(tile_row(), 2) == 0
+
+    @pl.when(up)
+    def _():
+        out_ref[...] = even_ref[...]
+
+    @pl.when(jnp.logical_not(up))
+    def _():
+        out_ref[...] = odd_ref[...]
+
+
+def above_parts(even_ref, odd_ref, n):
+    row = tile_row()
+    even, odd = even_ref[...].astype(f32), odd_ref[...].astype(f32)
+    above = jnp.where(lax.rem(row, 2) == 1, even, jnp.where(row == 0, jnp.zeros_like(odd), odd))
+    return [above[:n], above[n : 2 * n]], above[2 * n : 2 * n + 1] > 0
+
+
+def beside_kernel(next_ref, even_ref, odd_ref, out_ref):
+    above, split = above_parts(even_ref, odd_ref, out_ref.shape[1])
+    for part in range(2):
+        total = next_ref[part].astype(f32) + jnp.where(split, above[part], 0.0)
         out_ref[part] = total.astype(bf16)
 
 
-def part_kernel(home_ref, above_ref, left_ref, out_ref):
-    n = out_ref.shape[1]
-    split = above_ref[pl.ds(2 * n, 16), :].astype(f32)[0:1] > 0
-    for part in range(2):
-        above = above_ref[pl.ds(part * n, n), :].astype(f32)
-        total = home_ref[part].astype(f32) + jnp.where(split, 0.0, above)
+def part_kernel(home_ref, even_ref, odd_ref, left_ref, out_ref):
+    above, split = above_parts(even_ref, odd_ref, out_ref.shape[1])
+    for part in range(2):
+        total = home_ref[part].astype(f32) + jnp.where(split, 0.0, above[part])
         out_ref[part] = (total + left_ref[part].astype(f32)).astype(bf16)
 
 
@@ -428,8 +457,8 @@
     probe = probe.transpose(0, 1, 3, 2, 4).reshape(-1, 128)
 
     own = [tile_object[0, 0], tile_object[0, 1]]
-    below0 = from_behind(own[0], -1, 0)
-    right = from_behind(tile_object[0], 0, -1)
+    rows0 = from_rows(own[0])
+    right = from_left(tile_object[0], -1)
     exchanged = lax.axis_size("pos") == patterns.shape[2]
     message = shape_of(bf16, pixels + 16, pixels)
     own1, mine, sent, probe_planes, table = run(
@@ -442,13 +471,15 @@
         limit=16,
         after=[own[0]],
     )
-    below1 = from_behind(own1, -1, 0)
+    rows1 = from_rows(own1)
     if exchanged:
         sent = lax.ppermute(sent, "pos", [(i, 1 - i) for i in range(2)])
     else:
         sent = gathered_message(patterns, offsets, counts)
-    diag0 = from_behind(below0, 0, -1)
-    diag1 = from_behind(below1, 0, -1)
+    (below0,) = run(job(below_kernel, [tile], rows0))
+    diag0 = from_left(below0, -1)
+    (below1,) = run(job(below_kernel, [tile], rows1))
+    diag1 = from_left(below1, -1)
     near, arrive = run(
         job(
             arrive_kernel,
@@ -477,7 +508,7 @@
         return lax.psum(part.astype(f32), "pos") - part.astype(f32)
 
     core, groups = core_group(), exchange_groups()
-    above1 = from_behind(down1, 1, 0)
+    above1 = from_rows(down1)
     arrived = [swap_with(give, core, 1)]
     side = [job(spread_kernel, [tile, tile, down], [mine, sent, grad0])]
     scattered = []
@@ -486,30 +517,32 @@
         done = run(folded(group, keep, arrived), *side, limit=8)
         if side:
             done, (home0, next0, down0) = done
-            above0 = from_behind(down0, 1, 0)
+            above0 = from_rows(down0)
             side = []
         keep, *gives = done
         arrived = [swap_with(x, group, at) for at, x in enumerate(gives, 1)]
         scattered.append(group)
     (beside1,), (total,) = run(
-        job(beside_kernel, [tile], [next1, above1]),
+        job(beside_kernel, [tile], [next1, *above1]),
         job(add_kernel, [shape_of(bf16, *keep.shape)], [keep] + arrived),
     )
-    from_left1 = from_behind(beside1, 0, 1)
-    arrived = swapped(total, groups[0])
-    (beside0,) = run(job(beside_kernel, [tile], [next0, above0]), after=arrived[:1])
-    from_left0 = from_behind(beside0, 0, 1)
-    (part1,) = run(job(part_kernel, [tile], [home1, above1, from_left1]), after=[beside0])
-    other1 = over_owners(part1)
-    (total,) = run(joined(groups[0], total, arrived, True), after=[part1])
+    left1 = from_left(beside1, 1)
+    (total,), (part1,), (beside0,) = run(
+        joined(groups[0], total, swapped(total, groups[0]), True),
+        job(part_kernel, [tile], [home1, *above1, left1]),
+        job(beside_kernel, [tile], [next0, *above0]),
+    )
     for group in groups[1:]:
         (total,) = run(joined(group, total, swapped(total, group), True))
-    arrived = swapped(total, scattered[-1])
-    (part0,) = run(job(part_kernel, [tile], [home0, above0, from_left0]), after=arrived[1:2])
-    other0 = over_owners(part0)
-    (total,) = run(joined(scattered[-1], total, arrived, False), after=[part0])
+    other1 = over_owners(part1)
+    left0 = from_left(beside0, 1)
+    (total,), (part0,) = run(
+        joined(scattered[-1], total, swapped(total, scattered[-1]), False),
+        job(part_kernel, [tile], [home0, *above0, left0]),
+    )
     for group in reversed(scattered[:-1]):
         (total,) = run(joined(group, total, swapped(total, group), False))
+    other0 = over_owners(part0)
     other_half = swap_with(total, core, 1)
     positions_all = lax.axis_size("tile") * lax.axis_size("pos") * (patterns.shape[2] // 2)
     step = probe_rate / math.sqrt(positions_all)

time: 76.8 us -> 81.6 us (1.062)
  starting transfers between devices: 22.9 us -> 37.8 us
  waiting for transfers between devices: 37.6 us -> 26.9 us
    ppermute x9 -> x13, starting transfers between devices: 7.36 us -> 20.7 us  [the longest x8 18.9 us: from_rows(): blocks.append(lax.ppermute(block, 'tile', route))]
    ppermute x9 -> x13, waiting for transfers between devices: 13.8 us -> 7.86 us  [the longest x8 5.71 us: from_rows(): blocks.append(lax.ppermute(block, 'tile', route))]
    ppermute x11, waiting for transfers between devices: 16.3 us -> 12.1 us  [swap_with(): lax.ppermute(x, ('tile', 'pos'), [(i, i ^ mask) for i in range(devices)])]
    ppermute x11, starting transfers between devices: 11.5 us -> 12.6 us  [swap_with(): lax.ppermute(x, ('tile', 'pos'), [(i, i ^ mask) for i in range(devices)])]
    pallas_call x11 -> x10, Pallas kernels: 9.16 us -> 9.63 us  [run(): pl.pallas_call(body, out_shape=sum(outs, []), in_specs=sum(specs, []) + [...]
  transfers between devices with their start and end apart: 23 -> 27, of which waited for: 12 -> 11; matrix products, arithmetic and copies ran while one was open for 0% -> 0% of each run, Pallas kernels for 8% -> 7%
where the time goes in v6:
time: 81.6 us; the launch traced here: 81.3 us
  starting transfers between devices  37.8 us (46%)
  waiting for transfers between devices  26.9 us (33%)
  Pallas kernels  11.3 us (14%)
  local copies, waits for them, and re-layouts  3.82 us (5%)
  between operations  1.47 us (2%)
    ppermute x8, starting transfers between devices, from_rows(): blocks.append(lax.ppermute(block, 'tile', route))  18.9 us
    ppermute x11, starting transfers between devices, swap_with(): lax.ppermute(x, ('tile', 'pos'), [(i, i ^ mask) for i in range(devices)])  12.6 us
    ppermute x11, waiting for transfers between devices, swap_with(): lax.ppermute(x, ('tile', 'pos'), [(i, i ^ mask) for i in range(devices)])  12.1 us
    pallas_call x10, Pallas kernels, run(): pl.pallas_call(body, out_shape=sum(outs, []), in_specs=sum(specs, []) + [...  9.63 us
    ppermute x2, waiting for transfers between devices, over_owners(): return lax.ppermute(part, 'pos', [(0, 1), (1, 0)])  6.91 us
    ppermute x8, waiting for transfers between devices, from_rows(): blocks.append(lax.ppermute(block, 'tile', route))  5.71 us
    ppermute x2, starting transfers between devices, over_owners(): return lax.ppermute(part, 'pos', [(0, 1), (1, 0)])  2.97 us
    unnamed x10, local copies, waits for them, and re-layouts  2.67 us
  transfers between devices with their start and end apart: 27, of which 11 were waited for; matrix products, arithmetic and copies ran while one was open for 0% of the time, Pallas kernels for 7%

profile of v6, /device:TPU:0, one launch (start us, length us, event | category | flops | bytes accessed | tf_op | source)
XLA Modules:
  0.0 81.3 jit_solution(11847420572317629879)
XLA Ops:
  0.6 1.2 %slice_bitcast_fusion = (bf16[2,256,256]{2,1,0:T(8,128)(2,1)S(1)}, bf16[2,256,256]{2,1,0:T(8,128)(2,1)S(1)}) fusion(bf16[1,2,2,256,256]{4,3,2,1,0:T(8,128)(2,1)} %param.7), kind=kLoop, calls=%fused_computation | loop fusion | bytes 1048576 | tf_op jit(solution)/shard_map/squeeze | solution.py:459
  1.8 0.7 collective-permute-start.6
  2.5 5.9 %collective-permute-start.5 = (bf16[2,256,256]{2,1,0:T(8,128)(2,1)S(1)}, bf16[2,256,256]{2,1,0:T(8,128)(2,1)S(1)}, u32[]{:S(2)}, u32[]{:S(2)}) collective-permute-start(bf16[2,256,256]{2,1,0:T(8,128)(2,1)S(1)} %get-tuple-element.61.refs_6_.refs_2_.refs_0_), channel_id=1, source_target_pairs={{0,8},{2,10},{4,12},{6,14},{8,0},{10,2},{12,4},{14,6},{16,24},{18,... | collective-permute-start | bytes 786440 | tf_op jit(solution)/shard_map/ppermute | solution.py:38
  8.4 0.4 collective-permute-start.1
  9.4 0.7 copy-done.3
  10.1 1.0 %copy-done.1 = bf16[512,512]{1,0:T(8,128)(2,1)S(1)} copy-done((bf16[512,512]{1,0:T(8,128)(2,1)S(1)}, bf16[512,512]{1,0:T(8,128)(2,1)}, u32[]{:S(2)}) %copy-start.1) | copy-done | bytes 524312
  11.1 0.9 %copy-done.2 = bf16[1,1,2,256,256]{4,3,2,1,0:T(8,128)(2,1)S(1)} copy-done((bf16[1,1,2,256,256]{4,3,2,1,0:T(8,128)(2,1)S(1)}, bf16[1,1,2,256,256]{4,3,2,1,0:T(8,128)(2,1)}, u32[]{:S(2)}) %copy-start.2) | copy-done | bytes 262168
  12.1 0.7 shard_map.86
  12.8 0.7 collective-permute-start.3
  13.5 2.1 %collective-permute-start.2 = (bf16[2,256,256]{2,1,0:T(8,128)(2,1)S(1)}, bf16[2,256,256]{2,1,0:T(8,128)(2,1)S(1)}, u32[]{:S(2)}, u32[]{:S(2)}) collective-permute-start(bf16[2,256,256]{2,1,0:T(8,128)(2,1)S(1)} %get-tuple-element.33.refs_2_.refs_0_), channel_id=1, source_target_pairs={{0,8},{2,10},{4,12},{6,14},{8,0},{10,2},{12,4},{14,6},{16,24},{18,... | collective-permute-start | bytes 786440 | tf_op jit(solution)/shard_map/ppermute | solution.py:38
  15.6 0.4 collective-permute-start.7
  16.0 1.5 %collective-permute-start = (bf16[272,256]{1,0:T(8,128)(2,1)S(1)}, bf16[272,256]{1,0:T(8,128)(2,1)S(1)}, u32[]{:S(2)}, u32[]{:S(2)}) collective-permute-start(bf16[272,256]{1,0:T(8,128)(2,1)S(1)} %get-tuple-element.32), channel_id=1, source_target_pairs={{0,1},{1,0},{2,3},{3,2},{4,5},{5,4},{6,7},{7,6},{8,9},{9,8},{10,11... | collective-permute-start | bytes 417800 | tf_op jit(solution)/shard_map/ppermute | solution.py:476
  17.6 4.3 %collective-permute-done.2.refs_0_ = bf16[2,256,256]{2,1,0:T(8,128)(2,1)S(1)} collective-permute-done((bf16[2,256,256]{2,1,0:T(8,128)(2,1)S(1)}, bf16[2,256,256]{2,1,0:T(8,128)(2,1)S(1)}, u32[]{:S(2)}, u32[]{:S(2)}) %collective-permute-start.2) | collective-permute-done | bytes 262176 | tf_op jit(solution)/shard_map/ppermute | solution.py:38
  21.9 0.9 %collective-permute-start.4 = (bf16[2,256,256]{2,1,0:T(8,128)(2,1)S(1)}, bf16[2,256,256]{2,1,0:T(8,128)(2,1)S(1)}, u32[]{:S(2)}, u32[]{:S(2)}) collective-permute-start(bf16[2,256,256]{2,1,0:T(8,128)(2,1)S(1)} %shard_map.87.refs_4_), channel_id=1, source_target_pairs={{2,0},{4,2},{6,4},{0,6},{10,8},{12,10},{14,12},{8,14},{18,16},{20,... | collective-permute-start | bytes 786440 | tf_op jit(solution)/shard_map/ppermute | solution.py:26
  22.8 1.7 %shard_map.89 = (bf16[2,256,256]{2,1,0:T(8,128)(2,1)S(1)}, f32[2,256,512]{2,1,0:T(8,128)S(1)}) custom-call(bf16[272,256]{1,0:T(8,128)(2,1)S(1)} %get-tuple-element.31.refs_0_.refs_2_, bf16[272,256]{1,0:T(8,128)(2,1)S(1)} %collective-permute-done.refs_1_.refs_3_, bf16[2,256,256]{2,1,0:T(8,128)(2,1)S(1)} %get-tuple-element.61.refs_6_.refs_2_.refs_0_, ...), custom_call_target="tpu_custom_call" | custom-call | flops 1500000000 | bytes 4472832 | tf_op jit(solution)/shard_map/pallas_call | solution.py:308
  24.5 2.1 %collective-permute-done.4.refs_5_ = bf16[2,256,256]{2,1,0:T(8,128)(2,1)S(1)} collective-permute-done((bf16[2,256,256]{2,1,0:T(8,128)(2,1)S(1)}, bf16[2,256,256]{2,1,0:T(8,128)(2,1)S(1)}, u32[]{:S(2)}, u32[]{:S(2)}) %collective-permute-start.4) | collective-permute-done | bytes 262176 | tf_op jit(solution)/shard_map/ppermute | solution.py:26
  26.7 4.2 %shard_map.90 = (bf16[2,256,256]{2,1,0:T(8,128)(2,1)S(1)}, bf16[2,256,256]{2,1,0:T(8,128)(2,1)S(1)}, bf16[528,256]{1,0:T(8,128)(2,1)S(1)}, bf16[2,256,256]{2,1,0...) custom-call(bf16[272,256]{1,0:T(8,128)(2,1)S(1)} %get-tuple-element.31.refs_0_.refs_2_, ...), custom_call_target="tpu_custom_call" | custom-call | flops 4000000000 | bytes 6578176 | tf_op jit(solution)/shard_map/pallas_call | solution.py:308
  30.9 1.0 %collective-permute-start.10 = (bf16[256,512]{1,0:T(8,128)(2,1)S(1)}, bf16[256,512]{1,0:T(8,128)(2,1)S(1)}, u32[]{:S(2)}, u32[]{:S(2)}) collective-permute-start(bf16[256,512]{1,0:T(8,128)(2,1)S(1)} %get-tuple-element.41), channel_id=1, source_target_pairs={{0,2},{1,3},{2,0},{3,1},{4,6},{5,7},{6,4},{7,5},{8,10},{9,11},{10,... | collective-permute-start | bytes 786440 | tf_op jit(solution)/shard_map/ppermute | solution.py:421
  31.9 0.7 collective-permute-start.9
  32.6 4.3 %collective-permute-start.8 = (bf16[528,256]{1,0:T(8,128)(2,1)S(1)}, bf16[528,256]{1,0:T(8,128)(2,1)S(1)}, u32[]{:S(2)}, u32[]{:S(2)}) collective-permute-start(bf16[528,256]{1,0:T(8,128)(2,1)S(1)} %get-tuple-element.39), channel_id=1, source_target_pairs={{0,8},{2,10},{4,12},{6,14},{8,0},{10,2},{12,4},{14,6},{16,24},{18,... | collective-permute-start | bytes 811016 | tf_op jit(solution)/shard_map/ppermute | solution.py:38
  36.9 0.8 shard_map.91
  37.7 1.6 %collective-permute-start.11 = (bf16[64,512]{1,0:T(8,128)(2,1)S(1)}, bf16[64,512]{1,0:T(8,128)(2,1)S(1)}, u32[]{:S(2)}, u32[]{:S(2)}) collective-permute-start(bf16[64,512]{1,0:T(8,128)(2,1)S(1)} %get-tuple-element.44), channel_id=1, source_target_pairs={{0,1},{1,0},{2,3},{3,2},{4,5},{5,4},{6,7},{7,6},{8,9},{9,8},{10,11... | collective-permute-start | bytes 196616 | tf_op jit(solution)/shard_map/ppermute | solution.py:421
  39.3 1.0 %collective-permute-start.12 = (bf16[64,512]{1,0:T(8,128)(2,1)S(1)}, bf16[64,512]{1,0:T(8,128)(2,1)S(1)}, u32[]{:S(2)}, u32[]{:S(2)}) collective-permute-start(bf16[64,512]{1,0:T(8,128)(2,1)S(1)} %get-tuple-element.45), channel_id=1, source_target_pairs={{0,4},{1,5},{2,6},{3,7},{4,0},{5,1},{6,2},{7,3},{8,12},{9,13},{10,... | collective-permute-start | bytes 196616 | tf_op jit(solution)/shard_map/ppermute | solution.py:421
  40.3 0.9 %collective-permute-start.13 = (bf16[64,512]{1,0:T(8,128)(2,1)S(1)}, bf16[64,512]{1,0:T(8,128)(2,1)S(1)}, u32[]{:S(2)}, u32[]{:S(2)}) collective-permute-start(bf16[64,512]{1,0:T(8,128)(2,1)S(1)} %get-tuple-element.46), channel_id=1, source_target_pairs={{0,5},{1,4},{2,7},{3,6},{4,1},{5,0},{6,3},{7,2},{8,13},{9,12},{10,... | collective-permute-start | bytes 196616 | tf_op jit(solution)/shard_map/ppermute | solution.py:421
  41.2 0.7 collective-permute-start.19
  41.9 1.4 %collective-permute-done.8.refs_1_.refs_5_ = bf16[528,256]{1,0:T(8,128)(2,1)S(1)} collective-permute-done((bf16[528,256]{1,0:T(8,128)(2,1)S(1)}, bf16[528,256]{1,0:T(8,128)(2,1)S(1)}, u32[]{:S(2)}, u32[]{:S(2)}) %collective-permute-start.8) | collective-permute-done | bytes 270368 | tf_op jit(solution)/shard_map/ppermute | solution.py:38
  43.3 3.9 %collective-permute-start.18 = (bf16[528,256]{1,0:T(8,128)(2,1)S(1)}, bf16[528,256]{1,0:T(8,128)(2,1)S(1)}, u32[]{:S(2)}, u32[]{:S(2)}) collective-permute-start(bf16[528,256]{1,0:T(8,128)(2,1)S(1)} %get-tuple-element.51), channel_id=1, source_target_pairs={{0,8},{2,10},{4,12},{6,14},{8,0},{10,2},{12,4},{14,6},{16,24},{18,... | collective-permute-start | bytes 811016 | tf_op jit(solution)/shard_map/ppermute | solution.py:38
  47.5 1.4 %collective-permute-start.16 = (bf16[64,512]{1,0:T(8,128)(2,1)S(1)}, bf16[64,512]{1,0:T(8,128)(2,1)S(1)}, u32[]{:S(2)}, u32[]{:S(2)}) collective-permute-start(bf16[64,512]{1,0:T(8,128)(2,1)S(1)} %get-tuple-element.47.refs_0_), channel_id=1, source_target_pairs={{0,24},{1,25},{2,26},{3,27},{4,28},{5,29},{6,30},{7,31},{8,16},{9,... | collective-permute-start | bytes 196616 | tf_op jit(solution)/shard_map/ppermute | solution.py:421
  49.0 7.0 %collective-permute-done.16.refs_3_ = bf16[64,512]{1,0:T(8,128)(2,1)S(1)} collective-permute-done((bf16[64,512]{1,0:T(8,128)(2,1)S(1)}, bf16[64,512]{1,0:T(8,128)(2,1)S(1)}, u32[]{:S(2)}, u32[]{:S(2)}) %collective-permute-start.16) | collective-permute-done | bytes 65568 | tf_op jit(solution)/shard_map/ppermute | solution.py:421
  56.0 2.0 %collective-permute-start.14 = (bf16[64,512]{1,0:T(8,128)(2,1)S(1)}, bf16[64,512]{1,0:T(8,128)(2,1)S(1)}, u32[]{:S(2)}, u32[]{:S(2)}) collective-permute-start(bf16[64,512]{1,0:T(8,128)(2,1)S(1)} %get-tuple-element.47.refs_0_), channel_id=1, source_target_pairs={{0,8},{1,9},{2,10},{3,11},{4,12},{5,13},{6,14},{7,15},{8,0},{9,1},... | collective-permute-start | bytes 196616 | tf_op jit(solution)/shard_map/ppermute | solution.py:421
  58.0 0.2 collective-permute-done.15.refs_2_
  58.2 2.0 %collective-permute-done.14.refs_1_ = bf16[64,512]{1,0:T(8,128)(2,1)S(1)} collective-permute-done((bf16[64,512]{1,0:T(8,128)(2,1)S(1)}, bf16[64,512]{1,0:T(8,128)(2,1)S(1)}, u32[]{:S(2)}, u32[]{:S(2)}) %collective-permute-start.14) | collective-permute-done | bytes 65568 | tf_op jit(solution)/shard_map/ppermute | solution.py:421
  60.3 0.5 shard_map.93
  60.9 2.1 %collective-permute-start.22 = (bf16[64,512]{1,0:T(8,128)(2,1)S(1)}, bf16[64,512]{1,0:T(8,128)(2,1)S(1)}, u32[]{:S(2)}, u32[]{:S(2)}) collective-permute-start(bf16[64,512]{1,0:T(8,128)(2,1)S(1)} %get-tuple-element.52.refs_0_), channel_id=1, source_target_pairs={{0,5},{1,4},{2,7},{3,6},{4,1},{5,0},{6,3},{7,2},{8,13},{9,12},{10,... | collective-permute-start | bytes 196616 | tf_op jit(solution)/shard_map/ppermute | solution.py:421
  63.0 0.9 %collective-permute-start.21 = (bf16[64,512]{1,0:T(8,128)(2,1)S(1)}, bf16[64,512]{1,0:T(8,128)(2,1)S(1)}, u32[]{:S(2)}, u32[]{:S(2)}) collective-permute-start(bf16[64,512]{1,0:T(8,128)(2,1)S(1)} %get-tuple-element.52.refs_0_), channel_id=1, source_target_pairs={{0,4},{1,5},{2,6},{3,7},{4,0},{5,1},{6,2},{7,3},{8,12},{9,13},{10,... | collective-permute-start | bytes 196616 | tf_op jit(solution)/shard_map/ppermute | solution.py:421
  63.9 0.5 collective-permute-start.20
  64.4 1.5 %collective-permute-start.25 = (bf16[2,256,256]{2,1,0:T(8,128)(2,1)S(1)}, bf16[2,256,256]{2,1,0:T(8,128)(2,1)S(1)}, u32[]{:S(2)}, u32[]{:S(2)}) collective-permute-start(bf16[2,256,256]{2,1,0:T(8,128)(2,1)S(1)} %get-tuple-element.56.refs_1_), channel_id=1, source_target_pairs={{0,1},{1,0},{2,3},{3,2},{4,5},{5,4},{6,7},{7,6},{8,9},{9,8},{10,11... | collective-permute-start | bytes 786440 | tf_op jit(solution)/shard_map/ppermute | solution.py:507
  66.0 0.8 collective-permute-done.22.refs_3_
  66.7 1.6 %collective-permute-done.21.refs_2_ = bf16[64,512]{1,0:T(8,128)(2,1)S(1)} collective-permute-done((bf16[64,512]{1,0:T(8,128)(2,1)S(1)}, bf16[64,512]{1,0:T(8,128)(2,1)S(1)}, u32[]{:S(2)}, u32[]{:S(2)}) %collective-permute-start.21) | collective-permute-done | bytes 65568 | tf_op jit(solution)/shard_map/ppermute | solution.py:421
  68.3 0.5 collective-permute-done.20.refs_1_
  68.8 0.3 shard_map.94
  69.1 0.9 %collective-permute-start.26 = (bf16[256,512]{1,0:T(8,128)(2,1)S(1)}, bf16[256,512]{1,0:T(8,128)(2,1)S(1)}, u32[]{:S(2)}, u32[]{:S(2)}) collective-permute-start(bf16[256,512]{1,0:T(8,128)(2,1)S(1)} %get-tuple-element.57.refs_0_), channel_id=1, source_target_pairs={{0,2},{1,3},{2,0},{3,1},{4,6},{5,7},{6,4},{7,5},{8,10},{9,11},{10,... | collective-permute-start | bytes 786440 | tf_op jit(solution)/shard_map/ppermute | solution.py:421
  70.0 1.4 %collective-permute-start.24 = (bf16[2,256,256]{2,1,0:T(8,128)(2,1)S(1)}, bf16[2,256,256]{2,1,0:T(8,128)(2,1)S(1)}, u32[]{:S(2)}, u32[]{:S(2)}) collective-permute-start(bf16[2,256,256]{2,1,0:T(8,128)(2,1)S(1)} %get-tuple-element.55.refs_1_), channel_id=1, source_target_pairs={{0,1},{1,0},{2,3},{3,2},{4,5},{5,4},{6,7},{7,6},{8,9},{9,8},{10,11... | collective-permute-start | bytes 786440 | tf_op jit(solution)/shard_map/ppermute | solution.py:507
  71.5 3.7 %collective-permute-done.25.refs_2_ = bf16[2,256,256]{2,1,0:T(8,128)(2,1)S(1)} collective-permute-done((bf16[2,256,256]{2,1,0:T(8,128)(2,1)S(1)}, bf16[2,256,256]{2,1,0:T(8,128)(2,1)S(1)}, u32[]{:S(2)}, u32[]{:S(2)}) %collective-permute-start.25) | collective-permute-done | bytes 262176 | tf_op jit(solution)/shard_map/ppermute | solution.py:507
  75.1 0.8 %shard_map.95.refs_3_ = bf16[1,2,2,256,256]{4,3,2,1,0:T(8,128)(2,1)} custom-call(bf16[2,256,256]{2,1,0:T(8,128)(2,1)S(1)} %get-tuple-element.33.refs_2_.refs_0_, bf16[2,256,256]{2,1,0:T(8,128)(2,1)S(1)} %get-tuple-element.56.refs_1_, bf16[2,256,256]{2,1,0:T(8,128)(2,1)S(1)} %collective-permute-done.25.refs_2_), custom_call_target="tpu_custom_call" | custom-call | flops 131072 | bytes 1048576 | tf_op jit(solution)/shard_map/pallas_call | solution.py:325
  76.0 1.2 %shard_map.96 = (f32[2048,128]{1,0:T(8,128)}, f32[8,128]{1,0:T(8,128)S(1)}) custom-call(bf16[256,512]{1,0:T(8,128)(2,1)S(1)} %get-tuple-element.57.refs_0_, bf16[256,512]{1,0:T(8,128)(2,1)S(1)} %collective-permute-done.26.refs_1_, f32[2048,128]{1,0:T(8,128)S(1)} %bitcast.16), custom_call_target="tpu_custom_call" | custom-call | flops 1000000 | bytes 2625536 | tf_op jit(solution)/shard_map/pallas_call | solution.py:308
  77.2 3.3 %collective-permute-done.24.refs_2_ = bf16[2,256,256]{2,1,0:T(8,128)(2,1)S(1)} collective-permute-done((bf16[2,256,256]{2,1,0:T(8,128)(2,1)S(1)}, bf16[2,256,256]{2,1,0:T(8,128)(2,1)S(1)}, u32[]{:S(2)}, u32[]{:S(2)}) %collective-permute-start.24) | collective-permute-done | bytes 262176 | tf_op jit(solution)/shard_map/ppermute | solution.py:507
  80.4 0.8 %shard_map.97 = bf16[1,2,2,256,256]{4,3,2,1,0:T(8,128)(2,1)} custom-call(bf16[2,256,256]{2,1,0:T(8,128)(2,1)S(1)} %get-tuple-element.61.refs_6_.refs_2_.refs_0_, bf16[2,256,256]{2,1,0:T(8,128)(2,1)S(1)} %get-tuple-element.55.refs_1_, bf16[2,256,256]{2,1,0:T(8,128)(2,1)S(1)} %collective-permute-done.24.refs_2_, ...), custom_call_target="tpu_custom_call", output_to_operand_aliasing={{}: (3, {})} | custom-call | flops 131072 | bytes 1048576 | tf_op jit(solution)/shard_map/pallas_call | solution.py:325
  (29 shorter events, 0.6 us)
Async XLA Ops:
  0.6 8.8 %copy-start = (f32[2,256,2,256]{3,2,1,0:T(2,128)S(1)}, f32[2,256,2,256]{3,2,1,0:T(2,128)}, u32[]{:S(2)}) copy-start(f32[2,256,2,256]{3,2,1,0:T(2,128)} %param.8) | copy-start | bytes 3145732
  1.8 13.8 %collective-permute-start.6 = (bf16[2,256,256]{2,1,0:T(8,128)(2,1)S(1)}, bf16[2,256,256]{2,1,0:T(8,128)(2,1)S(1)}, u32[]{:S(2)}, u32[]{:S(2)}) collective-permute-start(bf16[2,256,256]{2,1,0:T(8,128)(2,1)S(1)} %get-tuple-element.61.refs_6_.refs_2_.refs_0_), channel_id=1, source_target_pairs={{0,0},{2,2},{4,4},{6,6},{8,16},{10,18},{12,20},{14,22},{16,8},{18,... | collective-permute-start | bytes 786440 | tf_op jit(solution)/shard_map/ppermute | solution.py:38
  2.5 13.1 %collective-permute-start.5 = (bf16[2,256,256]{2,1,0:T(8,128)(2,1)S(1)}, bf16[2,256,256]{2,1,0:T(8,128)(2,1)S(1)}, u32[]{:S(2)}, u32[]{:S(2)}) collective-permute-start(bf16[2,256,256]{2,1,0:T(8,128)(2,1)S(1)} %get-tuple-element.61.refs_6_.refs_2_.refs_0_), channel_id=1, source_target_pairs={{0,8},{2,10},{4,12},{6,14},{8,0},{10,2},{12,4},{14,6},{16,24},{18,... | collective-permute-start | bytes 786440 | tf_op jit(solution)/shard_map/ppermute | solution.py:38
  8.4 14.4 %collective-permute-start.1 = (bf16[2,2,256,256]{3,2,1,0:T(8,128)(2,1)}, bf16[2,2,256,256]{3,2,1,0:T(8,128)(2,1)S(1)}, u32[]{:S(2)}, u32[]{:S(2)}) collective-permute-start(bf16[2,2,256,256]{3,2,1,0:T(8,128)(2,1)} %bitcast.17), channel_id=1, source_target_pairs={{2,0},{4,2},{6,4},{0,6},{10,8},{12,10},{14,12},{8,14},{18,16},{20,... | collective-permute-start | bytes 1572872 | tf_op jit(solution)/shard_map/ppermute | solution.py:26
  9.4 0.7 copy-start.3
  10.1 1.0 %copy-start.1 = (bf16[512,512]{1,0:T(8,128)(2,1)S(1)}, bf16[512,512]{1,0:T(8,128)(2,1)}, u32[]{:S(2)}) copy-start(bf16[512,512]{1,0:T(8,128)(2,1)} %constant.10.refs_5_) | copy-start | bytes 1572868
  11.1 0.9 %copy-start.2 = (bf16[1,1,2,256,256]{4,3,2,1,0:T(8,128)(2,1)S(1)}, bf16[1,1,2,256,256]{4,3,2,1,0:T(8,128)(2,1)}, u32[]{:S(2)}) copy-start(bf16[1,1,2,256,256]{4,3,2,1,0:T(8,128)(2,1)} %refs_3_.1) | copy-start | bytes 786436
  12.8 4.8 %collective-permute-start.3 = (bf16[2,256,256]{2,1,0:T(8,128)(2,1)S(1)}, bf16[2,256,256]{2,1,0:T(8,128)(2,1)S(1)}, u32[]{:S(2)}, u32[]{:S(2)}) collective-permute-start(bf16[2,256,256]{2,1,0:T(8,128)(2,1)S(1)} %get-tuple-element.33.refs_2_.refs_0_), channel_id=1, source_target_pairs={{0,0},{2,2},{4,4},{6,6},{8,16},{10,18},{12,20},{14,22},{16,8},{18,... | collective-permute-start | bytes 786440 | tf_op jit(solution)/shard_map/ppermute | solution.py:38
  13.5 8.4 %collective-permute-start.2 = (bf16[2,256,256]{2,1,0:T(8,128)(2,1)S(1)}, bf16[2,256,256]{2,1,0:T(8,128)(2,1)S(1)}, u32[]{:S(2)}, u32[]{:S(2)}) collective-permute-start(bf16[2,256,256]{2,1,0:T(8,128)(2,1)S(1)} %get-tuple-element.33.refs_2_.refs_0_), channel_id=1, source_target_pairs={{0,8},{2,10},{4,12},{6,14},{8,0},{10,2},{12,4},{14,6},{16,24},{18,... | collective-permute-start | bytes 786440 | tf_op jit(solution)/shard_map/ppermute | solution.py:38
  15.6 7.2 %collective-permute-start.7 = (bf16[2,256,256]{2,1,0:T(8,128)(2,1)S(1)}, bf16[2,256,256]{2,1,0:T(8,128)(2,1)S(1)}, u32[]{:S(2)}, u32[]{:S(2)}) collective-permute-start(bf16[2,256,256]{2,1,0:T(8,128)(2,1)S(1)} %shard_map.88.refs_4_), channel_id=1, source_target_pairs={{2,0},{4,2},{6,4},{0,6},{10,8},{12,10},{14,12},{8,14},{18,16},{20,... | collective-permute-start | bytes 786440 | tf_op jit(solution)/shard_map/ppermute | solution.py:26
  16.0 6.7 %collective-permute-start = (bf16[272,256]{1,0:T(8,128)(2,1)S(1)}, bf16[272,256]{1,0:T(8,128)(2,1)S(1)}, u32[]{:S(2)}, u32[]{:S(2)}) collective-permute-start(bf16[272,256]{1,0:T(8,128)(2,1)S(1)} %get-tuple-element.32), channel_id=1, source_target_pairs={{0,1},{1,0},{2,3},{3,2},{4,5},{5,4},{6,7},{7,6},{8,9},{9,8},{10,11... | collective-permute-start | bytes 417800 | tf_op jit(solution)/shard_map/ppermute | solution.py:476
  21.9 4.8 %collective-permute-start.4 = (bf16[2,256,256]{2,1,0:T(8,128)(2,1)S(1)}, bf16[2,256,256]{2,1,0:T(8,128)(2,1)S(1)}, u32[]{:S(2)}, u32[]{:S(2)}) collective-permute-start(bf16[2,256,256]{2,1,0:T(8,128)(2,1)S(1)} %shard_map.87.refs_4_), channel_id=1, source_target_pairs={{2,0},{4,2},{6,4},{0,6},{10,8},{12,10},{14,12},{8,14},{18,16},{20,... | collective-permute-start | bytes 786440 | tf_op jit(solution)/shard_map/ppermute | solution.py:26
  22.8 3.9 %copy-start.4 = (bf16[512,512]{1,0:T(8,128)(2,1)S(1)}, bf16[512,512]{1,0:T(8,128)(2,1)}, u32[]{:S(2)}) copy-start(bf16[512,512]{1,0:T(8,128)(2,1)} %constant.11.refs_10_) | copy-start | bytes 1572868
  30.9 6.0 %collective-permute-start.10 = (bf16[256,512]{1,0:T(8,128)(2,1)S(1)}, bf16[256,512]{1,0:T(8,128)(2,1)S(1)}, u32[]{:S(2)}, u32[]{:S(2)}) collective-permute-start(bf16[256,512]{1,0:T(8,128)(2,1)S(1)} %get-tuple-element.41), channel_id=1, source_target_pairs={{0,2},{1,3},{2,0},{3,1},{4,6},{5,7},{6,4},{7,5},{8,10},{9,11},{10,... | collective-permute-start | bytes 786440 | tf_op jit(solution)/shard_map/ppermute | solution.py:421
  31.9 9.4 %collective-permute-start.9 = (bf16[528,256]{1,0:T(8,128)(2,1)S(1)}, bf16[528,256]{1,0:T(8,128)(2,1)S(1)}, u32[]{:S(2)}, u32[]{:S(2)}) collective-permute-start(bf16[528,256]{1,0:T(8,128)(2,1)S(1)} %get-tuple-element.39), channel_id=1, source_target_pairs={{0,0},{2,2},{4,4},{6,6},{8,16},{10,18},{12,20},{14,22},{16,8},{18,... | collective-permute-start | bytes 811016 | tf_op jit(solution)/shard_map/ppermute | solution.py:38
  32.6 10.7 %collective-permute-start.8 = (bf16[528,256]{1,0:T(8,128)(2,1)S(1)}, bf16[528,256]{1,0:T(8,128)(2,1)S(1)}, u32[]{:S(2)}, u32[]{:S(2)}) collective-permute-start(bf16[528,256]{1,0:T(8,128)(2,1)S(1)} %get-tuple-element.39), channel_id=1, source_target_pairs={{0,8},{2,10},{4,12},{6,14},{8,0},{10,2},{12,4},{14,6},{16,24},{18,... | collective-permute-start | bytes 811016 | tf_op jit(solution)/shard_map/ppermute | solution.py:38
  37.7 9.5 %collective-permute-start.11 = (bf16[64,512]{1,0:T(8,128)(2,1)S(1)}, bf16[64,512]{1,0:T(8,128)(2,1)S(1)}, u32[]{:S(2)}, u32[]{:S(2)}) collective-permute-start(bf16[64,512]{1,0:T(8,128)(2,1)S(1)} %get-tuple-element.44), channel_id=1, source_target_pairs={{0,1},{1,0},{2,3},{3,2},{4,5},{5,4},{6,7},{7,6},{8,9},{9,8},{10,11... | collective-permute-start | bytes 196616 | tf_op jit(solution)/shard_map/ppermute | solution.py:421
  39.3 7.9 %collective-permute-start.12 = (bf16[64,512]{1,0:T(8,128)(2,1)S(1)}, bf16[64,512]{1,0:T(8,128)(2,1)S(1)}, u32[]{:S(2)}, u32[]{:S(2)}) collective-permute-start(bf16[64,512]{1,0:T(8,128)(2,1)S(1)} %get-tuple-element.45), channel_id=1, source_target_pairs={{0,4},{1,5},{2,6},{3,7},{4,0},{5,1},{6,2},{7,3},{8,12},{9,13},{10,... | collective-permute-start | bytes 196616 | tf_op jit(solution)/shard_map/ppermute | solution.py:421
  40.3 6.9 %collective-permute-start.13 = (bf16[64,512]{1,0:T(8,128)(2,1)S(1)}, bf16[64,512]{1,0:T(8,128)(2,1)S(1)}, u32[]{:S(2)}, u32[]{:S(2)}) collective-permute-start(bf16[64,512]{1,0:T(8,128)(2,1)S(1)} %get-tuple-element.46), channel_id=1, source_target_pairs={{0,5},{1,4},{2,7},{3,6},{4,1},{5,0},{6,3},{7,2},{8,13},{9,12},{10,... | collective-permute-start | bytes 196616 | tf_op jit(solution)/shard_map/ppermute | solution.py:421
  41.2 19.0 %collective-permute-start.19 = (bf16[528,256]{1,0:T(8,128)(2,1)S(1)}, bf16[528,256]{1,0:T(8,128)(2,1)S(1)}, u32[]{:S(2)}, u32[]{:S(2)}) collective-permute-start(bf16[528,256]{1,0:T(8,128)(2,1)S(1)} %get-tuple-element.51), channel_id=1, source_target_pairs={{0,0},{2,2},{4,4},{6,6},{8,16},{10,18},{12,20},{14,22},{16,8},{18,... | collective-permute-start | bytes 811016 | tf_op jit(solution)/shard_map/ppermute | solution.py:38
  43.3 17.0 %collective-permute-start.18 = (bf16[528,256]{1,0:T(8,128)(2,1)S(1)}, bf16[528,256]{1,0:T(8,128)(2,1)S(1)}, u32[]{:S(2)}, u32[]{:S(2)}) collective-permute-start(bf16[528,256]{1,0:T(8,128)(2,1)S(1)} %get-tuple-element.51), channel_id=1, source_target_pairs={{0,8},{2,10},{4,12},{6,14},{8,0},{10,2},{12,4},{14,6},{16,24},{18,... | collective-permute-start | bytes 811016 | tf_op jit(solution)/shard_map/ppermute | solution.py:38
  47.4 12.9 %collective-permute-start.17 = (bf16[2,256,256]{2,1,0:T(8,128)(2,1)S(1)}, bf16[2,256,256]{2,1,0:T(8,128)(2,1)S(1)}, u32[]{:S(2)}, u32[]{:S(2)}) collective-permute-start(bf16[2,256,256]{2,1,0:T(8,128)(2,1)S(1)} %get-tuple-element.49), channel_id=1, source_target_pairs={{6,0},{0,2},{2,4},{4,6},{14,8},{8,10},{10,12},{12,14},{22,16},{16,... | collective-permute-start | bytes 786440 | tf_op jit(solution)/shard_map/ppermute | solution.py:26
  47.5 8.5 %collective-permute-start.16 = (bf16[64,512]{1,0:T(8,128)(2,1)S(1)}, bf16[64,512]{1,0:T(8,128)(2,1)S(1)}, u32[]{:S(2)}, u32[]{:S(2)}) collective-permute-start(bf16[64,512]{1,0:T(8,128)(2,1)S(1)} %get-tuple-element.47.refs_0_), channel_id=1, source_target_pairs={{0,24},{1,25},{2,26},{3,27},{4,28},{5,29},{6,30},{7,31},{8,16},{9,... | collective-permute-start | bytes 196616 | tf_op jit(solution)/shard_map/ppermute | solution.py:421
  48.9 9.4 %collective-permute-start.15 = (bf16[64,512]{1,0:T(8,128)(2,1)S(1)}, bf16[64,512]{1,0:T(8,128)(2,1)S(1)}, u32[]{:S(2)}, u32[]{:S(2)}) collective-permute-start(bf16[64,512]{1,0:T(8,128)(2,1)S(1)} %get-tuple-element.47.refs_0_), channel_id=1, source_target_pairs={{0,16},{1,17},{2,18},{3,19},{4,20},{5,21},{6,22},{7,23},{8,24},{9,... | collective-permute-start | bytes 196616 | tf_op jit(solution)/shard_map/ppermute | solution.py:421
  56.0 4.3 %collective-permute-start.14 = (bf16[64,512]{1,0:T(8,128)(2,1)S(1)}, bf16[64,512]{1,0:T(8,128)(2,1)S(1)}, u32[]{:S(2)}, u32[]{:S(2)}) collective-permute-start(bf16[64,512]{1,0:T(8,128)(2,1)S(1)} %get-tuple-element.47.refs_0_), channel_id=1, source_target_pairs={{0,8},{1,9},{2,10},{3,11},{4,12},{5,13},{6,14},{7,15},{8,0},{9,1},... | collective-permute-start | bytes 196616 | tf_op jit(solution)/shard_map/ppermute | solution.py:421
  60.8 8.0 %collective-permute-start.23 = (bf16[2,256,256]{2,1,0:T(8,128)(2,1)S(1)}, bf16[2,256,256]{2,1,0:T(8,128)(2,1)S(1)}, u32[]{:S(2)}, u32[]{:S(2)}) collective-permute-start(bf16[2,256,256]{2,1,0:T(8,128)(2,1)S(1)} %get-tuple-element.54), channel_id=1, source_target_pairs={{6,0},{0,2},{2,4},{4,6},{14,8},{8,10},{10,12},{12,14},{22,16},{16,... | collective-permute-start | bytes 786440 | tf_op jit(solution)/shard_map/ppermute | solution.py:26
  60.9 5.9 %collective-permute-start.22 = (bf16[64,512]{1,0:T(8,128)(2,1)S(1)}, bf16[64,512]{1,0:T(8,128)(2,1)S(1)}, u32[]{:S(2)}, u32[]{:S(2)}) collective-permute-start(bf16[64,512]{1,0:T(8,128)(2,1)S(1)} %get-tuple-element.52.refs_0_), channel_id=1, source_target_pairs={{0,5},{1,4},{2,7},{3,6},{4,1},{5,0},{6,3},{7,2},{8,13},{9,12},{10,... | collective-permute-start | bytes 196616 | tf_op jit(solution)/shard_map/ppermute | solution.py:421
  63.0 5.3 %collective-permute-start.21 = (bf16[64,512]{1,0:T(8,128)(2,1)S(1)}, bf16[64,512]{1,0:T(8,128)(2,1)S(1)}, u32[]{:S(2)}, u32[]{:S(2)}) collective-permute-start(bf16[64,512]{1,0:T(8,128)(2,1)S(1)} %get-tuple-element.52.refs_0_), channel_id=1, source_target_pairs={{0,4},{1,5},{2,6},{3,7},{4,0},{5,1},{6,2},{7,3},{8,12},{9,13},{10,... | collective-permute-start | bytes 196616 | tf_op jit(solution)/shard_map/ppermute | solution.py:421
  63.9 4.9 %collective-permute-start.20 = (bf16[64,512]{1,0:T(8,128)(2,1)S(1)}, bf16[64,512]{1,0:T(8,128)(2,1)S(1)}, u32[]{:S(2)}, u32[]{:S(2)}) collective-permute-start(bf16[64,512]{1,0:T(8,128)(2,1)S(1)} %get-tuple-element.52.refs_0_), channel_id=1, source_target_pairs={{0,1},{1,0},{2,3},{3,2},{4,5},{5,4},{6,7},{7,6},{8,9},{9,8},{10,11... | collective-permute-start | bytes 196616 | tf_op jit(solution)/shard_map/ppermute | solution.py:421
  64.4 10.7 %collective-permute-start.25 = (bf16[2,256,256]{2,1,0:T(8,128)(2,1)S(1)}, bf16[2,256,256]{2,1,0:T(8,128)(2,1)S(1)}, u32[]{:S(2)}, u32[]{:S(2)}) collective-permute-start(bf16[2,256,256]{2,1,0:T(8,128)(2,1)S(1)} %get-tuple-element.56.refs_1_), channel_id=1, source_target_pairs={{0,1},{1,0},{2,3},{3,2},{4,5},{5,4},{6,7},{7,6},{8,9},{9,8},{10,11... | collective-permute-start | bytes 786440 | tf_op jit(solution)/shard_map/ppermute | solution.py:507
  69.1 6.9 %collective-permute-start.26 = (bf16[256,512]{1,0:T(8,128)(2,1)S(1)}, bf16[256,512]{1,0:T(8,128)(2,1)S(1)}, u32[]{:S(2)}, u32[]{:S(2)}) collective-permute-start(bf16[256,512]{1,0:T(8,128)(2,1)S(1)} %get-tuple-element.57.refs_0_), channel_id=1, source_target_pairs={{0,2},{1,3},{2,0},{3,1},{4,6},{5,7},{6,4},{7,5},{8,10},{9,11},{10,... | collective-permute-start | bytes 786440 | tf_op jit(solution)/shard_map/ppermute | solution.py:421
  70.0 10.4 %collective-permute-start.24 = (bf16[2,256,256]{2,1,0:T(8,128)(2,1)S(1)}, bf16[2,256,256]{2,1,0:T(8,128)(2,1)S(1)}, u32[]{:S(2)}, u32[]{:S(2)}) collective-permute-start(bf16[2,256,256]{2,1,0:T(8,128)(2,1)S(1)} %get-tuple-element.55.refs_1_), channel_id=1, source_target_pairs={{0,1},{1,0},{2,3},{3,2},{4,5},{5,4},{6,7},{7,6},{8,9},{9,8},{10,11... | collective-permute-start | bytes 786440 | tf_op jit(solution)/shard_map/ppermute | solution.py:507

commit v7 on v5

--- a/solution.py
+++ b/solution.py
@@ -213,21 +213,22 @@
     spread(shifts, [grad_ref[part] for part in range(2)], home_ref, next_ref, down_ref)
 
 
+def above_parts(above_ref, n):
+    parts = [above_ref[pl.ds(part * n, n), :].astype(f32) for part in range(2)]
+    return parts, above_ref[pl.ds(2 * n, 16), :].astype(f32)[0:1] > 0
+
+
 def beside_kernel(next_ref, above_ref, out_ref):
-    n = out_ref.shape[1]
-    split = above_ref[pl.ds(2 * n, 16), :].astype(f32)[0:1] > 0
-    for part in range(2):
-        above = above_ref[pl.ds(part * n, n), :].astype(f32)
-        total = next_ref[part].astype(f32) + jnp.where(split, above, 0.0)
+    above, split = above_parts(above_ref, out_ref.shape[1])
+    for part in range(2):
+        total = next_ref[part].astype(f32) + jnp.where(split, above[part], 0.0)
         out_ref[part] = total.astype(bf16)
 
 
 def part_kernel(home_ref, above_ref, left_ref, out_ref):
-    n = out_ref.shape[1]
-    split = above_ref[pl.ds(2 * n, 16), :].astype(f32)[0:1] > 0
-    for part in range(2):
-        above = above_ref[pl.ds(part * n, n), :].astype(f32)
-        total = home_ref[part].astype(f32) + jnp.where(split, 0.0, above)
+    above, split = above_parts(above_ref, out_ref.shape[1])
+    for part in range(2):
+        total = home_ref[part].astype(f32) + jnp.where(split, 0.0, above[part])
         out_ref[part] = (total + left_ref[part].astype(f32)).astype(bf16)
 
 
@@ -348,20 +349,14 @@
     refs[-1][...] = total.astype(bf16)
 
 
-def place_kernel(group, add, *refs):
+def place_kernel(group, *refs):
     arrived, out_ref, blocks = refs[:-2], refs[-2], refs[-1]
     here = place_of(group)
     for distance, ref in enumerate(arrived):
         blocks[here ^ distance] = ref[...]
     size = blocks.shape[1]
-    if add:
-        total = blocks[0].astype(f32)
-        for block in range(1, blocks.shape[0]):
-            total += blocks[block].astype(f32)
-        out_ref[...] = total.astype(bf16)
-    else:
-        for block in range(blocks.shape[0]):
-            out_ref[pl.ds(block * size, size), :] = blocks[block]
+    for block in range(blocks.shape[0]):
+        out_ref[pl.ds(block * size, size), :] = blocks[block]
 
 
 def probe_kernel(step, modes, mine_ref, other_ref, probe_ref, out_ref, token_ref):
@@ -392,14 +387,18 @@
     return lax.ppermute(x, ("tile", "pos"), [(i, i ^ mask) for i in range(devices)])
 
 
-def joined(group, x, arrived, add):
+def joined(group, x, arrived):
     blocks = 1 << len(group)
     return job(
-        lambda *refs: place_kernel(group, add, *refs),
-        [shape_of(bf16, x.shape[0] * (1 if add else blocks), x.shape[1])],
+        lambda *refs: place_kernel(group, *refs),
+        [shape_of(bf16, x.shape[0] * blocks, x.shape[1])],
         [x] + arrived,
         scratch=[pltpu.VMEM((blocks,) + x.shape, bf16)],
     )
+
+
+def added(x, arrived):
+    return job(add_kernel, [shape_of(bf16, *x.shape)], [x] + arrived)
 
 
 def swapped(x, group):
@@ -491,25 +490,27 @@
         keep, *gives = done
         arrived = [swap_with(x, group, at) for at, x in enumerate(gives, 1)]
         scattered.append(group)
-    (beside1,), (total,) = run(
-        job(beside_kernel, [tile], [next1, above1]),
-        job(add_kernel, [shape_of(bf16, *keep.shape)], [keep] + arrived),
-    )
-    from_left1 = from_behind(beside1, 0, 1)
-    arrived = swapped(total, groups[0])
-    (beside0,) = run(job(beside_kernel, [tile], [next0, above0]), after=arrived[:1])
-    from_left0 = from_behind(beside0, 0, 1)
-    (part1,) = run(job(part_kernel, [tile], [home1, above1, from_left1]), after=[beside0])
+    (total,), (beside1,) = run(
+        added(keep, arrived), job(beside_kernel, [tile], [next1, above1])
+    )
+    left1 = from_behind(beside1, 0, 1)
+    first, second, *others = [[bit] for group in groups for bit in group]
+    (total,), (beside0,), (part1,) = run(
+        added(total, swapped(total, first)),
+        job(beside_kernel, [tile], [next0, above0]),
+        job(part_kernel, [tile], [home1, above1, left1]),
+    )
+    left0 = from_behind(beside0, 0, 1)
     other1 = over_owners(part1)
-    (total,) = run(joined(groups[0], total, arrived, True), after=[part1])
-    for group in groups[1:]:
-        (total,) = run(joined(group, total, swapped(total, group), True))
-    arrived = swapped(total, scattered[-1])
-    (part0,) = run(job(part_kernel, [tile], [home0, above0, from_left0]), after=arrived[1:2])
+    (total,), (part0,) = run(
+        added(total, swapped(total, second)),
+        job(part_kernel, [tile], [home0, above0, left0]),
+    )
     other0 = over_owners(part0)
-    (total,) = run(joined(scattered[-1], total, arrived, False), after=[part0])
-    for group in reversed(scattered[:-1]):
-        (total,) = run(joined(group, total, swapped(total, group), False))
+    for group in others:
+        (total,) = run(added(total, swapped(total, group)))
+    for group in reversed(scattered):
+        (total,) = run(joined(group, total, swapped(total, group)))
     other_half = swap_with(total, core, 1)
     positions_all = lax.axis_size("tile") * lax.axis_size("pos") * (patterns.shape[2] // 2)
     step = probe_rate / math.sqrt(positions_all)

time: 76.8 us -> 73.2 us (0.953)
  starting transfers between devices: 22.9 us -> 20 us
  waiting for transfers between devices: 37.6 us -> 36.8 us
    ppermute x11 -> x10, starting transfers between devices: 11.5 us -> 8.93 us  [swap_with(): lax.ppermute(x, ('tile', 'pos'), [(i, i ^ mask) for i in range(devices)])]
    ppermute x11 -> x10, waiting for transfers between devices: 16.3 us -> 15.9 us  [swap_with(): lax.ppermute(x, ('tile', 'pos'), [(i, i ^ mask) for i in range(devices)])]
    pallas_call x11 -> x9, Pallas kernels: 9.16 us -> 9.21 us  [run(): pl.pallas_call(body, out_shape=sum(outs, []), in_specs=sum(specs, []) + [...]
  transfers between devices with their start and end apart: 23 -> 22, of which waited for: 12 -> 12; matrix products, arithmetic and copies ran while one was open for 0% -> 0% of each run, Pallas kernels for 8% -> 7%
where the time goes in v7:
time: 73.2 us; the launch traced here: 72.9 us
  waiting for transfers between devices  36.8 us (50%)
  starting transfers between devices  20 us (27%)
  Pallas kernels  10.9 us (15%)
  local copies, waits for them, and re-layouts  3.82 us (5%)
  between operations  1.43 us (2%)
    ppermute x10, waiting for transfers between devices, swap_with(): lax.ppermute(x, ('tile', 'pos'), [(i, i ^ mask) for i in range(devices)])  15.9 us
    ppermute x9, waiting for transfers between devices, from_behind(): return lax.ppermute(block, 'tile', [(source(i), i) for i in range(tiles)])  13.7 us
    pallas_call x9, Pallas kernels, run(): pl.pallas_call(body, out_shape=sum(outs, []), in_specs=sum(specs, []) + [...  9.21 us
    ppermute x10, starting transfers between devices, swap_with(): lax.ppermute(x, ('tile', 'pos'), [(i, i ^ mask) for i in range(devices)])  8.93 us
    ppermute x9, starting transfers between devices, from_behind(): return lax.ppermute(block, 'tile', [(source(i), i) for i in range(tiles)])  7.31 us
    ppermute x2, waiting for transfers between devices, over_owners(): return lax.ppermute(part, 'pos', [(0, 1), (1, 0)])  7.2 us
    unnamed x10, local copies, waits for them, and re-layouts  2.67 us
    ppermute x2, starting transfers between devices, over_owners(): return lax.ppermute(part, 'pos', [(0, 1), (1, 0)])  2.25 us
  transfers between devices with their start and end apart: 22, of which 12 were waited for; matrix products, arithmetic and copies ran while one was open for 0% of the time, Pallas kernels for 7%

profile of v7, /device:TPU:0, one launch (start us, length us, event | category | flops | bytes accessed | tf_op | source)
XLA Modules:
  0.0 72.9 jit_solution(2882172845232308821)
XLA Ops:
  0.6 1.2 %slice_bitcast_fusion = (bf16[2,256,256]{2,1,0:T(8,128)(2,1)S(1)}, bf16[2,256,256]{2,1,0:T(8,128)(2,1)S(1)}) fusion(bf16[1,2,2,256,256]{4,3,2,1,0:T(8,128)(2,1)} %param.7), kind=kLoop, calls=%fused_computation | loop fusion | bytes 1048576 | tf_op jit(solution)/shard_map/squeeze | solution.py:429
  1.8 5.1 %collective-permute-start.4 = (bf16[2,256,256]{2,1,0:T(8,128)(2,1)S(1)}, bf16[2,256,256]{2,1,0:T(8,128)(2,1)S(1)}, u32[]{:S(2)}, u32[]{:S(2)}) collective-permute-start(bf16[2,256,256]{2,1,0:T(8,128)(2,1)S(1)} %get-tuple-element.61.refs_6_.refs_2_.refs_0_), channel_id=1, source_target_pairs={{8,0},{10,2},{12,4},{14,6},{16,8},{18,10},{20,12},{22,14},{24,16},... | collective-permute-start | bytes 786440 | tf_op jit(solution)/shard_map/ppermute | solution.py:29
  6.9 0.7 collective-permute-start.1
  8.2 0.0 copy-start.3
  8.2 0.7 copy-done.3
  8.9 1.0 %copy-done.1 = bf16[512,512]{1,0:T(8,128)(2,1)S(1)} copy-done((bf16[512,512]{1,0:T(8,128)(2,1)S(1)}, bf16[512,512]{1,0:T(8,128)(2,1)}, u32[]{:S(2)}) %copy-start.1) | copy-done | bytes 524312
  9.9 0.9 %copy-done.2 = bf16[1,1,2,256,256]{4,3,2,1,0:T(8,128)(2,1)S(1)} copy-done((bf16[1,1,2,256,256]{4,3,2,1,0:T(8,128)(2,1)S(1)}, bf16[1,1,2,256,256]{4,3,2,1,0:T(8,128)(2,1)}, u32[]{:S(2)}) %copy-start.2) | copy-done | bytes 262168
  10.9 0.7 shard_map.86
  11.6 0.5 collective-permute-start.2
  12.1 0.7 %collective-permute-done.4.refs_4_ = bf16[2,256,256]{2,1,0:T(8,128)(2,1)S(1)} collective-permute-done((bf16[2,256,256]{2,1,0:T(8,128)(2,1)S(1)}, bf16[2,256,256]{2,1,0:T(8,128)(2,1)S(1)}, u32[]{:S(2)}, u32[]{:S(2)}) %collective-permute-start.4) | collective-permute-done | bytes 262176 | tf_op jit(solution)/shard_map/ppermute | solution.py:29
  12.8 1.5 %collective-permute-start = (bf16[272,256]{1,0:T(8,128)(2,1)S(1)}, bf16[272,256]{1,0:T(8,128)(2,1)S(1)}, u32[]{:S(2)}, u32[]{:S(2)}) collective-permute-start(bf16[272,256]{1,0:T(8,128)(2,1)S(1)} %get-tuple-element.32), channel_id=1, source_target_pairs={{0,1},{1,0},{2,3},{3,2},{4,5},{5,4},{6,7},{7,6},{8,9},{9,8},{10,11... | collective-permute-start | bytes 417800 | tf_op jit(solution)/shard_map/ppermute | solution.py:446
  14.3 5.4 %collective-permute-done.2.refs_4_ = bf16[2,256,256]{2,1,0:T(8,128)(2,1)S(1)} collective-permute-done((bf16[2,256,256]{2,1,0:T(8,128)(2,1)S(1)}, bf16[2,256,256]{2,1,0:T(8,128)(2,1)S(1)}, u32[]{:S(2)}, u32[]{:S(2)}) %collective-permute-start.2) | collective-permute-done | bytes 262176 | tf_op jit(solution)/shard_map/ppermute | solution.py:29
  19.7 0.8 %collective-permute-start.3 = (bf16[2,256,256]{2,1,0:T(8,128)(2,1)S(1)}, bf16[2,256,256]{2,1,0:T(8,128)(2,1)S(1)}, u32[]{:S(2)}, u32[]{:S(2)}) collective-permute-start(bf16[2,256,256]{2,1,0:T(8,128)(2,1)S(1)} %collective-permute-done.2.refs_4_), channel_id=1, source_target_pairs={{2,0},{4,2},{6,4},{0,6},{10,8},{12,10},{14,12},{8,14},{18,16},{20,... | collective-permute-start | bytes 786440 | tf_op jit(solution)/shard_map/ppermute | solution.py:29
  20.5 0.0 copy-start.4
  20.5 1.8 %shard_map.87 = (bf16[2,256,256]{2,1,0:T(8,128)(2,1)S(1)}, f32[2,256,512]{2,1,0:T(8,128)S(1)}) custom-call(bf16[272,256]{1,0:T(8,128)(2,1)S(1)} %get-tuple-element.31.refs_0_.refs_2_, bf16[272,256]{1,0:T(8,128)(2,1)S(1)} %collective-permute-done.refs_1_.refs_3_, bf16[2,256,256]{2,1,0:T(8,128)(2,1)S(1)} %get-tuple-element.61.refs_6_.refs_2_.refs_0_, ...), custom_call_target="tpu_custom_call" | custom-call | flops 1500000000 | bytes 4472832 | tf_op jit(solution)/shard_map/pallas_call | solution.py:280
  22.3 2.1 %collective-permute-done.3.refs_5_ = bf16[2,256,256]{2,1,0:T(8,128)(2,1)S(1)} collective-permute-done((bf16[2,256,256]{2,1,0:T(8,128)(2,1)S(1)}, bf16[2,256,256]{2,1,0:T(8,128)(2,1)S(1)}, u32[]{:S(2)}, u32[]{:S(2)}) %collective-permute-start.3) | collective-permute-done | bytes 262176 | tf_op jit(solution)/shard_map/ppermute | solution.py:29
  24.4 4.3 %shard_map.88 = (bf16[2,256,256]{2,1,0:T(8,128)(2,1)S(1)}, bf16[2,256,256]{2,1,0:T(8,128)(2,1)S(1)}, bf16[528,256]{1,0:T(8,128)(2,1)S(1)}, bf16[2,256,256]{2,1,0...) custom-call(bf16[272,256]{1,0:T(8,128)(2,1)S(1)} %get-tuple-element.31.refs_0_.refs_2_, ...), custom_call_target="tpu_custom_call" | custom-call | flops 4000000000 | bytes 6578176 | tf_op jit(solution)/shard_map/pallas_call | solution.py:280
  28.7 1.0 %collective-permute-start.6 = (bf16[256,512]{1,0:T(8,128)(2,1)S(1)}, bf16[256,512]{1,0:T(8,128)(2,1)S(1)}, u32[]{:S(2)}, u32[]{:S(2)}) collective-permute-start(bf16[256,512]{1,0:T(8,128)(2,1)S(1)} %get-tuple-element.39), channel_id=1, source_target_pairs={{0,2},{1,3},{2,0},{3,1},{4,6},{5,7},{6,4},{7,5},{8,10},{9,11},{10,... | collective-permute-start | bytes 786440 | tf_op jit(solution)/shard_map/ppermute | solution.py:387
  29.7 1.2 %collective-permute-done.6.refs_1_ = bf16[256,512]{1,0:T(8,128)(2,1)S(1)} collective-permute-done((bf16[256,512]{1,0:T(8,128)(2,1)S(1)}, bf16[256,512]{1,0:T(8,128)(2,1)S(1)}, u32[]{:S(2)}, u32[]{:S(2)}) %collective-permute-start.6) | collective-permute-done | bytes 262176 | tf_op jit(solution)/shard_map/ppermute | solution.py:387
  30.9 0.8 %shard_map.89 = (f32[64,512]{1,0:T(8,128)S(1)}, bf16[64,512]{1,0:T(8,128)(2,1)S(1)}, bf16[64,512]{1,0:T(8,128)(2,1)S(1)}, bf16[64,512]{1,0:T(8,128)(2,1)S(1)}, b...) custom-call(bf16[256,512]{1,0:T(8,128)(2,1)S(1)} %get-tuple-element.38.refs_0_, ...), custom_call_target="tpu_custom_call" | custom-call | flops 1000000 | bytes 2187264 | tf_op jit(solution)/shard_map/pallas_call | solution.py:280
  31.6 1.6 %collective-permute-start.7 = (bf16[64,512]{1,0:T(8,128)(2,1)S(1)}, bf16[64,512]{1,0:T(8,128)(2,1)S(1)}, u32[]{:S(2)}, u32[]{:S(2)}) collective-permute-start(bf16[64,512]{1,0:T(8,128)(2,1)S(1)} %get-tuple-element.42), channel_id=1, source_target_pairs={{0,1},{1,0},{2,3},{3,2},{4,5},{5,4},{6,7},{7,6},{8,9},{9,8},{10,11... | collective-permute-start | bytes 196616 | tf_op jit(solution)/shard_map/ppermute | solution.py:387
  33.2 1.4 %collective-permute-start.8 = (bf16[64,512]{1,0:T(8,128)(2,1)S(1)}, bf16[64,512]{1,0:T(8,128)(2,1)S(1)}, u32[]{:S(2)}, u32[]{:S(2)}) collective-permute-start(bf16[64,512]{1,0:T(8,128)(2,1)S(1)} %get-tuple-element.43), channel_id=1, source_target_pairs={{0,4},{1,5},{2,6},{3,7},{4,0},{5,1},{6,2},{7,3},{8,12},{9,13},{10,... | collective-permute-start | bytes 196616 | tf_op jit(solution)/shard_map/ppermute | solution.py:387
  34.6 0.6 collective-permute-start.9
  35.2 5.5 %collective-permute-done.10.refs_5_ = bf16[528,256]{1,0:T(8,128)(2,1)S(1)} collective-permute-done((bf16[528,256]{1,0:T(8,128)(2,1)S(1)}, bf16[528,256]{1,0:T(8,128)(2,1)S(1)}, u32[]{:S(2)}, u32[]{:S(2)}) %collective-permute-start.10) | collective-permute-done | bytes 270368 | tf_op jit(solution)/shard_map/ppermute | solution.py:29
  40.7 0.1 shard_map.90
  40.9 0.1 collective-permute-start.13
  40.9 0.1 collective-permute-start.11
  41.0 6.1 %collective-permute-done.11.refs_1_ = bf16[64,512]{1,0:T(8,128)(2,1)S(1)} collective-permute-done((bf16[64,512]{1,0:T(8,128)(2,1)S(1)}, bf16[64,512]{1,0:T(8,128)(2,1)S(1)}, u32[]{:S(2)}, u32[]{:S(2)}) %collective-permute-start.11) | collective-permute-done | bytes 65568 | tf_op jit(solution)/shard_map/ppermute | solution.py:387
  47.1 0.2 shard_map.91
  47.3 0.2 collective-permute-start.15
  47.5 0.7 collective-permute-start.14
  48.2 5.6 %collective-permute-done.14.refs_1_ = bf16[64,512]{1,0:T(8,128)(2,1)S(1)} collective-permute-done((bf16[64,512]{1,0:T(8,128)(2,1)S(1)}, bf16[64,512]{1,0:T(8,128)(2,1)S(1)}, u32[]{:S(2)}, u32[]{:S(2)}) %collective-permute-start.14) | collective-permute-done | bytes 65568 | tf_op jit(solution)/shard_map/ppermute | solution.py:387
  53.8 0.1 shard_map.92
  53.9 1.9 %collective-permute-start.20 = (bf16[64,512]{1,0:T(8,128)(2,1)S(1)}, bf16[64,512]{1,0:T(8,128)(2,1)S(1)}, u32[]{:S(2)}, u32[]{:S(2)}) collective-permute-start(bf16[64,512]{1,0:T(8,128)(2,1)S(1)} %get-tuple-element.57.refs_0_), channel_id=1, source_target_pairs={{0,5},{1,4},{2,7},{3,6},{4,1},{5,0},{6,3},{7,2},{8,13},{9,12},{10,... | collective-permute-start | bytes 196616 | tf_op jit(solution)/shard_map/ppermute | solution.py:387
  55.8 1.1 %collective-permute-start.19 = (bf16[64,512]{1,0:T(8,128)(2,1)S(1)}, bf16[64,512]{1,0:T(8,128)(2,1)S(1)}, u32[]{:S(2)}, u32[]{:S(2)}) collective-permute-start(bf16[64,512]{1,0:T(8,128)(2,1)S(1)} %get-tuple-element.57.refs_0_), channel_id=1, source_target_pairs={{0,4},{1,5},{2,6},{3,7},{4,0},{5,1},{6,2},{7,3},{8,12},{9,13},{10,... | collective-permute-start | bytes 196616 | tf_op jit(solution)/shard_map/ppermute | solution.py:387
  57.0 0.5 collective-permute-start.18
  57.5 1.5 %collective-permute-start.17 = (bf16[2,256,256]{2,1,0:T(8,128)(2,1)S(1)}, bf16[2,256,256]{2,1,0:T(8,128)(2,1)S(1)}, u32[]{:S(2)}, u32[]{:S(2)}) collective-permute-start(bf16[2,256,256]{2,1,0:T(8,128)(2,1)S(1)} %get-tuple-element.56.refs_1_), channel_id=1, source_target_pairs={{0,1},{1,0},{2,3},{3,2},{4,5},{5,4},{6,7},{7,6},{8,9},{9,8},{10,11... | collective-permute-start | bytes 786440 | tf_op jit(solution)/shard_map/ppermute | solution.py:475
  59.0 0.8 %collective-permute-done.20.refs_3_ = bf16[64,512]{1,0:T(8,128)(2,1)S(1)} collective-permute-done((bf16[64,512]{1,0:T(8,128)(2,1)S(1)}, bf16[64,512]{1,0:T(8,128)(2,1)S(1)}, u32[]{:S(2)}, u32[]{:S(2)}) %collective-permute-start.20) | collective-permute-done | bytes 65568 | tf_op jit(solution)/shard_map/ppermute | solution.py:387
  59.8 0.7 collective-permute-done.19.refs_2_
  60.5 1.5 %collective-permute-done.18.refs_1_ = bf16[64,512]{1,0:T(8,128)(2,1)S(1)} collective-permute-done((bf16[64,512]{1,0:T(8,128)(2,1)S(1)}, bf16[64,512]{1,0:T(8,128)(2,1)S(1)}, u32[]{:S(2)}, u32[]{:S(2)}) %collective-permute-start.18) | collective-permute-done | bytes 65568 | tf_op jit(solution)/shard_map/ppermute | solution.py:387
  62.0 0.1 shard_map.94.refs_0_
  62.1 0.1 collective-permute-start.21
  62.1 0.7 %collective-permute-start.16 = (bf16[2,256,256]{2,1,0:T(8,128)(2,1)S(1)}, bf16[2,256,256]{2,1,0:T(8,128)(2,1)S(1)}, u32[]{:S(2)}, u32[]{:S(2)}) collective-permute-start(bf16[2,256,256]{2,1,0:T(8,128)(2,1)S(1)} %get-tuple-element.55.refs_1_), channel_id=1, source_target_pairs={{0,1},{1,0},{2,3},{3,2},{4,5},{5,4},{6,7},{7,6},{8,9},{9,8},{10,11... | collective-permute-start | bytes 786440 | tf_op jit(solution)/shard_map/ppermute | solution.py:475
  62.9 4.7 %collective-permute-done.17.refs_2_ = bf16[2,256,256]{2,1,0:T(8,128)(2,1)S(1)} collective-permute-done((bf16[2,256,256]{2,1,0:T(8,128)(2,1)S(1)}, bf16[2,256,256]{2,1,0:T(8,128)(2,1)S(1)}, u32[]{:S(2)}, u32[]{:S(2)}) %collective-permute-start.17) | collective-permute-done | bytes 262176 | tf_op jit(solution)/shard_map/ppermute | solution.py:475
  67.6 0.8 %shard_map.93.refs_3_ = bf16[1,2,2,256,256]{4,3,2,1,0:T(8,128)(2,1)} custom-call(bf16[2,256,256]{2,1,0:T(8,128)(2,1)S(1)} %get-tuple-element.33.refs_2_.refs_0_, bf16[2,256,256]{2,1,0:T(8,128)(2,1)S(1)} %get-tuple-element.56.refs_1_, bf16[2,256,256]{2,1,0:T(8,128)(2,1)S(1)} %collective-permute-done.17.refs_2_), custom_call_target="tpu_custom_call" | custom-call | flops 131072 | bytes 1048576 | tf_op jit(solution)/shard_map/pallas_call | solution.py:297
  68.5 1.2 %shard_map.95 = (f32[2048,128]{1,0:T(8,128)}, f32[8,128]{1,0:T(8,128)S(1)}) custom-call(bf16[256,512]{1,0:T(8,128)(2,1)S(1)} %shard_map.94.refs_0_, bf16[256,512]{1,0:T(8,128)(2,1)S(1)} %collective-permute-done.21.refs_1_, f32[2048,128]{1,0:T(8,128)S(1)} %bitcast.16), custom_call_target="tpu_custom_call" | custom-call | flops 1000000 | bytes 2625536 | tf_op jit(solution)/shard_map/pallas_call | solution.py:280
  69.7 2.5 %collective-permute-done.16.refs_2_ = bf16[2,256,256]{2,1,0:T(8,128)(2,1)S(1)} collective-permute-done((bf16[2,256,256]{2,1,0:T(8,128)(2,1)S(1)}, bf16[2,256,256]{2,1,0:T(8,128)(2,1)S(1)}, u32[]{:S(2)}, u32[]{:S(2)}) %collective-permute-start.16) | collective-permute-done | bytes 262176 | tf_op jit(solution)/shard_map/ppermute | solution.py:475
  72.1 0.8 %shard_map.96 = bf16[1,2,2,256,256]{4,3,2,1,0:T(8,128)(2,1)} custom-call(bf16[2,256,256]{2,1,0:T(8,128)(2,1)S(1)} %get-tuple-element.61.refs_6_.refs_2_.refs_0_, bf16[2,256,256]{2,1,0:T(8,128)(2,1)S(1)} %get-tuple-element.55.refs_1_, bf16[2,256,256]{2,1,0:T(8,128)(2,1)S(1)} %collective-permute-done.16.refs_2_, ...), custom_call_target="tpu_custom_call", output_to_operand_aliasing={{}: (3, {})} | custom-call | flops 131072 | bytes 1048576 | tf_op jit(solution)/shard_map/pallas_call | solution.py:297
  (18 shorter events, 0.0 us)
Async XLA Ops:
  0.6 7.6 %copy-start = (f32[2,256,2,256]{3,2,1,0:T(2,128)S(1)}, f32[2,256,2,256]{3,2,1,0:T(2,128)}, u32[]{:S(2)}) copy-start(f32[2,256,2,256]{3,2,1,0:T(2,128)} %param.8) | copy-start | bytes 3145732
  1.8 11.0 %collective-permute-start.4 = (bf16[2,256,256]{2,1,0:T(8,128)(2,1)S(1)}, bf16[2,256,256]{2,1,0:T(8,128)(2,1)S(1)}, u32[]{:S(2)}, u32[]{:S(2)}) collective-permute-start(bf16[2,256,256]{2,1,0:T(8,128)(2,1)S(1)} %get-tuple-element.61.refs_6_.refs_2_.refs_0_), channel_id=1, source_target_pairs={{8,0},{10,2},{12,4},{14,6},{16,8},{18,10},{20,12},{22,14},{24,16},... | collective-permute-start | bytes 786440 | tf_op jit(solution)/shard_map/ppermute | solution.py:29
  6.9 13.6 %collective-permute-start.1 = (bf16[2,2,256,256]{3,2,1,0:T(8,128)(2,1)}, bf16[2,2,256,256]{3,2,1,0:T(8,128)(2,1)S(1)}, u32[]{:S(2)}, u32[]{:S(2)}) collective-permute-start(bf16[2,2,256,256]{3,2,1,0:T(8,128)(2,1)} %bitcast.17), channel_id=1, source_target_pairs={{2,0},{4,2},{6,4},{0,6},{10,8},{12,10},{14,12},{8,14},{18,16},{20,... | collective-permute-start | bytes 1572872 | tf_op jit(solution)/shard_map/ppermute | solution.py:29
  8.2 0.7 copy-start.3
  8.9 1.0 %copy-start.1 = (bf16[512,512]{1,0:T(8,128)(2,1)S(1)}, bf16[512,512]{1,0:T(8,128)(2,1)}, u32[]{:S(2)}) copy-start(bf16[512,512]{1,0:T(8,128)(2,1)} %constant.10.refs_5_) | copy-start | bytes 1572868
  9.9 0.9 %copy-start.2 = (bf16[1,1,2,256,256]{4,3,2,1,0:T(8,128)(2,1)S(1)}, bf16[1,1,2,256,256]{4,3,2,1,0:T(8,128)(2,1)}, u32[]{:S(2)}) copy-start(bf16[1,1,2,256,256]{4,3,2,1,0:T(8,128)(2,1)} %refs_3_.1) | copy-start | bytes 786436
  11.6 8.1 %collective-permute-start.2 = (bf16[2,256,256]{2,1,0:T(8,128)(2,1)S(1)}, bf16[2,256,256]{2,1,0:T(8,128)(2,1)S(1)}, u32[]{:S(2)}, u32[]{:S(2)}) collective-permute-start(bf16[2,256,256]{2,1,0:T(8,128)(2,1)S(1)} %get-tuple-element.33.refs_2_.refs_0_), channel_id=1, source_target_pairs={{8,0},{10,2},{12,4},{14,6},{16,8},{18,10},{20,12},{22,14},{24,16},... | collective-permute-start | bytes 786440 | tf_op jit(solution)/shard_map/ppermute | solution.py:29
  12.8 7.7 %collective-permute-start.5 = (bf16[2,256,256]{2,1,0:T(8,128)(2,1)S(1)}, bf16[2,256,256]{2,1,0:T(8,128)(2,1)S(1)}, u32[]{:S(2)}, u32[]{:S(2)}) collective-permute-start(bf16[2,256,256]{2,1,0:T(8,128)(2,1)S(1)} %collective-permute-done.4.refs_4_), channel_id=1, source_target_pairs={{2,0},{4,2},{6,4},{0,6},{10,8},{12,10},{14,12},{8,14},{18,16},{20,... | collective-permute-start | bytes 786440 | tf_op jit(solution)/shard_map/ppermute | solution.py:29
  12.8 7.7 %collective-permute-start = (bf16[272,256]{1,0:T(8,128)(2,1)S(1)}, bf16[272,256]{1,0:T(8,128)(2,1)S(1)}, u32[]{:S(2)}, u32[]{:S(2)}) collective-permute-start(bf16[272,256]{1,0:T(8,128)(2,1)S(1)} %get-tuple-element.32), channel_id=1, source_target_pairs={{0,1},{1,0},{2,3},{3,2},{4,5},{5,4},{6,7},{7,6},{8,9},{9,8},{10,11... | collective-permute-start | bytes 417800 | tf_op jit(solution)/shard_map/ppermute | solution.py:446
  19.7 4.7 %collective-permute-start.3 = (bf16[2,256,256]{2,1,0:T(8,128)(2,1)S(1)}, bf16[2,256,256]{2,1,0:T(8,128)(2,1)S(1)}, u32[]{:S(2)}, u32[]{:S(2)}) collective-permute-start(bf16[2,256,256]{2,1,0:T(8,128)(2,1)S(1)} %collective-permute-done.2.refs_4_), channel_id=1, source_target_pairs={{2,0},{4,2},{6,4},{0,6},{10,8},{12,10},{14,12},{8,14},{18,16},{20,... | collective-permute-start | bytes 786440 | tf_op jit(solution)/shard_map/ppermute | solution.py:29
  20.5 3.9 %copy-start.4 = (bf16[512,512]{1,0:T(8,128)(2,1)S(1)}, bf16[512,512]{1,0:T(8,128)(2,1)}, u32[]{:S(2)}) copy-start(bf16[512,512]{1,0:T(8,128)(2,1)} %constant.11.refs_10_) | copy-start | bytes 1572868
  28.7 2.2 %collective-permute-start.6 = (bf16[256,512]{1,0:T(8,128)(2,1)S(1)}, bf16[256,512]{1,0:T(8,128)(2,1)S(1)}, u32[]{:S(2)}, u32[]{:S(2)}) collective-permute-start(bf16[256,512]{1,0:T(8,128)(2,1)S(1)} %get-tuple-element.39), channel_id=1, source_target_pairs={{0,2},{1,3},{2,0},{3,1},{4,6},{5,7},{6,4},{7,5},{8,10},{9,11},{10,... | collective-permute-start | bytes 786440 | tf_op jit(solution)/shard_map/ppermute | solution.py:387
  29.7 11.0 %collective-permute-start.10 = (bf16[528,256]{1,0:T(8,128)(2,1)S(1)}, bf16[528,256]{1,0:T(8,128)(2,1)S(1)}, u32[]{:S(2)}, u32[]{:S(2)}) collective-permute-start(bf16[528,256]{1,0:T(8,128)(2,1)S(1)} %get-tuple-element.46), channel_id=1, source_target_pairs={{24,0},{26,2},{28,4},{30,6},{0,8},{2,10},{4,12},{6,14},{8,16},{10,... | collective-permute-start | bytes 811016 | tf_op jit(solution)/shard_map/ppermute | solution.py:29
  31.6 9.1 %collective-permute-start.7 = (bf16[64,512]{1,0:T(8,128)(2,1)S(1)}, bf16[64,512]{1,0:T(8,128)(2,1)S(1)}, u32[]{:S(2)}, u32[]{:S(2)}) collective-permute-start(bf16[64,512]{1,0:T(8,128)(2,1)S(1)} %get-tuple-element.42), channel_id=1, source_target_pairs={{0,1},{1,0},{2,3},{3,2},{4,5},{5,4},{6,7},{7,6},{8,9},{9,8},{10,11... | collective-permute-start | bytes 196616 | tf_op jit(solution)/shard_map/ppermute | solution.py:387
  33.2 7.5 %collective-permute-start.8 = (bf16[64,512]{1,0:T(8,128)(2,1)S(1)}, bf16[64,512]{1,0:T(8,128)(2,1)S(1)}, u32[]{:S(2)}, u32[]{:S(2)}) collective-permute-start(bf16[64,512]{1,0:T(8,128)(2,1)S(1)} %get-tuple-element.43), channel_id=1, source_target_pairs={{0,4},{1,5},{2,6},{3,7},{4,0},{5,1},{6,2},{7,3},{8,12},{9,13},{10,... | collective-permute-start | bytes 196616 | tf_op jit(solution)/shard_map/ppermute | solution.py:387
  34.6 6.1 %collective-permute-start.9 = (bf16[64,512]{1,0:T(8,128)(2,1)S(1)}, bf16[64,512]{1,0:T(8,128)(2,1)S(1)}, u32[]{:S(2)}, u32[]{:S(2)}) collective-permute-start(bf16[64,512]{1,0:T(8,128)(2,1)S(1)} %get-tuple-element.44), channel_id=1, source_target_pairs={{0,5},{1,4},{2,7},{3,6},{4,1},{5,0},{6,3},{7,2},{8,13},{9,12},{10,... | collective-permute-start | bytes 196616 | tf_op jit(solution)/shard_map/ppermute | solution.py:387
  35.2 11.9 %collective-permute-start.12 = (bf16[528,256]{1,0:T(8,128)(2,1)S(1)}, bf16[528,256]{1,0:T(8,128)(2,1)S(1)}, u32[]{:S(2)}, u32[]{:S(2)}) collective-permute-start(bf16[528,256]{1,0:T(8,128)(2,1)S(1)} %get-tuple-element.49), channel_id=1, source_target_pairs={{24,0},{26,2},{28,4},{30,6},{0,8},{2,10},{4,12},{6,14},{8,16},{10,... | collective-permute-start | bytes 811016 | tf_op jit(solution)/shard_map/ppermute | solution.py:29
  40.9 6.3 %collective-permute-start.13 = (bf16[2,256,256]{2,1,0:T(8,128)(2,1)S(1)}, bf16[2,256,256]{2,1,0:T(8,128)(2,1)S(1)}, u32[]{:S(2)}, u32[]{:S(2)}) collective-permute-start(bf16[2,256,256]{2,1,0:T(8,128)(2,1)S(1)} %get-tuple-element.51), channel_id=1, source_target_pairs={{6,0},{0,2},{2,4},{4,6},{14,8},{8,10},{10,12},{12,14},{22,16},{16,... | collective-permute-start | bytes 786440 | tf_op jit(solution)/shard_map/ppermute | solution.py:29
  40.9 6.2 %collective-permute-start.11 = (bf16[64,512]{1,0:T(8,128)(2,1)S(1)}, bf16[64,512]{1,0:T(8,128)(2,1)S(1)}, u32[]{:S(2)}, u32[]{:S(2)}) collective-permute-start(bf16[64,512]{1,0:T(8,128)(2,1)S(1)} %get-tuple-element.47.refs_0_), channel_id=1, source_target_pairs={{0,8},{1,9},{2,10},{3,11},{4,12},{5,13},{6,14},{7,15},{8,0},{9,1},... | collective-permute-start | bytes 196616 | tf_op jit(solution)/shard_map/ppermute | solution.py:387
  47.3 6.5 %collective-permute-start.15 = (bf16[2,256,256]{2,1,0:T(8,128)(2,1)S(1)}, bf16[2,256,256]{2,1,0:T(8,128)(2,1)S(1)}, u32[]{:S(2)}, u32[]{:S(2)}) collective-permute-start(bf16[2,256,256]{2,1,0:T(8,128)(2,1)S(1)} %get-tuple-element.54), channel_id=1, source_target_pairs={{6,0},{0,2},{2,4},{4,6},{14,8},{8,10},{10,12},{12,14},{22,16},{16,... | collective-permute-start | bytes 786440 | tf_op jit(solution)/shard_map/ppermute | solution.py:29
  47.5 6.3 %collective-permute-start.14 = (bf16[64,512]{1,0:T(8,128)(2,1)S(1)}, bf16[64,512]{1,0:T(8,128)(2,1)S(1)}, u32[]{:S(2)}, u32[]{:S(2)}) collective-permute-start(bf16[64,512]{1,0:T(8,128)(2,1)S(1)} %get-tuple-element.52.refs_0_), channel_id=1, source_target_pairs={{0,16},{1,17},{2,18},{3,19},{4,20},{5,21},{6,22},{7,23},{8,24},{9,... | collective-permute-start | bytes 196616 | tf_op jit(solution)/shard_map/ppermute | solution.py:387
  53.9 5.9 %collective-permute-start.20 = (bf16[64,512]{1,0:T(8,128)(2,1)S(1)}, bf16[64,512]{1,0:T(8,128)(2,1)S(1)}, u32[]{:S(2)}, u32[]{:S(2)}) collective-permute-start(bf16[64,512]{1,0:T(8,128)(2,1)S(1)} %get-tuple-element.57.refs_0_), channel_id=1, source_target_pairs={{0,5},{1,4},{2,7},{3,6},{4,1},{5,0},{6,3},{7,2},{8,13},{9,12},{10,... | collective-permute-start | bytes 196616 | tf_op jit(solution)/shard_map/ppermute | solution.py:387
  55.8 4.6 %collective-permute-start.19 = (bf16[64,512]{1,0:T(8,128)(2,1)S(1)}, bf16[64,512]{1,0:T(8,128)(2,1)S(1)}, u32[]{:S(2)}, u32[]{:S(2)}) collective-permute-start(bf16[64,512]{1,0:T(8,128)(2,1)S(1)} %get-tuple-element.57.refs_0_), channel_id=1, source_target_pairs={{0,4},{1,5},{2,6},{3,7},{4,0},{5,1},{6,2},{7,3},{8,12},{9,13},{10,... | collective-permute-start | bytes 196616 | tf_op jit(solution)/shard_map/ppermute | solution.py:387
  57.0 5.0 %collective-permute-start.18 = (bf16[64,512]{1,0:T(8,128)(2,1)S(1)}, bf16[64,512]{1,0:T(8,128)(2,1)S(1)}, u32[]{:S(2)}, u32[]{:S(2)}) collective-permute-start(bf16[64,512]{1,0:T(8,128)(2,1)S(1)} %get-tuple-element.57.refs_0_), channel_id=1, source_target_pairs={{0,1},{1,0},{2,3},{3,2},{4,5},{5,4},{6,7},{7,6},{8,9},{9,8},{10,11... | collective-permute-start | bytes 196616 | tf_op jit(solution)/shard_map/ppermute | solution.py:387
  57.5 10.1 %collective-permute-start.17 = (bf16[2,256,256]{2,1,0:T(8,128)(2,1)S(1)}, bf16[2,256,256]{2,1,0:T(8,128)(2,1)S(1)}, u32[]{:S(2)}, u32[]{:S(2)}) collective-permute-start(bf16[2,256,256]{2,1,0:T(8,128)(2,1)S(1)} %get-tuple-element.56.refs_1_), channel_id=1, source_target_pairs={{0,1},{1,0},{2,3},{3,2},{4,5},{5,4},{6,7},{7,6},{8,9},{9,8},{10,11... | collective-permute-start | bytes 786440 | tf_op jit(solution)/shard_map/ppermute | solution.py:475
  62.1 6.4 %collective-permute-start.21 = (bf16[256,512]{1,0:T(8,128)(2,1)S(1)}, bf16[256,512]{1,0:T(8,128)(2,1)S(1)}, u32[]{:S(2)}, u32[]{:S(2)}) collective-permute-start(bf16[256,512]{1,0:T(8,128)(2,1)S(1)} %shard_map.94.refs_0_), channel_id=1, source_target_pairs={{0,2},{1,3},{2,0},{3,1},{4,6},{5,7},{6,4},{7,5},{8,10},{9,11},{10,... | collective-permute-start | bytes 786440 | tf_op jit(solution)/shard_map/ppermute | solution.py:387
  62.1 10.0 %collective-permute-start.16 = (bf16[2,256,256]{2,1,0:T(8,128)(2,1)S(1)}, bf16[2,256,256]{2,1,0:T(8,128)(2,1)S(1)}, u32[]{:S(2)}, u32[]{:S(2)}) collective-permute-start(bf16[2,256,256]{2,1,0:T(8,128)(2,1)S(1)} %get-tuple-element.55.refs_1_), channel_id=1, source_target_pairs={{0,1},{1,0},{2,3},{3,2},{4,5},{5,4},{6,7},{7,6},{8,9},{9,8},{10,11... | collective-permute-start | bytes 786440 | tf_op jit(solution)/shard_map/ppermute | solution.py:475

commit v8 on v7

--- a/solution.py
+++ b/solution.py
@@ -105,13 +105,9 @@
     return jnp.concatenate(halves, axis=1)
 
 
-def ready_kernel(
-    offsets_ref, counts_ref, own_ref, patterns_ref, probe_ref, prop_ref,
-    own_out, mine_ref, sent_ref, planes_ref, table_ref,
-):
+def message_kernel(offsets_ref, counts_ref, own_ref, patterns_ref, own_out, mine_ref, sent_ref):
     own_out[...] = own_ref[...]
-    table_ref[...] = prop_ref[...]
-    n = planes_ref.shape[1]
+    n = mine_ref.shape[1]
     at = lax.broadcasted_iota(jnp.int32, (16, n), 0)
     busy = (counts_ref[0, 0] == patterns_ref.shape[2]).astype(jnp.int32)
     for slot, ref in enumerate((mine_ref, sent_ref)):
@@ -119,6 +115,11 @@
         rows = jnp.where(at == 0, row, jnp.where(at == 1, col, busy))
         ref[pl.ds(0, n), :] = patterns_ref[0, 0, slot]
         ref[pl.ds(n, 16), :] = rows.astype(f32).astype(bf16)
+
+
+def ready_kernel(probe_ref, prop_ref, planes_ref, table_ref):
+    table_ref[...] = prop_ref[...]
+    n = planes_ref.shape[1]
     modes = planes_ref.shape[2] // n
     for part in range(2):
         for mode in range(modes):
@@ -233,7 +234,8 @@
 
 
 def update_kernel(layer, own_ref, part_ref, other_ref, *refs):
-    out_hbm, new_ref, sem = refs[-3:]
+    out_hbm, token_ref, new_ref, sem = refs[-4:]
+    token_ref[...] = jnp.zeros_like(token_ref)
     grad = part_ref[...].astype(f32) + other_ref[...].astype(f32)
     new_ref[...] = (own_ref[...].astype(f32) - object_rate * grad).astype(bf16)
     copy = pltpu.make_async_copy(new_ref, out_hbm.at[0, layer], sem.at[0])
@@ -290,20 +292,20 @@
     return results[0] if len(jobs) == 1 else results
 
 
-def updated(layer, own, part, other, like, so_far, after):
+def updated(layer, own, part, other, like, so_far=None, flops=0):
     vmem = pl.BlockSpec(memory_space=pltpu.VMEM)
     anywhere = pl.BlockSpec(memory_space=pl.ANY)
-    extra = [x for x in (so_far,) if x is not None] + list(after)
+    extra = [x for x in (so_far,) if x is not None]
     return pl.pallas_call(
         lambda *refs: update_kernel(layer, *refs),
-        out_shape=like,
+        out_shape=[like, shape_of(f32, 8, 128)],
         in_specs=[vmem] * 3 + [anywhere] * len(extra),
-        out_specs=pl.BlockSpec(memory_space=pl.ANY),
+        out_specs=[anywhere, vmem],
         scratch_shapes=[pltpu.VMEM(own.shape, bf16), pltpu.SemaphoreType.DMA((1,))],
         input_output_aliases={} if so_far is None else {3: 0},
         compiler_params=pltpu.CompilerParams(vmem_limit_bytes=4 * 2**20),
         cost_estimate=pl.CostEstimate(
-            flops=own.size, bytes_accessed=8 * own.size, transcendentals=0
+            flops=own.size + flops, bytes_accessed=8 * own.size, transcendentals=0
         ),
     )(own, part, other, *extra)
 
@@ -359,9 +361,8 @@
         out_ref[pl.ds(block * size, size), :] = blocks[block]
 
 
-def probe_kernel(step, modes, mine_ref, other_ref, probe_ref, out_ref, token_ref):
+def probe_kernel(step, modes, mine_ref, other_ref, probe_ref, out_ref):
     core = place_of(core_group())
-    token_ref[...] = jnp.zeros_like(token_ref)
     lane_tiles = 2
     n = mine_ref.shape[0]
     stride = lane_tiles * modes
@@ -431,15 +432,20 @@
     right = from_behind(tile_object[0], 0, -1)
     exchanged = lax.axis_size("pos") == patterns.shape[2]
     message = shape_of(bf16, pixels + 16, pixels)
-    own1, mine, sent, probe_planes, table = run(
+    own1, mine, sent = run(
         job(
-            ready_kernel,
-            [tile, message, message, planes, shape_of(bf16, *prop.shape)],
-            [own[1], patterns, probe, prop],
+            message_kernel,
+            [tile, message, message],
+            [own[1], patterns],
             scalars=[offsets, counts if exchanged else jnp.zeros_like(counts)],
         ),
-        limit=16,
+        limit=4,
         after=[own[0]],
+    )
+    probe_planes, table = run(
+        job(ready_kernel, [planes, shape_of(bf16, *prop.shape)], [probe, prop]),
+        limit=8,
+        after=[own1],
     )
     below1 = from_behind(own1, -1, 0)
     if exchanged:
@@ -509,22 +515,25 @@
     other0 = over_owners(part0)
     for group in others:
         (total,) = run(added(total, swapped(total, group)))
+    like = shape_of(bf16, *tile_object.shape)
+    new_object, token = updated(1, own1, part1, other1, like)
     for group in reversed(scattered):
-        (total,) = run(joined(group, total, swapped(total, group)))
+        (total,) = run(joined(group, total, swapped(total, group)), after=[token])
     other_half = swap_with(total, core, 1)
+    new_object, token = updated(
+        0, own[0], part0, other0, like, so_far=new_object, flops=3_000_000_000
+    )
     positions_all = lax.axis_size("tile") * lax.axis_size("pos") * (patterns.shape[2] // 2)
     step = probe_rate / math.sqrt(positions_all)
-    new_probe, token = run(
+    (new_probe,) = run(
         job(
             lambda *refs: probe_kernel(step, modes, *refs),
-            [shape_of(f32, *probe.shape), shape_of(f32, 8, 128)],
+            [shape_of(f32, *probe.shape)],
             [total, other_half, probe],
         ),
         limit=8,
-    )
-    like = shape_of(bf16, *tile_object.shape)
-    new_object = updated(1, own1, part1, other1, like, None, [])
-    new_object = updated(0, own[0], part0, other0, like, new_object, [token])
+        after=[token],
+    )
     new_probe = new_probe.reshape(2, pixels, lane_tiles, modes, 128).transpose(0, 1, 3, 2, 4)
     return (new_object, new_probe.reshape(probe_modes.shape))
 

time: 73.2 us -> 68 us (0.929)
  waiting for transfers between devices: 36.8 us -> 32 us
  local copies, waits for them, and re-layouts: 3.82 us -> 1.86 us
  starting transfers between devices: 20 us -> 21.7 us
    ppermute x2, waiting for transfers between devices: 7.2 us -> 0.01 us  [over_owners(): return lax.ppermute(part, 'pos', [(0, 1), (1, 0)])]
    ppermute x10, waiting for transfers between devices: 15.9 us -> 18.2 us  [swap_with(): lax.ppermute(x, ('tile', 'pos'), [(i, i ^ mask) for i in range(devices)])]
    unnamed x10, local copies, waits for them, and re-layouts: 2.67 us -> 0.69 us
    ppermute x1, waiting for transfers between devices: 0.01 us -> 1.16 us  [shards(): sent = lax.ppermute(sent, 'pos', [(i, 1 - i) for i in range(2)])]
    ppermute x9, waiting for transfers between devices: 13.7 us -> 12.6 us  [from_behind(): return lax.ppermute(block, 'tile', [(source(i), i) for i in range(tiles)])]
    ppermute x9, starting transfers between devices: 7.31 us -> 8.11 us  [from_behind(): return lax.ppermute(block, 'tile', [(source(i), i) for i in range(tiles)])]
    pallas_call x9 -> x10, Pallas kernels: 9.21 us -> 9.21 us  [run(): pl.pallas_call(body, out_shape=sum(outs, []), in_specs=sum(specs, []) + [...]
  transfers between devices with their start and end apart: 22 -> 22, of which waited for: 12 -> 11; matrix products, arithmetic and copies ran while one was open for 0% -> 0% of each run, Pallas kernels for 7% -> 8%
where the time goes in v8:
time: 68 us; the launch traced here: 67.9 us
  waiting for transfers between devices  32 us (47%)
  starting transfers between devices  21.7 us (32%)
  Pallas kernels  10.9 us (16%)
  local copies, waits for them, and re-layouts  1.86 us (3%)
  between operations  1.45 us (2%)
    ppermute x10, waiting for transfers between devices, swap_with(): lax.ppermute(x, ('tile', 'pos'), [(i, i ^ mask) for i in range(devices)])  18.2 us
    ppermute x9, waiting for transfers between devices, from_behind(): return lax.ppermute(block, 'tile', [(source(i), i) for i in range(tiles)])  12.6 us
    ppermute x10, starting transfers between devices, swap_with(): lax.ppermute(x, ('tile', 'pos'), [(i, i ^ mask) for i in range(devices)])  9.41 us
    pallas_call x10, Pallas kernels, run(): pl.pallas_call(body, out_shape=sum(outs, []), in_specs=sum(specs, []) + [...  9.21 us
    ppermute x9, starting transfers between devices, from_behind(): return lax.ppermute(block, 'tile', [(source(i), i) for i in range(tiles)])  8.11 us
    ppermute x2, starting transfers between devices, over_owners(): return lax.ppermute(part, 'pos', [(0, 1), (1, 0)])  2.69 us
    pallas_call x2, Pallas kernels, updated(): pl.pallas_call(lambda *refs: update_kernel(layer, *refs), out_shape=[like...  1.65 us
    ppermute x1, starting transfers between devices, shards(): sent = lax.ppermute(sent, 'pos', [(i, 1 - i) for i in range(2)])  1.52 us
  transfers between devices with their start and end apart: 22, of which 11 were waited for; matrix products, arithmetic and copies ran while one was open for 0% of the time, Pallas kernels for 8%

profile of v8, /device:TPU:0, one launch (start us, length us, event | category | flops | bytes accessed | tf_op | source)
XLA Modules:
  0.0 67.9 jit_solution(2900756413261925100)
XLA Ops:
  0.6 1.2 %slice_bitcast_fusion = (bf16[2,256,256]{2,1,0:T(8,128)(2,1)S(1)}, bf16[2,256,256]{2,1,0:T(8,128)(2,1)S(1)}) fusion(bf16[1,2,2,256,256]{4,3,2,1,0:T(8,128)(2,1)} %param.7), kind=kLoop, calls=%fused_computation | loop fusion | bytes 1048576 | tf_op jit(solution)/shard_map/squeeze | solution.py:430
  1.8 0.0 copy-start.1
  1.8 5.1 %collective-permute-start.4 = (bf16[2,256,256]{2,1,0:T(8,128)(2,1)S(1)}, bf16[2,256,256]{2,1,0:T(8,128)(2,1)S(1)}, u32[]{:S(2)}, u32[]{:S(2)}) collective-permute-start(bf16[2,256,256]{2,1,0:T(8,128)(2,1)S(1)} %get-tuple-element.65.refs_4_.refs_2_.refs_0_), channel_id=1, source_target_pairs={{8,0},{10,2},{12,4},{14,6},{16,8},{18,10},{20,12},{22,14},{24,16},... | collective-permute-start | bytes 786440 | tf_op jit(solution)/shard_map/ppermute | solution.py:29
  6.9 0.7 collective-permute-start.1
  8.2 0.0 copy-start.3
  8.3 0.7 copy-done.3
  8.9 0.6 shard_map.86
  9.5 0.5 collective-permute-start.2
  10.0 3.6 %collective-permute-done.4.refs_4_ = bf16[2,256,256]{2,1,0:T(8,128)(2,1)S(1)} collective-permute-done((bf16[2,256,256]{2,1,0:T(8,128)(2,1)S(1)}, bf16[2,256,256]{2,1,0:T(8,128)(2,1)S(1)}, u32[]{:S(2)}, u32[]{:S(2)}) %collective-permute-start.4) | collective-permute-done | bytes 262176 | tf_op jit(solution)/shard_map/ppermute | solution.py:29
  13.7 1.5 %collective-permute-start = (bf16[272,256]{1,0:T(8,128)(2,1)S(1)}, bf16[272,256]{1,0:T(8,128)(2,1)S(1)}, u32[]{:S(2)}, u32[]{:S(2)}) collective-permute-start(bf16[272,256]{1,0:T(8,128)(2,1)S(1)} %get-tuple-element.34), channel_id=1, source_target_pairs={{0,1},{1,0},{2,3},{3,2},{4,5},{5,4},{6,7},{7,6},{8,9},{9,8},{10,11... | collective-permute-start | bytes 417800 | tf_op jit(solution)/shard_map/ppermute | solution.py:452
  15.2 2.9 %collective-permute-done.2.refs_4_ = bf16[2,256,256]{2,1,0:T(8,128)(2,1)S(1)} collective-permute-done((bf16[2,256,256]{2,1,0:T(8,128)(2,1)S(1)}, bf16[2,256,256]{2,1,0:T(8,128)(2,1)S(1)}, u32[]{:S(2)}, u32[]{:S(2)}) %collective-permute-start.2) | collective-permute-done | bytes 262176 | tf_op jit(solution)/shard_map/ppermute | solution.py:29
  18.1 0.3 collective-permute-start.3
  18.5 0.1 shard_map.87
  18.6 1.2 %collective-permute-done.refs_1_.refs_3_ = bf16[272,256]{1,0:T(8,128)(2,1)S(1)} collective-permute-done((bf16[272,256]{1,0:T(8,128)(2,1)S(1)}, bf16[272,256]{1,0:T(8,128)(2,1)S(1)}, u32[]{:S(2)}, u32[]{:S(2)}) %collective-permute-start) | collective-permute-done | bytes 139296 | tf_op jit(solution)/shard_map/ppermute | solution.py:452
  19.7 1.8 %shard_map.88 = (bf16[2,256,256]{2,1,0:T(8,128)(2,1)S(1)}, f32[2,256,512]{2,1,0:T(8,128)S(1)}) custom-call(bf16[272,256]{1,0:T(8,128)(2,1)S(1)} %get-tuple-element.33.refs_0_.refs_2_, bf16[272,256]{1,0:T(8,128)(2,1)S(1)} %collective-permute-done.refs_1_.refs_3_, bf16[2,256,256]{2,1,0:T(8,128)(2,1)S(1)} %get-tuple-element.65.refs_4_.refs_2_.refs_0_, ...), custom_call_target="tpu_custom_call" | custom-call | flops 1500000000 | bytes 4472832 | tf_op jit(solution)/shard_map/pallas_call | solution.py:282
  21.5 0.8 %collective-permute-done.3.refs_5_ = bf16[2,256,256]{2,1,0:T(8,128)(2,1)S(1)} collective-permute-done((bf16[2,256,256]{2,1,0:T(8,128)(2,1)S(1)}, bf16[2,256,256]{2,1,0:T(8,128)(2,1)S(1)}, u32[]{:S(2)}, u32[]{:S(2)}) %collective-permute-start.3) | collective-permute-done | bytes 262176 | tf_op jit(solution)/shard_map/ppermute | solution.py:29
  22.4 4.3 %shard_map.89 = (bf16[2,256,256]{2,1,0:T(8,128)(2,1)S(1)}, bf16[2,256,256]{2,1,0:T(8,128)(2,1)S(1)}, bf16[528,256]{1,0:T(8,128)(2,1)S(1)}, bf16[2,256,256]{2,1,0...) custom-call(bf16[272,256]{1,0:T(8,128)(2,1)S(1)} %get-tuple-element.33.refs_0_.refs_2_, ...), custom_call_target="tpu_custom_call" | custom-call | flops 4000000000 | bytes 6578176 | tf_op jit(solution)/shard_map/pallas_call | solution.py:282
  26.6 1.5 %collective-permute-start.6 = (bf16[256,512]{1,0:T(8,128)(2,1)S(1)}, bf16[256,512]{1,0:T(8,128)(2,1)S(1)}, u32[]{:S(2)}, u32[]{:S(2)}) collective-permute-start(bf16[256,512]{1,0:T(8,128)(2,1)S(1)} %get-tuple-element.41), channel_id=1, source_target_pairs={{0,2},{1,3},{2,0},{3,1},{4,6},{5,7},{6,4},{7,5},{8,10},{9,11},{10,... | collective-permute-start | bytes 786440 | tf_op jit(solution)/shard_map/ppermute | solution.py:388
  28.1 0.5 collective-permute-start.10
  28.6 0.7 %collective-permute-done.6.refs_1_ = bf16[256,512]{1,0:T(8,128)(2,1)S(1)} collective-permute-done((bf16[256,512]{1,0:T(8,128)(2,1)S(1)}, bf16[256,512]{1,0:T(8,128)(2,1)S(1)}, u32[]{:S(2)}, u32[]{:S(2)}) %collective-permute-start.6) | collective-permute-done | bytes 262176 | tf_op jit(solution)/shard_map/ppermute | solution.py:388
  29.3 0.8 %shard_map.90 = (f32[64,512]{1,0:T(8,128)S(1)}, bf16[64,512]{1,0:T(8,128)(2,1)S(1)}, bf16[64,512]{1,0:T(8,128)(2,1)S(1)}, bf16[64,512]{1,0:T(8,128)(2,1)S(1)}, b...) custom-call(bf16[256,512]{1,0:T(8,128)(2,1)S(1)} %get-tuple-element.40.refs_0_, ...), custom_call_target="tpu_custom_call" | custom-call | flops 1000000 | bytes 2187264 | tf_op jit(solution)/shard_map/pallas_call | solution.py:282
  30.1 1.6 %collective-permute-start.7 = (bf16[64,512]{1,0:T(8,128)(2,1)S(1)}, bf16[64,512]{1,0:T(8,128)(2,1)S(1)}, u32[]{:S(2)}, u32[]{:S(2)}) collective-permute-start(bf16[64,512]{1,0:T(8,128)(2,1)S(1)} %get-tuple-element.44), channel_id=1, source_target_pairs={{0,1},{1,0},{2,3},{3,2},{4,5},{5,4},{6,7},{7,6},{8,9},{9,8},{10,11... | collective-permute-start | bytes 196616 | tf_op jit(solution)/shard_map/ppermute | solution.py:388
  31.7 0.9 %collective-permute-start.8 = (bf16[64,512]{1,0:T(8,128)(2,1)S(1)}, bf16[64,512]{1,0:T(8,128)(2,1)S(1)}, u32[]{:S(2)}, u32[]{:S(2)}) collective-permute-start(bf16[64,512]{1,0:T(8,128)(2,1)S(1)} %get-tuple-element.45), channel_id=1, source_target_pairs={{0,4},{1,5},{2,6},{3,7},{4,0},{5,1},{6,2},{7,3},{8,12},{9,13},{10,... | collective-permute-start | bytes 196616 | tf_op jit(solution)/shard_map/ppermute | solution.py:388
  32.5 1.1 %collective-permute-start.9 = (bf16[64,512]{1,0:T(8,128)(2,1)S(1)}, bf16[64,512]{1,0:T(8,128)(2,1)S(1)}, u32[]{:S(2)}, u32[]{:S(2)}) collective-permute-start(bf16[64,512]{1,0:T(8,128)(2,1)S(1)} %get-tuple-element.46), channel_id=1, source_target_pairs={{0,5},{1,4},{2,7},{3,6},{4,1},{5,0},{6,3},{7,2},{8,13},{9,12},{10,... | collective-permute-start | bytes 196616 | tf_op jit(solution)/shard_map/ppermute | solution.py:388
  33.6 0.9 %collective-permute-start.12 = (bf16[528,256]{1,0:T(8,128)(2,1)S(1)}, bf16[528,256]{1,0:T(8,128)(2,1)S(1)}, u32[]{:S(2)}, u32[]{:S(2)}) collective-permute-start(bf16[528,256]{1,0:T(8,128)(2,1)S(1)} %get-tuple-element.51), channel_id=1, source_target_pairs={{24,0},{26,2},{28,4},{30,6},{0,8},{2,10},{4,12},{6,14},{8,16},{10,... | collective-permute-start | bytes 811016 | tf_op jit(solution)/shard_map/ppermute | solution.py:29
  34.5 5.2 %collective-permute-done.10.refs_5_ = bf16[528,256]{1,0:T(8,128)(2,1)S(1)} collective-permute-done((bf16[528,256]{1,0:T(8,128)(2,1)S(1)}, bf16[528,256]{1,0:T(8,128)(2,1)S(1)}, u32[]{:S(2)}, u32[]{:S(2)}) %collective-permute-start.10) | collective-permute-done | bytes 270368 | tf_op jit(solution)/shard_map/ppermute | solution.py:29
  39.7 0.1 shard_map.91
  39.8 0.1 collective-permute-start.13
  39.9 0.1 collective-permute-start.11
  40.0 6.4 %collective-permute-done.11.refs_1_ = bf16[64,512]{1,0:T(8,128)(2,1)S(1)} collective-permute-done((bf16[64,512]{1,0:T(8,128)(2,1)S(1)}, bf16[64,512]{1,0:T(8,128)(2,1)S(1)}, u32[]{:S(2)}, u32[]{:S(2)}) %collective-permute-start.11) | collective-permute-done | bytes 65568 | tf_op jit(solution)/shard_map/ppermute | solution.py:388
  46.3 0.2 shard_map.92
  46.5 0.1 collective-permute-start.15
  46.7 0.7 %collective-permute-start.14 = (bf16[64,512]{1,0:T(8,128)(2,1)S(1)}, bf16[64,512]{1,0:T(8,128)(2,1)S(1)}, u32[]{:S(2)}, u32[]{:S(2)}) collective-permute-start(bf16[64,512]{1,0:T(8,128)(2,1)S(1)} %get-tuple-element.54.refs_0_), channel_id=1, source_target_pairs={{0,16},{1,17},{2,18},{3,19},{4,20},{5,21},{6,22},{7,23},{8,24},{9,... | collective-permute-start | bytes 196616 | tf_op jit(solution)/shard_map/ppermute | solution.py:388
  47.4 1.4 %collective-permute-start.17 = (bf16[2,256,256]{2,1,0:T(8,128)(2,1)S(1)}, bf16[2,256,256]{2,1,0:T(8,128)(2,1)S(1)}, u32[]{:S(2)}, u32[]{:S(2)}) collective-permute-start(bf16[2,256,256]{2,1,0:T(8,128)(2,1)S(1)} %get-tuple-element.58.refs_1_), channel_id=1, source_target_pairs={{0,1},{1,0},{2,3},{3,2},{4,5},{5,4},{6,7},{7,6},{8,9},{9,8},{10,11... | collective-permute-start | bytes 786440 | tf_op jit(solution)/shard_map/ppermute | solution.py:481
  48.8 4.2 %collective-permute-done.14.refs_1_ = bf16[64,512]{1,0:T(8,128)(2,1)S(1)} collective-permute-done((bf16[64,512]{1,0:T(8,128)(2,1)S(1)}, bf16[64,512]{1,0:T(8,128)(2,1)S(1)}, u32[]{:S(2)}, u32[]{:S(2)}) %collective-permute-start.14) | collective-permute-done | bytes 65568 | tf_op jit(solution)/shard_map/ppermute | solution.py:388
  52.9 0.1 shard_map.93
  53.1 1.3 %collective-permute-start.16 = (bf16[2,256,256]{2,1,0:T(8,128)(2,1)S(1)}, bf16[2,256,256]{2,1,0:T(8,128)(2,1)S(1)}, u32[]{:S(2)}, u32[]{:S(2)}) collective-permute-start(bf16[2,256,256]{2,1,0:T(8,128)(2,1)S(1)} %get-tuple-element.57.refs_1_), channel_id=1, source_target_pairs={{0,1},{1,0},{2,3},{3,2},{4,5},{5,4},{6,7},{7,6},{8,9},{9,8},{10,11... | collective-permute-start | bytes 786440 | tf_op jit(solution)/shard_map/ppermute | solution.py:481
  54.4 1.0 %collective-permute-start.20 = (bf16[64,512]{1,0:T(8,128)(2,1)S(1)}, bf16[64,512]{1,0:T(8,128)(2,1)S(1)}, u32[]{:S(2)}, u32[]{:S(2)}) collective-permute-start(bf16[64,512]{1,0:T(8,128)(2,1)S(1)} %get-tuple-element.61.refs_0_), channel_id=1, source_target_pairs={{0,5},{1,4},{2,7},{3,6},{4,1},{5,0},{6,3},{7,2},{8,13},{9,12},{10,... | collective-permute-start | bytes 196616 | tf_op jit(solution)/shard_map/ppermute | solution.py:388
  55.4 1.2 %collective-permute-start.19 = (bf16[64,512]{1,0:T(8,128)(2,1)S(1)}, bf16[64,512]{1,0:T(8,128)(2,1)S(1)}, u32[]{:S(2)}, u32[]{:S(2)}) collective-permute-start(bf16[64,512]{1,0:T(8,128)(2,1)S(1)} %get-tuple-element.61.refs_0_), channel_id=1, source_target_pairs={{0,4},{1,5},{2,6},{3,7},{4,0},{5,1},{6,2},{7,3},{8,12},{9,13},{10,... | collective-permute-start | bytes 196616 | tf_op jit(solution)/shard_map/ppermute | solution.py:388
  56.6 1.3 %collective-permute-start.18 = (bf16[64,512]{1,0:T(8,128)(2,1)S(1)}, bf16[64,512]{1,0:T(8,128)(2,1)S(1)}, u32[]{:S(2)}, u32[]{:S(2)}) collective-permute-start(bf16[64,512]{1,0:T(8,128)(2,1)S(1)} %get-tuple-element.61.refs_0_), channel_id=1, source_target_pairs={{0,1},{1,0},{2,3},{3,2},{4,5},{5,4},{6,7},{7,6},{8,9},{9,8},{10,11... | collective-permute-start | bytes 196616 | tf_op jit(solution)/shard_map/ppermute | solution.py:388
  57.9 0.8 %shard_map.94 = (bf16[1,2,2,256,256]{4,3,2,1,0:T(8,128)(2,1)}, f32[8,128]{1,0:T(8,128)S(1)}) custom-call(bf16[2,256,256]{2,1,0:T(8,128)(2,1)S(1)} %get-tuple-element.35.refs_2_.refs_0_, bf16[2,256,256]{2,1,0:T(8,128)(2,1)S(1)} %get-tuple-element.58.refs_1_, bf16[2,256,256]{2,1,0:T(8,128)(2,1)S(1)} %collective-permute-done.17.refs_2_), custom_call_target="tpu_custom_call" | custom-call | flops 131072 | bytes 1048576 | tf_op jit(solution)/shard_map/pallas_call | solution.py:299
  58.7 1.1 %collective-permute-done.20.refs_3_ = bf16[64,512]{1,0:T(8,128)(2,1)S(1)} collective-permute-done((bf16[64,512]{1,0:T(8,128)(2,1)S(1)}, bf16[64,512]{1,0:T(8,128)(2,1)S(1)}, u32[]{:S(2)}, u32[]{:S(2)}) %collective-permute-start.20) | collective-permute-done | bytes 65568 | tf_op jit(solution)/shard_map/ppermute | solution.py:388
  59.9 5.1 %collective-permute-done.18.refs_1_ = bf16[64,512]{1,0:T(8,128)(2,1)S(1)} collective-permute-done((bf16[64,512]{1,0:T(8,128)(2,1)S(1)}, bf16[64,512]{1,0:T(8,128)(2,1)S(1)}, u32[]{:S(2)}, u32[]{:S(2)}) %collective-permute-start.18) | collective-permute-done | bytes 65568 | tf_op jit(solution)/shard_map/ppermute | solution.py:388
  65.0 0.1 shard_map.96.refs_0_
  65.1 0.1 collective-permute-start.21
  65.2 0.8 %shard_map.95 = (bf16[1,2,2,256,256]{4,3,2,1,0:T(8,128)(2,1)}, f32[8,128]{1,0:T(8,128)S(1)}) custom-call(bf16[2,256,256]{2,1,0:T(8,128)(2,1)S(1)} %get-tuple-element.65.refs_4_.refs_2_.refs_0_, bf16[2,256,256]{2,1,0:T(8,128)(2,1)S(1)} %get-tuple-element.57.refs_1_, ...), custom_call_target="tpu_custom_call", output_to_operand_aliasing={{0}: (3, {})} | custom-call | flops 3000131072 | bytes 1048576 | tf_op jit(solution)/shard_map/pallas_call | solution.py:299
  66.0 0.7 collective-permute-done.21.refs_1_
  66.7 1.2 %shard_map.97 = f32[2048,128]{1,0:T(8,128)} custom-call(bf16[256,512]{1,0:T(8,128)(2,1)S(1)} %shard_map.96.refs_0_, bf16[256,512]{1,0:T(8,128)(2,1)S(1)} %collective-permute-done.21.refs_1_, f32[2048,128]{1,0:T(8,128)S(1)} %bitcast.16, f32[8,128]{1,0:T(8,128)S(1)} %get-tuple-element.63.refs_3_), custom_call_target="tpu_custom_call" | custom-call | flops 1000000 | bytes 2621440 | tf_op jit(solution)/shard_map/pallas_call | solution.py:282
  (19 shorter events, 0.0 us)
Async XLA Ops:
  0.6 7.6 %copy-start.2 = (bf16[1,1,2,256,256]{4,3,2,1,0:T(8,128)(2,1)S(1)}, bf16[1,1,2,256,256]{4,3,2,1,0:T(8,128)(2,1)}, u32[]{:S(2)}) copy-start(bf16[1,1,2,256,256]{4,3,2,1,0:T(8,128)(2,1)} %refs_3_.1) | copy-start | bytes 786436
  0.6 17.8 %copy-start = (f32[2,256,2,256]{3,2,1,0:T(2,128)S(1)}, f32[2,256,2,256]{3,2,1,0:T(2,128)}, u32[]{:S(2)}) copy-start(f32[2,256,2,256]{3,2,1,0:T(2,128)} %param.8) | copy-start | bytes 3145732
  1.8 16.7 %copy-start.1 = (bf16[512,512]{1,0:T(8,128)(2,1)S(1)}, bf16[512,512]{1,0:T(8,128)(2,1)}, u32[]{:S(2)}) copy-start(bf16[512,512]{1,0:T(8,128)(2,1)} %constant.10.refs_1_) | copy-start | bytes 1572868
  1.8 11.8 %collective-permute-start.4 = (bf16[2,256,256]{2,1,0:T(8,128)(2,1)S(1)}, bf16[2,256,256]{2,1,0:T(8,128)(2,1)S(1)}, u32[]{:S(2)}, u32[]{:S(2)}) collective-permute-start(bf16[2,256,256]{2,1,0:T(8,128)(2,1)S(1)} %get-tuple-element.65.refs_4_.refs_2_.refs_0_), channel_id=1, source_target_pairs={{8,0},{10,2},{12,4},{14,6},{16,8},{18,10},{20,12},{22,14},{24,16},... | collective-permute-start | bytes 786440 | tf_op jit(solution)/shard_map/ppermute | solution.py:29
  6.9 12.8 %collective-permute-start.1 = (bf16[2,2,256,256]{3,2,1,0:T(8,128)(2,1)}, bf16[2,2,256,256]{3,2,1,0:T(8,128)(2,1)S(1)}, u32[]{:S(2)}, u32[]{:S(2)}) collective-permute-start(bf16[2,2,256,256]{3,2,1,0:T(8,128)(2,1)} %bitcast.18), channel_id=1, source_target_pairs={{2,0},{4,2},{6,4},{0,6},{10,8},{12,10},{14,12},{8,14},{18,16},{20,... | collective-permute-start | bytes 1572872 | tf_op jit(solution)/shard_map/ppermute | solution.py:29
  8.2 0.7 %copy-start.3 = (s32[1,1,2,2]{3,2,1,0:T(2,128)S(1)}, s32[1,1,2,2]{3,2,1,0:T(2,128)}, u32[]{:S(2)}) copy-start(s32[1,1,2,2]{3,2,1,0:T(2,128)} %refs_0_.1) | copy-start | bytes 52
  9.5 8.6 %collective-permute-start.2 = (bf16[2,256,256]{2,1,0:T(8,128)(2,1)S(1)}, bf16[2,256,256]{2,1,0:T(8,128)(2,1)S(1)}, u32[]{:S(2)}, u32[]{:S(2)}) collective-permute-start(bf16[2,256,256]{2,1,0:T(8,128)(2,1)S(1)} %get-tuple-element.35.refs_2_.refs_0_), channel_id=1, source_target_pairs={{8,0},{10,2},{12,4},{14,6},{16,8},{18,10},{20,12},{22,14},{24,16},... | collective-permute-start | bytes 786440 | tf_op jit(solution)/shard_map/ppermute | solution.py:29
  13.6 6.1 %collective-permute-start.5 = (bf16[2,256,256]{2,1,0:T(8,128)(2,1)S(1)}, bf16[2,256,256]{2,1,0:T(8,128)(2,1)S(1)}, u32[]{:S(2)}, u32[]{:S(2)}) collective-permute-start(bf16[2,256,256]{2,1,0:T(8,128)(2,1)S(1)} %collective-permute-done.4.refs_4_), channel_id=1, source_target_pairs={{2,0},{4,2},{6,4},{0,6},{10,8},{12,10},{14,12},{8,14},{18,16},{20,... | collective-permute-start | bytes 786440 | tf_op jit(solution)/shard_map/ppermute | solution.py:29
  13.7 6.1 %collective-permute-start = (bf16[272,256]{1,0:T(8,128)(2,1)S(1)}, bf16[272,256]{1,0:T(8,128)(2,1)S(1)}, u32[]{:S(2)}, u32[]{:S(2)}) collective-permute-start(bf16[272,256]{1,0:T(8,128)(2,1)S(1)} %get-tuple-element.34), channel_id=1, source_target_pairs={{0,1},{1,0},{2,3},{3,2},{4,5},{5,4},{6,7},{7,6},{8,9},{9,8},{10,11... | collective-permute-start | bytes 417800 | tf_op jit(solution)/shard_map/ppermute | solution.py:452
  18.1 4.2 %collective-permute-start.3 = (bf16[2,256,256]{2,1,0:T(8,128)(2,1)S(1)}, bf16[2,256,256]{2,1,0:T(8,128)(2,1)S(1)}, u32[]{:S(2)}, u32[]{:S(2)}) collective-permute-start(bf16[2,256,256]{2,1,0:T(8,128)(2,1)S(1)} %collective-permute-done.2.refs_4_), channel_id=1, source_target_pairs={{2,0},{4,2},{6,4},{0,6},{10,8},{12,10},{14,12},{8,14},{18,16},{20,... | collective-permute-start | bytes 786440 | tf_op jit(solution)/shard_map/ppermute | solution.py:29
  19.7 2.6 %copy-start.4 = (bf16[512,512]{1,0:T(8,128)(2,1)S(1)}, bf16[512,512]{1,0:T(8,128)(2,1)}, u32[]{:S(2)}) copy-start(bf16[512,512]{1,0:T(8,128)(2,1)} %constant.11.refs_10_) | copy-start | bytes 1572868
  26.6 2.6 %collective-permute-start.6 = (bf16[256,512]{1,0:T(8,128)(2,1)S(1)}, bf16[256,512]{1,0:T(8,128)(2,1)S(1)}, u32[]{:S(2)}, u32[]{:S(2)}) collective-permute-start(bf16[256,512]{1,0:T(8,128)(2,1)S(1)} %get-tuple-element.41), channel_id=1, source_target_pairs={{0,2},{1,3},{2,0},{3,1},{4,6},{5,7},{6,4},{7,5},{8,10},{9,11},{10,... | collective-permute-start | bytes 786440 | tf_op jit(solution)/shard_map/ppermute | solution.py:388
  28.1 11.6 %collective-permute-start.10 = (bf16[528,256]{1,0:T(8,128)(2,1)S(1)}, bf16[528,256]{1,0:T(8,128)(2,1)S(1)}, u32[]{:S(2)}, u32[]{:S(2)}) collective-permute-start(bf16[528,256]{1,0:T(8,128)(2,1)S(1)} %get-tuple-element.48), channel_id=1, source_target_pairs={{24,0},{26,2},{28,4},{30,6},{0,8},{2,10},{4,12},{6,14},{8,16},{10,... | collective-permute-start | bytes 811016 | tf_op jit(solution)/shard_map/ppermute | solution.py:29
  30.1 9.6 %collective-permute-start.7 = (bf16[64,512]{1,0:T(8,128)(2,1)S(1)}, bf16[64,512]{1,0:T(8,128)(2,1)S(1)}, u32[]{:S(2)}, u32[]{:S(2)}) collective-permute-start(bf16[64,512]{1,0:T(8,128)(2,1)S(1)} %get-tuple-element.44), channel_id=1, source_target_pairs={{0,1},{1,0},{2,3},{3,2},{4,5},{5,4},{6,7},{7,6},{8,9},{9,8},{10,11... | collective-permute-start | bytes 196616 | tf_op jit(solution)/shard_map/ppermute | solution.py:388
  31.7 8.0 %collective-permute-start.8 = (bf16[64,512]{1,0:T(8,128)(2,1)S(1)}, bf16[64,512]{1,0:T(8,128)(2,1)S(1)}, u32[]{:S(2)}, u32[]{:S(2)}) collective-permute-start(bf16[64,512]{1,0:T(8,128)(2,1)S(1)} %get-tuple-element.45), channel_id=1, source_target_pairs={{0,4},{1,5},{2,6},{3,7},{4,0},{5,1},{6,2},{7,3},{8,12},{9,13},{10,... | collective-permute-start | bytes 196616 | tf_op jit(solution)/shard_map/ppermute | solution.py:388
  32.5 7.1 %collective-permute-start.9 = (bf16[64,512]{1,0:T(8,128)(2,1)S(1)}, bf16[64,512]{1,0:T(8,128)(2,1)S(1)}, u32[]{:S(2)}, u32[]{:S(2)}) collective-permute-start(bf16[64,512]{1,0:T(8,128)(2,1)S(1)} %get-tuple-element.46), channel_id=1, source_target_pairs={{0,5},{1,4},{2,7},{3,6},{4,1},{5,0},{6,3},{7,2},{8,13},{9,12},{10,... | collective-permute-start | bytes 196616 | tf_op jit(solution)/shard_map/ppermute | solution.py:388
  33.6 12.7 %collective-permute-start.12 = (bf16[528,256]{1,0:T(8,128)(2,1)S(1)}, bf16[528,256]{1,0:T(8,128)(2,1)S(1)}, u32[]{:S(2)}, u32[]{:S(2)}) collective-permute-start(bf16[528,256]{1,0:T(8,128)(2,1)S(1)} %get-tuple-element.51), channel_id=1, source_target_pairs={{24,0},{26,2},{28,4},{30,6},{0,8},{2,10},{4,12},{6,14},{8,16},{10,... | collective-permute-start | bytes 811016 | tf_op jit(solution)/shard_map/ppermute | solution.py:29
  39.8 6.5 %collective-permute-start.13 = (bf16[2,256,256]{2,1,0:T(8,128)(2,1)S(1)}, bf16[2,256,256]{2,1,0:T(8,128)(2,1)S(1)}, u32[]{:S(2)}, u32[]{:S(2)}) collective-permute-start(bf16[2,256,256]{2,1,0:T(8,128)(2,1)S(1)} %get-tuple-element.53), channel_id=1, source_target_pairs={{6,0},{0,2},{2,4},{4,6},{14,8},{8,10},{10,12},{12,14},{22,16},{16,... | collective-permute-start | bytes 786440 | tf_op jit(solution)/shard_map/ppermute | solution.py:29
  39.9 6.4 %collective-permute-start.11 = (bf16[64,512]{1,0:T(8,128)(2,1)S(1)}, bf16[64,512]{1,0:T(8,128)(2,1)S(1)}, u32[]{:S(2)}, u32[]{:S(2)}) collective-permute-start(bf16[64,512]{1,0:T(8,128)(2,1)S(1)} %get-tuple-element.49.refs_0_), channel_id=1, source_target_pairs={{0,8},{1,9},{2,10},{3,11},{4,12},{5,13},{6,14},{7,15},{8,0},{9,1},... | collective-permute-start | bytes 196616 | tf_op jit(solution)/shard_map/ppermute | solution.py:388
  46.5 6.4 %collective-permute-start.15 = (bf16[2,256,256]{2,1,0:T(8,128)(2,1)S(1)}, bf16[2,256,256]{2,1,0:T(8,128)(2,1)S(1)}, u32[]{:S(2)}, u32[]{:S(2)}) collective-permute-start(bf16[2,256,256]{2,1,0:T(8,128)(2,1)S(1)} %get-tuple-element.56), channel_id=1, source_target_pairs={{6,0},{0,2},{2,4},{4,6},{14,8},{8,10},{10,12},{12,14},{22,16},{16,... | collective-permute-start | bytes 786440 | tf_op jit(solution)/shard_map/ppermute | solution.py:29
  46.7 6.3 %collective-permute-start.14 = (bf16[64,512]{1,0:T(8,128)(2,1)S(1)}, bf16[64,512]{1,0:T(8,128)(2,1)S(1)}, u32[]{:S(2)}, u32[]{:S(2)}) collective-permute-start(bf16[64,512]{1,0:T(8,128)(2,1)S(1)} %get-tuple-element.54.refs_0_), channel_id=1, source_target_pairs={{0,16},{1,17},{2,18},{3,19},{4,20},{5,21},{6,22},{7,23},{8,24},{9,... | collective-permute-start | bytes 196616 | tf_op jit(solution)/shard_map/ppermute | solution.py:388
  47.4 10.5 %collective-permute-start.17 = (bf16[2,256,256]{2,1,0:T(8,128)(2,1)S(1)}, bf16[2,256,256]{2,1,0:T(8,128)(2,1)S(1)}, u32[]{:S(2)}, u32[]{:S(2)}) collective-permute-start(bf16[2,256,256]{2,1,0:T(8,128)(2,1)S(1)} %get-tuple-element.58.refs_1_), channel_id=1, source_target_pairs={{0,1},{1,0},{2,3},{3,2},{4,5},{5,4},{6,7},{7,6},{8,9},{9,8},{10,11... | collective-permute-start | bytes 786440 | tf_op jit(solution)/shard_map/ppermute | solution.py:481
  53.1 12.1 %collective-permute-start.16 = (bf16[2,256,256]{2,1,0:T(8,128)(2,1)S(1)}, bf16[2,256,256]{2,1,0:T(8,128)(2,1)S(1)}, u32[]{:S(2)}, u32[]{:S(2)}) collective-permute-start(bf16[2,256,256]{2,1,0:T(8,128)(2,1)S(1)} %get-tuple-element.57.refs_1_), channel_id=1, source_target_pairs={{0,1},{1,0},{2,3},{3,2},{4,5},{5,4},{6,7},{7,6},{8,9},{9,8},{10,11... | collective-permute-start | bytes 786440 | tf_op jit(solution)/shard_map/ppermute | solution.py:481
  54.4 5.4 %collective-permute-start.20 = (bf16[64,512]{1,0:T(8,128)(2,1)S(1)}, bf16[64,512]{1,0:T(8,128)(2,1)S(1)}, u32[]{:S(2)}, u32[]{:S(2)}) collective-permute-start(bf16[64,512]{1,0:T(8,128)(2,1)S(1)} %get-tuple-element.61.refs_0_), channel_id=1, source_target_pairs={{0,5},{1,4},{2,7},{3,6},{4,1},{5,0},{6,3},{7,2},{8,13},{9,12},{10,... | collective-permute-start | bytes 196616 | tf_op jit(solution)/shard_map/ppermute | solution.py:388
  55.4 4.5 %collective-permute-start.19 = (bf16[64,512]{1,0:T(8,128)(2,1)S(1)}, bf16[64,512]{1,0:T(8,128)(2,1)S(1)}, u32[]{:S(2)}, u32[]{:S(2)}) collective-permute-start(bf16[64,512]{1,0:T(8,128)(2,1)S(1)} %get-tuple-element.61.refs_0_), channel_id=1, source_target_pairs={{0,4},{1,5},{2,6},{3,7},{4,0},{5,1},{6,2},{7,3},{8,12},{9,13},{10,... | collective-permute-start | bytes 196616 | tf_op jit(solution)/shard_map/ppermute | solution.py:388
  56.6 8.4 %collective-permute-start.18 = (bf16[64,512]{1,0:T(8,128)(2,1)S(1)}, bf16[64,512]{1,0:T(8,128)(2,1)S(1)}, u32[]{:S(2)}, u32[]{:S(2)}) collective-permute-start(bf16[64,512]{1,0:T(8,128)(2,1)S(1)} %get-tuple-element.61.refs_0_), channel_id=1, source_target_pairs={{0,1},{1,0},{2,3},{3,2},{4,5},{5,4},{6,7},{7,6},{8,9},{9,8},{10,11... | collective-permute-start | bytes 196616 | tf_op jit(solution)/shard_map/ppermute | solution.py:388
  65.1 1.6 %collective-permute-start.21 = (bf16[256,512]{1,0:T(8,128)(2,1)S(1)}, bf16[256,512]{1,0:T(8,128)(2,1)S(1)}, u32[]{:S(2)}, u32[]{:S(2)}) collective-permute-start(bf16[256,512]{1,0:T(8,128)(2,1)S(1)} %shard_map.96.refs_0_), channel_id=1, source_target_pairs={{0,2},{1,3},{2,0},{3,1},{4,6},{5,7},{6,4},{7,5},{8,10},{9,11},{10,... | collective-permute-start | bytes 786440 | tf_op jit(solution)/shard_map/ppermute | solution.py:388

commit v9 on v8

--- a/solution.py
+++ b/solution.py
@@ -14,6 +14,8 @@
 fresnel_coeff = 0.25
 object_rate = 0.05
 probe_rate = 0.15
+
+LATE = [5_000_000_000] * 8 + [0, 0]
 
 f32 = jnp.float32
 bf16 = jnp.bfloat16
@@ -84,10 +86,13 @@
     return dot(rows, shifts[1])
 
 
-def transform(table_ref, wave_re, wave_im):
-    n = wave_re.shape[0]
+def stacked(wave_re, wave_im):
+    return jnp.concatenate([wave_re.astype(bf16), wave_im.astype(bf16)], axis=0)
+
+
+def transform(table_ref, wave):
+    n = wave.shape[1]
     table = table_ref[...]
-    wave = jnp.concatenate([wave_re.astype(bf16), wave_im.astype(bf16)], axis=0)
     first = dot(table, wave)
     first = jnp.concatenate([first[:n].astype(bf16), (-first[n:]).astype(bf16)], axis=1)
     out = dot(first, table)
@@ -139,9 +144,8 @@
     for mode in range(planes_ref.shape[2] // n):
         lanes = pl.ds(mode * n, n)
         p_re, p_im = planes_ref[0, :, lanes], planes_ref[1, :, lanes]
-        a_re, a_neg = transform(
-            prop_ref, p_re * near[0] - p_im * near[1], p_re * near[1] + p_im * near[0]
-        )
+        wave = stacked(p_re * near[0] - p_im * near[1], p_re * near[1] + p_im * near[0])
+        a_re, a_neg = transform(prop_ref, wave)
         arrive_ref[0, :, lanes] = a_re
         arrive_ref[1, :, lanes] = -a_neg
 
@@ -160,13 +164,12 @@
     down_ref[pl.ds(2 * n, 16), :] = edge.astype(f32).astype(bf16)
 
 
-def gradient_kernel(
-    mine_ref, sent_ref, own_ref, right_ref, below_ref, diag_ref, near_ref, arrive_ref,
-    planes_ref, prop_ref, dft_ref,
-    home_ref, next_ref, down_ref, grad_ref, keep_ref, give_ref, term_ref,
+def far_kernel(
+    mine_ref, sent_ref, own_ref, right_ref, below_ref, diag_ref, arrive_ref, dft_ref,
+    home_ref, next_ref, down_ref, waves_ref,
 ):
     n = own_ref.shape[1]
-    modes = planes_ref.shape[2] // n
+    modes = arrive_ref.shape[2] // n
     shifts = shift_tables(mine_ref, sent_ref)
     busy = shifts[5]
     tiles = (own_ref, right_ref.at[1], below_ref, diag_ref)
@@ -175,38 +178,41 @@
     for mode in range(modes):
         lanes = pl.ds(mode * n, n)
         a_re, a_im = arrive_ref[0, :, lanes], arrive_ref[1, :, lanes]
-        fields.append(
-            transform(dft_ref, far[0] * a_re - far[1] * a_im, far[0] * a_im + far[1] * a_re)
-        )
+        wave = stacked(far[0] * a_re - far[1] * a_im, far[0] * a_im + far[1] * a_re)
+        fields.append(transform(dft_ref, wave))
     intensity = sum(f_re * f_re + f_neg * f_neg for f_re, f_neg in fields)
     pattern = jnp.where(busy, mine_ref[:n, :].astype(f32), sent_ref[:n, :].astype(f32))
     residual = intensity - pattern
-    grad_far = [0.0, 0.0]
-    waves = []
+    grad = [0.0, 0.0]
     for mode in range(modes):
         lanes = pl.ds(mode * n, n)
         f_re, f_neg = fields[mode]
         a_re, a_im = arrive_ref[0, :, lanes], arrive_ref[1, :, lanes]
-        b_re, b_im = transform(dft_ref, f_re * residual, f_neg * residual)
-        grad_far[0] += a_re * b_re + a_im * b_im
-        grad_far[1] += a_re * b_im - a_im * b_re
-        waves.append((far[0] * b_re + far[1] * b_im, far[1] * b_re - far[0] * b_im))
-    grad_near = [0.0, 0.0]
+        b_re, b_im = transform(dft_ref, stacked(f_re * residual, f_neg * residual))
+        grad[0] += a_re * b_re + a_im * b_im
+        grad[1] += a_re * b_im - a_im * b_re
+        wave = stacked(far[0] * b_re + far[1] * b_im, far[1] * b_re - far[0] * b_im)
+        waves_ref[:, lanes] = wave
+    spread(shifts, grad, home_ref, next_ref, down_ref)
+
+
+def near_kernel(near_ref, planes_ref, waves_ref, prop_ref, grad_ref, keep_ref, give_ref, term_ref):
+    n = near_ref.shape[1]
+    grad = [0.0, 0.0]
     near = [near_ref[part].astype(f32) for part in range(2)]
-    for mode in range(modes):
+    for mode in range(planes_ref.shape[2] // n):
         lanes = pl.ds(mode * n, n)
-        b_re, b_im = transform(prop_ref, *waves[mode])
+        b_re, b_im = transform(prop_ref, waves_ref[:, lanes])
         p_re, p_im = planes_ref[0, :, lanes], planes_ref[1, :, lanes]
-        grad_near[0] += p_re * b_re + p_im * b_im
-        grad_near[1] += p_re * b_im - p_im * b_re
+        grad[0] += p_re * b_re + p_im * b_im
+        grad[1] += p_re * b_im - p_im * b_re
         term_ref[0, :, lanes] = (near[0] * b_re + near[1] * b_im).astype(bf16)
         term_ref[1, :, lanes] = (near[0] * b_im - near[1] * b_re).astype(bf16)
     core = place_of(core_group())
     keep_ref[...] = term_ref[core]
     give_ref[...] = term_ref[1 - core]
     for part in range(2):
-        grad_ref[part] = grad_near[part].astype(bf16)
-    spread(shifts, grad_far, home_ref, next_ref, down_ref)
+        grad_ref[part] = grad[part].astype(bf16)
 
 
 def spread_kernel(mine_ref, sent_ref, grad_ref, home_ref, next_ref, down_ref):
@@ -292,10 +298,10 @@
     return results[0] if len(jobs) == 1 else results
 
 
-def updated(layer, own, part, other, like, so_far=None, flops=0):
+def updated(layer, own, part, other, like, so_far=None, flops=0, after=()):
     vmem = pl.BlockSpec(memory_space=pltpu.VMEM)
     anywhere = pl.BlockSpec(memory_space=pl.ANY)
-    extra = [x for x in (so_far,) if x is not None]
+    extra = [x for x in (so_far,) if x is not None] + list(after)
     return pl.pallas_call(
         lambda *refs: update_kernel(layer, *refs),
         out_shape=[like, shape_of(f32, 8, 128)],
@@ -361,7 +367,8 @@
         out_ref[pl.ds(block * size, size), :] = blocks[block]
 
 
-def probe_kernel(step, modes, mine_ref, other_ref, probe_ref, out_ref):
+def probe_kernel(step, modes, mine_ref, other_ref, probe_ref, out_ref, token_ref):
+    token_ref[...] = jnp.zeros_like(token_ref)
     core = place_of(core_group())
     lane_tiles = 2
     n = mine_ref.shape[0]
@@ -465,14 +472,24 @@
     )
     half = shape_of(bf16, pixels, width)
     down = shape_of(bf16, 2 * pixels + 16, pixels)
-    home1, next1, down1, grad0, keep, give = run(
+    home1, next1, down1, waves = run(
         job(
-            gradient_kernel,
-            [tile, tile, down, tile, half, half],
-            [mine, sent, own1, right, below1, diag1, near, arrive, probe_planes, table, dft],
+            far_kernel,
+            [tile, tile, down, shape_of(bf16, 2 * pixels, width)],
+            [mine, sent, own1, right, below1, diag1, arrive, dft],
+        ),
+        flops=3_000_000_000,
+        limit=16,
+    )
+    above1 = from_behind(down1, 1, 0)
+    grad0, keep, give = run(
+        job(
+            near_kernel,
+            [tile, half, half],
+            [near, probe_planes, waves, table],
             scratch=[pltpu.VMEM((2, pixels, width), bf16)],
         ),
-        flops=4_000_000_000,
+        flops=1_500_000_000,
         limit=16,
     )
 
@@ -482,7 +499,6 @@
         return lax.psum(part.astype(f32), "pos") - part.astype(f32)
 
     core, groups = core_group(), exchange_groups()
-    above1 = from_behind(down1, 1, 0)
     arrived = [swap_with(give, core, 1)]
     side = [job(spread_kernel, [tile, tile, down], [mine, sent, grad0])]
     scattered = []
@@ -496,43 +512,51 @@
         keep, *gives = done
         arrived = [swap_with(x, group, at) for at, x in enumerate(gives, 1)]
         scattered.append(group)
-    (total,), (beside1,) = run(
-        added(keep, arrived), job(beside_kernel, [tile], [next1, above1])
+    first, second, *others = [[bit] for group in groups for bit in group]
+    (total,) = run(added(keep, arrived))
+    arrived = swapped(total, first)
+    (beside1,) = run(
+        job(beside_kernel, [tile], [next1, above1]), after=[total], flops=LATE[0]
     )
     left1 = from_behind(beside1, 0, 1)
-    first, second, *others = [[bit] for group in groups for bit in group]
-    (total,), (beside0,), (part1,) = run(
-        added(total, swapped(total, first)),
-        job(beside_kernel, [tile], [next0, above0]),
-        job(part_kernel, [tile], [home1, above1, left1]),
+    (total,) = run(added(total, arrived), after=[beside1], flops=LATE[1])
+    arrived = swapped(total, second)
+    (part1,) = run(
+        job(part_kernel, [tile], [home1, above1, left1]), after=[total], flops=LATE[2]
+    )
+    other1 = over_owners(part1)
+    (beside0,) = run(
+        job(beside_kernel, [tile], [next0, above0]), after=[part1], flops=LATE[3]
     )
     left0 = from_behind(beside0, 0, 1)
-    other1 = over_owners(part1)
-    (total,), (part0,) = run(
-        added(total, swapped(total, second)),
-        job(part_kernel, [tile], [home0, above0, left0]),
-    )
-    other0 = over_owners(part0)
+    (total,) = run(added(total, arrived), after=[beside0], flops=LATE[4])
     for group in others:
         (total,) = run(added(total, swapped(total, group)))
+    arrived = swapped(total, scattered[-1])
+    (part0,) = run(
+        job(part_kernel, [tile], [home0, above0, left0]), after=[total], flops=LATE[5]
+    )
+    other0 = over_owners(part0)
+    (total,) = run(joined(scattered[-1], total, arrived), after=[part0], flops=LATE[6])
+    for group in reversed(scattered[:-1]):
+        (total,) = run(joined(group, total, swapped(total, group)))
+    other_half = swap_with(total, core, 1)
     like = shape_of(bf16, *tile_object.shape)
-    new_object, token = updated(1, own1, part1, other1, like)
-    for group in reversed(scattered):
-        (total,) = run(joined(group, total, swapped(total, group)), after=[token])
-    other_half = swap_with(total, core, 1)
-    new_object, token = updated(
-        0, own[0], part0, other0, like, so_far=new_object, flops=3_000_000_000
-    )
+    new_object, token = updated(1, own1, part1, other1, like, flops=LATE[7], after=[total])
     positions_all = lax.axis_size("tile") * lax.axis_size("pos") * (patterns.shape[2] // 2)
     step = probe_rate / math.sqrt(positions_all)
-    (new_probe,) = run(
+    new_probe, token = run(
         job(
             lambda *refs: probe_kernel(step, modes, *refs),
-            [shape_of(f32, *probe.shape)],
+            [shape_of(f32, *probe.shape), shape_of(f32, 8, 128)],
             [total, other_half, probe],
         ),
         limit=8,
         after=[token],
+        flops=LATE[8],
+    )
+    new_object, _ = updated(
+        0, own[0], part0, other0, like, so_far=new_object, flops=LATE[9], after=[token]
     )
     new_probe = new_probe.reshape(2, pixels, lane_tiles, modes, 128).transpose(0, 1, 3, 2, 4)
     return (new_object, new_probe.reshape(probe_modes.shape))

time: 68 us -> 72.2 us (1.062)
  waiting for transfers between devices: 32 us -> 35.1 us
  Pallas kernels: 10.9 us -> 12 us
    ppermute x2, waiting for transfers between devices: 0.01 us -> 7.79 us  [over_owners(): return lax.ppermute(part, 'pos', [(0, 1), (1, 0)])]
    ppermute x9, waiting for transfers between devices: 12.6 us -> 8.77 us  [from_behind(): return lax.ppermute(block, 'tile', [(source(i), i) for i in range(tiles)])]
    ppermute x10, waiting for transfers between devices: 18.2 us -> 17.4 us  [swap_with(): lax.ppermute(x, ('tile', 'pos'), [(i, i ^ mask) for i in range(devices)])]
    pallas_call x10 -> x15, Pallas kernels: 9.21 us -> 9.8 us  [run(): pl.pallas_call(body, out_shape=sum(outs, []), in_specs=sum(specs, []) + [...]
  transfers between devices with their start and end apart: 22 -> 22, of which waited for: 11 -> 14; matrix products, arithmetic and copies ran while one was open for 0% -> 0% of each run, Pallas kernels for 8% -> 8%
where the time goes in v9:
time: 72.2 us; the launch traced here: 72 us
  waiting for transfers between devices  35.1 us (49%)
  starting transfers between devices  21.6 us (30%)
  Pallas kernels  12 us (17%)
  local copies, waits for them, and re-layouts  1.86 us (3%)
  between operations  1.47 us (2%)
    ppermute x10, waiting for transfers between devices, swap_with(): lax.ppermute(x, ('tile', 'pos'), [(i, i ^ mask) for i in range(devices)])  17.4 us
    ppermute x10, starting transfers between devices, swap_with(): lax.ppermute(x, ('tile', 'pos'), [(i, i ^ mask) for i in range(devices)])  9.95 us
    pallas_call x15, Pallas kernels, run(): pl.pallas_call(body, out_shape=sum(outs, []), in_specs=sum(specs, []) + [...  9.8 us
    ppermute x9, waiting for transfers between devices, from_behind(): return lax.ppermute(block, 'tile', [(source(i), i) for i in range(tiles)])  8.77 us
    ppermute x9, starting transfers between devices, from_behind(): return lax.ppermute(block, 'tile', [(source(i), i) for i in range(tiles)])  8.04 us
    ppermute x2, waiting for transfers between devices, over_owners(): return lax.ppermute(part, 'pos', [(0, 1), (1, 0)])  7.79 us
    pallas_call x2, Pallas kernels, updated(): pl.pallas_call(lambda *refs: update_kernel(layer, *refs), out_shape=[like...  2.24 us
    ppermute x2, starting transfers between devices, over_owners(): return lax.ppermute(part, 'pos', [(0, 1), (1, 0)])  2.11 us
  transfers between devices with their start and end apart: 22, of which 14 were waited for; matrix products, arithmetic and copies ran while one was open for 0% of the time, Pallas kernels for 8%

profile of v9, /device:TPU:0, one launch (start us, length us, event | category | flops | bytes accessed | tf_op | source)
XLA Modules:
  0.0 72.0 jit_solution(577890866364996502)
XLA Ops:
  0.6 1.2 %slice_bitcast_fusion = (bf16[2,256,256]{2,1,0:T(8,128)(2,1)S(1)}, bf16[2,256,256]{2,1,0:T(8,128)(2,1)S(1)}) fusion(bf16[1,2,2,256,256]{4,3,2,1,0:T(8,128)(2,1)} %param.7), kind=kLoop, calls=%fused_computation | loop fusion | bytes 1048576 | tf_op jit(solution)/shard_map/squeeze | solution.py:437
  1.8 5.1 %collective-permute-start.2 = (bf16[2,256,256]{2,1,0:T(8,128)(2,1)S(1)}, bf16[2,256,256]{2,1,0:T(8,128)(2,1)S(1)}, u32[]{:S(2)}, u32[]{:S(2)}) collective-permute-start(bf16[2,256,256]{2,1,0:T(8,128)(2,1)S(1)} %get-tuple-element.55.refs_4_.refs_2_.refs_0_), channel_id=1, source_target_pairs={{8,0},{10,2},{12,4},{14,6},{16,8},{18,10},{20,12},{22,14},{24,16},... | collective-permute-start | bytes 786440 | tf_op jit(solution)/shard_map/ppermute | solution.py:31
  6.9 0.7 collective-permute-start.1
  8.3 0.7 copy-done.3
  8.9 0.6 shard_map.86
  9.5 0.5 collective-permute-start.4
  10.0 3.6 %collective-permute-done.2.refs_4_ = bf16[2,256,256]{2,1,0:T(8,128)(2,1)S(1)} collective-permute-done((bf16[2,256,256]{2,1,0:T(8,128)(2,1)S(1)}, bf16[2,256,256]{2,1,0:T(8,128)(2,1)S(1)}, u32[]{:S(2)}, u32[]{:S(2)}) %collective-permute-start.2) | collective-permute-done | bytes 262176 | tf_op jit(solution)/shard_map/ppermute | solution.py:31
  13.7 1.5 %collective-permute-start = (bf16[272,256]{1,0:T(8,128)(2,1)S(1)}, bf16[272,256]{1,0:T(8,128)(2,1)S(1)}, u32[]{:S(2)}, u32[]{:S(2)}) collective-permute-start(bf16[272,256]{1,0:T(8,128)(2,1)S(1)} %get-tuple-element.29), channel_id=1, source_target_pairs={{0,1},{1,0},{2,3},{3,2},{4,5},{5,4},{6,7},{7,6},{8,9},{9,8},{10,11... | collective-permute-start | bytes 417800 | tf_op jit(solution)/shard_map/ppermute | solution.py:459
  15.2 2.9 %collective-permute-done.4.refs_4_ = bf16[2,256,256]{2,1,0:T(8,128)(2,1)S(1)} collective-permute-done((bf16[2,256,256]{2,1,0:T(8,128)(2,1)S(1)}, bf16[2,256,256]{2,1,0:T(8,128)(2,1)S(1)}, u32[]{:S(2)}, u32[]{:S(2)}) %collective-permute-start.4) | collective-permute-done | bytes 262176 | tf_op jit(solution)/shard_map/ppermute | solution.py:31
  18.1 0.3 collective-permute-start.5
  18.5 0.1 shard_map.87
  18.6 1.2 %collective-permute-done.refs_1_.refs_3_ = bf16[272,256]{1,0:T(8,128)(2,1)S(1)} collective-permute-done((bf16[272,256]{1,0:T(8,128)(2,1)S(1)}, bf16[272,256]{1,0:T(8,128)(2,1)S(1)}, u32[]{:S(2)}, u32[]{:S(2)}) %collective-permute-start) | collective-permute-done | bytes 139296 | tf_op jit(solution)/shard_map/ppermute | solution.py:459
  19.7 1.8 %shard_map.88 = (bf16[2,256,256]{2,1,0:T(8,128)(2,1)S(1)}, f32[2,256,512]{2,1,0:T(8,128)S(1)}) custom-call(bf16[272,256]{1,0:T(8,128)(2,1)S(1)} %get-tuple-element.28.refs_0_.refs_2_, bf16[272,256]{1,0:T(8,128)(2,1)S(1)} %collective-permute-done.refs_1_.refs_3_, bf16[2,256,256]{2,1,0:T(8,128)(2,1)S(1)} %get-tuple-element.55.refs_4_.refs_2_.refs_0_, ...), custom_call_target="tpu_custom_call" | custom-call | flops 1500000000 | bytes 4472832 | tf_op jit(solution)/shard_map/pallas_call | solution.py:288
  21.5 0.8 %collective-permute-done.5.refs_5_ = bf16[2,256,256]{2,1,0:T(8,128)(2,1)S(1)} collective-permute-done((bf16[2,256,256]{2,1,0:T(8,128)(2,1)S(1)}, bf16[2,256,256]{2,1,0:T(8,128)(2,1)S(1)}, u32[]{:S(2)}, u32[]{:S(2)}) %collective-permute-start.5) | collective-permute-done | bytes 262176 | tf_op jit(solution)/shard_map/ppermute | solution.py:31
  22.4 3.5 %shard_map.89 = (bf16[2,256,256]{2,1,0:T(8,128)(2,1)S(1)}, bf16[2,256,256]{2,1,0:T(8,128)(2,1)S(1)}, bf16[528,256]{1,0:T(8,128)(2,1)S(1)}, bf16[512,512]{1,0:T(8,128)(2,1)S(1)}) custom-call(bf16[272,256]{1,0:T(8,128)(2,1)S(1)} %get-tuple-element.28.refs_0_.refs_2_, bf16[272,256]{1,0:T(8,128)(2,1)S(1)} %collective-permute-done.refs_1_.refs_3_, ...), custom_call_target="tpu_custom_call" | custom-call | flops 3000000000 | bytes 4481024 | tf_op jit(solution)/shard_map/pallas_call | solution.py:288
  25.9 1.3 %shard_map.90 = (bf16[2,256,256]{2,1,0:T(8,128)(2,1)S(1)}, bf16[256,512]{1,0:T(8,128)(2,1)S(1)}, bf16[256,512]{1,0:T(8,128)(2,1)S(1)}) custom-call(bf16[2,256,256]{2,1,0:T(8,128)(2,1)S(1)} %get-tuple-element.33.refs_0_, f32[2,256,512]{2,1,0:T(8,128)S(1)} %get-tuple-element.31.refs_6_.refs_1_, bf16[512,512]{1,0:T(8,128)(2,1)S(1)} %get-tuple-element.35.refs_2_, ...), custom_call_target="tpu_custom_call" | custom-call | flops 1500000000 | bytes 3145728 | tf_op jit(solution)/shard_map/pallas_call | solution.py:288
  27.2 1.5 %collective-permute-start.6 = (bf16[256,512]{1,0:T(8,128)(2,1)S(1)}, bf16[256,512]{1,0:T(8,128)(2,1)S(1)}, u32[]{:S(2)}, u32[]{:S(2)}) collective-permute-start(bf16[256,512]{1,0:T(8,128)(2,1)S(1)} %get-tuple-element.37), channel_id=1, source_target_pairs={{0,2},{1,3},{2,0},{3,1},{4,6},{5,7},{6,4},{7,5},{8,10},{9,11},{10,... | collective-permute-start | bytes 786440 | tf_op jit(solution)/shard_map/ppermute | solution.py:395
  28.7 0.5 collective-permute-start.8
  29.2 0.7 collective-permute-done.6.refs_1_
  29.9 0.8 %shard_map.91 = (f32[64,512]{1,0:T(8,128)S(1)}, bf16[64,512]{1,0:T(8,128)(2,1)S(1)}, bf16[64,512]{1,0:T(8,128)(2,1)S(1)}, bf16[64,512]{1,0:T(8,128)(2,1)S(1)}, b...) custom-call(bf16[256,512]{1,0:T(8,128)(2,1)S(1)} %get-tuple-element.36.refs_0_, ...), custom_call_target="tpu_custom_call" | custom-call | flops 1000000 | bytes 2187264 | tf_op jit(solution)/shard_map/pallas_call | solution.py:288
  30.6 1.6 %collective-permute-start.9 = (bf16[64,512]{1,0:T(8,128)(2,1)S(1)}, bf16[64,512]{1,0:T(8,128)(2,1)S(1)}, u32[]{:S(2)}, u32[]{:S(2)}) collective-permute-start(bf16[64,512]{1,0:T(8,128)(2,1)S(1)} %get-tuple-element.46), channel_id=1, source_target_pairs={{0,1},{1,0},{2,3},{3,2},{4,5},{5,4},{6,7},{7,6},{8,9},{9,8},{10,11... | collective-permute-start | bytes 196616 | tf_op jit(solution)/shard_map/ppermute | solution.py:395
  32.3 0.9 %collective-permute-start.10 = (bf16[64,512]{1,0:T(8,128)(2,1)S(1)}, bf16[64,512]{1,0:T(8,128)(2,1)S(1)}, u32[]{:S(2)}, u32[]{:S(2)}) collective-permute-start(bf16[64,512]{1,0:T(8,128)(2,1)S(1)} %get-tuple-element.47), channel_id=1, source_target_pairs={{0,4},{1,5},{2,6},{3,7},{4,0},{5,1},{6,2},{7,3},{8,12},{9,13},{10,... | collective-permute-start | bytes 196616 | tf_op jit(solution)/shard_map/ppermute | solution.py:395
  33.1 1.1 %collective-permute-start.11 = (bf16[64,512]{1,0:T(8,128)(2,1)S(1)}, bf16[64,512]{1,0:T(8,128)(2,1)S(1)}, u32[]{:S(2)}, u32[]{:S(2)}) collective-permute-start(bf16[64,512]{1,0:T(8,128)(2,1)S(1)} %get-tuple-element.48), channel_id=1, source_target_pairs={{0,5},{1,4},{2,7},{3,6},{4,1},{5,0},{6,3},{7,2},{8,13},{9,12},{10,... | collective-permute-start | bytes 196616 | tf_op jit(solution)/shard_map/ppermute | solution.py:395
  34.2 0.9 %collective-permute-start.7 = (bf16[528,256]{1,0:T(8,128)(2,1)S(1)}, bf16[528,256]{1,0:T(8,128)(2,1)S(1)}, u32[]{:S(2)}, u32[]{:S(2)}) collective-permute-start(bf16[528,256]{1,0:T(8,128)(2,1)S(1)} %get-tuple-element.40), channel_id=1, source_target_pairs={{24,0},{26,2},{28,4},{30,6},{0,8},{2,10},{4,12},{6,14},{8,16},{10,... | collective-permute-start | bytes 811016 | tf_op jit(solution)/shard_map/ppermute | solution.py:31
  35.1 1.9 %collective-permute-done.10.refs_2_ = bf16[64,512]{1,0:T(8,128)(2,1)S(1)} collective-permute-done((bf16[64,512]{1,0:T(8,128)(2,1)S(1)}, bf16[64,512]{1,0:T(8,128)(2,1)S(1)}, u32[]{:S(2)}, u32[]{:S(2)}) %collective-permute-start.10) | collective-permute-done | bytes 65568 | tf_op jit(solution)/shard_map/ppermute | solution.py:395
  37.0 1.3 %collective-permute-done.11.refs_3_ = bf16[64,512]{1,0:T(8,128)(2,1)S(1)} collective-permute-done((bf16[64,512]{1,0:T(8,128)(2,1)S(1)}, bf16[64,512]{1,0:T(8,128)(2,1)S(1)}, u32[]{:S(2)}, u32[]{:S(2)}) %collective-permute-start.11) | collective-permute-done | bytes 65568 | tf_op jit(solution)/shard_map/ppermute | solution.py:395
  38.3 0.6 collective-permute-start.13
  39.0 1.3 %collective-permute-done.8.refs_1_ = bf16[528,256]{1,0:T(8,128)(2,1)S(1)} collective-permute-done((bf16[528,256]{1,0:T(8,128)(2,1)S(1)}, bf16[528,256]{1,0:T(8,128)(2,1)S(1)}, u32[]{:S(2)}, u32[]{:S(2)}) %collective-permute-start.8) | collective-permute-done | bytes 270368 | tf_op jit(solution)/shard_map/ppermute | solution.py:31
  40.3 0.1 shard_map.93.refs_2_
  40.5 6.5 %collective-permute-done.13.refs_1_ = bf16[64,512]{1,0:T(8,128)(2,1)S(1)} collective-permute-done((bf16[64,512]{1,0:T(8,128)(2,1)S(1)}, bf16[64,512]{1,0:T(8,128)(2,1)S(1)}, u32[]{:S(2)}, u32[]{:S(2)}) %collective-permute-start.13) | collective-permute-done | bytes 65568 | tf_op jit(solution)/shard_map/ppermute | solution.py:395
  46.9 0.6 collective-permute-start.15
  47.6 0.1 shard_map.95.refs_2_.refs_1_
  47.7 0.1 shard_map.96.refs_2_
  47.8 4.7 %collective-permute-done.15.refs_1_ = bf16[64,512]{1,0:T(8,128)(2,1)S(1)} collective-permute-done((bf16[64,512]{1,0:T(8,128)(2,1)S(1)}, bf16[64,512]{1,0:T(8,128)(2,1)S(1)}, u32[]{:S(2)}, u32[]{:S(2)}) %collective-permute-start.15) | collective-permute-done | bytes 65568 | tf_op jit(solution)/shard_map/ppermute | solution.py:395
  52.6 1.6 %collective-permute-start.20 = (bf16[64,512]{1,0:T(8,128)(2,1)S(1)}, bf16[64,512]{1,0:T(8,128)(2,1)S(1)}, u32[]{:S(2)}, u32[]{:S(2)}) collective-permute-start(bf16[64,512]{1,0:T(8,128)(2,1)S(1)} %shard_map.97.refs_3_.refs_0_), channel_id=1, source_target_pairs={{0,5},{1,4},{2,7},{3,6},{4,1},{5,0},{6,3},{7,2},{8,13},{9,12},{10,... | collective-permute-start | bytes 196616 | tf_op jit(solution)/shard_map/ppermute | solution.py:395
  54.2 1.4 %collective-permute-start.19 = (bf16[64,512]{1,0:T(8,128)(2,1)S(1)}, bf16[64,512]{1,0:T(8,128)(2,1)S(1)}, u32[]{:S(2)}, u32[]{:S(2)}) collective-permute-start(bf16[64,512]{1,0:T(8,128)(2,1)S(1)} %shard_map.97.refs_3_.refs_0_), channel_id=1, source_target_pairs={{0,4},{1,5},{2,6},{3,7},{4,0},{5,1},{6,2},{7,3},{8,12},{9,13},{10,... | collective-permute-start | bytes 196616 | tf_op jit(solution)/shard_map/ppermute | solution.py:395
  55.6 0.5 collective-permute-start.18
  56.1 1.5 %collective-permute-start.17 = (bf16[2,256,256]{2,1,0:T(8,128)(2,1)S(1)}, bf16[2,256,256]{2,1,0:T(8,128)(2,1)S(1)}, u32[]{:S(2)}, u32[]{:S(2)}) collective-permute-start(bf16[2,256,256]{2,1,0:T(8,128)(2,1)S(1)} %shard_map.95.refs_2_.refs_1_), channel_id=1, source_target_pairs={{0,1},{1,0},{2,3},{3,2},{4,5},{5,4},{6,7},{7,6},{8,9},{9,8},{10,11... | collective-permute-start | bytes 786440 | tf_op jit(solution)/shard_map/ppermute | solution.py:498
  57.6 0.1 shard_map.98.refs_4_.refs_1_
  57.8 0.6 collective-permute-start.16
  58.4 0.4 collective-permute-done.19.refs_2_
  58.8 1.9 %collective-permute-done.18.refs_1_ = bf16[64,512]{1,0:T(8,128)(2,1)S(1)} collective-permute-done((bf16[64,512]{1,0:T(8,128)(2,1)S(1)}, bf16[64,512]{1,0:T(8,128)(2,1)S(1)}, u32[]{:S(2)}, u32[]{:S(2)}) %collective-permute-start.18) | collective-permute-done | bytes 65568 | tf_op jit(solution)/shard_map/ppermute | solution.py:395
  60.7 0.1 collective-permute-start.21
  60.8 5.5 %collective-permute-done.17.refs_2_ = bf16[2,256,256]{2,1,0:T(8,128)(2,1)S(1)} collective-permute-done((bf16[2,256,256]{2,1,0:T(8,128)(2,1)S(1)}, bf16[2,256,256]{2,1,0:T(8,128)(2,1)S(1)}, u32[]{:S(2)}, u32[]{:S(2)}) %collective-permute-start.17) | collective-permute-done | bytes 262176 | tf_op jit(solution)/shard_map/ppermute | solution.py:498
  66.3 0.8 %shard_map.100 = (bf16[1,2,2,256,256]{4,3,2,1,0:T(8,128)(2,1)}, f32[8,128]{1,0:T(8,128)S(1)}) custom-call(bf16[2,256,256]{2,1,0:T(8,128)(2,1)S(1)} %get-tuple-element.30.refs_2_.refs_0_, bf16[2,256,256]{2,1,0:T(8,128)(2,1)S(1)} %shard_map.95.refs_2_.refs_1_, bf16[2,256,256]{2,1,0:T(8,128)(2,1)S(1)} %collective-permute-done.17.refs_2_, ...), custom_call_target="tpu_custom_call" | custom-call | flops 5000131072 | bytes 1048576 | tf_op jit(solution)/shard_map/pallas_call | solution.py:305
  67.1 1.2 %shard_map.101 = (f32[2048,128]{1,0:T(8,128)}, f32[8,128]{1,0:T(8,128)S(1)}) custom-call(bf16[256,512]{1,0:T(8,128)(2,1)S(1)} %shard_map.99.refs_3_.refs_0_, bf16[256,512]{1,0:T(8,128)(2,1)S(1)} %collective-permute-done.21.refs_1_, f32[2048,128]{1,0:T(8,128)S(1)} %bitcast.16, f32[8,128]{1,0:T(8,128)S(1)} %get-tuple-element.50.refs_3_), custom_call_target="tpu_custom_call" | custom-call | bytes 2625536 | tf_op jit(solution)/shard_map/pallas_call | solution.py:288
  68.3 2.3 %collective-permute-done.16.refs_2_ = bf16[2,256,256]{2,1,0:T(8,128)(2,1)S(1)} collective-permute-done((bf16[2,256,256]{2,1,0:T(8,128)(2,1)S(1)}, bf16[2,256,256]{2,1,0:T(8,128)(2,1)S(1)}, u32[]{:S(2)}, u32[]{:S(2)}) %collective-permute-start.16) | collective-permute-done | bytes 262176 | tf_op jit(solution)/shard_map/ppermute | solution.py:498
  70.6 1.4 %shard_map.102 = (bf16[1,2,2,256,256]{4,3,2,1,0:T(8,128)(2,1)}, f32[8,128]{1,0:T(8,128)}) custom-call(bf16[2,256,256]{2,1,0:T(8,128)(2,1)S(1)} %get-tuple-element.55.refs_4_.refs_2_.refs_0_, bf16[2,256,256]{2,1,0:T(8,128)(2,1)S(1)} %shard_map.98.refs_4_.refs_1_, ...), custom_call_target="tpu_custom_call", output_to_operand_aliasing={{0}: (3, {})} | custom-call | flops 131072 | bytes 1048576 | tf_op jit(solution)/shard_map/pallas_call | solution.py:305
  (24 shorter events, 0.3 us)
Async XLA Ops:
  0.6 7.6 %copy-start.2 = (bf16[1,1,2,256,256]{4,3,2,1,0:T(8,128)(2,1)S(1)}, bf16[1,1,2,256,256]{4,3,2,1,0:T(8,128)(2,1)}, u32[]{:S(2)}) copy-start(bf16[1,1,2,256,256]{4,3,2,1,0:T(8,128)(2,1)} %refs_3_.1) | copy-start | bytes 786436
  0.6 17.8 %copy-start = (f32[2,256,2,256]{3,2,1,0:T(2,128)S(1)}, f32[2,256,2,256]{3,2,1,0:T(2,128)}, u32[]{:S(2)}) copy-start(f32[2,256,2,256]{3,2,1,0:T(2,128)} %param.8) | copy-start | bytes 3145732
  1.8 16.7 %copy-start.1 = (bf16[512,512]{1,0:T(8,128)(2,1)S(1)}, bf16[512,512]{1,0:T(8,128)(2,1)}, u32[]{:S(2)}) copy-start(bf16[512,512]{1,0:T(8,128)(2,1)} %constant.10.refs_1_) | copy-start | bytes 1572868
  1.8 11.8 %collective-permute-start.2 = (bf16[2,256,256]{2,1,0:T(8,128)(2,1)S(1)}, bf16[2,256,256]{2,1,0:T(8,128)(2,1)S(1)}, u32[]{:S(2)}, u32[]{:S(2)}) collective-permute-start(bf16[2,256,256]{2,1,0:T(8,128)(2,1)S(1)} %get-tuple-element.55.refs_4_.refs_2_.refs_0_), channel_id=1, source_target_pairs={{8,0},{10,2},{12,4},{14,6},{16,8},{18,10},{20,12},{22,14},{24,16},... | collective-permute-start | bytes 786440 | tf_op jit(solution)/shard_map/ppermute | solution.py:31
  6.9 12.8 %collective-permute-start.1 = (bf16[2,2,256,256]{3,2,1,0:T(8,128)(2,1)}, bf16[2,2,256,256]{3,2,1,0:T(8,128)(2,1)S(1)}, u32[]{:S(2)}, u32[]{:S(2)}) collective-permute-start(bf16[2,2,256,256]{3,2,1,0:T(8,128)(2,1)} %bitcast.17), channel_id=1, source_target_pairs={{2,0},{4,2},{6,4},{0,6},{10,8},{12,10},{14,12},{8,14},{18,16},{20,... | collective-permute-start | bytes 1572872 | tf_op jit(solution)/shard_map/ppermute | solution.py:31
  8.2 0.7 copy-start.3
  9.5 8.6 %collective-permute-start.4 = (bf16[2,256,256]{2,1,0:T(8,128)(2,1)S(1)}, bf16[2,256,256]{2,1,0:T(8,128)(2,1)S(1)}, u32[]{:S(2)}, u32[]{:S(2)}) collective-permute-start(bf16[2,256,256]{2,1,0:T(8,128)(2,1)S(1)} %get-tuple-element.30.refs_2_.refs_0_), channel_id=1, source_target_pairs={{8,0},{10,2},{12,4},{14,6},{16,8},{18,10},{20,12},{22,14},{24,16},... | collective-permute-start | bytes 786440 | tf_op jit(solution)/shard_map/ppermute | solution.py:31
  13.6 6.1 %collective-permute-start.3 = (bf16[2,256,256]{2,1,0:T(8,128)(2,1)S(1)}, bf16[2,256,256]{2,1,0:T(8,128)(2,1)S(1)}, u32[]{:S(2)}, u32[]{:S(2)}) collective-permute-start(bf16[2,256,256]{2,1,0:T(8,128)(2,1)S(1)} %collective-permute-done.2.refs_4_), channel_id=1, source_target_pairs={{2,0},{4,2},{6,4},{0,6},{10,8},{12,10},{14,12},{8,14},{18,16},{20,... | collective-permute-start | bytes 786440 | tf_op jit(solution)/shard_map/ppermute | solution.py:31
  13.7 6.1 %collective-permute-start = (bf16[272,256]{1,0:T(8,128)(2,1)S(1)}, bf16[272,256]{1,0:T(8,128)(2,1)S(1)}, u32[]{:S(2)}, u32[]{:S(2)}) collective-permute-start(bf16[272,256]{1,0:T(8,128)(2,1)S(1)} %get-tuple-element.29), channel_id=1, source_target_pairs={{0,1},{1,0},{2,3},{3,2},{4,5},{5,4},{6,7},{7,6},{8,9},{9,8},{10,11... | collective-permute-start | bytes 417800 | tf_op jit(solution)/shard_map/ppermute | solution.py:459
  18.1 4.2 %collective-permute-start.5 = (bf16[2,256,256]{2,1,0:T(8,128)(2,1)S(1)}, bf16[2,256,256]{2,1,0:T(8,128)(2,1)S(1)}, u32[]{:S(2)}, u32[]{:S(2)}) collective-permute-start(bf16[2,256,256]{2,1,0:T(8,128)(2,1)S(1)} %collective-permute-done.4.refs_4_), channel_id=1, source_target_pairs={{2,0},{4,2},{6,4},{0,6},{10,8},{12,10},{14,12},{8,14},{18,16},{20,... | collective-permute-start | bytes 786440 | tf_op jit(solution)/shard_map/ppermute | solution.py:31
  19.7 2.6 %copy-start.4 = (bf16[512,512]{1,0:T(8,128)(2,1)S(1)}, bf16[512,512]{1,0:T(8,128)(2,1)}, u32[]{:S(2)}) copy-start(bf16[512,512]{1,0:T(8,128)(2,1)} %constant.11.refs_7_) | copy-start | bytes 1572868
  27.2 2.6 %collective-permute-start.6 = (bf16[256,512]{1,0:T(8,128)(2,1)S(1)}, bf16[256,512]{1,0:T(8,128)(2,1)S(1)}, u32[]{:S(2)}, u32[]{:S(2)}) collective-permute-start(bf16[256,512]{1,0:T(8,128)(2,1)S(1)} %get-tuple-element.37), channel_id=1, source_target_pairs={{0,2},{1,3},{2,0},{3,1},{4,6},{5,7},{6,4},{7,5},{8,10},{9,11},{10,... | collective-permute-start | bytes 786440 | tf_op jit(solution)/shard_map/ppermute | solution.py:395
  28.7 11.6 %collective-permute-start.8 = (bf16[528,256]{1,0:T(8,128)(2,1)S(1)}, bf16[528,256]{1,0:T(8,128)(2,1)S(1)}, u32[]{:S(2)}, u32[]{:S(2)}) collective-permute-start(bf16[528,256]{1,0:T(8,128)(2,1)S(1)} %get-tuple-element.43), channel_id=1, source_target_pairs={{24,0},{26,2},{28,4},{30,6},{0,8},{2,10},{4,12},{6,14},{8,16},{10,... | collective-permute-start | bytes 811016 | tf_op jit(solution)/shard_map/ppermute | solution.py:31
  30.6 4.4 %collective-permute-start.9 = (bf16[64,512]{1,0:T(8,128)(2,1)S(1)}, bf16[64,512]{1,0:T(8,128)(2,1)S(1)}, u32[]{:S(2)}, u32[]{:S(2)}) collective-permute-start(bf16[64,512]{1,0:T(8,128)(2,1)S(1)} %get-tuple-element.46), channel_id=1, source_target_pairs={{0,1},{1,0},{2,3},{3,2},{4,5},{5,4},{6,7},{7,6},{8,9},{9,8},{10,11... | collective-permute-start | bytes 196616 | tf_op jit(solution)/shard_map/ppermute | solution.py:395
  32.3 4.8 %collective-permute-start.10 = (bf16[64,512]{1,0:T(8,128)(2,1)S(1)}, bf16[64,512]{1,0:T(8,128)(2,1)S(1)}, u32[]{:S(2)}, u32[]{:S(2)}) collective-permute-start(bf16[64,512]{1,0:T(8,128)(2,1)S(1)} %get-tuple-element.47), channel_id=1, source_target_pairs={{0,4},{1,5},{2,6},{3,7},{4,0},{5,1},{6,2},{7,3},{8,12},{9,13},{10,... | collective-permute-start | bytes 196616 | tf_op jit(solution)/shard_map/ppermute | solution.py:395
  33.1 5.2 %collective-permute-start.11 = (bf16[64,512]{1,0:T(8,128)(2,1)S(1)}, bf16[64,512]{1,0:T(8,128)(2,1)S(1)}, u32[]{:S(2)}, u32[]{:S(2)}) collective-permute-start(bf16[64,512]{1,0:T(8,128)(2,1)S(1)} %get-tuple-element.48), channel_id=1, source_target_pairs={{0,5},{1,4},{2,7},{3,6},{4,1},{5,0},{6,3},{7,2},{8,13},{9,12},{10,... | collective-permute-start | bytes 196616 | tf_op jit(solution)/shard_map/ppermute | solution.py:395
  34.2 13.5 %collective-permute-start.7 = (bf16[528,256]{1,0:T(8,128)(2,1)S(1)}, bf16[528,256]{1,0:T(8,128)(2,1)S(1)}, u32[]{:S(2)}, u32[]{:S(2)}) collective-permute-start(bf16[528,256]{1,0:T(8,128)(2,1)S(1)} %get-tuple-element.40), channel_id=1, source_target_pairs={{24,0},{26,2},{28,4},{30,6},{0,8},{2,10},{4,12},{6,14},{8,16},{10,... | collective-permute-start | bytes 811016 | tf_op jit(solution)/shard_map/ppermute | solution.py:31
  38.3 8.6 %collective-permute-start.13 = (bf16[64,512]{1,0:T(8,128)(2,1)S(1)}, bf16[64,512]{1,0:T(8,128)(2,1)S(1)}, u32[]{:S(2)}, u32[]{:S(2)}) collective-permute-start(bf16[64,512]{1,0:T(8,128)(2,1)S(1)} %shard_map.92.refs_2_.refs_0_), channel_id=1, source_target_pairs={{0,8},{1,9},{2,10},{3,11},{4,12},{5,13},{6,14},{7,15},{8,0},{9,1},... | collective-permute-start | bytes 196616 | tf_op jit(solution)/shard_map/ppermute | solution.py:395
  40.4 7.2 %collective-permute-start.12 = (bf16[2,256,256]{2,1,0:T(8,128)(2,1)S(1)}, bf16[2,256,256]{2,1,0:T(8,128)(2,1)S(1)}, u32[]{:S(2)}, u32[]{:S(2)}) collective-permute-start(bf16[2,256,256]{2,1,0:T(8,128)(2,1)S(1)} %shard_map.93.refs_2_), channel_id=1, source_target_pairs={{6,0},{0,2},{2,4},{4,6},{14,8},{8,10},{10,12},{12,14},{22,16},{16,... | collective-permute-start | bytes 786440 | tf_op jit(solution)/shard_map/ppermute | solution.py:31
  46.9 5.6 %collective-permute-start.15 = (bf16[64,512]{1,0:T(8,128)(2,1)S(1)}, bf16[64,512]{1,0:T(8,128)(2,1)S(1)}, u32[]{:S(2)}, u32[]{:S(2)}) collective-permute-start(bf16[64,512]{1,0:T(8,128)(2,1)S(1)} %shard_map.94.refs_3_.refs_0_), channel_id=1, source_target_pairs={{0,16},{1,17},{2,18},{3,19},{4,20},{5,21},{6,22},{7,23},{8,24},{9,... | collective-permute-start | bytes 196616 | tf_op jit(solution)/shard_map/ppermute | solution.py:395
  47.8 9.9 %collective-permute-start.14 = (bf16[2,256,256]{2,1,0:T(8,128)(2,1)S(1)}, bf16[2,256,256]{2,1,0:T(8,128)(2,1)S(1)}, u32[]{:S(2)}, u32[]{:S(2)}) collective-permute-start(bf16[2,256,256]{2,1,0:T(8,128)(2,1)S(1)} %shard_map.96.refs_2_), channel_id=1, source_target_pairs={{6,0},{0,2},{2,4},{4,6},{14,8},{8,10},{10,12},{12,14},{22,16},{16,... | collective-permute-start | bytes 786440 | tf_op jit(solution)/shard_map/ppermute | solution.py:31
  52.6 5.8 %collective-permute-start.20 = (bf16[64,512]{1,0:T(8,128)(2,1)S(1)}, bf16[64,512]{1,0:T(8,128)(2,1)S(1)}, u32[]{:S(2)}, u32[]{:S(2)}) collective-permute-start(bf16[64,512]{1,0:T(8,128)(2,1)S(1)} %shard_map.97.refs_3_.refs_0_), channel_id=1, source_target_pairs={{0,5},{1,4},{2,7},{3,6},{4,1},{5,0},{6,3},{7,2},{8,13},{9,12},{10,... | collective-permute-start | bytes 196616 | tf_op jit(solution)/shard_map/ppermute | solution.py:395
  54.2 4.6 %collective-permute-start.19 = (bf16[64,512]{1,0:T(8,128)(2,1)S(1)}, bf16[64,512]{1,0:T(8,128)(2,1)S(1)}, u32[]{:S(2)}, u32[]{:S(2)}) collective-permute-start(bf16[64,512]{1,0:T(8,128)(2,1)S(1)} %shard_map.97.refs_3_.refs_0_), channel_id=1, source_target_pairs={{0,4},{1,5},{2,6},{3,7},{4,0},{5,1},{6,2},{7,3},{8,12},{9,13},{10,... | collective-permute-start | bytes 196616 | tf_op jit(solution)/shard_map/ppermute | solution.py:395
  55.6 5.0 %collective-permute-start.18 = (bf16[64,512]{1,0:T(8,128)(2,1)S(1)}, bf16[64,512]{1,0:T(8,128)(2,1)S(1)}, u32[]{:S(2)}, u32[]{:S(2)}) collective-permute-start(bf16[64,512]{1,0:T(8,128)(2,1)S(1)} %shard_map.97.refs_3_.refs_0_), channel_id=1, source_target_pairs={{0,1},{1,0},{2,3},{3,2},{4,5},{5,4},{6,7},{7,6},{8,9},{9,8},{10,11... | collective-permute-start | bytes 196616 | tf_op jit(solution)/shard_map/ppermute | solution.py:395
  56.1 10.1 %collective-permute-start.17 = (bf16[2,256,256]{2,1,0:T(8,128)(2,1)S(1)}, bf16[2,256,256]{2,1,0:T(8,128)(2,1)S(1)}, u32[]{:S(2)}, u32[]{:S(2)}) collective-permute-start(bf16[2,256,256]{2,1,0:T(8,128)(2,1)S(1)} %shard_map.95.refs_2_.refs_1_), channel_id=1, source_target_pairs={{0,1},{1,0},{2,3},{3,2},{4,5},{5,4},{6,7},{7,6},{8,9},{9,8},{10,11... | collective-permute-start | bytes 786440 | tf_op jit(solution)/shard_map/ppermute | solution.py:498
  57.8 12.9 %collective-permute-start.16 = (bf16[2,256,256]{2,1,0:T(8,128)(2,1)S(1)}, bf16[2,256,256]{2,1,0:T(8,128)(2,1)S(1)}, u32[]{:S(2)}, u32[]{:S(2)}) collective-permute-start(bf16[2,256,256]{2,1,0:T(8,128)(2,1)S(1)} %shard_map.98.refs_4_.refs_1_), channel_id=1, source_target_pairs={{0,1},{1,0},{2,3},{3,2},{4,5},{5,4},{6,7},{7,6},{8,9},{9,8},{10,11... | collective-permute-start | bytes 786440 | tf_op jit(solution)/shard_map/ppermute | solution.py:498
  60.7 6.4 %collective-permute-start.21 = (bf16[256,512]{1,0:T(8,128)(2,1)S(1)}, bf16[256,512]{1,0:T(8,128)(2,1)S(1)}, u32[]{:S(2)}, u32[]{:S(2)}) collective-permute-start(bf16[256,512]{1,0:T(8,128)(2,1)S(1)} %shard_map.99.refs_3_.refs_0_), channel_id=1, source_target_pairs={{0,2},{1,3},{2,0},{3,1},{4,6},{5,7},{6,4},{7,5},{8,10},{9,11},{10,... | collective-permute-start | bytes 786440 | tf_op jit(solution)/shard_map/ppermute | solution.py:395

commit v10 on v9

--- a/solution.py
+++ b/solution.py
@@ -15,7 +15,7 @@
 object_rate = 0.05
 probe_rate = 0.15
 
-LATE = [5_000_000_000] * 8 + [0, 0]
+LATE = [0, 8_000_000_000, 0, 30_000_000_000, 0, 15_000_000_000, 0, 4_000_000_000]
 
 f32 = jnp.float32
 bf16 = jnp.bfloat16
@@ -150,8 +150,8 @@
         arrive_ref[1, :, lanes] = -a_neg
 
 
-def spread(shifts, grad, home_ref, next_ref, down_ref):
-    rows_t, cols_t, col = shifts[2:5]
+def spread(shifts, grad, home_ref, next_ref, down_ref, layer):
+    rows_t, cols_t = shifts[2:4]
     n = rows_t.shape[1]
     wrap_cols = cols_t[:, :n] + cols_t[:, n:]
     for part in range(2):
@@ -159,17 +159,17 @@
         wide = dot(rows[:n], cols_t).astype(bf16)
         home_ref[part] = wide[:, :n]
         next_ref[part] = wide[:, n:]
-        down_ref[pl.ds(part * n, n), :] = dot(rows[n:], wrap_cols).astype(bf16)
-    edge = lax.broadcasted_iota(jnp.int32, (16, n), 1) < col
-    down_ref[pl.ds(2 * n, 16), :] = edge.astype(f32).astype(bf16)
-
-
-def far_kernel(
-    mine_ref, sent_ref, own_ref, right_ref, below_ref, diag_ref, arrive_ref, dft_ref,
-    home_ref, next_ref, down_ref, waves_ref,
+        where = pl.ds((2 * layer + part) * n, n)
+        down_ref[where, :] = dot(rows[n:], wrap_cols).astype(bf16)
+
+
+def gradient_kernel(
+    mine_ref, sent_ref, own_ref, right_ref, below_ref, diag_ref, near_ref, arrive_ref, planes_ref,
+    prop_ref, dft_ref,
+    home0_ref, next0_ref, home1_ref, next1_ref, down_ref, keep_ref, give_ref, term_ref,
 ):
     n = own_ref.shape[1]
-    modes = arrive_ref.shape[2] // n
+    modes = planes_ref.shape[2] // n
     shifts = shift_tables(mine_ref, sent_ref)
     busy = shifts[5]
     tiles = (own_ref, right_ref.at[1], below_ref, diag_ref)
@@ -183,6 +183,7 @@
     intensity = sum(f_re * f_re + f_neg * f_neg for f_re, f_neg in fields)
     pattern = jnp.where(busy, mine_ref[:n, :].astype(f32), sent_ref[:n, :].astype(f32))
     residual = intensity - pattern
+    waves = []
     grad = [0.0, 0.0]
     for mode in range(modes):
         lanes = pl.ds(mode * n, n)
@@ -191,18 +192,13 @@
         b_re, b_im = transform(dft_ref, stacked(f_re * residual, f_neg * residual))
         grad[0] += a_re * b_re + a_im * b_im
         grad[1] += a_re * b_im - a_im * b_re
-        wave = stacked(far[0] * b_re + far[1] * b_im, far[1] * b_re - far[0] * b_im)
-        waves_ref[:, lanes] = wave
-    spread(shifts, grad, home_ref, next_ref, down_ref)
-
-
-def near_kernel(near_ref, planes_ref, waves_ref, prop_ref, grad_ref, keep_ref, give_ref, term_ref):
-    n = near_ref.shape[1]
+        waves.append(stacked(far[0] * b_re + far[1] * b_im, far[1] * b_re - far[0] * b_im))
+    spread(shifts, grad, home1_ref, next1_ref, down_ref, 1)
     grad = [0.0, 0.0]
     near = [near_ref[part].astype(f32) for part in range(2)]
-    for mode in range(planes_ref.shape[2] // n):
+    for mode in range(modes):
         lanes = pl.ds(mode * n, n)
-        b_re, b_im = transform(prop_ref, waves_ref[:, lanes])
+        b_re, b_im = transform(prop_ref, waves[mode])
         p_re, p_im = planes_ref[0, :, lanes], planes_ref[1, :, lanes]
         grad[0] += p_re * b_re + p_im * b_im
         grad[1] += p_re * b_im - p_im * b_re
@@ -211,29 +207,26 @@
     core = place_of(core_group())
     keep_ref[...] = term_ref[core]
     give_ref[...] = term_ref[1 - core]
-    for part in range(2):
-        grad_ref[part] = grad[part].astype(bf16)
-
-
-def spread_kernel(mine_ref, sent_ref, grad_ref, home_ref, next_ref, down_ref):
-    shifts = shift_tables(mine_ref, sent_ref)
-    spread(shifts, [grad_ref[part] for part in range(2)], home_ref, next_ref, down_ref)
-
-
-def above_parts(above_ref, n):
-    parts = [above_ref[pl.ds(part * n, n), :].astype(f32) for part in range(2)]
-    return parts, above_ref[pl.ds(2 * n, 16), :].astype(f32)[0:1] > 0
-
-
-def beside_kernel(next_ref, above_ref, out_ref):
-    above, split = above_parts(above_ref, out_ref.shape[1])
+    spread(shifts, grad, home0_ref, next0_ref, down_ref, 0)
+    edge = lax.broadcasted_iota(jnp.int32, (16, n), 1) < shifts[4]
+    down_ref[pl.ds(4 * n, 16), :] = edge.astype(f32).astype(bf16)
+
+
+def above_parts(above_ref, layer, n):
+    where = [pl.ds((2 * layer + part) * n, n) for part in range(2)]
+    split = above_ref[pl.ds(4 * n, 16), :].astype(f32)[0:1] > 0
+    return [above_ref[rows, :].astype(f32) for rows in where], split
+
+
+def beside_kernel(layer, next_ref, above_ref, out_ref):
+    above, split = above_parts(above_ref, layer, out_ref.shape[1])
     for part in range(2):
         total = next_ref[part].astype(f32) + jnp.where(split, above[part], 0.0)
         out_ref[part] = total.astype(bf16)
 
 
-def part_kernel(home_ref, above_ref, left_ref, out_ref):
-    above, split = above_parts(above_ref, out_ref.shape[1])
+def part_kernel(layer, home_ref, above_ref, left_ref, out_ref):
+    above, split = above_parts(above_ref, layer, out_ref.shape[1])
     for part in range(2):
         total = home_ref[part].astype(f32) + jnp.where(split, 0.0, above[part])
         out_ref[part] = (total + left_ref[part].astype(f32)).astype(bf16)
@@ -367,8 +360,7 @@
         out_ref[pl.ds(block * size, size), :] = blocks[block]
 
 
-def probe_kernel(step, modes, mine_ref, other_ref, probe_ref, out_ref, token_ref):
-    token_ref[...] = jnp.zeros_like(token_ref)
+def probe_kernel(step, modes, mine_ref, other_ref, probe_ref, out_ref):
     core = place_of(core_group())
     lane_tiles = 2
     n = mine_ref.shape[0]
@@ -471,25 +463,14 @@
         limit=16,
     )
     half = shape_of(bf16, pixels, width)
-    down = shape_of(bf16, 2 * pixels + 16, pixels)
-    home1, next1, down1, waves = run(
+    home0, next0, home1, next1, down, keep, give = run(
         job(
-            far_kernel,
-            [tile, tile, down, shape_of(bf16, 2 * pixels, width)],
-            [mine, sent, own1, right, below1, diag1, arrive, dft],
-        ),
-        flops=3_000_000_000,
-        limit=16,
-    )
-    above1 = from_behind(down1, 1, 0)
-    grad0, keep, give = run(
-        job(
-            near_kernel,
-            [tile, half, half],
-            [near, probe_planes, waves, table],
+            gradient_kernel,
+            [tile] * 4 + [shape_of(bf16, 4 * pixels + 16, pixels), half, half],
+            [mine, sent, own1, right, below1, diag1, near, arrive, probe_planes, table, dft],
             scratch=[pltpu.VMEM((2, pixels, width), bf16)],
         ),
-        flops=1_500_000_000,
+        flops=4_000_000_000,
         limit=16,
     )
 
@@ -498,65 +479,60 @@
             return lax.ppermute(part, "pos", [(0, 1), (1, 0)])
         return lax.psum(part.astype(f32), "pos") - part.astype(f32)
 
+    def beside(layer, next_tile):
+        kernel = lambda *refs: beside_kernel(layer, *refs)
+        return job(kernel, [tile], [next_tile, above])
+
+    def part(layer, home, left):
+        kernel = lambda *refs: part_kernel(layer, *refs)
+        return job(kernel, [tile], [home, above, left])
+
     core, groups = core_group(), exchange_groups()
+    above = from_behind(down, 1, 0)
     arrived = [swap_with(give, core, 1)]
-    side = [job(spread_kernel, [tile, tile, down], [mine, sent, grad0])]
     scattered = []
     while len(groups) > 1 and keep.shape[0] >> len(groups[0]) >= 16:
         group, groups = groups[0], groups[1:]
-        done = run(folded(group, keep, arrived), *side, limit=8)
-        if side:
-            done, (home0, next0, down0) = done
-            above0 = from_behind(down0, 1, 0)
-            side = []
-        keep, *gives = done
+        keep, *gives = run(folded(group, keep, arrived))
         arrived = [swap_with(x, group, at) for at, x in enumerate(gives, 1)]
         scattered.append(group)
     first, second, *others = [[bit] for group in groups for bit in group]
     (total,) = run(added(keep, arrived))
     arrived = swapped(total, first)
-    (beside1,) = run(
-        job(beside_kernel, [tile], [next1, above1]), after=[total], flops=LATE[0]
+    (beside1,), (beside0,) = run(
+        beside(1, next1), beside(0, next0), after=[total], flops=LATE[0]
     )
     left1 = from_behind(beside1, 0, 1)
+    left0 = from_behind(beside0, 0, 1)
     (total,) = run(added(total, arrived), after=[beside1], flops=LATE[1])
     arrived = swapped(total, second)
-    (part1,) = run(
-        job(part_kernel, [tile], [home1, above1, left1]), after=[total], flops=LATE[2]
-    )
+    (part1,) = run(part(1, home1, left1), after=[total], flops=LATE[2])
     other1 = over_owners(part1)
-    (beside0,) = run(
-        job(beside_kernel, [tile], [next0, above0]), after=[part1], flops=LATE[3]
-    )
-    left0 = from_behind(beside0, 0, 1)
-    (total,) = run(added(total, arrived), after=[beside0], flops=LATE[4])
+    (total,) = run(added(total, arrived), after=[part1], flops=LATE[3])
     for group in others:
         (total,) = run(added(total, swapped(total, group)))
     arrived = swapped(total, scattered[-1])
-    (part0,) = run(
-        job(part_kernel, [tile], [home0, above0, left0]), after=[total], flops=LATE[5]
-    )
+    (part0,) = run(part(0, home0, left0), after=[total], flops=LATE[4])
     other0 = over_owners(part0)
-    (total,) = run(joined(scattered[-1], total, arrived), after=[part0], flops=LATE[6])
+    like = shape_of(bf16, *tile_object.shape)
+    new_object, token = updated(1, own1, part1, other1, like, flops=LATE[5], after=[part0])
+    (total,) = run(joined(scattered[-1], total, arrived), after=[token], flops=LATE[6])
     for group in reversed(scattered[:-1]):
         (total,) = run(joined(group, total, swapped(total, group)))
     other_half = swap_with(total, core, 1)
-    like = shape_of(bf16, *tile_object.shape)
-    new_object, token = updated(1, own1, part1, other1, like, flops=LATE[7], after=[total])
+    new_object, token = updated(
+        0, own[0], part0, other0, like, so_far=new_object, flops=LATE[7], after=[total]
+    )
     positions_all = lax.axis_size("tile") * lax.axis_size("pos") * (patterns.shape[2] // 2)
     step = probe_rate / math.sqrt(positions_all)
-    new_probe, token = run(
+    (new_probe,) = run(
         job(
             lambda *refs: probe_kernel(step, modes, *refs),
-            [shape_of(f32, *probe.shape), shape_of(f32, 8, 128)],
+            [shape_of(f32, *probe.shape)],
             [total, other_half, probe],
         ),
         limit=8,
         after=[token],
-        flops=LATE[8],
-    )
-    new_object, _ = updated(
-        0, own[0], part0, other0, like, so_far=new_object, flops=LATE[9], after=[token]
     )
     new_probe = new_probe.reshape(2, pixels, lane_tiles, modes, 128).transpose(0, 1, 3, 2, 4)
     return (new_object, new_probe.reshape(probe_modes.shape))

time: 72.2 us -> 68.6 us (0.950)
  waiting for transfers between devices: 35.1 us -> 30.7 us
  starting transfers between devices: 21.6 us -> 23.3 us
  Pallas kernels: 12 us -> 11.1 us
    ppermute x10, waiting for transfers between devices: 17.4 us -> 7.48 us  [swap_with(): lax.ppermute(x, ('tile', 'pos'), [(i, i ^ mask) for i in range(devices)])]
    ppermute x9 -> x8, waiting for transfers between devices: 8.77 us -> 14.6 us  [from_behind(): return lax.ppermute(block, 'tile', [(source(i), i) for i in range(tiles)])]
    ppermute x2, starting transfers between devices: 2.11 us -> 3.24 us  [over_owners(): return lax.ppermute(part, 'pos', [(0, 1), (1, 0)])]
    ppermute x10, starting transfers between devices: 9.95 us -> 10.8 us  [swap_with(): lax.ppermute(x, ('tile', 'pos'), [(i, i ^ mask) for i in range(devices)])]
    pallas_call x15 -> x13, Pallas kernels: 9.8 us -> 9.46 us  [run(): pl.pallas_call(body, out_shape=sum(outs, []), in_specs=sum(specs, []) + [...]
    ppermute x9 -> x8, starting transfers between devices: 8.04 us -> 7.73 us  [from_behind(): return lax.ppermute(block, 'tile', [(source(i), i) for i in range(tiles)])]
  transfers between devices with their start and end apart: 22 -> 21, of which waited for: 14 -> 15; matrix products, arithmetic and copies ran while one was open for 0% -> 0% of each run, Pallas kernels for 8% -> 7%
where the time goes in v10:
time: 68.6 us; the launch traced here: 68.4 us
  waiting for transfers between devices  30.7 us (45%)
  starting transfers between devices  23.3 us (34%)
  Pallas kernels  11.1 us (16%)
  local copies, waits for them, and re-layouts  1.86 us (3%)
  between operations  1.45 us (2%)
    ppermute x8, waiting for transfers between devices, from_behind(): return lax.ppermute(block, 'tile', [(source(i), i) for i in range(tiles)])  14.6 us
    ppermute x10, starting transfers between devices, swap_with(): lax.ppermute(x, ('tile', 'pos'), [(i, i ^ mask) for i in range(devices)])  10.8 us
    pallas_call x13, Pallas kernels, run(): pl.pallas_call(body, out_shape=sum(outs, []), in_specs=sum(specs, []) + [...  9.46 us
    ppermute x8, starting transfers between devices, from_behind(): return lax.ppermute(block, 'tile', [(source(i), i) for i in range(tiles)])  7.73 us
    ppermute x10, waiting for transfers between devices, swap_with(): lax.ppermute(x, ('tile', 'pos'), [(i, i ^ mask) for i in range(devices)])  7.48 us
    ppermute x2, waiting for transfers between devices, over_owners(): return lax.ppermute(part, 'pos', [(0, 1), (1, 0)])  7.45 us
    ppermute x2, starting transfers between devices, over_owners(): return lax.ppermute(part, 'pos', [(0, 1), (1, 0)])  3.24 us
    pallas_call x2, Pallas kernels, updated(): pl.pallas_call(lambda *refs: update_kernel(layer, *refs), out_shape=[like...  1.65 us
  transfers between devices with their start and end apart: 21, of which 15 were waited for; matrix products, arithmetic and copies ran while one was open for 0% of the time, Pallas kernels for 7%

profile of v10, /device:TPU:0, one launch (start us, length us, event | category | flops | bytes accessed | tf_op | source)
XLA Modules:
  0.0 68.4 jit_solution(15188638513930711501)
XLA Ops:
  0.6 1.2 %slice_bitcast_fusion = (bf16[2,256,256]{2,1,0:T(8,128)(2,1)S(1)}, bf16[2,256,256]{2,1,0:T(8,128)(2,1)S(1)}) fusion(bf16[1,2,2,256,256]{4,3,2,1,0:T(8,128)(2,1)} %param.7), kind=kLoop, calls=%fused_computation | loop fusion | bytes 1048576 | tf_op jit(solution)/shard_map/squeeze | solution.py:429
  1.8 5.1 %collective-permute-start.4 = (bf16[2,256,256]{2,1,0:T(8,128)(2,1)S(1)}, bf16[2,256,256]{2,1,0:T(8,128)(2,1)S(1)}, u32[]{:S(2)}, u32[]{:S(2)}) collective-permute-start(bf16[2,256,256]{2,1,0:T(8,128)(2,1)S(1)} %get-tuple-element.51.refs_4_.refs_2_.refs_0_), channel_id=1, source_target_pairs={{8,0},{10,2},{12,4},{14,6},{16,8},{18,10},{20,12},{22,14},{24,16},... | collective-permute-start | bytes 786440 | tf_op jit(solution)/shard_map/ppermute | solution.py:31
  6.9 0.7 collective-permute-start.1
  8.3 0.7 copy-done.3
  8.9 0.6 shard_map.86
  9.5 0.5 collective-permute-start.2
  10.0 3.6 %collective-permute-done.4.refs_4_ = bf16[2,256,256]{2,1,0:T(8,128)(2,1)S(1)} collective-permute-done((bf16[2,256,256]{2,1,0:T(8,128)(2,1)S(1)}, bf16[2,256,256]{2,1,0:T(8,128)(2,1)S(1)}, u32[]{:S(2)}, u32[]{:S(2)}) %collective-permute-start.4) | collective-permute-done | bytes 262176 | tf_op jit(solution)/shard_map/ppermute | solution.py:31
  13.7 1.5 %collective-permute-start = (bf16[272,256]{1,0:T(8,128)(2,1)S(1)}, bf16[272,256]{1,0:T(8,128)(2,1)S(1)}, u32[]{:S(2)}, u32[]{:S(2)}) collective-permute-start(bf16[272,256]{1,0:T(8,128)(2,1)S(1)} %get-tuple-element.27), channel_id=1, source_target_pairs={{0,1},{1,0},{2,3},{3,2},{4,5},{5,4},{6,7},{7,6},{8,9},{9,8},{10,11... | collective-permute-start | bytes 417800 | tf_op jit(solution)/shard_map/ppermute | solution.py:451
  15.2 2.9 %collective-permute-done.2.refs_4_ = bf16[2,256,256]{2,1,0:T(8,128)(2,1)S(1)} collective-permute-done((bf16[2,256,256]{2,1,0:T(8,128)(2,1)S(1)}, bf16[2,256,256]{2,1,0:T(8,128)(2,1)S(1)}, u32[]{:S(2)}, u32[]{:S(2)}) %collective-permute-start.2) | collective-permute-done | bytes 262176 | tf_op jit(solution)/shard_map/ppermute | solution.py:31
  18.1 0.3 collective-permute-start.3
  18.5 0.1 shard_map.87
  18.6 1.2 %collective-permute-done.refs_1_ = bf16[272,256]{1,0:T(8,128)(2,1)S(1)} collective-permute-done((bf16[272,256]{1,0:T(8,128)(2,1)S(1)}, bf16[272,256]{1,0:T(8,128)(2,1)S(1)}, u32[]{:S(2)}, u32[]{:S(2)}) %collective-permute-start) | collective-permute-done | bytes 139296 | tf_op jit(solution)/shard_map/ppermute | solution.py:451
  19.7 1.8 %shard_map.88 = (bf16[2,256,256]{2,1,0:T(8,128)(2,1)S(1)}, f32[2,256,512]{2,1,0:T(8,128)S(1)}) custom-call(bf16[272,256]{1,0:T(8,128)(2,1)S(1)} %get-tuple-element.26.refs_0_, bf16[272,256]{1,0:T(8,128)(2,1)S(1)} %collective-permute-done.refs_1_, bf16[2,256,256]{2,1,0:T(8,128)(2,1)S(1)} %get-tuple-element.51.refs_4_.refs_2_.refs_0_, ...), custom_call_target="tpu_custom_call" | custom-call | flops 1500000000 | bytes 4472832 | tf_op jit(solution)/shard_map/pallas_call | solution.py:281
  21.5 0.8 %collective-permute-done.3.refs_5_ = bf16[2,256,256]{2,1,0:T(8,128)(2,1)S(1)} collective-permute-done((bf16[2,256,256]{2,1,0:T(8,128)(2,1)S(1)}, bf16[2,256,256]{2,1,0:T(8,128)(2,1)S(1)}, u32[]{:S(2)}, u32[]{:S(2)}) %collective-permute-start.3) | collective-permute-done | bytes 262176 | tf_op jit(solution)/shard_map/ppermute | solution.py:31
  22.4 5.2 %shard_map.89 = (bf16[2,256,256]{2,1,0:T(8,128)(2,1)S(1)}, bf16[2,256,256]{2,1,0:T(8,128)(2,1)S(1)}, bf16[2,256,256]{2,1,0:T(8,128)(2,1)S(1)}, bf16[2,256,256]{2...) custom-call(bf16[272,256]{1,0:T(8,128)(2,1)S(1)} %get-tuple-element., ...), custom_call_target="tpu_custom_call" | custom-call | flops 4000000000 | bytes 7102464 | tf_op jit(solution)/shard_map/pallas_call | solution.py:281
  27.5 0.2 collective-permute-start.6
  27.8 1.4 %collective-permute-start.7 = (bf16[256,512]{1,0:T(8,128)(2,1)S(1)}, bf16[256,512]{1,0:T(8,128)(2,1)S(1)}, u32[]{:S(2)}, u32[]{:S(2)}) collective-permute-start(bf16[256,512]{1,0:T(8,128)(2,1)S(1)} %get-tuple-element.38), channel_id=1, source_target_pairs={{0,2},{1,3},{2,0},{3,1},{4,6},{5,7},{6,4},{7,5},{8,10},{9,11},{10,... | collective-permute-start | bytes 786440 | tf_op jit(solution)/shard_map/ppermute | solution.py:387
  29.2 1.2 %collective-permute-done.7.refs_1_ = bf16[256,512]{1,0:T(8,128)(2,1)S(1)} collective-permute-done((bf16[256,512]{1,0:T(8,128)(2,1)S(1)}, bf16[256,512]{1,0:T(8,128)(2,1)S(1)}, u32[]{:S(2)}, u32[]{:S(2)}) %collective-permute-start.7) | collective-permute-done | bytes 262176 | tf_op jit(solution)/shard_map/ppermute | solution.py:387
  30.4 0.1 shard_map.90
  30.5 1.6 %collective-permute-start.8 = (bf16[64,512]{1,0:T(8,128)(2,1)S(1)}, bf16[64,512]{1,0:T(8,128)(2,1)S(1)}, u32[]{:S(2)}, u32[]{:S(2)}) collective-permute-start(bf16[64,512]{1,0:T(8,128)(2,1)S(1)} %get-tuple-element.40), channel_id=1, source_target_pairs={{0,1},{1,0},{2,3},{3,2},{4,5},{5,4},{6,7},{7,6},{8,9},{9,8},{10,11... | collective-permute-start | bytes 196616 | tf_op jit(solution)/shard_map/ppermute | solution.py:387
  32.1 0.8 %collective-permute-start.9 = (bf16[64,512]{1,0:T(8,128)(2,1)S(1)}, bf16[64,512]{1,0:T(8,128)(2,1)S(1)}, u32[]{:S(2)}, u32[]{:S(2)}) collective-permute-start(bf16[64,512]{1,0:T(8,128)(2,1)S(1)} %get-tuple-element.41), channel_id=1, source_target_pairs={{0,4},{1,5},{2,6},{3,7},{4,0},{5,1},{6,2},{7,3},{8,12},{9,13},{10,... | collective-permute-start | bytes 196616 | tf_op jit(solution)/shard_map/ppermute | solution.py:387
  32.9 1.2 %collective-permute-start.10 = (bf16[64,512]{1,0:T(8,128)(2,1)S(1)}, bf16[64,512]{1,0:T(8,128)(2,1)S(1)}, u32[]{:S(2)}, u32[]{:S(2)}) collective-permute-start(bf16[64,512]{1,0:T(8,128)(2,1)S(1)} %get-tuple-element.42), channel_id=1, source_target_pairs={{0,5},{1,4},{2,7},{3,6},{4,1},{5,0},{6,3},{7,2},{8,13},{9,12},{10,... | collective-permute-start | bytes 196616 | tf_op jit(solution)/shard_map/ppermute | solution.py:387
  34.0 0.9 %collective-permute-done.8.refs_1_ = bf16[64,512]{1,0:T(8,128)(2,1)S(1)} collective-permute-done((bf16[64,512]{1,0:T(8,128)(2,1)S(1)}, bf16[64,512]{1,0:T(8,128)(2,1)S(1)}, u32[]{:S(2)}, u32[]{:S(2)}) %collective-permute-start.8) | collective-permute-done | bytes 65568 | tf_op jit(solution)/shard_map/ppermute | solution.py:387
  34.9 1.9 %collective-permute-done.9.refs_2_ = bf16[64,512]{1,0:T(8,128)(2,1)S(1)} collective-permute-done((bf16[64,512]{1,0:T(8,128)(2,1)S(1)}, bf16[64,512]{1,0:T(8,128)(2,1)S(1)}, u32[]{:S(2)}, u32[]{:S(2)}) %collective-permute-start.9) | collective-permute-done | bytes 65568 | tf_op jit(solution)/shard_map/ppermute | solution.py:387
  36.9 1.2 %collective-permute-done.10.refs_3_ = bf16[64,512]{1,0:T(8,128)(2,1)S(1)} collective-permute-done((bf16[64,512]{1,0:T(8,128)(2,1)S(1)}, bf16[64,512]{1,0:T(8,128)(2,1)S(1)}, u32[]{:S(2)}, u32[]{:S(2)}) %collective-permute-start.10) | collective-permute-done | bytes 65568 | tf_op jit(solution)/shard_map/ppermute | solution.py:387
  38.1 1.5 %collective-permute-start.12 = (bf16[64,512]{1,0:T(8,128)(2,1)S(1)}, bf16[64,512]{1,0:T(8,128)(2,1)S(1)}, u32[]{:S(2)}, u32[]{:S(2)}) collective-permute-start(bf16[64,512]{1,0:T(8,128)(2,1)S(1)} %shard_map.91.refs_4_.refs_0_), channel_id=1, source_target_pairs={{0,8},{1,9},{2,10},{3,11},{4,12},{5,13},{6,14},{7,15},{8,0},{9,1},... | collective-permute-start | bytes 196616 | tf_op jit(solution)/shard_map/ppermute | solution.py:387
  39.5 4.1 %collective-permute-done.6.refs_1_.refs_3_ = bf16[1040,256]{1,0:T(8,128)(2,1)S(1)} collective-permute-done((bf16[1040,256]{1,0:T(8,128)(2,1)S(1)}, bf16[1040,256]{1,0:T(8,128)(2,1)S(1)}, u32[]{:S(2)}, u32[]{:S(2)}) %collective-permute-start.6) | collective-permute-done | bytes 532512 | tf_op jit(solution)/shard_map/ppermute | solution.py:31
  43.6 0.2 shard_map.92
  43.8 0.9 %collective-permute-start.14 = (bf16[2,256,256]{2,1,0:T(8,128)(2,1)S(1)}, bf16[2,256,256]{2,1,0:T(8,128)(2,1)S(1)}, u32[]{:S(2)}, u32[]{:S(2)}) collective-permute-start(bf16[2,256,256]{2,1,0:T(8,128)(2,1)S(1)} %get-tuple-element.44.refs_2_), channel_id=1, source_target_pairs={{6,0},{0,2},{2,4},{4,6},{14,8},{8,10},{10,12},{12,14},{22,16},{16,... | collective-permute-start | bytes 786440 | tf_op jit(solution)/shard_map/ppermute | solution.py:31
  44.7 1.3 %collective-permute-done.12.refs_1_ = bf16[64,512]{1,0:T(8,128)(2,1)S(1)} collective-permute-done((bf16[64,512]{1,0:T(8,128)(2,1)S(1)}, bf16[64,512]{1,0:T(8,128)(2,1)S(1)}, u32[]{:S(2)}, u32[]{:S(2)}) %collective-permute-start.12) | collective-permute-done | bytes 65568 | tf_op jit(solution)/shard_map/ppermute | solution.py:387
  46.0 0.7 %collective-permute-start.13 = (bf16[64,512]{1,0:T(8,128)(2,1)S(1)}, bf16[64,512]{1,0:T(8,128)(2,1)S(1)}, u32[]{:S(2)}, u32[]{:S(2)}) collective-permute-start(bf16[64,512]{1,0:T(8,128)(2,1)S(1)} %shard_map.93.refs_3_.refs_0_), channel_id=1, source_target_pairs={{0,16},{1,17},{2,18},{3,19},{4,20},{5,21},{6,22},{7,23},{8,24},{9,... | collective-permute-start | bytes 196616 | tf_op jit(solution)/shard_map/ppermute | solution.py:387
  46.7 3.1 %collective-permute-done.14.refs_2_ = bf16[2,256,256]{2,1,0:T(8,128)(2,1)S(1)} collective-permute-done((bf16[2,256,256]{2,1,0:T(8,128)(2,1)S(1)}, bf16[2,256,256]{2,1,0:T(8,128)(2,1)S(1)}, u32[]{:S(2)}, u32[]{:S(2)}) %collective-permute-start.14) | collective-permute-done | bytes 262176 | tf_op jit(solution)/shard_map/ppermute | solution.py:31
  49.8 0.1 shard_map.94.refs_2_.refs_1_
  49.9 1.7 %collective-permute-start.16 = (bf16[2,256,256]{2,1,0:T(8,128)(2,1)S(1)}, bf16[2,256,256]{2,1,0:T(8,128)(2,1)S(1)}, u32[]{:S(2)}, u32[]{:S(2)}) collective-permute-start(bf16[2,256,256]{2,1,0:T(8,128)(2,1)S(1)} %shard_map.94.refs_2_.refs_1_), channel_id=1, source_target_pairs={{0,1},{1,0},{2,3},{3,2},{4,5},{5,4},{6,7},{7,6},{8,9},{9,8},{10,11... | collective-permute-start | bytes 786440 | tf_op jit(solution)/shard_map/ppermute | solution.py:479
  51.6 0.5 collective-permute-done.13.refs_1_
  52.1 2.0 %collective-permute-start.19 = (bf16[64,512]{1,0:T(8,128)(2,1)S(1)}, bf16[64,512]{1,0:T(8,128)(2,1)S(1)}, u32[]{:S(2)}, u32[]{:S(2)}) collective-permute-start(bf16[64,512]{1,0:T(8,128)(2,1)S(1)} %shard_map.95.refs_3_.refs_0_), channel_id=1, source_target_pairs={{0,5},{1,4},{2,7},{3,6},{4,1},{5,0},{6,3},{7,2},{8,13},{9,12},{10,... | collective-permute-start | bytes 196616 | tf_op jit(solution)/shard_map/ppermute | solution.py:387
  54.1 1.0 %collective-permute-start.18 = (bf16[64,512]{1,0:T(8,128)(2,1)S(1)}, bf16[64,512]{1,0:T(8,128)(2,1)S(1)}, u32[]{:S(2)}, u32[]{:S(2)}) collective-permute-start(bf16[64,512]{1,0:T(8,128)(2,1)S(1)} %shard_map.95.refs_3_.refs_0_), channel_id=1, source_target_pairs={{0,4},{1,5},{2,6},{3,7},{4,0},{5,1},{6,2},{7,3},{8,12},{9,13},{10,... | collective-permute-start | bytes 196616 | tf_op jit(solution)/shard_map/ppermute | solution.py:387
  55.2 0.5 collective-permute-start.17
  55.7 0.1 shard_map.96.refs_3_.refs_1_
  55.8 1.6 %collective-permute-start.15 = (bf16[2,256,256]{2,1,0:T(8,128)(2,1)S(1)}, bf16[2,256,256]{2,1,0:T(8,128)(2,1)S(1)}, u32[]{:S(2)}, u32[]{:S(2)}) collective-permute-start(bf16[2,256,256]{2,1,0:T(8,128)(2,1)S(1)} %shard_map.96.refs_3_.refs_1_), channel_id=1, source_target_pairs={{0,1},{1,0},{2,3},{3,2},{4,5},{5,4},{6,7},{7,6},{8,9},{9,8},{10,11... | collective-permute-start | bytes 786440 | tf_op jit(solution)/shard_map/ppermute | solution.py:479
  57.4 3.2 %collective-permute-done.16.refs_2_ = bf16[2,256,256]{2,1,0:T(8,128)(2,1)S(1)} collective-permute-done((bf16[2,256,256]{2,1,0:T(8,128)(2,1)S(1)}, bf16[2,256,256]{2,1,0:T(8,128)(2,1)S(1)}, u32[]{:S(2)}, u32[]{:S(2)}) %collective-permute-start.16) | collective-permute-done | bytes 262176 | tf_op jit(solution)/shard_map/ppermute | solution.py:479
  60.6 0.8 %shard_map.97 = (bf16[1,2,2,256,256]{4,3,2,1,0:T(8,128)(2,1)}, f32[8,128]{1,0:T(8,128)S(1)}) custom-call(bf16[2,256,256]{2,1,0:T(8,128)(2,1)S(1)} %get-tuple-element.28.refs_2_.refs_0_, bf16[2,256,256]{2,1,0:T(8,128)(2,1)S(1)} %shard_map.94.refs_2_.refs_1_, bf16[2,256,256]{2,1,0:T(8,128)(2,1)S(1)} %collective-permute-done.16.refs_2_, ...), custom_call_target="tpu_custom_call" | custom-call | flops 15000131584 | bytes 1048576 | tf_op jit(solution)/shard_map/pallas_call | solution.py:298
  61.4 0.6 collective-permute-done.17.refs_1_
  62.0 0.1 shard_map.98.refs_4_.refs_0_
  62.0 0.1 collective-permute-start.20
  62.1 4.2 %collective-permute-done.15.refs_2_ = bf16[2,256,256]{2,1,0:T(8,128)(2,1)S(1)} collective-permute-done((bf16[2,256,256]{2,1,0:T(8,128)(2,1)S(1)}, bf16[2,256,256]{2,1,0:T(8,128)(2,1)S(1)}, u32[]{:S(2)}, u32[]{:S(2)}) %collective-permute-start.15) | collective-permute-done | bytes 262176 | tf_op jit(solution)/shard_map/ppermute | solution.py:479
  66.4 0.8 %shard_map.99 = (bf16[1,2,2,256,256]{4,3,2,1,0:T(8,128)(2,1)}, f32[8,128]{1,0:T(8,128)S(1)}) custom-call(bf16[2,256,256]{2,1,0:T(8,128)(2,1)S(1)} %get-tuple-element.51.refs_4_.refs_2_.refs_0_, bf16[2,256,256]{2,1,0:T(8,128)(2,1)S(1)} %shard_map.96.refs_3_.refs_1_, ...), custom_call_target="tpu_custom_call", output_to_operand_aliasing={{0}: (3, {})} | custom-call | flops 4000131072 | bytes 1048576 | tf_op jit(solution)/shard_map/pallas_call | solution.py:298
  67.2 1.2 %shard_map.100 = f32[2048,128]{1,0:T(8,128)} custom-call(bf16[256,512]{1,0:T(8,128)(2,1)S(1)} %shard_map.98.refs_4_.refs_0_, bf16[256,512]{1,0:T(8,128)(2,1)S(1)} %collective-permute-done.20.refs_1_, f32[2048,128]{1,0:T(8,128)S(1)} %bitcast.16, f32[8,128]{1,0:T(8,128)S(1)} %get-tuple-element.49.refs_3_), custom_call_target="tpu_custom_call" | custom-call | flops 1000000 | bytes 2621440 | tf_op jit(solution)/shard_map/pallas_call | solution.py:281
  (20 shorter events, 0.1 us)
Async XLA Ops:
  0.6 7.6 %copy-start.2 = (bf16[1,1,2,256,256]{4,3,2,1,0:T(8,128)(2,1)S(1)}, bf16[1,1,2,256,256]{4,3,2,1,0:T(8,128)(2,1)}, u32[]{:S(2)}) copy-start(bf16[1,1,2,256,256]{4,3,2,1,0:T(8,128)(2,1)} %refs_3_.1) | copy-start | bytes 786436
  0.6 17.8 %copy-start = (f32[2,256,2,256]{3,2,1,0:T(2,128)S(1)}, f32[2,256,2,256]{3,2,1,0:T(2,128)}, u32[]{:S(2)}) copy-start(f32[2,256,2,256]{3,2,1,0:T(2,128)} %param.8) | copy-start | bytes 3145732
  1.8 16.7 %copy-start.1 = (bf16[512,512]{1,0:T(8,128)(2,1)S(1)}, bf16[512,512]{1,0:T(8,128)(2,1)}, u32[]{:S(2)}) copy-start(bf16[512,512]{1,0:T(8,128)(2,1)} %constant.10.refs_1_) | copy-start | bytes 1572868
  1.8 11.8 %collective-permute-start.4 = (bf16[2,256,256]{2,1,0:T(8,128)(2,1)S(1)}, bf16[2,256,256]{2,1,0:T(8,128)(2,1)S(1)}, u32[]{:S(2)}, u32[]{:S(2)}) collective-permute-start(bf16[2,256,256]{2,1,0:T(8,128)(2,1)S(1)} %get-tuple-element.51.refs_4_.refs_2_.refs_0_), channel_id=1, source_target_pairs={{8,0},{10,2},{12,4},{14,6},{16,8},{18,10},{20,12},{22,14},{24,16},... | collective-permute-start | bytes 786440 | tf_op jit(solution)/shard_map/ppermute | solution.py:31
  6.9 12.8 %collective-permute-start.1 = (bf16[2,2,256,256]{3,2,1,0:T(8,128)(2,1)}, bf16[2,2,256,256]{3,2,1,0:T(8,128)(2,1)S(1)}, u32[]{:S(2)}, u32[]{:S(2)}) collective-permute-start(bf16[2,2,256,256]{3,2,1,0:T(8,128)(2,1)} %bitcast.18), channel_id=1, source_target_pairs={{2,0},{4,2},{6,4},{0,6},{10,8},{12,10},{14,12},{8,14},{18,16},{20,... | collective-permute-start | bytes 1572872 | tf_op jit(solution)/shard_map/ppermute | solution.py:31
  8.2 0.7 copy-start.3
  9.5 8.6 %collective-permute-start.2 = (bf16[2,256,256]{2,1,0:T(8,128)(2,1)S(1)}, bf16[2,256,256]{2,1,0:T(8,128)(2,1)S(1)}, u32[]{:S(2)}, u32[]{:S(2)}) collective-permute-start(bf16[2,256,256]{2,1,0:T(8,128)(2,1)S(1)} %get-tuple-element.28.refs_2_.refs_0_), channel_id=1, source_target_pairs={{8,0},{10,2},{12,4},{14,6},{16,8},{18,10},{20,12},{22,14},{24,16},... | collective-permute-start | bytes 786440 | tf_op jit(solution)/shard_map/ppermute | solution.py:31
  13.6 6.1 %collective-permute-start.5 = (bf16[2,256,256]{2,1,0:T(8,128)(2,1)S(1)}, bf16[2,256,256]{2,1,0:T(8,128)(2,1)S(1)}, u32[]{:S(2)}, u32[]{:S(2)}) collective-permute-start(bf16[2,256,256]{2,1,0:T(8,128)(2,1)S(1)} %collective-permute-done.4.refs_4_), channel_id=1, source_target_pairs={{2,0},{4,2},{6,4},{0,6},{10,8},{12,10},{14,12},{8,14},{18,16},{20,... | collective-permute-start | bytes 786440 | tf_op jit(solution)/shard_map/ppermute | solution.py:31
  13.7 6.1 %collective-permute-start = (bf16[272,256]{1,0:T(8,128)(2,1)S(1)}, bf16[272,256]{1,0:T(8,128)(2,1)S(1)}, u32[]{:S(2)}, u32[]{:S(2)}) collective-permute-start(bf16[272,256]{1,0:T(8,128)(2,1)S(1)} %get-tuple-element.27), channel_id=1, source_target_pairs={{0,1},{1,0},{2,3},{3,2},{4,5},{5,4},{6,7},{7,6},{8,9},{9,8},{10,11... | collective-permute-start | bytes 417800 | tf_op jit(solution)/shard_map/ppermute | solution.py:451
  18.1 4.2 %collective-permute-start.3 = (bf16[2,256,256]{2,1,0:T(8,128)(2,1)S(1)}, bf16[2,256,256]{2,1,0:T(8,128)(2,1)S(1)}, u32[]{:S(2)}, u32[]{:S(2)}) collective-permute-start(bf16[2,256,256]{2,1,0:T(8,128)(2,1)S(1)} %collective-permute-done.2.refs_4_), channel_id=1, source_target_pairs={{2,0},{4,2},{6,4},{0,6},{10,8},{12,10},{14,12},{8,14},{18,16},{20,... | collective-permute-start | bytes 786440 | tf_op jit(solution)/shard_map/ppermute | solution.py:31
  19.7 2.6 %copy-start.4 = (bf16[512,512]{1,0:T(8,128)(2,1)S(1)}, bf16[512,512]{1,0:T(8,128)(2,1)}, u32[]{:S(2)}) copy-start(bf16[512,512]{1,0:T(8,128)(2,1)} %constant.11.refs_10_) | copy-start | bytes 1572868
  27.5 16.1 %collective-permute-start.6 = (bf16[1040,256]{1,0:T(8,128)(2,1)S(1)}, bf16[1040,256]{1,0:T(8,128)(2,1)S(1)}, u32[]{:S(2)}, u32[]{:S(2)}) collective-permute-start(bf16[1040,256]{1,0:T(8,128)(2,1)S(1)} %get-tuple-element.34), channel_id=1, source_target_pairs={{24,0},{26,2},{28,4},{30,6},{0,8},{2,10},{4,12},{6,14},{8,16},{10,... | collective-permute-start | bytes 1597448 | tf_op jit(solution)/shard_map/ppermute | solution.py:31
  27.8 2.6 %collective-permute-start.7 = (bf16[256,512]{1,0:T(8,128)(2,1)S(1)}, bf16[256,512]{1,0:T(8,128)(2,1)S(1)}, u32[]{:S(2)}, u32[]{:S(2)}) collective-permute-start(bf16[256,512]{1,0:T(8,128)(2,1)S(1)} %get-tuple-element.38), channel_id=1, source_target_pairs={{0,2},{1,3},{2,0},{3,1},{4,6},{5,7},{6,4},{7,5},{8,10},{9,11},{10,... | collective-permute-start | bytes 786440 | tf_op jit(solution)/shard_map/ppermute | solution.py:387
  30.5 4.4 %collective-permute-start.8 = (bf16[64,512]{1,0:T(8,128)(2,1)S(1)}, bf16[64,512]{1,0:T(8,128)(2,1)S(1)}, u32[]{:S(2)}, u32[]{:S(2)}) collective-permute-start(bf16[64,512]{1,0:T(8,128)(2,1)S(1)} %get-tuple-element.40), channel_id=1, source_target_pairs={{0,1},{1,0},{2,3},{3,2},{4,5},{5,4},{6,7},{7,6},{8,9},{9,8},{10,11... | collective-permute-start | bytes 196616 | tf_op jit(solution)/shard_map/ppermute | solution.py:387
  32.1 4.8 %collective-permute-start.9 = (bf16[64,512]{1,0:T(8,128)(2,1)S(1)}, bf16[64,512]{1,0:T(8,128)(2,1)S(1)}, u32[]{:S(2)}, u32[]{:S(2)}) collective-permute-start(bf16[64,512]{1,0:T(8,128)(2,1)S(1)} %get-tuple-element.41), channel_id=1, source_target_pairs={{0,4},{1,5},{2,6},{3,7},{4,0},{5,1},{6,2},{7,3},{8,12},{9,13},{10,... | collective-permute-start | bytes 196616 | tf_op jit(solution)/shard_map/ppermute | solution.py:387
  32.9 5.2 %collective-permute-start.10 = (bf16[64,512]{1,0:T(8,128)(2,1)S(1)}, bf16[64,512]{1,0:T(8,128)(2,1)S(1)}, u32[]{:S(2)}, u32[]{:S(2)}) collective-permute-start(bf16[64,512]{1,0:T(8,128)(2,1)S(1)} %get-tuple-element.42), channel_id=1, source_target_pairs={{0,5},{1,4},{2,7},{3,6},{4,1},{5,0},{6,3},{7,2},{8,13},{9,12},{10,... | collective-permute-start | bytes 196616 | tf_op jit(solution)/shard_map/ppermute | solution.py:387
  38.1 7.9 %collective-permute-start.12 = (bf16[64,512]{1,0:T(8,128)(2,1)S(1)}, bf16[64,512]{1,0:T(8,128)(2,1)S(1)}, u32[]{:S(2)}, u32[]{:S(2)}) collective-permute-start(bf16[64,512]{1,0:T(8,128)(2,1)S(1)} %shard_map.91.refs_4_.refs_0_), channel_id=1, source_target_pairs={{0,8},{1,9},{2,10},{3,11},{4,12},{5,13},{6,14},{7,15},{8,0},{9,1},... | collective-permute-start | bytes 196616 | tf_op jit(solution)/shard_map/ppermute | solution.py:387
  43.8 6.0 %collective-permute-start.14 = (bf16[2,256,256]{2,1,0:T(8,128)(2,1)S(1)}, bf16[2,256,256]{2,1,0:T(8,128)(2,1)S(1)}, u32[]{:S(2)}, u32[]{:S(2)}) collective-permute-start(bf16[2,256,256]{2,1,0:T(8,128)(2,1)S(1)} %get-tuple-element.44.refs_2_), channel_id=1, source_target_pairs={{6,0},{0,2},{2,4},{4,6},{14,8},{8,10},{10,12},{12,14},{22,16},{16,... | collective-permute-start | bytes 786440 | tf_op jit(solution)/shard_map/ppermute | solution.py:31
  46.0 6.1 %collective-permute-start.13 = (bf16[64,512]{1,0:T(8,128)(2,1)S(1)}, bf16[64,512]{1,0:T(8,128)(2,1)S(1)}, u32[]{:S(2)}, u32[]{:S(2)}) collective-permute-start(bf16[64,512]{1,0:T(8,128)(2,1)S(1)} %shard_map.93.refs_3_.refs_0_), channel_id=1, source_target_pairs={{0,16},{1,17},{2,18},{3,19},{4,20},{5,21},{6,22},{7,23},{8,24},{9,... | collective-permute-start | bytes 196616 | tf_op jit(solution)/shard_map/ppermute | solution.py:387
  46.7 9.0 %collective-permute-start.11 = (bf16[2,256,256]{2,1,0:T(8,128)(2,1)S(1)}, bf16[2,256,256]{2,1,0:T(8,128)(2,1)S(1)}, u32[]{:S(2)}, u32[]{:S(2)}) collective-permute-start(bf16[2,256,256]{2,1,0:T(8,128)(2,1)S(1)} %get-tuple-element.43), channel_id=1, source_target_pairs={{6,0},{0,2},{2,4},{4,6},{14,8},{8,10},{10,12},{12,14},{22,16},{16,... | collective-permute-start | bytes 786440 | tf_op jit(solution)/shard_map/ppermute | solution.py:31
  49.9 10.7 %collective-permute-start.16 = (bf16[2,256,256]{2,1,0:T(8,128)(2,1)S(1)}, bf16[2,256,256]{2,1,0:T(8,128)(2,1)S(1)}, u32[]{:S(2)}, u32[]{:S(2)}) collective-permute-start(bf16[2,256,256]{2,1,0:T(8,128)(2,1)S(1)} %shard_map.94.refs_2_.refs_1_), channel_id=1, source_target_pairs={{0,1},{1,0},{2,3},{3,2},{4,5},{5,4},{6,7},{7,6},{8,9},{9,8},{10,11... | collective-permute-start | bytes 786440 | tf_op jit(solution)/shard_map/ppermute | solution.py:479
  52.1 9.3 %collective-permute-start.19 = (bf16[64,512]{1,0:T(8,128)(2,1)S(1)}, bf16[64,512]{1,0:T(8,128)(2,1)S(1)}, u32[]{:S(2)}, u32[]{:S(2)}) collective-permute-start(bf16[64,512]{1,0:T(8,128)(2,1)S(1)} %shard_map.95.refs_3_.refs_0_), channel_id=1, source_target_pairs={{0,5},{1,4},{2,7},{3,6},{4,1},{5,0},{6,3},{7,2},{8,13},{9,12},{10,... | collective-permute-start | bytes 196616 | tf_op jit(solution)/shard_map/ppermute | solution.py:387
  54.1 7.3 %collective-permute-start.18 = (bf16[64,512]{1,0:T(8,128)(2,1)S(1)}, bf16[64,512]{1,0:T(8,128)(2,1)S(1)}, u32[]{:S(2)}, u32[]{:S(2)}) collective-permute-start(bf16[64,512]{1,0:T(8,128)(2,1)S(1)} %shard_map.95.refs_3_.refs_0_), channel_id=1, source_target_pairs={{0,4},{1,5},{2,6},{3,7},{4,0},{5,1},{6,2},{7,3},{8,12},{9,13},{10,... | collective-permute-start | bytes 196616 | tf_op jit(solution)/shard_map/ppermute | solution.py:387
  55.2 6.8 %collective-permute-start.17 = (bf16[64,512]{1,0:T(8,128)(2,1)S(1)}, bf16[64,512]{1,0:T(8,128)(2,1)S(1)}, u32[]{:S(2)}, u32[]{:S(2)}) collective-permute-start(bf16[64,512]{1,0:T(8,128)(2,1)S(1)} %shard_map.95.refs_3_.refs_0_), channel_id=1, source_target_pairs={{0,1},{1,0},{2,3},{3,2},{4,5},{5,4},{6,7},{7,6},{8,9},{9,8},{10,11... | collective-permute-start | bytes 196616 | tf_op jit(solution)/shard_map/ppermute | solution.py:387
  55.8 10.6 %collective-permute-start.15 = (bf16[2,256,256]{2,1,0:T(8,128)(2,1)S(1)}, bf16[2,256,256]{2,1,0:T(8,128)(2,1)S(1)}, u32[]{:S(2)}, u32[]{:S(2)}) collective-permute-start(bf16[2,256,256]{2,1,0:T(8,128)(2,1)S(1)} %shard_map.96.refs_3_.refs_1_), channel_id=1, source_target_pairs={{0,1},{1,0},{2,3},{3,2},{4,5},{5,4},{6,7},{7,6},{8,9},{9,8},{10,11... | collective-permute-start | bytes 786440 | tf_op jit(solution)/shard_map/ppermute | solution.py:479
  62.0 5.2 %collective-permute-start.20 = (bf16[256,512]{1,0:T(8,128)(2,1)S(1)}, bf16[256,512]{1,0:T(8,128)(2,1)S(1)}, u32[]{:S(2)}, u32[]{:S(2)}) collective-permute-start(bf16[256,512]{1,0:T(8,128)(2,1)S(1)} %shard_map.98.refs_4_.refs_0_), channel_id=1, source_target_pairs={{0,2},{1,3},{2,0},{3,1},{4,6},{5,7},{6,4},{7,5},{8,10},{9,11},{10,... | collective-permute-start | bytes 786440 | tf_op jit(solution)/shard_map/ppermute | solution.py:387

commit v11 on v10

--- a/solution.py
+++ b/solution.py
@@ -15,7 +15,7 @@
 object_rate = 0.05
 probe_rate = 0.15
 
-LATE = [0, 8_000_000_000, 0, 30_000_000_000, 0, 15_000_000_000, 0, 4_000_000_000]
+LATE = [0, 0, 5_000_000_000, 5_000_000_000, 0, 0, 15_000_000_000, 0, 4_000_000_000]
 
 f32 = jnp.float32
 bf16 = jnp.bfloat16
@@ -150,8 +150,8 @@
         arrive_ref[1, :, lanes] = -a_neg
 
 
-def spread(shifts, grad, home_ref, next_ref, down_ref, layer):
-    rows_t, cols_t = shifts[2:4]
+def spread(shifts, grad, home_ref, next_ref, down_ref):
+    rows_t, cols_t, col = shifts[2:5]
     n = rows_t.shape[1]
     wrap_cols = cols_t[:, :n] + cols_t[:, n:]
     for part in range(2):
@@ -159,14 +159,20 @@
         wide = dot(rows[:n], cols_t).astype(bf16)
         home_ref[part] = wide[:, :n]
         next_ref[part] = wide[:, n:]
-        where = pl.ds((2 * layer + part) * n, n)
-        down_ref[where, :] = dot(rows[n:], wrap_cols).astype(bf16)
+        down_ref[pl.ds(part * n, n), :] = dot(rows[n:], wrap_cols).astype(bf16)
+    edge = lax.broadcasted_iota(jnp.int32, (16, n), 1) < col
+    down_ref[pl.ds(2 * n, 16), :] = edge.astype(f32).astype(bf16)
+
+
+def spread_kernel(mine_ref, sent_ref, grad_ref, home_ref, next_ref, down_ref):
+    shifts = shift_tables(mine_ref, sent_ref)
+    spread(shifts, [grad_ref[part] for part in range(2)], home_ref, next_ref, down_ref)
 
 
 def gradient_kernel(
     mine_ref, sent_ref, own_ref, right_ref, below_ref, diag_ref, near_ref, arrive_ref, planes_ref,
     prop_ref, dft_ref,
-    home0_ref, next0_ref, home1_ref, next1_ref, down_ref, keep_ref, give_ref, term_ref,
+    home_ref, next_ref, down_ref, grad_ref, keep_ref, give_ref, term_ref,
 ):
     n = own_ref.shape[1]
     modes = planes_ref.shape[2] // n
@@ -193,7 +199,7 @@
         grad[0] += a_re * b_re + a_im * b_im
         grad[1] += a_re * b_im - a_im * b_re
         waves.append(stacked(far[0] * b_re + far[1] * b_im, far[1] * b_re - far[0] * b_im))
-    spread(shifts, grad, home1_ref, next1_ref, down_ref, 1)
+    spread(shifts, grad, home_ref, next_ref, down_ref)
     grad = [0.0, 0.0]
     near = [near_ref[part].astype(f32) for part in range(2)]
     for mode in range(modes):
@@ -207,26 +213,24 @@
     core = place_of(core_group())
     keep_ref[...] = term_ref[core]
     give_ref[...] = term_ref[1 - core]
-    spread(shifts, grad, home0_ref, next0_ref, down_ref, 0)
-    edge = lax.broadcasted_iota(jnp.int32, (16, n), 1) < shifts[4]
-    down_ref[pl.ds(4 * n, 16), :] = edge.astype(f32).astype(bf16)
-
-
-def above_parts(above_ref, layer, n):
-    where = [pl.ds((2 * layer + part) * n, n) for part in range(2)]
-    split = above_ref[pl.ds(4 * n, 16), :].astype(f32)[0:1] > 0
-    return [above_ref[rows, :].astype(f32) for rows in where], split
-
-
-def beside_kernel(layer, next_ref, above_ref, out_ref):
-    above, split = above_parts(above_ref, layer, out_ref.shape[1])
+    for part in range(2):
+        grad_ref[part] = grad[part].astype(bf16)
+
+
+def above_parts(above_ref, n):
+    parts = [above_ref[pl.ds(part * n, n), :].astype(f32) for part in range(2)]
+    return parts, above_ref[pl.ds(2 * n, 16), :].astype(f32)[0:1] > 0
+
+
+def beside_kernel(next_ref, above_ref, out_ref):
+    above, split = above_parts(above_ref, out_ref.shape[1])
     for part in range(2):
         total = next_ref[part].astype(f32) + jnp.where(split, above[part], 0.0)
         out_ref[part] = total.astype(bf16)
 
 
-def part_kernel(layer, home_ref, above_ref, left_ref, out_ref):
-    above, split = above_parts(above_ref, layer, out_ref.shape[1])
+def part_kernel(home_ref, above_ref, left_ref, out_ref):
+    above, split = above_parts(above_ref, out_ref.shape[1])
     for part in range(2):
         total = home_ref[part].astype(f32) + jnp.where(split, 0.0, above[part])
         out_ref[part] = (total + left_ref[part].astype(f32)).astype(bf16)
@@ -463,10 +467,11 @@
         limit=16,
     )
     half = shape_of(bf16, pixels, width)
-    home0, next0, home1, next1, down, keep, give = run(
+    down = shape_of(bf16, 2 * pixels + 16, pixels)
+    home1, next1, down1, grad0, keep, give = run(
         job(
             gradient_kernel,
-            [tile] * 4 + [shape_of(bf16, 4 * pixels + 16, pixels), half, half],
+            [tile, tile, down, tile, half, half],
             [mine, sent, own1, right, below1, diag1, near, arrive, probe_planes, table, dft],
             scratch=[pltpu.VMEM((2, pixels, width), bf16)],
         ),
@@ -479,49 +484,52 @@
             return lax.ppermute(part, "pos", [(0, 1), (1, 0)])
         return lax.psum(part.astype(f32), "pos") - part.astype(f32)
 
-    def beside(layer, next_tile):
-        kernel = lambda *refs: beside_kernel(layer, *refs)
-        return job(kernel, [tile], [next_tile, above])
-
-    def part(layer, home, left):
-        kernel = lambda *refs: part_kernel(layer, *refs)
-        return job(kernel, [tile], [home, above, left])
+    def beside(next_tile, above):
+        return job(beside_kernel, [tile], [next_tile, above])
+
+    def part(home, above, left):
+        return job(part_kernel, [tile], [home, above, left])
 
     core, groups = core_group(), exchange_groups()
-    above = from_behind(down, 1, 0)
+    above1 = from_behind(down1, 1, 0)
     arrived = [swap_with(give, core, 1)]
+    side = [job(spread_kernel, [tile, tile, down], [mine, sent, grad0])]
     scattered = []
     while len(groups) > 1 and keep.shape[0] >> len(groups[0]) >= 16:
         group, groups = groups[0], groups[1:]
-        keep, *gives = run(folded(group, keep, arrived))
+        done = run(folded(group, keep, arrived), *side, limit=8)
+        if side:
+            done, (home0, next0, down0) = done
+            above0 = from_behind(down0, 1, 0)
+            side = []
+        keep, *gives = done
         arrived = [swap_with(x, group, at) for at, x in enumerate(gives, 1)]
         scattered.append(group)
     first, second, *others = [[bit] for group in groups for bit in group]
     (total,) = run(added(keep, arrived))
     arrived = swapped(total, first)
-    (beside1,), (beside0,) = run(
-        beside(1, next1), beside(0, next0), after=[total], flops=LATE[0]
-    )
+    (beside1,) = run(beside(next1, above1), after=[total], flops=LATE[0])
     left1 = from_behind(beside1, 0, 1)
+    (part1,) = run(part(home1, above1, left1), flops=LATE[1])
+    other1 = over_owners(part1)
+    (beside0,) = run(beside(next0, above0), after=[part1], flops=LATE[2])
     left0 = from_behind(beside0, 0, 1)
-    (total,) = run(added(total, arrived), after=[beside1], flops=LATE[1])
+    (total,) = run(added(total, arrived), after=[beside0], flops=LATE[3])
     arrived = swapped(total, second)
-    (part1,) = run(part(1, home1, left1), after=[total], flops=LATE[2])
-    other1 = over_owners(part1)
-    (total,) = run(added(total, arrived), after=[part1], flops=LATE[3])
+    (total,) = run(added(total, arrived), flops=LATE[4])
     for group in others:
         (total,) = run(added(total, swapped(total, group)))
     arrived = swapped(total, scattered[-1])
-    (part0,) = run(part(0, home0, left0), after=[total], flops=LATE[4])
+    (part0,) = run(part(home0, above0, left0), after=[total], flops=LATE[5])
     other0 = over_owners(part0)
     like = shape_of(bf16, *tile_object.shape)
-    new_object, token = updated(1, own1, part1, other1, like, flops=LATE[5], after=[part0])
-    (total,) = run(joined(scattered[-1], total, arrived), after=[token], flops=LATE[6])
+    new_object, token = updated(1, own1, part1, other1, like, flops=LATE[6], after=[part0])
+    (total,) = run(joined(scattered[-1], total, arrived), after=[token], flops=LATE[7])
     for group in reversed(scattered[:-1]):
         (total,) = run(joined(group, total, swapped(total, group)))
     other_half = swap_with(total, core, 1)
     new_object, token = updated(
-        0, own[0], part0, other0, like, so_far=new_object, flops=LATE[7], after=[total]
+        0, own[0], part0, other0, like, so_far=new_object, flops=LATE[8], after=[total]
     )
     positions_all = lax.axis_size("tile") * lax.axis_size("pos") * (patterns.shape[2] // 2)
     step = probe_rate / math.sqrt(positions_all)

time: 68.6 us -> 68.5 us (level)
  starting transfers between devices: 23.3 us -> 21.3 us
  waiting for transfers between devices: 30.7 us -> 32.5 us
    ppermute x10, waiting for transfers between devices: 7.48 us -> 11.6 us  [swap_with(): lax.ppermute(x, ('tile', 'pos'), [(i, i ^ mask) for i in range(devices)])]
    ppermute x2, waiting for transfers between devices: 7.45 us -> 4.71 us  [over_owners(): return lax.ppermute(part, 'pos', [(0, 1), (1, 0)])]
    ppermute x10, starting transfers between devices: 10.8 us -> 9.42 us  [swap_with(): lax.ppermute(x, ('tile', 'pos'), [(i, i ^ mask) for i in range(devices)])]
    ppermute x2, starting transfers between devices: 3.24 us -> 2.29 us  [over_owners(): return lax.ppermute(part, 'pos', [(0, 1), (1, 0)])]
    ppermute x8 -> x9, waiting for transfers between devices: 14.6 us -> 15.1 us  [from_behind(): return lax.ppermute(block, 'tile', [(source(i), i) for i in range(tiles)])]
    ppermute x8 -> x9, starting transfers between devices: 7.73 us -> 8.04 us  [from_behind(): return lax.ppermute(block, 'tile', [(source(i), i) for i in range(tiles)])]
    pallas_call x13 -> x14, Pallas kernels: 9.46 us -> 9.55 us  [run(): pl.pallas_call(body, out_shape=sum(outs, []), in_specs=sum(specs, []) + [...]
  transfers between devices with their start and end apart: 21 -> 22, of which waited for: 15 -> 13; matrix products, arithmetic and copies ran while one was open for 0% -> 0% of each run, Pallas kernels for 7% -> 8%
where the time goes in v11:
time: 68.5 us; the launch traced here: 68.3 us
  waiting for transfers between devices  32.5 us (47%)
  starting transfers between devices  21.3 us (31%)
  Pallas kernels  11.2 us (16%)
  local copies, waits for them, and re-layouts  1.86 us (3%)
  between operations  1.47 us (2%)
    ppermute x9, waiting for transfers between devices, from_behind(): return lax.ppermute(block, 'tile', [(source(i), i) for i in range(tiles)])  15.1 us
    ppermute x10, waiting for transfers between devices, swap_with(): lax.ppermute(x, ('tile', 'pos'), [(i, i ^ mask) for i in range(devices)])  11.6 us
    pallas_call x14, Pallas kernels, run(): pl.pallas_call(body, out_shape=sum(outs, []), in_specs=sum(specs, []) + [...  9.55 us
    ppermute x10, starting transfers between devices, swap_with(): lax.ppermute(x, ('tile', 'pos'), [(i, i ^ mask) for i in range(devices)])  9.42 us
    ppermute x9, starting transfers between devices, from_behind(): return lax.ppermute(block, 'tile', [(source(i), i) for i in range(tiles)])  8.04 us
    ppermute x2, waiting for transfers between devices, over_owners(): return lax.ppermute(part, 'pos', [(0, 1), (1, 0)])  4.71 us
    ppermute x2, starting transfers between devices, over_owners(): return lax.ppermute(part, 'pos', [(0, 1), (1, 0)])  2.29 us
    pallas_call x2, Pallas kernels, updated(): pl.pallas_call(lambda *refs: update_kernel(layer, *refs), out_shape=[like...  1.65 us
  transfers between devices with their start and end apart: 22, of which 13 were waited for; matrix products, arithmetic and copies ran while one was open for 0% of the time, Pallas kernels for 8%

profile of v11, /device:TPU:0, one launch (start us, length us, event | category | flops | bytes accessed | tf_op | source)
XLA Modules:
  0.0 68.3 jit_solution(11183371704277871176)
XLA Ops:
  0.6 1.2 %slice_bitcast_fusion = (bf16[2,256,256]{2,1,0:T(8,128)(2,1)S(1)}, bf16[2,256,256]{2,1,0:T(8,128)(2,1)S(1)}) fusion(bf16[1,2,2,256,256]{4,3,2,1,0:T(8,128)(2,1)} %param.7), kind=kLoop, calls=%fused_computation | loop fusion | bytes 1048576 | tf_op jit(solution)/shard_map/squeeze | solution.py:433
  1.8 5.1 %collective-permute-start.4 = (bf16[2,256,256]{2,1,0:T(8,128)(2,1)S(1)}, bf16[2,256,256]{2,1,0:T(8,128)(2,1)S(1)}, u32[]{:S(2)}, u32[]{:S(2)}) collective-permute-start(bf16[2,256,256]{2,1,0:T(8,128)(2,1)S(1)} %get-tuple-element.51.refs_4_.refs_2_.refs_0_), channel_id=1, source_target_pairs={{8,0},{10,2},{12,4},{14,6},{16,8},{18,10},{20,12},{22,14},{24,16},... | collective-permute-start | bytes 786440 | tf_op jit(solution)/shard_map/ppermute | solution.py:31
  6.9 0.7 collective-permute-start.1
  8.3 0.7 copy-done.3
  8.9 0.6 shard_map.86
  9.5 0.5 collective-permute-start.2
  10.0 3.6 %collective-permute-done.4.refs_4_ = bf16[2,256,256]{2,1,0:T(8,128)(2,1)S(1)} collective-permute-done((bf16[2,256,256]{2,1,0:T(8,128)(2,1)S(1)}, bf16[2,256,256]{2,1,0:T(8,128)(2,1)S(1)}, u32[]{:S(2)}, u32[]{:S(2)}) %collective-permute-start.4) | collective-permute-done | bytes 262176 | tf_op jit(solution)/shard_map/ppermute | solution.py:31
  13.7 1.5 %collective-permute-start = (bf16[272,256]{1,0:T(8,128)(2,1)S(1)}, bf16[272,256]{1,0:T(8,128)(2,1)S(1)}, u32[]{:S(2)}, u32[]{:S(2)}) collective-permute-start(bf16[272,256]{1,0:T(8,128)(2,1)S(1)} %get-tuple-element.27), channel_id=1, source_target_pairs={{0,1},{1,0},{2,3},{3,2},{4,5},{5,4},{6,7},{7,6},{8,9},{9,8},{10,11... | collective-permute-start | bytes 417800 | tf_op jit(solution)/shard_map/ppermute | solution.py:455
  15.2 2.9 %collective-permute-done.2.refs_4_ = bf16[2,256,256]{2,1,0:T(8,128)(2,1)S(1)} collective-permute-done((bf16[2,256,256]{2,1,0:T(8,128)(2,1)S(1)}, bf16[2,256,256]{2,1,0:T(8,128)(2,1)S(1)}, u32[]{:S(2)}, u32[]{:S(2)}) %collective-permute-start.2) | collective-permute-done | bytes 262176 | tf_op jit(solution)/shard_map/ppermute | solution.py:31
  18.1 0.3 collective-permute-start.3
  18.5 0.1 shard_map.87
  18.6 1.2 %collective-permute-done.refs_1_.refs_3_ = bf16[272,256]{1,0:T(8,128)(2,1)S(1)} collective-permute-done((bf16[272,256]{1,0:T(8,128)(2,1)S(1)}, bf16[272,256]{1,0:T(8,128)(2,1)S(1)}, u32[]{:S(2)}, u32[]{:S(2)}) %collective-permute-start) | collective-permute-done | bytes 139296 | tf_op jit(solution)/shard_map/ppermute | solution.py:455
  19.7 1.8 %shard_map.88 = (bf16[2,256,256]{2,1,0:T(8,128)(2,1)S(1)}, f32[2,256,512]{2,1,0:T(8,128)S(1)}) custom-call(bf16[272,256]{1,0:T(8,128)(2,1)S(1)} %get-tuple-element.26.refs_0_.refs_2_, bf16[272,256]{1,0:T(8,128)(2,1)S(1)} %collective-permute-done.refs_1_.refs_3_, bf16[2,256,256]{2,1,0:T(8,128)(2,1)S(1)} %get-tuple-element.51.refs_4_.refs_2_.refs_0_, ...), custom_call_target="tpu_custom_call" | custom-call | flops 1500000000 | bytes 4472832 | tf_op jit(solution)/shard_map/pallas_call | solution.py:285
  21.5 0.8 %collective-permute-done.3.refs_5_ = bf16[2,256,256]{2,1,0:T(8,128)(2,1)S(1)} collective-permute-done((bf16[2,256,256]{2,1,0:T(8,128)(2,1)S(1)}, bf16[2,256,256]{2,1,0:T(8,128)(2,1)S(1)}, u32[]{:S(2)}, u32[]{:S(2)}) %collective-permute-start.3) | collective-permute-done | bytes 262176 | tf_op jit(solution)/shard_map/ppermute | solution.py:31
  22.4 4.6 %shard_map.89 = (bf16[2,256,256]{2,1,0:T(8,128)(2,1)S(1)}, bf16[2,256,256]{2,1,0:T(8,128)(2,1)S(1)}, bf16[528,256]{1,0:T(8,128)(2,1)S(1)}, bf16[2,256,256]{2,1,0...) custom-call(bf16[272,256]{1,0:T(8,128)(2,1)S(1)} %get-tuple-element.26.refs_0_.refs_2_, ...), custom_call_target="tpu_custom_call" | custom-call | flops 4000000000 | bytes 6578176 | tf_op jit(solution)/shard_map/pallas_call | solution.py:285
  27.0 1.5 %collective-permute-start.6 = (bf16[256,512]{1,0:T(8,128)(2,1)S(1)}, bf16[256,512]{1,0:T(8,128)(2,1)S(1)}, u32[]{:S(2)}, u32[]{:S(2)}) collective-permute-start(bf16[256,512]{1,0:T(8,128)(2,1)S(1)} %get-tuple-element.34), channel_id=1, source_target_pairs={{0,2},{1,3},{2,0},{3,1},{4,6},{5,7},{6,4},{7,5},{8,10},{9,11},{10,... | collective-permute-start | bytes 786440 | tf_op jit(solution)/shard_map/ppermute | solution.py:391
  28.5 0.5 collective-permute-start.8
  28.9 0.7 %collective-permute-done.6.refs_1_ = bf16[256,512]{1,0:T(8,128)(2,1)S(1)} collective-permute-done((bf16[256,512]{1,0:T(8,128)(2,1)S(1)}, bf16[256,512]{1,0:T(8,128)(2,1)S(1)}, u32[]{:S(2)}, u32[]{:S(2)}) %collective-permute-start.6) | collective-permute-done | bytes 262176 | tf_op jit(solution)/shard_map/ppermute | solution.py:391
  29.6 0.8 %shard_map.90 = (f32[64,512]{1,0:T(8,128)S(1)}, bf16[64,512]{1,0:T(8,128)(2,1)S(1)}, bf16[64,512]{1,0:T(8,128)(2,1)S(1)}, bf16[64,512]{1,0:T(8,128)(2,1)S(1)}, b...) custom-call(bf16[256,512]{1,0:T(8,128)(2,1)S(1)} %get-tuple-element.33.refs_0_, ...), custom_call_target="tpu_custom_call" | custom-call | flops 1000000 | bytes 2187264 | tf_op jit(solution)/shard_map/pallas_call | solution.py:285
  30.4 1.6 %collective-permute-start.9 = (bf16[64,512]{1,0:T(8,128)(2,1)S(1)}, bf16[64,512]{1,0:T(8,128)(2,1)S(1)}, u32[]{:S(2)}, u32[]{:S(2)}) collective-permute-start(bf16[64,512]{1,0:T(8,128)(2,1)S(1)} %get-tuple-element.43), channel_id=1, source_target_pairs={{0,1},{1,0},{2,3},{3,2},{4,5},{5,4},{6,7},{7,6},{8,9},{9,8},{10,11... | collective-permute-start | bytes 196616 | tf_op jit(solution)/shard_map/ppermute | solution.py:391
  32.0 0.9 %collective-permute-start.10 = (bf16[64,512]{1,0:T(8,128)(2,1)S(1)}, bf16[64,512]{1,0:T(8,128)(2,1)S(1)}, u32[]{:S(2)}, u32[]{:S(2)}) collective-permute-start(bf16[64,512]{1,0:T(8,128)(2,1)S(1)} %get-tuple-element.44), channel_id=1, source_target_pairs={{0,4},{1,5},{2,6},{3,7},{4,0},{5,1},{6,2},{7,3},{8,12},{9,13},{10,... | collective-permute-start | bytes 196616 | tf_op jit(solution)/shard_map/ppermute | solution.py:391
  32.9 1.1 %collective-permute-start.11 = (bf16[64,512]{1,0:T(8,128)(2,1)S(1)}, bf16[64,512]{1,0:T(8,128)(2,1)S(1)}, u32[]{:S(2)}, u32[]{:S(2)}) collective-permute-start(bf16[64,512]{1,0:T(8,128)(2,1)S(1)} %get-tuple-element.45), channel_id=1, source_target_pairs={{0,5},{1,4},{2,7},{3,6},{4,1},{5,0},{6,3},{7,2},{8,13},{9,12},{10,... | collective-permute-start | bytes 196616 | tf_op jit(solution)/shard_map/ppermute | solution.py:391
  34.0 0.9 %collective-permute-start.7 = (bf16[528,256]{1,0:T(8,128)(2,1)S(1)}, bf16[528,256]{1,0:T(8,128)(2,1)S(1)}, u32[]{:S(2)}, u32[]{:S(2)}) collective-permute-start(bf16[528,256]{1,0:T(8,128)(2,1)S(1)} %get-tuple-element.37), channel_id=1, source_target_pairs={{24,0},{26,2},{28,4},{30,6},{0,8},{2,10},{4,12},{6,14},{8,16},{10,... | collective-permute-start | bytes 811016 | tf_op jit(solution)/shard_map/ppermute | solution.py:31
  34.8 1.9 %collective-permute-done.10.refs_2_ = bf16[64,512]{1,0:T(8,128)(2,1)S(1)} collective-permute-done((bf16[64,512]{1,0:T(8,128)(2,1)S(1)}, bf16[64,512]{1,0:T(8,128)(2,1)S(1)}, u32[]{:S(2)}, u32[]{:S(2)}) %collective-permute-start.10) | collective-permute-done | bytes 65568 | tf_op jit(solution)/shard_map/ppermute | solution.py:391
  36.8 1.3 %collective-permute-done.11.refs_3_ = bf16[64,512]{1,0:T(8,128)(2,1)S(1)} collective-permute-done((bf16[64,512]{1,0:T(8,128)(2,1)S(1)}, bf16[64,512]{1,0:T(8,128)(2,1)S(1)}, u32[]{:S(2)}, u32[]{:S(2)}) %collective-permute-start.11) | collective-permute-done | bytes 65568 | tf_op jit(solution)/shard_map/ppermute | solution.py:391
  38.1 1.9 %collective-permute-done.8.refs_1_ = bf16[528,256]{1,0:T(8,128)(2,1)S(1)} collective-permute-done((bf16[528,256]{1,0:T(8,128)(2,1)S(1)}, bf16[528,256]{1,0:T(8,128)(2,1)S(1)}, u32[]{:S(2)}, u32[]{:S(2)}) %collective-permute-start.8) | collective-permute-done | bytes 270368 | tf_op jit(solution)/shard_map/ppermute | solution.py:31
  40.0 0.1 shard_map.92
  40.1 0.1 collective-permute-start.12
  40.2 0.1 collective-permute-start.14
  40.2 5.7 %collective-permute-done.12.refs_2_ = bf16[2,256,256]{2,1,0:T(8,128)(2,1)S(1)} collective-permute-done((bf16[2,256,256]{2,1,0:T(8,128)(2,1)S(1)}, bf16[2,256,256]{2,1,0:T(8,128)(2,1)S(1)}, u32[]{:S(2)}, u32[]{:S(2)}) %collective-permute-start.12) | collective-permute-done | bytes 262176 | tf_op jit(solution)/shard_map/ppermute | solution.py:31
  45.9 0.1 shard_map.93.refs_2_.refs_1_
  46.1 1.6 %collective-permute-start.17 = (bf16[2,256,256]{2,1,0:T(8,128)(2,1)S(1)}, bf16[2,256,256]{2,1,0:T(8,128)(2,1)S(1)}, u32[]{:S(2)}, u32[]{:S(2)}) collective-permute-start(bf16[2,256,256]{2,1,0:T(8,128)(2,1)S(1)} %shard_map.93.refs_2_.refs_1_), channel_id=1, source_target_pairs={{0,1},{1,0},{2,3},{3,2},{4,5},{5,4},{6,7},{7,6},{8,9},{9,8},{10,11... | collective-permute-start | bytes 786440 | tf_op jit(solution)/shard_map/ppermute | solution.py:484
  47.7 0.1 shard_map.94.refs_2_
  47.7 0.1 collective-permute-start.13
  47.9 0.7 collective-permute-start.15
  48.5 5.7 %collective-permute-done.15.refs_1_ = bf16[64,512]{1,0:T(8,128)(2,1)S(1)} collective-permute-done((bf16[64,512]{1,0:T(8,128)(2,1)S(1)}, bf16[64,512]{1,0:T(8,128)(2,1)S(1)}, u32[]{:S(2)}, u32[]{:S(2)}) %collective-permute-start.15) | collective-permute-done | bytes 65568 | tf_op jit(solution)/shard_map/ppermute | solution.py:391
  54.2 1.5 %collective-permute-start.20 = (bf16[64,512]{1,0:T(8,128)(2,1)S(1)}, bf16[64,512]{1,0:T(8,128)(2,1)S(1)}, u32[]{:S(2)}, u32[]{:S(2)}) collective-permute-start(bf16[64,512]{1,0:T(8,128)(2,1)S(1)} %shard_map.96.refs_3_.refs_0_), channel_id=1, source_target_pairs={{0,5},{1,4},{2,7},{3,6},{4,1},{5,0},{6,3},{7,2},{8,13},{9,12},{10,... | collective-permute-start | bytes 196616 | tf_op jit(solution)/shard_map/ppermute | solution.py:391
  55.7 0.7 collective-permute-start.19
  56.4 1.4 %collective-permute-start.18 = (bf16[64,512]{1,0:T(8,128)(2,1)S(1)}, bf16[64,512]{1,0:T(8,128)(2,1)S(1)}, u32[]{:S(2)}, u32[]{:S(2)}) collective-permute-start(bf16[64,512]{1,0:T(8,128)(2,1)S(1)} %shard_map.96.refs_3_.refs_0_), channel_id=1, source_target_pairs={{0,1},{1,0},{2,3},{3,2},{4,5},{5,4},{6,7},{7,6},{8,9},{9,8},{10,11... | collective-permute-start | bytes 196616 | tf_op jit(solution)/shard_map/ppermute | solution.py:391
  57.8 0.1 shard_map.97.refs_3_.refs_1_
  57.9 0.7 %collective-permute-start.16 = (bf16[2,256,256]{2,1,0:T(8,128)(2,1)S(1)}, bf16[2,256,256]{2,1,0:T(8,128)(2,1)S(1)}, u32[]{:S(2)}, u32[]{:S(2)}) collective-permute-start(bf16[2,256,256]{2,1,0:T(8,128)(2,1)S(1)} %shard_map.97.refs_3_.refs_1_), channel_id=1, source_target_pairs={{0,1},{1,0},{2,3},{3,2},{4,5},{5,4},{6,7},{7,6},{8,9},{9,8},{10,11... | collective-permute-start | bytes 786440 | tf_op jit(solution)/shard_map/ppermute | solution.py:484
  58.6 0.8 %shard_map.98 = (bf16[1,2,2,256,256]{4,3,2,1,0:T(8,128)(2,1)}, f32[8,128]{1,0:T(8,128)S(1)}) custom-call(bf16[2,256,256]{2,1,0:T(8,128)(2,1)S(1)} %get-tuple-element.28.refs_2_.refs_0_, bf16[2,256,256]{2,1,0:T(8,128)(2,1)S(1)} %shard_map.93.refs_2_.refs_1_, bf16[2,256,256]{2,1,0:T(8,128)(2,1)S(1)} %collective-permute-done.17.refs_2_, ...), custom_call_target="tpu_custom_call" | custom-call | flops 15000131584 | bytes 1048576 | tf_op jit(solution)/shard_map/pallas_call | solution.py:302
  59.4 0.6 collective-permute-done.20.refs_3_
  60.0 1.4 %collective-permute-done.18.refs_1_ = bf16[64,512]{1,0:T(8,128)(2,1)S(1)} collective-permute-done((bf16[64,512]{1,0:T(8,128)(2,1)S(1)}, bf16[64,512]{1,0:T(8,128)(2,1)S(1)}, u32[]{:S(2)}, u32[]{:S(2)}) %collective-permute-start.18) | collective-permute-done | bytes 65568 | tf_op jit(solution)/shard_map/ppermute | solution.py:391
  61.5 0.1 collective-permute-start.21
  61.6 4.7 %collective-permute-done.16.refs_2_ = bf16[2,256,256]{2,1,0:T(8,128)(2,1)S(1)} collective-permute-done((bf16[2,256,256]{2,1,0:T(8,128)(2,1)S(1)}, bf16[2,256,256]{2,1,0:T(8,128)(2,1)S(1)}, u32[]{:S(2)}, u32[]{:S(2)}) %collective-permute-start.16) | collective-permute-done | bytes 262176 | tf_op jit(solution)/shard_map/ppermute | solution.py:484
  66.3 0.8 %shard_map.100 = (bf16[1,2,2,256,256]{4,3,2,1,0:T(8,128)(2,1)}, f32[8,128]{1,0:T(8,128)S(1)}) custom-call(bf16[2,256,256]{2,1,0:T(8,128)(2,1)S(1)} %get-tuple-element.51.refs_4_.refs_2_.refs_0_, bf16[2,256,256]{2,1,0:T(8,128)(2,1)S(1)} %shard_map.97.refs_3_.refs_1_, ...), custom_call_target="tpu_custom_call", output_to_operand_aliasing={{0}: (3, {})} | custom-call | flops 4000131072 | bytes 1048576 | tf_op jit(solution)/shard_map/pallas_call | solution.py:302
  67.1 1.2 %shard_map.101 = f32[2048,128]{1,0:T(8,128)} custom-call(bf16[256,512]{1,0:T(8,128)(2,1)S(1)} %shard_map.99.refs_4_.refs_0_, bf16[256,512]{1,0:T(8,128)(2,1)S(1)} %collective-permute-done.21.refs_1_, f32[2048,128]{1,0:T(8,128)S(1)} %bitcast.16, f32[8,128]{1,0:T(8,128)S(1)} %get-tuple-element.49.refs_3_), custom_call_target="tpu_custom_call" | custom-call | flops 1000000 | bytes 2621440 | tf_op jit(solution)/shard_map/pallas_call | solution.py:285
  (23 shorter events, 0.2 us)
Async XLA Ops:
  0.6 7.6 %copy-start.2 = (bf16[1,1,2,256,256]{4,3,2,1,0:T(8,128)(2,1)S(1)}, bf16[1,1,2,256,256]{4,3,2,1,0:T(8,128)(2,1)}, u32[]{:S(2)}) copy-start(bf16[1,1,2,256,256]{4,3,2,1,0:T(8,128)(2,1)} %refs_3_.1) | copy-start | bytes 786436
  0.6 17.8 %copy-start = (f32[2,256,2,256]{3,2,1,0:T(2,128)S(1)}, f32[2,256,2,256]{3,2,1,0:T(2,128)}, u32[]{:S(2)}) copy-start(f32[2,256,2,256]{3,2,1,0:T(2,128)} %param.8) | copy-start | bytes 3145732
  1.8 16.7 %copy-start.1 = (bf16[512,512]{1,0:T(8,128)(2,1)S(1)}, bf16[512,512]{1,0:T(8,128)(2,1)}, u32[]{:S(2)}) copy-start(bf16[512,512]{1,0:T(8,128)(2,1)} %constant.10.refs_1_) | copy-start | bytes 1572868
  1.8 11.8 %collective-permute-start.4 = (bf16[2,256,256]{2,1,0:T(8,128)(2,1)S(1)}, bf16[2,256,256]{2,1,0:T(8,128)(2,1)S(1)}, u32[]{:S(2)}, u32[]{:S(2)}) collective-permute-start(bf16[2,256,256]{2,1,0:T(8,128)(2,1)S(1)} %get-tuple-element.51.refs_4_.refs_2_.refs_0_), channel_id=1, source_target_pairs={{8,0},{10,2},{12,4},{14,6},{16,8},{18,10},{20,12},{22,14},{24,16},... | collective-permute-start | bytes 786440 | tf_op jit(solution)/shard_map/ppermute | solution.py:31
  6.9 12.8 %collective-permute-start.1 = (bf16[2,2,256,256]{3,2,1,0:T(8,128)(2,1)}, bf16[2,2,256,256]{3,2,1,0:T(8,128)(2,1)S(1)}, u32[]{:S(2)}, u32[]{:S(2)}) collective-permute-start(bf16[2,2,256,256]{3,2,1,0:T(8,128)(2,1)} %bitcast.18), channel_id=1, source_target_pairs={{2,0},{4,2},{6,4},{0,6},{10,8},{12,10},{14,12},{8,14},{18,16},{20,... | collective-permute-start | bytes 1572872 | tf_op jit(solution)/shard_map/ppermute | solution.py:31
  8.2 0.7 copy-start.3
  9.5 8.6 %collective-permute-start.2 = (bf16[2,256,256]{2,1,0:T(8,128)(2,1)S(1)}, bf16[2,256,256]{2,1,0:T(8,128)(2,1)S(1)}, u32[]{:S(2)}, u32[]{:S(2)}) collective-permute-start(bf16[2,256,256]{2,1,0:T(8,128)(2,1)S(1)} %get-tuple-element.28.refs_2_.refs_0_), channel_id=1, source_target_pairs={{8,0},{10,2},{12,4},{14,6},{16,8},{18,10},{20,12},{22,14},{24,16},... | collective-permute-start | bytes 786440 | tf_op jit(solution)/shard_map/ppermute | solution.py:31
  13.6 6.1 %collective-permute-start.5 = (bf16[2,256,256]{2,1,0:T(8,128)(2,1)S(1)}, bf16[2,256,256]{2,1,0:T(8,128)(2,1)S(1)}, u32[]{:S(2)}, u32[]{:S(2)}) collective-permute-start(bf16[2,256,256]{2,1,0:T(8,128)(2,1)S(1)} %collective-permute-done.4.refs_4_), channel_id=1, source_target_pairs={{2,0},{4,2},{6,4},{0,6},{10,8},{12,10},{14,12},{8,14},{18,16},{20,... | collective-permute-start | bytes 786440 | tf_op jit(solution)/shard_map/ppermute | solution.py:31
  13.7 6.1 %collective-permute-start = (bf16[272,256]{1,0:T(8,128)(2,1)S(1)}, bf16[272,256]{1,0:T(8,128)(2,1)S(1)}, u32[]{:S(2)}, u32[]{:S(2)}) collective-permute-start(bf16[272,256]{1,0:T(8,128)(2,1)S(1)} %get-tuple-element.27), channel_id=1, source_target_pairs={{0,1},{1,0},{2,3},{3,2},{4,5},{5,4},{6,7},{7,6},{8,9},{9,8},{10,11... | collective-permute-start | bytes 417800 | tf_op jit(solution)/shard_map/ppermute | solution.py:455
  18.1 4.2 %collective-permute-start.3 = (bf16[2,256,256]{2,1,0:T(8,128)(2,1)S(1)}, bf16[2,256,256]{2,1,0:T(8,128)(2,1)S(1)}, u32[]{:S(2)}, u32[]{:S(2)}) collective-permute-start(bf16[2,256,256]{2,1,0:T(8,128)(2,1)S(1)} %collective-permute-done.2.refs_4_), channel_id=1, source_target_pairs={{2,0},{4,2},{6,4},{0,6},{10,8},{12,10},{14,12},{8,14},{18,16},{20,... | collective-permute-start | bytes 786440 | tf_op jit(solution)/shard_map/ppermute | solution.py:31
  19.7 2.6 %copy-start.4 = (bf16[512,512]{1,0:T(8,128)(2,1)S(1)}, bf16[512,512]{1,0:T(8,128)(2,1)}, u32[]{:S(2)}) copy-start(bf16[512,512]{1,0:T(8,128)(2,1)} %constant.11.refs_10_) | copy-start | bytes 1572868
  27.0 2.6 %collective-permute-start.6 = (bf16[256,512]{1,0:T(8,128)(2,1)S(1)}, bf16[256,512]{1,0:T(8,128)(2,1)S(1)}, u32[]{:S(2)}, u32[]{:S(2)}) collective-permute-start(bf16[256,512]{1,0:T(8,128)(2,1)S(1)} %get-tuple-element.34), channel_id=1, source_target_pairs={{0,2},{1,3},{2,0},{3,1},{4,6},{5,7},{6,4},{7,5},{8,10},{9,11},{10,... | collective-permute-start | bytes 786440 | tf_op jit(solution)/shard_map/ppermute | solution.py:391
  28.5 11.6 %collective-permute-start.8 = (bf16[528,256]{1,0:T(8,128)(2,1)S(1)}, bf16[528,256]{1,0:T(8,128)(2,1)S(1)}, u32[]{:S(2)}, u32[]{:S(2)}) collective-permute-start(bf16[528,256]{1,0:T(8,128)(2,1)S(1)} %get-tuple-element.40), channel_id=1, source_target_pairs={{24,0},{26,2},{28,4},{30,6},{0,8},{2,10},{4,12},{6,14},{8,16},{10,... | collective-permute-start | bytes 811016 | tf_op jit(solution)/shard_map/ppermute | solution.py:31
  30.4 4.4 %collective-permute-start.9 = (bf16[64,512]{1,0:T(8,128)(2,1)S(1)}, bf16[64,512]{1,0:T(8,128)(2,1)S(1)}, u32[]{:S(2)}, u32[]{:S(2)}) collective-permute-start(bf16[64,512]{1,0:T(8,128)(2,1)S(1)} %get-tuple-element.43), channel_id=1, source_target_pairs={{0,1},{1,0},{2,3},{3,2},{4,5},{5,4},{6,7},{7,6},{8,9},{9,8},{10,11... | collective-permute-start | bytes 196616 | tf_op jit(solution)/shard_map/ppermute | solution.py:391
  32.0 4.8 %collective-permute-start.10 = (bf16[64,512]{1,0:T(8,128)(2,1)S(1)}, bf16[64,512]{1,0:T(8,128)(2,1)S(1)}, u32[]{:S(2)}, u32[]{:S(2)}) collective-permute-start(bf16[64,512]{1,0:T(8,128)(2,1)S(1)} %get-tuple-element.44), channel_id=1, source_target_pairs={{0,4},{1,5},{2,6},{3,7},{4,0},{5,1},{6,2},{7,3},{8,12},{9,13},{10,... | collective-permute-start | bytes 196616 | tf_op jit(solution)/shard_map/ppermute | solution.py:391
  32.9 5.2 %collective-permute-start.11 = (bf16[64,512]{1,0:T(8,128)(2,1)S(1)}, bf16[64,512]{1,0:T(8,128)(2,1)S(1)}, u32[]{:S(2)}, u32[]{:S(2)}) collective-permute-start(bf16[64,512]{1,0:T(8,128)(2,1)S(1)} %get-tuple-element.45), channel_id=1, source_target_pairs={{0,5},{1,4},{2,7},{3,6},{4,1},{5,0},{6,3},{7,2},{8,13},{9,12},{10,... | collective-permute-start | bytes 196616 | tf_op jit(solution)/shard_map/ppermute | solution.py:391
  34.0 13.7 %collective-permute-start.7 = (bf16[528,256]{1,0:T(8,128)(2,1)S(1)}, bf16[528,256]{1,0:T(8,128)(2,1)S(1)}, u32[]{:S(2)}, u32[]{:S(2)}) collective-permute-start(bf16[528,256]{1,0:T(8,128)(2,1)S(1)} %get-tuple-element.37), channel_id=1, source_target_pairs={{24,0},{26,2},{28,4},{30,6},{0,8},{2,10},{4,12},{6,14},{8,16},{10,... | collective-permute-start | bytes 811016 | tf_op jit(solution)/shard_map/ppermute | solution.py:31
  40.1 5.8 %collective-permute-start.12 = (bf16[2,256,256]{2,1,0:T(8,128)(2,1)S(1)}, bf16[2,256,256]{2,1,0:T(8,128)(2,1)S(1)}, u32[]{:S(2)}, u32[]{:S(2)}) collective-permute-start(bf16[2,256,256]{2,1,0:T(8,128)(2,1)S(1)} %shard_map.92), channel_id=1, source_target_pairs={{6,0},{0,2},{2,4},{4,6},{14,8},{8,10},{10,12},{12,14},{22,16},{16,... | collective-permute-start | bytes 786440 | tf_op jit(solution)/shard_map/ppermute | solution.py:31
  40.2 7.7 %collective-permute-start.14 = (bf16[64,512]{1,0:T(8,128)(2,1)S(1)}, bf16[64,512]{1,0:T(8,128)(2,1)S(1)}, u32[]{:S(2)}, u32[]{:S(2)}) collective-permute-start(bf16[64,512]{1,0:T(8,128)(2,1)S(1)} %shard_map.91.refs_2_.refs_0_), channel_id=1, source_target_pairs={{0,8},{1,9},{2,10},{3,11},{4,12},{5,13},{6,14},{7,15},{8,0},{9,1},... | collective-permute-start | bytes 196616 | tf_op jit(solution)/shard_map/ppermute | solution.py:391
  46.1 12.5 %collective-permute-start.17 = (bf16[2,256,256]{2,1,0:T(8,128)(2,1)S(1)}, bf16[2,256,256]{2,1,0:T(8,128)(2,1)S(1)}, u32[]{:S(2)}, u32[]{:S(2)}) collective-permute-start(bf16[2,256,256]{2,1,0:T(8,128)(2,1)S(1)} %shard_map.93.refs_2_.refs_1_), channel_id=1, source_target_pairs={{0,1},{1,0},{2,3},{3,2},{4,5},{5,4},{6,7},{7,6},{8,9},{9,8},{10,11... | collective-permute-start | bytes 786440 | tf_op jit(solution)/shard_map/ppermute | solution.py:484
  47.7 10.0 %collective-permute-start.13 = (bf16[2,256,256]{2,1,0:T(8,128)(2,1)S(1)}, bf16[2,256,256]{2,1,0:T(8,128)(2,1)S(1)}, u32[]{:S(2)}, u32[]{:S(2)}) collective-permute-start(bf16[2,256,256]{2,1,0:T(8,128)(2,1)S(1)} %shard_map.94.refs_2_), channel_id=1, source_target_pairs={{6,0},{0,2},{2,4},{4,6},{14,8},{8,10},{10,12},{12,14},{22,16},{16,... | collective-permute-start | bytes 786440 | tf_op jit(solution)/shard_map/ppermute | solution.py:31
  47.9 6.4 %collective-permute-start.15 = (bf16[64,512]{1,0:T(8,128)(2,1)S(1)}, bf16[64,512]{1,0:T(8,128)(2,1)S(1)}, u32[]{:S(2)}, u32[]{:S(2)}) collective-permute-start(bf16[64,512]{1,0:T(8,128)(2,1)S(1)} %shard_map.95.refs_0_), channel_id=1, source_target_pairs={{0,16},{1,17},{2,18},{3,19},{4,20},{5,21},{6,22},{7,23},{8,24},{9,... | collective-permute-start | bytes 196616 | tf_op jit(solution)/shard_map/ppermute | solution.py:391
  54.2 5.8 %collective-permute-start.20 = (bf16[64,512]{1,0:T(8,128)(2,1)S(1)}, bf16[64,512]{1,0:T(8,128)(2,1)S(1)}, u32[]{:S(2)}, u32[]{:S(2)}) collective-permute-start(bf16[64,512]{1,0:T(8,128)(2,1)S(1)} %shard_map.96.refs_3_.refs_0_), channel_id=1, source_target_pairs={{0,5},{1,4},{2,7},{3,6},{4,1},{5,0},{6,3},{7,2},{8,13},{9,12},{10,... | collective-permute-start | bytes 196616 | tf_op jit(solution)/shard_map/ppermute | solution.py:391
  55.7 4.3 %collective-permute-start.19 = (bf16[64,512]{1,0:T(8,128)(2,1)S(1)}, bf16[64,512]{1,0:T(8,128)(2,1)S(1)}, u32[]{:S(2)}, u32[]{:S(2)}) collective-permute-start(bf16[64,512]{1,0:T(8,128)(2,1)S(1)} %shard_map.96.refs_3_.refs_0_), channel_id=1, source_target_pairs={{0,4},{1,5},{2,6},{3,7},{4,0},{5,1},{6,2},{7,3},{8,12},{9,13},{10,... | collective-permute-start | bytes 196616 | tf_op jit(solution)/shard_map/ppermute | solution.py:391
  56.4 5.1 %collective-permute-start.18 = (bf16[64,512]{1,0:T(8,128)(2,1)S(1)}, bf16[64,512]{1,0:T(8,128)(2,1)S(1)}, u32[]{:S(2)}, u32[]{:S(2)}) collective-permute-start(bf16[64,512]{1,0:T(8,128)(2,1)S(1)} %shard_map.96.refs_3_.refs_0_), channel_id=1, source_target_pairs={{0,1},{1,0},{2,3},{3,2},{4,5},{5,4},{6,7},{7,6},{8,9},{9,8},{10,11... | collective-permute-start | bytes 196616 | tf_op jit(solution)/shard_map/ppermute | solution.py:391
  57.9 8.4 %collective-permute-start.16 = (bf16[2,256,256]{2,1,0:T(8,128)(2,1)S(1)}, bf16[2,256,256]{2,1,0:T(8,128)(2,1)S(1)}, u32[]{:S(2)}, u32[]{:S(2)}) collective-permute-start(bf16[2,256,256]{2,1,0:T(8,128)(2,1)S(1)} %shard_map.97.refs_3_.refs_1_), channel_id=1, source_target_pairs={{0,1},{1,0},{2,3},{3,2},{4,5},{5,4},{6,7},{7,6},{8,9},{9,8},{10,11... | collective-permute-start | bytes 786440 | tf_op jit(solution)/shard_map/ppermute | solution.py:484
  61.5 5.6 %collective-permute-start.21 = (bf16[256,512]{1,0:T(8,128)(2,1)S(1)}, bf16[256,512]{1,0:T(8,128)(2,1)S(1)}, u32[]{:S(2)}, u32[]{:S(2)}) collective-permute-start(bf16[256,512]{1,0:T(8,128)(2,1)S(1)} %shard_map.99.refs_4_.refs_0_), channel_id=1, source_target_pairs={{0,2},{1,3},{2,0},{3,1},{4,6},{5,7},{6,4},{7,5},{8,10},{9,11},{10,... | collective-permute-start | bytes 786440 | tf_op jit(solution)/shard_map/ppermute | solution.py:391

commit v12 on v11

--- a/solution.py
+++ b/solution.py
@@ -19,6 +19,12 @@
 
 f32 = jnp.float32
 bf16 = jnp.bfloat16
+
+
+def from_below(block):
+    tiles = lax.axis_size("tile")
+    across = tiles // GRID_ROWS
+    return lax.ppermute(block, "tile", [(i + across, i) for i in range(tiles - across)])
 
 
 def from_behind(block, rows, cols):
@@ -79,9 +85,14 @@
     return rows, cols, rows_t, cols_t, col, busy
 
 
-def patch(shifts, own_ref, right_ref, below_ref, diag_ref, part):
+def halve_kernel(block_ref, *half_refs):
+    for part, ref in enumerate(half_refs):
+        ref[...] = block_ref[part]
+
+
+def patch(shifts, own_ref, right_ref, below_ref, diag_refs, part):
     upper = jnp.concatenate([own_ref[part], right_ref[part]], axis=1)
-    lower = jnp.concatenate([below_ref[part], diag_ref[part]], axis=1)
+    lower = jnp.concatenate([below_ref[part], diag_refs[part][...]], axis=1)
     rows = dot(shifts[0], jnp.concatenate([upper, lower], axis=0)).astype(bf16)
     return dot(rows, shifts[1])
 
@@ -137,7 +148,7 @@
 ):
     n = own_ref.shape[1]
     shifts = shift_tables(mine_ref, sent_ref)
-    tiles = (own_ref, right_ref.at[0], below_ref, diag_ref)
+    tiles = (own_ref, right_ref.at[0], below_ref, [diag_ref.at[part] for part in range(2)])
     near = [patch(shifts, *tiles, part) for part in range(2)]
     for part in range(2):
         near_ref[part] = near[part].astype(bf16)
@@ -170,15 +181,15 @@
 
 
 def gradient_kernel(
-    mine_ref, sent_ref, own_ref, right_ref, below_ref, diag_ref, near_ref, arrive_ref, planes_ref,
-    prop_ref, dft_ref,
+    mine_ref, sent_ref, own_ref, right_ref, below_ref, diag_re_ref, diag_im_ref, near_ref,
+    arrive_ref, planes_ref, prop_ref, dft_ref,
     home_ref, next_ref, down_ref, grad_ref, keep_ref, give_ref, term_ref,
 ):
     n = own_ref.shape[1]
     modes = planes_ref.shape[2] // n
     shifts = shift_tables(mine_ref, sent_ref)
     busy = shifts[5]
-    tiles = (own_ref, right_ref.at[1], below_ref, diag_ref)
+    tiles = (own_ref, right_ref.at[1], below_ref, (diag_re_ref, diag_im_ref))
     far = [patch(shifts, *tiles, part) for part in range(2)]
     fields = []
     for mode in range(modes):
@@ -222,18 +233,18 @@
     return parts, above_ref[pl.ds(2 * n, 16), :].astype(f32)[0:1] > 0
 
 
-def beside_kernel(next_ref, above_ref, out_ref):
+def beside_kernel(next_ref, above_ref, *out_refs):
+    above, split = above_parts(above_ref, next_ref.shape[1])
+    for part, ref in enumerate(out_refs):
+        total = next_ref[part].astype(f32) + jnp.where(split, above[part], 0.0)
+        ref[...] = total.astype(bf16)
+
+
+def part_kernel(home_ref, above_ref, left_re_ref, left_im_ref, out_ref):
     above, split = above_parts(above_ref, out_ref.shape[1])
-    for part in range(2):
-        total = next_ref[part].astype(f32) + jnp.where(split, above[part], 0.0)
-        out_ref[part] = total.astype(bf16)
-
-
-def part_kernel(home_ref, above_ref, left_ref, out_ref):
-    above, split = above_parts(above_ref, out_ref.shape[1])
-    for part in range(2):
+    for part, left_ref in enumerate((left_re_ref, left_im_ref)):
         total = home_ref[part].astype(f32) + jnp.where(split, 0.0, above[part])
-        out_ref[part] = (total + left_ref[part].astype(f32)).astype(bf16)
+        out_ref[part] = (total + left_ref[...].astype(f32)).astype(bf16)
 
 
 def update_kernel(layer, own_ref, part_ref, other_ref, *refs):
@@ -426,12 +437,13 @@
     lane_tiles = pixels // 128
     prop, dft = build_tables(pixels)
     tile = shape_of(bf16, 2, pixels, pixels)
+    plane = shape_of(bf16, pixels, pixels)
     planes = shape_of(f32, 2, pixels, width)
     probe = probe_modes.reshape(2, pixels, modes, lane_tiles, 128)
     probe = probe.transpose(0, 1, 3, 2, 4).reshape(-1, 128)
 
     own = [tile_object[0, 0], tile_object[0, 1]]
-    below0 = from_behind(own[0], -1, 0)
+    below0 = from_below(own[0])
     right = from_behind(tile_object[0], 0, -1)
     exchanged = lax.axis_size("pos") == patterns.shape[2]
     message = shape_of(bf16, pixels + 16, pixels)
@@ -450,13 +462,14 @@
         limit=8,
         after=[own1],
     )
-    below1 = from_behind(own1, -1, 0)
+    below1 = from_below(own1)
     if exchanged:
         sent = lax.ppermute(sent, "pos", [(i, 1 - i) for i in range(2)])
     else:
         sent = gathered_message(patterns, offsets, counts)
     diag0 = from_behind(below0, 0, -1)
-    diag1 = from_behind(below1, 0, -1)
+    halves = run(job(halve_kernel, [plane, plane], [below1]))
+    diag1 = [from_behind(half, 0, -1) for half in halves]
     near, arrive = run(
         job(
             arrive_kernel,
@@ -472,7 +485,7 @@
         job(
             gradient_kernel,
             [tile, tile, down, tile, half, half],
-            [mine, sent, own1, right, below1, diag1, near, arrive, probe_planes, table, dft],
+            [mine, sent, own1, right, below1, *diag1, near, arrive, probe_planes, table, dft],
             scratch=[pltpu.VMEM((2, pixels, width), bf16)],
         ),
         flops=4_000_000_000,
@@ -485,10 +498,10 @@
         return lax.psum(part.astype(f32), "pos") - part.astype(f32)
 
     def beside(next_tile, above):
-        return job(beside_kernel, [tile], [next_tile, above])
+        return job(beside_kernel, [plane, plane], [next_tile, above])
 
     def part(home, above, left):
-        return job(part_kernel, [tile], [home, above, left])
+        return job(part_kernel, [tile], [home, above, *left])
 
     core, groups = core_group(), exchange_groups()
     above1 = from_behind(down1, 1, 0)
@@ -508,13 +521,13 @@
     first, second, *others = [[bit] for group in groups for bit in group]
     (total,) = run(added(keep, arrived))
     arrived = swapped(total, first)
-    (beside1,) = run(beside(next1, above1), after=[total], flops=LATE[0])
-    left1 = from_behind(beside1, 0, 1)
+    beside1 = run(beside(next1, above1), after=[total], flops=LATE[0])
+    left1 = [from_behind(half, 0, 1) for half in beside1]
     (part1,) = run(part(home1, above1, left1), flops=LATE[1])
     other1 = over_owners(part1)
-    (beside0,) = run(beside(next0, above0), after=[part1], flops=LATE[2])
-    left0 = from_behind(beside0, 0, 1)
-    (total,) = run(added(total, arrived), after=[beside0], flops=LATE[3])
+    beside0 = run(beside(next0, above0), after=[part1], flops=LATE[2])
+    left0 = [from_behind(half, 0, 1) for half in beside0]
+    (total,) = run(added(total, arrived), after=beside0[:1], flops=LATE[3])
     arrived = swapped(total, second)
     (total,) = run(added(total, arrived), flops=LATE[4])
     for group in others:

time: 68.5 us -> 69.9 us (1.020)
  starting transfers between devices: 21.3 us -> 26.4 us
  waiting for transfers between devices: 32.5 us -> 28.7 us
    ppermute x9 -> x10, waiting for transfers between devices: 15.1 us -> 4.71 us  [from_behind(): return lax.ppermute(block, 'tile', [(source(i), i) for i in range(tiles)])]
    ppermute x0 -> x2, waiting for transfers between devices: none -> 8.24 us  [from_below(): lax.ppermute(block, 'tile', [(i + across, i) for i in range(tiles - acros...]
    ppermute x0 -> x2, starting transfers between devices: none -> 2.72 us  [from_below(): lax.ppermute(block, 'tile', [(i + across, i) for i in range(tiles - acros...]
    ppermute x9 -> x10, starting transfers between devices: 8.04 us -> 9.63 us  [from_behind(): return lax.ppermute(block, 'tile', [(source(i), i) for i in range(tiles)])]
    ppermute x10, starting transfers between devices: 9.42 us -> 10.6 us  [swap_with(): lax.ppermute(x, ('tile', 'pos'), [(i, i ^ mask) for i in range(devices)])]
    ppermute x1, waiting for transfers between devices: 1.16 us -> 0.01 us  [shards(): sent = lax.ppermute(sent, 'pos', [(i, 1 - i) for i in range(2)])]
    ppermute x2, waiting for transfers between devices: 4.71 us -> 3.99 us  [over_owners(): return lax.ppermute(part, 'pos', [(0, 1), (1, 0)])]
    pallas_call x14 -> x15, Pallas kernels: 9.55 us -> 9.58 us  [run(): pl.pallas_call(body, out_shape=sum(outs, []), in_specs=sum(specs, []) + [...]
  transfers between devices with their start and end apart: 22 -> 25, of which waited for: 13 -> 12; matrix products, arithmetic and copies ran while one was open for 0% -> 0% of each run, Pallas kernels for 8% -> 8%
where the time goes in v12:
time: 69.9 us; the launch traced here: 69.7 us
  waiting for transfers between devices  28.7 us (41%)
  starting transfers between devices  26.4 us (38%)
  Pallas kernels  11.2 us (16%)
  local copies, waits for them, and re-layouts  1.86 us (3%)
  between operations  1.51 us (2%)
    ppermute x10, waiting for transfers between devices, swap_with(): lax.ppermute(x, ('tile', 'pos'), [(i, i ^ mask) for i in range(devices)])  11.7 us
    ppermute x10, starting transfers between devices, swap_with(): lax.ppermute(x, ('tile', 'pos'), [(i, i ^ mask) for i in range(devices)])  10.6 us
    ppermute x10, starting transfers between devices, from_behind(): return lax.ppermute(block, 'tile', [(source(i), i) for i in range(tiles)])  9.63 us
    pallas_call x15, Pallas kernels, run(): pl.pallas_call(body, out_shape=sum(outs, []), in_specs=sum(specs, []) + [...  9.58 us
    ppermute x2, waiting for transfers between devices, from_below(): lax.ppermute(block, 'tile', [(i + across, i) for i in range(tiles - acros...  8.24 us
    ppermute x10, waiting for transfers between devices, from_behind(): return lax.ppermute(block, 'tile', [(source(i), i) for i in range(tiles)])  4.71 us
    ppermute x2, waiting for transfers between devices, over_owners(): return lax.ppermute(part, 'pos', [(0, 1), (1, 0)])  3.99 us
    ppermute x2, starting transfers between devices, from_below(): lax.ppermute(block, 'tile', [(i + across, i) for i in range(tiles - acros...  2.72 us
  transfers between devices with their start and end apart: 25, of which 12 were waited for; matrix products, arithmetic and copies ran while one was open for 0% of the time, Pallas kernels for 8%

profile of v12, /device:TPU:0, one launch (start us, length us, event | category | flops | bytes accessed | tf_op | source)
XLA Modules:
  0.0 69.7 jit_solution(5222331842313470416)
XLA Ops:
  0.6 1.2 %slice_bitcast_fusion = (bf16[2,256,256]{2,1,0:T(8,128)(2,1)S(1)}, bf16[2,256,256]{2,1,0:T(8,128)(2,1)S(1)}) fusion(bf16[1,2,2,256,256]{4,3,2,1,0:T(8,128)(2,1)} %param.7), kind=kLoop, calls=%fused_computation | loop fusion | bytes 1048576 | tf_op jit(solution)/shard_map/squeeze | solution.py:445
  1.8 1.4 %collective-permute-start.5 = (bf16[2,256,256]{2,1,0:T(8,128)(2,1)S(1)}, bf16[2,256,256]{2,1,0:T(8,128)(2,1)S(1)}, u32[]{:S(2)}, u32[]{:S(2)}) collective-permute-start(bf16[2,256,256]{2,1,0:T(8,128)(2,1)S(1)} %get-tuple-element.63.refs_4_.refs_2_.refs_0_), channel_id=1, source_target_pairs={{8,0},{10,2},{12,4},{14,6},{16,8},{18,10},{20,12},{22,14},{24,16},... | collective-permute-start | bytes 786440 | tf_op jit(solution)/shard_map/ppermute | solution.py:27
  3.3 2.4 %collective-permute-start.1 = (bf16[2,2,256,256]{3,2,1,0:T(8,128)(2,1)}, bf16[2,2,256,256]{3,2,1,0:T(8,128)(2,1)S(1)}, u32[]{:S(2)}, u32[]{:S(2)}) collective-permute-start(bf16[2,2,256,256]{3,2,1,0:T(8,128)(2,1)} %bitcast.18), channel_id=1, source_target_pairs={{2,0},{4,2},{6,4},{0,6},{10,8},{12,10},{14,12},{8,14},{18,16},{20,... | collective-permute-start | bytes 1572872 | tf_op jit(solution)/shard_map/ppermute | solution.py:37
  6.4 0.7 copy-done.3
  7.0 0.6 shard_map.86
  7.6 1.3 %collective-permute-start.2 = (bf16[2,256,256]{2,1,0:T(8,128)(2,1)S(1)}, bf16[2,256,256]{2,1,0:T(8,128)(2,1)S(1)}, u32[]{:S(2)}, u32[]{:S(2)}) collective-permute-start(bf16[2,256,256]{2,1,0:T(8,128)(2,1)S(1)} %get-tuple-element.34.refs_2_.refs_0_), channel_id=1, source_target_pairs={{8,0},{10,2},{12,4},{14,6},{16,8},{18,10},{20,12},{22,14},{24,16},... | collective-permute-start | bytes 786440 | tf_op jit(solution)/shard_map/ppermute | solution.py:27
  8.9 5.1 %collective-permute-done.5.refs_4_ = bf16[2,256,256]{2,1,0:T(8,128)(2,1)S(1)} collective-permute-done((bf16[2,256,256]{2,1,0:T(8,128)(2,1)S(1)}, bf16[2,256,256]{2,1,0:T(8,128)(2,1)S(1)}, u32[]{:S(2)}, u32[]{:S(2)}) %collective-permute-start.5) | collective-permute-done | bytes 262176 | tf_op jit(solution)/shard_map/ppermute | solution.py:27
  14.0 1.5 %collective-permute-start = (bf16[272,256]{1,0:T(8,128)(2,1)S(1)}, bf16[272,256]{1,0:T(8,128)(2,1)S(1)}, u32[]{:S(2)}, u32[]{:S(2)}) collective-permute-start(bf16[272,256]{1,0:T(8,128)(2,1)S(1)} %get-tuple-element.33), channel_id=1, source_target_pairs={{0,1},{1,0},{2,3},{3,2},{4,5},{5,4},{6,7},{7,6},{8,9},{9,8},{10,11... | collective-permute-start | bytes 417800 | tf_op jit(solution)/shard_map/ppermute | solution.py:467
  15.6 0.1 shard_map.88
  15.7 3.1 %collective-permute-done.2.refs_0_.refs_4_ = bf16[2,256,256]{2,1,0:T(8,128)(2,1)S(1)} collective-permute-done((bf16[2,256,256]{2,1,0:T(8,128)(2,1)S(1)}, bf16[2,256,256]{2,1,0:T(8,128)(2,1)S(1)}, u32[]{:S(2)}, u32[]{:S(2)}) %collective-permute-start.2) | collective-permute-done | bytes 262176 | tf_op jit(solution)/shard_map/ppermute | solution.py:27
  18.8 0.7 %collective-permute-start.3 = (bf16[256,256]{1,0:T(8,128)(2,1)S(1)}, bf16[256,256]{1,0:T(8,128)(2,1)S(1)}, u32[]{:S(2)}, u32[]{:S(2)}) collective-permute-start(bf16[256,256]{1,0:T(8,128)(2,1)S(1)} %get-tuple-element.35), channel_id=1, source_target_pairs={{2,0},{4,2},{6,4},{0,6},{10,8},{12,10},{14,12},{8,14},{18,16},{20,... | collective-permute-start | bytes 393224 | tf_op jit(solution)/shard_map/ppermute | solution.py:37
  19.6 1.1 %collective-permute-start.4 = (bf16[256,256]{1,0:T(8,128)(2,1)S(1)}, bf16[256,256]{1,0:T(8,128)(2,1)S(1)}, u32[]{:S(2)}, u32[]{:S(2)}) collective-permute-start(bf16[256,256]{1,0:T(8,128)(2,1)S(1)} %get-tuple-element.36), channel_id=1, source_target_pairs={{2,0},{4,2},{6,4},{0,6},{10,8},{12,10},{14,12},{8,14},{18,16},{20,... | collective-permute-start | bytes 393224 | tf_op jit(solution)/shard_map/ppermute | solution.py:37
  20.7 1.8 %shard_map.89 = (bf16[2,256,256]{2,1,0:T(8,128)(2,1)S(1)}, f32[2,256,512]{2,1,0:T(8,128)S(1)}) custom-call(bf16[272,256]{1,0:T(8,128)(2,1)S(1)} %get-tuple-element.32.refs_0_.refs_2_, bf16[272,256]{1,0:T(8,128)(2,1)S(1)} %collective-permute-done.refs_1_.refs_3_, bf16[2,256,256]{2,1,0:T(8,128)(2,1)S(1)} %get-tuple-element.63.refs_4_.refs_2_.refs_0_, ...), custom_call_target="tpu_custom_call" | custom-call | flops 1500000000 | bytes 4472832 | tf_op jit(solution)/shard_map/pallas_call | solution.py:296
  22.5 1.0 %collective-permute-done.4.refs_6_ = bf16[256,256]{1,0:T(8,128)(2,1)S(1)} collective-permute-done((bf16[256,256]{1,0:T(8,128)(2,1)S(1)}, bf16[256,256]{1,0:T(8,128)(2,1)S(1)}, u32[]{:S(2)}, u32[]{:S(2)}) %collective-permute-start.4) | collective-permute-done | bytes 131104 | tf_op jit(solution)/shard_map/ppermute | solution.py:37
  23.5 4.6 %shard_map.90 = (bf16[2,256,256]{2,1,0:T(8,128)(2,1)S(1)}, bf16[2,256,256]{2,1,0:T(8,128)(2,1)S(1)}, bf16[528,256]{1,0:T(8,128)(2,1)S(1)}, bf16[2,256,256]{2,1,0...) custom-call(bf16[272,256]{1,0:T(8,128)(2,1)S(1)} %get-tuple-element.32.refs_0_.refs_2_, ...), custom_call_target="tpu_custom_call" | custom-call | flops 4000000000 | bytes 6578176 | tf_op jit(solution)/shard_map/pallas_call | solution.py:296
  28.1 1.3 %collective-permute-start.7 = (bf16[256,512]{1,0:T(8,128)(2,1)S(1)}, bf16[256,512]{1,0:T(8,128)(2,1)S(1)}, u32[]{:S(2)}, u32[]{:S(2)}) collective-permute-start(bf16[256,512]{1,0:T(8,128)(2,1)S(1)} %get-tuple-element.42), channel_id=1, source_target_pairs={{0,2},{1,3},{2,0},{3,1},{4,6},{5,7},{6,4},{7,5},{8,10},{9,11},{10,... | collective-permute-start | bytes 786440 | tf_op jit(solution)/shard_map/ppermute | solution.py:402
  29.4 1.6 %collective-permute-start.9 = (bf16[528,256]{1,0:T(8,128)(2,1)S(1)}, bf16[528,256]{1,0:T(8,128)(2,1)S(1)}, u32[]{:S(2)}, u32[]{:S(2)}) collective-permute-start(bf16[528,256]{1,0:T(8,128)(2,1)S(1)} %get-tuple-element.48), channel_id=1, source_target_pairs={{24,0},{26,2},{28,4},{30,6},{0,8},{2,10},{4,12},{6,14},{8,16},{10,... | collective-permute-start | bytes 811016 | tf_op jit(solution)/shard_map/ppermute | solution.py:37
  31.0 0.8 %shard_map.91 = (f32[64,512]{1,0:T(8,128)S(1)}, bf16[64,512]{1,0:T(8,128)(2,1)S(1)}, bf16[64,512]{1,0:T(8,128)(2,1)S(1)}, bf16[64,512]{1,0:T(8,128)(2,1)S(1)}, b...) custom-call(bf16[256,512]{1,0:T(8,128)(2,1)S(1)} %get-tuple-element.41.refs_0_, ...), custom_call_target="tpu_custom_call" | custom-call | flops 1000000 | bytes 2187264 | tf_op jit(solution)/shard_map/pallas_call | solution.py:296
  31.7 1.6 %collective-permute-start.8 = (bf16[528,256]{1,0:T(8,128)(2,1)S(1)}, bf16[528,256]{1,0:T(8,128)(2,1)S(1)}, u32[]{:S(2)}, u32[]{:S(2)}) collective-permute-start(bf16[528,256]{1,0:T(8,128)(2,1)S(1)} %get-tuple-element.45), channel_id=1, source_target_pairs={{24,0},{26,2},{28,4},{30,6},{0,8},{2,10},{4,12},{6,14},{8,16},{10,... | collective-permute-start | bytes 811016 | tf_op jit(solution)/shard_map/ppermute | solution.py:37
  33.4 1.5 %collective-permute-start.10 = (bf16[64,512]{1,0:T(8,128)(2,1)S(1)}, bf16[64,512]{1,0:T(8,128)(2,1)S(1)}, u32[]{:S(2)}, u32[]{:S(2)}) collective-permute-start(bf16[64,512]{1,0:T(8,128)(2,1)S(1)} %get-tuple-element.51), channel_id=1, source_target_pairs={{0,1},{1,0},{2,3},{3,2},{4,5},{5,4},{6,7},{7,6},{8,9},{9,8},{10,11... | collective-permute-start | bytes 196616 | tf_op jit(solution)/shard_map/ppermute | solution.py:402
  34.9 1.2 %collective-permute-start.11 = (bf16[64,512]{1,0:T(8,128)(2,1)S(1)}, bf16[64,512]{1,0:T(8,128)(2,1)S(1)}, u32[]{:S(2)}, u32[]{:S(2)}) collective-permute-start(bf16[64,512]{1,0:T(8,128)(2,1)S(1)} %get-tuple-element.52), channel_id=1, source_target_pairs={{0,4},{1,5},{2,6},{3,7},{4,0},{5,1},{6,2},{7,3},{8,12},{9,13},{10,... | collective-permute-start | bytes 196616 | tf_op jit(solution)/shard_map/ppermute | solution.py:402
  36.1 0.8 %collective-permute-start.12 = (bf16[64,512]{1,0:T(8,128)(2,1)S(1)}, bf16[64,512]{1,0:T(8,128)(2,1)S(1)}, u32[]{:S(2)}, u32[]{:S(2)}) collective-permute-start(bf16[64,512]{1,0:T(8,128)(2,1)S(1)} %get-tuple-element.53), channel_id=1, source_target_pairs={{0,5},{1,4},{2,7},{3,6},{4,1},{5,0},{6,3},{7,2},{8,13},{9,12},{10,... | collective-permute-start | bytes 196616 | tf_op jit(solution)/shard_map/ppermute | solution.py:402
  36.9 0.8 %collective-permute-done.10.refs_1_ = bf16[64,512]{1,0:T(8,128)(2,1)S(1)} collective-permute-done((bf16[64,512]{1,0:T(8,128)(2,1)S(1)}, bf16[64,512]{1,0:T(8,128)(2,1)S(1)}, u32[]{:S(2)}, u32[]{:S(2)}) %collective-permute-start.10) | collective-permute-done | bytes 65568 | tf_op jit(solution)/shard_map/ppermute | solution.py:402
  37.6 1.5 %collective-permute-done.11.refs_2_ = bf16[64,512]{1,0:T(8,128)(2,1)S(1)} collective-permute-done((bf16[64,512]{1,0:T(8,128)(2,1)S(1)}, bf16[64,512]{1,0:T(8,128)(2,1)S(1)}, u32[]{:S(2)}, u32[]{:S(2)}) %collective-permute-start.11) | collective-permute-done | bytes 65568 | tf_op jit(solution)/shard_map/ppermute | solution.py:402
  39.2 2.1 %collective-permute-done.12.refs_3_ = bf16[64,512]{1,0:T(8,128)(2,1)S(1)} collective-permute-done((bf16[64,512]{1,0:T(8,128)(2,1)S(1)}, bf16[64,512]{1,0:T(8,128)(2,1)S(1)}, u32[]{:S(2)}, u32[]{:S(2)}) %collective-permute-start.12) | collective-permute-done | bytes 65568 | tf_op jit(solution)/shard_map/ppermute | solution.py:402
  41.3 0.1 shard_map.93
  41.5 0.9 %collective-permute-start.14 = (bf16[256,256]{1,0:T(8,128)(2,1)S(1)}, bf16[256,256]{1,0:T(8,128)(2,1)S(1)}, u32[]{:S(2)}, u32[]{:S(2)}) collective-permute-start(bf16[256,256]{1,0:T(8,128)(2,1)S(1)} %get-tuple-element.55), channel_id=1, source_target_pairs={{6,0},{0,2},{2,4},{4,6},{14,8},{8,10},{10,12},{12,14},{22,16},{16,... | collective-permute-start | bytes 393224 | tf_op jit(solution)/shard_map/ppermute | solution.py:37
  42.4 1.2 %collective-permute-start.17 = (bf16[64,512]{1,0:T(8,128)(2,1)S(1)}, bf16[64,512]{1,0:T(8,128)(2,1)S(1)}, u32[]{:S(2)}, u32[]{:S(2)}) collective-permute-start(bf16[64,512]{1,0:T(8,128)(2,1)S(1)} %shard_map.92.refs_2_.refs_0_), channel_id=1, source_target_pairs={{0,8},{1,9},{2,10},{3,11},{4,12},{5,13},{6,14},{7,15},{8,0},{9,1},... | collective-permute-start | bytes 196616 | tf_op jit(solution)/shard_map/ppermute | solution.py:402
  43.6 2.3 %collective-permute-done.13.refs_2_ = bf16[256,256]{1,0:T(8,128)(2,1)S(1)} collective-permute-done((bf16[256,256]{1,0:T(8,128)(2,1)S(1)}, bf16[256,256]{1,0:T(8,128)(2,1)S(1)}, u32[]{:S(2)}, u32[]{:S(2)}) %collective-permute-start.13) | collective-permute-done | bytes 131104 | tf_op jit(solution)/shard_map/ppermute | solution.py:37
  45.9 1.4 %collective-permute-done.14.refs_3_ = bf16[256,256]{1,0:T(8,128)(2,1)S(1)} collective-permute-done((bf16[256,256]{1,0:T(8,128)(2,1)S(1)}, bf16[256,256]{1,0:T(8,128)(2,1)S(1)}, u32[]{:S(2)}, u32[]{:S(2)}) %collective-permute-start.14) | collective-permute-done | bytes 131104 | tf_op jit(solution)/shard_map/ppermute | solution.py:37
  47.3 0.1 shard_map.94.refs_2_.refs_1_
  47.4 0.8 %collective-permute-start.20 = (bf16[2,256,256]{2,1,0:T(8,128)(2,1)S(1)}, bf16[2,256,256]{2,1,0:T(8,128)(2,1)S(1)}, u32[]{:S(2)}, u32[]{:S(2)}) collective-permute-start(bf16[2,256,256]{2,1,0:T(8,128)(2,1)S(1)} %shard_map.94.refs_2_.refs_1_), channel_id=1, source_target_pairs={{0,1},{1,0},{2,3},{3,2},{4,5},{5,4},{6,7},{7,6},{8,9},{9,8},{10,11... | collective-permute-start | bytes 786440 | tf_op jit(solution)/shard_map/ppermute | solution.py:497
  48.2 0.1 shard_map.95
  48.3 1.1 %collective-permute-start.15 = (bf16[256,256]{1,0:T(8,128)(2,1)S(1)}, bf16[256,256]{1,0:T(8,128)(2,1)S(1)}, u32[]{:S(2)}, u32[]{:S(2)}) collective-permute-start(bf16[256,256]{1,0:T(8,128)(2,1)S(1)} %get-tuple-element.56.refs_2_), channel_id=1, source_target_pairs={{6,0},{0,2},{2,4},{4,6},{14,8},{8,10},{10,12},{12,14},{22,16},{16,... | collective-permute-start | bytes 393224 | tf_op jit(solution)/shard_map/ppermute | solution.py:37
  49.5 1.0 %collective-permute-start.18 = (bf16[64,512]{1,0:T(8,128)(2,1)S(1)}, bf16[64,512]{1,0:T(8,128)(2,1)S(1)}, u32[]{:S(2)}, u32[]{:S(2)}) collective-permute-start(bf16[64,512]{1,0:T(8,128)(2,1)S(1)} %shard_map.96.refs_0_), channel_id=1, source_target_pairs={{0,16},{1,17},{2,18},{3,19},{4,20},{5,21},{6,22},{7,23},{8,24},{9,... | collective-permute-start | bytes 196616 | tf_op jit(solution)/shard_map/ppermute | solution.py:402
  50.5 5.4 %collective-permute-done.18.refs_1_ = bf16[64,512]{1,0:T(8,128)(2,1)S(1)} collective-permute-done((bf16[64,512]{1,0:T(8,128)(2,1)S(1)}, bf16[64,512]{1,0:T(8,128)(2,1)S(1)}, u32[]{:S(2)}, u32[]{:S(2)}) %collective-permute-start.18) | collective-permute-done | bytes 65568 | tf_op jit(solution)/shard_map/ppermute | solution.py:402
  55.9 1.8 %collective-permute-start.23 = (bf16[64,512]{1,0:T(8,128)(2,1)S(1)}, bf16[64,512]{1,0:T(8,128)(2,1)S(1)}, u32[]{:S(2)}, u32[]{:S(2)}) collective-permute-start(bf16[64,512]{1,0:T(8,128)(2,1)S(1)} %shard_map.97.refs_4_.refs_0_), channel_id=1, source_target_pairs={{0,5},{1,4},{2,7},{3,6},{4,1},{5,0},{6,3},{7,2},{8,13},{9,12},{10,... | collective-permute-start | bytes 196616 | tf_op jit(solution)/shard_map/ppermute | solution.py:402
  57.7 0.8 %collective-permute-start.22 = (bf16[64,512]{1,0:T(8,128)(2,1)S(1)}, bf16[64,512]{1,0:T(8,128)(2,1)S(1)}, u32[]{:S(2)}, u32[]{:S(2)}) collective-permute-start(bf16[64,512]{1,0:T(8,128)(2,1)S(1)} %shard_map.97.refs_4_.refs_0_), channel_id=1, source_target_pairs={{0,4},{1,5},{2,6},{3,7},{4,0},{5,1},{6,2},{7,3},{8,12},{9,13},{10,... | collective-permute-start | bytes 196616 | tf_op jit(solution)/shard_map/ppermute | solution.py:402
  58.5 1.0 %collective-permute-start.21 = (bf16[64,512]{1,0:T(8,128)(2,1)S(1)}, bf16[64,512]{1,0:T(8,128)(2,1)S(1)}, u32[]{:S(2)}, u32[]{:S(2)}) collective-permute-start(bf16[64,512]{1,0:T(8,128)(2,1)S(1)} %shard_map.97.refs_4_.refs_0_), channel_id=1, source_target_pairs={{0,1},{1,0},{2,3},{3,2},{4,5},{5,4},{6,7},{7,6},{8,9},{9,8},{10,11... | collective-permute-start | bytes 196616 | tf_op jit(solution)/shard_map/ppermute | solution.py:402
  59.5 0.1 shard_map.98.refs_3_.refs_1_
  59.6 1.1 %collective-permute-start.19 = (bf16[2,256,256]{2,1,0:T(8,128)(2,1)S(1)}, bf16[2,256,256]{2,1,0:T(8,128)(2,1)S(1)}, u32[]{:S(2)}, u32[]{:S(2)}) collective-permute-start(bf16[2,256,256]{2,1,0:T(8,128)(2,1)S(1)} %shard_map.98.refs_3_.refs_1_), channel_id=1, source_target_pairs={{0,1},{1,0},{2,3},{3,2},{4,5},{5,4},{6,7},{7,6},{8,9},{9,8},{10,11... | collective-permute-start | bytes 786440 | tf_op jit(solution)/shard_map/ppermute | solution.py:497
  60.8 0.8 %shard_map.99 = (bf16[1,2,2,256,256]{4,3,2,1,0:T(8,128)(2,1)}, f32[8,128]{1,0:T(8,128)S(1)}) custom-call(bf16[2,256,256]{2,1,0:T(8,128)(2,1)S(1)} %get-tuple-element.34.refs_2_.refs_0_, bf16[2,256,256]{2,1,0:T(8,128)(2,1)S(1)} %shard_map.94.refs_2_.refs_1_, bf16[2,256,256]{2,1,0:T(8,128)(2,1)S(1)} %collective-permute-done.20.refs_2_, ...), custom_call_target="tpu_custom_call" | custom-call | flops 15000131584 | bytes 1048576 | tf_op jit(solution)/shard_map/pallas_call | solution.py:313
  61.6 0.4 collective-permute-done.22.refs_2_
  62.0 1.5 %collective-permute-done.21.refs_1_ = bf16[64,512]{1,0:T(8,128)(2,1)S(1)} collective-permute-done((bf16[64,512]{1,0:T(8,128)(2,1)S(1)}, bf16[64,512]{1,0:T(8,128)(2,1)S(1)}, u32[]{:S(2)}, u32[]{:S(2)}) %collective-permute-start.21) | collective-permute-done | bytes 65568 | tf_op jit(solution)/shard_map/ppermute | solution.py:402
  63.6 0.1 collective-permute-start.24
  63.6 4.0 %collective-permute-done.19.refs_2_ = bf16[2,256,256]{2,1,0:T(8,128)(2,1)S(1)} collective-permute-done((bf16[2,256,256]{2,1,0:T(8,128)(2,1)S(1)}, bf16[2,256,256]{2,1,0:T(8,128)(2,1)S(1)}, u32[]{:S(2)}, u32[]{:S(2)}) %collective-permute-start.19) | collective-permute-done | bytes 262176 | tf_op jit(solution)/shard_map/ppermute | solution.py:497
  67.6 0.8 %shard_map.101 = (bf16[1,2,2,256,256]{4,3,2,1,0:T(8,128)(2,1)}, f32[8,128]{1,0:T(8,128)S(1)}) custom-call(bf16[2,256,256]{2,1,0:T(8,128)(2,1)S(1)} %get-tuple-element.63.refs_4_.refs_2_.refs_0_, bf16[2,256,256]{2,1,0:T(8,128)(2,1)S(1)} %shard_map.98.refs_3_.refs_1_, ...), custom_call_target="tpu_custom_call", output_to_operand_aliasing={{0}: (3, {})} | custom-call | flops 4000131072 | bytes 1048576 | tf_op jit(solution)/shard_map/pallas_call | solution.py:313
  68.5 1.2 %shard_map.102 = f32[2048,128]{1,0:T(8,128)} custom-call(bf16[256,512]{1,0:T(8,128)(2,1)S(1)} %shard_map.100.refs_4_.refs_0_, bf16[256,512]{1,0:T(8,128)(2,1)S(1)} %collective-permute-done.24.refs_1_, f32[2048,128]{1,0:T(8,128)S(1)} %bitcast.16, f32[8,128]{1,0:T(8,128)S(1)} %get-tuple-element.61.refs_3_), custom_call_target="tpu_custom_call" | custom-call | flops 1000000 | bytes 2621440 | tf_op jit(solution)/shard_map/pallas_call | solution.py:296
  (30 shorter events, 0.3 us)
Async XLA Ops:
  0.6 5.7 %copy-start.2 = (bf16[1,1,2,256,256]{4,3,2,1,0:T(8,128)(2,1)S(1)}, bf16[1,1,2,256,256]{4,3,2,1,0:T(8,128)(2,1)}, u32[]{:S(2)}) copy-start(bf16[1,1,2,256,256]{4,3,2,1,0:T(8,128)(2,1)} %refs_3_.1) | copy-start | bytes 786436
  0.6 14.9 %copy-start = (f32[2,256,2,256]{3,2,1,0:T(2,128)S(1)}, f32[2,256,2,256]{3,2,1,0:T(2,128)}, u32[]{:S(2)}) copy-start(f32[2,256,2,256]{3,2,1,0:T(2,128)} %param.8) | copy-start | bytes 3145732
  1.8 13.7 %copy-start.1 = (bf16[512,512]{1,0:T(8,128)(2,1)S(1)}, bf16[512,512]{1,0:T(8,128)(2,1)}, u32[]{:S(2)}) copy-start(bf16[512,512]{1,0:T(8,128)(2,1)} %constant.10.refs_1_) | copy-start | bytes 1572868
  1.8 12.2 %collective-permute-start.5 = (bf16[2,256,256]{2,1,0:T(8,128)(2,1)S(1)}, bf16[2,256,256]{2,1,0:T(8,128)(2,1)S(1)}, u32[]{:S(2)}, u32[]{:S(2)}) collective-permute-start(bf16[2,256,256]{2,1,0:T(8,128)(2,1)S(1)} %get-tuple-element.63.refs_4_.refs_2_.refs_0_), channel_id=1, source_target_pairs={{8,0},{10,2},{12,4},{14,6},{16,8},{18,10},{20,12},{22,14},{24,16},... | collective-permute-start | bytes 786440 | tf_op jit(solution)/shard_map/ppermute | solution.py:27
  3.3 17.4 %collective-permute-start.1 = (bf16[2,2,256,256]{3,2,1,0:T(8,128)(2,1)}, bf16[2,2,256,256]{3,2,1,0:T(8,128)(2,1)S(1)}, u32[]{:S(2)}, u32[]{:S(2)}) collective-permute-start(bf16[2,2,256,256]{3,2,1,0:T(8,128)(2,1)} %bitcast.18), channel_id=1, source_target_pairs={{2,0},{4,2},{6,4},{0,6},{10,8},{12,10},{14,12},{8,14},{18,16},{20,... | collective-permute-start | bytes 1572872 | tf_op jit(solution)/shard_map/ppermute | solution.py:37
  6.4 0.7 copy-start.3
  7.6 11.2 %collective-permute-start.2 = (bf16[2,256,256]{2,1,0:T(8,128)(2,1)S(1)}, bf16[2,256,256]{2,1,0:T(8,128)(2,1)S(1)}, u32[]{:S(2)}, u32[]{:S(2)}) collective-permute-start(bf16[2,256,256]{2,1,0:T(8,128)(2,1)S(1)} %get-tuple-element.34.refs_2_.refs_0_), channel_id=1, source_target_pairs={{8,0},{10,2},{12,4},{14,6},{16,8},{18,10},{20,12},{22,14},{24,16},... | collective-permute-start | bytes 786440 | tf_op jit(solution)/shard_map/ppermute | solution.py:27
  14.0 6.6 %collective-permute-start.6 = (bf16[2,256,256]{2,1,0:T(8,128)(2,1)S(1)}, bf16[2,256,256]{2,1,0:T(8,128)(2,1)S(1)}, u32[]{:S(2)}, u32[]{:S(2)}) collective-permute-start(bf16[2,256,256]{2,1,0:T(8,128)(2,1)S(1)} %collective-permute-done.5.refs_4_), channel_id=1, source_target_pairs={{2,0},{4,2},{6,4},{0,6},{10,8},{12,10},{14,12},{8,14},{18,16},{20,... | collective-permute-start | bytes 786440 | tf_op jit(solution)/shard_map/ppermute | solution.py:37
  14.0 6.6 %collective-permute-start = (bf16[272,256]{1,0:T(8,128)(2,1)S(1)}, bf16[272,256]{1,0:T(8,128)(2,1)S(1)}, u32[]{:S(2)}, u32[]{:S(2)}) collective-permute-start(bf16[272,256]{1,0:T(8,128)(2,1)S(1)} %get-tuple-element.33), channel_id=1, source_target_pairs={{0,1},{1,0},{2,3},{3,2},{4,5},{5,4},{6,7},{7,6},{8,9},{9,8},{10,11... | collective-permute-start | bytes 417800 | tf_op jit(solution)/shard_map/ppermute | solution.py:467
  18.8 3.6 %collective-permute-start.3 = (bf16[256,256]{1,0:T(8,128)(2,1)S(1)}, bf16[256,256]{1,0:T(8,128)(2,1)S(1)}, u32[]{:S(2)}, u32[]{:S(2)}) collective-permute-start(bf16[256,256]{1,0:T(8,128)(2,1)S(1)} %get-tuple-element.35), channel_id=1, source_target_pairs={{2,0},{4,2},{6,4},{0,6},{10,8},{12,10},{14,12},{8,14},{18,16},{20,... | collective-permute-start | bytes 393224 | tf_op jit(solution)/shard_map/ppermute | solution.py:37
  19.6 3.9 %collective-permute-start.4 = (bf16[256,256]{1,0:T(8,128)(2,1)S(1)}, bf16[256,256]{1,0:T(8,128)(2,1)S(1)}, u32[]{:S(2)}, u32[]{:S(2)}) collective-permute-start(bf16[256,256]{1,0:T(8,128)(2,1)S(1)} %get-tuple-element.36), channel_id=1, source_target_pairs={{2,0},{4,2},{6,4},{0,6},{10,8},{12,10},{14,12},{8,14},{18,16},{20,... | collective-permute-start | bytes 393224 | tf_op jit(solution)/shard_map/ppermute | solution.py:37
  20.7 2.8 %copy-start.4 = (bf16[512,512]{1,0:T(8,128)(2,1)S(1)}, bf16[512,512]{1,0:T(8,128)(2,1)}, u32[]{:S(2)}) copy-start(bf16[512,512]{1,0:T(8,128)(2,1)} %constant.11.refs_11_) | copy-start | bytes 1572868
  28.1 2.9 %collective-permute-start.7 = (bf16[256,512]{1,0:T(8,128)(2,1)S(1)}, bf16[256,512]{1,0:T(8,128)(2,1)S(1)}, u32[]{:S(2)}, u32[]{:S(2)}) collective-permute-start(bf16[256,512]{1,0:T(8,128)(2,1)S(1)} %get-tuple-element.42), channel_id=1, source_target_pairs={{0,2},{1,3},{2,0},{3,1},{4,6},{5,7},{6,4},{7,5},{8,10},{9,11},{10,... | collective-permute-start | bytes 786440 | tf_op jit(solution)/shard_map/ppermute | solution.py:402
  29.4 11.9 %collective-permute-start.9 = (bf16[528,256]{1,0:T(8,128)(2,1)S(1)}, bf16[528,256]{1,0:T(8,128)(2,1)S(1)}, u32[]{:S(2)}, u32[]{:S(2)}) collective-permute-start(bf16[528,256]{1,0:T(8,128)(2,1)S(1)} %get-tuple-element.48), channel_id=1, source_target_pairs={{24,0},{26,2},{28,4},{30,6},{0,8},{2,10},{4,12},{6,14},{8,16},{10,... | collective-permute-start | bytes 811016 | tf_op jit(solution)/shard_map/ppermute | solution.py:37
  31.7 16.4 %collective-permute-start.8 = (bf16[528,256]{1,0:T(8,128)(2,1)S(1)}, bf16[528,256]{1,0:T(8,128)(2,1)S(1)}, u32[]{:S(2)}, u32[]{:S(2)}) collective-permute-start(bf16[528,256]{1,0:T(8,128)(2,1)S(1)} %get-tuple-element.45), channel_id=1, source_target_pairs={{24,0},{26,2},{28,4},{30,6},{0,8},{2,10},{4,12},{6,14},{8,16},{10,... | collective-permute-start | bytes 811016 | tf_op jit(solution)/shard_map/ppermute | solution.py:37
  33.4 4.3 %collective-permute-start.10 = (bf16[64,512]{1,0:T(8,128)(2,1)S(1)}, bf16[64,512]{1,0:T(8,128)(2,1)S(1)}, u32[]{:S(2)}, u32[]{:S(2)}) collective-permute-start(bf16[64,512]{1,0:T(8,128)(2,1)S(1)} %get-tuple-element.51), channel_id=1, source_target_pairs={{0,1},{1,0},{2,3},{3,2},{4,5},{5,4},{6,7},{7,6},{8,9},{9,8},{10,11... | collective-permute-start | bytes 196616 | tf_op jit(solution)/shard_map/ppermute | solution.py:402
  34.9 4.3 %collective-permute-start.11 = (bf16[64,512]{1,0:T(8,128)(2,1)S(1)}, bf16[64,512]{1,0:T(8,128)(2,1)S(1)}, u32[]{:S(2)}, u32[]{:S(2)}) collective-permute-start(bf16[64,512]{1,0:T(8,128)(2,1)S(1)} %get-tuple-element.52), channel_id=1, source_target_pairs={{0,4},{1,5},{2,6},{3,7},{4,0},{5,1},{6,2},{7,3},{8,12},{9,13},{10,... | collective-permute-start | bytes 196616 | tf_op jit(solution)/shard_map/ppermute | solution.py:402
  36.1 5.2 %collective-permute-start.12 = (bf16[64,512]{1,0:T(8,128)(2,1)S(1)}, bf16[64,512]{1,0:T(8,128)(2,1)S(1)}, u32[]{:S(2)}, u32[]{:S(2)}) collective-permute-start(bf16[64,512]{1,0:T(8,128)(2,1)S(1)} %get-tuple-element.53), channel_id=1, source_target_pairs={{0,5},{1,4},{2,7},{3,6},{4,1},{5,0},{6,3},{7,2},{8,13},{9,12},{10,... | collective-permute-start | bytes 196616 | tf_op jit(solution)/shard_map/ppermute | solution.py:402
  41.4 4.4 %collective-permute-start.13 = (bf16[256,256]{1,0:T(8,128)(2,1)S(1)}, bf16[256,256]{1,0:T(8,128)(2,1)S(1)}, u32[]{:S(2)}, u32[]{:S(2)}) collective-permute-start(bf16[256,256]{1,0:T(8,128)(2,1)S(1)} %get-tuple-element.54), channel_id=1, source_target_pairs={{6,0},{0,2},{2,4},{4,6},{14,8},{8,10},{10,12},{12,14},{22,16},{16,... | collective-permute-start | bytes 393224 | tf_op jit(solution)/shard_map/ppermute | solution.py:37
  41.5 5.8 %collective-permute-start.14 = (bf16[256,256]{1,0:T(8,128)(2,1)S(1)}, bf16[256,256]{1,0:T(8,128)(2,1)S(1)}, u32[]{:S(2)}, u32[]{:S(2)}) collective-permute-start(bf16[256,256]{1,0:T(8,128)(2,1)S(1)} %get-tuple-element.55), channel_id=1, source_target_pairs={{6,0},{0,2},{2,4},{4,6},{14,8},{8,10},{10,12},{12,14},{22,16},{16,... | collective-permute-start | bytes 393224 | tf_op jit(solution)/shard_map/ppermute | solution.py:37
  42.4 7.1 %collective-permute-start.17 = (bf16[64,512]{1,0:T(8,128)(2,1)S(1)}, bf16[64,512]{1,0:T(8,128)(2,1)S(1)}, u32[]{:S(2)}, u32[]{:S(2)}) collective-permute-start(bf16[64,512]{1,0:T(8,128)(2,1)S(1)} %shard_map.92.refs_2_.refs_0_), channel_id=1, source_target_pairs={{0,8},{1,9},{2,10},{3,11},{4,12},{5,13},{6,14},{7,15},{8,0},{9,1},... | collective-permute-start | bytes 196616 | tf_op jit(solution)/shard_map/ppermute | solution.py:402
  47.4 13.4 %collective-permute-start.20 = (bf16[2,256,256]{2,1,0:T(8,128)(2,1)S(1)}, bf16[2,256,256]{2,1,0:T(8,128)(2,1)S(1)}, u32[]{:S(2)}, u32[]{:S(2)}) collective-permute-start(bf16[2,256,256]{2,1,0:T(8,128)(2,1)S(1)} %shard_map.94.refs_2_.refs_1_), channel_id=1, source_target_pairs={{0,1},{1,0},{2,3},{3,2},{4,5},{5,4},{6,7},{7,6},{8,9},{9,8},{10,11... | collective-permute-start | bytes 786440 | tf_op jit(solution)/shard_map/ppermute | solution.py:497
  48.3 10.3 %collective-permute-start.16 = (bf16[256,256]{1,0:T(8,128)(2,1)S(1)}, bf16[256,256]{1,0:T(8,128)(2,1)S(1)}, u32[]{:S(2)}, u32[]{:S(2)}) collective-permute-start(bf16[256,256]{1,0:T(8,128)(2,1)S(1)} %get-tuple-element.57), channel_id=1, source_target_pairs={{6,0},{0,2},{2,4},{4,6},{14,8},{8,10},{10,12},{12,14},{22,16},{16,... | collective-permute-start | bytes 393224 | tf_op jit(solution)/shard_map/ppermute | solution.py:37
  48.3 11.2 %collective-permute-start.15 = (bf16[256,256]{1,0:T(8,128)(2,1)S(1)}, bf16[256,256]{1,0:T(8,128)(2,1)S(1)}, u32[]{:S(2)}, u32[]{:S(2)}) collective-permute-start(bf16[256,256]{1,0:T(8,128)(2,1)S(1)} %get-tuple-element.56.refs_2_), channel_id=1, source_target_pairs={{6,0},{0,2},{2,4},{4,6},{14,8},{8,10},{10,12},{12,14},{22,16},{16,... | collective-permute-start | bytes 393224 | tf_op jit(solution)/shard_map/ppermute | solution.py:37
  49.5 6.4 %collective-permute-start.18 = (bf16[64,512]{1,0:T(8,128)(2,1)S(1)}, bf16[64,512]{1,0:T(8,128)(2,1)S(1)}, u32[]{:S(2)}, u32[]{:S(2)}) collective-permute-start(bf16[64,512]{1,0:T(8,128)(2,1)S(1)} %shard_map.96.refs_0_), channel_id=1, source_target_pairs={{0,16},{1,17},{2,18},{3,19},{4,20},{5,21},{6,22},{7,23},{8,24},{9,... | collective-permute-start | bytes 196616 | tf_op jit(solution)/shard_map/ppermute | solution.py:402
  55.9 5.7 %collective-permute-start.23 = (bf16[64,512]{1,0:T(8,128)(2,1)S(1)}, bf16[64,512]{1,0:T(8,128)(2,1)S(1)}, u32[]{:S(2)}, u32[]{:S(2)}) collective-permute-start(bf16[64,512]{1,0:T(8,128)(2,1)S(1)} %shard_map.97.refs_4_.refs_0_), channel_id=1, source_target_pairs={{0,5},{1,4},{2,7},{3,6},{4,1},{5,0},{6,3},{7,2},{8,13},{9,12},{10,... | collective-permute-start | bytes 196616 | tf_op jit(solution)/shard_map/ppermute | solution.py:402
  57.7 4.3 %collective-permute-start.22 = (bf16[64,512]{1,0:T(8,128)(2,1)S(1)}, bf16[64,512]{1,0:T(8,128)(2,1)S(1)}, u32[]{:S(2)}, u32[]{:S(2)}) collective-permute-start(bf16[64,512]{1,0:T(8,128)(2,1)S(1)} %shard_map.97.refs_4_.refs_0_), channel_id=1, source_target_pairs={{0,4},{1,5},{2,6},{3,7},{4,0},{5,1},{6,2},{7,3},{8,12},{9,13},{10,... | collective-permute-start | bytes 196616 | tf_op jit(solution)/shard_map/ppermute | solution.py:402
  58.5 5.0 %collective-permute-start.21 = (bf16[64,512]{1,0:T(8,128)(2,1)S(1)}, bf16[64,512]{1,0:T(8,128)(2,1)S(1)}, u32[]{:S(2)}, u32[]{:S(2)}) collective-permute-start(bf16[64,512]{1,0:T(8,128)(2,1)S(1)} %shard_map.97.refs_4_.refs_0_), channel_id=1, source_target_pairs={{0,1},{1,0},{2,3},{3,2},{4,5},{5,4},{6,7},{7,6},{8,9},{9,8},{10,11... | collective-permute-start | bytes 196616 | tf_op jit(solution)/shard_map/ppermute | solution.py:402
  59.6 8.0 %collective-permute-start.19 = (bf16[2,256,256]{2,1,0:T(8,128)(2,1)S(1)}, bf16[2,256,256]{2,1,0:T(8,128)(2,1)S(1)}, u32[]{:S(2)}, u32[]{:S(2)}) collective-permute-start(bf16[2,256,256]{2,1,0:T(8,128)(2,1)S(1)} %shard_map.98.refs_3_.refs_1_), channel_id=1, source_target_pairs={{0,1},{1,0},{2,3},{3,2},{4,5},{5,4},{6,7},{7,6},{8,9},{9,8},{10,11... | collective-permute-start | bytes 786440 | tf_op jit(solution)/shard_map/ppermute | solution.py:497
  63.6 4.9 %collective-permute-start.24 = (bf16[256,512]{1,0:T(8,128)(2,1)S(1)}, bf16[256,512]{1,0:T(8,128)(2,1)S(1)}, u32[]{:S(2)}, u32[]{:S(2)}) collective-permute-start(bf16[256,512]{1,0:T(8,128)(2,1)S(1)} %shard_map.100.refs_4_.refs_0_), channel_id=1, source_target_pairs={{0,2},{1,3},{2,0},{3,1},{4,6},{5,7},{6,4},{7,5},{8,10},{9,11},{10,... | collective-permute-start | bytes 786440 | tf_op jit(solution)/shard_map/ppermute | solution.py:402

commit v13 on v10

--- a/solution.py
+++ b/solution.py
@@ -15,7 +15,7 @@
 object_rate = 0.05
 probe_rate = 0.15
 
-LATE = [0, 8_000_000_000, 0, 30_000_000_000, 0, 15_000_000_000, 0, 4_000_000_000]
+LATE = [work * 1_000_000_000 for work in (0, 8, 0, 0, 8, 0, 8, 4)]
 
 f32 = jnp.float32
 bf16 = jnp.bfloat16
@@ -59,24 +59,36 @@
     return jnp.dot(a, b, preferred_element_type=f32)
 
 
-def shift_tables(mine_ref, sent_ref):
+def spots(mine_ref, sent_ref):
     n = mine_ref.shape[1]
     mine = mine_ref[n:, :].astype(f32)
-    sent = sent_ref[n:, :].astype(f32)
     busy = mine[2:3] > 0
-    row = jnp.where(busy, mine[0:1], sent[0:1]).astype(jnp.int32)
-    col = jnp.where(busy, mine[1:2], sent[1:2]).astype(jnp.int32)
+    rows = jnp.where(busy, mine, sent_ref[n:, :].astype(f32)).astype(jnp.int32)
+    return (rows[0:1], rows[1:2]), (rows[3:4], rows[4:5]), busy
+
+
+def shift_in(spot):
+    row, col = spot
+    n = row.shape[1]
     i_out = lax.broadcasted_iota(jnp.int32, (n, 2 * n), 0)
     i_in = lax.broadcasted_iota(jnp.int32, (n, 2 * n), 1)
     j_in = lax.broadcasted_iota(jnp.int32, (2 * n, n), 0)
     j_out = lax.broadcasted_iota(jnp.int32, (2 * n, n), 1)
-    row2 = jnp.concatenate([row, row], axis=1)
-    col2 = jnp.concatenate([col, col], axis=1)
-    rows = (i_in == i_out + row2).astype(f32).astype(bf16)
-    cols = (j_in == j_out + col).astype(f32).astype(bf16)
-    rows_t = (j_in == j_out + row).astype(f32).astype(bf16)
-    cols_t = (i_in == i_out + col2).astype(f32).astype(bf16)
-    return rows, cols, rows_t, cols_t, col, busy
+    rows = i_in == i_out + jnp.concatenate([row, row], axis=1)
+    cols = j_in == j_out + col
+    return rows.astype(f32).astype(bf16), cols.astype(f32).astype(bf16)
+
+
+def shift_out(spot):
+    row, col = spot
+    n = row.shape[1]
+    i_out = lax.broadcasted_iota(jnp.int32, (n, 2 * n), 0)
+    i_in = lax.broadcasted_iota(jnp.int32, (n, 2 * n), 1)
+    j_in = lax.broadcasted_iota(jnp.int32, (2 * n, n), 0)
+    j_out = lax.broadcasted_iota(jnp.int32, (2 * n, n), 1)
+    rows = j_in == j_out + row
+    cols = i_in == i_out + jnp.concatenate([col, col], axis=1)
+    return rows.astype(f32).astype(bf16), cols.astype(f32).astype(bf16)
 
 
 def patch(shifts, own_ref, right_ref, below_ref, diag_ref, part):
@@ -117,7 +129,9 @@
     busy = (counts_ref[0, 0] == patterns_ref.shape[2]).astype(jnp.int32)
     for slot, ref in enumerate((mine_ref, sent_ref)):
         row, col = offsets_ref[0, 0, slot, 0], offsets_ref[0, 0, slot, 1]
+        row2, col2 = offsets_ref[0, 0, 1 - slot, 0], offsets_ref[0, 0, 1 - slot, 1]
         rows = jnp.where(at == 0, row, jnp.where(at == 1, col, busy))
+        rows = jnp.where(at == 3, row2, jnp.where(at == 4, col2, rows))
         ref[pl.ds(0, n), :] = patterns_ref[0, 0, slot]
         ref[pl.ds(n, 16), :] = rows.astype(f32).astype(bf16)
 
@@ -136,7 +150,7 @@
     near_ref, arrive_ref,
 ):
     n = own_ref.shape[1]
-    shifts = shift_tables(mine_ref, sent_ref)
+    shifts = shift_in(spots(mine_ref, sent_ref)[0])
     tiles = (own_ref, right_ref.at[0], below_ref, diag_ref)
     near = [patch(shifts, *tiles, part) for part in range(2)]
     for part in range(2):
@@ -150,28 +164,15 @@
         arrive_ref[1, :, lanes] = -a_neg
 
 
-def spread(shifts, grad, home_ref, next_ref, down_ref, layer):
-    rows_t, cols_t = shifts[2:4]
-    n = rows_t.shape[1]
-    wrap_cols = cols_t[:, :n] + cols_t[:, n:]
-    for part in range(2):
-        rows = dot(rows_t, grad[part].astype(bf16)).astype(bf16)
-        wide = dot(rows[:n], cols_t).astype(bf16)
-        home_ref[part] = wide[:, :n]
-        next_ref[part] = wide[:, n:]
-        where = pl.ds((2 * layer + part) * n, n)
-        down_ref[where, :] = dot(rows[n:], wrap_cols).astype(bf16)
-
-
 def gradient_kernel(
     mine_ref, sent_ref, own_ref, right_ref, below_ref, diag_ref, near_ref, arrive_ref, planes_ref,
     prop_ref, dft_ref,
-    home0_ref, next0_ref, home1_ref, next1_ref, down_ref, keep_ref, give_ref, term_ref,
+    kept_ref, given_ref, keep_ref, give_ref, grad_ref, term_ref, *, layer
 ):
     n = own_ref.shape[1]
     modes = planes_ref.shape[2] // n
-    shifts = shift_tables(mine_ref, sent_ref)
-    busy = shifts[5]
+    spot, _, busy = spots(mine_ref, sent_ref)
+    shifts = shift_in(spot)
     tiles = (own_ref, right_ref.at[1], below_ref, diag_ref)
     far = [patch(shifts, *tiles, part) for part in range(2)]
     fields = []
@@ -193,7 +194,8 @@
         grad[0] += a_re * b_re + a_im * b_im
         grad[1] += a_re * b_im - a_im * b_re
         waves.append(stacked(far[0] * b_re + far[1] * b_im, far[1] * b_re - far[0] * b_im))
-    spread(shifts, grad, home1_ref, next1_ref, down_ref, 1)
+    for part in range(2):
+        grad_ref[1, part] = grad[part].astype(bf16)
     grad = [0.0, 0.0]
     near = [near_ref[part].astype(f32) for part in range(2)]
     for mode in range(modes):
@@ -207,39 +209,44 @@
     core = place_of(core_group())
     keep_ref[...] = term_ref[core]
     give_ref[...] = term_ref[1 - core]
-    spread(shifts, grad, home0_ref, next0_ref, down_ref, 0)
-    edge = lax.broadcasted_iota(jnp.int32, (16, n), 1) < shifts[4]
-    down_ref[pl.ds(4 * n, 16), :] = edge.astype(f32).astype(bf16)
-
-
-def above_parts(above_ref, layer, n):
-    where = [pl.ds((2 * layer + part) * n, n) for part in range(2)]
-    split = above_ref[pl.ds(4 * n, 16), :].astype(f32)[0:1] > 0
-    return [above_ref[rows, :].astype(f32) for rows in where], split
-
-
-def beside_kernel(layer, next_ref, above_ref, out_ref):
-    above, split = above_parts(above_ref, layer, out_ref.shape[1])
     for part in range(2):
-        total = next_ref[part].astype(f32) + jnp.where(split, above[part], 0.0)
-        out_ref[part] = total.astype(bf16)
-
-
-def part_kernel(layer, home_ref, above_ref, left_ref, out_ref):
-    above, split = above_parts(above_ref, layer, out_ref.shape[1])
+        grad_ref[0, part] = grad[part].astype(bf16)
+    layer = layer()
+    kept_ref[...] = grad_ref[layer]
+    given_ref[...] = grad_ref[1 - layer]
+
+
+def spread_kernel(
+    mine_ref, sent_ref, kept_ref, got_ref, home_ref, below_ref, right_ref, diag_ref
+):
+    n = mine_ref.shape[1]
+    first, second, _ = spots(mine_ref, sent_ref)
+    rows1, cols1 = shift_out(first)
+    rows2, cols2 = shift_out(second)
+    cols = jnp.concatenate([cols1, cols2], axis=0)
     for part in range(2):
-        total = home_ref[part].astype(f32) + jnp.where(split, 0.0, above[part])
-        out_ref[part] = (total + left_ref[part].astype(f32)).astype(bf16)
-
-
-def update_kernel(layer, own_ref, part_ref, other_ref, *refs):
-    out_hbm, token_ref, new_ref, sem = refs[-4:]
+        tall1 = dot(rows1, kept_ref[part]).astype(bf16)
+        tall2 = dot(rows2, got_ref[part]).astype(bf16)
+        wide = dot(jnp.concatenate([tall1, tall2], axis=1), cols)
+        home_ref[part] = wide[:n, :n]
+        right_ref[part] = wide[:n, n:].astype(bf16)
+        below_ref[part] = wide[n:, :n]
+        diag_ref[part] = wide[n:, n:].astype(bf16)
+
+
+def beside_kernel(home_ref, below_ref, right_ref, diag_ref, home_out, down_ref):
+    home_out[...] = home_ref[...] + right_ref[...].astype(f32)
+    down_ref[...] = (below_ref[...] + diag_ref[...].astype(f32)).astype(bf16)
+
+
+def slice_kernel(layer, own0_ref, own1_ref, home_ref, above_ref, out_ref):
+    grad = home_ref[...] + above_ref[...].astype(f32)
+    own = jnp.where(layer() == 0, own0_ref[...].astype(f32), own1_ref[...].astype(f32))
+    out_ref[...] = (own - object_rate * grad).astype(bf16)
+
+
+def token_kernel(token_ref):
     token_ref[...] = jnp.zeros_like(token_ref)
-    grad = part_ref[...].astype(f32) + other_ref[...].astype(f32)
-    new_ref[...] = (own_ref[...].astype(f32) - object_rate * grad).astype(bf16)
-    copy = pltpu.make_async_copy(new_ref, out_hbm.at[0, layer], sem.at[0])
-    copy.start()
-    copy.wait()
 
 
 def core_group():
@@ -291,22 +298,35 @@
     return results[0] if len(jobs) == 1 else results
 
 
-def updated(layer, own, part, other, like, so_far=None, flops=0, after=()):
+def finished(layer, step, modes, halves, probe, slices, like, after):
     vmem = pl.BlockSpec(memory_space=pltpu.VMEM)
     anywhere = pl.BlockSpec(memory_space=pl.ANY)
-    extra = [x for x in (so_far,) if x is not None] + list(after)
+    inputs = [*halves, probe, *slices]
+
+    def body(*refs):
+        blocks, (out_probe, out_tile, sems) = refs[3 : len(inputs)], refs[-3:]
+        places = [layer(), 1 - layer()][: len(blocks)]
+        copies = [
+            pltpu.make_async_copy(block, out_tile.at[0, place], sems.at[at])
+            for at, (block, place) in enumerate(zip(blocks, places))
+        ]
+        for copy in copies:
+            copy.start()
+        probe_kernel(step, modes, *refs[:3], out_probe)
+        for copy in copies:
+            copy.wait()
+
     return pl.pallas_call(
-        lambda *refs: update_kernel(layer, *refs),
-        out_shape=[like, shape_of(f32, 8, 128)],
-        in_specs=[vmem] * 3 + [anywhere] * len(extra),
-        out_specs=[anywhere, vmem],
-        scratch_shapes=[pltpu.VMEM(own.shape, bf16), pltpu.SemaphoreType.DMA((1,))],
-        input_output_aliases={} if so_far is None else {3: 0},
-        compiler_params=pltpu.CompilerParams(vmem_limit_bytes=4 * 2**20),
+        body,
+        out_shape=[shape_of(f32, *probe.shape), like],
+        in_specs=[vmem] * len(inputs) + [anywhere] * len(after),
+        out_specs=[vmem, anywhere],
+        scratch_shapes=[pltpu.SemaphoreType.DMA((2,))],
+        compiler_params=pltpu.CompilerParams(vmem_limit_bytes=8 * 2**20),
         cost_estimate=pl.CostEstimate(
-            flops=own.size + flops, bytes_accessed=8 * own.size, transcendentals=0
+            flops=4 * probe.size, bytes_accessed=12 * probe.size, transcendentals=0
         ),
-    )(own, part, other, *extra)
+    )(*inputs, *after)
 
 
 def shape_of(kind, *dims):
@@ -463,32 +483,34 @@
         limit=16,
     )
     half = shape_of(bf16, pixels, width)
-    home0, next0, home1, next1, down, keep, give = run(
+    grads = pltpu.VMEM((2, 2, pixels, pixels), bf16)
+    this_layer = (lambda: lax.axis_index("pos")) if exchanged else (lambda: 0)
+    kept, given, keep, give = run(
         job(
-            gradient_kernel,
-            [tile] * 4 + [shape_of(bf16, 4 * pixels + 16, pixels), half, half],
+            lambda *refs: gradient_kernel(*refs, layer=this_layer),
+            [tile, tile, half, half],
             [mine, sent, own1, right, below1, diag1, near, arrive, probe_planes, table, dft],
-            scratch=[pltpu.VMEM((2, pixels, width), bf16)],
+            scratch=[grads, pltpu.VMEM((2, pixels, width), bf16)],
         ),
         flops=4_000_000_000,
         limit=16,
     )
 
-    def over_owners(part):
-        if lax.axis_size("pos") == 2:
-            return lax.ppermute(part, "pos", [(0, 1), (1, 0)])
-        return lax.psum(part.astype(f32), "pos") - part.astype(f32)
-
-    def beside(layer, next_tile):
-        kernel = lambda *refs: beside_kernel(layer, *refs)
-        return job(kernel, [tile], [next_tile, above])
-
-    def part(layer, home, left):
-        kernel = lambda *refs: part_kernel(layer, *refs)
-        return job(kernel, [tile], [home, above, left])
+    swap = [(i, 1 - i) for i in range(2)]
+    real = shape_of(f32, 2, pixels, pixels)
+    like = shape_of(bf16, *tile_object.shape)
+
+    def laid_out(patch, got, after, flops):
+        return run(
+            job(spread_kernel, [real, real, tile, tile], [mine, sent, patch, got]),
+            limit=16,
+            after=after,
+            flops=flops,
+        )
 
     core, groups = core_group(), exchange_groups()
-    above = from_behind(down, 1, 0)
+    if exchanged:
+        got = lax.ppermute(given, "pos", swap)
     arrived = [swap_with(give, core, 1)]
     scattered = []
     while len(groups) > 1 and keep.shape[0] >> len(groups[0]) >= 16:
@@ -497,43 +519,63 @@
         arrived = [swap_with(x, group, at) for at, x in enumerate(gives, 1)]
         scattered.append(group)
     first, second, *others = [[bit] for group in groups for bit in group]
-    (total,) = run(added(keep, arrived))
-    arrived = swapped(total, first)
-    (beside1,), (beside0,) = run(
-        beside(1, next1), beside(0, next0), after=[total], flops=LATE[0]
-    )
-    left1 = from_behind(beside1, 0, 1)
-    left0 = from_behind(beside0, 0, 1)
-    (total,) = run(added(total, arrived), after=[beside1], flops=LATE[1])
+    if exchanged:
+        home, below, to_right, to_diag = laid_out(kept, got, [keep], LATE[0])
+        from_left = [from_behind(x, 0, 1) for x in (to_right, to_diag)]
+    (total,) = run(added(keep, arrived), after=[to_right] if exchanged else [], flops=LATE[1])
+    (total,) = run(added(total, swapped(total, first)), flops=LATE[2])
     arrived = swapped(total, second)
-    (part1,) = run(part(1, home1, left1), after=[total], flops=LATE[2])
-    other1 = over_owners(part1)
-    (total,) = run(added(total, arrived), after=[part1], flops=LATE[3])
+    if exchanged:
+        home, down = run(
+            job(beside_kernel, [real, tile], [home, below, *from_left]),
+            after=[total],
+            flops=LATE[3],
+        )
+        above = from_behind(down, 1, 0)
+    (total,) = run(added(total, arrived), after=[down] if exchanged else [], flops=LATE[4])
     for group in others:
         (total,) = run(added(total, swapped(total, group)))
     arrived = swapped(total, scattered[-1])
-    (part0,) = run(part(0, home0, left0), after=[total], flops=LATE[4])
-    other0 = over_owners(part0)
-    like = shape_of(bf16, *tile_object.shape)
-    new_object, token = updated(1, own1, part1, other1, like, flops=LATE[5], after=[part0])
-    (total,) = run(joined(scattered[-1], total, arrived), after=[token], flops=LATE[6])
+    if exchanged:
+        (this_slice,) = run(
+            job(
+                lambda *refs: slice_kernel(this_layer, *refs),
+                [tile],
+                [own[0], own1, home, above],
+            ),
+            after=[total],
+            flops=LATE[5],
+        )
+        other_slice = lax.ppermute(this_slice, "pos", swap)
+    (total,) = run(
+        joined(scattered[-1], total, arrived),
+        after=[this_slice] if exchanged else [],
+        flops=LATE[6],
+    )
     for group in reversed(scattered[:-1]):
         (total,) = run(joined(group, total, swapped(total, group)))
     other_half = swap_with(total, core, 1)
-    new_object, token = updated(
-        0, own[0], part0, other0, like, so_far=new_object, flops=LATE[7], after=[total]
-    )
     positions_all = lax.axis_size("tile") * lax.axis_size("pos") * (patterns.shape[2] // 2)
     step = probe_rate / math.sqrt(positions_all)
-    (new_probe,) = run(
-        job(
-            lambda *refs: probe_kernel(step, modes, *refs),
-            [shape_of(f32, *probe.shape)],
-            [total, other_half, probe],
-        ),
-        limit=8,
-        after=[token],
-    )
+    halves = (total, other_half)
+    if exchanged:
+        token = run(
+            job(token_kernel, [shape_of(f32, 8, 128)], []),
+            after=[total, other_slice],
+            flops=LATE[7],
+        )
+        slices = (this_slice, other_slice)
+        new_probe, new_object = finished(this_layer, step, modes, halves, probe, slices, like, token)
+    else:
+        new_probe, _ = finished(this_layer, step, modes, halves, probe, (), like, ())
+        slices = []
+        for patch_grad, old in ((kept, own[0]), (given, own1)):
+            home, below, to_right, to_diag = laid_out(patch_grad, jnp.zeros_like(kept), [], 0)
+            from_left = [from_behind(x, 0, 1) for x in (to_right, to_diag)]
+            home, down = run(job(beside_kernel, [real, tile], [home, below, *from_left]))
+            grad = lax.psum(home + from_behind(down, 1, 0).astype(f32), "pos")
+            slices.append((old.astype(f32) - object_rate * grad).astype(bf16))
+        new_object = jnp.stack(slices)[None]
     new_probe = new_probe.reshape(2, pixels, lane_tiles, modes, 128).transpose(0, 1, 3, 2, 4)
     return (new_object, new_probe.reshape(probe_modes.shape))
 

time: 68.6 us -> 65.5 us (0.955)
  waiting for transfers between devices: 30.7 us -> 27.1 us
  starting transfers between devices: 23.3 us -> 25.3 us
  Pallas kernels: 11.1 us -> 9.61 us
    ppermute x8, waiting for transfers between devices: 14.6 us -> 11.1 us  [from_behind(): return lax.ppermute(block, 'tile', [(source(i), i) for i in range(tiles)])]
    ppermute x10, waiting for transfers between devices: 7.48 us -> 4.87 us  [swap_with(): lax.ppermute(x, ('tile', 'pos'), [(i, i ^ mask) for i in range(devices)])]
    ppermute x2, waiting for transfers between devices: 7.45 us -> 9.9 us  [the longest x1 5.21 us: shards(): got = lax.ppermute(given, 'pos', swap)]
    pallas_call x13, Pallas kernels: 9.46 us -> 7.83 us  [run(): pl.pallas_call(body, out_shape=sum(outs, []), in_specs=sum(specs, []) + [...]
    ppermute x8, starting transfers between devices: 7.73 us -> 9.13 us  [from_behind(): return lax.ppermute(block, 'tile', [(source(i), i) for i in range(tiles)])]
    ppermute x10, starting transfers between devices: 10.8 us -> 11.6 us  [swap_with(): lax.ppermute(x, ('tile', 'pos'), [(i, i ^ mask) for i in range(devices)])]
    pallas_call x2 -> x1, Pallas kernels: 1.65 us -> 1.78 us  [finished(): pl.pallas_call(body, out_shape=[shape_of(f32, *probe.shape), like], in_sp...]
  transfers between devices with their start and end apart: 21 -> 21, of which waited for: 15 -> 10; matrix products, arithmetic and copies ran while one was open for 0% -> 0% of each run, Pallas kernels for 7% -> 6%
where the time goes in v13:
time: 65.5 us; the launch traced here: 65.3 us
  waiting for transfers between devices  27.1 us (41%)
  starting transfers between devices  25.3 us (39%)
  Pallas kernels  9.61 us (15%)
  local copies, waits for them, and re-layouts  1.86 us (3%)
  between operations  1.43 us (2%)
    ppermute x10, starting transfers between devices, swap_with(): lax.ppermute(x, ('tile', 'pos'), [(i, i ^ mask) for i in range(devices)])  11.6 us
    ppermute x8, waiting for transfers between devices, from_behind(): return lax.ppermute(block, 'tile', [(source(i), i) for i in range(tiles)])  11.1 us
    ppermute x8, starting transfers between devices, from_behind(): return lax.ppermute(block, 'tile', [(source(i), i) for i in range(tiles)])  9.13 us
    pallas_call x13, Pallas kernels, run(): pl.pallas_call(body, out_shape=sum(outs, []), in_specs=sum(specs, []) + [...  7.83 us
    ppermute x1, waiting for transfers between devices, shards(): got = lax.ppermute(given, 'pos', swap)  5.21 us
    ppermute x10, waiting for transfers between devices, swap_with(): lax.ppermute(x, ('tile', 'pos'), [(i, i ^ mask) for i in range(devices)])  4.87 us
    ppermute x1, waiting for transfers between devices, shards(): other_slice = lax.ppermute(this_slice, 'pos', swap)  4.7 us
    pallas_call x1, Pallas kernels, finished(): pl.pallas_call(body, out_shape=[shape_of(f32, *probe.shape), like], in_sp...  1.78 us
  transfers between devices with their start and end apart: 21, of which 10 were waited for; matrix products, arithmetic and copies ran while one was open for 0% of the time, Pallas kernels for 6%

profile of v13, /device:TPU:0, one launch (start us, length us, event | category | flops | bytes accessed | tf_op | source)
XLA Modules:
  0.0 65.3 jit_solution(15803555662971827277)
XLA Ops:
  0.6 1.2 %slice_bitcast_fusion = (bf16[2,256,256]{2,1,0:T(8,128)(2,1)S(1)}, bf16[2,256,256]{2,1,0:T(8,128)(2,1)S(1)}) fusion(bf16[1,2,2,256,256]{4,3,2,1,0:T(8,128)(2,1)} %param.7), kind=kLoop, calls=%fused_computation | loop fusion | bytes 1048576 | tf_op jit(solution)/shard_map/squeeze | solution.py:449
  1.8 0.0 copy-start.1
  1.8 5.1 %collective-permute-start.4 = (bf16[2,256,256]{2,1,0:T(8,128)(2,1)S(1)}, bf16[2,256,256]{2,1,0:T(8,128)(2,1)S(1)}, u32[]{:S(2)}, u32[]{:S(2)}) collective-permute-start(bf16[2,256,256]{2,1,0:T(8,128)(2,1)S(1)} %get-tuple-element.48.refs_4_.refs_2_.refs_0_), channel_id=1, source_target_pairs={{8,0},{10,2},{12,4},{14,6},{16,8},{18,10},{20,12},{22,14},{24,16},... | collective-permute-start | bytes 786440 | tf_op jit(solution)/shard_map/ppermute | solution.py:31
  6.9 0.7 collective-permute-start.1
  8.2 0.0 copy-start.3
  8.3 0.7 %copy-done.3 = s32[1,1,2,2]{3,2,1,0:T(2,128)S(1)} copy-done((s32[1,1,2,2]{3,2,1,0:T(2,128)S(1)}, s32[1,1,2,2]{3,2,1,0:T(2,128)}, u32[]{:S(2)}) %copy-start.3) | copy-done | bytes 40
  8.9 0.6 shard_map.86
  9.5 0.5 collective-permute-start.2
  10.0 3.6 %collective-permute-done.4.refs_4_ = bf16[2,256,256]{2,1,0:T(8,128)(2,1)S(1)} collective-permute-done((bf16[2,256,256]{2,1,0:T(8,128)(2,1)S(1)}, bf16[2,256,256]{2,1,0:T(8,128)(2,1)S(1)}, u32[]{:S(2)}, u32[]{:S(2)}) %collective-permute-start.4) | collective-permute-done | bytes 262176 | tf_op jit(solution)/shard_map/ppermute | solution.py:31
  13.6 0.0 collective-permute-start.5
  13.6 1.5 %collective-permute-start = (bf16[272,256]{1,0:T(8,128)(2,1)S(1)}, bf16[272,256]{1,0:T(8,128)(2,1)S(1)}, u32[]{:S(2)}, u32[]{:S(2)}) collective-permute-start(bf16[272,256]{1,0:T(8,128)(2,1)S(1)} %get-tuple-element.26), channel_id=1, source_target_pairs={{0,1},{1,0},{2,3},{3,2},{4,5},{5,4},{6,7},{7,6},{8,9},{9,8},{10,11... | collective-permute-start | bytes 417800 | tf_op jit(solution)/shard_map/ppermute | solution.py:471
  15.2 2.9 %collective-permute-done.2.refs_4_ = bf16[2,256,256]{2,1,0:T(8,128)(2,1)S(1)} collective-permute-done((bf16[2,256,256]{2,1,0:T(8,128)(2,1)S(1)}, bf16[2,256,256]{2,1,0:T(8,128)(2,1)S(1)}, u32[]{:S(2)}, u32[]{:S(2)}) %collective-permute-start.2) | collective-permute-done | bytes 262176 | tf_op jit(solution)/shard_map/ppermute | solution.py:31
  18.1 0.3 collective-permute-start.3
  18.5 0.1 shard_map.87
  18.6 1.2 %collective-permute-done.refs_1_ = bf16[272,256]{1,0:T(8,128)(2,1)S(1)} collective-permute-done((bf16[272,256]{1,0:T(8,128)(2,1)S(1)}, bf16[272,256]{1,0:T(8,128)(2,1)S(1)}, u32[]{:S(2)}, u32[]{:S(2)}) %collective-permute-start) | collective-permute-done | bytes 139296 | tf_op jit(solution)/shard_map/ppermute | solution.py:471
  19.7 1.8 %shard_map.88 = (bf16[2,256,256]{2,1,0:T(8,128)(2,1)S(1)}, f32[2,256,512]{2,1,0:T(8,128)S(1)}) custom-call(bf16[272,256]{1,0:T(8,128)(2,1)S(1)} %get-tuple-element.25.refs_0_, bf16[272,256]{1,0:T(8,128)(2,1)S(1)} %collective-permute-done.refs_1_, bf16[2,256,256]{2,1,0:T(8,128)(2,1)S(1)} %get-tuple-element.48.refs_4_.refs_2_.refs_0_, ...), custom_call_target="tpu_custom_call" | custom-call | flops 1500000000 | bytes 4472832 | tf_op jit(solution)/shard_map/pallas_call | solution.py:288
  21.5 0.8 %collective-permute-done.3.refs_5_ = bf16[2,256,256]{2,1,0:T(8,128)(2,1)S(1)} collective-permute-done((bf16[2,256,256]{2,1,0:T(8,128)(2,1)S(1)}, bf16[2,256,256]{2,1,0:T(8,128)(2,1)S(1)}, u32[]{:S(2)}, u32[]{:S(2)}) %collective-permute-start.3) | collective-permute-done | bytes 262176 | tf_op jit(solution)/shard_map/ppermute | solution.py:31
  22.4 3.8 %shard_map.89 = (bf16[2,256,256]{2,1,0:T(8,128)(2,1)S(1)}, bf16[2,256,256]{2,1,0:T(8,128)(2,1)S(1)}, bf16[256,512]{1,0:T(8,128)(2,1)S(1)}, bf16[256,512]{1,0:T(8,128)(2,1)S(1)}) custom-call(bf16[272,256]{1,0:T(8,128)(2,1)S(1)} %get-tuple-element.25.refs_0_, bf16[272,256]{1,0:T(8,128)(2,1)S(1)} %collective-permute-done.refs_1_, ...), custom_call_target="tpu_custom_call" | custom-call | flops 4000000000 | bytes 6045696 | tf_op jit(solution)/shard_map/pallas_call | solution.py:288
  26.2 1.5 %collective-permute-start.6 = (bf16[256,512]{1,0:T(8,128)(2,1)S(1)}, bf16[256,512]{1,0:T(8,128)(2,1)S(1)}, u32[]{:S(2)}, u32[]{:S(2)}) collective-permute-start(bf16[256,512]{1,0:T(8,128)(2,1)S(1)} %get-tuple-element.33), channel_id=1, source_target_pairs={{0,2},{1,3},{2,0},{3,1},{4,6},{5,7},{6,4},{7,5},{8,10},{9,11},{10,... | collective-permute-start | bytes 786440 | tf_op jit(solution)/shard_map/ppermute | solution.py:407
  27.7 1.5 %collective-permute-start.10 = (bf16[2,256,256]{2,1,0:T(8,128)(2,1)S(1)}, bf16[2,256,256]{2,1,0:T(8,128)(2,1)S(1)}, u32[]{:S(2)}, u32[]{:S(2)}) collective-permute-start(bf16[2,256,256]{2,1,0:T(8,128)(2,1)S(1)} %get-tuple-element.39), channel_id=1, source_target_pairs={{0,1},{1,0},{2,3},{3,2},{4,5},{5,4},{6,7},{7,6},{8,9},{9,8},{10,11... | collective-permute-start | bytes 786440 | tf_op jit(solution)/shard_map/ppermute | solution.py:513
  29.2 0.1 shard_map.90
  29.3 1.2 %collective-permute-start.7 = (bf16[64,512]{1,0:T(8,128)(2,1)S(1)}, bf16[64,512]{1,0:T(8,128)(2,1)S(1)}, u32[]{:S(2)}, u32[]{:S(2)}) collective-permute-start(bf16[64,512]{1,0:T(8,128)(2,1)S(1)} %get-tuple-element.35), channel_id=1, source_target_pairs={{0,1},{1,0},{2,3},{3,2},{4,5},{5,4},{6,7},{7,6},{8,9},{9,8},{10,11... | collective-permute-start | bytes 196616 | tf_op jit(solution)/shard_map/ppermute | solution.py:407
  30.6 0.9 %collective-permute-start.8 = (bf16[64,512]{1,0:T(8,128)(2,1)S(1)}, bf16[64,512]{1,0:T(8,128)(2,1)S(1)}, u32[]{:S(2)}, u32[]{:S(2)}) collective-permute-start(bf16[64,512]{1,0:T(8,128)(2,1)S(1)} %get-tuple-element.36), channel_id=1, source_target_pairs={{0,4},{1,5},{2,6},{3,7},{4,0},{5,1},{6,2},{7,3},{8,12},{9,13},{10,... | collective-permute-start | bytes 196616 | tf_op jit(solution)/shard_map/ppermute | solution.py:407
  31.4 1.4 %collective-permute-start.9 = (bf16[64,512]{1,0:T(8,128)(2,1)S(1)}, bf16[64,512]{1,0:T(8,128)(2,1)S(1)}, u32[]{:S(2)}, u32[]{:S(2)}) collective-permute-start(bf16[64,512]{1,0:T(8,128)(2,1)S(1)} %get-tuple-element.37), channel_id=1, source_target_pairs={{0,5},{1,4},{2,7},{3,6},{4,1},{5,0},{6,3},{7,2},{8,13},{9,12},{10,... | collective-permute-start | bytes 196616 | tf_op jit(solution)/shard_map/ppermute | solution.py:407
  32.9 5.2 %collective-permute-done.10.refs_3_ = bf16[2,256,256]{2,1,0:T(8,128)(2,1)S(1)} collective-permute-done((bf16[2,256,256]{2,1,0:T(8,128)(2,1)S(1)}, bf16[2,256,256]{2,1,0:T(8,128)(2,1)S(1)}, u32[]{:S(2)}, u32[]{:S(2)}) %collective-permute-start.10) | collective-permute-done | bytes 262176 | tf_op jit(solution)/shard_map/ppermute | solution.py:513
  38.1 1.1 %shard_map.91 = (f32[2,256,256]{2,1,0:T(8,128)S(1)}, f32[2,256,256]{2,1,0:T(8,128)S(1)}, bf16[2,256,256]{2,1,0:T(8,128)(2,1)S(1)}, bf16[2,256,256]{2,1,0:T(8,128)(2,1)S(1)}) custom-call(bf16[272,256]{1,0:T(8,128)(2,1)S(1)} %get-tuple-element.25.refs_0_, bf16[272,256]{1,0:T(8,128)(2,1)S(1)} %collective-permute-done.refs_1_, ...), custom_call_target="tpu_custom_call" | custom-call | bytes 2375680 | tf_op jit(solution)/shard_map/pallas_call | solution.py:288
  39.2 0.1 collective-permute-start.14
  39.2 1.0 %collective-permute-start.13 = (bf16[2,256,256]{2,1,0:T(8,128)(2,1)S(1)}, bf16[2,256,256]{2,1,0:T(8,128)(2,1)S(1)}, u32[]{:S(2)}, u32[]{:S(2)}) collective-permute-start(bf16[2,256,256]{2,1,0:T(8,128)(2,1)S(1)} %get-tuple-element.40.refs_4_), channel_id=1, source_target_pairs={{6,0},{0,2},{2,4},{4,6},{14,8},{8,10},{10,12},{12,14},{22,16},{16,... | collective-permute-start | bytes 786440 | tf_op jit(solution)/shard_map/ppermute | solution.py:31
  40.2 0.0 collective-permute-done.7.refs_1_
  40.2 0.0 collective-permute-done.8.refs_2_
  40.2 0.0 collective-permute-done.9.refs_3_
  40.3 0.2 collective-permute-start.11
  40.5 4.1 %collective-permute-done.11.refs_1_ = bf16[64,512]{1,0:T(8,128)(2,1)S(1)} collective-permute-done((bf16[64,512]{1,0:T(8,128)(2,1)S(1)}, bf16[64,512]{1,0:T(8,128)(2,1)S(1)}, u32[]{:S(2)}, u32[]{:S(2)}) %collective-permute-start.11) | collective-permute-done | bytes 65568 | tf_op jit(solution)/shard_map/ppermute | solution.py:407
  44.6 2.7 %collective-permute-start.12 = (bf16[64,512]{1,0:T(8,128)(2,1)S(1)}, bf16[64,512]{1,0:T(8,128)(2,1)S(1)}, u32[]{:S(2)}, u32[]{:S(2)}) collective-permute-start(bf16[64,512]{1,0:T(8,128)(2,1)S(1)} %shard_map.93.refs_4_.refs_0_), channel_id=1, source_target_pairs={{0,16},{1,17},{2,18},{3,19},{4,20},{5,21},{6,22},{7,23},{8,24},{9,... | collective-permute-start | bytes 196616 | tf_op jit(solution)/shard_map/ppermute | solution.py:407
  47.3 0.5 collective-permute-done.13.refs_2_
  47.8 0.1 shard_map.94
  47.9 1.5 %collective-permute-start.18 = (bf16[2,256,256]{2,1,0:T(8,128)(2,1)S(1)}, bf16[2,256,256]{2,1,0:T(8,128)(2,1)S(1)}, u32[]{:S(2)}, u32[]{:S(2)}) collective-permute-start(bf16[2,256,256]{2,1,0:T(8,128)(2,1)S(1)} %get-tuple-element.44.refs_2_), channel_id=1, source_target_pairs={{24,0},{26,2},{28,4},{30,6},{0,8},{2,10},{4,12},{6,14},{8,16},{10,... | collective-permute-start | bytes 786440 | tf_op jit(solution)/shard_map/ppermute | solution.py:31
  49.4 0.8 %collective-permute-done.12.refs_1_ = bf16[64,512]{1,0:T(8,128)(2,1)S(1)} collective-permute-done((bf16[64,512]{1,0:T(8,128)(2,1)S(1)}, bf16[64,512]{1,0:T(8,128)(2,1)S(1)}, u32[]{:S(2)}, u32[]{:S(2)}) %collective-permute-start.12) | collective-permute-done | bytes 65568 | tf_op jit(solution)/shard_map/ppermute | solution.py:407
  50.2 2.5 %collective-permute-start.17 = (bf16[64,512]{1,0:T(8,128)(2,1)S(1)}, bf16[64,512]{1,0:T(8,128)(2,1)S(1)}, u32[]{:S(2)}, u32[]{:S(2)}) collective-permute-start(bf16[64,512]{1,0:T(8,128)(2,1)S(1)} %shard_map.95.refs_4_.refs_0_), channel_id=1, source_target_pairs={{0,5},{1,4},{2,7},{3,6},{4,1},{5,0},{6,3},{7,2},{8,13},{9,12},{10,... | collective-permute-start | bytes 196616 | tf_op jit(solution)/shard_map/ppermute | solution.py:407
  52.6 0.6 collective-permute-start.16
  53.2 0.5 collective-permute-start.15
  53.7 3.2 %collective-permute-done.18.refs_3_ = bf16[2,256,256]{2,1,0:T(8,128)(2,1)S(1)} collective-permute-done((bf16[2,256,256]{2,1,0:T(8,128)(2,1)S(1)}, bf16[2,256,256]{2,1,0:T(8,128)(2,1)S(1)}, u32[]{:S(2)}, u32[]{:S(2)}) %collective-permute-start.18) | collective-permute-done | bytes 262176 | tf_op jit(solution)/shard_map/ppermute | solution.py:31
  56.9 0.1 shard_map.96.refs_4_.refs_3_
  57.1 1.6 %collective-permute-start.20 = (bf16[2,256,256]{2,1,0:T(8,128)(2,1)S(1)}, bf16[2,256,256]{2,1,0:T(8,128)(2,1)S(1)}, u32[]{:S(2)}, u32[]{:S(2)}) collective-permute-start(bf16[2,256,256]{2,1,0:T(8,128)(2,1)S(1)} %shard_map.96.refs_4_.refs_3_), channel_id=1, source_target_pairs={{0,1},{1,0},{2,3},{3,2},{4,5},{5,4},{6,7},{7,6},{8,9},{9,8},{10,11... | collective-permute-start | bytes 786440 | tf_op jit(solution)/shard_map/ppermute | solution.py:549
  58.7 0.1 shard_map.97.refs_0_
  58.7 0.1 collective-permute-start.19
  58.8 4.7 %collective-permute-done.20.refs_1_.refs_4_ = bf16[2,256,256]{2,1,0:T(8,128)(2,1)S(1)} collective-permute-done((bf16[2,256,256]{2,1,0:T(8,128)(2,1)S(1)}, bf16[2,256,256]{2,1,0:T(8,128)(2,1)S(1)}, u32[]{:S(2)}, u32[]{:S(2)}) %collective-permute-start.20) | collective-permute-done | bytes 262176 | tf_op jit(solution)/shard_map/ppermute | solution.py:549
  63.5 1.8 %shard_map.99 = (f32[2048,128]{1,0:T(8,128)}, bf16[1,2,2,256,256]{4,3,2,1,0:T(8,128)(2,1)}) custom-call(bf16[256,512]{1,0:T(8,128)(2,1)S(1)} %shard_map.97.refs_0_, bf16[256,512]{1,0:T(8,128)(2,1)S(1)} %collective-permute-done.19.refs_1_, f32[2048,128]{1,0:T(8,128)S(1)} %bitcast.16, bf16[2,256,256]{2,1,0:T(8,128)(2,1)S(1)} %shard_map.96.refs_4_.refs_3_, ...), custom_call_target="tpu_custom_call" | custom-call | flops 1048576 | bytes 3145728 | tf_op jit(solution)/shard_map/pallas_call | solution.py:319
  (19 shorter events, 0.1 us)
Async XLA Ops:
  0.6 7.6 %copy-start.2 = (bf16[1,1,2,256,256]{4,3,2,1,0:T(8,128)(2,1)S(1)}, bf16[1,1,2,256,256]{4,3,2,1,0:T(8,128)(2,1)}, u32[]{:S(2)}) copy-start(bf16[1,1,2,256,256]{4,3,2,1,0:T(8,128)(2,1)} %refs_3_.1) | copy-start | bytes 786436
  0.6 17.8 %copy-start = (f32[2,256,2,256]{3,2,1,0:T(2,128)S(1)}, f32[2,256,2,256]{3,2,1,0:T(2,128)}, u32[]{:S(2)}) copy-start(f32[2,256,2,256]{3,2,1,0:T(2,128)} %param.8) | copy-start | bytes 3145732
  1.8 16.7 %copy-start.1 = (bf16[512,512]{1,0:T(8,128)(2,1)S(1)}, bf16[512,512]{1,0:T(8,128)(2,1)}, u32[]{:S(2)}) copy-start(bf16[512,512]{1,0:T(8,128)(2,1)} %constant.10.refs_1_) | copy-start | bytes 1572868
  1.8 11.8 %collective-permute-start.4 = (bf16[2,256,256]{2,1,0:T(8,128)(2,1)S(1)}, bf16[2,256,256]{2,1,0:T(8,128)(2,1)S(1)}, u32[]{:S(2)}, u32[]{:S(2)}) collective-permute-start(bf16[2,256,256]{2,1,0:T(8,128)(2,1)S(1)} %get-tuple-element.48.refs_4_.refs_2_.refs_0_), channel_id=1, source_target_pairs={{8,0},{10,2},{12,4},{14,6},{16,8},{18,10},{20,12},{22,14},{24,16},... | collective-permute-start | bytes 786440 | tf_op jit(solution)/shard_map/ppermute | solution.py:31
  6.9 12.8 %collective-permute-start.1 = (bf16[2,2,256,256]{3,2,1,0:T(8,128)(2,1)}, bf16[2,2,256,256]{3,2,1,0:T(8,128)(2,1)S(1)}, u32[]{:S(2)}, u32[]{:S(2)}) collective-permute-start(bf16[2,2,256,256]{3,2,1,0:T(8,128)(2,1)} %bitcast.17), channel_id=1, source_target_pairs={{2,0},{4,2},{6,4},{0,6},{10,8},{12,10},{14,12},{8,14},{18,16},{20,... | collective-permute-start | bytes 1572872 | tf_op jit(solution)/shard_map/ppermute | solution.py:31
  8.2 0.7 %copy-start.3 = (s32[1,1,2,2]{3,2,1,0:T(2,128)S(1)}, s32[1,1,2,2]{3,2,1,0:T(2,128)}, u32[]{:S(2)}) copy-start(s32[1,1,2,2]{3,2,1,0:T(2,128)} %refs_0_.1) | copy-start | bytes 52
  9.5 8.6 %collective-permute-start.2 = (bf16[2,256,256]{2,1,0:T(8,128)(2,1)S(1)}, bf16[2,256,256]{2,1,0:T(8,128)(2,1)S(1)}, u32[]{:S(2)}, u32[]{:S(2)}) collective-permute-start(bf16[2,256,256]{2,1,0:T(8,128)(2,1)S(1)} %get-tuple-element.27.refs_2_.refs_1_), channel_id=1, source_target_pairs={{8,0},{10,2},{12,4},{14,6},{16,8},{18,10},{20,12},{22,14},{24,16},... | collective-permute-start | bytes 786440 | tf_op jit(solution)/shard_map/ppermute | solution.py:31
  13.6 6.1 %collective-permute-start.5 = (bf16[2,256,256]{2,1,0:T(8,128)(2,1)S(1)}, bf16[2,256,256]{2,1,0:T(8,128)(2,1)S(1)}, u32[]{:S(2)}, u32[]{:S(2)}) collective-permute-start(bf16[2,256,256]{2,1,0:T(8,128)(2,1)S(1)} %collective-permute-done.4.refs_4_), channel_id=1, source_target_pairs={{2,0},{4,2},{6,4},{0,6},{10,8},{12,10},{14,12},{8,14},{18,16},{20,... | collective-permute-start | bytes 786440 | tf_op jit(solution)/shard_map/ppermute | solution.py:31
  13.6 6.1 %collective-permute-start = (bf16[272,256]{1,0:T(8,128)(2,1)S(1)}, bf16[272,256]{1,0:T(8,128)(2,1)S(1)}, u32[]{:S(2)}, u32[]{:S(2)}) collective-permute-start(bf16[272,256]{1,0:T(8,128)(2,1)S(1)} %get-tuple-element.26), channel_id=1, source_target_pairs={{0,1},{1,0},{2,3},{3,2},{4,5},{5,4},{6,7},{7,6},{8,9},{9,8},{10,11... | collective-permute-start | bytes 417800 | tf_op jit(solution)/shard_map/ppermute | solution.py:471
  18.1 4.2 %collective-permute-start.3 = (bf16[2,256,256]{2,1,0:T(8,128)(2,1)S(1)}, bf16[2,256,256]{2,1,0:T(8,128)(2,1)S(1)}, u32[]{:S(2)}, u32[]{:S(2)}) collective-permute-start(bf16[2,256,256]{2,1,0:T(8,128)(2,1)S(1)} %collective-permute-done.2.refs_4_), channel_id=1, source_target_pairs={{2,0},{4,2},{6,4},{0,6},{10,8},{12,10},{14,12},{8,14},{18,16},{20,... | collective-permute-start | bytes 786440 | tf_op jit(solution)/shard_map/ppermute | solution.py:31
  19.7 2.6 %copy-start.4 = (bf16[512,512]{1,0:T(8,128)(2,1)S(1)}, bf16[512,512]{1,0:T(8,128)(2,1)}, u32[]{:S(2)}) copy-start(bf16[512,512]{1,0:T(8,128)(2,1)} %constant.11.refs_10_) | copy-start | bytes 1572868
  26.2 3.0 %collective-permute-start.6 = (bf16[256,512]{1,0:T(8,128)(2,1)S(1)}, bf16[256,512]{1,0:T(8,128)(2,1)S(1)}, u32[]{:S(2)}, u32[]{:S(2)}) collective-permute-start(bf16[256,512]{1,0:T(8,128)(2,1)S(1)} %get-tuple-element.33), channel_id=1, source_target_pairs={{0,2},{1,3},{2,0},{3,1},{4,6},{5,7},{6,4},{7,5},{8,10},{9,11},{10,... | collective-permute-start | bytes 786440 | tf_op jit(solution)/shard_map/ppermute | solution.py:407
  27.7 10.4 %collective-permute-start.10 = (bf16[2,256,256]{2,1,0:T(8,128)(2,1)S(1)}, bf16[2,256,256]{2,1,0:T(8,128)(2,1)S(1)}, u32[]{:S(2)}, u32[]{:S(2)}) collective-permute-start(bf16[2,256,256]{2,1,0:T(8,128)(2,1)S(1)} %get-tuple-element.39), channel_id=1, source_target_pairs={{0,1},{1,0},{2,3},{3,2},{4,5},{5,4},{6,7},{7,6},{8,9},{9,8},{10,11... | collective-permute-start | bytes 786440 | tf_op jit(solution)/shard_map/ppermute | solution.py:513
  29.3 10.9 %collective-permute-start.7 = (bf16[64,512]{1,0:T(8,128)(2,1)S(1)}, bf16[64,512]{1,0:T(8,128)(2,1)S(1)}, u32[]{:S(2)}, u32[]{:S(2)}) collective-permute-start(bf16[64,512]{1,0:T(8,128)(2,1)S(1)} %get-tuple-element.35), channel_id=1, source_target_pairs={{0,1},{1,0},{2,3},{3,2},{4,5},{5,4},{6,7},{7,6},{8,9},{9,8},{10,11... | collective-permute-start | bytes 196616 | tf_op jit(solution)/shard_map/ppermute | solution.py:407
  30.6 9.6 %collective-permute-start.8 = (bf16[64,512]{1,0:T(8,128)(2,1)S(1)}, bf16[64,512]{1,0:T(8,128)(2,1)S(1)}, u32[]{:S(2)}, u32[]{:S(2)}) collective-permute-start(bf16[64,512]{1,0:T(8,128)(2,1)S(1)} %get-tuple-element.36), channel_id=1, source_target_pairs={{0,4},{1,5},{2,6},{3,7},{4,0},{5,1},{6,2},{7,3},{8,12},{9,13},{10,... | collective-permute-start | bytes 196616 | tf_op jit(solution)/shard_map/ppermute | solution.py:407
  31.4 8.8 %collective-permute-start.9 = (bf16[64,512]{1,0:T(8,128)(2,1)S(1)}, bf16[64,512]{1,0:T(8,128)(2,1)S(1)}, u32[]{:S(2)}, u32[]{:S(2)}) collective-permute-start(bf16[64,512]{1,0:T(8,128)(2,1)S(1)} %get-tuple-element.37), channel_id=1, source_target_pairs={{0,5},{1,4},{2,7},{3,6},{4,1},{5,0},{6,3},{7,2},{8,13},{9,12},{10,... | collective-permute-start | bytes 196616 | tf_op jit(solution)/shard_map/ppermute | solution.py:407
  39.2 8.1 %collective-permute-start.14 = (bf16[2,256,256]{2,1,0:T(8,128)(2,1)S(1)}, bf16[2,256,256]{2,1,0:T(8,128)(2,1)S(1)}, u32[]{:S(2)}, u32[]{:S(2)}) collective-permute-start(bf16[2,256,256]{2,1,0:T(8,128)(2,1)S(1)} %get-tuple-element.43), channel_id=1, source_target_pairs={{6,0},{0,2},{2,4},{4,6},{14,8},{8,10},{10,12},{12,14},{22,16},{16,... | collective-permute-start | bytes 786440 | tf_op jit(solution)/shard_map/ppermute | solution.py:31
  39.2 8.6 %collective-permute-start.13 = (bf16[2,256,256]{2,1,0:T(8,128)(2,1)S(1)}, bf16[2,256,256]{2,1,0:T(8,128)(2,1)S(1)}, u32[]{:S(2)}, u32[]{:S(2)}) collective-permute-start(bf16[2,256,256]{2,1,0:T(8,128)(2,1)S(1)} %get-tuple-element.40.refs_4_), channel_id=1, source_target_pairs={{6,0},{0,2},{2,4},{4,6},{14,8},{8,10},{10,12},{12,14},{22,16},{16,... | collective-permute-start | bytes 786440 | tf_op jit(solution)/shard_map/ppermute | solution.py:31
  40.3 4.3 %collective-permute-start.11 = (bf16[64,512]{1,0:T(8,128)(2,1)S(1)}, bf16[64,512]{1,0:T(8,128)(2,1)S(1)}, u32[]{:S(2)}, u32[]{:S(2)}) collective-permute-start(bf16[64,512]{1,0:T(8,128)(2,1)S(1)} %shard_map.92.refs_0_), channel_id=1, source_target_pairs={{0,8},{1,9},{2,10},{3,11},{4,12},{5,13},{6,14},{7,15},{8,0},{9,1},... | collective-permute-start | bytes 196616 | tf_op jit(solution)/shard_map/ppermute | solution.py:407
  44.6 5.5 %collective-permute-start.12 = (bf16[64,512]{1,0:T(8,128)(2,1)S(1)}, bf16[64,512]{1,0:T(8,128)(2,1)S(1)}, u32[]{:S(2)}, u32[]{:S(2)}) collective-permute-start(bf16[64,512]{1,0:T(8,128)(2,1)S(1)} %shard_map.93.refs_4_.refs_0_), channel_id=1, source_target_pairs={{0,16},{1,17},{2,18},{3,19},{4,20},{5,21},{6,22},{7,23},{8,24},{9,... | collective-permute-start | bytes 196616 | tf_op jit(solution)/shard_map/ppermute | solution.py:407
  47.9 9.0 %collective-permute-start.18 = (bf16[2,256,256]{2,1,0:T(8,128)(2,1)S(1)}, bf16[2,256,256]{2,1,0:T(8,128)(2,1)S(1)}, u32[]{:S(2)}, u32[]{:S(2)}) collective-permute-start(bf16[2,256,256]{2,1,0:T(8,128)(2,1)S(1)} %get-tuple-element.44.refs_2_), channel_id=1, source_target_pairs={{24,0},{26,2},{28,4},{30,6},{0,8},{2,10},{4,12},{6,14},{8,16},{10,... | collective-permute-start | bytes 786440 | tf_op jit(solution)/shard_map/ppermute | solution.py:31
  50.2 8.5 %collective-permute-start.17 = (bf16[64,512]{1,0:T(8,128)(2,1)S(1)}, bf16[64,512]{1,0:T(8,128)(2,1)S(1)}, u32[]{:S(2)}, u32[]{:S(2)}) collective-permute-start(bf16[64,512]{1,0:T(8,128)(2,1)S(1)} %shard_map.95.refs_4_.refs_0_), channel_id=1, source_target_pairs={{0,5},{1,4},{2,7},{3,6},{4,1},{5,0},{6,3},{7,2},{8,13},{9,12},{10,... | collective-permute-start | bytes 196616 | tf_op jit(solution)/shard_map/ppermute | solution.py:407
  52.6 6.0 %collective-permute-start.16 = (bf16[64,512]{1,0:T(8,128)(2,1)S(1)}, bf16[64,512]{1,0:T(8,128)(2,1)S(1)}, u32[]{:S(2)}, u32[]{:S(2)}) collective-permute-start(bf16[64,512]{1,0:T(8,128)(2,1)S(1)} %shard_map.95.refs_4_.refs_0_), channel_id=1, source_target_pairs={{0,4},{1,5},{2,6},{3,7},{4,0},{5,1},{6,2},{7,3},{8,12},{9,13},{10,... | collective-permute-start | bytes 196616 | tf_op jit(solution)/shard_map/ppermute | solution.py:407
  53.2 5.5 %collective-permute-start.15 = (bf16[64,512]{1,0:T(8,128)(2,1)S(1)}, bf16[64,512]{1,0:T(8,128)(2,1)S(1)}, u32[]{:S(2)}, u32[]{:S(2)}) collective-permute-start(bf16[64,512]{1,0:T(8,128)(2,1)S(1)} %shard_map.95.refs_4_.refs_0_), channel_id=1, source_target_pairs={{0,1},{1,0},{2,3},{3,2},{4,5},{5,4},{6,7},{7,6},{8,9},{9,8},{10,11... | collective-permute-start | bytes 196616 | tf_op jit(solution)/shard_map/ppermute | solution.py:407
  57.1 6.4 %collective-permute-start.20 = (bf16[2,256,256]{2,1,0:T(8,128)(2,1)S(1)}, bf16[2,256,256]{2,1,0:T(8,128)(2,1)S(1)}, u32[]{:S(2)}, u32[]{:S(2)}) collective-permute-start(bf16[2,256,256]{2,1,0:T(8,128)(2,1)S(1)} %shard_map.96.refs_4_.refs_3_), channel_id=1, source_target_pairs={{0,1},{1,0},{2,3},{3,2},{4,5},{5,4},{6,7},{7,6},{8,9},{9,8},{10,11... | collective-permute-start | bytes 786440 | tf_op jit(solution)/shard_map/ppermute | solution.py:549
  58.7 4.8 %collective-permute-start.19 = (bf16[256,512]{1,0:T(8,128)(2,1)S(1)}, bf16[256,512]{1,0:T(8,128)(2,1)S(1)}, u32[]{:S(2)}, u32[]{:S(2)}) collective-permute-start(bf16[256,512]{1,0:T(8,128)(2,1)S(1)} %shard_map.97.refs_0_), channel_id=1, source_target_pairs={{0,2},{1,3},{2,0},{3,1},{4,6},{5,7},{6,4},{7,5},{8,10},{9,11},{10,... | collective-permute-start | bytes 786440 | tf_op jit(solution)/shard_map/ppermute | solution.py:407

commit v14 on v13

--- a/solution.py
+++ b/solution.py
@@ -15,7 +15,7 @@
 object_rate = 0.05
 probe_rate = 0.15
 
-LATE = [work * 1_000_000_000 for work in (0, 8, 0, 0, 8, 0, 8, 4)]
+LATE = [work * 1_000_000_000 for work in (5, 0, 0, 5, 8, 0, 8, 4)]
 
 f32 = jnp.float32
 bf16 = jnp.bfloat16
@@ -234,15 +234,18 @@
         diag_ref[part] = wide[n:, n:].astype(bf16)
 
 
-def beside_kernel(home_ref, below_ref, right_ref, diag_ref, home_out, down_ref):
-    home_out[...] = home_ref[...] + right_ref[...].astype(f32)
+def down_kernel(below_ref, diag_ref, down_ref):
     down_ref[...] = (below_ref[...] + diag_ref[...].astype(f32)).astype(bf16)
 
 
-def slice_kernel(layer, own0_ref, own1_ref, home_ref, above_ref, out_ref):
-    grad = home_ref[...] + above_ref[...].astype(f32)
+def slice_kernel(layer, own0_ref, own1_ref, home_ref, left_ref, above_ref, out_ref):
+    grad = home_ref[...] + left_ref[...].astype(f32) + above_ref[...].astype(f32)
     own = jnp.where(layer() == 0, own0_ref[...].astype(f32), own1_ref[...].astype(f32))
     out_ref[...] = (own - object_rate * grad).astype(bf16)
+
+
+def pass_kernel(block_ref, out_ref):
+    out_ref[...] = block_ref[...]
 
 
 def token_kernel(token_ref):
@@ -515,24 +518,30 @@
     scattered = []
     while len(groups) > 1 and keep.shape[0] >> len(groups[0]) >= 16:
         group, groups = groups[0], groups[1:]
-        keep, *gives = run(folded(group, keep, arrived))
-        arrived = [swap_with(x, group, at) for at, x in enumerate(gives, 1)]
+        for bit in reversed(group):
+            if exchanged and scattered == [] and bit == group[0]:
+                home, below, to_right, to_diag = laid_out(kept, got, [keep], LATE[0])
+                diag_in = from_behind(to_diag, 0, 1)
+                keep, give = run(folded([bit], keep, arrived), after=[to_right])
+            else:
+                keep, give = run(folded([bit], keep, arrived))
+            arrived = [swap_with(give, [bit], 1)]
         scattered.append(group)
     first, second, *others = [[bit] for group in groups for bit in group]
-    if exchanged:
-        home, below, to_right, to_diag = laid_out(kept, got, [keep], LATE[0])
-        from_left = [from_behind(x, 0, 1) for x in (to_right, to_diag)]
-    (total,) = run(added(keep, arrived), after=[to_right] if exchanged else [], flops=LATE[1])
+    (total,) = run(added(keep, arrived), flops=LATE[1])
     (total,) = run(added(total, swapped(total, first)), flops=LATE[2])
     arrived = swapped(total, second)
     if exchanged:
-        home, down = run(
-            job(beside_kernel, [real, tile], [home, below, *from_left]),
-            after=[total],
-            flops=LATE[3],
+        (down,) = run(
+            job(down_kernel, [tile], [below, diag_in]), after=[total], flops=LATE[3]
         )
         above = from_behind(down, 1, 0)
-    (total,) = run(added(total, arrived), after=[down] if exchanged else [], flops=LATE[4])
+        (total,), (to_right,) = run(
+            added(total, arrived), job(pass_kernel, [tile], [to_right]), after=[down], flops=LATE[4]
+        )
+        left_in = from_behind(to_right, 0, 1)
+    else:
+        (total,) = run(added(total, arrived))
     for group in others:
         (total,) = run(added(total, swapped(total, group)))
     arrived = swapped(total, scattered[-1])
@@ -541,7 +550,7 @@
             job(
                 lambda *refs: slice_kernel(this_layer, *refs),
                 [tile],
-                [own[0], own1, home, above],
+                [own[0], own1, home, left_in, above],
             ),
             after=[total],
             flops=LATE[5],
@@ -571,9 +580,9 @@
         slices = []
         for patch_grad, old in ((kept, own[0]), (given, own1)):
             home, below, to_right, to_diag = laid_out(patch_grad, jnp.zeros_like(kept), [], 0)
-            from_left = [from_behind(x, 0, 1) for x in (to_right, to_diag)]
-            home, down = run(job(beside_kernel, [real, tile], [home, below, *from_left]))
-            grad = lax.psum(home + from_behind(down, 1, 0).astype(f32), "pos")
+            (down,) = run(job(down_kernel, [tile], [below, from_behind(to_diag, 0, 1)]))
+            above = from_behind(down, 1, 0).astype(f32)
+            grad = lax.psum(home + from_behind(to_right, 0, 1).astype(f32) + above, "pos")
             slices.append((old.astype(f32) - object_rate * grad).astype(bf16))
         new_object = jnp.stack(slices)[None]
     new_probe = new_probe.reshape(2, pixels, lane_tiles, modes, 128).transpose(0, 1, 3, 2, 4)

time: 65.5 us -> 69 us (1.053)
  waiting for transfers between devices: 27.1 us -> 31.2 us
    ppermute x10 -> x9, waiting for transfers between devices: 4.87 us -> 8.05 us  [swap_with(): lax.ppermute(x, ('tile', 'pos'), [(i, i ^ mask) for i in range(devices)])]
    ppermute x1, waiting for transfers between devices: 4.7 us -> 6.08 us  [shards(): other_slice = lax.ppermute(this_slice, 'pos', swap)]
    ppermute x8, waiting for transfers between devices: 11.1 us -> 10.3 us  [from_behind(): return lax.ppermute(block, 'tile', [(source(i), i) for i in range(tiles)])]
    ppermute x10 -> x9, starting transfers between devices: 11.6 us -> 10.7 us  [swap_with(): lax.ppermute(x, ('tile', 'pos'), [(i, i ^ mask) for i in range(devices)])]
    pallas_call x13 -> x14, Pallas kernels: 7.83 us -> 7.76 us  [run(): pl.pallas_call(body, out_shape=sum(outs, []), in_specs=sum(specs, []) + [...]
  transfers between devices with their start and end apart: 21 -> 20, of which waited for: 10 -> 10; matrix products, arithmetic and copies ran while one was open for 0% -> 0% of each run, Pallas kernels for 6% -> 6%
where the time goes in v14:
time: 69 us; the launch traced here: 68.8 us
  waiting for transfers between devices  31.2 us (45%)
  starting transfers between devices  24.7 us (36%)
  Pallas kernels  9.54 us (14%)
  local copies, waits for them, and re-layouts  1.86 us (3%)
  between operations  1.45 us (2%)
    ppermute x9, starting transfers between devices, swap_with(): lax.ppermute(x, ('tile', 'pos'), [(i, i ^ mask) for i in range(devices)])  10.7 us
    ppermute x8, waiting for transfers between devices, from_behind(): return lax.ppermute(block, 'tile', [(source(i), i) for i in range(tiles)])  10.3 us
    ppermute x8, starting transfers between devices, from_behind(): return lax.ppermute(block, 'tile', [(source(i), i) for i in range(tiles)])  8.79 us
    ppermute x9, waiting for transfers between devices, swap_with(): lax.ppermute(x, ('tile', 'pos'), [(i, i ^ mask) for i in range(devices)])  8.05 us
    pallas_call x14, Pallas kernels, run(): pl.pallas_call(body, out_shape=sum(outs, []), in_specs=sum(specs, []) + [...  7.76 us
    ppermute x1, waiting for transfers between devices, shards(): other_slice = lax.ppermute(this_slice, 'pos', swap)  6.08 us
    ppermute x1, waiting for transfers between devices, shards(): got = lax.ppermute(given, 'pos', swap)  5.7 us
    ppermute x1, starting transfers between devices, shards(): other_slice = lax.ppermute(this_slice, 'pos', swap)  2.17 us
  transfers between devices with their start and end apart: 20, of which 10 were waited for; matrix products, arithmetic and copies ran while one was open for 0% of the time, Pallas kernels for 6%

profile of v14, /device:TPU:0, one launch (start us, length us, event | category | flops | bytes accessed | tf_op | source)
XLA Modules:
  0.0 68.8 jit_solution(2034029423769933340)
XLA Ops:
  0.6 1.2 %slice_bitcast_fusion = (bf16[2,256,256]{2,1,0:T(8,128)(2,1)S(1)}, bf16[2,256,256]{2,1,0:T(8,128)(2,1)S(1)}) fusion(bf16[1,2,2,256,256]{4,3,2,1,0:T(8,128)(2,1)} %param.7), kind=kLoop, calls=%fused_computation | loop fusion | bytes 1048576 | tf_op jit(solution)/shard_map/squeeze | solution.py:452
  1.8 0.0 copy-start.1
  1.8 5.1 %collective-permute-start.4 = (bf16[2,256,256]{2,1,0:T(8,128)(2,1)S(1)}, bf16[2,256,256]{2,1,0:T(8,128)(2,1)S(1)}, u32[]{:S(2)}, u32[]{:S(2)}) collective-permute-start(bf16[2,256,256]{2,1,0:T(8,128)(2,1)S(1)} %get-tuple-element.48.refs_4_.refs_2_.refs_0_), channel_id=1, source_target_pairs={{8,0},{10,2},{12,4},{14,6},{16,8},{18,10},{20,12},{22,14},{24,16},... | collective-permute-start | bytes 786440 | tf_op jit(solution)/shard_map/ppermute | solution.py:31
  6.9 0.7 collective-permute-start.1
  8.2 0.0 copy-start.3
  8.3 0.7 copy-done.3
  8.9 0.6 shard_map.86
  9.5 0.5 collective-permute-start.2
  10.0 3.6 %collective-permute-done.4.refs_4_ = bf16[2,256,256]{2,1,0:T(8,128)(2,1)S(1)} collective-permute-done((bf16[2,256,256]{2,1,0:T(8,128)(2,1)S(1)}, bf16[2,256,256]{2,1,0:T(8,128)(2,1)S(1)}, u32[]{:S(2)}, u32[]{:S(2)}) %collective-permute-start.4) | collective-permute-done | bytes 262176 | tf_op jit(solution)/shard_map/ppermute | solution.py:31
  13.6 0.0 collective-permute-start.5
  13.6 1.5 %collective-permute-start = (bf16[272,256]{1,0:T(8,128)(2,1)S(1)}, bf16[272,256]{1,0:T(8,128)(2,1)S(1)}, u32[]{:S(2)}, u32[]{:S(2)}) collective-permute-start(bf16[272,256]{1,0:T(8,128)(2,1)S(1)} %get-tuple-element.26), channel_id=1, source_target_pairs={{0,1},{1,0},{2,3},{3,2},{4,5},{5,4},{6,7},{7,6},{8,9},{9,8},{10,11... | collective-permute-start | bytes 417800 | tf_op jit(solution)/shard_map/ppermute | solution.py:474
  15.2 2.9 %collective-permute-done.2.refs_4_ = bf16[2,256,256]{2,1,0:T(8,128)(2,1)S(1)} collective-permute-done((bf16[2,256,256]{2,1,0:T(8,128)(2,1)S(1)}, bf16[2,256,256]{2,1,0:T(8,128)(2,1)S(1)}, u32[]{:S(2)}, u32[]{:S(2)}) %collective-permute-start.2) | collective-permute-done | bytes 262176 | tf_op jit(solution)/shard_map/ppermute | solution.py:31
  18.1 0.3 collective-permute-start.3
  18.5 0.1 shard_map.87
  18.6 1.2 %collective-permute-done.refs_1_ = bf16[272,256]{1,0:T(8,128)(2,1)S(1)} collective-permute-done((bf16[272,256]{1,0:T(8,128)(2,1)S(1)}, bf16[272,256]{1,0:T(8,128)(2,1)S(1)}, u32[]{:S(2)}, u32[]{:S(2)}) %collective-permute-start) | collective-permute-done | bytes 139296 | tf_op jit(solution)/shard_map/ppermute | solution.py:474
  19.7 0.0 collective-permute-done.5.refs_5_
  19.7 0.0 collective-permute-done.1.refs_3_
  19.7 1.7 %shard_map.88 = (bf16[2,256,256]{2,1,0:T(8,128)(2,1)S(1)}, f32[2,256,512]{2,1,0:T(8,128)S(1)}) custom-call(bf16[272,256]{1,0:T(8,128)(2,1)S(1)} %get-tuple-element.25.refs_0_, bf16[272,256]{1,0:T(8,128)(2,1)S(1)} %collective-permute-done.refs_1_, bf16[2,256,256]{2,1,0:T(8,128)(2,1)S(1)} %get-tuple-element.48.refs_4_.refs_2_.refs_0_, ...), custom_call_target="tpu_custom_call" | custom-call | flops 1500000000 | bytes 4472832 | tf_op jit(solution)/shard_map/pallas_call | solution.py:291
  21.5 0.9 %collective-permute-done.3.refs_5_ = bf16[2,256,256]{2,1,0:T(8,128)(2,1)S(1)} collective-permute-done((bf16[2,256,256]{2,1,0:T(8,128)(2,1)S(1)}, bf16[2,256,256]{2,1,0:T(8,128)(2,1)S(1)}, u32[]{:S(2)}, u32[]{:S(2)}) %collective-permute-start.3) | collective-permute-done | bytes 262176 | tf_op jit(solution)/shard_map/ppermute | solution.py:31
  22.4 3.8 %shard_map.89 = (bf16[2,256,256]{2,1,0:T(8,128)(2,1)S(1)}, bf16[2,256,256]{2,1,0:T(8,128)(2,1)S(1)}, bf16[256,512]{1,0:T(8,128)(2,1)S(1)}, bf16[256,512]{1,0:T(8,128)(2,1)S(1)}) custom-call(bf16[272,256]{1,0:T(8,128)(2,1)S(1)} %get-tuple-element.25.refs_0_, bf16[272,256]{1,0:T(8,128)(2,1)S(1)} %collective-permute-done.refs_1_, ...), custom_call_target="tpu_custom_call" | custom-call | flops 4000000000 | bytes 6045696 | tf_op jit(solution)/shard_map/pallas_call | solution.py:291
  26.1 1.5 %collective-permute-start.6 = (bf16[256,512]{1,0:T(8,128)(2,1)S(1)}, bf16[256,512]{1,0:T(8,128)(2,1)S(1)}, u32[]{:S(2)}, u32[]{:S(2)}) collective-permute-start(bf16[256,512]{1,0:T(8,128)(2,1)S(1)} %get-tuple-element.33), channel_id=1, source_target_pairs={{0,2},{1,3},{2,0},{3,1},{4,6},{5,7},{6,4},{7,5},{8,10},{9,11},{10,... | collective-permute-start | bytes 786440 | tf_op jit(solution)/shard_map/ppermute | solution.py:410
  27.6 1.5 %collective-permute-start.8 = (bf16[2,256,256]{2,1,0:T(8,128)(2,1)S(1)}, bf16[2,256,256]{2,1,0:T(8,128)(2,1)S(1)}, u32[]{:S(2)}, u32[]{:S(2)}) collective-permute-start(bf16[2,256,256]{2,1,0:T(8,128)(2,1)S(1)} %get-tuple-element.37), channel_id=1, source_target_pairs={{0,1},{1,0},{2,3},{3,2},{4,5},{5,4},{6,7},{7,6},{8,9},{9,8},{10,11... | collective-permute-start | bytes 786440 | tf_op jit(solution)/shard_map/ppermute | solution.py:516
  29.2 0.0 collective-permute-done.6.refs_1_
  29.2 0.1 shard_map.90
  29.3 0.9 %collective-permute-start.7 = (bf16[128,512]{1,0:T(8,128)(2,1)S(1)}, bf16[128,512]{1,0:T(8,128)(2,1)S(1)}, u32[]{:S(2)}, u32[]{:S(2)}) collective-permute-start(bf16[128,512]{1,0:T(8,128)(2,1)S(1)} %get-tuple-element.35), channel_id=1, source_target_pairs={{0,4},{1,5},{2,6},{3,7},{4,0},{5,1},{6,2},{7,3},{8,12},{9,13},{10,... | collective-permute-start | bytes 393224 | tf_op jit(solution)/shard_map/ppermute | solution.py:410
  30.2 5.7 %collective-permute-done.8.refs_3_ = bf16[2,256,256]{2,1,0:T(8,128)(2,1)S(1)} collective-permute-done((bf16[2,256,256]{2,1,0:T(8,128)(2,1)S(1)}, bf16[2,256,256]{2,1,0:T(8,128)(2,1)S(1)}, u32[]{:S(2)}, u32[]{:S(2)}) %collective-permute-start.8) | collective-permute-done | bytes 262176 | tf_op jit(solution)/shard_map/ppermute | solution.py:516
  35.9 1.1 %shard_map.91 = (f32[2,256,256]{2,1,0:T(8,128)S(1)}, f32[2,256,256]{2,1,0:T(8,128)S(1)}, bf16[2,256,256]{2,1,0:T(8,128)(2,1)S(1)}, bf16[2,256,256]{2,1,0:T(8,128)(2,1)S(1)}) custom-call(bf16[272,256]{1,0:T(8,128)(2,1)S(1)} %get-tuple-element.25.refs_0_, bf16[272,256]{1,0:T(8,128)(2,1)S(1)} %collective-permute-done.refs_1_, ...), custom_call_target="tpu_custom_call" | custom-call | flops 5000000000 | bytes 2375680 | tf_op jit(solution)/shard_map/pallas_call | solution.py:291
  37.0 0.1 collective-permute-start.12
  37.1 1.6 %collective-permute-start.9 = (bf16[64,512]{1,0:T(8,128)(2,1)S(1)}, bf16[64,512]{1,0:T(8,128)(2,1)S(1)}, u32[]{:S(2)}, u32[]{:S(2)}) collective-permute-start(bf16[64,512]{1,0:T(8,128)(2,1)S(1)} %get-tuple-element.40), channel_id=1, source_target_pairs={{0,1},{1,0},{2,3},{3,2},{4,5},{5,4},{6,7},{7,6},{8,9},{9,8},{10,11... | collective-permute-start | bytes 196616 | tf_op jit(solution)/shard_map/ppermute | solution.py:410
  38.7 3.4 %collective-permute-done.9.refs_1_ = bf16[64,512]{1,0:T(8,128)(2,1)S(1)} collective-permute-done((bf16[64,512]{1,0:T(8,128)(2,1)S(1)}, bf16[64,512]{1,0:T(8,128)(2,1)S(1)}, u32[]{:S(2)}, u32[]{:S(2)}) %collective-permute-start.9) | collective-permute-done | bytes 65568 | tf_op jit(solution)/shard_map/ppermute | solution.py:410
  42.2 0.2 collective-permute-start.10
  42.4 4.1 %collective-permute-done.10.refs_1_ = bf16[64,512]{1,0:T(8,128)(2,1)S(1)} collective-permute-done((bf16[64,512]{1,0:T(8,128)(2,1)S(1)}, bf16[64,512]{1,0:T(8,128)(2,1)S(1)}, u32[]{:S(2)}, u32[]{:S(2)}) %collective-permute-start.10) | collective-permute-done | bytes 65568 | tf_op jit(solution)/shard_map/ppermute | solution.py:410
  46.5 2.6 %collective-permute-start.11 = (bf16[64,512]{1,0:T(8,128)(2,1)S(1)}, bf16[64,512]{1,0:T(8,128)(2,1)S(1)}, u32[]{:S(2)}, u32[]{:S(2)}) collective-permute-start(bf16[64,512]{1,0:T(8,128)(2,1)S(1)} %shard_map.94.refs_2_.refs_0_), channel_id=1, source_target_pairs={{0,16},{1,17},{2,18},{3,19},{4,20},{5,21},{6,22},{7,23},{8,24},{9,... | collective-permute-start | bytes 196616 | tf_op jit(solution)/shard_map/ppermute | solution.py:410
  49.1 0.0 collective-permute-done.12.refs_1_
  49.2 2.1 %collective-permute-start.17 = (bf16[2,256,256]{2,1,0:T(8,128)(2,1)S(1)}, bf16[2,256,256]{2,1,0:T(8,128)(2,1)S(1)}, u32[]{:S(2)}, u32[]{:S(2)}) collective-permute-start(bf16[2,256,256]{2,1,0:T(8,128)(2,1)S(1)} %shard_map.95.refs_3_), channel_id=1, source_target_pairs={{24,0},{26,2},{28,4},{30,6},{0,8},{2,10},{4,12},{6,14},{8,16},{10,... | collective-permute-start | bytes 786440 | tf_op jit(solution)/shard_map/ppermute | solution.py:31
  51.3 0.5 collective-permute-done.11.refs_1_
  51.8 0.1 collective-permute-start.16
  51.8 3.2 %collective-permute-start.15 = (bf16[64,512]{1,0:T(8,128)(2,1)S(1)}, bf16[64,512]{1,0:T(8,128)(2,1)S(1)}, u32[]{:S(2)}, u32[]{:S(2)}) collective-permute-start(bf16[64,512]{1,0:T(8,128)(2,1)S(1)} %get-tuple-element.43.refs_5_.refs_0_), channel_id=1, source_target_pairs={{0,5},{1,4},{2,7},{3,6},{4,1},{5,0},{6,3},{7,2},{8,13},{9,12},{10,... | collective-permute-start | bytes 196616 | tf_op jit(solution)/shard_map/ppermute | solution.py:410
  55.0 0.0 collective-permute-start.14
  55.0 0.6 collective-permute-start.13
  55.6 2.8 %collective-permute-done.17.refs_4_ = bf16[2,256,256]{2,1,0:T(8,128)(2,1)S(1)} collective-permute-done((bf16[2,256,256]{2,1,0:T(8,128)(2,1)S(1)}, bf16[2,256,256]{2,1,0:T(8,128)(2,1)S(1)}, u32[]{:S(2)}, u32[]{:S(2)}) %collective-permute-start.17) | collective-permute-done | bytes 262176 | tf_op jit(solution)/shard_map/ppermute | solution.py:31
  58.4 0.2 shard_map.97.refs_4_.refs_3_
  58.6 2.2 %collective-permute-start.19 = (bf16[2,256,256]{2,1,0:T(8,128)(2,1)S(1)}, bf16[2,256,256]{2,1,0:T(8,128)(2,1)S(1)}, u32[]{:S(2)}, u32[]{:S(2)}) collective-permute-start(bf16[2,256,256]{2,1,0:T(8,128)(2,1)S(1)} %shard_map.97.refs_4_.refs_3_), channel_id=1, source_target_pairs={{0,1},{1,0},{2,3},{3,2},{4,5},{5,4},{6,7},{7,6},{8,9},{9,8},{10,11... | collective-permute-start | bytes 786440 | tf_op jit(solution)/shard_map/ppermute | solution.py:558
  60.8 0.1 shard_map.98.refs_0_
  60.9 0.1 collective-permute-start.18
  60.9 6.1 %collective-permute-done.19.refs_1_.refs_4_ = bf16[2,256,256]{2,1,0:T(8,128)(2,1)S(1)} collective-permute-done((bf16[2,256,256]{2,1,0:T(8,128)(2,1)S(1)}, bf16[2,256,256]{2,1,0:T(8,128)(2,1)S(1)}, u32[]{:S(2)}, u32[]{:S(2)}) %collective-permute-start.19) | collective-permute-done | bytes 262176 | tf_op jit(solution)/shard_map/ppermute | solution.py:558
  67.0 0.0 collective-permute-done.18.refs_1_
  67.0 1.8 %shard_map.100 = (f32[2048,128]{1,0:T(8,128)}, bf16[1,2,2,256,256]{4,3,2,1,0:T(8,128)(2,1)}) custom-call(bf16[256,512]{1,0:T(8,128)(2,1)S(1)} %shard_map.98.refs_0_, bf16[256,512]{1,0:T(8,128)(2,1)S(1)} %collective-permute-done.18.refs_1_, f32[2048,128]{1,0:T(8,128)S(1)} %bitcast.16, bf16[2,256,256]{2,1,0:T(8,128)(2,1)S(1)} %shard_map.97.refs_4_.refs_3_, ...), custom_call_target="tpu_custom_call" | custom-call | flops 1048576 | bytes 3145728 | tf_op jit(solution)/shard_map/pallas_call | solution.py:322
  (18 shorter events, 0.2 us)
Async XLA Ops:
  0.6 7.6 %copy-start.2 = (bf16[1,1,2,256,256]{4,3,2,1,0:T(8,128)(2,1)S(1)}, bf16[1,1,2,256,256]{4,3,2,1,0:T(8,128)(2,1)}, u32[]{:S(2)}) copy-start(bf16[1,1,2,256,256]{4,3,2,1,0:T(8,128)(2,1)} %refs_3_.1) | copy-start | bytes 786436
  0.6 17.8 %copy-start = (f32[2,256,2,256]{3,2,1,0:T(2,128)S(1)}, f32[2,256,2,256]{3,2,1,0:T(2,128)}, u32[]{:S(2)}) copy-start(f32[2,256,2,256]{3,2,1,0:T(2,128)} %param.8) | copy-start | bytes 3145732
  1.8 16.7 %copy-start.1 = (bf16[512,512]{1,0:T(8,128)(2,1)S(1)}, bf16[512,512]{1,0:T(8,128)(2,1)}, u32[]{:S(2)}) copy-start(bf16[512,512]{1,0:T(8,128)(2,1)} %constant.10.refs_1_) | copy-start | bytes 1572868
  1.8 11.8 %collective-permute-start.4 = (bf16[2,256,256]{2,1,0:T(8,128)(2,1)S(1)}, bf16[2,256,256]{2,1,0:T(8,128)(2,1)S(1)}, u32[]{:S(2)}, u32[]{:S(2)}) collective-permute-start(bf16[2,256,256]{2,1,0:T(8,128)(2,1)S(1)} %get-tuple-element.48.refs_4_.refs_2_.refs_0_), channel_id=1, source_target_pairs={{8,0},{10,2},{12,4},{14,6},{16,8},{18,10},{20,12},{22,14},{24,16},... | collective-permute-start | bytes 786440 | tf_op jit(solution)/shard_map/ppermute | solution.py:31
  6.9 12.8 %collective-permute-start.1 = (bf16[2,2,256,256]{3,2,1,0:T(8,128)(2,1)}, bf16[2,2,256,256]{3,2,1,0:T(8,128)(2,1)S(1)}, u32[]{:S(2)}, u32[]{:S(2)}) collective-permute-start(bf16[2,2,256,256]{3,2,1,0:T(8,128)(2,1)} %bitcast.17), channel_id=1, source_target_pairs={{2,0},{4,2},{6,4},{0,6},{10,8},{12,10},{14,12},{8,14},{18,16},{20,... | collective-permute-start | bytes 1572872 | tf_op jit(solution)/shard_map/ppermute | solution.py:31
  8.2 0.7 copy-start.3
  9.5 8.6 %collective-permute-start.2 = (bf16[2,256,256]{2,1,0:T(8,128)(2,1)S(1)}, bf16[2,256,256]{2,1,0:T(8,128)(2,1)S(1)}, u32[]{:S(2)}, u32[]{:S(2)}) collective-permute-start(bf16[2,256,256]{2,1,0:T(8,128)(2,1)S(1)} %get-tuple-element.27.refs_2_.refs_1_), channel_id=1, source_target_pairs={{8,0},{10,2},{12,4},{14,6},{16,8},{18,10},{20,12},{22,14},{24,16},... | collective-permute-start | bytes 786440 | tf_op jit(solution)/shard_map/ppermute | solution.py:31
  13.6 6.1 %collective-permute-start.5 = (bf16[2,256,256]{2,1,0:T(8,128)(2,1)S(1)}, bf16[2,256,256]{2,1,0:T(8,128)(2,1)S(1)}, u32[]{:S(2)}, u32[]{:S(2)}) collective-permute-start(bf16[2,256,256]{2,1,0:T(8,128)(2,1)S(1)} %collective-permute-done.4.refs_4_), channel_id=1, source_target_pairs={{2,0},{4,2},{6,4},{0,6},{10,8},{12,10},{14,12},{8,14},{18,16},{20,... | collective-permute-start | bytes 786440 | tf_op jit(solution)/shard_map/ppermute | solution.py:31
  13.6 6.1 %collective-permute-start = (bf16[272,256]{1,0:T(8,128)(2,1)S(1)}, bf16[272,256]{1,0:T(8,128)(2,1)S(1)}, u32[]{:S(2)}, u32[]{:S(2)}) collective-permute-start(bf16[272,256]{1,0:T(8,128)(2,1)S(1)} %get-tuple-element.26), channel_id=1, source_target_pairs={{0,1},{1,0},{2,3},{3,2},{4,5},{5,4},{6,7},{7,6},{8,9},{9,8},{10,11... | collective-permute-start | bytes 417800 | tf_op jit(solution)/shard_map/ppermute | solution.py:474
  18.1 4.2 %collective-permute-start.3 = (bf16[2,256,256]{2,1,0:T(8,128)(2,1)S(1)}, bf16[2,256,256]{2,1,0:T(8,128)(2,1)S(1)}, u32[]{:S(2)}, u32[]{:S(2)}) collective-permute-start(bf16[2,256,256]{2,1,0:T(8,128)(2,1)S(1)} %collective-permute-done.2.refs_4_), channel_id=1, source_target_pairs={{2,0},{4,2},{6,4},{0,6},{10,8},{12,10},{14,12},{8,14},{18,16},{20,... | collective-permute-start | bytes 786440 | tf_op jit(solution)/shard_map/ppermute | solution.py:31
  19.7 2.6 %copy-start.4 = (bf16[512,512]{1,0:T(8,128)(2,1)S(1)}, bf16[512,512]{1,0:T(8,128)(2,1)}, u32[]{:S(2)}) copy-start(bf16[512,512]{1,0:T(8,128)(2,1)} %constant.11.refs_10_) | copy-start | bytes 1572868
  26.1 3.0 %collective-permute-start.6 = (bf16[256,512]{1,0:T(8,128)(2,1)S(1)}, bf16[256,512]{1,0:T(8,128)(2,1)S(1)}, u32[]{:S(2)}, u32[]{:S(2)}) collective-permute-start(bf16[256,512]{1,0:T(8,128)(2,1)S(1)} %get-tuple-element.33), channel_id=1, source_target_pairs={{0,2},{1,3},{2,0},{3,1},{4,6},{5,7},{6,4},{7,5},{8,10},{9,11},{10,... | collective-permute-start | bytes 786440 | tf_op jit(solution)/shard_map/ppermute | solution.py:410
  27.6 8.3 %collective-permute-start.8 = (bf16[2,256,256]{2,1,0:T(8,128)(2,1)S(1)}, bf16[2,256,256]{2,1,0:T(8,128)(2,1)S(1)}, u32[]{:S(2)}, u32[]{:S(2)}) collective-permute-start(bf16[2,256,256]{2,1,0:T(8,128)(2,1)S(1)} %get-tuple-element.37), channel_id=1, source_target_pairs={{0,1},{1,0},{2,3},{3,2},{4,5},{5,4},{6,7},{7,6},{8,9},{9,8},{10,11... | collective-permute-start | bytes 786440 | tf_op jit(solution)/shard_map/ppermute | solution.py:516
  29.3 7.8 %collective-permute-start.7 = (bf16[128,512]{1,0:T(8,128)(2,1)S(1)}, bf16[128,512]{1,0:T(8,128)(2,1)S(1)}, u32[]{:S(2)}, u32[]{:S(2)}) collective-permute-start(bf16[128,512]{1,0:T(8,128)(2,1)S(1)} %get-tuple-element.35), channel_id=1, source_target_pairs={{0,4},{1,5},{2,6},{3,7},{4,0},{5,1},{6,2},{7,3},{8,12},{9,13},{10,... | collective-permute-start | bytes 393224 | tf_op jit(solution)/shard_map/ppermute | solution.py:410
  37.0 12.1 %collective-permute-start.12 = (bf16[2,256,256]{2,1,0:T(8,128)(2,1)S(1)}, bf16[2,256,256]{2,1,0:T(8,128)(2,1)S(1)}, u32[]{:S(2)}, u32[]{:S(2)}) collective-permute-start(bf16[2,256,256]{2,1,0:T(8,128)(2,1)S(1)} %get-tuple-element.42), channel_id=1, source_target_pairs={{6,0},{0,2},{2,4},{4,6},{14,8},{8,10},{10,12},{12,14},{22,16},{16,... | collective-permute-start | bytes 786440 | tf_op jit(solution)/shard_map/ppermute | solution.py:31
  37.1 5.0 %collective-permute-start.9 = (bf16[64,512]{1,0:T(8,128)(2,1)S(1)}, bf16[64,512]{1,0:T(8,128)(2,1)S(1)}, u32[]{:S(2)}, u32[]{:S(2)}) collective-permute-start(bf16[64,512]{1,0:T(8,128)(2,1)S(1)} %get-tuple-element.40), channel_id=1, source_target_pairs={{0,1},{1,0},{2,3},{3,2},{4,5},{5,4},{6,7},{7,6},{8,9},{9,8},{10,11... | collective-permute-start | bytes 196616 | tf_op jit(solution)/shard_map/ppermute | solution.py:410
  42.2 4.3 %collective-permute-start.10 = (bf16[64,512]{1,0:T(8,128)(2,1)S(1)}, bf16[64,512]{1,0:T(8,128)(2,1)S(1)}, u32[]{:S(2)}, u32[]{:S(2)}) collective-permute-start(bf16[64,512]{1,0:T(8,128)(2,1)S(1)} %shard_map.93.refs_0_), channel_id=1, source_target_pairs={{0,8},{1,9},{2,10},{3,11},{4,12},{5,13},{6,14},{7,15},{8,0},{9,1},... | collective-permute-start | bytes 196616 | tf_op jit(solution)/shard_map/ppermute | solution.py:410
  46.5 5.2 %collective-permute-start.11 = (bf16[64,512]{1,0:T(8,128)(2,1)S(1)}, bf16[64,512]{1,0:T(8,128)(2,1)S(1)}, u32[]{:S(2)}, u32[]{:S(2)}) collective-permute-start(bf16[64,512]{1,0:T(8,128)(2,1)S(1)} %shard_map.94.refs_2_.refs_0_), channel_id=1, source_target_pairs={{0,16},{1,17},{2,18},{3,19},{4,20},{5,21},{6,22},{7,23},{8,24},{9,... | collective-permute-start | bytes 196616 | tf_op jit(solution)/shard_map/ppermute | solution.py:410
  49.2 9.3 %collective-permute-start.17 = (bf16[2,256,256]{2,1,0:T(8,128)(2,1)S(1)}, bf16[2,256,256]{2,1,0:T(8,128)(2,1)S(1)}, u32[]{:S(2)}, u32[]{:S(2)}) collective-permute-start(bf16[2,256,256]{2,1,0:T(8,128)(2,1)S(1)} %shard_map.95.refs_3_), channel_id=1, source_target_pairs={{24,0},{26,2},{28,4},{30,6},{0,8},{2,10},{4,12},{6,14},{8,16},{10,... | collective-permute-start | bytes 786440 | tf_op jit(solution)/shard_map/ppermute | solution.py:31
  51.8 6.7 %collective-permute-start.16 = (bf16[2,256,256]{2,1,0:T(8,128)(2,1)S(1)}, bf16[2,256,256]{2,1,0:T(8,128)(2,1)S(1)}, u32[]{:S(2)}, u32[]{:S(2)}) collective-permute-start(bf16[2,256,256]{2,1,0:T(8,128)(2,1)S(1)} %get-tuple-element.45), channel_id=1, source_target_pairs={{6,0},{0,2},{2,4},{4,6},{14,8},{8,10},{10,12},{12,14},{22,16},{16,... | collective-permute-start | bytes 786440 | tf_op jit(solution)/shard_map/ppermute | solution.py:31
  51.8 8.9 %collective-permute-start.15 = (bf16[64,512]{1,0:T(8,128)(2,1)S(1)}, bf16[64,512]{1,0:T(8,128)(2,1)S(1)}, u32[]{:S(2)}, u32[]{:S(2)}) collective-permute-start(bf16[64,512]{1,0:T(8,128)(2,1)S(1)} %get-tuple-element.43.refs_5_.refs_0_), channel_id=1, source_target_pairs={{0,5},{1,4},{2,7},{3,6},{4,1},{5,0},{6,3},{7,2},{8,13},{9,12},{10,... | collective-permute-start | bytes 196616 | tf_op jit(solution)/shard_map/ppermute | solution.py:410
  55.0 5.8 %collective-permute-start.14 = (bf16[64,512]{1,0:T(8,128)(2,1)S(1)}, bf16[64,512]{1,0:T(8,128)(2,1)S(1)}, u32[]{:S(2)}, u32[]{:S(2)}) collective-permute-start(bf16[64,512]{1,0:T(8,128)(2,1)S(1)} %get-tuple-element.43.refs_5_.refs_0_), channel_id=1, source_target_pairs={{0,4},{1,5},{2,6},{3,7},{4,0},{5,1},{6,2},{7,3},{8,12},{9,13},{10,... | collective-permute-start | bytes 196616 | tf_op jit(solution)/shard_map/ppermute | solution.py:410
  55.0 5.8 %collective-permute-start.13 = (bf16[64,512]{1,0:T(8,128)(2,1)S(1)}, bf16[64,512]{1,0:T(8,128)(2,1)S(1)}, u32[]{:S(2)}, u32[]{:S(2)}) collective-permute-start(bf16[64,512]{1,0:T(8,128)(2,1)S(1)} %get-tuple-element.43.refs_5_.refs_0_), channel_id=1, source_target_pairs={{0,1},{1,0},{2,3},{3,2},{4,5},{5,4},{6,7},{7,6},{8,9},{9,8},{10,11... | collective-permute-start | bytes 196616 | tf_op jit(solution)/shard_map/ppermute | solution.py:410
  58.6 8.4 %collective-permute-start.19 = (bf16[2,256,256]{2,1,0:T(8,128)(2,1)S(1)}, bf16[2,256,256]{2,1,0:T(8,128)(2,1)S(1)}, u32[]{:S(2)}, u32[]{:S(2)}) collective-permute-start(bf16[2,256,256]{2,1,0:T(8,128)(2,1)S(1)} %shard_map.97.refs_4_.refs_3_), channel_id=1, source_target_pairs={{0,1},{1,0},{2,3},{3,2},{4,5},{5,4},{6,7},{7,6},{8,9},{9,8},{10,11... | collective-permute-start | bytes 786440 | tf_op jit(solution)/shard_map/ppermute | solution.py:558
  60.9 6.2 %collective-permute-start.18 = (bf16[256,512]{1,0:T(8,128)(2,1)S(1)}, bf16[256,512]{1,0:T(8,128)(2,1)S(1)}, u32[]{:S(2)}, u32[]{:S(2)}) collective-permute-start(bf16[256,512]{1,0:T(8,128)(2,1)S(1)} %shard_map.98.refs_0_), channel_id=1, source_target_pairs={{0,2},{1,3},{2,0},{3,1},{4,6},{5,7},{6,4},{7,5},{8,10},{9,11},{10,... | collective-permute-start | bytes 786440 | tf_op jit(solution)/shard_map/ppermute | solution.py:410

commit v15 on v14

--- a/solution.py
+++ b/solution.py
@@ -15,7 +15,7 @@
 object_rate = 0.05
 probe_rate = 0.15
 
-LATE = [work * 1_000_000_000 for work in (5, 0, 0, 5, 8, 0, 8, 4)]
+LATE = [work * 1_000_000_000 for work in (5, 0, 0, 5, 0, 0, 8, 4)]
 
 f32 = jnp.float32
 bf16 = jnp.bfloat16
@@ -238,7 +238,7 @@
     down_ref[...] = (below_ref[...] + diag_ref[...].astype(f32)).astype(bf16)
 
 
-def slice_kernel(layer, own0_ref, own1_ref, home_ref, left_ref, above_ref, out_ref):
+def slice_kernel(layer, own0_ref, own1_ref, home_ref, above_ref, left_ref, out_ref):
     grad = home_ref[...] + left_ref[...].astype(f32) + above_ref[...].astype(f32)
     own = jnp.where(layer() == 0, own0_ref[...].astype(f32), own1_ref[...].astype(f32))
     out_ref[...] = (own - object_rate * grad).astype(bf16)
@@ -529,19 +529,18 @@
         scattered.append(group)
     first, second, *others = [[bit] for group in groups for bit in group]
     (total,) = run(added(keep, arrived), flops=LATE[1])
-    (total,) = run(added(total, swapped(total, first)), flops=LATE[2])
-    arrived = swapped(total, second)
+    arrived = swapped(total, first)
     if exchanged:
-        (down,) = run(
-            job(down_kernel, [tile], [below, diag_in]), after=[total], flops=LATE[3]
+        (down,), (to_right,) = run(
+            job(down_kernel, [tile], [below, diag_in]),
+            job(pass_kernel, [tile], [to_right]),
+            after=[total],
+            flops=LATE[2],
         )
         above = from_behind(down, 1, 0)
-        (total,), (to_right,) = run(
-            added(total, arrived), job(pass_kernel, [tile], [to_right]), after=[down], flops=LATE[4]
-        )
         left_in = from_behind(to_right, 0, 1)
-    else:
-        (total,) = run(added(total, arrived))
+    (total,) = run(added(total, arrived), after=[down] if exchanged else [], flops=LATE[3])
+    (total,) = run(added(total, swapped(total, second)), flops=LATE[4])
     for group in others:
         (total,) = run(added(total, swapped(total, group)))
     arrived = swapped(total, scattered[-1])
@@ -550,7 +549,7 @@
             job(
                 lambda *refs: slice_kernel(this_layer, *refs),
                 [tile],
-                [own[0], own1, home, left_in, above],
+                [own[0], own1, home, above, left_in],
             ),
             after=[total],
             flops=LATE[5],

time: 69 us -> 71.7 us (1.039)
  waiting for transfers between devices: 31.2 us -> 35.4 us
  starting transfers between devices: 24.7 us -> 23.3 us
    ppermute x9, waiting for transfers between devices: 8.05 us -> 16.4 us  [swap_with(): lax.ppermute(x, ('tile', 'pos'), [(i, i ^ mask) for i in range(devices)])]
    ppermute x8, waiting for transfers between devices: 10.3 us -> 7.89 us  [from_behind(): return lax.ppermute(block, 'tile', [(source(i), i) for i in range(tiles)])]
    ppermute x1, waiting for transfers between devices: 6.08 us -> 4.31 us  [shards(): other_slice = lax.ppermute(this_slice, 'pos', swap)]
  transfers between devices with their start and end apart: 20 -> 20, of which waited for: 10 -> 13; matrix products, arithmetic and copies ran while one was open for 0% -> 0% of each run, Pallas kernels for 6% -> 6%
where the time goes in v15:
time: 71.7 us; the launch traced here: 71.6 us
  waiting for transfers between devices  35.4 us (49%)
  starting transfers between devices  23.3 us (32%)
  Pallas kernels  9.53 us (13%)
  local copies, waits for them, and re-layouts  1.86 us (3%)
  between operations  1.44 us (2%)
    ppermute x9, waiting for transfers between devices, swap_with(): lax.ppermute(x, ('tile', 'pos'), [(i, i ^ mask) for i in range(devices)])  16.4 us
    ppermute x9, starting transfers between devices, swap_with(): lax.ppermute(x, ('tile', 'pos'), [(i, i ^ mask) for i in range(devices)])  10.5 us
    ppermute x8, starting transfers between devices, from_behind(): return lax.ppermute(block, 'tile', [(source(i), i) for i in range(tiles)])  8.19 us
    ppermute x8, waiting for transfers between devices, from_behind(): return lax.ppermute(block, 'tile', [(source(i), i) for i in range(tiles)])  7.89 us
    pallas_call x14, Pallas kernels, run(): pl.pallas_call(body, out_shape=sum(outs, []), in_specs=sum(specs, []) + [...  7.75 us
    ppermute x1, waiting for transfers between devices, shards(): got = lax.ppermute(given, 'pos', swap)  5.7 us
    ppermute x1, waiting for transfers between devices, shards(): other_slice = lax.ppermute(this_slice, 'pos', swap)  4.31 us
    pallas_call x1, Pallas kernels, finished(): pl.pallas_call(body, out_shape=[shape_of(f32, *probe.shape), like], in_sp...  1.78 us
  transfers between devices with their start and end apart: 20, of which 13 were waited for; matrix products, arithmetic and copies ran while one was open for 0% of the time, Pallas kernels for 6%

profile of v15, /device:TPU:0, one launch (start us, length us, event | category | flops | bytes accessed | tf_op | source)
XLA Modules:
  0.0 71.6 jit_solution(7883943187281295234)
XLA Ops:
  0.6 1.2 %slice_bitcast_fusion = (bf16[2,256,256]{2,1,0:T(8,128)(2,1)S(1)}, bf16[2,256,256]{2,1,0:T(8,128)(2,1)S(1)}) fusion(bf16[1,2,2,256,256]{4,3,2,1,0:T(8,128)(2,1)} %param.7), kind=kLoop, calls=%fused_computation | loop fusion | bytes 1048576 | tf_op jit(solution)/shard_map/squeeze | solution.py:452
  1.8 0.0 copy-start.1
  1.8 5.1 %collective-permute-start.4 = (bf16[2,256,256]{2,1,0:T(8,128)(2,1)S(1)}, bf16[2,256,256]{2,1,0:T(8,128)(2,1)S(1)}, u32[]{:S(2)}, u32[]{:S(2)}) collective-permute-start(bf16[2,256,256]{2,1,0:T(8,128)(2,1)S(1)} %get-tuple-element.48.refs_4_.refs_2_.refs_0_), channel_id=1, source_target_pairs={{8,0},{10,2},{12,4},{14,6},{16,8},{18,10},{20,12},{22,14},{24,16},... | collective-permute-start | bytes 786440 | tf_op jit(solution)/shard_map/ppermute | solution.py:31
  6.9 0.7 collective-permute-start.1
  8.2 0.0 copy-start.3
  8.3 0.7 copy-done.3
  8.9 0.6 shard_map.86
  9.5 0.5 collective-permute-start.2
  10.0 3.6 %collective-permute-done.4.refs_4_ = bf16[2,256,256]{2,1,0:T(8,128)(2,1)S(1)} collective-permute-done((bf16[2,256,256]{2,1,0:T(8,128)(2,1)S(1)}, bf16[2,256,256]{2,1,0:T(8,128)(2,1)S(1)}, u32[]{:S(2)}, u32[]{:S(2)}) %collective-permute-start.4) | collective-permute-done | bytes 262176 | tf_op jit(solution)/shard_map/ppermute | solution.py:31
  13.6 0.0 collective-permute-start.5
  13.6 1.5 %collective-permute-start = (bf16[272,256]{1,0:T(8,128)(2,1)S(1)}, bf16[272,256]{1,0:T(8,128)(2,1)S(1)}, u32[]{:S(2)}, u32[]{:S(2)}) collective-permute-start(bf16[272,256]{1,0:T(8,128)(2,1)S(1)} %get-tuple-element.26), channel_id=1, source_target_pairs={{0,1},{1,0},{2,3},{3,2},{4,5},{5,4},{6,7},{7,6},{8,9},{9,8},{10,11... | collective-permute-start | bytes 417800 | tf_op jit(solution)/shard_map/ppermute | solution.py:474
  15.2 2.9 %collective-permute-done.2.refs_4_ = bf16[2,256,256]{2,1,0:T(8,128)(2,1)S(1)} collective-permute-done((bf16[2,256,256]{2,1,0:T(8,128)(2,1)S(1)}, bf16[2,256,256]{2,1,0:T(8,128)(2,1)S(1)}, u32[]{:S(2)}, u32[]{:S(2)}) %collective-permute-start.2) | collective-permute-done | bytes 262176 | tf_op jit(solution)/shard_map/ppermute | solution.py:31
  18.1 0.3 collective-permute-start.3
  18.5 0.1 shard_map.87
  18.6 1.2 %collective-permute-done.refs_1_ = bf16[272,256]{1,0:T(8,128)(2,1)S(1)} collective-permute-done((bf16[272,256]{1,0:T(8,128)(2,1)S(1)}, bf16[272,256]{1,0:T(8,128)(2,1)S(1)}, u32[]{:S(2)}, u32[]{:S(2)}) %collective-permute-start) | collective-permute-done | bytes 139296 | tf_op jit(solution)/shard_map/ppermute | solution.py:474
  19.7 0.0 collective-permute-done.5.refs_5_
  19.7 1.7 %shard_map.88 = (bf16[2,256,256]{2,1,0:T(8,128)(2,1)S(1)}, f32[2,256,512]{2,1,0:T(8,128)S(1)}) custom-call(bf16[272,256]{1,0:T(8,128)(2,1)S(1)} %get-tuple-element.25.refs_0_, bf16[272,256]{1,0:T(8,128)(2,1)S(1)} %collective-permute-done.refs_1_, bf16[2,256,256]{2,1,0:T(8,128)(2,1)S(1)} %get-tuple-element.48.refs_4_.refs_2_.refs_0_, ...), custom_call_target="tpu_custom_call" | custom-call | flops 1500000000 | bytes 4472832 | tf_op jit(solution)/shard_map/pallas_call | solution.py:291
  21.5 0.9 %collective-permute-done.3.refs_5_ = bf16[2,256,256]{2,1,0:T(8,128)(2,1)S(1)} collective-permute-done((bf16[2,256,256]{2,1,0:T(8,128)(2,1)S(1)}, bf16[2,256,256]{2,1,0:T(8,128)(2,1)S(1)}, u32[]{:S(2)}, u32[]{:S(2)}) %collective-permute-start.3) | collective-permute-done | bytes 262176 | tf_op jit(solution)/shard_map/ppermute | solution.py:31
  22.4 3.8 %shard_map.89 = (bf16[2,256,256]{2,1,0:T(8,128)(2,1)S(1)}, bf16[2,256,256]{2,1,0:T(8,128)(2,1)S(1)}, bf16[256,512]{1,0:T(8,128)(2,1)S(1)}, bf16[256,512]{1,0:T(8,128)(2,1)S(1)}) custom-call(bf16[272,256]{1,0:T(8,128)(2,1)S(1)} %get-tuple-element.25.refs_0_, bf16[272,256]{1,0:T(8,128)(2,1)S(1)} %collective-permute-done.refs_1_, ...), custom_call_target="tpu_custom_call" | custom-call | flops 4000000000 | bytes 6045696 | tf_op jit(solution)/shard_map/pallas_call | solution.py:291
  26.1 1.5 %collective-permute-start.6 = (bf16[256,512]{1,0:T(8,128)(2,1)S(1)}, bf16[256,512]{1,0:T(8,128)(2,1)S(1)}, u32[]{:S(2)}, u32[]{:S(2)}) collective-permute-start(bf16[256,512]{1,0:T(8,128)(2,1)S(1)} %get-tuple-element.33), channel_id=1, source_target_pairs={{0,2},{1,3},{2,0},{3,1},{4,6},{5,7},{6,4},{7,5},{8,10},{9,11},{10,... | collective-permute-start | bytes 786440 | tf_op jit(solution)/shard_map/ppermute | solution.py:410
  27.6 1.5 %collective-permute-start.8 = (bf16[2,256,256]{2,1,0:T(8,128)(2,1)S(1)}, bf16[2,256,256]{2,1,0:T(8,128)(2,1)S(1)}, u32[]{:S(2)}, u32[]{:S(2)}) collective-permute-start(bf16[2,256,256]{2,1,0:T(8,128)(2,1)S(1)} %get-tuple-element.37), channel_id=1, source_target_pairs={{0,1},{1,0},{2,3},{3,2},{4,5},{5,4},{6,7},{7,6},{8,9},{9,8},{10,11... | collective-permute-start | bytes 786440 | tf_op jit(solution)/shard_map/ppermute | solution.py:516
  29.2 0.1 shard_map.90
  29.3 0.9 %collective-permute-start.7 = (bf16[128,512]{1,0:T(8,128)(2,1)S(1)}, bf16[128,512]{1,0:T(8,128)(2,1)S(1)}, u32[]{:S(2)}, u32[]{:S(2)}) collective-permute-start(bf16[128,512]{1,0:T(8,128)(2,1)S(1)} %get-tuple-element.35), channel_id=1, source_target_pairs={{0,4},{1,5},{2,6},{3,7},{4,0},{5,1},{6,2},{7,3},{8,12},{9,13},{10,... | collective-permute-start | bytes 393224 | tf_op jit(solution)/shard_map/ppermute | solution.py:410
  30.2 5.7 %collective-permute-done.8.refs_3_ = bf16[2,256,256]{2,1,0:T(8,128)(2,1)S(1)} collective-permute-done((bf16[2,256,256]{2,1,0:T(8,128)(2,1)S(1)}, bf16[2,256,256]{2,1,0:T(8,128)(2,1)S(1)}, u32[]{:S(2)}, u32[]{:S(2)}) %collective-permute-start.8) | collective-permute-done | bytes 262176 | tf_op jit(solution)/shard_map/ppermute | solution.py:516
  35.9 1.1 %shard_map.91 = (f32[2,256,256]{2,1,0:T(8,128)S(1)}, f32[2,256,256]{2,1,0:T(8,128)S(1)}, bf16[2,256,256]{2,1,0:T(8,128)(2,1)S(1)}, bf16[2,256,256]{2,1,0:T(8,128)(2,1)S(1)}) custom-call(bf16[272,256]{1,0:T(8,128)(2,1)S(1)} %get-tuple-element.25.refs_0_, bf16[272,256]{1,0:T(8,128)(2,1)S(1)} %collective-permute-done.refs_1_, ...), custom_call_target="tpu_custom_call" | custom-call | flops 5000000000 | bytes 2375680 | tf_op jit(solution)/shard_map/pallas_call | solution.py:291
  37.0 0.1 collective-permute-start.11
  37.1 1.6 %collective-permute-start.9 = (bf16[64,512]{1,0:T(8,128)(2,1)S(1)}, bf16[64,512]{1,0:T(8,128)(2,1)S(1)}, u32[]{:S(2)}, u32[]{:S(2)}) collective-permute-start(bf16[64,512]{1,0:T(8,128)(2,1)S(1)} %get-tuple-element.40), channel_id=1, source_target_pairs={{0,1},{1,0},{2,3},{3,2},{4,5},{5,4},{6,7},{7,6},{8,9},{9,8},{10,11... | collective-permute-start | bytes 196616 | tf_op jit(solution)/shard_map/ppermute | solution.py:410
  38.7 3.4 %collective-permute-done.9.refs_1_ = bf16[64,512]{1,0:T(8,128)(2,1)S(1)} collective-permute-done((bf16[64,512]{1,0:T(8,128)(2,1)S(1)}, bf16[64,512]{1,0:T(8,128)(2,1)S(1)}, u32[]{:S(2)}, u32[]{:S(2)}) %collective-permute-start.9) | collective-permute-done | bytes 65568 | tf_op jit(solution)/shard_map/ppermute | solution.py:410
  42.2 0.2 collective-permute-start.10
  42.4 0.4 collective-permute-done.11.refs_1_
  42.8 0.1 shard_map.94
  42.9 0.1 collective-permute-start.17
  43.0 1.5 %collective-permute-start.16 = (bf16[2,256,256]{2,1,0:T(8,128)(2,1)S(1)}, bf16[2,256,256]{2,1,0:T(8,128)(2,1)S(1)}, u32[]{:S(2)}, u32[]{:S(2)}) collective-permute-start(bf16[2,256,256]{2,1,0:T(8,128)(2,1)S(1)} %get-tuple-element.43.refs_2_), channel_id=1, source_target_pairs={{24,0},{26,2},{28,4},{30,6},{0,8},{2,10},{4,12},{6,14},{8,16},{10,... | collective-permute-start | bytes 786440 | tf_op jit(solution)/shard_map/ppermute | solution.py:31
  44.4 2.1 %collective-permute-done.10.refs_1_ = bf16[64,512]{1,0:T(8,128)(2,1)S(1)} collective-permute-done((bf16[64,512]{1,0:T(8,128)(2,1)S(1)}, bf16[64,512]{1,0:T(8,128)(2,1)S(1)}, u32[]{:S(2)}, u32[]{:S(2)}) %collective-permute-start.10) | collective-permute-done | bytes 65568 | tf_op jit(solution)/shard_map/ppermute | solution.py:410
  46.5 2.6 %collective-permute-start.12 = (bf16[64,512]{1,0:T(8,128)(2,1)S(1)}, bf16[64,512]{1,0:T(8,128)(2,1)S(1)}, u32[]{:S(2)}, u32[]{:S(2)}) collective-permute-start(bf16[64,512]{1,0:T(8,128)(2,1)S(1)} %shard_map.95.refs_0_), channel_id=1, source_target_pairs={{0,16},{1,17},{2,18},{3,19},{4,20},{5,21},{6,22},{7,23},{8,24},{9,... | collective-permute-start | bytes 196616 | tf_op jit(solution)/shard_map/ppermute | solution.py:410
  49.1 8.1 %collective-permute-done.12.refs_1_ = bf16[64,512]{1,0:T(8,128)(2,1)S(1)} collective-permute-done((bf16[64,512]{1,0:T(8,128)(2,1)S(1)}, bf16[64,512]{1,0:T(8,128)(2,1)S(1)}, u32[]{:S(2)}, u32[]{:S(2)}) %collective-permute-start.12) | collective-permute-done | bytes 65568 | tf_op jit(solution)/shard_map/ppermute | solution.py:410
  57.2 1.7 %collective-permute-start.15 = (bf16[64,512]{1,0:T(8,128)(2,1)S(1)}, bf16[64,512]{1,0:T(8,128)(2,1)S(1)}, u32[]{:S(2)}, u32[]{:S(2)}) collective-permute-start(bf16[64,512]{1,0:T(8,128)(2,1)S(1)} %shard_map.96.refs_5_.refs_0_), channel_id=1, source_target_pairs={{0,5},{1,4},{2,7},{3,6},{4,1},{5,0},{6,3},{7,2},{8,13},{9,12},{10,... | collective-permute-start | bytes 196616 | tf_op jit(solution)/shard_map/ppermute | solution.py:410
  59.0 1.3 %collective-permute-start.14 = (bf16[64,512]{1,0:T(8,128)(2,1)S(1)}, bf16[64,512]{1,0:T(8,128)(2,1)S(1)}, u32[]{:S(2)}, u32[]{:S(2)}) collective-permute-start(bf16[64,512]{1,0:T(8,128)(2,1)S(1)} %shard_map.96.refs_5_.refs_0_), channel_id=1, source_target_pairs={{0,4},{1,5},{2,6},{3,7},{4,0},{5,1},{6,2},{7,3},{8,12},{9,13},{10,... | collective-permute-start | bytes 196616 | tf_op jit(solution)/shard_map/ppermute | solution.py:410
  60.3 0.5 collective-permute-start.13
  60.8 0.2 shard_map.97.refs_4_.refs_3_
  61.0 1.6 %collective-permute-start.19 = (bf16[2,256,256]{2,1,0:T(8,128)(2,1)S(1)}, bf16[2,256,256]{2,1,0:T(8,128)(2,1)S(1)}, u32[]{:S(2)}, u32[]{:S(2)}) collective-permute-start(bf16[2,256,256]{2,1,0:T(8,128)(2,1)S(1)} %shard_map.97.refs_4_.refs_3_), channel_id=1, source_target_pairs={{0,1},{1,0},{2,3},{3,2},{4,5},{5,4},{6,7},{7,6},{8,9},{9,8},{10,11... | collective-permute-start | bytes 786440 | tf_op jit(solution)/shard_map/ppermute | solution.py:557
  62.6 0.5 collective-permute-done.15.refs_3_
  63.0 0.7 collective-permute-done.14.refs_2_
  63.7 1.6 %collective-permute-done.13.refs_1_ = bf16[64,512]{1,0:T(8,128)(2,1)S(1)} collective-permute-done((bf16[64,512]{1,0:T(8,128)(2,1)S(1)}, bf16[64,512]{1,0:T(8,128)(2,1)S(1)}, u32[]{:S(2)}, u32[]{:S(2)}) %collective-permute-start.13) | collective-permute-done | bytes 65568 | tf_op jit(solution)/shard_map/ppermute | solution.py:410
  65.3 0.1 shard_map.98.refs_0_
  65.4 0.1 collective-permute-start.18
  65.5 4.3 %collective-permute-done.19.refs_1_.refs_4_ = bf16[2,256,256]{2,1,0:T(8,128)(2,1)S(1)} collective-permute-done((bf16[2,256,256]{2,1,0:T(8,128)(2,1)S(1)}, bf16[2,256,256]{2,1,0:T(8,128)(2,1)S(1)}, u32[]{:S(2)}, u32[]{:S(2)}) %collective-permute-start.19) | collective-permute-done | bytes 262176 | tf_op jit(solution)/shard_map/ppermute | solution.py:557
  69.8 1.8 %shard_map.100 = (f32[2048,128]{1,0:T(8,128)}, bf16[1,2,2,256,256]{4,3,2,1,0:T(8,128)(2,1)}) custom-call(bf16[256,512]{1,0:T(8,128)(2,1)S(1)} %shard_map.98.refs_0_, bf16[256,512]{1,0:T(8,128)(2,1)S(1)} %collective-permute-done.18.refs_1_, f32[2048,128]{1,0:T(8,128)S(1)} %bitcast.16, bf16[2,256,256]{2,1,0:T(8,128)(2,1)S(1)} %shard_map.97.refs_4_.refs_3_, ...), custom_call_target="tpu_custom_call" | custom-call | flops 1048576 | bytes 3145728 | tf_op jit(solution)/shard_map/pallas_call | solution.py:322
  (18 shorter events, 0.1 us)
Async XLA Ops:
  0.6 7.6 %copy-start.2 = (bf16[1,1,2,256,256]{4,3,2,1,0:T(8,128)(2,1)S(1)}, bf16[1,1,2,256,256]{4,3,2,1,0:T(8,128)(2,1)}, u32[]{:S(2)}) copy-start(bf16[1,1,2,256,256]{4,3,2,1,0:T(8,128)(2,1)} %refs_3_.1) | copy-start | bytes 786436
  0.6 17.8 %copy-start = (f32[2,256,2,256]{3,2,1,0:T(2,128)S(1)}, f32[2,256,2,256]{3,2,1,0:T(2,128)}, u32[]{:S(2)}) copy-start(f32[2,256,2,256]{3,2,1,0:T(2,128)} %param.8) | copy-start | bytes 3145732
  1.8 16.7 %copy-start.1 = (bf16[512,512]{1,0:T(8,128)(2,1)S(1)}, bf16[512,512]{1,0:T(8,128)(2,1)}, u32[]{:S(2)}) copy-start(bf16[512,512]{1,0:T(8,128)(2,1)} %constant.10.refs_1_) | copy-start | bytes 1572868
  1.8 11.8 %collective-permute-start.4 = (bf16[2,256,256]{2,1,0:T(8,128)(2,1)S(1)}, bf16[2,256,256]{2,1,0:T(8,128)(2,1)S(1)}, u32[]{:S(2)}, u32[]{:S(2)}) collective-permute-start(bf16[2,256,256]{2,1,0:T(8,128)(2,1)S(1)} %get-tuple-element.48.refs_4_.refs_2_.refs_0_), channel_id=1, source_target_pairs={{8,0},{10,2},{12,4},{14,6},{16,8},{18,10},{20,12},{22,14},{24,16},... | collective-permute-start | bytes 786440 | tf_op jit(solution)/shard_map/ppermute | solution.py:31
  6.9 12.8 %collective-permute-start.1 = (bf16[2,2,256,256]{3,2,1,0:T(8,128)(2,1)}, bf16[2,2,256,256]{3,2,1,0:T(8,128)(2,1)S(1)}, u32[]{:S(2)}, u32[]{:S(2)}) collective-permute-start(bf16[2,2,256,256]{3,2,1,0:T(8,128)(2,1)} %bitcast.17), channel_id=1, source_target_pairs={{2,0},{4,2},{6,4},{0,6},{10,8},{12,10},{14,12},{8,14},{18,16},{20,... | collective-permute-start | bytes 1572872 | tf_op jit(solution)/shard_map/ppermute | solution.py:31
  8.2 0.7 copy-start.3
  9.5 8.6 %collective-permute-start.2 = (bf16[2,256,256]{2,1,0:T(8,128)(2,1)S(1)}, bf16[2,256,256]{2,1,0:T(8,128)(2,1)S(1)}, u32[]{:S(2)}, u32[]{:S(2)}) collective-permute-start(bf16[2,256,256]{2,1,0:T(8,128)(2,1)S(1)} %get-tuple-element.27.refs_2_.refs_1_), channel_id=1, source_target_pairs={{8,0},{10,2},{12,4},{14,6},{16,8},{18,10},{20,12},{22,14},{24,16},... | collective-permute-start | bytes 786440 | tf_op jit(solution)/shard_map/ppermute | solution.py:31
  13.6 6.1 %collective-permute-start.5 = (bf16[2,256,256]{2,1,0:T(8,128)(2,1)S(1)}, bf16[2,256,256]{2,1,0:T(8,128)(2,1)S(1)}, u32[]{:S(2)}, u32[]{:S(2)}) collective-permute-start(bf16[2,256,256]{2,1,0:T(8,128)(2,1)S(1)} %collective-permute-done.4.refs_4_), channel_id=1, source_target_pairs={{2,0},{4,2},{6,4},{0,6},{10,8},{12,10},{14,12},{8,14},{18,16},{20,... | collective-permute-start | bytes 786440 | tf_op jit(solution)/shard_map/ppermute | solution.py:31
  13.6 6.1 %collective-permute-start = (bf16[272,256]{1,0:T(8,128)(2,1)S(1)}, bf16[272,256]{1,0:T(8,128)(2,1)S(1)}, u32[]{:S(2)}, u32[]{:S(2)}) collective-permute-start(bf16[272,256]{1,0:T(8,128)(2,1)S(1)} %get-tuple-element.26), channel_id=1, source_target_pairs={{0,1},{1,0},{2,3},{3,2},{4,5},{5,4},{6,7},{7,6},{8,9},{9,8},{10,11... | collective-permute-start | bytes 417800 | tf_op jit(solution)/shard_map/ppermute | solution.py:474
  18.1 4.2 %collective-permute-start.3 = (bf16[2,256,256]{2,1,0:T(8,128)(2,1)S(1)}, bf16[2,256,256]{2,1,0:T(8,128)(2,1)S(1)}, u32[]{:S(2)}, u32[]{:S(2)}) collective-permute-start(bf16[2,256,256]{2,1,0:T(8,128)(2,1)S(1)} %collective-permute-done.2.refs_4_), channel_id=1, source_target_pairs={{2,0},{4,2},{6,4},{0,6},{10,8},{12,10},{14,12},{8,14},{18,16},{20,... | collective-permute-start | bytes 786440 | tf_op jit(solution)/shard_map/ppermute | solution.py:31
  19.7 2.6 %copy-start.4 = (bf16[512,512]{1,0:T(8,128)(2,1)S(1)}, bf16[512,512]{1,0:T(8,128)(2,1)}, u32[]{:S(2)}) copy-start(bf16[512,512]{1,0:T(8,128)(2,1)} %constant.11.refs_10_) | copy-start | bytes 1572868
  26.1 3.0 %collective-permute-start.6 = (bf16[256,512]{1,0:T(8,128)(2,1)S(1)}, bf16[256,512]{1,0:T(8,128)(2,1)S(1)}, u32[]{:S(2)}, u32[]{:S(2)}) collective-permute-start(bf16[256,512]{1,0:T(8,128)(2,1)S(1)} %get-tuple-element.33), channel_id=1, source_target_pairs={{0,2},{1,3},{2,0},{3,1},{4,6},{5,7},{6,4},{7,5},{8,10},{9,11},{10,... | collective-permute-start | bytes 786440 | tf_op jit(solution)/shard_map/ppermute | solution.py:410
  27.6 8.3 %collective-permute-start.8 = (bf16[2,256,256]{2,1,0:T(8,128)(2,1)S(1)}, bf16[2,256,256]{2,1,0:T(8,128)(2,1)S(1)}, u32[]{:S(2)}, u32[]{:S(2)}) collective-permute-start(bf16[2,256,256]{2,1,0:T(8,128)(2,1)S(1)} %get-tuple-element.37), channel_id=1, source_target_pairs={{0,1},{1,0},{2,3},{3,2},{4,5},{5,4},{6,7},{7,6},{8,9},{9,8},{10,11... | collective-permute-start | bytes 786440 | tf_op jit(solution)/shard_map/ppermute | solution.py:516
  29.3 7.8 %collective-permute-start.7 = (bf16[128,512]{1,0:T(8,128)(2,1)S(1)}, bf16[128,512]{1,0:T(8,128)(2,1)S(1)}, u32[]{:S(2)}, u32[]{:S(2)}) collective-permute-start(bf16[128,512]{1,0:T(8,128)(2,1)S(1)} %get-tuple-element.35), channel_id=1, source_target_pairs={{0,4},{1,5},{2,6},{3,7},{4,0},{5,1},{6,2},{7,3},{8,12},{9,13},{10,... | collective-permute-start | bytes 393224 | tf_op jit(solution)/shard_map/ppermute | solution.py:410
  37.0 5.8 %collective-permute-start.11 = (bf16[2,256,256]{2,1,0:T(8,128)(2,1)S(1)}, bf16[2,256,256]{2,1,0:T(8,128)(2,1)S(1)}, u32[]{:S(2)}, u32[]{:S(2)}) collective-permute-start(bf16[2,256,256]{2,1,0:T(8,128)(2,1)S(1)} %get-tuple-element.42), channel_id=1, source_target_pairs={{6,0},{0,2},{2,4},{4,6},{14,8},{8,10},{10,12},{12,14},{22,16},{16,... | collective-permute-start | bytes 786440 | tf_op jit(solution)/shard_map/ppermute | solution.py:31
  37.1 5.0 %collective-permute-start.9 = (bf16[64,512]{1,0:T(8,128)(2,1)S(1)}, bf16[64,512]{1,0:T(8,128)(2,1)S(1)}, u32[]{:S(2)}, u32[]{:S(2)}) collective-permute-start(bf16[64,512]{1,0:T(8,128)(2,1)S(1)} %get-tuple-element.40), channel_id=1, source_target_pairs={{0,1},{1,0},{2,3},{3,2},{4,5},{5,4},{6,7},{7,6},{8,9},{9,8},{10,11... | collective-permute-start | bytes 196616 | tf_op jit(solution)/shard_map/ppermute | solution.py:410
  42.2 4.3 %collective-permute-start.10 = (bf16[64,512]{1,0:T(8,128)(2,1)S(1)}, bf16[64,512]{1,0:T(8,128)(2,1)S(1)}, u32[]{:S(2)}, u32[]{:S(2)}) collective-permute-start(bf16[64,512]{1,0:T(8,128)(2,1)S(1)} %shard_map.93.refs_3_.refs_0_), channel_id=1, source_target_pairs={{0,8},{1,9},{2,10},{3,11},{4,12},{5,13},{6,14},{7,15},{8,0},{9,1},... | collective-permute-start | bytes 196616 | tf_op jit(solution)/shard_map/ppermute | solution.py:410
  42.9 17.9 %collective-permute-start.17 = (bf16[2,256,256]{2,1,0:T(8,128)(2,1)S(1)}, bf16[2,256,256]{2,1,0:T(8,128)(2,1)S(1)}, u32[]{:S(2)}, u32[]{:S(2)}) collective-permute-start(bf16[2,256,256]{2,1,0:T(8,128)(2,1)S(1)} %get-tuple-element.45), channel_id=1, source_target_pairs={{6,0},{0,2},{2,4},{4,6},{14,8},{8,10},{10,12},{12,14},{22,16},{16,... | collective-permute-start | bytes 786440 | tf_op jit(solution)/shard_map/ppermute | solution.py:31
  43.0 17.8 %collective-permute-start.16 = (bf16[2,256,256]{2,1,0:T(8,128)(2,1)S(1)}, bf16[2,256,256]{2,1,0:T(8,128)(2,1)S(1)}, u32[]{:S(2)}, u32[]{:S(2)}) collective-permute-start(bf16[2,256,256]{2,1,0:T(8,128)(2,1)S(1)} %get-tuple-element.43.refs_2_), channel_id=1, source_target_pairs={{24,0},{26,2},{28,4},{30,6},{0,8},{2,10},{4,12},{6,14},{8,16},{10,... | collective-permute-start | bytes 786440 | tf_op jit(solution)/shard_map/ppermute | solution.py:31
  46.5 10.7 %collective-permute-start.12 = (bf16[64,512]{1,0:T(8,128)(2,1)S(1)}, bf16[64,512]{1,0:T(8,128)(2,1)S(1)}, u32[]{:S(2)}, u32[]{:S(2)}) collective-permute-start(bf16[64,512]{1,0:T(8,128)(2,1)S(1)} %shard_map.95.refs_0_), channel_id=1, source_target_pairs={{0,16},{1,17},{2,18},{3,19},{4,20},{5,21},{6,22},{7,23},{8,24},{9,... | collective-permute-start | bytes 196616 | tf_op jit(solution)/shard_map/ppermute | solution.py:410
  57.2 5.8 %collective-permute-start.15 = (bf16[64,512]{1,0:T(8,128)(2,1)S(1)}, bf16[64,512]{1,0:T(8,128)(2,1)S(1)}, u32[]{:S(2)}, u32[]{:S(2)}) collective-permute-start(bf16[64,512]{1,0:T(8,128)(2,1)S(1)} %shard_map.96.refs_5_.refs_0_), channel_id=1, source_target_pairs={{0,5},{1,4},{2,7},{3,6},{4,1},{5,0},{6,3},{7,2},{8,13},{9,12},{10,... | collective-permute-start | bytes 196616 | tf_op jit(solution)/shard_map/ppermute | solution.py:410
  59.0 4.7 %collective-permute-start.14 = (bf16[64,512]{1,0:T(8,128)(2,1)S(1)}, bf16[64,512]{1,0:T(8,128)(2,1)S(1)}, u32[]{:S(2)}, u32[]{:S(2)}) collective-permute-start(bf16[64,512]{1,0:T(8,128)(2,1)S(1)} %shard_map.96.refs_5_.refs_0_), channel_id=1, source_target_pairs={{0,4},{1,5},{2,6},{3,7},{4,0},{5,1},{6,2},{7,3},{8,12},{9,13},{10,... | collective-permute-start | bytes 196616 | tf_op jit(solution)/shard_map/ppermute | solution.py:410
  60.3 5.0 %collective-permute-start.13 = (bf16[64,512]{1,0:T(8,128)(2,1)S(1)}, bf16[64,512]{1,0:T(8,128)(2,1)S(1)}, u32[]{:S(2)}, u32[]{:S(2)}) collective-permute-start(bf16[64,512]{1,0:T(8,128)(2,1)S(1)} %shard_map.96.refs_5_.refs_0_), channel_id=1, source_target_pairs={{0,1},{1,0},{2,3},{3,2},{4,5},{5,4},{6,7},{7,6},{8,9},{9,8},{10,11... | collective-permute-start | bytes 196616 | tf_op jit(solution)/shard_map/ppermute | solution.py:410
  61.0 8.8 %collective-permute-start.19 = (bf16[2,256,256]{2,1,0:T(8,128)(2,1)S(1)}, bf16[2,256,256]{2,1,0:T(8,128)(2,1)S(1)}, u32[]{:S(2)}, u32[]{:S(2)}) collective-permute-start(bf16[2,256,256]{2,1,0:T(8,128)(2,1)S(1)} %shard_map.97.refs_4_.refs_3_), channel_id=1, source_target_pairs={{0,1},{1,0},{2,3},{3,2},{4,5},{5,4},{6,7},{7,6},{8,9},{9,8},{10,11... | collective-permute-start | bytes 786440 | tf_op jit(solution)/shard_map/ppermute | solution.py:557
  65.4 4.4 %collective-permute-start.18 = (bf16[256,512]{1,0:T(8,128)(2,1)S(1)}, bf16[256,512]{1,0:T(8,128)(2,1)S(1)}, u32[]{:S(2)}, u32[]{:S(2)}) collective-permute-start(bf16[256,512]{1,0:T(8,128)(2,1)S(1)} %shard_map.98.refs_0_), channel_id=1, source_target_pairs={{0,2},{1,3},{2,0},{3,1},{4,6},{5,7},{6,4},{7,5},{8,10},{9,11},{10,... | collective-permute-start | bytes 786440 | tf_op jit(solution)/shard_map/ppermute | solution.py:410

commit v16 on v15

--- a/solution.py
+++ b/solution.py
@@ -15,7 +15,7 @@
 object_rate = 0.05
 probe_rate = 0.15
 
-LATE = [work * 1_000_000_000 for work in (5, 0, 0, 5, 0, 0, 8, 4)]
+LATE = [work * 1_000_000_000 for work in (0, 8, 0, 0, 8, 0, 8, 4)]
 
 f32 = jnp.float32
 bf16 = jnp.bfloat16
@@ -76,18 +76,6 @@
     j_out = lax.broadcasted_iota(jnp.int32, (2 * n, n), 1)
     rows = i_in == i_out + jnp.concatenate([row, row], axis=1)
     cols = j_in == j_out + col
-    return rows.astype(f32).astype(bf16), cols.astype(f32).astype(bf16)
-
-
-def shift_out(spot):
-    row, col = spot
-    n = row.shape[1]
-    i_out = lax.broadcasted_iota(jnp.int32, (n, 2 * n), 0)
-    i_in = lax.broadcasted_iota(jnp.int32, (n, 2 * n), 1)
-    j_in = lax.broadcasted_iota(jnp.int32, (2 * n, n), 0)
-    j_out = lax.broadcasted_iota(jnp.int32, (2 * n, n), 1)
-    rows = j_in == j_out + row
-    cols = i_in == i_out + jnp.concatenate([col, col], axis=1)
     return rows.astype(f32).astype(bf16), cols.astype(f32).astype(bf16)
 
 
@@ -216,36 +204,59 @@
     given_ref[...] = grad_ref[1 - layer]
 
 
-def spread_kernel(
-    mine_ref, sent_ref, kept_ref, got_ref, home_ref, below_ref, right_ref, diag_ref
-):
+def laid_rows(mine_ref, sent_ref, kept_ref, got_ref, part, below):
     n = mine_ref.shape[1]
     first, second, _ = spots(mine_ref, sent_ref)
-    rows1, cols1 = shift_out(first)
-    rows2, cols2 = shift_out(second)
-    cols = jnp.concatenate([cols1, cols2], axis=0)
+    from_row = n if below else 0
+    i_out = lax.broadcasted_iota(jnp.int32, (n, n), 0) + from_row
+    i_in = lax.broadcasted_iota(jnp.int32, (n, n), 1)
+    tall = []
+    for (row, _), ref in ((first, kept_ref), (second, got_ref)):
+        rows = (i_out == i_in + row).astype(f32).astype(bf16)
+        tall.append(dot(rows, ref[part]).astype(bf16))
+    return jnp.concatenate(tall, axis=1)
+
+
+def laid_cols(mine_ref, sent_ref, beyond):
+    n = mine_ref.shape[1]
+    first, second, _ = spots(mine_ref, sent_ref)
+    from_col = n if beyond else 0
+    i_in = lax.broadcasted_iota(jnp.int32, (n, n), 0)
+    i_out = lax.broadcasted_iota(jnp.int32, (n, n), 1) + from_col
+    cols = [(i_out == i_in + col).astype(f32).astype(bf16) for _, col in (first, second)]
+    return jnp.concatenate(cols, axis=0)
+
+
+def diag_kernel(mine_ref, sent_ref, kept_ref, got_ref, diag_ref):
+    cols = laid_cols(mine_ref, sent_ref, True)
     for part in range(2):
-        tall1 = dot(rows1, kept_ref[part]).astype(bf16)
-        tall2 = dot(rows2, got_ref[part]).astype(bf16)
-        wide = dot(jnp.concatenate([tall1, tall2], axis=1), cols)
-        home_ref[part] = wide[:n, :n]
-        right_ref[part] = wide[:n, n:].astype(bf16)
-        below_ref[part] = wide[n:, :n]
-        diag_ref[part] = wide[n:, n:].astype(bf16)
+        tall = laid_rows(mine_ref, sent_ref, kept_ref, got_ref, part, True)
+        diag_ref[part] = dot(tall, cols).astype(bf16)
+
+
+def spread_kernel(mine_ref, sent_ref, kept_ref, got_ref, home_ref, below_ref, right_ref):
+    here = laid_cols(mine_ref, sent_ref, False)
+    beyond = laid_cols(mine_ref, sent_ref, True)
+    for part in range(2):
+        tall = laid_rows(mine_ref, sent_ref, kept_ref, got_ref, part, False)
+        home_ref[part] = dot(tall, here)
+        right_ref[part] = dot(tall, beyond).astype(bf16)
+        tall = laid_rows(mine_ref, sent_ref, kept_ref, got_ref, part, True)
+        below_ref[part] = dot(tall, here)
 
 
 def down_kernel(below_ref, diag_ref, down_ref):
     down_ref[...] = (below_ref[...] + diag_ref[...].astype(f32)).astype(bf16)
+
+
+def pass_kernel(block_ref, out_ref):
+    out_ref[...] = block_ref[...]
 
 
 def slice_kernel(layer, own0_ref, own1_ref, home_ref, above_ref, left_ref, out_ref):
     grad = home_ref[...] + left_ref[...].astype(f32) + above_ref[...].astype(f32)
     own = jnp.where(layer() == 0, own0_ref[...].astype(f32), own1_ref[...].astype(f32))
     out_ref[...] = (own - object_rate * grad).astype(bf16)
-
-
-def pass_kernel(block_ref, out_ref):
-    out_ref[...] = block_ref[...]
 
 
 def token_kernel(token_ref):
@@ -307,7 +318,7 @@
     inputs = [*halves, probe, *slices]
 
     def body(*refs):
-        blocks, (out_probe, out_tile, sems) = refs[3 : len(inputs)], refs[-3:]
+        blocks, (out_probe, out_tile, new_ref, sems, probe_sems) = refs[3 : len(inputs)], refs[-5:]
         places = [layer(), 1 - layer()][: len(blocks)]
         copies = [
             pltpu.make_async_copy(block, out_tile.at[0, place], sems.at[at])
@@ -315,7 +326,7 @@
         ]
         for copy in copies:
             copy.start()
-        probe_kernel(step, modes, *refs[:3], out_probe)
+        copies += probe_kernel(step, modes, *refs[:3], new_ref, out_probe, probe_sems)
         for copy in copies:
             copy.wait()
 
@@ -323,8 +334,12 @@
         body,
         out_shape=[shape_of(f32, *probe.shape), like],
         in_specs=[vmem] * len(inputs) + [anywhere] * len(after),
-        out_specs=[vmem, anywhere],
-        scratch_shapes=[pltpu.SemaphoreType.DMA((2,))],
+        out_specs=[anywhere, anywhere],
+        scratch_shapes=[
+            pltpu.VMEM(probe.shape, f32),
+            pltpu.SemaphoreType.DMA((2,)),
+            pltpu.SemaphoreType.DMA((8,)),
+        ],
         compiler_params=pltpu.CompilerParams(vmem_limit_bytes=8 * 2**20),
         cost_estimate=pl.CostEstimate(
             flops=4 * probe.size, bytes_accessed=12 * probe.size, transcendentals=0
@@ -383,18 +398,32 @@
         out_ref[pl.ds(block * size, size), :] = blocks[block]
 
 
-def probe_kernel(step, modes, mine_ref, other_ref, probe_ref, out_ref):
+def probe_kernel(step, modes, mine_ref, other_ref, probe_ref, new_ref, out_hbm, sems):
     core = place_of(core_group())
     lane_tiles = 2
     n = mine_ref.shape[0]
     stride = lane_tiles * modes
+    pieces = sems.shape[0] // 2
+    size = n // pieces
+    copies = []
     for part in range(2):
-        total = jnp.where(core == part, mine_ref[...].astype(f32), other_ref[...].astype(f32))
-        for mode in range(modes):
-            for tile in range(lane_tiles):
-                lane = (mode * lane_tiles + tile) * 128
-                where = pl.ds(part * n * stride + tile * modes + mode, n, stride=stride)
-                out_ref[where, :] = probe_ref[where, :] - step * total[:, lane : lane + 128]
+        for piece in range(pieces):
+            at = pl.ds(piece * size, size)
+            mine, other = mine_ref[at, :].astype(f32), other_ref[at, :].astype(f32)
+            total = jnp.where(core == part, mine, other)
+            start = (part * n + piece * size) * stride
+            for mode in range(modes):
+                for tile in range(lane_tiles):
+                    lane = (mode * lane_tiles + tile) * 128
+                    where = pl.ds(start + tile * modes + mode, size, stride=stride)
+                    new_ref[where, :] = probe_ref[where, :] - step * total[:, lane : lane + 128]
+            rows = pl.ds(start, size * stride)
+            copy = pltpu.make_async_copy(
+                new_ref.at[rows, :], out_hbm.at[rows, :], sems.at[len(copies)]
+            )
+            copy.start()
+            copies.append(copy)
+    return copies
 
 
 def exchange_groups():
@@ -503,14 +532,6 @@
     real = shape_of(f32, 2, pixels, pixels)
     like = shape_of(bf16, *tile_object.shape)
 
-    def laid_out(patch, got, after, flops):
-        return run(
-            job(spread_kernel, [real, real, tile, tile], [mine, sent, patch, got]),
-            limit=16,
-            after=after,
-            flops=flops,
-        )
-
     core, groups = core_group(), exchange_groups()
     if exchanged:
         got = lax.ppermute(given, "pos", swap)
@@ -518,29 +539,32 @@
     scattered = []
     while len(groups) > 1 and keep.shape[0] >> len(groups[0]) >= 16:
         group, groups = groups[0], groups[1:]
-        for bit in reversed(group):
-            if exchanged and scattered == [] and bit == group[0]:
-                home, below, to_right, to_diag = laid_out(kept, got, [keep], LATE[0])
-                diag_in = from_behind(to_diag, 0, 1)
-                keep, give = run(folded([bit], keep, arrived), after=[to_right])
-            else:
-                keep, give = run(folded([bit], keep, arrived))
-            arrived = [swap_with(give, [bit], 1)]
+        keep, *gives = run(folded(group, keep, arrived))
+        arrived = [swap_with(x, group, at) for at, x in enumerate(gives, 1)]
         scattered.append(group)
     first, second, *others = [[bit] for group in groups for bit in group]
-    (total,) = run(added(keep, arrived), flops=LATE[1])
-    arrived = swapped(total, first)
+    if exchanged:
+        patches = [mine, sent, kept, got]
+        (to_diag,) = run(
+            job(diag_kernel, [tile], patches), limit=16, after=[keep], flops=LATE[0]
+        )
+        diag_in = from_behind(to_diag, 0, 1)
+        home, below, to_right = run(
+            job(spread_kernel, [real, real, tile], patches), limit=16, after=[to_diag]
+        )
+    (total,) = run(added(keep, arrived), after=[below] if exchanged else [], flops=LATE[1])
+    (total,) = run(added(total, swapped(total, first)), flops=LATE[2])
+    arrived = swapped(total, second)
     if exchanged:
         (down,), (to_right,) = run(
             job(down_kernel, [tile], [below, diag_in]),
             job(pass_kernel, [tile], [to_right]),
             after=[total],
-            flops=LATE[2],
+            flops=LATE[3],
         )
         above = from_behind(down, 1, 0)
         left_in = from_behind(to_right, 0, 1)
-    (total,) = run(added(total, arrived), after=[down] if exchanged else [], flops=LATE[3])
-    (total,) = run(added(total, swapped(total, second)), flops=LATE[4])
+    (total,) = run(added(total, arrived), after=[down] if exchanged else [], flops=LATE[4])
     for group in others:
         (total,) = run(added(total, swapped(total, group)))
     arrived = swapped(total, scattered[-1])
@@ -578,7 +602,11 @@
         new_probe, _ = finished(this_layer, step, modes, halves, probe, (), like, ())
         slices = []
         for patch_grad, old in ((kept, own[0]), (given, own1)):
-            home, below, to_right, to_diag = laid_out(patch_grad, jnp.zeros_like(kept), [], 0)
+            patches = [mine, sent, patch_grad, jnp.zeros_like(kept)]
+            (to_diag,) = run(job(diag_kernel, [tile], patches), limit=16)
+            home, below, to_right = run(
+                job(spread_kernel, [real, real, tile], patches), limit=16
+            )
             (down,) = run(job(down_kernel, [tile], [below, from_behind(to_diag, 0, 1)]))
             above = from_behind(down, 1, 0).astype(f32)
             grad = lax.psum(home + from_behind(to_right, 0, 1).astype(f32) + above, "pos")

time: 71.7 us -> 67 us (0.934)
  waiting for transfers between devices: 35.4 us -> 28.5 us
  starting transfers between devices: 23.3 us -> 25.2 us
    ppermute x9 -> x10, waiting for transfers between devices: 16.4 us -> 6.36 us  [swap_with(): lax.ppermute(x, ('tile', 'pos'), [(i, i ^ mask) for i in range(devices)])]
    ppermute x8, waiting for transfers between devices: 7.89 us -> 10.2 us  [from_behind(): return lax.ppermute(block, 'tile', [(source(i), i) for i in range(tiles)])]
    ppermute x9 -> x10, starting transfers between devices: 10.5 us -> 12.1 us  [swap_with(): lax.ppermute(x, ('tile', 'pos'), [(i, i ^ mask) for i in range(devices)])]
    ppermute x1, waiting for transfers between devices: 4.31 us -> 5.62 us  [shards(): other_slice = lax.ppermute(this_slice, 'pos', swap)]
    pallas_call x14, Pallas kernels: 7.75 us -> 8.47 us  [run(): pl.pallas_call(body, out_shape=sum(outs, []), in_specs=sum(specs, []) + [...]
  transfers between devices with their start and end apart: 20 -> 21, of which waited for: 13 -> 9; matrix products, arithmetic and copies ran while one was open for 0% -> 0% of each run, Pallas kernels for 6% -> 7%
where the time goes in v16:
time: 67 us; the launch traced here: 66.8 us
  waiting for transfers between devices  28.5 us (43%)
  starting transfers between devices  25.2 us (38%)
  Pallas kernels  9.73 us (15%)
  local copies, waits for them, and re-layouts  1.86 us (3%)
  between operations  1.46 us (2%)
    ppermute x10, starting transfers between devices, swap_with(): lax.ppermute(x, ('tile', 'pos'), [(i, i ^ mask) for i in range(devices)])  12.1 us
    ppermute x8, waiting for transfers between devices, from_behind(): return lax.ppermute(block, 'tile', [(source(i), i) for i in range(tiles)])  10.2 us
    ppermute x8, starting transfers between devices, from_behind(): return lax.ppermute(block, 'tile', [(source(i), i) for i in range(tiles)])  8.52 us
    pallas_call x14, Pallas kernels, run(): pl.pallas_call(body, out_shape=sum(outs, []), in_specs=sum(specs, []) + [...  8.47 us
    ppermute x10, waiting for transfers between devices, swap_with(): lax.ppermute(x, ('tile', 'pos'), [(i, i ^ mask) for i in range(devices)])  6.36 us
    ppermute x1, waiting for transfers between devices, shards(): other_slice = lax.ppermute(this_slice, 'pos', swap)  5.62 us
    ppermute x1, waiting for transfers between devices, shards(): got = lax.ppermute(given, 'pos', swap)  5.21 us
    ppermute x1, starting transfers between devices, shards(): other_slice = lax.ppermute(this_slice, 'pos', swap)  1.58 us
  transfers between devices with their start and end apart: 21, of which 9 were waited for; matrix products, arithmetic and copies ran while one was open for 0% of the time, Pallas kernels for 7%

profile of v16, /device:TPU:0, one launch (start us, length us, event | category | flops | bytes accessed | tf_op | source)
XLA Modules:
  0.0 66.8 jit_solution(10600841577325036153)
XLA Ops:
  0.6 1.2 %slice_bitcast_fusion = (bf16[2,256,256]{2,1,0:T(8,128)(2,1)S(1)}, bf16[2,256,256]{2,1,0:T(8,128)(2,1)S(1)}) fusion(bf16[1,2,2,256,256]{4,3,2,1,0:T(8,128)(2,1)} %param.7), kind=kLoop, calls=%fused_computation | loop fusion | bytes 1048576 | tf_op jit(solution)/shard_map/squeeze | solution.py:481
  1.8 0.0 copy-start.1
  1.8 5.1 %collective-permute-start.4 = (bf16[2,256,256]{2,1,0:T(8,128)(2,1)S(1)}, bf16[2,256,256]{2,1,0:T(8,128)(2,1)S(1)}, u32[]{:S(2)}, u32[]{:S(2)}) collective-permute-start(bf16[2,256,256]{2,1,0:T(8,128)(2,1)S(1)} %get-tuple-element.46.refs_4_.refs_2_.refs_0_), channel_id=1, source_target_pairs={{8,0},{10,2},{12,4},{14,6},{16,8},{18,10},{20,12},{22,14},{24,16},... | collective-permute-start | bytes 786440 | tf_op jit(solution)/shard_map/ppermute | solution.py:31
  6.9 0.7 collective-permute-start.1
  8.2 0.0 copy-start.3
  8.3 0.7 %copy-done.3 = s32[1,1,2,2]{3,2,1,0:T(2,128)S(1)} copy-done((s32[1,1,2,2]{3,2,1,0:T(2,128)S(1)}, s32[1,1,2,2]{3,2,1,0:T(2,128)}, u32[]{:S(2)}) %copy-start.3) | copy-done | bytes 40
  8.9 0.6 shard_map.86
  9.5 0.5 collective-permute-start.2
  10.0 3.6 %collective-permute-done.4.refs_4_ = bf16[2,256,256]{2,1,0:T(8,128)(2,1)S(1)} collective-permute-done((bf16[2,256,256]{2,1,0:T(8,128)(2,1)S(1)}, bf16[2,256,256]{2,1,0:T(8,128)(2,1)S(1)}, u32[]{:S(2)}, u32[]{:S(2)}) %collective-permute-start.4) | collective-permute-done | bytes 262176 | tf_op jit(solution)/shard_map/ppermute | solution.py:31
  13.6 1.5 %collective-permute-start = (bf16[272,256]{1,0:T(8,128)(2,1)S(1)}, bf16[272,256]{1,0:T(8,128)(2,1)S(1)}, u32[]{:S(2)}, u32[]{:S(2)}) collective-permute-start(bf16[272,256]{1,0:T(8,128)(2,1)S(1)} %get-tuple-element.25), channel_id=1, source_target_pairs={{0,1},{1,0},{2,3},{3,2},{4,5},{5,4},{6,7},{7,6},{8,9},{9,8},{10,11... | collective-permute-start | bytes 417800 | tf_op jit(solution)/shard_map/ppermute | solution.py:503
  15.2 2.9 %collective-permute-done.2.refs_4_ = bf16[2,256,256]{2,1,0:T(8,128)(2,1)S(1)} collective-permute-done((bf16[2,256,256]{2,1,0:T(8,128)(2,1)S(1)}, bf16[2,256,256]{2,1,0:T(8,128)(2,1)S(1)}, u32[]{:S(2)}, u32[]{:S(2)}) %collective-permute-start.2) | collective-permute-done | bytes 262176 | tf_op jit(solution)/shard_map/ppermute | solution.py:31
  18.1 0.3 collective-permute-start.3
  18.5 0.1 shard_map.87
  18.6 1.2 %collective-permute-done.refs_1_ = bf16[272,256]{1,0:T(8,128)(2,1)S(1)} collective-permute-done((bf16[272,256]{1,0:T(8,128)(2,1)S(1)}, bf16[272,256]{1,0:T(8,128)(2,1)S(1)}, u32[]{:S(2)}, u32[]{:S(2)}) %collective-permute-start) | collective-permute-done | bytes 139296 | tf_op jit(solution)/shard_map/ppermute | solution.py:503
  19.7 0.0 collective-permute-done.5.refs_5_
  19.7 0.0 collective-permute-done.1.refs_3_
  19.7 1.8 %shard_map.88 = (bf16[2,256,256]{2,1,0:T(8,128)(2,1)S(1)}, f32[2,256,512]{2,1,0:T(8,128)S(1)}) custom-call(bf16[272,256]{1,0:T(8,128)(2,1)S(1)} %get-tuple-element.24.refs_0_, bf16[272,256]{1,0:T(8,128)(2,1)S(1)} %collective-permute-done.refs_1_, bf16[2,256,256]{2,1,0:T(8,128)(2,1)S(1)} %get-tuple-element.46.refs_4_.refs_2_.refs_0_, ...), custom_call_target="tpu_custom_call" | custom-call | flops 1500000000 | bytes 4472832 | tf_op jit(solution)/shard_map/pallas_call | solution.py:302
  21.5 0.8 %collective-permute-done.3.refs_5_ = bf16[2,256,256]{2,1,0:T(8,128)(2,1)S(1)} collective-permute-done((bf16[2,256,256]{2,1,0:T(8,128)(2,1)S(1)}, bf16[2,256,256]{2,1,0:T(8,128)(2,1)S(1)}, u32[]{:S(2)}, u32[]{:S(2)}) %collective-permute-start.3) | collective-permute-done | bytes 262176 | tf_op jit(solution)/shard_map/ppermute | solution.py:31
  22.4 3.9 %shard_map.89 = (bf16[2,256,256]{2,1,0:T(8,128)(2,1)S(1)}, bf16[2,256,256]{2,1,0:T(8,128)(2,1)S(1)}, bf16[256,512]{1,0:T(8,128)(2,1)S(1)}, bf16[256,512]{1,0:T(8,128)(2,1)S(1)}) custom-call(bf16[272,256]{1,0:T(8,128)(2,1)S(1)} %get-tuple-element.24.refs_0_, bf16[272,256]{1,0:T(8,128)(2,1)S(1)} %collective-permute-done.refs_1_, ...), custom_call_target="tpu_custom_call" | custom-call | flops 4000000000 | bytes 6045696 | tf_op jit(solution)/shard_map/pallas_call | solution.py:302
  26.3 1.5 %collective-permute-start.6 = (bf16[256,512]{1,0:T(8,128)(2,1)S(1)}, bf16[256,512]{1,0:T(8,128)(2,1)S(1)}, u32[]{:S(2)}, u32[]{:S(2)}) collective-permute-start(bf16[256,512]{1,0:T(8,128)(2,1)S(1)} %get-tuple-element.32), channel_id=1, source_target_pairs={{0,2},{1,3},{2,0},{3,1},{4,6},{5,7},{6,4},{7,5},{8,10},{9,11},{10,... | collective-permute-start | bytes 786440 | tf_op jit(solution)/shard_map/ppermute | solution.py:439
  27.8 1.5 %collective-permute-start.10 = (bf16[2,256,256]{2,1,0:T(8,128)(2,1)S(1)}, bf16[2,256,256]{2,1,0:T(8,128)(2,1)S(1)}, u32[]{:S(2)}, u32[]{:S(2)}) collective-permute-start(bf16[2,256,256]{2,1,0:T(8,128)(2,1)S(1)} %get-tuple-element.38), channel_id=1, source_target_pairs={{0,1},{1,0},{2,3},{3,2},{4,5},{5,4},{6,7},{7,6},{8,9},{9,8},{10,11... | collective-permute-start | bytes 786440 | tf_op jit(solution)/shard_map/ppermute | solution.py:537
  29.3 0.1 shard_map.90
  29.4 1.2 %collective-permute-start.7 = (bf16[64,512]{1,0:T(8,128)(2,1)S(1)}, bf16[64,512]{1,0:T(8,128)(2,1)S(1)}, u32[]{:S(2)}, u32[]{:S(2)}) collective-permute-start(bf16[64,512]{1,0:T(8,128)(2,1)S(1)} %get-tuple-element.34), channel_id=1, source_target_pairs={{0,1},{1,0},{2,3},{3,2},{4,5},{5,4},{6,7},{7,6},{8,9},{9,8},{10,11... | collective-permute-start | bytes 196616 | tf_op jit(solution)/shard_map/ppermute | solution.py:439
  30.6 0.9 %collective-permute-start.8 = (bf16[64,512]{1,0:T(8,128)(2,1)S(1)}, bf16[64,512]{1,0:T(8,128)(2,1)S(1)}, u32[]{:S(2)}, u32[]{:S(2)}) collective-permute-start(bf16[64,512]{1,0:T(8,128)(2,1)S(1)} %get-tuple-element.35), channel_id=1, source_target_pairs={{0,4},{1,5},{2,6},{3,7},{4,0},{5,1},{6,2},{7,3},{8,12},{9,13},{10,... | collective-permute-start | bytes 196616 | tf_op jit(solution)/shard_map/ppermute | solution.py:439
  31.5 1.4 %collective-permute-start.9 = (bf16[64,512]{1,0:T(8,128)(2,1)S(1)}, bf16[64,512]{1,0:T(8,128)(2,1)S(1)}, u32[]{:S(2)}, u32[]{:S(2)}) collective-permute-start(bf16[64,512]{1,0:T(8,128)(2,1)S(1)} %get-tuple-element.36), channel_id=1, source_target_pairs={{0,5},{1,4},{2,7},{3,6},{4,1},{5,0},{6,3},{7,2},{8,13},{9,12},{10,... | collective-permute-start | bytes 196616 | tf_op jit(solution)/shard_map/ppermute | solution.py:439
  33.0 5.2 %collective-permute-done.10.refs_3_ = bf16[2,256,256]{2,1,0:T(8,128)(2,1)S(1)} collective-permute-done((bf16[2,256,256]{2,1,0:T(8,128)(2,1)S(1)}, bf16[2,256,256]{2,1,0:T(8,128)(2,1)S(1)}, u32[]{:S(2)}, u32[]{:S(2)}) %collective-permute-start.10) | collective-permute-done | bytes 262176 | tf_op jit(solution)/shard_map/ppermute | solution.py:537
  38.2 0.5 shard_map.91.refs_4_
  38.7 0.1 collective-permute-start.13
  38.8 1.1 %shard_map.92 = (f32[2,256,256]{2,1,0:T(8,128)S(1)}, f32[2,256,256]{2,1,0:T(8,128)S(1)}, bf16[2,256,256]{2,1,0:T(8,128)(2,1)S(1)}) custom-call(bf16[272,256]{1,0:T(8,128)(2,1)S(1)} %get-tuple-element.24.refs_0_, bf16[272,256]{1,0:T(8,128)(2,1)S(1)} %collective-permute-done.refs_1_, bf16[2,256,256]{2,1,0:T(8,128)(2,1)S(1)} %get-tuple-element.37.refs_2_, ...), custom_call_target="tpu_custom_call" | custom-call | flops 1000000 | bytes 2113536 | tf_op jit(solution)/shard_map/pallas_call | solution.py:302
  39.9 0.0 collective-permute-done.7.refs_1_
  39.9 0.0 collective-permute-done.9.refs_3_
  39.9 0.5 collective-permute-start.11
  40.5 4.5 %collective-permute-done.11.refs_1_ = bf16[64,512]{1,0:T(8,128)(2,1)S(1)} collective-permute-done((bf16[64,512]{1,0:T(8,128)(2,1)S(1)}, bf16[64,512]{1,0:T(8,128)(2,1)S(1)}, u32[]{:S(2)}, u32[]{:S(2)}) %collective-permute-start.11) | collective-permute-done | bytes 65568 | tf_op jit(solution)/shard_map/ppermute | solution.py:439
  45.0 2.9 %collective-permute-start.12 = (bf16[64,512]{1,0:T(8,128)(2,1)S(1)}, bf16[64,512]{1,0:T(8,128)(2,1)S(1)}, u32[]{:S(2)}, u32[]{:S(2)}) collective-permute-start(bf16[64,512]{1,0:T(8,128)(2,1)S(1)} %shard_map.94.refs_3_.refs_0_), channel_id=1, source_target_pairs={{0,16},{1,17},{2,18},{3,19},{4,20},{5,21},{6,22},{7,23},{8,24},{9,... | collective-permute-start | bytes 196616 | tf_op jit(solution)/shard_map/ppermute | solution.py:439
  47.9 0.1 shard_map.95
  47.9 0.1 collective-permute-start.18
  48.0 1.8 %collective-permute-start.17 = (bf16[2,256,256]{2,1,0:T(8,128)(2,1)S(1)}, bf16[2,256,256]{2,1,0:T(8,128)(2,1)S(1)}, u32[]{:S(2)}, u32[]{:S(2)}) collective-permute-start(bf16[2,256,256]{2,1,0:T(8,128)(2,1)S(1)} %get-tuple-element.41.refs_2_), channel_id=1, source_target_pairs={{24,0},{26,2},{28,4},{30,6},{0,8},{2,10},{4,12},{6,14},{8,16},{10,... | collective-permute-start | bytes 786440 | tf_op jit(solution)/shard_map/ppermute | solution.py:31
  49.8 1.8 %collective-permute-done.12.refs_1_ = bf16[64,512]{1,0:T(8,128)(2,1)S(1)} collective-permute-done((bf16[64,512]{1,0:T(8,128)(2,1)S(1)}, bf16[64,512]{1,0:T(8,128)(2,1)S(1)}, u32[]{:S(2)}, u32[]{:S(2)}) %collective-permute-start.12) | collective-permute-done | bytes 65568 | tf_op jit(solution)/shard_map/ppermute | solution.py:439
  51.7 1.6 %collective-permute-start.16 = (bf16[64,512]{1,0:T(8,128)(2,1)S(1)}, bf16[64,512]{1,0:T(8,128)(2,1)S(1)}, u32[]{:S(2)}, u32[]{:S(2)}) collective-permute-start(bf16[64,512]{1,0:T(8,128)(2,1)S(1)} %shard_map.96.refs_5_.refs_0_), channel_id=1, source_target_pairs={{0,5},{1,4},{2,7},{3,6},{4,1},{5,0},{6,3},{7,2},{8,13},{9,12},{10,... | collective-permute-start | bytes 196616 | tf_op jit(solution)/shard_map/ppermute | solution.py:439
  53.3 1.4 %collective-permute-start.15 = (bf16[64,512]{1,0:T(8,128)(2,1)S(1)}, bf16[64,512]{1,0:T(8,128)(2,1)S(1)}, u32[]{:S(2)}, u32[]{:S(2)}) collective-permute-start(bf16[64,512]{1,0:T(8,128)(2,1)S(1)} %shard_map.96.refs_5_.refs_0_), channel_id=1, source_target_pairs={{0,4},{1,5},{2,6},{3,7},{4,0},{5,1},{6,2},{7,3},{8,12},{9,13},{10,... | collective-permute-start | bytes 196616 | tf_op jit(solution)/shard_map/ppermute | solution.py:439
  54.7 0.5 collective-permute-start.14
  55.2 2.8 %collective-permute-done.17.refs_3_ = bf16[2,256,256]{2,1,0:T(8,128)(2,1)S(1)} collective-permute-done((bf16[2,256,256]{2,1,0:T(8,128)(2,1)S(1)}, bf16[2,256,256]{2,1,0:T(8,128)(2,1)S(1)}, u32[]{:S(2)}, u32[]{:S(2)}) %collective-permute-start.17) | collective-permute-done | bytes 262176 | tf_op jit(solution)/shard_map/ppermute | solution.py:31
  58.0 0.2 shard_map.97.refs_4_.refs_3_
  58.2 1.6 %collective-permute-start.20 = (bf16[2,256,256]{2,1,0:T(8,128)(2,1)S(1)}, bf16[2,256,256]{2,1,0:T(8,128)(2,1)S(1)}, u32[]{:S(2)}, u32[]{:S(2)}) collective-permute-start(bf16[2,256,256]{2,1,0:T(8,128)(2,1)S(1)} %shard_map.97.refs_4_.refs_3_), channel_id=1, source_target_pairs={{0,1},{1,0},{2,3},{3,2},{4,5},{5,4},{6,7},{7,6},{8,9},{9,8},{10,11... | collective-permute-start | bytes 786440 | tf_op jit(solution)/shard_map/ppermute | solution.py:581
  59.8 0.1 shard_map.98.refs_0_
  59.9 0.1 collective-permute-start.19
  59.9 5.6 %collective-permute-done.20.refs_1_.refs_4_ = bf16[2,256,256]{2,1,0:T(8,128)(2,1)S(1)} collective-permute-done((bf16[2,256,256]{2,1,0:T(8,128)(2,1)S(1)}, bf16[2,256,256]{2,1,0:T(8,128)(2,1)S(1)}, u32[]{:S(2)}, u32[]{:S(2)}) %collective-permute-start.20) | collective-permute-done | bytes 262176 | tf_op jit(solution)/shard_map/ppermute | solution.py:581
  65.6 1.3 %shard_map.100 = (f32[2048,128]{1,0:T(8,128)}, bf16[1,2,2,256,256]{4,3,2,1,0:T(8,128)(2,1)}) custom-call(bf16[256,512]{1,0:T(8,128)(2,1)S(1)} %shard_map.98.refs_0_, bf16[256,512]{1,0:T(8,128)(2,1)S(1)} %collective-permute-done.19.refs_1_, f32[2048,128]{1,0:T(8,128)S(1)} %bitcast.16, bf16[2,256,256]{2,1,0:T(8,128)(2,1)S(1)} %shard_map.97.refs_4_.refs_3_, ...), custom_call_target="tpu_custom_call" | custom-call | flops 1048576 | bytes 3145728 | tf_op jit(solution)/shard_map/pallas_call | solution.py:333
  (20 shorter events, 0.1 us)
Async XLA Ops:
  0.6 7.6 %copy-start.2 = (bf16[1,1,2,256,256]{4,3,2,1,0:T(8,128)(2,1)S(1)}, bf16[1,1,2,256,256]{4,3,2,1,0:T(8,128)(2,1)}, u32[]{:S(2)}) copy-start(bf16[1,1,2,256,256]{4,3,2,1,0:T(8,128)(2,1)} %refs_3_.1) | copy-start | bytes 786436
  0.6 17.8 %copy-start = (f32[2,256,2,256]{3,2,1,0:T(2,128)S(1)}, f32[2,256,2,256]{3,2,1,0:T(2,128)}, u32[]{:S(2)}) copy-start(f32[2,256,2,256]{3,2,1,0:T(2,128)} %param.8) | copy-start | bytes 3145732
  1.8 16.7 %copy-start.1 = (bf16[512,512]{1,0:T(8,128)(2,1)S(1)}, bf16[512,512]{1,0:T(8,128)(2,1)}, u32[]{:S(2)}) copy-start(bf16[512,512]{1,0:T(8,128)(2,1)} %constant.10.refs_1_) | copy-start | bytes 1572868
  1.8 11.8 %collective-permute-start.4 = (bf16[2,256,256]{2,1,0:T(8,128)(2,1)S(1)}, bf16[2,256,256]{2,1,0:T(8,128)(2,1)S(1)}, u32[]{:S(2)}, u32[]{:S(2)}) collective-permute-start(bf16[2,256,256]{2,1,0:T(8,128)(2,1)S(1)} %get-tuple-element.46.refs_4_.refs_2_.refs_0_), channel_id=1, source_target_pairs={{8,0},{10,2},{12,4},{14,6},{16,8},{18,10},{20,12},{22,14},{24,16},... | collective-permute-start | bytes 786440 | tf_op jit(solution)/shard_map/ppermute | solution.py:31
  6.9 12.8 %collective-permute-start.1 = (bf16[2,2,256,256]{3,2,1,0:T(8,128)(2,1)}, bf16[2,2,256,256]{3,2,1,0:T(8,128)(2,1)S(1)}, u32[]{:S(2)}, u32[]{:S(2)}) collective-permute-start(bf16[2,2,256,256]{3,2,1,0:T(8,128)(2,1)} %bitcast.17), channel_id=1, source_target_pairs={{2,0},{4,2},{6,4},{0,6},{10,8},{12,10},{14,12},{8,14},{18,16},{20,... | collective-permute-start | bytes 1572872 | tf_op jit(solution)/shard_map/ppermute | solution.py:31
  8.2 0.7 %copy-start.3 = (s32[1,1,2,2]{3,2,1,0:T(2,128)S(1)}, s32[1,1,2,2]{3,2,1,0:T(2,128)}, u32[]{:S(2)}) copy-start(s32[1,1,2,2]{3,2,1,0:T(2,128)} %refs_0_.1) | copy-start | bytes 52
  9.5 8.6 %collective-permute-start.2 = (bf16[2,256,256]{2,1,0:T(8,128)(2,1)S(1)}, bf16[2,256,256]{2,1,0:T(8,128)(2,1)S(1)}, u32[]{:S(2)}, u32[]{:S(2)}) collective-permute-start(bf16[2,256,256]{2,1,0:T(8,128)(2,1)S(1)} %get-tuple-element.26.refs_2_.refs_1_), channel_id=1, source_target_pairs={{8,0},{10,2},{12,4},{14,6},{16,8},{18,10},{20,12},{22,14},{24,16},... | collective-permute-start | bytes 786440 | tf_op jit(solution)/shard_map/ppermute | solution.py:31
  13.6 6.1 %collective-permute-start.5 = (bf16[2,256,256]{2,1,0:T(8,128)(2,1)S(1)}, bf16[2,256,256]{2,1,0:T(8,128)(2,1)S(1)}, u32[]{:S(2)}, u32[]{:S(2)}) collective-permute-start(bf16[2,256,256]{2,1,0:T(8,128)(2,1)S(1)} %collective-permute-done.4.refs_4_), channel_id=1, source_target_pairs={{2,0},{4,2},{6,4},{0,6},{10,8},{12,10},{14,12},{8,14},{18,16},{20,... | collective-permute-start | bytes 786440 | tf_op jit(solution)/shard_map/ppermute | solution.py:31
  13.6 6.1 %collective-permute-start = (bf16[272,256]{1,0:T(8,128)(2,1)S(1)}, bf16[272,256]{1,0:T(8,128)(2,1)S(1)}, u32[]{:S(2)}, u32[]{:S(2)}) collective-permute-start(bf16[272,256]{1,0:T(8,128)(2,1)S(1)} %get-tuple-element.25), channel_id=1, source_target_pairs={{0,1},{1,0},{2,3},{3,2},{4,5},{5,4},{6,7},{7,6},{8,9},{9,8},{10,11... | collective-permute-start | bytes 417800 | tf_op jit(solution)/shard_map/ppermute | solution.py:503
  18.1 4.2 %collective-permute-start.3 = (bf16[2,256,256]{2,1,0:T(8,128)(2,1)S(1)}, bf16[2,256,256]{2,1,0:T(8,128)(2,1)S(1)}, u32[]{:S(2)}, u32[]{:S(2)}) collective-permute-start(bf16[2,256,256]{2,1,0:T(8,128)(2,1)S(1)} %collective-permute-done.2.refs_4_), channel_id=1, source_target_pairs={{2,0},{4,2},{6,4},{0,6},{10,8},{12,10},{14,12},{8,14},{18,16},{20,... | collective-permute-start | bytes 786440 | tf_op jit(solution)/shard_map/ppermute | solution.py:31
  19.7 2.6 %copy-start.4 = (bf16[512,512]{1,0:T(8,128)(2,1)S(1)}, bf16[512,512]{1,0:T(8,128)(2,1)}, u32[]{:S(2)}) copy-start(bf16[512,512]{1,0:T(8,128)(2,1)} %constant.11.refs_10_) | copy-start | bytes 1572868
  26.3 3.0 %collective-permute-start.6 = (bf16[256,512]{1,0:T(8,128)(2,1)S(1)}, bf16[256,512]{1,0:T(8,128)(2,1)S(1)}, u32[]{:S(2)}, u32[]{:S(2)}) collective-permute-start(bf16[256,512]{1,0:T(8,128)(2,1)S(1)} %get-tuple-element.32), channel_id=1, source_target_pairs={{0,2},{1,3},{2,0},{3,1},{4,6},{5,7},{6,4},{7,5},{8,10},{9,11},{10,... | collective-permute-start | bytes 786440 | tf_op jit(solution)/shard_map/ppermute | solution.py:439
  27.8 10.4 %collective-permute-start.10 = (bf16[2,256,256]{2,1,0:T(8,128)(2,1)S(1)}, bf16[2,256,256]{2,1,0:T(8,128)(2,1)S(1)}, u32[]{:S(2)}, u32[]{:S(2)}) collective-permute-start(bf16[2,256,256]{2,1,0:T(8,128)(2,1)S(1)} %get-tuple-element.38), channel_id=1, source_target_pairs={{0,1},{1,0},{2,3},{3,2},{4,5},{5,4},{6,7},{7,6},{8,9},{9,8},{10,11... | collective-permute-start | bytes 786440 | tf_op jit(solution)/shard_map/ppermute | solution.py:537
  29.4 10.5 %collective-permute-start.7 = (bf16[64,512]{1,0:T(8,128)(2,1)S(1)}, bf16[64,512]{1,0:T(8,128)(2,1)S(1)}, u32[]{:S(2)}, u32[]{:S(2)}) collective-permute-start(bf16[64,512]{1,0:T(8,128)(2,1)S(1)} %get-tuple-element.34), channel_id=1, source_target_pairs={{0,1},{1,0},{2,3},{3,2},{4,5},{5,4},{6,7},{7,6},{8,9},{9,8},{10,11... | collective-permute-start | bytes 196616 | tf_op jit(solution)/shard_map/ppermute | solution.py:439
  30.6 9.2 %collective-permute-start.8 = (bf16[64,512]{1,0:T(8,128)(2,1)S(1)}, bf16[64,512]{1,0:T(8,128)(2,1)S(1)}, u32[]{:S(2)}, u32[]{:S(2)}) collective-permute-start(bf16[64,512]{1,0:T(8,128)(2,1)S(1)} %get-tuple-element.35), channel_id=1, source_target_pairs={{0,4},{1,5},{2,6},{3,7},{4,0},{5,1},{6,2},{7,3},{8,12},{9,13},{10,... | collective-permute-start | bytes 196616 | tf_op jit(solution)/shard_map/ppermute | solution.py:439
  31.5 8.4 %collective-permute-start.9 = (bf16[64,512]{1,0:T(8,128)(2,1)S(1)}, bf16[64,512]{1,0:T(8,128)(2,1)S(1)}, u32[]{:S(2)}, u32[]{:S(2)}) collective-permute-start(bf16[64,512]{1,0:T(8,128)(2,1)S(1)} %get-tuple-element.36), channel_id=1, source_target_pairs={{0,5},{1,4},{2,7},{3,6},{4,1},{5,0},{6,3},{7,2},{8,13},{9,12},{10,... | collective-permute-start | bytes 196616 | tf_op jit(solution)/shard_map/ppermute | solution.py:439
  38.7 9.2 %collective-permute-start.13 = (bf16[2,256,256]{2,1,0:T(8,128)(2,1)S(1)}, bf16[2,256,256]{2,1,0:T(8,128)(2,1)S(1)}, u32[]{:S(2)}, u32[]{:S(2)}) collective-permute-start(bf16[2,256,256]{2,1,0:T(8,128)(2,1)S(1)} %shard_map.91.refs_4_), channel_id=1, source_target_pairs={{6,0},{0,2},{2,4},{4,6},{14,8},{8,10},{10,12},{12,14},{22,16},{16,... | collective-permute-start | bytes 786440 | tf_op jit(solution)/shard_map/ppermute | solution.py:31
  39.9 5.0 %collective-permute-start.11 = (bf16[64,512]{1,0:T(8,128)(2,1)S(1)}, bf16[64,512]{1,0:T(8,128)(2,1)S(1)}, u32[]{:S(2)}, u32[]{:S(2)}) collective-permute-start(bf16[64,512]{1,0:T(8,128)(2,1)S(1)} %shard_map.93.refs_0_), channel_id=1, source_target_pairs={{0,8},{1,9},{2,10},{3,11},{4,12},{5,13},{6,14},{7,15},{8,0},{9,1},... | collective-permute-start | bytes 196616 | tf_op jit(solution)/shard_map/ppermute | solution.py:439
  45.0 6.7 %collective-permute-start.12 = (bf16[64,512]{1,0:T(8,128)(2,1)S(1)}, bf16[64,512]{1,0:T(8,128)(2,1)S(1)}, u32[]{:S(2)}, u32[]{:S(2)}) collective-permute-start(bf16[64,512]{1,0:T(8,128)(2,1)S(1)} %shard_map.94.refs_3_.refs_0_), channel_id=1, source_target_pairs={{0,16},{1,17},{2,18},{3,19},{4,20},{5,21},{6,22},{7,23},{8,24},{9,... | collective-permute-start | bytes 196616 | tf_op jit(solution)/shard_map/ppermute | solution.py:439
  47.9 7.3 %collective-permute-start.18 = (bf16[2,256,256]{2,1,0:T(8,128)(2,1)S(1)}, bf16[2,256,256]{2,1,0:T(8,128)(2,1)S(1)}, u32[]{:S(2)}, u32[]{:S(2)}) collective-permute-start(bf16[2,256,256]{2,1,0:T(8,128)(2,1)S(1)} %get-tuple-element.43), channel_id=1, source_target_pairs={{6,0},{0,2},{2,4},{4,6},{14,8},{8,10},{10,12},{12,14},{22,16},{16,... | collective-permute-start | bytes 786440 | tf_op jit(solution)/shard_map/ppermute | solution.py:31
  48.0 10.0 %collective-permute-start.17 = (bf16[2,256,256]{2,1,0:T(8,128)(2,1)S(1)}, bf16[2,256,256]{2,1,0:T(8,128)(2,1)S(1)}, u32[]{:S(2)}, u32[]{:S(2)}) collective-permute-start(bf16[2,256,256]{2,1,0:T(8,128)(2,1)S(1)} %get-tuple-element.41.refs_2_), channel_id=1, source_target_pairs={{24,0},{26,2},{28,4},{30,6},{0,8},{2,10},{4,12},{6,14},{8,16},{10,... | collective-permute-start | bytes 786440 | tf_op jit(solution)/shard_map/ppermute | solution.py:31
  51.7 8.1 %collective-permute-start.16 = (bf16[64,512]{1,0:T(8,128)(2,1)S(1)}, bf16[64,512]{1,0:T(8,128)(2,1)S(1)}, u32[]{:S(2)}, u32[]{:S(2)}) collective-permute-start(bf16[64,512]{1,0:T(8,128)(2,1)S(1)} %shard_map.96.refs_5_.refs_0_), channel_id=1, source_target_pairs={{0,5},{1,4},{2,7},{3,6},{4,1},{5,0},{6,3},{7,2},{8,13},{9,12},{10,... | collective-permute-start | bytes 196616 | tf_op jit(solution)/shard_map/ppermute | solution.py:439
  53.3 6.5 %collective-permute-start.15 = (bf16[64,512]{1,0:T(8,128)(2,1)S(1)}, bf16[64,512]{1,0:T(8,128)(2,1)S(1)}, u32[]{:S(2)}, u32[]{:S(2)}) collective-permute-start(bf16[64,512]{1,0:T(8,128)(2,1)S(1)} %shard_map.96.refs_5_.refs_0_), channel_id=1, source_target_pairs={{0,4},{1,5},{2,6},{3,7},{4,0},{5,1},{6,2},{7,3},{8,12},{9,13},{10,... | collective-permute-start | bytes 196616 | tf_op jit(solution)/shard_map/ppermute | solution.py:439
  54.7 5.1 %collective-permute-start.14 = (bf16[64,512]{1,0:T(8,128)(2,1)S(1)}, bf16[64,512]{1,0:T(8,128)(2,1)S(1)}, u32[]{:S(2)}, u32[]{:S(2)}) collective-permute-start(bf16[64,512]{1,0:T(8,128)(2,1)S(1)} %shard_map.96.refs_5_.refs_0_), channel_id=1, source_target_pairs={{0,1},{1,0},{2,3},{3,2},{4,5},{5,4},{6,7},{7,6},{8,9},{9,8},{10,11... | collective-permute-start | bytes 196616 | tf_op jit(solution)/shard_map/ppermute | solution.py:439
  58.2 7.4 %collective-permute-start.20 = (bf16[2,256,256]{2,1,0:T(8,128)(2,1)S(1)}, bf16[2,256,256]{2,1,0:T(8,128)(2,1)S(1)}, u32[]{:S(2)}, u32[]{:S(2)}) collective-permute-start(bf16[2,256,256]{2,1,0:T(8,128)(2,1)S(1)} %shard_map.97.refs_4_.refs_3_), channel_id=1, source_target_pairs={{0,1},{1,0},{2,3},{3,2},{4,5},{5,4},{6,7},{7,6},{8,9},{9,8},{10,11... | collective-permute-start | bytes 786440 | tf_op jit(solution)/shard_map/ppermute | solution.py:581
  59.9 5.7 %collective-permute-start.19 = (bf16[256,512]{1,0:T(8,128)(2,1)S(1)}, bf16[256,512]{1,0:T(8,128)(2,1)S(1)}, u32[]{:S(2)}, u32[]{:S(2)}) collective-permute-start(bf16[256,512]{1,0:T(8,128)(2,1)S(1)} %shard_map.98.refs_0_), channel_id=1, source_target_pairs={{0,2},{1,3},{2,0},{3,1},{4,6},{5,7},{6,4},{7,5},{8,10},{9,11},{10,... | collective-permute-start | bytes 786440 | tf_op jit(solution)/shard_map/ppermute | solution.py:439

commit v17 on v13

--- a/solution.py
+++ b/solution.py
@@ -167,7 +167,7 @@
 def gradient_kernel(
     mine_ref, sent_ref, own_ref, right_ref, below_ref, diag_ref, near_ref, arrive_ref, planes_ref,
     prop_ref, dft_ref,
-    kept_ref, given_ref, keep_ref, give_ref, grad_ref, term_ref, *, layer
+    kept_ref, given_ref, keep_ref, give1_ref, give2_ref, grad_ref, term_ref, *, layer
 ):
     n = own_ref.shape[1]
     modes = planes_ref.shape[2] // n
@@ -208,7 +208,8 @@
         term_ref[1, :, lanes] = (near[0] * b_im - near[1] * b_re).astype(bf16)
     core = place_of(core_group())
     keep_ref[...] = term_ref[core]
-    give_ref[...] = term_ref[1 - core]
+    give1_ref[...] = term_ref[1 - core, : n // 2]
+    give2_ref[...] = term_ref[1 - core, n // 2 :]
     for part in range(2):
         grad_ref[0, part] = grad[part].astype(bf16)
     layer = layer()
@@ -304,7 +305,7 @@
     inputs = [*halves, probe, *slices]
 
     def body(*refs):
-        blocks, (out_probe, out_tile, sems) = refs[3 : len(inputs)], refs[-3:]
+        blocks, (out_probe, out_tile, new_ref, sems, probe_sems) = refs[3 : len(inputs)], refs[-5:]
         places = [layer(), 1 - layer()][: len(blocks)]
         copies = [
             pltpu.make_async_copy(block, out_tile.at[0, place], sems.at[at])
@@ -312,7 +313,7 @@
         ]
         for copy in copies:
             copy.start()
-        probe_kernel(step, modes, *refs[:3], out_probe)
+        copies += probe_kernel(step, modes, *refs[:3], new_ref, out_probe, probe_sems)
         for copy in copies:
             copy.wait()
 
@@ -320,8 +321,12 @@
         body,
         out_shape=[shape_of(f32, *probe.shape), like],
         in_specs=[vmem] * len(inputs) + [anywhere] * len(after),
-        out_specs=[vmem, anywhere],
-        scratch_shapes=[pltpu.SemaphoreType.DMA((2,))],
+        out_specs=[anywhere, anywhere],
+        scratch_shapes=[
+            pltpu.VMEM(probe.shape, f32),
+            pltpu.SemaphoreType.DMA((2,)),
+            pltpu.SemaphoreType.DMA((8,)),
+        ],
         compiler_params=pltpu.CompilerParams(vmem_limit_bytes=8 * 2**20),
         cost_estimate=pl.CostEstimate(
             flops=4 * probe.size, bytes_accessed=12 * probe.size, transcendentals=0
@@ -352,8 +357,11 @@
     got = len(refs) - 1 - blocks.shape[0]
     arrived, keep_out, give_outs = refs[:got], refs[got], refs[got + 1 : -1]
     total = keep_ref[...].astype(f32)
-    for ref in arrived:
-        total += ref[...].astype(f32)
+    if arrived[0].shape != keep_ref.shape:
+        total += jnp.concatenate([ref[...].astype(f32) for ref in arrived], axis=0)
+    else:
+        for ref in arrived:
+            total += ref[...].astype(f32)
     size = blocks.shape[1]
     for block in range(blocks.shape[0]):
         blocks[block] = total[block * size : (block + 1) * size]
@@ -380,18 +388,32 @@
         out_ref[pl.ds(block * size, size), :] = blocks[block]
 
 
-def probe_kernel(step, modes, mine_ref, other_ref, probe_ref, out_ref):
+def probe_kernel(step, modes, mine_ref, other_ref, probe_ref, new_ref, out_hbm, sems):
     core = place_of(core_group())
     lane_tiles = 2
     n = mine_ref.shape[0]
     stride = lane_tiles * modes
+    pieces = sems.shape[0] // 2
+    size = n // pieces
+    copies = []
     for part in range(2):
-        total = jnp.where(core == part, mine_ref[...].astype(f32), other_ref[...].astype(f32))
-        for mode in range(modes):
-            for tile in range(lane_tiles):
-                lane = (mode * lane_tiles + tile) * 128
-                where = pl.ds(part * n * stride + tile * modes + mode, n, stride=stride)
-                out_ref[where, :] = probe_ref[where, :] - step * total[:, lane : lane + 128]
+        for piece in range(pieces):
+            at = pl.ds(piece * size, size)
+            mine, other = mine_ref[at, :].astype(f32), other_ref[at, :].astype(f32)
+            total = jnp.where(core == part, mine, other)
+            start = (part * n + piece * size) * stride
+            for mode in range(modes):
+                for tile in range(lane_tiles):
+                    lane = (mode * lane_tiles + tile) * 128
+                    where = pl.ds(start + tile * modes + mode, size, stride=stride)
+                    new_ref[where, :] = probe_ref[where, :] - step * total[:, lane : lane + 128]
+            rows = pl.ds(start, size * stride)
+            copy = pltpu.make_async_copy(
+                new_ref.at[rows, :], out_hbm.at[rows, :], sems.at[len(copies)]
+            )
+            copy.start()
+            copies.append(copy)
+    return copies
 
 
 def exchange_groups():
@@ -483,12 +505,13 @@
         limit=16,
     )
     half = shape_of(bf16, pixels, width)
+    quarter = shape_of(bf16, pixels // 2, width)
     grads = pltpu.VMEM((2, 2, pixels, pixels), bf16)
     this_layer = (lambda: lax.axis_index("pos")) if exchanged else (lambda: 0)
-    kept, given, keep, give = run(
+    kept, given, keep, *gives = run(
         job(
             lambda *refs: gradient_kernel(*refs, layer=this_layer),
-            [tile, tile, half, half],
+            [tile, tile, half, quarter, quarter],
             [mine, sent, own1, right, below1, diag1, near, arrive, probe_planes, table, dft],
             scratch=[grads, pltpu.VMEM((2, pixels, width), bf16)],
         ),
@@ -511,7 +534,7 @@
     core, groups = core_group(), exchange_groups()
     if exchanged:
         got = lax.ppermute(given, "pos", swap)
-    arrived = [swap_with(give, core, 1)]
+    arrived = [swap_with(x, core, 1) for x in gives]
     scattered = []
     while len(groups) > 1 and keep.shape[0] >> len(groups[0]) >= 16:
         group, groups = groups[0], groups[1:]

time: 65.5 us -> 63.8 us (0.974)
  waiting for transfers between devices: 27.1 us -> 24 us
  starting transfers between devices: 25.3 us -> 27.2 us
    ppermute x1, waiting for transfers between devices: 5.21 us -> 1.13 us  [shards(): got = lax.ppermute(given, 'pos', swap)]
    ppermute x8, starting transfers between devices: 9.13 us -> 10.6 us  [from_behind(): return lax.ppermute(block, 'tile', [(source(i), i) for i in range(tiles)])]
    ppermute x10 -> x11, waiting for transfers between devices: 4.87 us -> 6.18 us  [swap_with(): lax.ppermute(x, ('tile', 'pos'), [(i, i ^ mask) for i in range(devices)])]
    ppermute x10 -> x11, starting transfers between devices: 11.6 us -> 11.7 us  [swap_with(): lax.ppermute(x, ('tile', 'pos'), [(i, i ^ mask) for i in range(devices)])]
  transfers between devices with their start and end apart: 21 -> 22, of which waited for: 10 -> 11; matrix products, arithmetic and copies ran while one was open for 0% -> 0% of each run, Pallas kernels for 6% -> 6%
where the time goes in v17:
time: 63.8 us; the launch traced here: 63.6 us
  starting transfers between devices  27.2 us (43%)
  waiting for transfers between devices  24 us (38%)
  Pallas kernels  9.08 us (14%)
  local copies, waits for them, and re-layouts  1.86 us (3%)
  between operations  1.42 us (2%)
    ppermute x11, starting transfers between devices, swap_with(): lax.ppermute(x, ('tile', 'pos'), [(i, i ^ mask) for i in range(devices)])  11.7 us
    ppermute x8, starting transfers between devices, from_behind(): return lax.ppermute(block, 'tile', [(source(i), i) for i in range(tiles)])  10.6 us
    ppermute x8, waiting for transfers between devices, from_behind(): return lax.ppermute(block, 'tile', [(source(i), i) for i in range(tiles)])  10.6 us
    pallas_call x13, Pallas kernels, run(): pl.pallas_call(body, out_shape=sum(outs, []), in_specs=sum(specs, []) + [...  7.83 us
    ppermute x11, waiting for transfers between devices, swap_with(): lax.ppermute(x, ('tile', 'pos'), [(i, i ^ mask) for i in range(devices)])  6.18 us
    ppermute x1, waiting for transfers between devices, shards(): other_slice = lax.ppermute(this_slice, 'pos', swap)  4.87 us
    ppermute x1, starting transfers between devices, shards(): other_slice = lax.ppermute(this_slice, 'pos', swap)  1.82 us
    ppermute x1, starting transfers between devices, shards(): got = lax.ppermute(given, 'pos', swap)  1.58 us
  transfers between devices with their start and end apart: 22, of which 11 were waited for; matrix products, arithmetic and copies ran while one was open for 0% of the time, Pallas kernels for 6%

profile of v17, /device:TPU:0, one launch (start us, length us, event | category | flops | bytes accessed | tf_op | source)
XLA Modules:
  0.0 63.6 jit_solution(4090520667998305501)
XLA Ops:
  0.6 1.2 %slice_bitcast_fusion = (bf16[2,256,256]{2,1,0:T(8,128)(2,1)S(1)}, bf16[2,256,256]{2,1,0:T(8,128)(2,1)S(1)}) fusion(bf16[1,2,2,256,256]{4,3,2,1,0:T(8,128)(2,1)} %param.7), kind=kLoop, calls=%fused_computation | loop fusion | bytes 1048576 | tf_op jit(solution)/shard_map/squeeze | solution.py:471
  1.8 0.0 copy-start.1
  1.8 5.1 %collective-permute-start.4 = (bf16[2,256,256]{2,1,0:T(8,128)(2,1)S(1)}, bf16[2,256,256]{2,1,0:T(8,128)(2,1)S(1)}, u32[]{:S(2)}, u32[]{:S(2)}) collective-permute-start(bf16[2,256,256]{2,1,0:T(8,128)(2,1)S(1)} %get-tuple-element.50.refs_4_.refs_2_.refs_0_), channel_id=1, source_target_pairs={{8,0},{10,2},{12,4},{14,6},{16,8},{18,10},{20,12},{22,14},{24,16},... | collective-permute-start | bytes 786440 | tf_op jit(solution)/shard_map/ppermute | solution.py:31
  6.9 0.7 %collective-permute-start.1 = (bf16[2,2,256,256]{3,2,1,0:T(8,128)(2,1)}, bf16[2,2,256,256]{3,2,1,0:T(8,128)(2,1)S(1)}, u32[]{:S(2)}, u32[]{:S(2)}) collective-permute-start(bf16[2,2,256,256]{3,2,1,0:T(8,128)(2,1)} %bitcast.17), channel_id=1, source_target_pairs={{2,0},{4,2},{6,4},{0,6},{10,8},{12,10},{14,12},{8,14},{18,16},{20,... | collective-permute-start | bytes 1572872 | tf_op jit(solution)/shard_map/ppermute | solution.py:31
  8.2 0.0 copy-start.3
  8.3 0.7 %copy-done.3 = s32[1,1,2,2]{3,2,1,0:T(2,128)S(1)} copy-done((s32[1,1,2,2]{3,2,1,0:T(2,128)S(1)}, s32[1,1,2,2]{3,2,1,0:T(2,128)}, u32[]{:S(2)}) %copy-start.3) | copy-done | bytes 40
  8.9 0.6 shard_map.86
  9.5 0.5 collective-permute-start.2
  10.0 3.6 %collective-permute-done.4.refs_4_ = bf16[2,256,256]{2,1,0:T(8,128)(2,1)S(1)} collective-permute-done((bf16[2,256,256]{2,1,0:T(8,128)(2,1)S(1)}, bf16[2,256,256]{2,1,0:T(8,128)(2,1)S(1)}, u32[]{:S(2)}, u32[]{:S(2)}) %collective-permute-start.4) | collective-permute-done | bytes 262176 | tf_op jit(solution)/shard_map/ppermute | solution.py:31
  13.6 0.0 collective-permute-start.5
  13.6 1.5 %collective-permute-start = (bf16[272,256]{1,0:T(8,128)(2,1)S(1)}, bf16[272,256]{1,0:T(8,128)(2,1)S(1)}, u32[]{:S(2)}, u32[]{:S(2)}) collective-permute-start(bf16[272,256]{1,0:T(8,128)(2,1)S(1)} %get-tuple-element.27), channel_id=1, source_target_pairs={{0,1},{1,0},{2,3},{3,2},{4,5},{5,4},{6,7},{7,6},{8,9},{9,8},{10,11... | collective-permute-start | bytes 417800 | tf_op jit(solution)/shard_map/ppermute | solution.py:493
  15.2 2.9 %collective-permute-done.2.refs_4_ = bf16[2,256,256]{2,1,0:T(8,128)(2,1)S(1)} collective-permute-done((bf16[2,256,256]{2,1,0:T(8,128)(2,1)S(1)}, bf16[2,256,256]{2,1,0:T(8,128)(2,1)S(1)}, u32[]{:S(2)}, u32[]{:S(2)}) %collective-permute-start.2) | collective-permute-done | bytes 262176 | tf_op jit(solution)/shard_map/ppermute | solution.py:31
  18.1 0.3 collective-permute-start.3
  18.5 0.1 shard_map.87
  18.6 1.2 %collective-permute-done.refs_1_ = bf16[272,256]{1,0:T(8,128)(2,1)S(1)} collective-permute-done((bf16[272,256]{1,0:T(8,128)(2,1)S(1)}, bf16[272,256]{1,0:T(8,128)(2,1)S(1)}, u32[]{:S(2)}, u32[]{:S(2)}) %collective-permute-start) | collective-permute-done | bytes 139296 | tf_op jit(solution)/shard_map/ppermute | solution.py:493
  19.7 0.0 collective-permute-done.5.refs_5_
  19.7 0.0 collective-permute-done.1.refs_3_
  19.7 1.8 %shard_map.88 = (bf16[2,256,256]{2,1,0:T(8,128)(2,1)S(1)}, f32[2,256,512]{2,1,0:T(8,128)S(1)}) custom-call(bf16[272,256]{1,0:T(8,128)(2,1)S(1)} %get-tuple-element.26.refs_0_, bf16[272,256]{1,0:T(8,128)(2,1)S(1)} %collective-permute-done.refs_1_, bf16[2,256,256]{2,1,0:T(8,128)(2,1)S(1)} %get-tuple-element.50.refs_4_.refs_2_.refs_0_, ...), custom_call_target="tpu_custom_call" | custom-call | flops 1500000000 | bytes 4472832 | tf_op jit(solution)/shard_map/pallas_call | solution.py:289
  21.5 0.8 %collective-permute-done.3.refs_5_ = bf16[2,256,256]{2,1,0:T(8,128)(2,1)S(1)} collective-permute-done((bf16[2,256,256]{2,1,0:T(8,128)(2,1)S(1)}, bf16[2,256,256]{2,1,0:T(8,128)(2,1)S(1)}, u32[]{:S(2)}, u32[]{:S(2)}) %collective-permute-start.3) | collective-permute-done | bytes 262176 | tf_op jit(solution)/shard_map/ppermute | solution.py:31
  22.4 3.8 %shard_map.89 = (bf16[2,256,256]{2,1,0:T(8,128)(2,1)S(1)}, bf16[2,256,256]{2,1,0:T(8,128)(2,1)S(1)}, bf16[256,512]{1,0:T(8,128)(2,1)S(1)}, bf16[128,512]{1,0:T(8,128)(2,1)S(1)}, bf16[128,512]{1,0:T(8,128)(2,1)S(1)}) custom-call(bf16[272,256]{1,0:T(8,128)(2,1)S(1)} %get-tuple-element.26.refs_0_, bf16[272,256]{1,0:T(8,128)(2,1)S(1)} %collective-permute-done.refs_1_, ...), custom_call_target="tpu_custom_call" | custom-call | flops 4000000000 | bytes 6045696 | tf_op jit(solution)/shard_map/pallas_call | solution.py:289
  26.2 1.6 %collective-permute-start.11 = (bf16[2,256,256]{2,1,0:T(8,128)(2,1)S(1)}, bf16[2,256,256]{2,1,0:T(8,128)(2,1)S(1)}, u32[]{:S(2)}, u32[]{:S(2)}) collective-permute-start(bf16[2,256,256]{2,1,0:T(8,128)(2,1)S(1)} %get-tuple-element.41), channel_id=1, source_target_pairs={{0,1},{1,0},{2,3},{3,2},{4,5},{5,4},{6,7},{7,6},{8,9},{9,8},{10,11... | collective-permute-start | bytes 786440 | tf_op jit(solution)/shard_map/ppermute | solution.py:536
  27.8 1.1 %collective-permute-start.6 = (bf16[128,512]{1,0:T(8,128)(2,1)S(1)}, bf16[128,512]{1,0:T(8,128)(2,1)S(1)}, u32[]{:S(2)}, u32[]{:S(2)}) collective-permute-start(bf16[128,512]{1,0:T(8,128)(2,1)S(1)} %get-tuple-element.34), channel_id=1, source_target_pairs={{0,2},{1,3},{2,0},{3,1},{4,6},{5,7},{6,4},{7,5},{8,10},{9,11},{10,... | collective-permute-start | bytes 393224 | tf_op jit(solution)/shard_map/ppermute | solution.py:429
  28.9 1.0 %collective-permute-done.6.refs_1_ = bf16[128,512]{1,0:T(8,128)(2,1)S(1)} collective-permute-done((bf16[128,512]{1,0:T(8,128)(2,1)S(1)}, bf16[128,512]{1,0:T(8,128)(2,1)S(1)}, u32[]{:S(2)}, u32[]{:S(2)}) %collective-permute-start.6) | collective-permute-done | bytes 131104 | tf_op jit(solution)/shard_map/ppermute | solution.py:429
  29.9 0.4 collective-permute-done.7.refs_2_
  30.3 0.1 shard_map.90
  30.4 0.6 collective-permute-start.8
  31.0 0.9 %collective-permute-start.9 = (bf16[64,512]{1,0:T(8,128)(2,1)S(1)}, bf16[64,512]{1,0:T(8,128)(2,1)S(1)}, u32[]{:S(2)}, u32[]{:S(2)}) collective-permute-start(bf16[64,512]{1,0:T(8,128)(2,1)S(1)} %get-tuple-element.38), channel_id=1, source_target_pairs={{0,4},{1,5},{2,6},{3,7},{4,0},{5,1},{6,2},{7,3},{8,12},{9,13},{10,... | collective-permute-start | bytes 196616 | tf_op jit(solution)/shard_map/ppermute | solution.py:429
  31.8 2.1 %collective-permute-start.10 = (bf16[64,512]{1,0:T(8,128)(2,1)S(1)}, bf16[64,512]{1,0:T(8,128)(2,1)S(1)}, u32[]{:S(2)}, u32[]{:S(2)}) collective-permute-start(bf16[64,512]{1,0:T(8,128)(2,1)S(1)} %get-tuple-element.39), channel_id=1, source_target_pairs={{0,5},{1,4},{2,7},{3,6},{4,1},{5,0},{6,3},{7,2},{8,13},{9,12},{10,... | collective-permute-start | bytes 196616 | tf_op jit(solution)/shard_map/ppermute | solution.py:429
  33.9 1.1 %collective-permute-done.11.refs_3_ = bf16[2,256,256]{2,1,0:T(8,128)(2,1)S(1)} collective-permute-done((bf16[2,256,256]{2,1,0:T(8,128)(2,1)S(1)}, bf16[2,256,256]{2,1,0:T(8,128)(2,1)S(1)}, u32[]{:S(2)}, u32[]{:S(2)}) %collective-permute-start.11) | collective-permute-done | bytes 262176 | tf_op jit(solution)/shard_map/ppermute | solution.py:536
  35.1 1.1 %shard_map.91 = (f32[2,256,256]{2,1,0:T(8,128)S(1)}, f32[2,256,256]{2,1,0:T(8,128)S(1)}, bf16[2,256,256]{2,1,0:T(8,128)(2,1)S(1)}, bf16[2,256,256]{2,1,0:T(8,128)(2,1)S(1)}) custom-call(bf16[272,256]{1,0:T(8,128)(2,1)S(1)} %get-tuple-element.26.refs_0_, bf16[272,256]{1,0:T(8,128)(2,1)S(1)} %collective-permute-done.refs_1_, ...), custom_call_target="tpu_custom_call" | custom-call | bytes 2375680 | tf_op jit(solution)/shard_map/pallas_call | solution.py:289
  36.1 1.6 %collective-permute-start.15 = (bf16[2,256,256]{2,1,0:T(8,128)(2,1)S(1)}, bf16[2,256,256]{2,1,0:T(8,128)(2,1)S(1)}, u32[]{:S(2)}, u32[]{:S(2)}) collective-permute-start(bf16[2,256,256]{2,1,0:T(8,128)(2,1)S(1)} %get-tuple-element.45), channel_id=1, source_target_pairs={{6,0},{0,2},{2,4},{4,6},{14,8},{8,10},{10,12},{12,14},{22,16},{16,... | collective-permute-start | bytes 786440 | tf_op jit(solution)/shard_map/ppermute | solution.py:31
  37.8 0.4 collective-permute-start.14
  38.2 0.6 %collective-permute-start.12 = (bf16[64,512]{1,0:T(8,128)(2,1)S(1)}, bf16[64,512]{1,0:T(8,128)(2,1)S(1)}, u32[]{:S(2)}, u32[]{:S(2)}) collective-permute-start(bf16[64,512]{1,0:T(8,128)(2,1)S(1)} %shard_map.92.refs_0_), channel_id=1, source_target_pairs={{0,8},{1,9},{2,10},{3,11},{4,12},{5,13},{6,14},{7,15},{8,0},{9,1},... | collective-permute-start | bytes 196616 | tf_op jit(solution)/shard_map/ppermute | solution.py:429
  38.9 4.1 %collective-permute-done.12.refs_1_ = bf16[64,512]{1,0:T(8,128)(2,1)S(1)} collective-permute-done((bf16[64,512]{1,0:T(8,128)(2,1)S(1)}, bf16[64,512]{1,0:T(8,128)(2,1)S(1)}, u32[]{:S(2)}, u32[]{:S(2)}) %collective-permute-start.12) | collective-permute-done | bytes 65568 | tf_op jit(solution)/shard_map/ppermute | solution.py:429
  43.0 2.7 %collective-permute-start.13 = (bf16[64,512]{1,0:T(8,128)(2,1)S(1)}, bf16[64,512]{1,0:T(8,128)(2,1)S(1)}, u32[]{:S(2)}, u32[]{:S(2)}) collective-permute-start(bf16[64,512]{1,0:T(8,128)(2,1)S(1)} %shard_map.93.refs_4_.refs_0_), channel_id=1, source_target_pairs={{0,16},{1,17},{2,18},{3,19},{4,20},{5,21},{6,22},{7,23},{8,24},{9,... | collective-permute-start | bytes 196616 | tf_op jit(solution)/shard_map/ppermute | solution.py:429
  45.7 0.1 shard_map.94
  45.8 2.0 %collective-permute-start.19 = (bf16[2,256,256]{2,1,0:T(8,128)(2,1)S(1)}, bf16[2,256,256]{2,1,0:T(8,128)(2,1)S(1)}, u32[]{:S(2)}, u32[]{:S(2)}) collective-permute-start(bf16[2,256,256]{2,1,0:T(8,128)(2,1)S(1)} %get-tuple-element.46.refs_2_), channel_id=1, source_target_pairs={{24,0},{26,2},{28,4},{30,6},{0,8},{2,10},{4,12},{6,14},{8,16},{10,... | collective-permute-start | bytes 786440 | tf_op jit(solution)/shard_map/ppermute | solution.py:31
  47.8 0.8 %collective-permute-done.13.refs_1_ = bf16[64,512]{1,0:T(8,128)(2,1)S(1)} collective-permute-done((bf16[64,512]{1,0:T(8,128)(2,1)S(1)}, bf16[64,512]{1,0:T(8,128)(2,1)S(1)}, u32[]{:S(2)}, u32[]{:S(2)}) %collective-permute-start.13) | collective-permute-done | bytes 65568 | tf_op jit(solution)/shard_map/ppermute | solution.py:429
  48.5 2.2 %collective-permute-start.18 = (bf16[64,512]{1,0:T(8,128)(2,1)S(1)}, bf16[64,512]{1,0:T(8,128)(2,1)S(1)}, u32[]{:S(2)}, u32[]{:S(2)}) collective-permute-start(bf16[64,512]{1,0:T(8,128)(2,1)S(1)} %shard_map.95.refs_4_.refs_0_), channel_id=1, source_target_pairs={{0,5},{1,4},{2,7},{3,6},{4,1},{5,0},{6,3},{7,2},{8,13},{9,12},{10,... | collective-permute-start | bytes 196616 | tf_op jit(solution)/shard_map/ppermute | solution.py:429
  50.7 1.1 %collective-permute-start.17 = (bf16[64,512]{1,0:T(8,128)(2,1)S(1)}, bf16[64,512]{1,0:T(8,128)(2,1)S(1)}, u32[]{:S(2)}, u32[]{:S(2)}) collective-permute-start(bf16[64,512]{1,0:T(8,128)(2,1)S(1)} %shard_map.95.refs_4_.refs_0_), channel_id=1, source_target_pairs={{0,4},{1,5},{2,6},{3,7},{4,0},{5,1},{6,2},{7,3},{8,12},{9,13},{10,... | collective-permute-start | bytes 196616 | tf_op jit(solution)/shard_map/ppermute | solution.py:429
  51.8 0.3 collective-permute-start.16
  52.1 3.2 %collective-permute-done.19.refs_3_ = bf16[2,256,256]{2,1,0:T(8,128)(2,1)S(1)} collective-permute-done((bf16[2,256,256]{2,1,0:T(8,128)(2,1)S(1)}, bf16[2,256,256]{2,1,0:T(8,128)(2,1)S(1)}, u32[]{:S(2)}, u32[]{:S(2)}) %collective-permute-start.19) | collective-permute-done | bytes 262176 | tf_op jit(solution)/shard_map/ppermute | solution.py:31
  55.3 0.1 shard_map.96.refs_4_.refs_3_
  55.5 1.8 %collective-permute-start.21 = (bf16[2,256,256]{2,1,0:T(8,128)(2,1)S(1)}, bf16[2,256,256]{2,1,0:T(8,128)(2,1)S(1)}, u32[]{:S(2)}, u32[]{:S(2)}) collective-permute-start(bf16[2,256,256]{2,1,0:T(8,128)(2,1)S(1)} %shard_map.96.refs_4_.refs_3_), channel_id=1, source_target_pairs={{0,1},{1,0},{2,3},{3,2},{4,5},{5,4},{6,7},{7,6},{8,9},{9,8},{10,11... | collective-permute-start | bytes 786440 | tf_op jit(solution)/shard_map/ppermute | solution.py:572
  57.3 0.1 shard_map.97.refs_0_
  57.4 0.1 collective-permute-start.20
  57.4 4.9 %collective-permute-done.21.refs_1_.refs_4_ = bf16[2,256,256]{2,1,0:T(8,128)(2,1)S(1)} collective-permute-done((bf16[2,256,256]{2,1,0:T(8,128)(2,1)S(1)}, bf16[2,256,256]{2,1,0:T(8,128)(2,1)S(1)}, u32[]{:S(2)}, u32[]{:S(2)}) %collective-permute-start.21) | collective-permute-done | bytes 262176 | tf_op jit(solution)/shard_map/ppermute | solution.py:572
  62.3 1.3 %shard_map.99 = (f32[2048,128]{1,0:T(8,128)}, bf16[1,2,2,256,256]{4,3,2,1,0:T(8,128)(2,1)}) custom-call(bf16[256,512]{1,0:T(8,128)(2,1)S(1)} %shard_map.97.refs_0_, bf16[256,512]{1,0:T(8,128)(2,1)S(1)} %collective-permute-done.20.refs_1_, f32[2048,128]{1,0:T(8,128)S(1)} %bitcast.16, bf16[2,256,256]{2,1,0:T(8,128)(2,1)S(1)} %shard_map.96.refs_4_.refs_3_, ...), custom_call_target="tpu_custom_call" | custom-call | flops 1048576 | bytes 3145728 | tf_op jit(solution)/shard_map/pallas_call | solution.py:320
  (21 shorter events, 0.1 us)
Async XLA Ops:
  0.6 7.6 %copy-start.2 = (bf16[1,1,2,256,256]{4,3,2,1,0:T(8,128)(2,1)S(1)}, bf16[1,1,2,256,256]{4,3,2,1,0:T(8,128)(2,1)}, u32[]{:S(2)}) copy-start(bf16[1,1,2,256,256]{4,3,2,1,0:T(8,128)(2,1)} %refs_3_.1) | copy-start | bytes 786436
  0.6 17.8 %copy-start = (f32[2,256,2,256]{3,2,1,0:T(2,128)S(1)}, f32[2,256,2,256]{3,2,1,0:T(2,128)}, u32[]{:S(2)}) copy-start(f32[2,256,2,256]{3,2,1,0:T(2,128)} %param.8) | copy-start | bytes 3145732
  1.8 16.7 %copy-start.1 = (bf16[512,512]{1,0:T(8,128)(2,1)S(1)}, bf16[512,512]{1,0:T(8,128)(2,1)}, u32[]{:S(2)}) copy-start(bf16[512,512]{1,0:T(8,128)(2,1)} %constant.10.refs_1_) | copy-start | bytes 1572868
  1.8 11.8 %collective-permute-start.4 = (bf16[2,256,256]{2,1,0:T(8,128)(2,1)S(1)}, bf16[2,256,256]{2,1,0:T(8,128)(2,1)S(1)}, u32[]{:S(2)}, u32[]{:S(2)}) collective-permute-start(bf16[2,256,256]{2,1,0:T(8,128)(2,1)S(1)} %get-tuple-element.50.refs_4_.refs_2_.refs_0_), channel_id=1, source_target_pairs={{8,0},{10,2},{12,4},{14,6},{16,8},{18,10},{20,12},{22,14},{24,16},... | collective-permute-start | bytes 786440 | tf_op jit(solution)/shard_map/ppermute | solution.py:31
  6.9 12.8 %collective-permute-start.1 = (bf16[2,2,256,256]{3,2,1,0:T(8,128)(2,1)}, bf16[2,2,256,256]{3,2,1,0:T(8,128)(2,1)S(1)}, u32[]{:S(2)}, u32[]{:S(2)}) collective-permute-start(bf16[2,2,256,256]{3,2,1,0:T(8,128)(2,1)} %bitcast.17), channel_id=1, source_target_pairs={{2,0},{4,2},{6,4},{0,6},{10,8},{12,10},{14,12},{8,14},{18,16},{20,... | collective-permute-start | bytes 1572872 | tf_op jit(solution)/shard_map/ppermute | solution.py:31
  8.2 0.7 %copy-start.3 = (s32[1,1,2,2]{3,2,1,0:T(2,128)S(1)}, s32[1,1,2,2]{3,2,1,0:T(2,128)}, u32[]{:S(2)}) copy-start(s32[1,1,2,2]{3,2,1,0:T(2,128)} %refs_0_.1) | copy-start | bytes 52
  9.5 8.6 %collective-permute-start.2 = (bf16[2,256,256]{2,1,0:T(8,128)(2,1)S(1)}, bf16[2,256,256]{2,1,0:T(8,128)(2,1)S(1)}, u32[]{:S(2)}, u32[]{:S(2)}) collective-permute-start(bf16[2,256,256]{2,1,0:T(8,128)(2,1)S(1)} %get-tuple-element.28.refs_2_.refs_1_), channel_id=1, source_target_pairs={{8,0},{10,2},{12,4},{14,6},{16,8},{18,10},{20,12},{22,14},{24,16},... | collective-permute-start | bytes 786440 | tf_op jit(solution)/shard_map/ppermute | solution.py:31
  13.6 6.1 %collective-permute-start.5 = (bf16[2,256,256]{2,1,0:T(8,128)(2,1)S(1)}, bf16[2,256,256]{2,1,0:T(8,128)(2,1)S(1)}, u32[]{:S(2)}, u32[]{:S(2)}) collective-permute-start(bf16[2,256,256]{2,1,0:T(8,128)(2,1)S(1)} %collective-permute-done.4.refs_4_), channel_id=1, source_target_pairs={{2,0},{4,2},{6,4},{0,6},{10,8},{12,10},{14,12},{8,14},{18,16},{20,... | collective-permute-start | bytes 786440 | tf_op jit(solution)/shard_map/ppermute | solution.py:31
  13.6 6.1 %collective-permute-start = (bf16[272,256]{1,0:T(8,128)(2,1)S(1)}, bf16[272,256]{1,0:T(8,128)(2,1)S(1)}, u32[]{:S(2)}, u32[]{:S(2)}) collective-permute-start(bf16[272,256]{1,0:T(8,128)(2,1)S(1)} %get-tuple-element.27), channel_id=1, source_target_pairs={{0,1},{1,0},{2,3},{3,2},{4,5},{5,4},{6,7},{7,6},{8,9},{9,8},{10,11... | collective-permute-start | bytes 417800 | tf_op jit(solution)/shard_map/ppermute | solution.py:493
  18.1 4.2 %collective-permute-start.3 = (bf16[2,256,256]{2,1,0:T(8,128)(2,1)S(1)}, bf16[2,256,256]{2,1,0:T(8,128)(2,1)S(1)}, u32[]{:S(2)}, u32[]{:S(2)}) collective-permute-start(bf16[2,256,256]{2,1,0:T(8,128)(2,1)S(1)} %collective-permute-done.2.refs_4_), channel_id=1, source_target_pairs={{2,0},{4,2},{6,4},{0,6},{10,8},{12,10},{14,12},{8,14},{18,16},{20,... | collective-permute-start | bytes 786440 | tf_op jit(solution)/shard_map/ppermute | solution.py:31
  19.7 2.6 %copy-start.4 = (bf16[512,512]{1,0:T(8,128)(2,1)S(1)}, bf16[512,512]{1,0:T(8,128)(2,1)}, u32[]{:S(2)}) copy-start(bf16[512,512]{1,0:T(8,128)(2,1)} %constant.11.refs_10_) | copy-start | bytes 1572868
  26.2 8.9 %collective-permute-start.11 = (bf16[2,256,256]{2,1,0:T(8,128)(2,1)S(1)}, bf16[2,256,256]{2,1,0:T(8,128)(2,1)S(1)}, u32[]{:S(2)}, u32[]{:S(2)}) collective-permute-start(bf16[2,256,256]{2,1,0:T(8,128)(2,1)S(1)} %get-tuple-element.41), channel_id=1, source_target_pairs={{0,1},{1,0},{2,3},{3,2},{4,5},{5,4},{6,7},{7,6},{8,9},{9,8},{10,11... | collective-permute-start | bytes 786440 | tf_op jit(solution)/shard_map/ppermute | solution.py:536
  27.8 2.1 %collective-permute-start.6 = (bf16[128,512]{1,0:T(8,128)(2,1)S(1)}, bf16[128,512]{1,0:T(8,128)(2,1)S(1)}, u32[]{:S(2)}, u32[]{:S(2)}) collective-permute-start(bf16[128,512]{1,0:T(8,128)(2,1)S(1)} %get-tuple-element.34), channel_id=1, source_target_pairs={{0,2},{1,3},{2,0},{3,1},{4,6},{5,7},{6,4},{7,5},{8,10},{9,11},{10,... | collective-permute-start | bytes 393224 | tf_op jit(solution)/shard_map/ppermute | solution.py:429
  28.9 1.3 %collective-permute-start.7 = (bf16[128,512]{1,0:T(8,128)(2,1)S(1)}, bf16[128,512]{1,0:T(8,128)(2,1)S(1)}, u32[]{:S(2)}, u32[]{:S(2)}) collective-permute-start(bf16[128,512]{1,0:T(8,128)(2,1)S(1)} %get-tuple-element.35), channel_id=1, source_target_pairs={{0,2},{1,3},{2,0},{3,1},{4,6},{5,7},{6,4},{7,5},{8,10},{9,11},{10,... | collective-permute-start | bytes 393224 | tf_op jit(solution)/shard_map/ppermute | solution.py:429
  30.4 7.8 %collective-permute-start.8 = (bf16[64,512]{1,0:T(8,128)(2,1)S(1)}, bf16[64,512]{1,0:T(8,128)(2,1)S(1)}, u32[]{:S(2)}, u32[]{:S(2)}) collective-permute-start(bf16[64,512]{1,0:T(8,128)(2,1)S(1)} %get-tuple-element.37), channel_id=1, source_target_pairs={{0,1},{1,0},{2,3},{3,2},{4,5},{5,4},{6,7},{7,6},{8,9},{9,8},{10,11... | collective-permute-start | bytes 196616 | tf_op jit(solution)/shard_map/ppermute | solution.py:429
  31.0 7.2 %collective-permute-start.9 = (bf16[64,512]{1,0:T(8,128)(2,1)S(1)}, bf16[64,512]{1,0:T(8,128)(2,1)S(1)}, u32[]{:S(2)}, u32[]{:S(2)}) collective-permute-start(bf16[64,512]{1,0:T(8,128)(2,1)S(1)} %get-tuple-element.38), channel_id=1, source_target_pairs={{0,4},{1,5},{2,6},{3,7},{4,0},{5,1},{6,2},{7,3},{8,12},{9,13},{10,... | collective-permute-start | bytes 196616 | tf_op jit(solution)/shard_map/ppermute | solution.py:429
  31.8 6.3 %collective-permute-start.10 = (bf16[64,512]{1,0:T(8,128)(2,1)S(1)}, bf16[64,512]{1,0:T(8,128)(2,1)S(1)}, u32[]{:S(2)}, u32[]{:S(2)}) collective-permute-start(bf16[64,512]{1,0:T(8,128)(2,1)S(1)} %get-tuple-element.39), channel_id=1, source_target_pairs={{0,5},{1,4},{2,7},{3,6},{4,1},{5,0},{6,3},{7,2},{8,13},{9,12},{10,... | collective-permute-start | bytes 196616 | tf_op jit(solution)/shard_map/ppermute | solution.py:429
  36.1 9.5 %collective-permute-start.15 = (bf16[2,256,256]{2,1,0:T(8,128)(2,1)S(1)}, bf16[2,256,256]{2,1,0:T(8,128)(2,1)S(1)}, u32[]{:S(2)}, u32[]{:S(2)}) collective-permute-start(bf16[2,256,256]{2,1,0:T(8,128)(2,1)S(1)} %get-tuple-element.45), channel_id=1, source_target_pairs={{6,0},{0,2},{2,4},{4,6},{14,8},{8,10},{10,12},{12,14},{22,16},{16,... | collective-permute-start | bytes 786440 | tf_op jit(solution)/shard_map/ppermute | solution.py:31
  37.8 7.9 %collective-permute-start.14 = (bf16[2,256,256]{2,1,0:T(8,128)(2,1)S(1)}, bf16[2,256,256]{2,1,0:T(8,128)(2,1)S(1)}, u32[]{:S(2)}, u32[]{:S(2)}) collective-permute-start(bf16[2,256,256]{2,1,0:T(8,128)(2,1)S(1)} %get-tuple-element.42.refs_4_), channel_id=1, source_target_pairs={{6,0},{0,2},{2,4},{4,6},{14,8},{8,10},{10,12},{12,14},{22,16},{16,... | collective-permute-start | bytes 786440 | tf_op jit(solution)/shard_map/ppermute | solution.py:31
  38.2 4.7 %collective-permute-start.12 = (bf16[64,512]{1,0:T(8,128)(2,1)S(1)}, bf16[64,512]{1,0:T(8,128)(2,1)S(1)}, u32[]{:S(2)}, u32[]{:S(2)}) collective-permute-start(bf16[64,512]{1,0:T(8,128)(2,1)S(1)} %shard_map.92.refs_0_), channel_id=1, source_target_pairs={{0,8},{1,9},{2,10},{3,11},{4,12},{5,13},{6,14},{7,15},{8,0},{9,1},... | collective-permute-start | bytes 196616 | tf_op jit(solution)/shard_map/ppermute | solution.py:429
  43.0 5.5 %collective-permute-start.13 = (bf16[64,512]{1,0:T(8,128)(2,1)S(1)}, bf16[64,512]{1,0:T(8,128)(2,1)S(1)}, u32[]{:S(2)}, u32[]{:S(2)}) collective-permute-start(bf16[64,512]{1,0:T(8,128)(2,1)S(1)} %shard_map.93.refs_4_.refs_0_), channel_id=1, source_target_pairs={{0,16},{1,17},{2,18},{3,19},{4,20},{5,21},{6,22},{7,23},{8,24},{9,... | collective-permute-start | bytes 196616 | tf_op jit(solution)/shard_map/ppermute | solution.py:429
  45.8 9.5 %collective-permute-start.19 = (bf16[2,256,256]{2,1,0:T(8,128)(2,1)S(1)}, bf16[2,256,256]{2,1,0:T(8,128)(2,1)S(1)}, u32[]{:S(2)}, u32[]{:S(2)}) collective-permute-start(bf16[2,256,256]{2,1,0:T(8,128)(2,1)S(1)} %get-tuple-element.46.refs_2_), channel_id=1, source_target_pairs={{24,0},{26,2},{28,4},{30,6},{0,8},{2,10},{4,12},{6,14},{8,16},{10,... | collective-permute-start | bytes 786440 | tf_op jit(solution)/shard_map/ppermute | solution.py:31
  48.5 8.7 %collective-permute-start.18 = (bf16[64,512]{1,0:T(8,128)(2,1)S(1)}, bf16[64,512]{1,0:T(8,128)(2,1)S(1)}, u32[]{:S(2)}, u32[]{:S(2)}) collective-permute-start(bf16[64,512]{1,0:T(8,128)(2,1)S(1)} %shard_map.95.refs_4_.refs_0_), channel_id=1, source_target_pairs={{0,5},{1,4},{2,7},{3,6},{4,1},{5,0},{6,3},{7,2},{8,13},{9,12},{10,... | collective-permute-start | bytes 196616 | tf_op jit(solution)/shard_map/ppermute | solution.py:429
  50.7 6.6 %collective-permute-start.17 = (bf16[64,512]{1,0:T(8,128)(2,1)S(1)}, bf16[64,512]{1,0:T(8,128)(2,1)S(1)}, u32[]{:S(2)}, u32[]{:S(2)}) collective-permute-start(bf16[64,512]{1,0:T(8,128)(2,1)S(1)} %shard_map.95.refs_4_.refs_0_), channel_id=1, source_target_pairs={{0,4},{1,5},{2,6},{3,7},{4,0},{5,1},{6,2},{7,3},{8,12},{9,13},{10,... | collective-permute-start | bytes 196616 | tf_op jit(solution)/shard_map/ppermute | solution.py:429
  51.8 5.5 %collective-permute-start.16 = (bf16[64,512]{1,0:T(8,128)(2,1)S(1)}, bf16[64,512]{1,0:T(8,128)(2,1)S(1)}, u32[]{:S(2)}, u32[]{:S(2)}) collective-permute-start(bf16[64,512]{1,0:T(8,128)(2,1)S(1)} %shard_map.95.refs_4_.refs_0_), channel_id=1, source_target_pairs={{0,1},{1,0},{2,3},{3,2},{4,5},{5,4},{6,7},{7,6},{8,9},{9,8},{10,11... | collective-permute-start | bytes 196616 | tf_op jit(solution)/shard_map/ppermute | solution.py:429
  55.5 6.9 %collective-permute-start.21 = (bf16[2,256,256]{2,1,0:T(8,128)(2,1)S(1)}, bf16[2,256,256]{2,1,0:T(8,128)(2,1)S(1)}, u32[]{:S(2)}, u32[]{:S(2)}) collective-permute-start(bf16[2,256,256]{2,1,0:T(8,128)(2,1)S(1)} %shard_map.96.refs_4_.refs_3_), channel_id=1, source_target_pairs={{0,1},{1,0},{2,3},{3,2},{4,5},{5,4},{6,7},{7,6},{8,9},{9,8},{10,11... | collective-permute-start | bytes 786440 | tf_op jit(solution)/shard_map/ppermute | solution.py:572
  57.4 5.0 %collective-permute-start.20 = (bf16[256,512]{1,0:T(8,128)(2,1)S(1)}, bf16[256,512]{1,0:T(8,128)(2,1)S(1)}, u32[]{:S(2)}, u32[]{:S(2)}) collective-permute-start(bf16[256,512]{1,0:T(8,128)(2,1)S(1)} %shard_map.97.refs_0_), channel_id=1, source_target_pairs={{0,2},{1,3},{2,0},{3,1},{4,6},{5,7},{6,4},{7,5},{8,10},{9,11},{10,... | collective-permute-start | bytes 786440 | tf_op jit(solution)/shard_map/ppermute | solution.py:429

commit v18 on v17

--- a/solution.py
+++ b/solution.py
@@ -15,7 +15,7 @@
 object_rate = 0.05
 probe_rate = 0.15
 
-LATE = [work * 1_000_000_000 for work in (0, 8, 0, 0, 8, 0, 8, 4)]
+LATE = [work * 1_000_000_000 for work in (0, 8, 0, 0, 0, 0, 8, 4)]
 
 f32 = jnp.float32
 bf16 = jnp.bfloat16

time: 63.8 us -> 72.2 us (1.13)
  waiting for transfers between devices: 24 us -> 33.1 us
    ppermute x11, waiting for transfers between devices: 6.18 us -> 17 us  [swap_with(): lax.ppermute(x, ('tile', 'pos'), [(i, i ^ mask) for i in range(devices)])]
    ppermute x8, starting transfers between devices: 10.6 us -> 8.7 us  [from_behind(): return lax.ppermute(block, 'tile', [(source(i), i) for i in range(tiles)])]
    ppermute x11, starting transfers between devices: 11.7 us -> 13 us  [swap_with(): lax.ppermute(x, ('tile', 'pos'), [(i, i ^ mask) for i in range(devices)])]
    ppermute x8, waiting for transfers between devices: 10.6 us -> 9.61 us  [from_behind(): return lax.ppermute(block, 'tile', [(source(i), i) for i in range(tiles)])]
  transfers between devices with their start and end apart: 22 -> 22, of which waited for: 11 -> 14; matrix products, arithmetic and copies ran while one was open for 0% -> 0% of each run, Pallas kernels for 6% -> 5%
where the time goes in v18:
time: 72.2 us; the launch traced here: 72.1 us
  waiting for transfers between devices  33.1 us (46%)
  starting transfers between devices  26.6 us (37%)
  Pallas kernels  9.08 us (13%)
  local copies, waits for them, and re-layouts  1.86 us (3%)
  between operations  1.43 us (2%)
    ppermute x11, waiting for transfers between devices, swap_with(): lax.ppermute(x, ('tile', 'pos'), [(i, i ^ mask) for i in range(devices)])  17 us
    ppermute x11, starting transfers between devices, swap_with(): lax.ppermute(x, ('tile', 'pos'), [(i, i ^ mask) for i in range(devices)])  13 us
    ppermute x8, waiting for transfers between devices, from_behind(): return lax.ppermute(block, 'tile', [(source(i), i) for i in range(tiles)])  9.61 us
    ppermute x8, starting transfers between devices, from_behind(): return lax.ppermute(block, 'tile', [(source(i), i) for i in range(tiles)])  8.7 us
    pallas_call x13, Pallas kernels, run(): pl.pallas_call(body, out_shape=sum(outs, []), in_specs=sum(specs, []) + [...  7.82 us
    ppermute x1, waiting for transfers between devices, shards(): other_slice = lax.ppermute(this_slice, 'pos', swap)  4.19 us
    ppermute x1, starting transfers between devices, shards(): other_slice = lax.ppermute(this_slice, 'pos', swap)  1.82 us
    ppermute x1, starting transfers between devices, shards(): got = lax.ppermute(given, 'pos', swap)  1.58 us
  transfers between devices with their start and end apart: 22, of which 14 were waited for; matrix products, arithmetic and copies ran while one was open for 0% of the time, Pallas kernels for 5%

profile of v18, /device:TPU:0, one launch (start us, length us, event | category | flops | bytes accessed | tf_op | source)
XLA Modules:
  0.0 72.1 jit_solution(2491588269759418703)
XLA Ops:
  0.6 1.2 %slice_bitcast_fusion = (bf16[2,256,256]{2,1,0:T(8,128)(2,1)S(1)}, bf16[2,256,256]{2,1,0:T(8,128)(2,1)S(1)}) fusion(bf16[1,2,2,256,256]{4,3,2,1,0:T(8,128)(2,1)} %param.7), kind=kLoop, calls=%fused_computation | loop fusion | bytes 1048576 | tf_op jit(solution)/shard_map/squeeze | solution.py:471
  1.8 0.0 copy-start.1
  1.8 5.1 %collective-permute-start.4 = (bf16[2,256,256]{2,1,0:T(8,128)(2,1)S(1)}, bf16[2,256,256]{2,1,0:T(8,128)(2,1)S(1)}, u32[]{:S(2)}, u32[]{:S(2)}) collective-permute-start(bf16[2,256,256]{2,1,0:T(8,128)(2,1)S(1)} %get-tuple-element.50.refs_4_.refs_2_.refs_0_), channel_id=1, source_target_pairs={{8,0},{10,2},{12,4},{14,6},{16,8},{18,10},{20,12},{22,14},{24,16},... | collective-permute-start | bytes 786440 | tf_op jit(solution)/shard_map/ppermute | solution.py:31
  6.9 0.7 collective-permute-start.1
  8.2 0.0 copy-start.3
  8.3 0.7 copy-done.3
  8.9 0.6 shard_map.86
  9.5 0.5 collective-permute-start.2
  10.0 3.6 %collective-permute-done.4.refs_4_ = bf16[2,256,256]{2,1,0:T(8,128)(2,1)S(1)} collective-permute-done((bf16[2,256,256]{2,1,0:T(8,128)(2,1)S(1)}, bf16[2,256,256]{2,1,0:T(8,128)(2,1)S(1)}, u32[]{:S(2)}, u32[]{:S(2)}) %collective-permute-start.4) | collective-permute-done | bytes 262176 | tf_op jit(solution)/shard_map/ppermute | solution.py:31
  13.6 1.5 %collective-permute-start = (bf16[272,256]{1,0:T(8,128)(2,1)S(1)}, bf16[272,256]{1,0:T(8,128)(2,1)S(1)}, u32[]{:S(2)}, u32[]{:S(2)}) collective-permute-start(bf16[272,256]{1,0:T(8,128)(2,1)S(1)} %get-tuple-element.27), channel_id=1, source_target_pairs={{0,1},{1,0},{2,3},{3,2},{4,5},{5,4},{6,7},{7,6},{8,9},{9,8},{10,11... | collective-permute-start | bytes 417800 | tf_op jit(solution)/shard_map/ppermute | solution.py:493
  15.2 2.9 %collective-permute-done.2.refs_4_ = bf16[2,256,256]{2,1,0:T(8,128)(2,1)S(1)} collective-permute-done((bf16[2,256,256]{2,1,0:T(8,128)(2,1)S(1)}, bf16[2,256,256]{2,1,0:T(8,128)(2,1)S(1)}, u32[]{:S(2)}, u32[]{:S(2)}) %collective-permute-start.2) | collective-permute-done | bytes 262176 | tf_op jit(solution)/shard_map/ppermute | solution.py:31
  18.1 0.3 collective-permute-start.3
  18.5 0.1 shard_map.87
  18.6 1.2 %collective-permute-done.refs_1_ = bf16[272,256]{1,0:T(8,128)(2,1)S(1)} collective-permute-done((bf16[272,256]{1,0:T(8,128)(2,1)S(1)}, bf16[272,256]{1,0:T(8,128)(2,1)S(1)}, u32[]{:S(2)}, u32[]{:S(2)}) %collective-permute-start) | collective-permute-done | bytes 139296 | tf_op jit(solution)/shard_map/ppermute | solution.py:493
  19.7 1.8 %shard_map.88 = (bf16[2,256,256]{2,1,0:T(8,128)(2,1)S(1)}, f32[2,256,512]{2,1,0:T(8,128)S(1)}) custom-call(bf16[272,256]{1,0:T(8,128)(2,1)S(1)} %get-tuple-element.26.refs_0_, bf16[272,256]{1,0:T(8,128)(2,1)S(1)} %collective-permute-done.refs_1_, bf16[2,256,256]{2,1,0:T(8,128)(2,1)S(1)} %get-tuple-element.50.refs_4_.refs_2_.refs_0_, ...), custom_call_target="tpu_custom_call" | custom-call | flops 1500000000 | bytes 4472832 | tf_op jit(solution)/shard_map/pallas_call | solution.py:289
  21.5 0.8 %collective-permute-done.3.refs_5_ = bf16[2,256,256]{2,1,0:T(8,128)(2,1)S(1)} collective-permute-done((bf16[2,256,256]{2,1,0:T(8,128)(2,1)S(1)}, bf16[2,256,256]{2,1,0:T(8,128)(2,1)S(1)}, u32[]{:S(2)}, u32[]{:S(2)}) %collective-permute-start.3) | collective-permute-done | bytes 262176 | tf_op jit(solution)/shard_map/ppermute | solution.py:31
  22.4 3.8 %shard_map.89 = (bf16[2,256,256]{2,1,0:T(8,128)(2,1)S(1)}, bf16[2,256,256]{2,1,0:T(8,128)(2,1)S(1)}, bf16[256,512]{1,0:T(8,128)(2,1)S(1)}, bf16[128,512]{1,0:T(8,128)(2,1)S(1)}, bf16[128,512]{1,0:T(8,128)(2,1)S(1)}) custom-call(bf16[272,256]{1,0:T(8,128)(2,1)S(1)} %get-tuple-element.26.refs_0_, bf16[272,256]{1,0:T(8,128)(2,1)S(1)} %collective-permute-done.refs_1_, ...), custom_call_target="tpu_custom_call" | custom-call | flops 4000000000 | bytes 6045696 | tf_op jit(solution)/shard_map/pallas_call | solution.py:289
  26.2 1.6 %collective-permute-start.11 = (bf16[2,256,256]{2,1,0:T(8,128)(2,1)S(1)}, bf16[2,256,256]{2,1,0:T(8,128)(2,1)S(1)}, u32[]{:S(2)}, u32[]{:S(2)}) collective-permute-start(bf16[2,256,256]{2,1,0:T(8,128)(2,1)S(1)} %get-tuple-element.41), channel_id=1, source_target_pairs={{0,1},{1,0},{2,3},{3,2},{4,5},{5,4},{6,7},{7,6},{8,9},{9,8},{10,11... | collective-permute-start | bytes 786440 | tf_op jit(solution)/shard_map/ppermute | solution.py:536
  27.8 1.1 %collective-permute-start.6 = (bf16[128,512]{1,0:T(8,128)(2,1)S(1)}, bf16[128,512]{1,0:T(8,128)(2,1)S(1)}, u32[]{:S(2)}, u32[]{:S(2)}) collective-permute-start(bf16[128,512]{1,0:T(8,128)(2,1)S(1)} %get-tuple-element.34), channel_id=1, source_target_pairs={{0,2},{1,3},{2,0},{3,1},{4,6},{5,7},{6,4},{7,5},{8,10},{9,11},{10,... | collective-permute-start | bytes 393224 | tf_op jit(solution)/shard_map/ppermute | solution.py:429
  28.9 1.0 %collective-permute-done.6.refs_1_ = bf16[128,512]{1,0:T(8,128)(2,1)S(1)} collective-permute-done((bf16[128,512]{1,0:T(8,128)(2,1)S(1)}, bf16[128,512]{1,0:T(8,128)(2,1)S(1)}, u32[]{:S(2)}, u32[]{:S(2)}) %collective-permute-start.6) | collective-permute-done | bytes 131104 | tf_op jit(solution)/shard_map/ppermute | solution.py:429
  29.9 0.4 collective-permute-done.7.refs_2_
  30.3 0.1 shard_map.90
  30.4 0.6 collective-permute-start.8
  31.0 0.9 %collective-permute-start.9 = (bf16[64,512]{1,0:T(8,128)(2,1)S(1)}, bf16[64,512]{1,0:T(8,128)(2,1)S(1)}, u32[]{:S(2)}, u32[]{:S(2)}) collective-permute-start(bf16[64,512]{1,0:T(8,128)(2,1)S(1)} %get-tuple-element.38), channel_id=1, source_target_pairs={{0,4},{1,5},{2,6},{3,7},{4,0},{5,1},{6,2},{7,3},{8,12},{9,13},{10,... | collective-permute-start | bytes 196616 | tf_op jit(solution)/shard_map/ppermute | solution.py:429
  31.8 2.1 %collective-permute-start.10 = (bf16[64,512]{1,0:T(8,128)(2,1)S(1)}, bf16[64,512]{1,0:T(8,128)(2,1)S(1)}, u32[]{:S(2)}, u32[]{:S(2)}) collective-permute-start(bf16[64,512]{1,0:T(8,128)(2,1)S(1)} %get-tuple-element.39), channel_id=1, source_target_pairs={{0,5},{1,4},{2,7},{3,6},{4,1},{5,0},{6,3},{7,2},{8,13},{9,12},{10,... | collective-permute-start | bytes 196616 | tf_op jit(solution)/shard_map/ppermute | solution.py:429
  33.9 1.1 %collective-permute-done.11.refs_3_ = bf16[2,256,256]{2,1,0:T(8,128)(2,1)S(1)} collective-permute-done((bf16[2,256,256]{2,1,0:T(8,128)(2,1)S(1)}, bf16[2,256,256]{2,1,0:T(8,128)(2,1)S(1)}, u32[]{:S(2)}, u32[]{:S(2)}) %collective-permute-start.11) | collective-permute-done | bytes 262176 | tf_op jit(solution)/shard_map/ppermute | solution.py:536
  35.1 1.1 %shard_map.91 = (f32[2,256,256]{2,1,0:T(8,128)S(1)}, f32[2,256,256]{2,1,0:T(8,128)S(1)}, bf16[2,256,256]{2,1,0:T(8,128)(2,1)S(1)}, bf16[2,256,256]{2,1,0:T(8,128)(2,1)S(1)}) custom-call(bf16[272,256]{1,0:T(8,128)(2,1)S(1)} %get-tuple-element.26.refs_0_, bf16[272,256]{1,0:T(8,128)(2,1)S(1)} %collective-permute-done.refs_1_, ...), custom_call_target="tpu_custom_call" | custom-call | bytes 2375680 | tf_op jit(solution)/shard_map/pallas_call | solution.py:289
  36.1 1.6 %collective-permute-start.15 = (bf16[2,256,256]{2,1,0:T(8,128)(2,1)S(1)}, bf16[2,256,256]{2,1,0:T(8,128)(2,1)S(1)}, u32[]{:S(2)}, u32[]{:S(2)}) collective-permute-start(bf16[2,256,256]{2,1,0:T(8,128)(2,1)S(1)} %get-tuple-element.45), channel_id=1, source_target_pairs={{6,0},{0,2},{2,4},{4,6},{14,8},{8,10},{10,12},{12,14},{22,16},{16,... | collective-permute-start | bytes 786440 | tf_op jit(solution)/shard_map/ppermute | solution.py:31
  37.8 0.4 collective-permute-start.14
  38.2 0.6 collective-permute-start.12
  38.9 4.1 %collective-permute-done.12.refs_1_ = bf16[64,512]{1,0:T(8,128)(2,1)S(1)} collective-permute-done((bf16[64,512]{1,0:T(8,128)(2,1)S(1)}, bf16[64,512]{1,0:T(8,128)(2,1)S(1)}, u32[]{:S(2)}, u32[]{:S(2)}) %collective-permute-start.12) | collective-permute-done | bytes 65568 | tf_op jit(solution)/shard_map/ppermute | solution.py:429
  43.0 2.2 %collective-permute-done.14.refs_2_ = bf16[2,256,256]{2,1,0:T(8,128)(2,1)S(1)} collective-permute-done((bf16[2,256,256]{2,1,0:T(8,128)(2,1)S(1)}, bf16[2,256,256]{2,1,0:T(8,128)(2,1)S(1)}, u32[]{:S(2)}, u32[]{:S(2)}) %collective-permute-start.14) | collective-permute-done | bytes 262176 | tf_op jit(solution)/shard_map/ppermute | solution.py:31
  45.2 0.1 shard_map.94
  45.3 0.1 collective-permute-start.19
  45.3 4.0 %collective-permute-start.13 = (bf16[64,512]{1,0:T(8,128)(2,1)S(1)}, bf16[64,512]{1,0:T(8,128)(2,1)S(1)}, u32[]{:S(2)}, u32[]{:S(2)}) collective-permute-start(bf16[64,512]{1,0:T(8,128)(2,1)S(1)} %shard_map.93.refs_4_.refs_0_), channel_id=1, source_target_pairs={{0,16},{1,17},{2,18},{3,19},{4,20},{5,21},{6,22},{7,23},{8,24},{9,... | collective-permute-start | bytes 196616 | tf_op jit(solution)/shard_map/ppermute | solution.py:429
  49.4 8.8 %collective-permute-done.13.refs_1_ = bf16[64,512]{1,0:T(8,128)(2,1)S(1)} collective-permute-done((bf16[64,512]{1,0:T(8,128)(2,1)S(1)}, bf16[64,512]{1,0:T(8,128)(2,1)S(1)}, u32[]{:S(2)}, u32[]{:S(2)}) %collective-permute-start.13) | collective-permute-done | bytes 65568 | tf_op jit(solution)/shard_map/ppermute | solution.py:429
  58.1 1.1 %collective-permute-start.18 = (bf16[64,512]{1,0:T(8,128)(2,1)S(1)}, bf16[64,512]{1,0:T(8,128)(2,1)S(1)}, u32[]{:S(2)}, u32[]{:S(2)}) collective-permute-start(bf16[64,512]{1,0:T(8,128)(2,1)S(1)} %shard_map.95.refs_4_.refs_0_), channel_id=1, source_target_pairs={{0,5},{1,4},{2,7},{3,6},{4,1},{5,0},{6,3},{7,2},{8,13},{9,12},{10,... | collective-permute-start | bytes 196616 | tf_op jit(solution)/shard_map/ppermute | solution.py:429
  59.3 2.1 %collective-permute-start.17 = (bf16[64,512]{1,0:T(8,128)(2,1)S(1)}, bf16[64,512]{1,0:T(8,128)(2,1)S(1)}, u32[]{:S(2)}, u32[]{:S(2)}) collective-permute-start(bf16[64,512]{1,0:T(8,128)(2,1)S(1)} %shard_map.95.refs_4_.refs_0_), channel_id=1, source_target_pairs={{0,4},{1,5},{2,6},{3,7},{4,0},{5,1},{6,2},{7,3},{8,12},{9,13},{10,... | collective-permute-start | bytes 196616 | tf_op jit(solution)/shard_map/ppermute | solution.py:429
  61.4 0.3 collective-permute-start.16
  61.7 0.1 shard_map.96.refs_4_.refs_3_
  61.8 1.8 %collective-permute-start.21 = (bf16[2,256,256]{2,1,0:T(8,128)(2,1)S(1)}, bf16[2,256,256]{2,1,0:T(8,128)(2,1)S(1)}, u32[]{:S(2)}, u32[]{:S(2)}) collective-permute-start(bf16[2,256,256]{2,1,0:T(8,128)(2,1)S(1)} %shard_map.96.refs_4_.refs_3_), channel_id=1, source_target_pairs={{0,1},{1,0},{2,3},{3,2},{4,5},{5,4},{6,7},{7,6},{8,9},{9,8},{10,11... | collective-permute-start | bytes 786440 | tf_op jit(solution)/shard_map/ppermute | solution.py:572
  63.7 0.3 collective-permute-done.18.refs_3_
  63.9 0.9 %collective-permute-done.17.refs_2_ = bf16[64,512]{1,0:T(8,128)(2,1)S(1)} collective-permute-done((bf16[64,512]{1,0:T(8,128)(2,1)S(1)}, bf16[64,512]{1,0:T(8,128)(2,1)S(1)}, u32[]{:S(2)}, u32[]{:S(2)}) %collective-permute-start.17) | collective-permute-done | bytes 65568 | tf_op jit(solution)/shard_map/ppermute | solution.py:429
  64.8 1.6 %collective-permute-done.16.refs_1_ = bf16[64,512]{1,0:T(8,128)(2,1)S(1)} collective-permute-done((bf16[64,512]{1,0:T(8,128)(2,1)S(1)}, bf16[64,512]{1,0:T(8,128)(2,1)S(1)}, u32[]{:S(2)}, u32[]{:S(2)}) %collective-permute-start.16) | collective-permute-done | bytes 65568 | tf_op jit(solution)/shard_map/ppermute | solution.py:429
  66.5 0.1 shard_map.97.refs_0_
  66.5 0.1 collective-permute-start.20
  66.6 4.2 %collective-permute-done.21.refs_1_.refs_4_ = bf16[2,256,256]{2,1,0:T(8,128)(2,1)S(1)} collective-permute-done((bf16[2,256,256]{2,1,0:T(8,128)(2,1)S(1)}, bf16[2,256,256]{2,1,0:T(8,128)(2,1)S(1)}, u32[]{:S(2)}, u32[]{:S(2)}) %collective-permute-start.21) | collective-permute-done | bytes 262176 | tf_op jit(solution)/shard_map/ppermute | solution.py:572
  70.8 1.3 %shard_map.99 = (f32[2048,128]{1,0:T(8,128)}, bf16[1,2,2,256,256]{4,3,2,1,0:T(8,128)(2,1)}) custom-call(bf16[256,512]{1,0:T(8,128)(2,1)S(1)} %shard_map.97.refs_0_, bf16[256,512]{1,0:T(8,128)(2,1)S(1)} %collective-permute-done.20.refs_1_, f32[2048,128]{1,0:T(8,128)S(1)} %bitcast.16, bf16[2,256,256]{2,1,0:T(8,128)(2,1)S(1)} %shard_map.96.refs_4_.refs_3_, ...), custom_call_target="tpu_custom_call" | custom-call | flops 1048576 | bytes 3145728 | tf_op jit(solution)/shard_map/pallas_call | solution.py:320
  (21 shorter events, 0.1 us)
Async XLA Ops:
  0.6 7.6 %copy-start.2 = (bf16[1,1,2,256,256]{4,3,2,1,0:T(8,128)(2,1)S(1)}, bf16[1,1,2,256,256]{4,3,2,1,0:T(8,128)(2,1)}, u32[]{:S(2)}) copy-start(bf16[1,1,2,256,256]{4,3,2,1,0:T(8,128)(2,1)} %refs_3_.1) | copy-start | bytes 786436
  0.6 17.8 %copy-start = (f32[2,256,2,256]{3,2,1,0:T(2,128)S(1)}, f32[2,256,2,256]{3,2,1,0:T(2,128)}, u32[]{:S(2)}) copy-start(f32[2,256,2,256]{3,2,1,0:T(2,128)} %param.8) | copy-start | bytes 3145732
  1.8 16.7 %copy-start.1 = (bf16[512,512]{1,0:T(8,128)(2,1)S(1)}, bf16[512,512]{1,0:T(8,128)(2,1)}, u32[]{:S(2)}) copy-start(bf16[512,512]{1,0:T(8,128)(2,1)} %constant.10.refs_1_) | copy-start | bytes 1572868
  1.8 11.8 %collective-permute-start.4 = (bf16[2,256,256]{2,1,0:T(8,128)(2,1)S(1)}, bf16[2,256,256]{2,1,0:T(8,128)(2,1)S(1)}, u32[]{:S(2)}, u32[]{:S(2)}) collective-permute-start(bf16[2,256,256]{2,1,0:T(8,128)(2,1)S(1)} %get-tuple-element.50.refs_4_.refs_2_.refs_0_), channel_id=1, source_target_pairs={{8,0},{10,2},{12,4},{14,6},{16,8},{18,10},{20,12},{22,14},{24,16},... | collective-permute-start | bytes 786440 | tf_op jit(solution)/shard_map/ppermute | solution.py:31
  6.9 12.8 %collective-permute-start.1 = (bf16[2,2,256,256]{3,2,1,0:T(8,128)(2,1)}, bf16[2,2,256,256]{3,2,1,0:T(8,128)(2,1)S(1)}, u32[]{:S(2)}, u32[]{:S(2)}) collective-permute-start(bf16[2,2,256,256]{3,2,1,0:T(8,128)(2,1)} %bitcast.17), channel_id=1, source_target_pairs={{2,0},{4,2},{6,4},{0,6},{10,8},{12,10},{14,12},{8,14},{18,16},{20,... | collective-permute-start | bytes 1572872 | tf_op jit(solution)/shard_map/ppermute | solution.py:31
  8.2 0.7 copy-start.3
  9.5 8.6 %collective-permute-start.2 = (bf16[2,256,256]{2,1,0:T(8,128)(2,1)S(1)}, bf16[2,256,256]{2,1,0:T(8,128)(2,1)S(1)}, u32[]{:S(2)}, u32[]{:S(2)}) collective-permute-start(bf16[2,256,256]{2,1,0:T(8,128)(2,1)S(1)} %get-tuple-element.28.refs_2_.refs_1_), channel_id=1, source_target_pairs={{8,0},{10,2},{12,4},{14,6},{16,8},{18,10},{20,12},{22,14},{24,16},... | collective-permute-start | bytes 786440 | tf_op jit(solution)/shard_map/ppermute | solution.py:31
  13.6 6.1 %collective-permute-start.5 = (bf16[2,256,256]{2,1,0:T(8,128)(2,1)S(1)}, bf16[2,256,256]{2,1,0:T(8,128)(2,1)S(1)}, u32[]{:S(2)}, u32[]{:S(2)}) collective-permute-start(bf16[2,256,256]{2,1,0:T(8,128)(2,1)S(1)} %collective-permute-done.4.refs_4_), channel_id=1, source_target_pairs={{2,0},{4,2},{6,4},{0,6},{10,8},{12,10},{14,12},{8,14},{18,16},{20,... | collective-permute-start | bytes 786440 | tf_op jit(solution)/shard_map/ppermute | solution.py:31
  13.6 6.1 %collective-permute-start = (bf16[272,256]{1,0:T(8,128)(2,1)S(1)}, bf16[272,256]{1,0:T(8,128)(2,1)S(1)}, u32[]{:S(2)}, u32[]{:S(2)}) collective-permute-start(bf16[272,256]{1,0:T(8,128)(2,1)S(1)} %get-tuple-element.27), channel_id=1, source_target_pairs={{0,1},{1,0},{2,3},{3,2},{4,5},{5,4},{6,7},{7,6},{8,9},{9,8},{10,11... | collective-permute-start | bytes 417800 | tf_op jit(solution)/shard_map/ppermute | solution.py:493
  18.1 4.2 %collective-permute-start.3 = (bf16[2,256,256]{2,1,0:T(8,128)(2,1)S(1)}, bf16[2,256,256]{2,1,0:T(8,128)(2,1)S(1)}, u32[]{:S(2)}, u32[]{:S(2)}) collective-permute-start(bf16[2,256,256]{2,1,0:T(8,128)(2,1)S(1)} %collective-permute-done.2.refs_4_), channel_id=1, source_target_pairs={{2,0},{4,2},{6,4},{0,6},{10,8},{12,10},{14,12},{8,14},{18,16},{20,... | collective-permute-start | bytes 786440 | tf_op jit(solution)/shard_map/ppermute | solution.py:31
  19.7 2.6 %copy-start.4 = (bf16[512,512]{1,0:T(8,128)(2,1)S(1)}, bf16[512,512]{1,0:T(8,128)(2,1)}, u32[]{:S(2)}) copy-start(bf16[512,512]{1,0:T(8,128)(2,1)} %constant.11.refs_10_) | copy-start | bytes 1572868
  26.2 8.9 %collective-permute-start.11 = (bf16[2,256,256]{2,1,0:T(8,128)(2,1)S(1)}, bf16[2,256,256]{2,1,0:T(8,128)(2,1)S(1)}, u32[]{:S(2)}, u32[]{:S(2)}) collective-permute-start(bf16[2,256,256]{2,1,0:T(8,128)(2,1)S(1)} %get-tuple-element.41), channel_id=1, source_target_pairs={{0,1},{1,0},{2,3},{3,2},{4,5},{5,4},{6,7},{7,6},{8,9},{9,8},{10,11... | collective-permute-start | bytes 786440 | tf_op jit(solution)/shard_map/ppermute | solution.py:536
  27.8 2.1 %collective-permute-start.6 = (bf16[128,512]{1,0:T(8,128)(2,1)S(1)}, bf16[128,512]{1,0:T(8,128)(2,1)S(1)}, u32[]{:S(2)}, u32[]{:S(2)}) collective-permute-start(bf16[128,512]{1,0:T(8,128)(2,1)S(1)} %get-tuple-element.34), channel_id=1, source_target_pairs={{0,2},{1,3},{2,0},{3,1},{4,6},{5,7},{6,4},{7,5},{8,10},{9,11},{10,... | collective-permute-start | bytes 393224 | tf_op jit(solution)/shard_map/ppermute | solution.py:429
  28.9 1.3 %collective-permute-start.7 = (bf16[128,512]{1,0:T(8,128)(2,1)S(1)}, bf16[128,512]{1,0:T(8,128)(2,1)S(1)}, u32[]{:S(2)}, u32[]{:S(2)}) collective-permute-start(bf16[128,512]{1,0:T(8,128)(2,1)S(1)} %get-tuple-element.35), channel_id=1, source_target_pairs={{0,2},{1,3},{2,0},{3,1},{4,6},{5,7},{6,4},{7,5},{8,10},{9,11},{10,... | collective-permute-start | bytes 393224 | tf_op jit(solution)/shard_map/ppermute | solution.py:429
  30.4 7.8 %collective-permute-start.8 = (bf16[64,512]{1,0:T(8,128)(2,1)S(1)}, bf16[64,512]{1,0:T(8,128)(2,1)S(1)}, u32[]{:S(2)}, u32[]{:S(2)}) collective-permute-start(bf16[64,512]{1,0:T(8,128)(2,1)S(1)} %get-tuple-element.37), channel_id=1, source_target_pairs={{0,1},{1,0},{2,3},{3,2},{4,5},{5,4},{6,7},{7,6},{8,9},{9,8},{10,11... | collective-permute-start | bytes 196616 | tf_op jit(solution)/shard_map/ppermute | solution.py:429
  31.0 7.2 %collective-permute-start.9 = (bf16[64,512]{1,0:T(8,128)(2,1)S(1)}, bf16[64,512]{1,0:T(8,128)(2,1)S(1)}, u32[]{:S(2)}, u32[]{:S(2)}) collective-permute-start(bf16[64,512]{1,0:T(8,128)(2,1)S(1)} %get-tuple-element.38), channel_id=1, source_target_pairs={{0,4},{1,5},{2,6},{3,7},{4,0},{5,1},{6,2},{7,3},{8,12},{9,13},{10,... | collective-permute-start | bytes 196616 | tf_op jit(solution)/shard_map/ppermute | solution.py:429
  31.8 6.3 %collective-permute-start.10 = (bf16[64,512]{1,0:T(8,128)(2,1)S(1)}, bf16[64,512]{1,0:T(8,128)(2,1)S(1)}, u32[]{:S(2)}, u32[]{:S(2)}) collective-permute-start(bf16[64,512]{1,0:T(8,128)(2,1)S(1)} %get-tuple-element.39), channel_id=1, source_target_pairs={{0,5},{1,4},{2,7},{3,6},{4,1},{5,0},{6,3},{7,2},{8,13},{9,12},{10,... | collective-permute-start | bytes 196616 | tf_op jit(solution)/shard_map/ppermute | solution.py:429
  36.1 6.8 %collective-permute-start.15 = (bf16[2,256,256]{2,1,0:T(8,128)(2,1)S(1)}, bf16[2,256,256]{2,1,0:T(8,128)(2,1)S(1)}, u32[]{:S(2)}, u32[]{:S(2)}) collective-permute-start(bf16[2,256,256]{2,1,0:T(8,128)(2,1)S(1)} %get-tuple-element.45), channel_id=1, source_target_pairs={{6,0},{0,2},{2,4},{4,6},{14,8},{8,10},{10,12},{12,14},{22,16},{16,... | collective-permute-start | bytes 786440 | tf_op jit(solution)/shard_map/ppermute | solution.py:31
  37.8 7.4 %collective-permute-start.14 = (bf16[2,256,256]{2,1,0:T(8,128)(2,1)S(1)}, bf16[2,256,256]{2,1,0:T(8,128)(2,1)S(1)}, u32[]{:S(2)}, u32[]{:S(2)}) collective-permute-start(bf16[2,256,256]{2,1,0:T(8,128)(2,1)S(1)} %get-tuple-element.42.refs_4_), channel_id=1, source_target_pairs={{6,0},{0,2},{2,4},{4,6},{14,8},{8,10},{10,12},{12,14},{22,16},{16,... | collective-permute-start | bytes 786440 | tf_op jit(solution)/shard_map/ppermute | solution.py:31
  38.2 4.7 %collective-permute-start.12 = (bf16[64,512]{1,0:T(8,128)(2,1)S(1)}, bf16[64,512]{1,0:T(8,128)(2,1)S(1)}, u32[]{:S(2)}, u32[]{:S(2)}) collective-permute-start(bf16[64,512]{1,0:T(8,128)(2,1)S(1)} %shard_map.92.refs_0_), channel_id=1, source_target_pairs={{0,8},{1,9},{2,10},{3,11},{4,12},{5,13},{6,14},{7,15},{8,0},{9,1},... | collective-permute-start | bytes 196616 | tf_op jit(solution)/shard_map/ppermute | solution.py:429
  45.3 16.4 %collective-permute-start.19 = (bf16[2,256,256]{2,1,0:T(8,128)(2,1)S(1)}, bf16[2,256,256]{2,1,0:T(8,128)(2,1)S(1)}, u32[]{:S(2)}, u32[]{:S(2)}) collective-permute-start(bf16[2,256,256]{2,1,0:T(8,128)(2,1)S(1)} %get-tuple-element.46.refs_2_), channel_id=1, source_target_pairs={{24,0},{26,2},{28,4},{30,6},{0,8},{2,10},{4,12},{6,14},{8,16},{10,... | collective-permute-start | bytes 786440 | tf_op jit(solution)/shard_map/ppermute | solution.py:31
  45.3 12.8 %collective-permute-start.13 = (bf16[64,512]{1,0:T(8,128)(2,1)S(1)}, bf16[64,512]{1,0:T(8,128)(2,1)S(1)}, u32[]{:S(2)}, u32[]{:S(2)}) collective-permute-start(bf16[64,512]{1,0:T(8,128)(2,1)S(1)} %shard_map.93.refs_4_.refs_0_), channel_id=1, source_target_pairs={{0,16},{1,17},{2,18},{3,19},{4,20},{5,21},{6,22},{7,23},{8,24},{9,... | collective-permute-start | bytes 196616 | tf_op jit(solution)/shard_map/ppermute | solution.py:429
  58.1 5.8 %collective-permute-start.18 = (bf16[64,512]{1,0:T(8,128)(2,1)S(1)}, bf16[64,512]{1,0:T(8,128)(2,1)S(1)}, u32[]{:S(2)}, u32[]{:S(2)}) collective-permute-start(bf16[64,512]{1,0:T(8,128)(2,1)S(1)} %shard_map.95.refs_4_.refs_0_), channel_id=1, source_target_pairs={{0,5},{1,4},{2,7},{3,6},{4,1},{5,0},{6,3},{7,2},{8,13},{9,12},{10,... | collective-permute-start | bytes 196616 | tf_op jit(solution)/shard_map/ppermute | solution.py:429
  59.3 5.5 %collective-permute-start.17 = (bf16[64,512]{1,0:T(8,128)(2,1)S(1)}, bf16[64,512]{1,0:T(8,128)(2,1)S(1)}, u32[]{:S(2)}, u32[]{:S(2)}) collective-permute-start(bf16[64,512]{1,0:T(8,128)(2,1)S(1)} %shard_map.95.refs_4_.refs_0_), channel_id=1, source_target_pairs={{0,4},{1,5},{2,6},{3,7},{4,0},{5,1},{6,2},{7,3},{8,12},{9,13},{10,... | collective-permute-start | bytes 196616 | tf_op jit(solution)/shard_map/ppermute | solution.py:429
  61.4 5.0 %collective-permute-start.16 = (bf16[64,512]{1,0:T(8,128)(2,1)S(1)}, bf16[64,512]{1,0:T(8,128)(2,1)S(1)}, u32[]{:S(2)}, u32[]{:S(2)}) collective-permute-start(bf16[64,512]{1,0:T(8,128)(2,1)S(1)} %shard_map.95.refs_4_.refs_0_), channel_id=1, source_target_pairs={{0,1},{1,0},{2,3},{3,2},{4,5},{5,4},{6,7},{7,6},{8,9},{9,8},{10,11... | collective-permute-start | bytes 196616 | tf_op jit(solution)/shard_map/ppermute | solution.py:429
  61.8 9.0 %collective-permute-start.21 = (bf16[2,256,256]{2,1,0:T(8,128)(2,1)S(1)}, bf16[2,256,256]{2,1,0:T(8,128)(2,1)S(1)}, u32[]{:S(2)}, u32[]{:S(2)}) collective-permute-start(bf16[2,256,256]{2,1,0:T(8,128)(2,1)S(1)} %shard_map.96.refs_4_.refs_3_), channel_id=1, source_target_pairs={{0,1},{1,0},{2,3},{3,2},{4,5},{5,4},{6,7},{7,6},{8,9},{9,8},{10,11... | collective-permute-start | bytes 786440 | tf_op jit(solution)/shard_map/ppermute | solution.py:572
  66.5 4.3 %collective-permute-start.20 = (bf16[256,512]{1,0:T(8,128)(2,1)S(1)}, bf16[256,512]{1,0:T(8,128)(2,1)S(1)}, u32[]{:S(2)}, u32[]{:S(2)}) collective-permute-start(bf16[256,512]{1,0:T(8,128)(2,1)S(1)} %shard_map.97.refs_0_), channel_id=1, source_target_pairs={{0,2},{1,3},{2,0},{3,1},{4,6},{5,7},{6,4},{7,5},{8,10},{9,11},{10,... | collective-permute-start | bytes 786440 | tf_op jit(solution)/shard_map/ppermute | solution.py:429

commit v19 on v17

--- a/solution.py
+++ b/solution.py
@@ -19,6 +19,12 @@
 
 f32 = jnp.float32
 bf16 = jnp.bfloat16
+
+
+def from_below(block):
+    tiles = lax.axis_size("tile")
+    across = tiles // GRID_ROWS
+    return lax.ppermute(block, "tile", [(i + across, i) for i in range(tiles - across)])
 
 
 def from_behind(block, rows, cols):
@@ -488,7 +494,7 @@
         limit=8,
         after=[own1],
     )
-    below1 = from_behind(own1, -1, 0)
+    below1 = from_below(own1)
     if exchanged:
         sent = lax.ppermute(sent, "pos", [(i, 1 - i) for i in range(2)])
     else:

time: 63.8 us -> 70.8 us (1.11)
  waiting for transfers between devices: 24 us -> 37.3 us
  starting transfers between devices: 27.2 us -> 20.8 us
    ppermute x11, waiting for transfers between devices: 6.18 us -> 19 us  [swap_with(): lax.ppermute(x, ('tile', 'pos'), [(i, i ^ mask) for i in range(devices)])]
    ppermute x0 -> x1, waiting for transfers between devices: none -> 5.41 us  [from_below(): lax.ppermute(block, 'tile', [(i + across, i) for i in range(tiles - acros...]
    ppermute x8 -> x7, waiting for transfers between devices: 10.6 us -> 6.13 us  [from_behind(): return lax.ppermute(block, 'tile', [(source(i), i) for i in range(tiles)])]
    ppermute x8 -> x7, starting transfers between devices: 10.6 us -> 6.85 us  [from_behind(): return lax.ppermute(block, 'tile', [(source(i), i) for i in range(tiles)])]
    ppermute x11, starting transfers between devices: 11.7 us -> 7.99 us  [swap_with(): lax.ppermute(x, ('tile', 'pos'), [(i, i ^ mask) for i in range(devices)])]
    ppermute x1, waiting for transfers between devices: 1.13 us -> 2.49 us  [shards(): got = lax.ppermute(given, 'pos', swap)]
    ppermute x0 -> x1, starting transfers between devices: none -> 1.29 us  [from_below(): lax.ppermute(block, 'tile', [(i + across, i) for i in range(tiles - acros...]
    ppermute x1, waiting for transfers between devices: 1.16 us -> 0.01 us  [shards(): sent = lax.ppermute(sent, 'pos', [(i, 1 - i) for i in range(2)])]
  transfers between devices with their start and end apart: 22 -> 22, of which waited for: 11 -> 14; matrix products, arithmetic and copies ran while one was open for 0% -> 0% of each run, Pallas kernels for 6% -> 6%
where the time goes in v19:
time: 70.8 us; the launch traced here: 70.6 us
  waiting for transfers between devices  37.3 us (53%)
  starting transfers between devices  20.8 us (29%)
  Pallas kernels  9.08 us (13%)
  local copies, waits for them, and re-layouts  1.86 us (3%)
  between operations  1.49 us (2%)
    ppermute x11, waiting for transfers between devices, swap_with(): lax.ppermute(x, ('tile', 'pos'), [(i, i ^ mask) for i in range(devices)])  19 us
    ppermute x11, starting transfers between devices, swap_with(): lax.ppermute(x, ('tile', 'pos'), [(i, i ^ mask) for i in range(devices)])  7.99 us
    pallas_call x13, Pallas kernels, run(): pl.pallas_call(body, out_shape=sum(outs, []), in_specs=sum(specs, []) + [...  7.82 us
    ppermute x7, starting transfers between devices, from_behind(): return lax.ppermute(block, 'tile', [(source(i), i) for i in range(tiles)])  6.85 us
    ppermute x7, waiting for transfers between devices, from_behind(): return lax.ppermute(block, 'tile', [(source(i), i) for i in range(tiles)])  6.13 us
    ppermute x1, waiting for transfers between devices, from_below(): lax.ppermute(block, 'tile', [(i + across, i) for i in range(tiles - acros...  5.41 us
    ppermute x1, waiting for transfers between devices, shards(): other_slice = lax.ppermute(this_slice, 'pos', swap)  4.34 us
    ppermute x1, waiting for transfers between devices, shards(): got = lax.ppermute(given, 'pos', swap)  2.49 us
  transfers between devices with their start and end apart: 22, of which 14 were waited for; matrix products, arithmetic and copies ran while one was open for 0% of the time, Pallas kernels for 6%

profile of v19, /device:TPU:0, one launch (start us, length us, event | category | flops | bytes accessed | tf_op | source)
XLA Modules:
  0.0 70.6 jit_solution(12024394552202955659)
XLA Ops:
  0.6 1.2 %slice_bitcast_fusion = (bf16[2,256,256]{2,1,0:T(8,128)(2,1)S(1)}, bf16[2,256,256]{2,1,0:T(8,128)(2,1)S(1)}) fusion(bf16[1,2,2,256,256]{4,3,2,1,0:T(8,128)(2,1)} %param.7), kind=kLoop, calls=%fused_computation | loop fusion | bytes 1048576 | tf_op jit(solution)/shard_map/squeeze | solution.py:477
  1.8 5.1 %collective-permute-start.4 = (bf16[2,256,256]{2,1,0:T(8,128)(2,1)S(1)}, bf16[2,256,256]{2,1,0:T(8,128)(2,1)S(1)}, u32[]{:S(2)}, u32[]{:S(2)}) collective-permute-start(bf16[2,256,256]{2,1,0:T(8,128)(2,1)S(1)} %get-tuple-element.50.refs_4_.refs_2_.refs_0_), channel_id=1, source_target_pairs={{8,0},{10,2},{12,4},{14,6},{16,8},{18,10},{20,12},{22,14},{24,16},... | collective-permute-start | bytes 786440 | tf_op jit(solution)/shard_map/ppermute | solution.py:37
  6.9 0.7 collective-permute-start.1
  8.3 0.7 copy-done.3
  8.9 0.6 shard_map.86
  9.5 1.3 %collective-permute-start.2 = (bf16[2,256,256]{2,1,0:T(8,128)(2,1)S(1)}, bf16[2,256,256]{2,1,0:T(8,128)(2,1)S(1)}, u32[]{:S(2)}, u32[]{:S(2)}) collective-permute-start(bf16[2,256,256]{2,1,0:T(8,128)(2,1)S(1)} %get-tuple-element.28.refs_2_.refs_1_), channel_id=1, source_target_pairs={{8,0},{10,2},{12,4},{14,6},{16,8},{18,10},{20,12},{22,14},{24,16},... | collective-permute-start | bytes 786440 | tf_op jit(solution)/shard_map/ppermute | solution.py:27
  10.8 1.7 %collective-permute-done.4.refs_4_ = bf16[2,256,256]{2,1,0:T(8,128)(2,1)S(1)} collective-permute-done((bf16[2,256,256]{2,1,0:T(8,128)(2,1)S(1)}, bf16[2,256,256]{2,1,0:T(8,128)(2,1)S(1)}, u32[]{:S(2)}, u32[]{:S(2)}) %collective-permute-start.4) | collective-permute-done | bytes 262176 | tf_op jit(solution)/shard_map/ppermute | solution.py:37
  12.5 0.1 collective-permute-start.5
  12.6 1.5 %collective-permute-start = (bf16[272,256]{1,0:T(8,128)(2,1)S(1)}, bf16[272,256]{1,0:T(8,128)(2,1)S(1)}, u32[]{:S(2)}, u32[]{:S(2)}) collective-permute-start(bf16[272,256]{1,0:T(8,128)(2,1)S(1)} %get-tuple-element.27), channel_id=1, source_target_pairs={{0,1},{1,0},{2,3},{3,2},{4,5},{5,4},{6,7},{7,6},{8,9},{9,8},{10,11... | collective-permute-start | bytes 417800 | tf_op jit(solution)/shard_map/ppermute | solution.py:499
  14.1 5.4 %collective-permute-done.2.refs_4_ = bf16[2,256,256]{2,1,0:T(8,128)(2,1)S(1)} collective-permute-done((bf16[2,256,256]{2,1,0:T(8,128)(2,1)S(1)}, bf16[2,256,256]{2,1,0:T(8,128)(2,1)S(1)}, u32[]{:S(2)}, u32[]{:S(2)}) %collective-permute-start.2) | collective-permute-done | bytes 262176 | tf_op jit(solution)/shard_map/ppermute | solution.py:27
  19.5 0.8 %collective-permute-start.3 = (bf16[2,256,256]{2,1,0:T(8,128)(2,1)S(1)}, bf16[2,256,256]{2,1,0:T(8,128)(2,1)S(1)}, u32[]{:S(2)}, u32[]{:S(2)}) collective-permute-start(bf16[2,256,256]{2,1,0:T(8,128)(2,1)S(1)} %collective-permute-done.2.refs_4_), channel_id=1, source_target_pairs={{2,0},{4,2},{6,4},{0,6},{10,8},{12,10},{14,12},{8,14},{18,16},{20,... | collective-permute-start | bytes 786440 | tf_op jit(solution)/shard_map/ppermute | solution.py:37
  20.3 0.1 shard_map.87
  20.4 0.0 copy-start.4
  20.5 1.8 %shard_map.88 = (bf16[2,256,256]{2,1,0:T(8,128)(2,1)S(1)}, f32[2,256,512]{2,1,0:T(8,128)S(1)}) custom-call(bf16[272,256]{1,0:T(8,128)(2,1)S(1)} %get-tuple-element.26.refs_0_, bf16[272,256]{1,0:T(8,128)(2,1)S(1)} %collective-permute-done.refs_1_, bf16[2,256,256]{2,1,0:T(8,128)(2,1)S(1)} %get-tuple-element.50.refs_4_.refs_2_.refs_0_, ...), custom_call_target="tpu_custom_call" | custom-call | flops 1500000000 | bytes 4472832 | tf_op jit(solution)/shard_map/pallas_call | solution.py:295
  22.2 2.0 %collective-permute-done.3.refs_5_ = bf16[2,256,256]{2,1,0:T(8,128)(2,1)S(1)} collective-permute-done((bf16[2,256,256]{2,1,0:T(8,128)(2,1)S(1)}, bf16[2,256,256]{2,1,0:T(8,128)(2,1)S(1)}, u32[]{:S(2)}, u32[]{:S(2)}) %collective-permute-start.3) | collective-permute-done | bytes 262176 | tf_op jit(solution)/shard_map/ppermute | solution.py:37
  24.2 3.8 %shard_map.89 = (bf16[2,256,256]{2,1,0:T(8,128)(2,1)S(1)}, bf16[2,256,256]{2,1,0:T(8,128)(2,1)S(1)}, bf16[256,512]{1,0:T(8,128)(2,1)S(1)}, bf16[128,512]{1,0:T(8,128)(2,1)S(1)}, bf16[128,512]{1,0:T(8,128)(2,1)S(1)}) custom-call(bf16[272,256]{1,0:T(8,128)(2,1)S(1)} %get-tuple-element.26.refs_0_, bf16[272,256]{1,0:T(8,128)(2,1)S(1)} %collective-permute-done.refs_1_, ...), custom_call_target="tpu_custom_call" | custom-call | flops 4000000000 | bytes 6045696 | tf_op jit(solution)/shard_map/pallas_call | solution.py:295
  28.1 1.6 %collective-permute-start.11 = (bf16[2,256,256]{2,1,0:T(8,128)(2,1)S(1)}, bf16[2,256,256]{2,1,0:T(8,128)(2,1)S(1)}, u32[]{:S(2)}, u32[]{:S(2)}) collective-permute-start(bf16[2,256,256]{2,1,0:T(8,128)(2,1)S(1)} %get-tuple-element.41), channel_id=1, source_target_pairs={{0,1},{1,0},{2,3},{3,2},{4,5},{5,4},{6,7},{7,6},{8,9},{9,8},{10,11... | collective-permute-start | bytes 786440 | tf_op jit(solution)/shard_map/ppermute | solution.py:542
  29.6 0.7 collective-permute-start.6
  30.3 1.0 %collective-permute-done.6.refs_1_ = bf16[128,512]{1,0:T(8,128)(2,1)S(1)} collective-permute-done((bf16[128,512]{1,0:T(8,128)(2,1)S(1)}, bf16[128,512]{1,0:T(8,128)(2,1)S(1)}, u32[]{:S(2)}, u32[]{:S(2)}) %collective-permute-start.6) | collective-permute-done | bytes 131104 | tf_op jit(solution)/shard_map/ppermute | solution.py:435
  31.3 0.4 collective-permute-done.7.refs_2_
  31.7 0.1 shard_map.90
  31.8 0.6 collective-permute-start.8
  32.3 1.4 %collective-permute-start.9 = (bf16[64,512]{1,0:T(8,128)(2,1)S(1)}, bf16[64,512]{1,0:T(8,128)(2,1)S(1)}, u32[]{:S(2)}, u32[]{:S(2)}) collective-permute-start(bf16[64,512]{1,0:T(8,128)(2,1)S(1)} %get-tuple-element.38), channel_id=1, source_target_pairs={{0,4},{1,5},{2,6},{3,7},{4,0},{5,1},{6,2},{7,3},{8,12},{9,13},{10,... | collective-permute-start | bytes 196616 | tf_op jit(solution)/shard_map/ppermute | solution.py:435
  33.7 1.6 %collective-permute-start.10 = (bf16[64,512]{1,0:T(8,128)(2,1)S(1)}, bf16[64,512]{1,0:T(8,128)(2,1)S(1)}, u32[]{:S(2)}, u32[]{:S(2)}) collective-permute-start(bf16[64,512]{1,0:T(8,128)(2,1)S(1)} %get-tuple-element.39), channel_id=1, source_target_pairs={{0,5},{1,4},{2,7},{3,6},{4,1},{5,0},{6,3},{7,2},{8,13},{9,12},{10,... | collective-permute-start | bytes 196616 | tf_op jit(solution)/shard_map/ppermute | solution.py:435
  35.3 2.5 %collective-permute-done.11.refs_3_ = bf16[2,256,256]{2,1,0:T(8,128)(2,1)S(1)} collective-permute-done((bf16[2,256,256]{2,1,0:T(8,128)(2,1)S(1)}, bf16[2,256,256]{2,1,0:T(8,128)(2,1)S(1)}, u32[]{:S(2)}, u32[]{:S(2)}) %collective-permute-start.11) | collective-permute-done | bytes 262176 | tf_op jit(solution)/shard_map/ppermute | solution.py:542
  37.8 1.1 %shard_map.91 = (f32[2,256,256]{2,1,0:T(8,128)S(1)}, f32[2,256,256]{2,1,0:T(8,128)S(1)}, bf16[2,256,256]{2,1,0:T(8,128)(2,1)S(1)}, bf16[2,256,256]{2,1,0:T(8,128)(2,1)S(1)}) custom-call(bf16[272,256]{1,0:T(8,128)(2,1)S(1)} %get-tuple-element.26.refs_0_, bf16[272,256]{1,0:T(8,128)(2,1)S(1)} %collective-permute-done.refs_1_, ...), custom_call_target="tpu_custom_call" | custom-call | bytes 2375680 | tf_op jit(solution)/shard_map/pallas_call | solution.py:295
  38.9 0.1 collective-permute-start.15
  39.0 0.1 collective-permute-start.14
  39.0 1.1 %collective-permute-done.8.refs_1_ = bf16[64,512]{1,0:T(8,128)(2,1)S(1)} collective-permute-done((bf16[64,512]{1,0:T(8,128)(2,1)S(1)}, bf16[64,512]{1,0:T(8,128)(2,1)S(1)}, u32[]{:S(2)}, u32[]{:S(2)}) %collective-permute-start.8) | collective-permute-done | bytes 65568 | tf_op jit(solution)/shard_map/ppermute | solution.py:435
  40.1 0.1 collective-permute-start.12
  40.2 4.7 %collective-permute-done.12.refs_1_ = bf16[64,512]{1,0:T(8,128)(2,1)S(1)} collective-permute-done((bf16[64,512]{1,0:T(8,128)(2,1)S(1)}, bf16[64,512]{1,0:T(8,128)(2,1)S(1)}, u32[]{:S(2)}, u32[]{:S(2)}) %collective-permute-start.12) | collective-permute-done | bytes 65568 | tf_op jit(solution)/shard_map/ppermute | solution.py:435
  45.0 0.1 collective-permute-start.13
  45.1 2.5 %collective-permute-done.14.refs_2_ = bf16[2,256,256]{2,1,0:T(8,128)(2,1)S(1)} collective-permute-done((bf16[2,256,256]{2,1,0:T(8,128)(2,1)S(1)}, bf16[2,256,256]{2,1,0:T(8,128)(2,1)S(1)}, u32[]{:S(2)}, u32[]{:S(2)}) %collective-permute-start.14) | collective-permute-done | bytes 262176 | tf_op jit(solution)/shard_map/ppermute | solution.py:37
  47.5 0.1 shard_map.94
  47.6 0.1 collective-permute-start.19
  47.7 9.0 %collective-permute-done.13.refs_1_ = bf16[64,512]{1,0:T(8,128)(2,1)S(1)} collective-permute-done((bf16[64,512]{1,0:T(8,128)(2,1)S(1)}, bf16[64,512]{1,0:T(8,128)(2,1)S(1)}, u32[]{:S(2)}, u32[]{:S(2)}) %collective-permute-start.13) | collective-permute-done | bytes 65568 | tf_op jit(solution)/shard_map/ppermute | solution.py:435
  56.7 0.1 collective-permute-start.18
  56.8 3.0 %collective-permute-start.17 = (bf16[64,512]{1,0:T(8,128)(2,1)S(1)}, bf16[64,512]{1,0:T(8,128)(2,1)S(1)}, u32[]{:S(2)}, u32[]{:S(2)}) collective-permute-start(bf16[64,512]{1,0:T(8,128)(2,1)S(1)} %shard_map.95.refs_4_.refs_0_), channel_id=1, source_target_pairs={{0,4},{1,5},{2,6},{3,7},{4,0},{5,1},{6,2},{7,3},{8,12},{9,13},{10,... | collective-permute-start | bytes 196616 | tf_op jit(solution)/shard_map/ppermute | solution.py:435
  59.8 0.5 collective-permute-start.16
  60.3 0.1 shard_map.96.refs_4_.refs_3_
  60.4 1.6 %collective-permute-start.21 = (bf16[2,256,256]{2,1,0:T(8,128)(2,1)S(1)}, bf16[2,256,256]{2,1,0:T(8,128)(2,1)S(1)}, u32[]{:S(2)}, u32[]{:S(2)}) collective-permute-start(bf16[2,256,256]{2,1,0:T(8,128)(2,1)S(1)} %shard_map.96.refs_4_.refs_3_), channel_id=1, source_target_pairs={{0,1},{1,0},{2,3},{3,2},{4,5},{5,4},{6,7},{7,6},{8,9},{9,8},{10,11... | collective-permute-start | bytes 786440 | tf_op jit(solution)/shard_map/ppermute | solution.py:578
  62.0 0.5 collective-permute-done.18.refs_3_
  62.5 0.7 collective-permute-done.17.refs_2_
  63.2 1.6 %collective-permute-done.16.refs_1_ = bf16[64,512]{1,0:T(8,128)(2,1)S(1)} collective-permute-done((bf16[64,512]{1,0:T(8,128)(2,1)S(1)}, bf16[64,512]{1,0:T(8,128)(2,1)S(1)}, u32[]{:S(2)}, u32[]{:S(2)}) %collective-permute-start.16) | collective-permute-done | bytes 65568 | tf_op jit(solution)/shard_map/ppermute | solution.py:435
  64.8 0.1 shard_map.97.refs_0_
  64.9 0.1 collective-permute-start.20
  65.0 4.3 %collective-permute-done.21.refs_1_.refs_4_ = bf16[2,256,256]{2,1,0:T(8,128)(2,1)S(1)} collective-permute-done((bf16[2,256,256]{2,1,0:T(8,128)(2,1)S(1)}, bf16[2,256,256]{2,1,0:T(8,128)(2,1)S(1)}, u32[]{:S(2)}, u32[]{:S(2)}) %collective-permute-start.21) | collective-permute-done | bytes 262176 | tf_op jit(solution)/shard_map/ppermute | solution.py:578
  69.3 1.3 %shard_map.99 = (f32[2048,128]{1,0:T(8,128)}, bf16[1,2,2,256,256]{4,3,2,1,0:T(8,128)(2,1)}) custom-call(bf16[256,512]{1,0:T(8,128)(2,1)S(1)} %shard_map.97.refs_0_, bf16[256,512]{1,0:T(8,128)(2,1)S(1)} %collective-permute-done.20.refs_1_, f32[2048,128]{1,0:T(8,128)S(1)} %bitcast.16, bf16[2,256,256]{2,1,0:T(8,128)(2,1)S(1)} %shard_map.96.refs_4_.refs_3_, ...), custom_call_target="tpu_custom_call" | custom-call | flops 1048576 | bytes 3145728 | tf_op jit(solution)/shard_map/pallas_call | solution.py:326
  (21 shorter events, 0.1 us)
Async XLA Ops:
  0.6 7.6 %copy-start.2 = (bf16[1,1,2,256,256]{4,3,2,1,0:T(8,128)(2,1)S(1)}, bf16[1,1,2,256,256]{4,3,2,1,0:T(8,128)(2,1)}, u32[]{:S(2)}) copy-start(bf16[1,1,2,256,256]{4,3,2,1,0:T(8,128)(2,1)} %refs_3_.1) | copy-start | bytes 786436
  0.6 19.7 %copy-start = (f32[2,256,2,256]{3,2,1,0:T(2,128)S(1)}, f32[2,256,2,256]{3,2,1,0:T(2,128)}, u32[]{:S(2)}) copy-start(f32[2,256,2,256]{3,2,1,0:T(2,128)} %param.8) | copy-start | bytes 3145732
  1.8 18.5 %copy-start.1 = (bf16[512,512]{1,0:T(8,128)(2,1)S(1)}, bf16[512,512]{1,0:T(8,128)(2,1)}, u32[]{:S(2)}) copy-start(bf16[512,512]{1,0:T(8,128)(2,1)} %constant.10.refs_1_) | copy-start | bytes 1572868
  1.8 10.7 %collective-permute-start.4 = (bf16[2,256,256]{2,1,0:T(8,128)(2,1)S(1)}, bf16[2,256,256]{2,1,0:T(8,128)(2,1)S(1)}, u32[]{:S(2)}, u32[]{:S(2)}) collective-permute-start(bf16[2,256,256]{2,1,0:T(8,128)(2,1)S(1)} %get-tuple-element.50.refs_4_.refs_2_.refs_0_), channel_id=1, source_target_pairs={{8,0},{10,2},{12,4},{14,6},{16,8},{18,10},{20,12},{22,14},{24,16},... | collective-permute-start | bytes 786440 | tf_op jit(solution)/shard_map/ppermute | solution.py:37
  6.9 13.5 %collective-permute-start.1 = (bf16[2,2,256,256]{3,2,1,0:T(8,128)(2,1)}, bf16[2,2,256,256]{3,2,1,0:T(8,128)(2,1)S(1)}, u32[]{:S(2)}, u32[]{:S(2)}) collective-permute-start(bf16[2,2,256,256]{3,2,1,0:T(8,128)(2,1)} %bitcast.17), channel_id=1, source_target_pairs={{2,0},{4,2},{6,4},{0,6},{10,8},{12,10},{14,12},{8,14},{18,16},{20,... | collective-permute-start | bytes 1572872 | tf_op jit(solution)/shard_map/ppermute | solution.py:37
  8.2 0.7 copy-start.3
  9.5 10.0 %collective-permute-start.2 = (bf16[2,256,256]{2,1,0:T(8,128)(2,1)S(1)}, bf16[2,256,256]{2,1,0:T(8,128)(2,1)S(1)}, u32[]{:S(2)}, u32[]{:S(2)}) collective-permute-start(bf16[2,256,256]{2,1,0:T(8,128)(2,1)S(1)} %get-tuple-element.28.refs_2_.refs_1_), channel_id=1, source_target_pairs={{8,0},{10,2},{12,4},{14,6},{16,8},{18,10},{20,12},{22,14},{24,16},... | collective-permute-start | bytes 786440 | tf_op jit(solution)/shard_map/ppermute | solution.py:27
  12.5 7.9 %collective-permute-start.5 = (bf16[2,256,256]{2,1,0:T(8,128)(2,1)S(1)}, bf16[2,256,256]{2,1,0:T(8,128)(2,1)S(1)}, u32[]{:S(2)}, u32[]{:S(2)}) collective-permute-start(bf16[2,256,256]{2,1,0:T(8,128)(2,1)S(1)} %collective-permute-done.4.refs_4_), channel_id=1, source_target_pairs={{2,0},{4,2},{6,4},{0,6},{10,8},{12,10},{14,12},{8,14},{18,16},{20,... | collective-permute-start | bytes 786440 | tf_op jit(solution)/shard_map/ppermute | solution.py:37
  12.6 7.9 %collective-permute-start = (bf16[272,256]{1,0:T(8,128)(2,1)S(1)}, bf16[272,256]{1,0:T(8,128)(2,1)S(1)}, u32[]{:S(2)}, u32[]{:S(2)}) collective-permute-start(bf16[272,256]{1,0:T(8,128)(2,1)S(1)} %get-tuple-element.27), channel_id=1, source_target_pairs={{0,1},{1,0},{2,3},{3,2},{4,5},{5,4},{6,7},{7,6},{8,9},{9,8},{10,11... | collective-permute-start | bytes 417800 | tf_op jit(solution)/shard_map/ppermute | solution.py:499
  19.5 4.7 %collective-permute-start.3 = (bf16[2,256,256]{2,1,0:T(8,128)(2,1)S(1)}, bf16[2,256,256]{2,1,0:T(8,128)(2,1)S(1)}, u32[]{:S(2)}, u32[]{:S(2)}) collective-permute-start(bf16[2,256,256]{2,1,0:T(8,128)(2,1)S(1)} %collective-permute-done.2.refs_4_), channel_id=1, source_target_pairs={{2,0},{4,2},{6,4},{0,6},{10,8},{12,10},{14,12},{8,14},{18,16},{20,... | collective-permute-start | bytes 786440 | tf_op jit(solution)/shard_map/ppermute | solution.py:37
  20.4 3.8 %copy-start.4 = (bf16[512,512]{1,0:T(8,128)(2,1)S(1)}, bf16[512,512]{1,0:T(8,128)(2,1)}, u32[]{:S(2)}) copy-start(bf16[512,512]{1,0:T(8,128)(2,1)} %constant.11.refs_10_) | copy-start | bytes 1572868
  28.1 9.8 %collective-permute-start.11 = (bf16[2,256,256]{2,1,0:T(8,128)(2,1)S(1)}, bf16[2,256,256]{2,1,0:T(8,128)(2,1)S(1)}, u32[]{:S(2)}, u32[]{:S(2)}) collective-permute-start(bf16[2,256,256]{2,1,0:T(8,128)(2,1)S(1)} %get-tuple-element.41), channel_id=1, source_target_pairs={{0,1},{1,0},{2,3},{3,2},{4,5},{5,4},{6,7},{7,6},{8,9},{9,8},{10,11... | collective-permute-start | bytes 786440 | tf_op jit(solution)/shard_map/ppermute | solution.py:542
  29.6 1.7 %collective-permute-start.6 = (bf16[128,512]{1,0:T(8,128)(2,1)S(1)}, bf16[128,512]{1,0:T(8,128)(2,1)S(1)}, u32[]{:S(2)}, u32[]{:S(2)}) collective-permute-start(bf16[128,512]{1,0:T(8,128)(2,1)S(1)} %get-tuple-element.34), channel_id=1, source_target_pairs={{0,2},{1,3},{2,0},{3,1},{4,6},{5,7},{6,4},{7,5},{8,10},{9,11},{10,... | collective-permute-start | bytes 393224 | tf_op jit(solution)/shard_map/ppermute | solution.py:435
  30.3 1.3 %collective-permute-start.7 = (bf16[128,512]{1,0:T(8,128)(2,1)S(1)}, bf16[128,512]{1,0:T(8,128)(2,1)S(1)}, u32[]{:S(2)}, u32[]{:S(2)}) collective-permute-start(bf16[128,512]{1,0:T(8,128)(2,1)S(1)} %get-tuple-element.35), channel_id=1, source_target_pairs={{0,2},{1,3},{2,0},{3,1},{4,6},{5,7},{6,4},{7,5},{8,10},{9,11},{10,... | collective-permute-start | bytes 393224 | tf_op jit(solution)/shard_map/ppermute | solution.py:435
  31.8 8.3 %collective-permute-start.8 = (bf16[64,512]{1,0:T(8,128)(2,1)S(1)}, bf16[64,512]{1,0:T(8,128)(2,1)S(1)}, u32[]{:S(2)}, u32[]{:S(2)}) collective-permute-start(bf16[64,512]{1,0:T(8,128)(2,1)S(1)} %get-tuple-element.37), channel_id=1, source_target_pairs={{0,1},{1,0},{2,3},{3,2},{4,5},{5,4},{6,7},{7,6},{8,9},{9,8},{10,11... | collective-permute-start | bytes 196616 | tf_op jit(solution)/shard_map/ppermute | solution.py:435
  32.3 7.8 %collective-permute-start.9 = (bf16[64,512]{1,0:T(8,128)(2,1)S(1)}, bf16[64,512]{1,0:T(8,128)(2,1)S(1)}, u32[]{:S(2)}, u32[]{:S(2)}) collective-permute-start(bf16[64,512]{1,0:T(8,128)(2,1)S(1)} %get-tuple-element.38), channel_id=1, source_target_pairs={{0,4},{1,5},{2,6},{3,7},{4,0},{5,1},{6,2},{7,3},{8,12},{9,13},{10,... | collective-permute-start | bytes 196616 | tf_op jit(solution)/shard_map/ppermute | solution.py:435
  33.7 6.4 %collective-permute-start.10 = (bf16[64,512]{1,0:T(8,128)(2,1)S(1)}, bf16[64,512]{1,0:T(8,128)(2,1)S(1)}, u32[]{:S(2)}, u32[]{:S(2)}) collective-permute-start(bf16[64,512]{1,0:T(8,128)(2,1)S(1)} %get-tuple-element.39), channel_id=1, source_target_pairs={{0,5},{1,4},{2,7},{3,6},{4,1},{5,0},{6,3},{7,2},{8,13},{9,12},{10,... | collective-permute-start | bytes 196616 | tf_op jit(solution)/shard_map/ppermute | solution.py:435
  38.9 6.2 %collective-permute-start.15 = (bf16[2,256,256]{2,1,0:T(8,128)(2,1)S(1)}, bf16[2,256,256]{2,1,0:T(8,128)(2,1)S(1)}, u32[]{:S(2)}, u32[]{:S(2)}) collective-permute-start(bf16[2,256,256]{2,1,0:T(8,128)(2,1)S(1)} %get-tuple-element.45), channel_id=1, source_target_pairs={{6,0},{0,2},{2,4},{4,6},{14,8},{8,10},{10,12},{12,14},{22,16},{16,... | collective-permute-start | bytes 786440 | tf_op jit(solution)/shard_map/ppermute | solution.py:37
  39.0 8.6 %collective-permute-start.14 = (bf16[2,256,256]{2,1,0:T(8,128)(2,1)S(1)}, bf16[2,256,256]{2,1,0:T(8,128)(2,1)S(1)}, u32[]{:S(2)}, u32[]{:S(2)}) collective-permute-start(bf16[2,256,256]{2,1,0:T(8,128)(2,1)S(1)} %get-tuple-element.42.refs_4_), channel_id=1, source_target_pairs={{6,0},{0,2},{2,4},{4,6},{14,8},{8,10},{10,12},{12,14},{22,16},{16,... | collective-permute-start | bytes 786440 | tf_op jit(solution)/shard_map/ppermute | solution.py:37
  40.1 4.8 %collective-permute-start.12 = (bf16[64,512]{1,0:T(8,128)(2,1)S(1)}, bf16[64,512]{1,0:T(8,128)(2,1)S(1)}, u32[]{:S(2)}, u32[]{:S(2)}) collective-permute-start(bf16[64,512]{1,0:T(8,128)(2,1)S(1)} %shard_map.92.refs_0_), channel_id=1, source_target_pairs={{0,8},{1,9},{2,10},{3,11},{4,12},{5,13},{6,14},{7,15},{8,0},{9,1},... | collective-permute-start | bytes 196616 | tf_op jit(solution)/shard_map/ppermute | solution.py:435
  45.0 11.8 %collective-permute-start.13 = (bf16[64,512]{1,0:T(8,128)(2,1)S(1)}, bf16[64,512]{1,0:T(8,128)(2,1)S(1)}, u32[]{:S(2)}, u32[]{:S(2)}) collective-permute-start(bf16[64,512]{1,0:T(8,128)(2,1)S(1)} %shard_map.93.refs_4_.refs_0_), channel_id=1, source_target_pairs={{0,16},{1,17},{2,18},{3,19},{4,20},{5,21},{6,22},{7,23},{8,24},{9,... | collective-permute-start | bytes 196616 | tf_op jit(solution)/shard_map/ppermute | solution.py:435
  47.6 12.7 %collective-permute-start.19 = (bf16[2,256,256]{2,1,0:T(8,128)(2,1)S(1)}, bf16[2,256,256]{2,1,0:T(8,128)(2,1)S(1)}, u32[]{:S(2)}, u32[]{:S(2)}) collective-permute-start(bf16[2,256,256]{2,1,0:T(8,128)(2,1)S(1)} %get-tuple-element.46.refs_2_), channel_id=1, source_target_pairs={{24,0},{26,2},{28,4},{30,6},{0,8},{2,10},{4,12},{6,14},{8,16},{10,... | collective-permute-start | bytes 786440 | tf_op jit(solution)/shard_map/ppermute | solution.py:37
  56.7 5.8 %collective-permute-start.18 = (bf16[64,512]{1,0:T(8,128)(2,1)S(1)}, bf16[64,512]{1,0:T(8,128)(2,1)S(1)}, u32[]{:S(2)}, u32[]{:S(2)}) collective-permute-start(bf16[64,512]{1,0:T(8,128)(2,1)S(1)} %shard_map.95.refs_4_.refs_0_), channel_id=1, source_target_pairs={{0,5},{1,4},{2,7},{3,6},{4,1},{5,0},{6,3},{7,2},{8,13},{9,12},{10,... | collective-permute-start | bytes 196616 | tf_op jit(solution)/shard_map/ppermute | solution.py:435
  56.8 6.4 %collective-permute-start.17 = (bf16[64,512]{1,0:T(8,128)(2,1)S(1)}, bf16[64,512]{1,0:T(8,128)(2,1)S(1)}, u32[]{:S(2)}, u32[]{:S(2)}) collective-permute-start(bf16[64,512]{1,0:T(8,128)(2,1)S(1)} %shard_map.95.refs_4_.refs_0_), channel_id=1, source_target_pairs={{0,4},{1,5},{2,6},{3,7},{4,0},{5,1},{6,2},{7,3},{8,12},{9,13},{10,... | collective-permute-start | bytes 196616 | tf_op jit(solution)/shard_map/ppermute | solution.py:435
  59.8 5.0 %collective-permute-start.16 = (bf16[64,512]{1,0:T(8,128)(2,1)S(1)}, bf16[64,512]{1,0:T(8,128)(2,1)S(1)}, u32[]{:S(2)}, u32[]{:S(2)}) collective-permute-start(bf16[64,512]{1,0:T(8,128)(2,1)S(1)} %shard_map.95.refs_4_.refs_0_), channel_id=1, source_target_pairs={{0,1},{1,0},{2,3},{3,2},{4,5},{5,4},{6,7},{7,6},{8,9},{9,8},{10,11... | collective-permute-start | bytes 196616 | tf_op jit(solution)/shard_map/ppermute | solution.py:435
  60.4 8.9 %collective-permute-start.21 = (bf16[2,256,256]{2,1,0:T(8,128)(2,1)S(1)}, bf16[2,256,256]{2,1,0:T(8,128)(2,1)S(1)}, u32[]{:S(2)}, u32[]{:S(2)}) collective-permute-start(bf16[2,256,256]{2,1,0:T(8,128)(2,1)S(1)} %shard_map.96.refs_4_.refs_3_), channel_id=1, source_target_pairs={{0,1},{1,0},{2,3},{3,2},{4,5},{5,4},{6,7},{7,6},{8,9},{9,8},{10,11... | collective-permute-start | bytes 786440 | tf_op jit(solution)/shard_map/ppermute | solution.py:578
  64.9 4.4 %collective-permute-start.20 = (bf16[256,512]{1,0:T(8,128)(2,1)S(1)}, bf16[256,512]{1,0:T(8,128)(2,1)S(1)}, u32[]{:S(2)}, u32[]{:S(2)}) collective-permute-start(bf16[256,512]{1,0:T(8,128)(2,1)S(1)} %shard_map.97.refs_0_), channel_id=1, source_target_pairs={{0,2},{1,3},{2,0},{3,1},{4,6},{5,7},{6,4},{7,5},{8,10},{9,11},{10,... | collective-permute-start | bytes 786440 | tf_op jit(solution)/shard_map/ppermute | solution.py:435

commit v20 on v17

--- a/solution.py
+++ b/solution.py
@@ -325,7 +325,7 @@
         scratch_shapes=[
             pltpu.VMEM(probe.shape, f32),
             pltpu.SemaphoreType.DMA((2,)),
-            pltpu.SemaphoreType.DMA((8,)),
+            pltpu.SemaphoreType.DMA((16,)),
         ],
         compiler_params=pltpu.CompilerParams(vmem_limit_bytes=8 * 2**20),
         cost_estimate=pl.CostEstimate(

time: 63.8 us -> 63.8 us (level)
  no operation moved by 1% of the time
where the time goes in v20:
time: 63.8 us; the launch traced here: 63.6 us
  starting transfers between devices  27.2 us (43%)
  waiting for transfers between devices  24 us (38%)
  Pallas kernels  9.13 us (14%)
  local copies, waits for them, and re-layouts  1.86 us (3%)
  between operations  1.42 us (2%)
    ppermute x11, starting transfers between devices, swap_with(): lax.ppermute(x, ('tile', 'pos'), [(i, i ^ mask) for i in range(devices)])  11.7 us
    ppermute x8, starting transfers between devices, from_behind(): return lax.ppermute(block, 'tile', [(source(i), i) for i in range(tiles)])  10.6 us
    ppermute x8, waiting for transfers between devices, from_behind(): return lax.ppermute(block, 'tile', [(source(i), i) for i in range(tiles)])  10.6 us
    pallas_call x13, Pallas kernels, run(): pl.pallas_call(body, out_shape=sum(outs, []), in_specs=sum(specs, []) + [...  7.83 us
    ppermute x11, waiting for transfers between devices, swap_with(): lax.ppermute(x, ('tile', 'pos'), [(i, i ^ mask) for i in range(devices)])  6.18 us
    ppermute x1, waiting for transfers between devices, shards(): other_slice = lax.ppermute(this_slice, 'pos', swap)  4.87 us
    ppermute x1, starting transfers between devices, shards(): other_slice = lax.ppermute(this_slice, 'pos', swap)  1.82 us
    ppermute x1, starting transfers between devices, shards(): got = lax.ppermute(given, 'pos', swap)  1.58 us
  transfers between devices with their start and end apart: 22, of which 11 were waited for; matrix products, arithmetic and copies ran while one was open for 0% of the time, Pallas kernels for 6%

profile of v20, /device:TPU:0, one launch (start us, length us, event | category | flops | bytes accessed | tf_op | source)
XLA Modules:
  0.0 63.6 jit_solution(10910932517737682058)
XLA Ops:
  0.6 1.2 %slice_bitcast_fusion = (bf16[2,256,256]{2,1,0:T(8,128)(2,1)S(1)}, bf16[2,256,256]{2,1,0:T(8,128)(2,1)S(1)}) fusion(bf16[1,2,2,256,256]{4,3,2,1,0:T(8,128)(2,1)} %param.7), kind=kLoop, calls=%fused_computation | loop fusion | bytes 1048576 | tf_op jit(solution)/shard_map/squeeze | solution.py:471
  1.8 0.0 copy-start.1
  1.8 5.1 %collective-permute-start.4 = (bf16[2,256,256]{2,1,0:T(8,128)(2,1)S(1)}, bf16[2,256,256]{2,1,0:T(8,128)(2,1)S(1)}, u32[]{:S(2)}, u32[]{:S(2)}) collective-permute-start(bf16[2,256,256]{2,1,0:T(8,128)(2,1)S(1)} %get-tuple-element.50.refs_4_.refs_2_.refs_0_), channel_id=1, source_target_pairs={{8,0},{10,2},{12,4},{14,6},{16,8},{18,10},{20,12},{22,14},{24,16},... | collective-permute-start | bytes 786440 | tf_op jit(solution)/shard_map/ppermute | solution.py:31
  6.9 0.7 %collective-permute-start.1 = (bf16[2,2,256,256]{3,2,1,0:T(8,128)(2,1)}, bf16[2,2,256,256]{3,2,1,0:T(8,128)(2,1)S(1)}, u32[]{:S(2)}, u32[]{:S(2)}) collective-permute-start(bf16[2,2,256,256]{3,2,1,0:T(8,128)(2,1)} %bitcast.17), channel_id=1, source_target_pairs={{2,0},{4,2},{6,4},{0,6},{10,8},{12,10},{14,12},{8,14},{18,16},{20,... | collective-permute-start | bytes 1572872 | tf_op jit(solution)/shard_map/ppermute | solution.py:31
  8.2 0.0 copy-start.3
  8.3 0.7 %copy-done.3 = s32[1,1,2,2]{3,2,1,0:T(2,128)S(1)} copy-done((s32[1,1,2,2]{3,2,1,0:T(2,128)S(1)}, s32[1,1,2,2]{3,2,1,0:T(2,128)}, u32[]{:S(2)}) %copy-start.3) | copy-done | bytes 40
  8.9 0.6 shard_map.86
  9.5 0.5 collective-permute-start.2
  10.0 3.6 %collective-permute-done.4.refs_4_ = bf16[2,256,256]{2,1,0:T(8,128)(2,1)S(1)} collective-permute-done((bf16[2,256,256]{2,1,0:T(8,128)(2,1)S(1)}, bf16[2,256,256]{2,1,0:T(8,128)(2,1)S(1)}, u32[]{:S(2)}, u32[]{:S(2)}) %collective-permute-start.4) | collective-permute-done | bytes 262176 | tf_op jit(solution)/shard_map/ppermute | solution.py:31
  13.6 0.0 collective-permute-start.5
  13.6 1.5 %collective-permute-start = (bf16[272,256]{1,0:T(8,128)(2,1)S(1)}, bf16[272,256]{1,0:T(8,128)(2,1)S(1)}, u32[]{:S(2)}, u32[]{:S(2)}) collective-permute-start(bf16[272,256]{1,0:T(8,128)(2,1)S(1)} %get-tuple-element.27), channel_id=1, source_target_pairs={{0,1},{1,0},{2,3},{3,2},{4,5},{5,4},{6,7},{7,6},{8,9},{9,8},{10,11... | collective-permute-start | bytes 417800 | tf_op jit(solution)/shard_map/ppermute | solution.py:493
  15.2 2.9 %collective-permute-done.2.refs_4_ = bf16[2,256,256]{2,1,0:T(8,128)(2,1)S(1)} collective-permute-done((bf16[2,256,256]{2,1,0:T(8,128)(2,1)S(1)}, bf16[2,256,256]{2,1,0:T(8,128)(2,1)S(1)}, u32[]{:S(2)}, u32[]{:S(2)}) %collective-permute-start.2) | collective-permute-done | bytes 262176 | tf_op jit(solution)/shard_map/ppermute | solution.py:31
  18.1 0.3 collective-permute-start.3
  18.5 0.1 shard_map.87
  18.6 1.2 %collective-permute-done.refs_1_ = bf16[272,256]{1,0:T(8,128)(2,1)S(1)} collective-permute-done((bf16[272,256]{1,0:T(8,128)(2,1)S(1)}, bf16[272,256]{1,0:T(8,128)(2,1)S(1)}, u32[]{:S(2)}, u32[]{:S(2)}) %collective-permute-start) | collective-permute-done | bytes 139296 | tf_op jit(solution)/shard_map/ppermute | solution.py:493
  19.7 0.0 collective-permute-done.5.refs_5_
  19.7 0.0 collective-permute-done.1.refs_3_
  19.7 1.8 %shard_map.88 = (bf16[2,256,256]{2,1,0:T(8,128)(2,1)S(1)}, f32[2,256,512]{2,1,0:T(8,128)S(1)}) custom-call(bf16[272,256]{1,0:T(8,128)(2,1)S(1)} %get-tuple-element.26.refs_0_, bf16[272,256]{1,0:T(8,128)(2,1)S(1)} %collective-permute-done.refs_1_, bf16[2,256,256]{2,1,0:T(8,128)(2,1)S(1)} %get-tuple-element.50.refs_4_.refs_2_.refs_0_, ...), custom_call_target="tpu_custom_call" | custom-call | flops 1500000000 | bytes 4472832 | tf_op jit(solution)/shard_map/pallas_call | solution.py:289
  21.5 0.8 %collective-permute-done.3.refs_5_ = bf16[2,256,256]{2,1,0:T(8,128)(2,1)S(1)} collective-permute-done((bf16[2,256,256]{2,1,0:T(8,128)(2,1)S(1)}, bf16[2,256,256]{2,1,0:T(8,128)(2,1)S(1)}, u32[]{:S(2)}, u32[]{:S(2)}) %collective-permute-start.3) | collective-permute-done | bytes 262176 | tf_op jit(solution)/shard_map/ppermute | solution.py:31
  22.4 3.8 %shard_map.89 = (bf16[2,256,256]{2,1,0:T(8,128)(2,1)S(1)}, bf16[2,256,256]{2,1,0:T(8,128)(2,1)S(1)}, bf16[256,512]{1,0:T(8,128)(2,1)S(1)}, bf16[128,512]{1,0:T(8,128)(2,1)S(1)}, bf16[128,512]{1,0:T(8,128)(2,1)S(1)}) custom-call(bf16[272,256]{1,0:T(8,128)(2,1)S(1)} %get-tuple-element.26.refs_0_, bf16[272,256]{1,0:T(8,128)(2,1)S(1)} %collective-permute-done.refs_1_, ...), custom_call_target="tpu_custom_call" | custom-call | flops 4000000000 | bytes 6045696 | tf_op jit(solution)/shard_map/pallas_call | solution.py:289
  26.2 1.6 %collective-permute-start.11 = (bf16[2,256,256]{2,1,0:T(8,128)(2,1)S(1)}, bf16[2,256,256]{2,1,0:T(8,128)(2,1)S(1)}, u32[]{:S(2)}, u32[]{:S(2)}) collective-permute-start(bf16[2,256,256]{2,1,0:T(8,128)(2,1)S(1)} %get-tuple-element.41), channel_id=1, source_target_pairs={{0,1},{1,0},{2,3},{3,2},{4,5},{5,4},{6,7},{7,6},{8,9},{9,8},{10,11... | collective-permute-start | bytes 786440 | tf_op jit(solution)/shard_map/ppermute | solution.py:536
  27.8 1.1 %collective-permute-start.6 = (bf16[128,512]{1,0:T(8,128)(2,1)S(1)}, bf16[128,512]{1,0:T(8,128)(2,1)S(1)}, u32[]{:S(2)}, u32[]{:S(2)}) collective-permute-start(bf16[128,512]{1,0:T(8,128)(2,1)S(1)} %get-tuple-element.34), channel_id=1, source_target_pairs={{0,2},{1,3},{2,0},{3,1},{4,6},{5,7},{6,4},{7,5},{8,10},{9,11},{10,... | collective-permute-start | bytes 393224 | tf_op jit(solution)/shard_map/ppermute | solution.py:429
  28.9 1.0 %collective-permute-done.6.refs_1_ = bf16[128,512]{1,0:T(8,128)(2,1)S(1)} collective-permute-done((bf16[128,512]{1,0:T(8,128)(2,1)S(1)}, bf16[128,512]{1,0:T(8,128)(2,1)S(1)}, u32[]{:S(2)}, u32[]{:S(2)}) %collective-permute-start.6) | collective-permute-done | bytes 131104 | tf_op jit(solution)/shard_map/ppermute | solution.py:429
  29.9 0.4 collective-permute-done.7.refs_2_
  30.3 0.1 shard_map.90
  30.4 0.6 collective-permute-start.8
  31.0 0.9 %collective-permute-start.9 = (bf16[64,512]{1,0:T(8,128)(2,1)S(1)}, bf16[64,512]{1,0:T(8,128)(2,1)S(1)}, u32[]{:S(2)}, u32[]{:S(2)}) collective-permute-start(bf16[64,512]{1,0:T(8,128)(2,1)S(1)} %get-tuple-element.38), channel_id=1, source_target_pairs={{0,4},{1,5},{2,6},{3,7},{4,0},{5,1},{6,2},{7,3},{8,12},{9,13},{10,... | collective-permute-start | bytes 196616 | tf_op jit(solution)/shard_map/ppermute | solution.py:429
  31.8 2.1 %collective-permute-start.10 = (bf16[64,512]{1,0:T(8,128)(2,1)S(1)}, bf16[64,512]{1,0:T(8,128)(2,1)S(1)}, u32[]{:S(2)}, u32[]{:S(2)}) collective-permute-start(bf16[64,512]{1,0:T(8,128)(2,1)S(1)} %get-tuple-element.39), channel_id=1, source_target_pairs={{0,5},{1,4},{2,7},{3,6},{4,1},{5,0},{6,3},{7,2},{8,13},{9,12},{10,... | collective-permute-start | bytes 196616 | tf_op jit(solution)/shard_map/ppermute | solution.py:429
  33.9 1.1 %collective-permute-done.11.refs_3_ = bf16[2,256,256]{2,1,0:T(8,128)(2,1)S(1)} collective-permute-done((bf16[2,256,256]{2,1,0:T(8,128)(2,1)S(1)}, bf16[2,256,256]{2,1,0:T(8,128)(2,1)S(1)}, u32[]{:S(2)}, u32[]{:S(2)}) %collective-permute-start.11) | collective-permute-done | bytes 262176 | tf_op jit(solution)/shard_map/ppermute | solution.py:536
  35.1 1.1 %shard_map.91 = (f32[2,256,256]{2,1,0:T(8,128)S(1)}, f32[2,256,256]{2,1,0:T(8,128)S(1)}, bf16[2,256,256]{2,1,0:T(8,128)(2,1)S(1)}, bf16[2,256,256]{2,1,0:T(8,128)(2,1)S(1)}) custom-call(bf16[272,256]{1,0:T(8,128)(2,1)S(1)} %get-tuple-element.26.refs_0_, bf16[272,256]{1,0:T(8,128)(2,1)S(1)} %collective-permute-done.refs_1_, ...), custom_call_target="tpu_custom_call" | custom-call | bytes 2375680 | tf_op jit(solution)/shard_map/pallas_call | solution.py:289
  36.1 1.6 %collective-permute-start.15 = (bf16[2,256,256]{2,1,0:T(8,128)(2,1)S(1)}, bf16[2,256,256]{2,1,0:T(8,128)(2,1)S(1)}, u32[]{:S(2)}, u32[]{:S(2)}) collective-permute-start(bf16[2,256,256]{2,1,0:T(8,128)(2,1)S(1)} %get-tuple-element.45), channel_id=1, source_target_pairs={{6,0},{0,2},{2,4},{4,6},{14,8},{8,10},{10,12},{12,14},{22,16},{16,... | collective-permute-start | bytes 786440 | tf_op jit(solution)/shard_map/ppermute | solution.py:31
  37.8 0.4 collective-permute-start.14
  38.2 0.6 %collective-permute-start.12 = (bf16[64,512]{1,0:T(8,128)(2,1)S(1)}, bf16[64,512]{1,0:T(8,128)(2,1)S(1)}, u32[]{:S(2)}, u32[]{:S(2)}) collective-permute-start(bf16[64,512]{1,0:T(8,128)(2,1)S(1)} %shard_map.92.refs_0_), channel_id=1, source_target_pairs={{0,8},{1,9},{2,10},{3,11},{4,12},{5,13},{6,14},{7,15},{8,0},{9,1},... | collective-permute-start | bytes 196616 | tf_op jit(solution)/shard_map/ppermute | solution.py:429
  38.9 4.1 %collective-permute-done.12.refs_1_ = bf16[64,512]{1,0:T(8,128)(2,1)S(1)} collective-permute-done((bf16[64,512]{1,0:T(8,128)(2,1)S(1)}, bf16[64,512]{1,0:T(8,128)(2,1)S(1)}, u32[]{:S(2)}, u32[]{:S(2)}) %collective-permute-start.12) | collective-permute-done | bytes 65568 | tf_op jit(solution)/shard_map/ppermute | solution.py:429
  43.0 2.7 %collective-permute-start.13 = (bf16[64,512]{1,0:T(8,128)(2,1)S(1)}, bf16[64,512]{1,0:T(8,128)(2,1)S(1)}, u32[]{:S(2)}, u32[]{:S(2)}) collective-permute-start(bf16[64,512]{1,0:T(8,128)(2,1)S(1)} %shard_map.93.refs_4_.refs_0_), channel_id=1, source_target_pairs={{0,16},{1,17},{2,18},{3,19},{4,20},{5,21},{6,22},{7,23},{8,24},{9,... | collective-permute-start | bytes 196616 | tf_op jit(solution)/shard_map/ppermute | solution.py:429
  45.7 0.1 shard_map.94
  45.8 2.0 %collective-permute-start.19 = (bf16[2,256,256]{2,1,0:T(8,128)(2,1)S(1)}, bf16[2,256,256]{2,1,0:T(8,128)(2,1)S(1)}, u32[]{:S(2)}, u32[]{:S(2)}) collective-permute-start(bf16[2,256,256]{2,1,0:T(8,128)(2,1)S(1)} %get-tuple-element.46.refs_2_), channel_id=1, source_target_pairs={{24,0},{26,2},{28,4},{30,6},{0,8},{2,10},{4,12},{6,14},{8,16},{10,... | collective-permute-start | bytes 786440 | tf_op jit(solution)/shard_map/ppermute | solution.py:31
  47.8 0.8 %collective-permute-done.13.refs_1_ = bf16[64,512]{1,0:T(8,128)(2,1)S(1)} collective-permute-done((bf16[64,512]{1,0:T(8,128)(2,1)S(1)}, bf16[64,512]{1,0:T(8,128)(2,1)S(1)}, u32[]{:S(2)}, u32[]{:S(2)}) %collective-permute-start.13) | collective-permute-done | bytes 65568 | tf_op jit(solution)/shard_map/ppermute | solution.py:429
  48.5 2.2 %collective-permute-start.18 = (bf16[64,512]{1,0:T(8,128)(2,1)S(1)}, bf16[64,512]{1,0:T(8,128)(2,1)S(1)}, u32[]{:S(2)}, u32[]{:S(2)}) collective-permute-start(bf16[64,512]{1,0:T(8,128)(2,1)S(1)} %shard_map.95.refs_4_.refs_0_), channel_id=1, source_target_pairs={{0,5},{1,4},{2,7},{3,6},{4,1},{5,0},{6,3},{7,2},{8,13},{9,12},{10,... | collective-permute-start | bytes 196616 | tf_op jit(solution)/shard_map/ppermute | solution.py:429
  50.7 1.1 %collective-permute-start.17 = (bf16[64,512]{1,0:T(8,128)(2,1)S(1)}, bf16[64,512]{1,0:T(8,128)(2,1)S(1)}, u32[]{:S(2)}, u32[]{:S(2)}) collective-permute-start(bf16[64,512]{1,0:T(8,128)(2,1)S(1)} %shard_map.95.refs_4_.refs_0_), channel_id=1, source_target_pairs={{0,4},{1,5},{2,6},{3,7},{4,0},{5,1},{6,2},{7,3},{8,12},{9,13},{10,... | collective-permute-start | bytes 196616 | tf_op jit(solution)/shard_map/ppermute | solution.py:429
  51.8 0.3 collective-permute-start.16
  52.1 3.2 %collective-permute-done.19.refs_3_ = bf16[2,256,256]{2,1,0:T(8,128)(2,1)S(1)} collective-permute-done((bf16[2,256,256]{2,1,0:T(8,128)(2,1)S(1)}, bf16[2,256,256]{2,1,0:T(8,128)(2,1)S(1)}, u32[]{:S(2)}, u32[]{:S(2)}) %collective-permute-start.19) | collective-permute-done | bytes 262176 | tf_op jit(solution)/shard_map/ppermute | solution.py:31
  55.3 0.1 shard_map.96.refs_4_.refs_3_
  55.5 1.8 %collective-permute-start.21 = (bf16[2,256,256]{2,1,0:T(8,128)(2,1)S(1)}, bf16[2,256,256]{2,1,0:T(8,128)(2,1)S(1)}, u32[]{:S(2)}, u32[]{:S(2)}) collective-permute-start(bf16[2,256,256]{2,1,0:T(8,128)(2,1)S(1)} %shard_map.96.refs_4_.refs_3_), channel_id=1, source_target_pairs={{0,1},{1,0},{2,3},{3,2},{4,5},{5,4},{6,7},{7,6},{8,9},{9,8},{10,11... | collective-permute-start | bytes 786440 | tf_op jit(solution)/shard_map/ppermute | solution.py:572
  57.3 0.1 shard_map.97.refs_0_
  57.4 0.1 collective-permute-start.20
  57.4 4.9 %collective-permute-done.21.refs_1_.refs_4_ = bf16[2,256,256]{2,1,0:T(8,128)(2,1)S(1)} collective-permute-done((bf16[2,256,256]{2,1,0:T(8,128)(2,1)S(1)}, bf16[2,256,256]{2,1,0:T(8,128)(2,1)S(1)}, u32[]{:S(2)}, u32[]{:S(2)}) %collective-permute-start.21) | collective-permute-done | bytes 262176 | tf_op jit(solution)/shard_map/ppermute | solution.py:572
  62.3 1.3 %shard_map.99 = (f32[2048,128]{1,0:T(8,128)}, bf16[1,2,2,256,256]{4,3,2,1,0:T(8,128)(2,1)}) custom-call(bf16[256,512]{1,0:T(8,128)(2,1)S(1)} %shard_map.97.refs_0_, bf16[256,512]{1,0:T(8,128)(2,1)S(1)} %collective-permute-done.20.refs_1_, f32[2048,128]{1,0:T(8,128)S(1)} %bitcast.16, bf16[2,256,256]{2,1,0:T(8,128)(2,1)S(1)} %shard_map.96.refs_4_.refs_3_, ...), custom_call_target="tpu_custom_call" | custom-call | flops 1048576 | bytes 3145728 | tf_op jit(solution)/shard_map/pallas_call | solution.py:320
  (21 shorter events, 0.1 us)
Async XLA Ops:
  0.6 7.6 %copy-start.2 = (bf16[1,1,2,256,256]{4,3,2,1,0:T(8,128)(2,1)S(1)}, bf16[1,1,2,256,256]{4,3,2,1,0:T(8,128)(2,1)}, u32[]{:S(2)}) copy-start(bf16[1,1,2,256,256]{4,3,2,1,0:T(8,128)(2,1)} %refs_3_.1) | copy-start | bytes 786436
  0.6 17.8 %copy-start = (f32[2,256,2,256]{3,2,1,0:T(2,128)S(1)}, f32[2,256,2,256]{3,2,1,0:T(2,128)}, u32[]{:S(2)}) copy-start(f32[2,256,2,256]{3,2,1,0:T(2,128)} %param.8) | copy-start | bytes 3145732
  1.8 16.7 %copy-start.1 = (bf16[512,512]{1,0:T(8,128)(2,1)S(1)}, bf16[512,512]{1,0:T(8,128)(2,1)}, u32[]{:S(2)}) copy-start(bf16[512,512]{1,0:T(8,128)(2,1)} %constant.10.refs_1_) | copy-start | bytes 1572868
  1.8 11.8 %collective-permute-start.4 = (bf16[2,256,256]{2,1,0:T(8,128)(2,1)S(1)}, bf16[2,256,256]{2,1,0:T(8,128)(2,1)S(1)}, u32[]{:S(2)}, u32[]{:S(2)}) collective-permute-start(bf16[2,256,256]{2,1,0:T(8,128)(2,1)S(1)} %get-tuple-element.50.refs_4_.refs_2_.refs_0_), channel_id=1, source_target_pairs={{8,0},{10,2},{12,4},{14,6},{16,8},{18,10},{20,12},{22,14},{24,16},... | collective-permute-start | bytes 786440 | tf_op jit(solution)/shard_map/ppermute | solution.py:31
  6.9 12.8 %collective-permute-start.1 = (bf16[2,2,256,256]{3,2,1,0:T(8,128)(2,1)}, bf16[2,2,256,256]{3,2,1,0:T(8,128)(2,1)S(1)}, u32[]{:S(2)}, u32[]{:S(2)}) collective-permute-start(bf16[2,2,256,256]{3,2,1,0:T(8,128)(2,1)} %bitcast.17), channel_id=1, source_target_pairs={{2,0},{4,2},{6,4},{0,6},{10,8},{12,10},{14,12},{8,14},{18,16},{20,... | collective-permute-start | bytes 1572872 | tf_op jit(solution)/shard_map/ppermute | solution.py:31
  8.2 0.7 %copy-start.3 = (s32[1,1,2,2]{3,2,1,0:T(2,128)S(1)}, s32[1,1,2,2]{3,2,1,0:T(2,128)}, u32[]{:S(2)}) copy-start(s32[1,1,2,2]{3,2,1,0:T(2,128)} %refs_0_.1) | copy-start | bytes 52
  9.5 8.6 %collective-permute-start.2 = (bf16[2,256,256]{2,1,0:T(8,128)(2,1)S(1)}, bf16[2,256,256]{2,1,0:T(8,128)(2,1)S(1)}, u32[]{:S(2)}, u32[]{:S(2)}) collective-permute-start(bf16[2,256,256]{2,1,0:T(8,128)(2,1)S(1)} %get-tuple-element.28.refs_2_.refs_1_), channel_id=1, source_target_pairs={{8,0},{10,2},{12,4},{14,6},{16,8},{18,10},{20,12},{22,14},{24,16},... | collective-permute-start | bytes 786440 | tf_op jit(solution)/shard_map/ppermute | solution.py:31
  13.6 6.1 %collective-permute-start.5 = (bf16[2,256,256]{2,1,0:T(8,128)(2,1)S(1)}, bf16[2,256,256]{2,1,0:T(8,128)(2,1)S(1)}, u32[]{:S(2)}, u32[]{:S(2)}) collective-permute-start(bf16[2,256,256]{2,1,0:T(8,128)(2,1)S(1)} %collective-permute-done.4.refs_4_), channel_id=1, source_target_pairs={{2,0},{4,2},{6,4},{0,6},{10,8},{12,10},{14,12},{8,14},{18,16},{20,... | collective-permute-start | bytes 786440 | tf_op jit(solution)/shard_map/ppermute | solution.py:31
  13.6 6.1 %collective-permute-start = (bf16[272,256]{1,0:T(8,128)(2,1)S(1)}, bf16[272,256]{1,0:T(8,128)(2,1)S(1)}, u32[]{:S(2)}, u32[]{:S(2)}) collective-permute-start(bf16[272,256]{1,0:T(8,128)(2,1)S(1)} %get-tuple-element.27), channel_id=1, source_target_pairs={{0,1},{1,0},{2,3},{3,2},{4,5},{5,4},{6,7},{7,6},{8,9},{9,8},{10,11... | collective-permute-start | bytes 417800 | tf_op jit(solution)/shard_map/ppermute | solution.py:493
  18.1 4.2 %collective-permute-start.3 = (bf16[2,256,256]{2,1,0:T(8,128)(2,1)S(1)}, bf16[2,256,256]{2,1,0:T(8,128)(2,1)S(1)}, u32[]{:S(2)}, u32[]{:S(2)}) collective-permute-start(bf16[2,256,256]{2,1,0:T(8,128)(2,1)S(1)} %collective-permute-done.2.refs_4_), channel_id=1, source_target_pairs={{2,0},{4,2},{6,4},{0,6},{10,8},{12,10},{14,12},{8,14},{18,16},{20,... | collective-permute-start | bytes 786440 | tf_op jit(solution)/shard_map/ppermute | solution.py:31
  19.7 2.6 %copy-start.4 = (bf16[512,512]{1,0:T(8,128)(2,1)S(1)}, bf16[512,512]{1,0:T(8,128)(2,1)}, u32[]{:S(2)}) copy-start(bf16[512,512]{1,0:T(8,128)(2,1)} %constant.11.refs_10_) | copy-start | bytes 1572868
  26.2 8.9 %collective-permute-start.11 = (bf16[2,256,256]{2,1,0:T(8,128)(2,1)S(1)}, bf16[2,256,256]{2,1,0:T(8,128)(2,1)S(1)}, u32[]{:S(2)}, u32[]{:S(2)}) collective-permute-start(bf16[2,256,256]{2,1,0:T(8,128)(2,1)S(1)} %get-tuple-element.41), channel_id=1, source_target_pairs={{0,1},{1,0},{2,3},{3,2},{4,5},{5,4},{6,7},{7,6},{8,9},{9,8},{10,11... | collective-permute-start | bytes 786440 | tf_op jit(solution)/shard_map/ppermute | solution.py:536
  27.8 2.1 %collective-permute-start.6 = (bf16[128,512]{1,0:T(8,128)(2,1)S(1)}, bf16[128,512]{1,0:T(8,128)(2,1)S(1)}, u32[]{:S(2)}, u32[]{:S(2)}) collective-permute-start(bf16[128,512]{1,0:T(8,128)(2,1)S(1)} %get-tuple-element.34), channel_id=1, source_target_pairs={{0,2},{1,3},{2,0},{3,1},{4,6},{5,7},{6,4},{7,5},{8,10},{9,11},{10,... | collective-permute-start | bytes 393224 | tf_op jit(solution)/shard_map/ppermute | solution.py:429
  28.9 1.3 %collective-permute-start.7 = (bf16[128,512]{1,0:T(8,128)(2,1)S(1)}, bf16[128,512]{1,0:T(8,128)(2,1)S(1)}, u32[]{:S(2)}, u32[]{:S(2)}) collective-permute-start(bf16[128,512]{1,0:T(8,128)(2,1)S(1)} %get-tuple-element.35), channel_id=1, source_target_pairs={{0,2},{1,3},{2,0},{3,1},{4,6},{5,7},{6,4},{7,5},{8,10},{9,11},{10,... | collective-permute-start | bytes 393224 | tf_op jit(solution)/shard_map/ppermute | solution.py:429
  30.4 7.8 %collective-permute-start.8 = (bf16[64,512]{1,0:T(8,128)(2,1)S(1)}, bf16[64,512]{1,0:T(8,128)(2,1)S(1)}, u32[]{:S(2)}, u32[]{:S(2)}) collective-permute-start(bf16[64,512]{1,0:T(8,128)(2,1)S(1)} %get-tuple-element.37), channel_id=1, source_target_pairs={{0,1},{1,0},{2,3},{3,2},{4,5},{5,4},{6,7},{7,6},{8,9},{9,8},{10,11... | collective-permute-start | bytes 196616 | tf_op jit(solution)/shard_map/ppermute | solution.py:429
  31.0 7.2 %collective-permute-start.9 = (bf16[64,512]{1,0:T(8,128)(2,1)S(1)}, bf16[64,512]{1,0:T(8,128)(2,1)S(1)}, u32[]{:S(2)}, u32[]{:S(2)}) collective-permute-start(bf16[64,512]{1,0:T(8,128)(2,1)S(1)} %get-tuple-element.38), channel_id=1, source_target_pairs={{0,4},{1,5},{2,6},{3,7},{4,0},{5,1},{6,2},{7,3},{8,12},{9,13},{10,... | collective-permute-start | bytes 196616 | tf_op jit(solution)/shard_map/ppermute | solution.py:429
  31.8 6.3 %collective-permute-start.10 = (bf16[64,512]{1,0:T(8,128)(2,1)S(1)}, bf16[64,512]{1,0:T(8,128)(2,1)S(1)}, u32[]{:S(2)}, u32[]{:S(2)}) collective-permute-start(bf16[64,512]{1,0:T(8,128)(2,1)S(1)} %get-tuple-element.39), channel_id=1, source_target_pairs={{0,5},{1,4},{2,7},{3,6},{4,1},{5,0},{6,3},{7,2},{8,13},{9,12},{10,... | collective-permute-start | bytes 196616 | tf_op jit(solution)/shard_map/ppermute | solution.py:429
  36.1 9.5 %collective-permute-start.15 = (bf16[2,256,256]{2,1,0:T(8,128)(2,1)S(1)}, bf16[2,256,256]{2,1,0:T(8,128)(2,1)S(1)}, u32[]{:S(2)}, u32[]{:S(2)}) collective-permute-start(bf16[2,256,256]{2,1,0:T(8,128)(2,1)S(1)} %get-tuple-element.45), channel_id=1, source_target_pairs={{6,0},{0,2},{2,4},{4,6},{14,8},{8,10},{10,12},{12,14},{22,16},{16,... | collective-permute-start | bytes 786440 | tf_op jit(solution)/shard_map/ppermute | solution.py:31
  37.8 7.9 %collective-permute-start.14 = (bf16[2,256,256]{2,1,0:T(8,128)(2,1)S(1)}, bf16[2,256,256]{2,1,0:T(8,128)(2,1)S(1)}, u32[]{:S(2)}, u32[]{:S(2)}) collective-permute-start(bf16[2,256,256]{2,1,0:T(8,128)(2,1)S(1)} %get-tuple-element.42.refs_4_), channel_id=1, source_target_pairs={{6,0},{0,2},{2,4},{4,6},{14,8},{8,10},{10,12},{12,14},{22,16},{16,... | collective-permute-start | bytes 786440 | tf_op jit(solution)/shard_map/ppermute | solution.py:31
  38.2 4.7 %collective-permute-start.12 = (bf16[64,512]{1,0:T(8,128)(2,1)S(1)}, bf16[64,512]{1,0:T(8,128)(2,1)S(1)}, u32[]{:S(2)}, u32[]{:S(2)}) collective-permute-start(bf16[64,512]{1,0:T(8,128)(2,1)S(1)} %shard_map.92.refs_0_), channel_id=1, source_target_pairs={{0,8},{1,9},{2,10},{3,11},{4,12},{5,13},{6,14},{7,15},{8,0},{9,1},... | collective-permute-start | bytes 196616 | tf_op jit(solution)/shard_map/ppermute | solution.py:429
  43.0 5.5 %collective-permute-start.13 = (bf16[64,512]{1,0:T(8,128)(2,1)S(1)}, bf16[64,512]{1,0:T(8,128)(2,1)S(1)}, u32[]{:S(2)}, u32[]{:S(2)}) collective-permute-start(bf16[64,512]{1,0:T(8,128)(2,1)S(1)} %shard_map.93.refs_4_.refs_0_), channel_id=1, source_target_pairs={{0,16},{1,17},{2,18},{3,19},{4,20},{5,21},{6,22},{7,23},{8,24},{9,... | collective-permute-start | bytes 196616 | tf_op jit(solution)/shard_map/ppermute | solution.py:429
  45.8 9.5 %collective-permute-start.19 = (bf16[2,256,256]{2,1,0:T(8,128)(2,1)S(1)}, bf16[2,256,256]{2,1,0:T(8,128)(2,1)S(1)}, u32[]{:S(2)}, u32[]{:S(2)}) collective-permute-start(bf16[2,256,256]{2,1,0:T(8,128)(2,1)S(1)} %get-tuple-element.46.refs_2_), channel_id=1, source_target_pairs={{24,0},{26,2},{28,4},{30,6},{0,8},{2,10},{4,12},{6,14},{8,16},{10,... | collective-permute-start | bytes 786440 | tf_op jit(solution)/shard_map/ppermute | solution.py:31
  48.5 8.7 %collective-permute-start.18 = (bf16[64,512]{1,0:T(8,128)(2,1)S(1)}, bf16[64,512]{1,0:T(8,128)(2,1)S(1)}, u32[]{:S(2)}, u32[]{:S(2)}) collective-permute-start(bf16[64,512]{1,0:T(8,128)(2,1)S(1)} %shard_map.95.refs_4_.refs_0_), channel_id=1, source_target_pairs={{0,5},{1,4},{2,7},{3,6},{4,1},{5,0},{6,3},{7,2},{8,13},{9,12},{10,... | collective-permute-start | bytes 196616 | tf_op jit(solution)/shard_map/ppermute | solution.py:429
  50.7 6.6 %collective-permute-start.17 = (bf16[64,512]{1,0:T(8,128)(2,1)S(1)}, bf16[64,512]{1,0:T(8,128)(2,1)S(1)}, u32[]{:S(2)}, u32[]{:S(2)}) collective-permute-start(bf16[64,512]{1,0:T(8,128)(2,1)S(1)} %shard_map.95.refs_4_.refs_0_), channel_id=1, source_target_pairs={{0,4},{1,5},{2,6},{3,7},{4,0},{5,1},{6,2},{7,3},{8,12},{9,13},{10,... | collective-permute-start | bytes 196616 | tf_op jit(solution)/shard_map/ppermute | solution.py:429
  51.8 5.5 %collective-permute-start.16 = (bf16[64,512]{1,0:T(8,128)(2,1)S(1)}, bf16[64,512]{1,0:T(8,128)(2,1)S(1)}, u32[]{:S(2)}, u32[]{:S(2)}) collective-permute-start(bf16[64,512]{1,0:T(8,128)(2,1)S(1)} %shard_map.95.refs_4_.refs_0_), channel_id=1, source_target_pairs={{0,1},{1,0},{2,3},{3,2},{4,5},{5,4},{6,7},{7,6},{8,9},{9,8},{10,11... | collective-permute-start | bytes 196616 | tf_op jit(solution)/shard_map/ppermute | solution.py:429
  55.5 6.9 %collective-permute-start.21 = (bf16[2,256,256]{2,1,0:T(8,128)(2,1)S(1)}, bf16[2,256,256]{2,1,0:T(8,128)(2,1)S(1)}, u32[]{:S(2)}, u32[]{:S(2)}) collective-permute-start(bf16[2,256,256]{2,1,0:T(8,128)(2,1)S(1)} %shard_map.96.refs_4_.refs_3_), channel_id=1, source_target_pairs={{0,1},{1,0},{2,3},{3,2},{4,5},{5,4},{6,7},{7,6},{8,9},{9,8},{10,11... | collective-permute-start | bytes 786440 | tf_op jit(solution)/shard_map/ppermute | solution.py:572
  57.4 5.0 %collective-permute-start.20 = (bf16[256,512]{1,0:T(8,128)(2,1)S(1)}, bf16[256,512]{1,0:T(8,128)(2,1)S(1)}, u32[]{:S(2)}, u32[]{:S(2)}) collective-permute-start(bf16[256,512]{1,0:T(8,128)(2,1)S(1)} %shard_map.97.refs_0_), channel_id=1, source_target_pairs={{0,2},{1,3},{2,0},{3,1},{4,6},{5,7},{6,4},{7,5},{8,10},{9,11},{10,... | collective-permute-start | bytes 786440 | tf_op jit(solution)/shard_map/ppermute | solution.py:429
